TPU v7x, 256 devices: a whole 4x4x8 slice. The times are simulated.
256 devices in a mesh: lat: 8 (over z), lon: 8 (over x_hi, y), mp: 4 (over x_lo, core).
Axes of the slice: x: 4 (x_hi: 2, x_lo: 2; x = x_hi * 2 + x_lo), y: 4, z: 8, core: 2. Of those that a mesh axis runs over, the one named last changes fastest.
Arguments:
- tokens: bfloat16 [4, 48, 96, 1024], P(None, 'lat', 'lon'), may hold values from -6 to 6
- qkv_first: bfloat16 [1024, 3, 1024], P(None, None, 'mp'), may hold values from -5 to 5
- qkv_second: bfloat16 [1024, 3, 1024], P(None, None, 'mp'), may hold values from -5 to 5
- out_first: bfloat16 [1024, 1024], P('mp'), may hold values from -0.1875 to 0.1875
- out_second: bfloat16 [1024, 1024], P('mp'), may hold values from -0.1875 to 0.1875
- rel_tables: float32 [2, 16, 37], P(None, 'mp'), may hold values from -4 to 4
- up_weight: bfloat16 [1024, 4096], P(None, 'mp'), may hold values from -0.1875 to 0.1875
- down_weight: bfloat16 [4096, 1024], P('mp'), may hold values from -0.09375 to 0.09375
Outputs:
- blocks_out: bfloat16 [4, 48, 96, 1024], P(None, 'lat', 'lon')
All inputs are finite; a program needn't handle non-finite values.
Results may differ from a plain program's by a relative error of at most 0.024.
Values may be sent and summed in bfloat16 or wider, within the bound.
No kernel may reach another device: no remote copies, remote signals or barrier semaphores. Data moves between devices by JAX's collectives and lax.ppermute only.
A program may use at most 64 MiB of HBM per device.

v0:
```python
import jax
import jax.numpy as jnp
from jax import lax
from jax.sharding import PartitionSpec as P

WL = 2
WY = 6
WX = 12
SL = 1
SY = 3
SX = 6


NEG = -1000000000.0
HIGH = lax.Precision.HIGHEST


def from_behind(value, axis, steps):
    count = lax.axis_size(axis)
    pairs = [(source, (source + steps) % count) for source in range(count)]
    return lax.ppermute(value, axis, pairs)


def normalize(values):
    floats = values.astype(jnp.float32)
    center = floats - jnp.mean(floats, axis=-1, keepdims=True)
    spread = jnp.mean(center * center, axis=-1, keepdims=True)
    return (center * lax.rsqrt(spread + 1e-05)).astype(jnp.bfloat16)


def to_windows(values):
    levels, rows, cols, width = values.shape
    blocks = values.reshape(levels // WL, WL, rows // WY, WY, cols // WX, WX, width)
    return blocks.transpose(0, 2, 4, 1, 3, 5, 6).reshape(-1, WL * WY * WX, width)


def from_windows(windows, levels, rows, cols):
    width = windows.shape[-1]
    blocks = windows.reshape(levels // WL, rows // WY, cols // WX, WL, WY, WX, width)
    return blocks.transpose(0, 3, 1, 4, 2, 5, 6).reshape(levels, rows, cols, width)


def bias_matrix(table):
    index = jnp.arange(WL * WY * WX)
    level = index // (WY * WX)
    row_pos = index // WX % WY
    col_pos = index % WX
    offset = 0
    result = jnp.zeros((table.shape[0], WL * WY * WX, WL * WY * WX), jnp.float32)
    for coord, extent in ((level, WL), (row_pos, WY), (col_pos, WX)):
        span = 2 * extent - 1
        delta = coord[:, None] - coord[None, :] + extent - 1
        onehot = (delta[:, :, None] == jnp.arange(span)[None, None, :]).astype(jnp.float32)
        result = result + jnp.einsum(
            "hk,ijk->hij", table[:, offset : offset + span], onehot, precision=HIGH
        )
        offset += span
    return result


def attend(packed, table, allowed):
    count, size, triple = packed.shape
    heads = table.shape[0]
    width = triple // 3
    split = packed.reshape(count, size, 3, heads, width // heads)
    query, key_part, value = (split[:, :, 0], split[:, :, 1], split[:, :, 2])
    scores = jnp.einsum("wihd,wjhd->whij", query, key_part, preferred_element_type=jnp.float32)
    scores = scores * (width // heads) ** (-0.5) + bias_matrix(table)[None]
    if allowed is not None:
        scores = jnp.where(allowed[:, None], scores, NEG)
    peak = jnp.max(scores, axis=-1, keepdims=True)
    expo = jnp.exp(scores - peak)
    probs = (expo / jnp.sum(expo, axis=-1, keepdims=True)).astype(jnp.bfloat16)
    mixed = jnp.einsum("whij,wjhd->wihd", probs, value, preferred_element_type=jnp.float32)
    return mixed.astype(jnp.bfloat16).reshape(count, size, width)


def region_allowed(levels, rows, cols):
    total_rows = rows * lax.axis_size("lat")
    lev_coord = jnp.arange(levels)
    row_coord = lax.axis_index("lat") * rows + jnp.arange(rows)
    lev_region = (lev_coord >= levels - WL).astype(jnp.int32) + (lev_coord >= levels - SL).astype(
        jnp.int32
    )
    row_region = (row_coord >= total_rows - WY).astype(jnp.int32) + (
        row_coord >= total_rows - SY
    ).astype(jnp.int32)
    ident = lev_region[:, None] * 3 + row_region[None, :]
    ident = jnp.broadcast_to(ident[:, :, None, None], (levels, rows, cols, 1))
    flat = to_windows(ident)[:, :, 0]
    return flat[:, :, None] == flat[:, None, :]


def roll_forward(values):
    values = jnp.roll(values, -SL, axis=0)
    upper = from_behind(values[:, :SY], "lat", -1)
    values = jnp.concatenate([values[:, SY:], upper], axis=1)
    right = from_behind(values[:, :, :SX], "lon", -1)
    return jnp.concatenate([values[:, :, SX:], right], axis=2)


def roll_back(values):
    left = from_behind(values[:, :, -SX:], "lon", 1)
    values = jnp.concatenate([left, values[:, :, :-SX]], axis=2)
    upper = from_behind(values[:, -SY:], "lat", 1)
    values = jnp.concatenate([upper, values[:, :-SY]], axis=1)
    return jnp.roll(values, SL, axis=0)


def reduce_rows(terms):
    return lax.psum(terms.astype(jnp.bfloat16), "mp")


def project_qkv(normed, weight):
    levels, rows, cols, width = normed.shape
    packed = jnp.dot(
        normed.reshape(-1, width), weight.reshape(width, -1), preferred_element_type=jnp.float32
    )
    return packed.astype(jnp.bfloat16).reshape(levels, rows, cols, -1)


def add_branch(residual, branch):
    return (residual.astype(jnp.float32) + branch.astype(jnp.float32)).astype(jnp.bfloat16)


def body(tokens, qkv_first, qkv_second, out_first, out_second, rel_tables, up_weight, down_weight):
    levels, rows, cols, width = tokens.shape
    count = levels * rows * cols
    packed = project_qkv(normalize(tokens), qkv_first)
    mixed = from_windows(attend(to_windows(packed), rel_tables[0], None), levels, rows, cols)
    branch = reduce_rows(
        jnp.dot(mixed.reshape(count, -1), out_first, preferred_element_type=jnp.float32)
    )
    first = add_branch(tokens.reshape(count, width), branch)
    normed = normalize(first).reshape(levels, rows, cols, width)
    allowed = region_allowed(levels, rows, cols)
    packed = project_qkv(roll_forward(normed), qkv_second)
    mixed = from_windows(attend(to_windows(packed), rel_tables[1], allowed), levels, rows, cols)
    branch = reduce_rows(
        jnp.dot(mixed.reshape(count, -1), out_second, preferred_element_type=jnp.float32)
    )
    branch = roll_back(branch.reshape(levels, rows, cols, width)).reshape(count, width)
    second = add_branch(first, branch)
    hidden = jax.nn.gelu(
        jnp.dot(normalize(second), up_weight, preferred_element_type=jnp.float32), approximate=False
    )
    hidden = hidden.astype(jnp.bfloat16)
    branch = reduce_rows(jnp.dot(hidden, down_weight, preferred_element_type=jnp.float32))
    return add_branch(second, branch).reshape(levels, rows, cols, width)


def solution(mesh):
    return jax.shard_map(
        body,
        mesh=mesh,
        in_specs=(
            P(None, "lat", "lon", None),
            P(None, None, "mp"),
            P(None, None, "mp"),
            P("mp", None),
            P("mp", None),
            P(None, "mp", None),
            P(None, "mp"),
            P("mp", None),
        ),
        out_specs=P(None, "lat", "lon", None),
        check_vma=False,
    )
```

profile of v0, /device:TPU:1, one launch (start us, length us, event | category | flops | bytes accessed | tf_op | source)
XLA Modules:
  0.0 278.5 jit_solution(18261302311826503748)
XLA Ops:
  9.5 1.5 fusion.22
  14.6 2.7 copy.23
  17.2 2.9 %convolution_convert_fusion.4 = bf16[288,768]{1,0:T(8,128)(2,1)} fusion(bf16[288,1024]{1,0:T(8,128)(2,1)S(1)} %copy-done.13, bf16[1024,768]{0,1:T(8,128)(2,1)} %bitcast.72), kind=kOutput, calls=%fused_computation.34 | convolution fusion | flops 453206016 | bytes 2605056 | tf_op jit(solution)/shard_map/dot_general | solution.py:116
  20.1 2.6 reshape_reshape_transpose_reshape_reshape.12
  22.7 2.3 fusion.153
  26.2 1.9 copy.42
  28.0 2.3 fusion.16
  30.3 1.5 fusion.156
  33.0 2.0 fusion.41
  35.5 2.2 convolution_convert_fusion.2
  39.4 2.5 reshape.286
  44.5 40.8 %all-reduce.4.cloned.1.call-done = bf16[288,1024]{1,0:T(8,128)(2,1)} async-done(((bf16[288,1024]{1,0:T(8,128)(2,1)}), bf16[288,1024]{1,0:T(8,128)(2,1)}) %all-reduce.4.cloned.1.call-update) | async-done | bytes 589840 | tf_op jit(solution)/shard_map/psum | solution.py:111
  85.2 1.6 convert_reduce_fusion.1
  90.2 1.6 slice.98
  92.9 3.1 %collective-permute-start = (bf16[4,3,12,1024]{3,2,1,0:T(8,128)(2,1)S(1)}, bf16[4,3,12,1024]{3,2,1,0:T(8,128)(2,1)S(1)}, u32[]{:S(2)}, u32[]{:S(2)}) collective-permute-start(bf16[4,3,12,1024]{3,2,1,0:T(8,128)(2,1)S(1)} %get-tuple-element.20), channel_id=1, source_target_pairs={{0,224},{32,0},{64,32},{96,64},{128,96},{160,128},{192,160},{224,1... | collective-permute-start | bytes 884744 | tf_op jit(solution)/shard_map/ppermute | solution.py:21
  97.5 6.9 %collective-permute-done = bf16[4,3,12,1024]{3,2,1,0:T(8,128)(2,1)S(1)} collective-permute-done((bf16[4,3,12,1024]{3,2,1,0:T(8,128)(2,1)S(1)}, bf16[4,3,12,1024]{3,2,1,0:T(8,128)(2,1)S(1)}, u32[]{:S(2)}, u32[]{:S(2)}) %collective-permute-start) | collective-permute-done | bytes 294944 | tf_op jit(solution)/shard_map/ppermute | solution.py:21
  105.4 4.6 %collective-permute-start.1 = (bf16[4,6,6,1024]{3,2,1,0:T(8,128)(2,1)}, bf16[4,6,6,1024]{3,2,1,0:T(8,128)(2,1)}, u32[]{:S(2)}, u32[]{:S(2)}) collective-permute-start(bf16[4,6,6,1024]{3,2,1,0:T(8,128)(2,1)} %get-tuple-element.18), channel_id=1, source_target_pairs={{0,28},{4,0},{8,4},{12,8},{16,12},{20,16},{24,20},{28,24},{1,29},{... | collective-permute-start | bytes 884744 | tf_op jit(solution)/shard_map/ppermute | solution.py:21
  110.1 2.6 copy.30
  114.7 3.0 %collective-permute-done.1 = bf16[4,6,6,1024]{3,2,1,0:T(8,128)(2,1)} collective-permute-done((bf16[4,6,6,1024]{3,2,1,0:T(8,128)(2,1)}, bf16[4,6,6,1024]{3,2,1,0:T(8,128)(2,1)}, u32[]{:S(2)}, u32[]{:S(2)}) %collective-permute-start.1) | collective-permute-done | bytes 294944 | tf_op jit(solution)/shard_map/ppermute | solution.py:21
  120.1 2.3 convolution_convert_fusion.3
  123.8 2.3 fusion.152
  127.2 1.9 copy.45
  132.6 2.0 fusion.42
  137.6 47.3 %all-reduce.6.cloned.1.call-done = bf16[4,6,12,1024]{3,2,1,0:T(8,128)(2,1)} async-done(((bf16[4,6,12,1024]{3,2,1,0:T(8,128)(2,1)}), bf16[4,6,12,1024]{3,2,1,0:T(8,128)(2,1)}) %all-reduce.6.cloned.1.call-update) | async-done | bytes 589840 | tf_op jit(solution)/shard_map/psum | solution.py:111
  187.6 13.0 %collective-permute-done.2 = bf16[4,6,6,1024]{3,2,1,0:T(8,128)(2,1)S(1)} collective-permute-done((bf16[4,6,6,1024]{3,2,1,0:T(8,128)(2,1)S(1)}, bf16[4,6,6,1024]{3,2,1,0:T(8,128)(2,1)S(1)}, u32[]{:S(2)}, u32[]{:S(2)}) %collective-permute-start.2) | collective-permute-done | bytes 294944 | tf_op jit(solution)/shard_map/ppermute | solution.py:21
  200.7 1.6 collective-permute-start.3
  202.3 10.3 %collective-permute-done.3 = bf16[4,3,12,1024]{3,2,1,0:T(8,128)(2,1)S(1)} collective-permute-done((bf16[4,3,12,1024]{3,2,1,0:T(8,128)(2,1)S(1)}, bf16[4,3,12,1024]{3,2,1,0:T(8,128)(2,1)S(1)}, u32[]{:S(2)}, u32[]{:S(2)}) %collective-permute-start.3) | collective-permute-done | bytes 294944 | tf_op jit(solution)/shard_map/ppermute | solution.py:21
  213.9 2.5 reshape.287
  216.4 1.5 convert_reduce_fusion
  218.2 6.2 %convolution_convert_fusion = bf16[288,1024]{1,0:T(8,128)(2,1)} fusion(bf16[1024,1024]{1,0:T(8,128)(2,1)S(1)} %copy-done, bf16[1024,1024]{1,0:T(8,128)(2,1)} %param.14, bf16[288,1024]{1,0:T(8,128)(2,1)S(1)} %get-tuple-element.6, f32[288]{0:T(512)S(1)} %add_rsqrt_fusion.1, f32[288]{0:T(512)S(1)} %broadcast_multiply_fusion.1), kind=kOutput, calls=%fused_computation.30 | convolution fusion | flops 1228603392 | bytes 5376256 | tf_op jit(solution)/shard_map/dot_general | solution.py:148
  224.5 42.8 %all-reduce.8.cloned.1.call-done = bf16[288,1024]{1,0:T(8,128)(2,1)} async-done(((bf16[288,1024]{1,0:T(8,128)(2,1)}), bf16[288,1024]{1,0:T(8,128)(2,1)}) %all-reduce.8.cloned.1.call-update) | async-done | bytes 589840 | tf_op jit(solution)/shard_map/psum | solution.py:111
  267.3 2.1 fusion.28
  (97 shorter events, 40.8 us)
Async XLA Ops:
  6.5 211.7 %copy-start = (bf16[1024,1024]{1,0:T(8,128)(2,1)S(1)}, bf16[1024,1024]{1,0:T(8,128)(2,1)}, u32[]{:S(2)}) copy-start(bf16[1024,1024]{1,0:T(8,128)(2,1)} %param.15) | copy-start | bytes 6291460
  6.5 78.7 %all-reduce.4.cloned.1.call-start = ((), (), s32[]{:S(2)}) async-start(), calls=%async_computation | async-start | bytes 1179648 | tf_op jit(solution)/shard_map/psum | solution.py:111
  7.5 1.3 copy-start.8
  7.6 1.2 copy-start.10
  7.7 1.8 copy-start.6
  9.5 2.6 copy-start.1
  14.6 2.7 copy-start.13
  22.7 5.3 %copy-start.3 = (f32[4,144,144]{1,2,0:T(8,128)S(1)}, f32[4,144,144]{1,2,0:T(8,128)}, u32[]{:S(2)}) copy-start(f32[4,144,144]{1,2,0:T(8,128)} %copy.27) | copy-start | bytes 995332
  37.7 147.2 %all-reduce.6.cloned.1.call-start = ((), (), s32[]{:S(2)}) async-start(), calls=%async_computation.1 | async-start | bytes 1572864 | tf_op jit(solution)/shard_map/psum | solution.py:111
  39.4 2.5 copy-start.9
  39.4 3.6 %copy-start.11 = (s32[144,144]{1,0:T(8,128)S(1)}, s32[144,144]{1,0:T(8,128)}, u32[]{:S(2)}) copy-start(s32[144,144]{1,0:T(8,128)} %copy-done.10) | copy-start | bytes 248836
  91.8 4.2 %copy-start.4 = (f32[144,144,4]{1,2,0:T(4,128)S(1)}, f32[144,144,4]{1,2,0:T(4,128)}, u32[]{:S(2)}) copy-start(f32[144,144,4]{1,2,0:T(4,128)} %convolution_add_fusion) | copy-start | bytes 995332
  91.8 4.2 %copy-start.7 = (s32[144,144]{1,0:T(8,128)S(1)}, s32[144,144]{1,0:T(8,128)}, u32[]{:S(2)}) copy-start(s32[144,144]{1,0:T(8,128)} %copy-done.6) | copy-start | bytes 248836
  92.9 11.5 %collective-permute-start = (bf16[4,3,12,1024]{3,2,1,0:T(8,128)(2,1)S(1)}, bf16[4,3,12,1024]{3,2,1,0:T(8,128)(2,1)S(1)}, u32[]{:S(2)}, u32[]{:S(2)}) collective-permute-start(bf16[4,3,12,1024]{3,2,1,0:T(8,128)(2,1)S(1)} %get-tuple-element.20), channel_id=1, source_target_pairs={{0,224},{32,0},{64,32},{96,64},{128,96},{160,128},{192,160},{224,1... | collective-permute-start | bytes 884744 | tf_op jit(solution)/shard_map/ppermute | solution.py:21
  105.4 12.3 %collective-permute-start.1 = (bf16[4,6,6,1024]{3,2,1,0:T(8,128)(2,1)}, bf16[4,6,6,1024]{3,2,1,0:T(8,128)(2,1)}, u32[]{:S(2)}, u32[]{:S(2)}) collective-permute-start(bf16[4,6,6,1024]{3,2,1,0:T(8,128)(2,1)} %get-tuple-element.18), channel_id=1, source_target_pairs={{0,28},{4,0},{8,4},{12,8},{16,12},{20,16},{24,20},{28,24},{1,29},{... | collective-permute-start | bytes 884744 | tf_op jit(solution)/shard_map/ppermute | solution.py:21
  123.8 5.3 %copy-start.5 = (f32[4,144,144]{1,2,0:T(8,128)S(1)}, f32[4,144,144]{1,2,0:T(8,128)}, u32[]{:S(2)}) copy-start(f32[4,144,144]{1,2,0:T(8,128)} %copy.34) | copy-start | bytes 995332
  130.4 1.0 copy-start.2
  131.5 1.0 copy-start.12
  137.6 129.8 %all-reduce.8.cloned.1.call-start = ((), (), s32[]{:S(2)}) async-start(), calls=%async_computation.2 | async-start | bytes 1179648 | tf_op jit(solution)/shard_map/psum | solution.py:111
  186.3 14.3 %collective-permute-start.2 = (bf16[4,6,6,1024]{3,2,1,0:T(8,128)(2,1)S(1)}, bf16[4,6,6,1024]{3,2,1,0:T(8,128)(2,1)S(1)}, u32[]{:S(2)}, u32[]{:S(2)}) collective-permute-start(bf16[4,6,6,1024]{3,2,1,0:T(8,128)(2,1)S(1)} %get-tuple-element.16), channel_id=1, source_target_pairs={{0,4},{4,8},{8,12},{12,16},{16,20},{20,24},{24,28},{28,0},{1,5},{5... | collective-permute-start | bytes 884744 | tf_op jit(solution)/shard_map/ppermute | solution.py:21
  200.7 11.8 %collective-permute-start.3 = (bf16[4,3,12,1024]{3,2,1,0:T(8,128)(2,1)S(1)}, bf16[4,3,12,1024]{3,2,1,0:T(8,128)(2,1)S(1)}, u32[]{:S(2)}, u32[]{:S(2)}) collective-permute-start(bf16[4,3,12,1024]{3,2,1,0:T(8,128)(2,1)S(1)} %fusion.86), channel_id=1, source_target_pairs={{0,32},{32,64},{64,96},{96,128},{128,160},{160,192},{192,224},{224... | collective-permute-start | bytes 884744 | tf_op jit(solution)/shard_map/ppermute | solution.py:21
Sparse Core Ops, SparseCore 0:
  37.9 47.3 all-reduce.3
  137.7 47.1 all-reduce.5
  224.6 42.6 all-reduce.7
where the time goes:
time: 280 us; the launch traced here: 278 us
  waiting for transfers between devices  164 us (59%)
  local copies, waits for them, and re-layouts  46 us (16%)
  matrix products  31.4 us (11%)
  between operations  13.5 us (5%)
  other arithmetic  12.7 us (5%)
  starting transfers between devices  10.8 us (4%)
    psum x3, waiting for transfers between devices, reduce_rows(): return lax.psum(terms.astype(jnp.bfloat16), 'mp')  131 us
    ppermute x4, waiting for transfers between devices, from_behind(): return lax.ppermute(value, axis, pairs)  33.1 us
    unnamed x37, local copies, waits for them, and re-layouts  15.5 us
    ppermute x4, starting transfers between devices, from_behind(): return lax.ppermute(value, axis, pairs)  10.5 us
    dot_general x6, matrix products, bias_matrix(): jnp.einsum('hk,ijk->hij', table[:, offset:offset + span], onehot, precisi...  7.24 us
    dot_general x1, matrix products, body(): jnp.dot(hidden, down_weight, preferred_element_type=jnp.float32)  6.25 us
  transfers between devices with their start and end apart: 7, of which 7 were waited for; matrix products, arithmetic and copies ran while one was open for 5% of the time, Pallas kernels for 0%

commit v1 on v0

v1 whole, which is shorter than its diff:
```python
import functools

import jax
import jax.numpy as jnp
import numpy as np
from jax import lax
from jax.experimental import pallas as pl
from jax.experimental.pallas import tpu as pltpu
from jax.sharding import PartitionSpec as P

WL = 2
WY = 6
WX = 12
SY = 3
SX = 6
HD = 64
NEG = -1000000000.0
AXES = ("lat", "lon", "mp")
MIB = 1024 * 1024

USED = 36
ROWS = 40
KEPT = 4 * ROWS
FEAT = 32
F_Y = 4
F_X = 10
F_PAD = 22


def quadrant_start(q):
    return (3, 0, 3, 0)[q], (6, 6, 0, 0)[q]


def build_constants():
    tokens = 4 * WY * WX
    select = np.zeros((2, KEPT, tokens), np.float32)
    for core in range(2):
        levels = (1, 2) if core == 0 else (3, 0)
        for q in range(4):
            y0, x0 = quadrant_start(q)
            row = q * ROWS
            for level in levels:
                for y in range(3):
                    for x in range(6):
                        select[core, row, (level * WY + y0 + y) * WX + x0 + x] = 1.0
                        row += 1
    flat = np.zeros((tokens, FEAT), np.float32)
    for t in range(tokens):
        flat[t, t // (WY * WX)] = 1.0
        flat[t, F_Y + t // WX % WY] = 1.0
        flat[t, F_X + t % WX] = 1.0
    rolled = np.zeros((KEPT, FEAT), np.float32)
    level_ban = np.zeros((KEPT, 128), np.float32)
    row_ban = np.zeros((KEPT, 128), np.float32)
    for q in range(4):
        for s in range(ROWS):
            i = q * ROWS + s
            if s >= USED:
                rolled[i, F_PAD] = 1.0
                continue
            level, y, x = s // 18, s // 6 % 3 + 3 * (q % 2), s % 6 + 6 * (q // 2)
            rolled[i, level] = 1.0
            rolled[i, F_Y + y] = 1.0
            rolled[i, F_X + x] = 1.0
            for half in (0, 64):
                level_ban[i, half + 1 - level] = NEG
                for other in range(WY):
                    if (other < 3) != (y < 3):
                        row_ban[i, half + F_Y + other] = NEG
    index = np.full((2, FEAT, FEAT), 37, np.int64)
    for block in range(2):
        for i in range(4):
            for j in range(4):
                near = i // 2 == j // 2
                index[block, i, j] = i - j + 1 if near else 38
            index[block, i, F_PAD] = 38
        for i in range(WY):
            for j in range(WY):
                index[block, F_Y + i, F_Y + j] = 3 + i - j + 5
        for i in range(WX):
            for j in range(WX):
                index[block, F_X + i, F_X + j] = 14 + i - j + 11
    pick = (index.reshape(2, 1, -1) == np.arange(39).reshape(1, 39, 1)).astype(np.float32)
    return {
        "select": select.astype(jnp.bfloat16),
        "place": select.transpose(0, 2, 1).astype(jnp.bfloat16),
        "flat": np.tile(flat, (1, 4)).astype(jnp.bfloat16),
        "rolled": np.tile(rolled, (1, 4)).astype(jnp.bfloat16),
        "level_ban": level_ban,
        "row_ban": row_ban,
        "pick": pick,
    }


def pairs(counts, target):
    lats, lons, mps = counts
    result = []
    for a in range(lats):
        for b in range(lons):
            for m in range(mps):
                ta, tb, tm = target(a, b, m)
                dest = ((ta % lats) * lons + tb % lons) * mps + tm
                result.append(((a * lons + b) * mps + m, dest))
    return result


def dot(left, right):
    return jnp.dot(left, right, preferred_element_type=jnp.float32)


def dot_t(left, right):
    return lax.dot_general(left, right, (((1,), (1,)), ((), ())), preferred_element_type=jnp.float32)


def normalize(floats):
    center = floats - jnp.mean(floats, axis=-1, keepdims=True)
    spread = jnp.mean(center * center, axis=-1, keepdims=True)
    return (center * lax.rsqrt(spread + 1e-05)).astype(jnp.bfloat16)


def four_heads(xq, xk, weight, extra, key_feat):
    query = (dot(xq, weight[:, :256]) * HD**-0.5).astype(jnp.bfloat16)
    rest = dot(xk, weight[:, 256:]).astype(jnp.bfloat16)
    results = []
    for pair in range(2):
        cols = slice(pair * 128, pair * 128 + 128)
        q, k, v = query[:, cols], rest[:, cols], rest[:, 256 + pair * 128 : 384 + pair * 128]
        e = extra[:, cols]
        low_q = lax.broadcasted_iota(jnp.int32, q.shape, 1) < HD
        low_k = lax.broadcasted_iota(jnp.int32, k.shape, 1) < HD
        outs = []
        for head in range(2):
            mine_q, mine_k = (low_q, low_k) if head == 0 else (~low_q, ~low_k)
            scores = dot_t(jnp.where(mine_q, q, e), jnp.where(mine_k, k, key_feat))
            expo = jnp.exp(scores - jnp.max(scores, axis=-1, keepdims=True))
            probs = (expo / jnp.sum(expo, axis=-1, keepdims=True)).astype(jnp.bfloat16)
            outs.append(dot(probs, v))
        results.append(jnp.where(low_q, outs[0], outs[1]).astype(jnp.bfloat16))
    return results


def core_index():
    return lax.rem(lax.axis_index("mp"), 2)


def first_kernel(tokens, weight, bias, select, flat, *refs):
    out = refs[-1]
    pick = select[core_index()]
    xk = normalize(tokens[...].astype(jnp.float32))
    xq = dot(pick, xk).astype(jnp.bfloat16)
    feat = dot(pick, flat[...]).astype(jnp.bfloat16)
    extra = dot(feat[:, :FEAT], bias[...]).astype(jnp.bfloat16)
    heads = four_heads(xq, xk, weight[...], extra, flat[...])
    start = 0
    if len(refs) == 2:
        out[:, :256] = refs[0][...]
        start = 256
    out[:, start : start + 128] = heads[0]
    out[:, start + 128 : start + 256] = heads[1]


def projected(mine, other, w0, w1, w2, w3):
    total = dot(mine[:, :256], w0[...]) + dot(mine[:, 256:], w1[...])
    total = total + dot(other[:, :256], w2[...]) + dot(other[:, 256:], w3[...])
    return total.astype(jnp.bfloat16).astype(jnp.float32)


def residual_kernel(mine, other, w0, w1, w2, w3, tokens, select, *outs):
    base = dot(select[core_index()], tokens[...])
    first = base + projected(mine, other, w0, w1, w2, w3)
    for q in range(4):
        outs[q][...] = first[q * ROWS : (q + 1) * ROWS].astype(jnp.bfloat16)


def joined(pieces):
    return jnp.concatenate([p[...].astype(jnp.float32) for p in pieces], axis=0)


def second_kernel(p0, p1, p2, p3, w_own, w_sib, b_own, b_sib, rolled, level_ban, row_ban, out):
    xn = normalize(joined((p0, p1, p2, p3)))
    ban_levels = (core_index() == 1).astype(jnp.float32)
    ban_rows = (lax.axis_index("lat") == lax.axis_size("lat") - 1).astype(jnp.float32)
    ban = level_ban[...] * ban_levels + row_ban[...] * ban_rows
    ban = jnp.concatenate([ban, ban], axis=1)
    key_feat = rolled[...]
    for part, (weight, bias) in enumerate(((w_own, b_own), (w_sib, b_sib))):
        extra = (dot(key_feat[:, :FEAT], bias[...]) + ban).astype(jnp.bfloat16)
        heads = four_heads(xn, xn, weight[...], extra, key_feat)
        out[:, part * 256 : part * 256 + 128] = heads[0]
        out[:, part * 256 + 128 : part * 256 + 256] = heads[1]


def gelu(x):
    return 0.5 * x * (1.0 + lax.erf(x * np.float32(np.sqrt(0.5))))


def mlp_kernel(mine, other, w0, w1, w2, w3, p0, p1, p2, p3, u0, u1, d0, d1, *outs):
    second = joined((p0, p1, p2, p3)) + projected(mine, other, w0, w1, w2, w3)
    second = second.astype(jnp.bfloat16).astype(jnp.float32)
    xn = normalize(second)
    h0 = gelu(dot(xn, u0[...])).astype(jnp.bfloat16)
    h1 = gelu(dot(xn, u1[...])).astype(jnp.bfloat16)
    total = 0.5 * second + dot(h0, d0[...]) + dot(h1, d1[...])
    for q in range(4):
        outs[q][...] = total[q * ROWS : (q + 1) * ROWS].astype(jnp.bfloat16)


def sum_kernel(*refs):
    out = refs[-1]
    parts = []
    for q in range(4):
        parts.append(refs[2 * q][...].astype(jnp.float32) + refs[2 * q + 1][...].astype(jnp.float32))
    out[...] = jnp.concatenate(parts, axis=0).astype(jnp.bfloat16)


def place_kernel(mine, other, place, out):
    core = core_index()
    out[...] = (dot(place[core], mine[...]) + dot(place[1 - core], other[...])).astype(jnp.bfloat16)


def call(kernel, outs, operands, flops, limit):
    shapes = [jax.ShapeDtypeStruct(s, jnp.bfloat16) for s in outs]
    moved = sum(o.size * o.dtype.itemsize for o in operands) + sum(2 * s.size for s in shapes)
    vmem = pl.BlockSpec(memory_space=pltpu.VMEM)
    result = pl.pallas_call(
        kernel,
        out_shape=shapes,
        in_specs=[vmem] * len(operands),
        out_specs=[vmem] * len(shapes),
        compiler_params=pltpu.CompilerParams(vmem_limit_bytes=limit * MIB),
        cost_estimate=pl.CostEstimate(flops=flops, bytes_accessed=moved, transcendentals=0),
    )(*operands)
    return result if len(result) > 1 else result[0]


def bias_rows(tables, pick):
    heads = tables.shape[1]
    fill = jnp.broadcast_to(jnp.array([0.0, NEG], jnp.float32), (2, heads, 2))
    wide = jnp.concatenate([tables, fill], axis=2)
    rows = jnp.einsum("bhk,bkn->bhn", wide, pick, precision=lax.Precision.HIGHEST)
    high = lax.reduce_precision(rows, 8, 7)
    both = jnp.stack([high, rows - high], axis=2).astype(jnp.bfloat16)
    both = both.reshape(2, heads // 2, 2, 2, FEAT, FEAT)[:, :, ::-1]
    return both.transpose(0, 4, 1, 2, 3, 5).reshape(2, FEAT, heads * 2 * FEAT)


def body(counts, tokens, qkv_first, qkv_second, out_first, out_second, rel_tables, up_weight, down_weight):
    levels, rows, cols, width = tokens.shape
    count = levels * rows * cols
    consts = {name: jnp.asarray(value) for name, value in build_constants().items()}
    select, place = consts["select"], consts["place"]

    def move(value, target):
        return lax.ppermute(value, AXES, pairs(counts, target))

    def core_swap(value):
        return move(value, lambda a, b, m: (a, b, m ^ 1))

    def chip_swap(value):
        return move(value, lambda a, b, m: (a, b, m ^ 2))

    offsets = ((0, 0), (1, 0), (0, 1), (1, 1))
    turn = counts[1] // 2

    flat_tokens = tokens.reshape(count, width)
    wide_first = qkv_first.reshape(width, -1)
    wide_second = qkv_second.reshape(width, -1)

    of2 = chip_swap(out_first)
    of1 = core_swap(out_first)
    sib_first = core_swap(wide_first)
    bias = bias_rows(rel_tables, consts["pick"])
    sib_bias = core_swap(bias)

    part = call(
        first_kernel, [(KEPT, 256)], (flat_tokens, wide_first, bias[0], select, consts["flat"]), 10**9, 24
    )
    mixed = call(
        first_kernel,
        [(KEPT, 512)],
        (flat_tokens, sib_first, sib_bias[0], select, consts["flat"], part),
        10**9,
        24,
    )
    of3 = core_swap(of2)
    other = chip_swap(mixed)
    sib_second = core_swap(wide_second)
    os2 = chip_swap(out_second)
    os1 = core_swap(out_second)
    os3 = core_swap(os2)
    sib_up = core_swap(up_weight)
    sib_down = core_swap(down_weight)

    firsts = call(
        residual_kernel,
        [(ROWS, width)] * 4,
        (mixed, other, out_first, of1, of2, of3, flat_tokens, select),
        5 * 10**8,
        24,
    )
    shifted = [firsts[0]]
    for q in (1, 2, 3):
        dy, dx = offsets[q]

        def target(a, b, m, dy=dy, dx=dx):
            return a - dy, b - dx, m ^ 2 if dx and b % turn == 0 else m

        shifted.append(move(firsts[q], target))

    mixed = call(
        second_kernel,
        [(KEPT, 512)],
        (
            *shifted,
            wide_second,
            sib_second,
            bias[1],
            sib_bias[1],
            consts["rolled"],
            consts["level_ban"],
            consts["row_ban"],
        ),
        10**9,
        24,
    )
    other = chip_swap(mixed)
    partial = call(
        mlp_kernel,
        [(ROWS, width)] * 4,
        (mixed, other, out_second, os1, os2, os3, *shifted, up_weight, sib_up, down_weight, sib_down),
        2 * 10**9,
        40,
    )
    terms = []
    for q in (3, 2, 1, 0):
        dy, dx = offsets[q]
        far = move(partial[q], lambda a, b, m, dy=dy, dx=dx: (a + dy, b + dx, m ^ 2))
        near = move(partial[q], lambda a, b, m, dy=dy, dx=dx: (a + dy, b + dx, m)) if q else partial[q]
        terms = [near, far] + terms
    done = call(sum_kernel, [(KEPT, width)], terms, 10**6, 16)
    result = call(place_kernel, [(count, width)], (done, core_swap(done), place), 2 * 10**8, 16)
    return result.reshape(levels, rows, cols, width)


def solution(mesh):
    counts = tuple(mesh.shape[name] for name in AXES)
    return jax.shard_map(
        functools.partial(body, counts),
        mesh=mesh,
        in_specs=(
            P(None, "lat", "lon", None),
            P(None, None, "mp"),
            P(None, None, "mp"),
            P("mp", None),
            P("mp", None),
            P(None, "mp", None),
            P(None, "mp"),
            P("mp", None),
        ),
        out_specs=P(None, "lat", "lon", None),
        check_vma=False,
    )
```

time: 280 us -> 113 us (0.40)
  waiting for transfers between devices: 164 us -> 32.4 us
  matrix products: 31.4 us -> 0.28 us
  starting transfers between devices: 10.8 us -> 38.5 us
  local copies, waits for them, and re-layouts: 46 us -> 20.7 us
  Pallas kernels: 0 us -> 20.2 us
  between operations: 13.5 us -> 0.31 us
  other arithmetic: 12.7 us -> 0.35 us
    psum x3 -> x0, waiting for transfers between devices: 131 us -> none  [reduce_rows(): return lax.psum(terms.astype(jnp.bfloat16), 'mp')]
    dot_general x15 -> x1, matrix products: 29.9 us -> 0.28 us  [bias_rows(): jnp.einsum('bhk,bkn->bhn', wide, pick, precision=lax.Precision.HIGHEST)]
    ppermute x4 -> x24, starting transfers between devices: 10.5 us -> 38.5 us  [move(): return lax.ppermute(value, AXES, pairs(counts, target))]
    pallas_call x0 -> x7, Pallas kernels: none -> 20.2 us  [call(): pl.pallas_call(kernel, out_shape=shapes, in_specs=[vmem] * len(operands),...]
    slice x8 -> x1, local copies, waits for them, and re-layouts: 9.35 us -> 0.73 us  [body(): bias[1]]
    convert_element_type x6 -> x0, local copies, waits for them, and re-layouts: 7 us -> none  [the longest x2 3.9 us: add_branch(): residual.astype(jnp.float32) + branch.astype(jnp.float32)]
    unnamed x37, local copies, waits for them, and re-layouts: 15.5 us -> 10 us
    reduce_sum x6 -> x0, other arithmetic: 4.62 us -> none  [the longest x3 3.45 us: normalize(): center = floats - jnp.mean(floats, axis=-1, keepdims=True)]
  transfers between devices with their start and end apart: 7 -> 24, of which waited for: 7 -> 11; matrix products, arithmetic and copies ran while one was open for 5% -> 11% of each run, Pallas kernels for 0% -> 12%
where the time goes in v1:
time: 113 us
  starting transfers between devices  38.5 us (34%)
  waiting for transfers between devices  32.4 us (29%)
  local copies, waits for them, and re-layouts  20.7 us (18%)
  Pallas kernels  20.2 us (18%)
    ppermute x24, starting transfers between devices, move(): return lax.ppermute(value, AXES, pairs(counts, target))  38.5 us
    ppermute x24, waiting for transfers between devices, move(): return lax.ppermute(value, AXES, pairs(counts, target))  32.4 us
    pallas_call x7, Pallas kernels, call(): pl.pallas_call(kernel, out_shape=shapes, in_specs=[vmem] * len(operands),...  20.2 us
    unnamed x37, local copies, waits for them, and re-layouts  10 us
  transfers between devices with their start and end apart: 24, of which 11 were waited for; matrix products, arithmetic and copies ran while one was open for 11% of the time, Pallas kernels for 12%

profile of v1, /device:TPU:1, one launch (start us, length us, event | category | flops | bytes accessed | tf_op | source)
XLA Modules:
  0.0 112.8 jit_solution(14927651828815701060)
XLA Ops:
  0.0 1.7 %copy.24 = bf16[1024,3,256]{0,2,1:T(8,128)(2,1)S(1)} copy(bf16[1024,3,256]{2,0,1:T(8,128)(2,1)} %param.17) | data formatting | bytes 3145728 | tf_op args[1]
  1.8 1.6 %copy.25.weight = bf16[1024,768]{1,0:T(8,128)(2,1)} copy(bf16[1024,768]{0,1:T(8,128)(2,1)S(1)} %bitcast.9) | data formatting | bytes 3145728 | tf_op jit(solution)/shard_map/reshape | solution.py:266
  3.3 3.2 %collective-permute-start = (bf16[1024,768]{1,0:T(8,128)(2,1)}, bf16[1024,768]{1,0:T(8,128)(2,1)}, u32[]{:S(2)}, u32[]{:S(2)}) collective-permute-start(bf16[1024,768]{1,0:T(8,128)(2,1)} %copy.25.weight), channel_id=1, source_target_pairs={{0,1},{1,0},{2,3},{3,2},{4,5},{5,4},{6,7},{7,6},{8,9},{9,8},{10,11... | collective-permute-start | bytes 4718600 | tf_op jit(solution)/shard_map/ppermute | solution.py:254
  9.2 1.8 %copy.29 = bf16[1024,3,256]{0,2,1:T(8,128)(2,1)} copy(bf16[1024,3,256]{2,0,1:T(8,128)(2,1)S(1)} %copy-done.13) | data formatting | bytes 3145728 | tf_op args[2]
  11.1 1.8 %copy.31.w_own = bf16[1024,768]{1,0:T(8,128)(2,1)S(1)} copy(bf16[1024,768]{0,1:T(8,128)(2,1)} %bitcast.10) | data formatting | bytes 3145728 | tf_op jit(solution)/shard_map/reshape | solution.py:267
  13.4 6.7 %collective-permute-done.4.w2 = bf16[256,1024]{1,0:T(8,128)(2,1)S(1)} collective-permute-done((bf16[256,1024]{1,0:T(8,128)(2,1)S(1)}, bf16[256,1024]{1,0:T(8,128)(2,1)S(1)}, u32[]{:S(2)}, u32[]{:S(2)}) %collective-permute-start.4) | collective-permute-done | bytes 524320 | tf_op jit(solution)/shard_map/ppermute | solution.py:254
  20.9 1.5 %collective-permute-done.3.w1 = bf16[256,1024]{1,0:T(8,128)(2,1)S(1)} collective-permute-done((bf16[256,1024]{1,0:T(8,128)(2,1)S(1)}, bf16[256,1024]{1,0:T(8,128)(2,1)S(1)}, u32[]{:S(2)}, u32[]{:S(2)}) %collective-permute-start.3) | collective-permute-done | bytes 524320 | tf_op jit(solution)/shard_map/ppermute | solution.py:254
  24.0 1.0 squeeze.13.bias
  25.0 2.2 %copy.23 = bf16[4,6,12,1024]{3,2,1,0:T(8,128)(2,1)} copy(bf16[4,6,12,1024]{3,0,2,1:T(4,128)(2,1)} %param.16) | data formatting | bytes 1179648 | tf_op args[0]
  27.1 1.3 %reshape.26.tokens = bf16[288,1024]{1,0:T(8,128)(2,1)S(1)} reshape(bf16[4,6,12,1024]{3,2,1,0:T(8,128)(2,1)} %copy.23) | data formatting | bytes 1179648 | tf_op jit(solution)/shard_map/reshape | solution.py:265
  30.0 4.1 %shard_map.154.refs_0_ = bf16[160,256]{1,0:T(8,128)(2,1)S(1)} custom-call(bf16[288,1024]{1,0:T(8,128)(2,1)S(1)} %reshape.26.tokens, bf16[1024,768]{1,0:T(8,128)(2,1)} %copy.25.weight, bf16[32,256]{1,0:T(8,128)(2,1)S(1)} %squeeze.13.bias, bf16[2,160,288]{2,1,0:T(8,128)(2,1)S(1)} %copy-done.7, bf16[288,128]{1,0:T(8,128)(2,1)S(1)} %copy-done.11), custom_call_target="tpu_custom_call" | custom-call | flops 1000000000 | bytes 2519040 | tf_op jit(solution)/shard_map/pallas_call | solution.py:225
  34.9 4.2 %shard_map.155.mine = bf16[160,512]{1,0:T(8,128)(2,1)S(1)} custom-call(bf16[288,1024]{1,0:T(8,128)(2,1)S(1)} %reshape.26.tokens, bf16[1024,768]{1,0:T(8,128)(2,1)} %collective-permute-done.weight, bf16[32,256]{1,0:T(8,128)(2,1)S(1)} %get-tuple-element.24.bias, bf16[2,160,288]{2,1,0:T(8,128)(2,1)S(1)} %copy-done.7, bf16[288,128]{1,0:T(8,128)(2,1)S(1)} %copy-done.12, ...), custom_call_target="tpu_custom_call" | custom-call | flops 1000000000 | bytes 2682880 | tf_op jit(solution)/shard_map/pallas_call | solution.py:225
  39.1 1.7 %collective-permute-start.2 = (bf16[160,512]{1,0:T(8,128)(2,1)S(1)}, bf16[160,512]{1,0:T(8,128)(2,1)S(1)}, u32[]{:S(2)}, u32[]{:S(2)}) collective-permute-start(bf16[160,512]{1,0:T(8,128)(2,1)S(1)} %shard_map.155.mine), channel_id=1, source_target_pairs={{0,2},{1,3},{2,0},{3,1},{4,6},{5,7},{6,4},{7,5},{8,10},{9,11},{10,... | collective-permute-start | bytes 491528 | tf_op jit(solution)/shard_map/ppermute | solution.py:254
  41.2 4.1 %collective-permute-done.2.other = bf16[160,512]{1,0:T(8,128)(2,1)S(1)} collective-permute-done((bf16[160,512]{1,0:T(8,128)(2,1)S(1)}, bf16[160,512]{1,0:T(8,128)(2,1)S(1)}, u32[]{:S(2)}, u32[]{:S(2)}) %collective-permute-start.2) | collective-permute-done | bytes 163872 | tf_op jit(solution)/shard_map/ppermute | solution.py:254
  46.0 1.3 %shard_map.156 = (bf16[40,1024]{1,0:T(8,128)(2,1)S(1)}, bf16[40,1024]{1,0:T(8,128)(2,1)S(1)}, bf16[40,1024]{1,0:T(8,128)(2,1)S(1)}, bf16[40,1024]{1,0:T(8,128)(2,1)}) custom-call(bf16[160,512]{1,0:T(8,128)(2,1)S(1)} %shard_map.155.mine, bf16[160,512]{1,0:T(8,128)(2,1)S(1)} %collective-permute-done.2.other, bf16[256,1024]{1,0:T(8,128)(2,1)S(1)} %copy-done, ...), custom_call_target="tpu_custom_call" | custom-call | flops 500000000 | bytes 3526656 | tf_op jit(solution)/shard_map/pallas_call | solution.py:225
  47.4 5.0 %collective-permute-start.6 = (bf16[40,1024]{1,0:T(8,128)(2,1)S(1)}, bf16[40,1024]{1,0:T(8,128)(2,1)S(1)}, u32[]{:S(2)}, u32[]{:S(2)}) collective-permute-start(bf16[40,1024]{1,0:T(8,128)(2,1)S(1)} %get-tuple-element.14), channel_id=1, source_target_pairs={{0,224},{1,225},{2,226},{3,227},{4,228},{5,229},{6,230},{7,231},{8... | collective-permute-start | bytes 245768 | tf_op jit(solution)/shard_map/ppermute | solution.py:254
  52.4 1.9 %collective-permute-done.6.p1 = bf16[40,1024]{1,0:T(8,128)(2,1)S(1)} collective-permute-done((bf16[40,1024]{1,0:T(8,128)(2,1)S(1)}, bf16[40,1024]{1,0:T(8,128)(2,1)S(1)}, u32[]{:S(2)}, u32[]{:S(2)}) %collective-permute-start.6) | collective-permute-done | bytes 81952 | tf_op jit(solution)/shard_map/ppermute | solution.py:254
  54.3 4.3 %collective-permute-start.7 = (bf16[40,1024]{1,0:T(8,128)(2,1)S(1)}, bf16[40,1024]{1,0:T(8,128)(2,1)S(1)}, u32[]{:S(2)}, u32[]{:S(2)}) collective-permute-start(bf16[40,1024]{1,0:T(8,128)(2,1)S(1)} %get-tuple-element.15), channel_id=1, source_target_pairs={{0,30},{1,31},{2,28},{3,29},{4,0},{5,1},{6,2},{7,3},{8,4},{9,5},{1... | collective-permute-start | bytes 245768 | tf_op jit(solution)/shard_map/ppermute | solution.py:254
  58.5 1.5 %collective-permute-done.7.p2 = bf16[40,1024]{1,0:T(8,128)(2,1)S(1)} collective-permute-done((bf16[40,1024]{1,0:T(8,128)(2,1)S(1)}, bf16[40,1024]{1,0:T(8,128)(2,1)S(1)}, u32[]{:S(2)}, u32[]{:S(2)}) %collective-permute-start.7) | collective-permute-done | bytes 81952 | tf_op jit(solution)/shard_map/ppermute | solution.py:254
  60.0 8.3 %collective-permute-start.8 = (bf16[40,1024]{1,0:T(8,128)(2,1)}, bf16[40,1024]{1,0:T(8,128)(2,1)S(1)}, u32[]{:S(2)}, u32[]{:S(2)}) collective-permute-start(bf16[40,1024]{1,0:T(8,128)(2,1)} %get-tuple-element.16), channel_id=1, source_target_pairs={{0,254},{1,255},{2,252},{3,253},{4,224},{5,225},{6,226},{7,227},{8... | collective-permute-start | bytes 245768 | tf_op jit(solution)/shard_map/ppermute | solution.py:254
  68.3 1.0 squeeze.14.b_own
  72.6 3.9 %shard_map.157.mine = bf16[160,512]{1,0:T(8,128)(2,1)S(1)} custom-call(bf16[40,1024]{1,0:T(8,128)(2,1)S(1)} %get-tuple-element.13.p0, bf16[40,1024]{1,0:T(8,128)(2,1)S(1)} %collective-permute-done.6.p1, bf16[40,1024]{1,0:T(8,128)(2,1)S(1)} %collective-permute-done.7.p2, bf16[40,1024]{1,0:T(8,128)(2,1)S(1)} %collective-permute-done.8.p3, ...), custom_call_target="tpu_custom_call" | custom-call | flops 1000000000 | bytes 3874816 | tf_op jit(solution)/shard_map/pallas_call | solution.py:225
  76.7 4.1 %collective-permute-done.10.other = bf16[160,512]{1,0:T(8,128)(2,1)S(1)} collective-permute-done((bf16[160,512]{1,0:T(8,128)(2,1)S(1)}, bf16[160,512]{1,0:T(8,128)(2,1)S(1)}, u32[]{:S(2)}, u32[]{:S(2)}) %collective-permute-start.10) | collective-permute-done | bytes 163872 | tf_op jit(solution)/shard_map/ppermute | solution.py:254
  80.8 6.2 %shard_map.158 = (bf16[40,1024]{1,0:T(8,128)(2,1)S(1)}, bf16[40,1024]{1,0:T(8,128)(2,1)S(1)}, bf16[40,1024]{1,0:T(8,128)(2,1)S(1)}, bf16[40,1024]{1,0:T(8,128)(2,1)S(1)}) custom-call(bf16[160,512]{1,0:T(8,128)(2,1)S(1)} %shard_map.157.mine, bf16[160,512]{1,0:T(8,128)(2,1)S(1)} %collective-permute-done.10.other, bf16[256,1024]{1,0:T(8,128)(2,1)S(1)} %copy-done.1, ...), custom_call_target="tpu_custom_call" | custom-call | flops 2000000000 | bytes 11468800 | tf_op jit(solution)/shard_map/pallas_call | solution.py:225
  87.4 2.9 %collective-permute-done.16.refs_1_ = bf16[40,1024]{1,0:T(8,128)(2,1)S(1)} collective-permute-done((bf16[40,1024]{1,0:T(8,128)(2,1)S(1)}, bf16[40,1024]{1,0:T(8,128)(2,1)S(1)}, u32[]{:S(2)}, u32[]{:S(2)}) %collective-permute-start.16) | collective-permute-done | bytes 81952 | tf_op jit(solution)/shard_map/ppermute | solution.py:254
  90.4 3.8 %collective-permute-start.21 = (bf16[40,1024]{1,0:T(8,128)(2,1)S(1)}, bf16[40,1024]{1,0:T(8,128)(2,1)S(1)}, u32[]{:S(2)}, u32[]{:S(2)}) collective-permute-start(bf16[40,1024]{1,0:T(8,128)(2,1)S(1)} %get-tuple-element.20), channel_id=1, source_target_pairs={{0,36},{1,37},{2,38},{3,39},{4,40},{5,41},{6,42},{7,43},{8,44},{9,... | collective-permute-start | bytes 245768 | tf_op jit(solution)/shard_map/ppermute | solution.py:254
  94.1 1.2 %collective-permute-start.22 = (bf16[40,1024]{1,0:T(8,128)(2,1)S(1)}, bf16[40,1024]{1,0:T(8,128)(2,1)S(1)}, u32[]{:S(2)}, u32[]{:S(2)}) collective-permute-start(bf16[40,1024]{1,0:T(8,128)(2,1)S(1)} %get-tuple-element.20), channel_id=1, source_target_pairs={{0,38},{1,39},{2,36},{3,37},{4,42},{5,43},{6,40},{7,41},{8,46},{9,... | collective-permute-start | bytes 245768 | tf_op jit(solution)/shard_map/ppermute | solution.py:254
  95.3 4.1 %collective-permute-done.21.refs_6_ = bf16[40,1024]{1,0:T(8,128)(2,1)S(1)} collective-permute-done((bf16[40,1024]{1,0:T(8,128)(2,1)S(1)}, bf16[40,1024]{1,0:T(8,128)(2,1)S(1)}, u32[]{:S(2)}, u32[]{:S(2)}) %collective-permute-start.21) | collective-permute-done | bytes 81952 | tf_op jit(solution)/shard_map/ppermute | solution.py:254
  99.4 3.4 %collective-permute-done.22.refs_7_ = bf16[40,1024]{1,0:T(8,128)(2,1)S(1)} collective-permute-done((bf16[40,1024]{1,0:T(8,128)(2,1)S(1)}, bf16[40,1024]{1,0:T(8,128)(2,1)S(1)}, u32[]{:S(2)}, u32[]{:S(2)}) %collective-permute-start.22) | collective-permute-done | bytes 81952 | tf_op jit(solution)/shard_map/ppermute | solution.py:254
  102.9 6.8 %collective-permute-start.23 = (bf16[160,1024]{1,0:T(8,128)(2,1)S(1)}, bf16[160,1024]{1,0:T(8,128)(2,1)S(1)}, u32[]{:S(2)}, u32[]{:S(2)}) collective-permute-start(bf16[160,1024]{1,0:T(8,128)(2,1)S(1)} %shard_map.159.mine), channel_id=1, source_target_pairs={{0,1},{1,0},{2,3},{3,2},{4,5},{5,4},{6,7},{7,6},{8,9},{9,8},{10,11... | collective-permute-start | bytes 983048 | tf_op jit(solution)/shard_map/ppermute | solution.py:254
  109.7 1.3 %collective-permute-done.23.other = bf16[160,1024]{1,0:T(8,128)(2,1)S(1)} collective-permute-done((bf16[160,1024]{1,0:T(8,128)(2,1)S(1)}, bf16[160,1024]{1,0:T(8,128)(2,1)S(1)}, u32[]{:S(2)}, u32[]{:S(2)}) %collective-permute-start.23) | collective-permute-done | bytes 327712 | tf_op jit(solution)/shard_map/ppermute | solution.py:254
  111.6 1.3 %copy.32 = bf16[4,6,12,1024]{3,0,2,1:T(4,128)(2,1)} copy(bf16[4,6,12,1024]{3,2,1,0:T(8,128)(2,1)S(1)} %reshape.30) | data formatting | bytes 1179648 | tf_op jit(solution)/shard_map/reshape | solution.py:342
  (78 shorter events, 13.6 us)
Async XLA Ops:
  1.7 4.9 %copy-start.14 = (f32[2,39,1024]{2,1,0:T(8,128)S(1)}, f32[2,39,1024]{2,1,0:T(8,128)}, u32[]{:S(2)}) copy-start(f32[2,39,1024]{2,1,0:T(8,128)} %constant.22.clone) | copy-start | bytes 958468
  1.8 4.9 %copy-start.15 = (f32[2,4,37]{2,1,0:T(4,128)S(1)}, f32[2,4,37]{2,1,0:T(4,128)}, u32[]{:S(2)}) copy-start(f32[2,4,37]{2,1,0:T(4,128)} %param.21) | copy-start | bytes 3556
  3.3 5.9 %copy-start.13 = (bf16[1024,3,256]{2,0,1:T(8,128)(2,1)S(1)}, bf16[1024,3,256]{2,0,1:T(8,128)(2,1)}, u32[]{:S(2)}) copy-start(bf16[1024,3,256]{2,0,1:T(8,128)(2,1)} %param.18) | copy-start | bytes 4718596
  3.3 25.1 %collective-permute-start = (bf16[1024,768]{1,0:T(8,128)(2,1)}, bf16[1024,768]{1,0:T(8,128)(2,1)}, u32[]{:S(2)}, u32[]{:S(2)}) collective-permute-start(bf16[1024,768]{1,0:T(8,128)(2,1)} %copy.25.weight), channel_id=1, source_target_pairs={{0,1},{1,0},{2,3},{3,2},{4,5},{5,4},{6,7},{7,6},{8,9},{9,8},{10,11... | collective-permute-start | bytes 4718600 | tf_op jit(solution)/shard_map/ppermute | solution.py:254
  6.6 13.5 %collective-permute-start.4 = (bf16[256,1024]{1,0:T(8,128)(2,1)S(1)}, bf16[256,1024]{1,0:T(8,128)(2,1)S(1)}, u32[]{:S(2)}, u32[]{:S(2)}) collective-permute-start(bf16[256,1024]{1,0:T(8,128)(2,1)S(1)} %copy-done), channel_id=1, source_target_pairs={{0,2},{1,3},{2,0},{3,1},{4,6},{5,7},{6,4},{7,5},{8,10},{9,11},{10,... | collective-permute-start | bytes 1572872 | tf_op jit(solution)/shard_map/ppermute | solution.py:254
  8.6 4.3 %collective-permute-start.1 = (bf16[2,32,256]{2,1,0:T(8,128)(2,1)}, bf16[2,32,256]{2,1,0:T(8,128)(2,1)}, u32[]{:S(2)}, u32[]{:S(2)}) collective-permute-start(bf16[2,32,256]{2,1,0:T(8,128)(2,1)} %reshape.28), channel_id=1, source_target_pairs={{0,1},{1,0},{2,3},{3,2},{4,5},{5,4},{6,7},{7,6},{8,9},{9,8},{10,11... | collective-permute-start | bytes 98312 | tf_op jit(solution)/shard_map/ppermute | solution.py:254
  8.7 72.1 %collective-permute-start.14 = (bf16[1024,1024]{1,0:T(8,128)(2,1)}, bf16[1024,1024]{1,0:T(8,128)(2,1)}, u32[]{:S(2)}, u32[]{:S(2)}) collective-permute-start(bf16[1024,1024]{1,0:T(8,128)(2,1)} %u0.1), channel_id=1, source_target_pairs={{0,1},{1,0},{2,3},{3,2},{4,5},{5,4},{6,7},{7,6},{8,9},{9,8},{10,11... | collective-permute-start | bytes 6291464 | tf_op jit(solution)/shard_map/ppermute | solution.py:254
  9.1 71.7 %collective-permute-start.15 = (bf16[1024,1024]{1,0:T(8,128)(2,1)}, bf16[1024,1024]{1,0:T(8,128)(2,1)}, u32[]{:S(2)}, u32[]{:S(2)}) collective-permute-start(bf16[1024,1024]{1,0:T(8,128)(2,1)} %d0.1), channel_id=1, source_target_pairs={{0,1},{1,0},{2,3},{3,2},{4,5},{5,4},{6,7},{7,6},{8,9},{9,8},{10,11... | collective-permute-start | bytes 6291464 | tf_op jit(solution)/shard_map/ppermute | solution.py:254
  11.1 12.2 %copy-start.1 = (bf16[256,1024]{1,0:T(8,128)(2,1)S(1)}, bf16[256,1024]{1,0:T(8,128)(2,1)}, u32[]{:S(2)}) copy-start(bf16[256,1024]{1,0:T(8,128)(2,1)} %w0.3) | copy-start | bytes 1572868
  12.9 16.3 %copy-start.7 = (bf16[2,160,288]{2,1,0:T(8,128)(2,1)S(1)}, bf16[2,160,288]{2,1,0:T(8,128)(2,1)}, u32[]{:S(2)}) copy-start(bf16[2,160,288]{2,1,0:T(8,128)(2,1)} %constant.16.clone.select) | copy-start | bytes 552964
  12.9 34.5 %collective-permute-start.9 = (bf16[1024,768]{1,0:T(8,128)(2,1)S(1)}, bf16[1024,768]{1,0:T(8,128)(2,1)}, u32[]{:S(2)}, u32[]{:S(2)}) collective-permute-start(bf16[1024,768]{1,0:T(8,128)(2,1)S(1)} %copy.31.w_own), channel_id=1, source_target_pairs={{0,1},{1,0},{2,3},{3,2},{4,5},{5,4},{6,7},{7,6},{8,9},{9,8},{10,11... | collective-permute-start | bytes 4718600 | tf_op jit(solution)/shard_map/ppermute | solution.py:254
  20.1 2.4 %collective-permute-start.3 = (bf16[256,1024]{1,0:T(8,128)(2,1)S(1)}, bf16[256,1024]{1,0:T(8,128)(2,1)S(1)}, u32[]{:S(2)}, u32[]{:S(2)}) collective-permute-start(bf16[256,1024]{1,0:T(8,128)(2,1)S(1)} %copy-done), channel_id=1, source_target_pairs={{0,1},{1,0},{2,3},{3,2},{4,5},{5,4},{6,7},{7,6},{8,9},{9,8},{10,11... | collective-permute-start | bytes 1572872 | tf_op jit(solution)/shard_map/ppermute | solution.py:254
  23.3 15.8 %collective-permute-start.12 = (bf16[256,1024]{1,0:T(8,128)(2,1)S(1)}, bf16[256,1024]{1,0:T(8,128)(2,1)}, u32[]{:S(2)}, u32[]{:S(2)}) collective-permute-start(bf16[256,1024]{1,0:T(8,128)(2,1)S(1)} %copy-done.1), channel_id=1, source_target_pairs={{0,2},{1,3},{2,0},{3,1},{4,6},{5,7},{6,4},{7,5},{8,10},{9,11},{10,... | collective-permute-start | bytes 1572872 | tf_op jit(solution)/shard_map/ppermute | solution.py:254
  28.4 12.5 %collective-permute-start.5 = (bf16[256,1024]{1,0:T(8,128)(2,1)}, bf16[256,1024]{1,0:T(8,128)(2,1)S(1)}, u32[]{:S(2)}, u32[]{:S(2)}) collective-permute-start(bf16[256,1024]{1,0:T(8,128)(2,1)} %copy-done.2), channel_id=1, source_target_pairs={{0,1},{1,0},{2,3},{3,2},{4,5},{5,4},{6,7},{7,6},{8,9},{9,8},{10,11... | collective-permute-start | bytes 1572872 | tf_op jit(solution)/shard_map/ppermute | solution.py:254
  34.9 11.1 %copy-start.3 = (bf16[256,1024]{1,0:T(8,128)(2,1)S(1)}, bf16[256,1024]{1,0:T(8,128)(2,1)}, u32[]{:S(2)}) copy-start(bf16[256,1024]{1,0:T(8,128)(2,1)} %copy-done.2) | copy-start | bytes 1572868
  34.9 11.1 %copy-start.5 = (bf16[256,1024]{1,0:T(8,128)(2,1)S(1)}, bf16[256,1024]{1,0:T(8,128)(2,1)}, u32[]{:S(2)}) copy-start(bf16[256,1024]{1,0:T(8,128)(2,1)} %copy-done.4) | copy-start | bytes 1572868
  39.1 6.1 %collective-permute-start.2 = (bf16[160,512]{1,0:T(8,128)(2,1)S(1)}, bf16[160,512]{1,0:T(8,128)(2,1)S(1)}, u32[]{:S(2)}, u32[]{:S(2)}) collective-permute-start(bf16[160,512]{1,0:T(8,128)(2,1)S(1)} %shard_map.155.mine), channel_id=1, source_target_pairs={{0,2},{1,3},{2,0},{3,1},{4,6},{5,7},{6,4},{7,5},{8,10},{9,11},{10,... | collective-permute-start | bytes 491528 | tf_op jit(solution)/shard_map/ppermute | solution.py:254
  40.9 35.8 %collective-permute-start.11 = (bf16[256,1024]{1,0:T(8,128)(2,1)S(1)}, bf16[256,1024]{1,0:T(8,128)(2,1)}, u32[]{:S(2)}, u32[]{:S(2)}) collective-permute-start(bf16[256,1024]{1,0:T(8,128)(2,1)S(1)} %copy-done.1), channel_id=1, source_target_pairs={{0,1},{1,0},{2,3},{3,2},{4,5},{5,4},{6,7},{7,6},{8,9},{9,8},{10,11... | collective-permute-start | bytes 1572872 | tf_op jit(solution)/shard_map/ppermute | solution.py:254
  45.3 31.4 %collective-permute-start.13 = (bf16[256,1024]{1,0:T(8,128)(2,1)}, bf16[256,1024]{1,0:T(8,128)(2,1)}, u32[]{:S(2)}, u32[]{:S(2)}) collective-permute-start(bf16[256,1024]{1,0:T(8,128)(2,1)} %collective-permute-done.12.w2), channel_id=1, source_target_pairs={{0,1},{1,0},{2,3},{3,2},{4,5},{5,4},{6,7},{7,6},{8,9},{9,8},{10,11... | collective-permute-start | bytes 1572872 | tf_op jit(solution)/shard_map/ppermute | solution.py:254
  47.4 6.9 %collective-permute-start.6 = (bf16[40,1024]{1,0:T(8,128)(2,1)S(1)}, bf16[40,1024]{1,0:T(8,128)(2,1)S(1)}, u32[]{:S(2)}, u32[]{:S(2)}) collective-permute-start(bf16[40,1024]{1,0:T(8,128)(2,1)S(1)} %get-tuple-element.14), channel_id=1, source_target_pairs={{0,224},{1,225},{2,226},{3,227},{4,228},{5,229},{6,230},{7,231},{8... | collective-permute-start | bytes 245768 | tf_op jit(solution)/shard_map/ppermute | solution.py:254
  54.3 5.8 %collective-permute-start.7 = (bf16[40,1024]{1,0:T(8,128)(2,1)S(1)}, bf16[40,1024]{1,0:T(8,128)(2,1)S(1)}, u32[]{:S(2)}, u32[]{:S(2)}) collective-permute-start(bf16[40,1024]{1,0:T(8,128)(2,1)S(1)} %get-tuple-element.15), channel_id=1, source_target_pairs={{0,30},{1,31},{2,28},{3,29},{4,0},{5,1},{6,2},{7,3},{8,4},{9,5},{1... | collective-permute-start | bytes 245768 | tf_op jit(solution)/shard_map/ppermute | solution.py:254
  60.0 10.1 %collective-permute-start.8 = (bf16[40,1024]{1,0:T(8,128)(2,1)}, bf16[40,1024]{1,0:T(8,128)(2,1)S(1)}, u32[]{:S(2)}, u32[]{:S(2)}) collective-permute-start(bf16[40,1024]{1,0:T(8,128)(2,1)} %get-tuple-element.16), channel_id=1, source_target_pairs={{0,254},{1,255},{2,252},{3,253},{4,224},{5,225},{6,226},{7,227},{8... | collective-permute-start | bytes 245768 | tf_op jit(solution)/shard_map/ppermute | solution.py:254
  76.5 34.4 %copy-start.6 = (bf16[2,288,160]{2,1,0:T(8,128)(2,1)S(1)}, bf16[2,288,160]{2,1,0:T(8,128)(2,1)}, u32[]{:S(2)}) copy-start(bf16[2,288,160]{2,1,0:T(8,128)(2,1)} %constant.17.clone.place) | copy-start | bytes 552964
  76.5 4.3 %collective-permute-start.10 = (bf16[160,512]{1,0:T(8,128)(2,1)S(1)}, bf16[160,512]{1,0:T(8,128)(2,1)S(1)}, u32[]{:S(2)}, u32[]{:S(2)}) collective-permute-start(bf16[160,512]{1,0:T(8,128)(2,1)S(1)} %shard_map.157.mine), channel_id=1, source_target_pairs={{0,2},{1,3},{2,0},{3,1},{4,6},{5,7},{6,4},{7,5},{8,10},{9,11},{10,... | collective-permute-start | bytes 491528 | tf_op jit(solution)/shard_map/ppermute | solution.py:254
  87.0 3.4 %collective-permute-start.16 = (bf16[40,1024]{1,0:T(8,128)(2,1)S(1)}, bf16[40,1024]{1,0:T(8,128)(2,1)S(1)}, u32[]{:S(2)}, u32[]{:S(2)}) collective-permute-start(bf16[40,1024]{1,0:T(8,128)(2,1)S(1)} %get-tuple-element.17.refs_0_), channel_id=1, source_target_pairs={{0,2},{1,3},{2,0},{3,1},{4,6},{5,7},{6,4},{7,5},{8,10},{9,11},{10,... | collective-permute-start | bytes 245768 | tf_op jit(solution)/shard_map/ppermute | solution.py:254
  87.1 7.0 %collective-permute-start.17 = (bf16[40,1024]{1,0:T(8,128)(2,1)S(1)}, bf16[40,1024]{1,0:T(8,128)(2,1)S(1)}, u32[]{:S(2)}, u32[]{:S(2)}) collective-permute-start(bf16[40,1024]{1,0:T(8,128)(2,1)S(1)} %get-tuple-element.18), channel_id=1, source_target_pairs={{0,32},{1,33},{2,34},{3,35},{4,36},{5,37},{6,38},{7,39},{8,40},{9,... | collective-permute-start | bytes 245768 | tf_op jit(solution)/shard_map/ppermute | solution.py:254
  87.2 8.1 %collective-permute-start.18 = (bf16[40,1024]{1,0:T(8,128)(2,1)S(1)}, bf16[40,1024]{1,0:T(8,128)(2,1)S(1)}, u32[]{:S(2)}, u32[]{:S(2)}) collective-permute-start(bf16[40,1024]{1,0:T(8,128)(2,1)S(1)} %get-tuple-element.18), channel_id=1, source_target_pairs={{0,34},{1,35},{2,32},{3,33},{4,38},{5,39},{6,36},{7,37},{8,42},{9,... | collective-permute-start | bytes 245768 | tf_op jit(solution)/shard_map/ppermute | solution.py:254
  87.3 8.0 %collective-permute-start.19 = (bf16[40,1024]{1,0:T(8,128)(2,1)S(1)}, bf16[40,1024]{1,0:T(8,128)(2,1)S(1)}, u32[]{:S(2)}, u32[]{:S(2)}) collective-permute-start(bf16[40,1024]{1,0:T(8,128)(2,1)S(1)} %get-tuple-element.19), channel_id=1, source_target_pairs={{0,4},{1,5},{2,6},{3,7},{4,8},{5,9},{6,10},{7,11},{8,12},{9,13},{1... | collective-permute-start | bytes 245768 | tf_op jit(solution)/shard_map/ppermute | solution.py:254
  87.4 8.0 %collective-permute-start.20 = (bf16[40,1024]{1,0:T(8,128)(2,1)S(1)}, bf16[40,1024]{1,0:T(8,128)(2,1)S(1)}, u32[]{:S(2)}, u32[]{:S(2)}) collective-permute-start(bf16[40,1024]{1,0:T(8,128)(2,1)S(1)} %get-tuple-element.19), channel_id=1, source_target_pairs={{0,6},{1,7},{2,4},{3,5},{4,10},{5,11},{6,8},{7,9},{8,14},{9,15},{1... | collective-permute-start | bytes 245768 | tf_op jit(solution)/shard_map/ppermute | solution.py:254
  90.4 9.1 %collective-permute-start.21 = (bf16[40,1024]{1,0:T(8,128)(2,1)S(1)}, bf16[40,1024]{1,0:T(8,128)(2,1)S(1)}, u32[]{:S(2)}, u32[]{:S(2)}) collective-permute-start(bf16[40,1024]{1,0:T(8,128)(2,1)S(1)} %get-tuple-element.20), channel_id=1, source_target_pairs={{0,36},{1,37},{2,38},{3,39},{4,40},{5,41},{6,42},{7,43},{8,44},{9,... | collective-permute-start | bytes 245768 | tf_op jit(solution)/shard_map/ppermute | solution.py:254
  94.1 8.7 %collective-permute-start.22 = (bf16[40,1024]{1,0:T(8,128)(2,1)S(1)}, bf16[40,1024]{1,0:T(8,128)(2,1)S(1)}, u32[]{:S(2)}, u32[]{:S(2)}) collective-permute-start(bf16[40,1024]{1,0:T(8,128)(2,1)S(1)} %get-tuple-element.20), channel_id=1, source_target_pairs={{0,38},{1,39},{2,36},{3,37},{4,42},{5,43},{6,40},{7,41},{8,46},{9,... | collective-permute-start | bytes 245768 | tf_op jit(solution)/shard_map/ppermute | solution.py:254
  102.9 8.0 %collective-permute-start.23 = (bf16[160,1024]{1,0:T(8,128)(2,1)S(1)}, bf16[160,1024]{1,0:T(8,128)(2,1)S(1)}, u32[]{:S(2)}, u32[]{:S(2)}) collective-permute-start(bf16[160,1024]{1,0:T(8,128)(2,1)S(1)} %shard_map.159.mine), channel_id=1, source_target_pairs={{0,1},{1,0},{2,3},{3,2},{4,5},{5,4},{6,7},{7,6},{8,9},{9,8},{10,11... | collective-permute-start | bytes 983048 | tf_op jit(solution)/shard_map/ppermute | solution.py:254
  (9 other events, 23.7 us)

commit v2 on v0

v2 whole, which is shorter than its diff:
```python
import functools

import jax
import jax.numpy as jnp
import numpy as np
from jax import lax
from jax.experimental import pallas as pl
from jax.experimental.pallas import tpu as pltpu
from jax.sharding import PartitionSpec as P

WL = 2
WY = 6
WX = 12
SY = 3
SX = 6
HD = 64
NEG = -1000000000.0
AXES = ("lat", "lon", "mp")
MIB = 1024 * 1024

USED = 36
ROWS = 40
KEPT = 4 * ROWS
PATCH = 4 * WY * WX
WINDOW = WL * WY * WX
FEAT = 32
F_Y = 4
F_X = 10
F_PAD = 22


def pairs(counts, target):
    lats, lons, mps = counts
    result = []
    for a in range(lats):
        for b in range(lons):
            for m in range(mps):
                ta, tb, tm = target(a, b, m)
                dest = ((ta % lats) * lons + tb % lons) * mps + tm
                result.append(((a * lons + b) * mps + m, dest))
    return result


def dot(left, right):
    return jnp.dot(left, right, preferred_element_type=jnp.float32)


def dot_t(left, right):
    return lax.dot_general(left, right, (((1,), (1,)), ((), ())), preferred_element_type=jnp.float32)


def normalize(floats):
    center = floats - jnp.mean(floats, axis=-1, keepdims=True)
    spread = jnp.mean(center * center, axis=-1, keepdims=True)
    return (center * lax.rsqrt(spread + 1e-05)).astype(jnp.bfloat16)


def core_index():
    return lax.rem(lax.axis_index("mp"), 2)


def iota(shape, axis):
    return lax.broadcasted_iota(jnp.int32, shape, axis)


def one_hot(condition):
    return jnp.where(condition, 1.0, 0.0).astype(jnp.bfloat16)


def piece_place(slot):
    level = (slot * 57) >> 10
    rest = slot - level * 18
    row = (rest * 43) >> 8
    return level, row, rest - row * 6


def kept_place(index):
    q = (index * 205) >> 13
    return (q, index - q * ROWS) + piece_place(index - q * ROWS)


def real_level(level, core):
    return jnp.where(core == 0, 1 + level, 3 - 3 * level)


def patch_place(q, row, col):
    return row + 3 - 3 * (q & 1), col + 6 - 3 * (q & 2)


def bias_rows(table, block, pair):
    shape = (FEAT, 4 * FEAT)
    i, lane = iota(shape, 0), iota(shape, 1)
    j = lane & (FEAT - 1)
    kind = jnp.full(shape, 37, jnp.int32)
    kind = jnp.where((i < WL) & (j < WL), i - j + 1, kind)
    kind = jnp.where((i < WL) & (j == F_PAD), 38, kind)
    in_y = (i >= F_Y) & (i < F_Y + WY) & (j >= F_Y) & (j < F_Y + WY)
    kind = jnp.where(in_y, 3 + i - j + 5, kind)
    in_x = (i >= F_X) & (i < F_X + WX) & (j >= F_X) & (j < F_X + WX)
    kind = jnp.where(in_x, 14 + i - j + 11, kind)
    total = jnp.where(kind == 38, NEG, 0.0)
    for k in range(37):
        value = jnp.where(lane < HD, table[block, 2 * pair + 1, k], table[block, 2 * pair, k])
        total = jnp.where(kind == k, value, total)
    high = total.astype(jnp.bfloat16).astype(jnp.float32)
    return jnp.where((lane & FEAT) != 0, total - high, high).astype(jnp.bfloat16)


def features(level, row, col, used, count):
    j = iota((count, 128), 1) & (FEAT - 1)
    hit = (j == level) | (j == F_Y + row) | (j == F_X + col)
    return one_hot(jnp.where(used, jnp.where(hit, 1, 0), jnp.where(j == F_PAD, 1, 0)) == 1)


def pair_heads(query, key, value, extra, key_feat):
    low_q = iota(query.shape, 1) < HD
    low_k = iota(key.shape, 1) < HD
    outs = []
    for head in range(2):
        mine_q, mine_k = (low_q, low_k) if head == 0 else (~low_q, ~low_k)
        scores = dot_t(jnp.where(mine_q, query, extra), jnp.where(mine_k, key, key_feat))
        expo = jnp.exp(scores - jnp.max(scores, axis=-1, keepdims=True))
        probs = (expo / jnp.sum(expo, axis=-1, keepdims=True)).astype(jnp.bfloat16)
        outs.append(dot(probs, value))
    return jnp.where(low_q, outs[0], outs[1]).astype(jnp.bfloat16)


def first_kernel(tokens, weight, table, keep, give, base):
    core = core_index()
    floats = tokens[...].astype(jnp.float32).reshape(PATCH, -1)
    xn = normalize(floats)
    q = (dot(xn, weight[0]) * HD**-0.5).astype(jnp.bfloat16)
    k = dot(xn, weight[1]).astype(jnp.bfloat16)
    v = dot(xn, weight[2]).astype(jnp.bfloat16)
    index = iota((PATCH, 1), 0)
    level = (index * 911) >> 16
    order = one_hot(iota((PATCH, PATCH), 1) == (index - 72 * level) * 4 + level)
    q, k, v = (dot(order, part).astype(jnp.bfloat16) for part in (q, k, v))
    index = iota((WINDOW, 1), 0)
    level = (index * 911) >> 16
    rest = index - 72 * level
    row = (rest * 171) >> 11
    feat = features(level, row, rest - 12 * row, index >= 0, WINDOW)
    parts = []
    for pair in range(2):
        cols = slice(pair * 128, pair * 128 + 128)
        extra = dot(feat[:, :FEAT], bias_rows(table, 0, pair)).astype(jnp.bfloat16)
        halves = []
        for w in range(2):
            rows = slice(w * WINDOW, (w + 1) * WINDOW)
            halves.append(pair_heads(q[rows, cols], k[rows, cols], v[rows, cols], extra, feat))
        parts.append(jnp.concatenate(halves, axis=0))
    mixed = jnp.concatenate(parts, axis=1)
    quad, slot, level, row, col = kept_place(iota((KEPT, 1), 0))
    row, col = patch_place(quad, row, col)
    lanes = iota((KEPT, PATCH), 1)
    for out, chosen in ((keep, core), (give, 1 - core)):
        place = real_level(level, chosen) * 72 + row * 12 + col
        place = jnp.where(slot < USED, place, -1)
        out[...] = dot(one_hot(lanes == place), mixed).astype(jnp.bfloat16)
    place = (row * 12 + col) * 4 + real_level(level, core)
    place = jnp.where(slot < USED, place, -1)
    base[...] = dot(one_hot(lanes == place), floats.astype(jnp.bfloat16)).astype(jnp.bfloat16)


def residual_kernel(o0, o1, o2, o3, w0, w1, w2a, w2b, w3a, w3b, base, *outs):
    total = dot(o0[...], w0[...]) + dot(o1[...], w1[...])
    total = total + dot(o2[:, :128], w2a[...]) + dot(o2[:, 128:], w2b[...])
    total = total + dot(o3[:, :128], w3a[...]) + dot(o3[:, 128:], w3b[...])
    first = base[...].astype(jnp.float32) + total.astype(jnp.bfloat16).astype(jnp.float32)
    for q in range(4):
        outs[q][...] = first[q * ROWS : (q + 1) * ROWS].astype(jnp.bfloat16)


def joined(pieces):
    return jnp.concatenate([p[...].astype(jnp.float32) for p in pieces], axis=0)


def second_kernel(p0, p1, p2, p3, w_own, w_sib, t_own, t_sib, out):
    xn = normalize(joined((p0, p1, p2, p3)))
    quad, slot, level, row, col = kept_place(iota((KEPT, 1), 0))
    row, col = row + 3 * (quad & 1), col + 3 * (quad & 2)
    feat = features(level, row, col, slot < USED, KEPT)
    lane = iota((KEPT, 128), 1)
    j = lane & (FEAT - 1)
    split_levels = core_index() == 1
    split_rows = lax.axis_index("lat") == lax.axis_size("lat") - 1
    ban_level = (j < WL) & (j != level)
    ban_row = (j >= F_Y) & (j < F_Y + WY) & ((j >= F_Y + SY) != (row >= SY))
    ban = jnp.where(ban_level, split_levels.astype(jnp.int32), jnp.where(ban_row, split_rows.astype(jnp.int32), 0))
    ban = jnp.where((lane & FEAT) == 0, ban, 0) == 1
    for part, (weight, table) in enumerate(((w_own, t_own), (w_sib, t_sib))):
        q = (dot(xn, weight[0]) * HD**-0.5).astype(jnp.bfloat16)
        k = dot(xn, weight[1]).astype(jnp.bfloat16)
        v = dot(xn, weight[2]).astype(jnp.bfloat16)
        for pair in range(2):
            cols = slice(pair * 128, pair * 128 + 128)
            extra = dot(feat[:, :FEAT], bias_rows(table, 1, pair))
            extra = jnp.where(ban, NEG, extra).astype(jnp.bfloat16)
            start = part * 256 + pair * 128
            out[:, start : start + 128] = pair_heads(q[:, cols], k[:, cols], v[:, cols], extra, feat)


def gelu(x):
    return 0.5 * x * (1.0 + lax.erf(x * np.float32(np.sqrt(0.5))))


def owned(member):
    return jnp.where(member == 0, 0, jnp.where(member == 1, 3, member - 1))


def mlp_kernel(mine, other, w0, w1, w2, w3, p0, p1, p2, p3, u0, u1, d0, d1, *refs):
    outs, held = refs[:4], refs[4]
    total = dot(mine[:, :256], w0[...]) + dot(mine[:, 256:], w1[...])
    total = total + dot(other[:, :256], w2[...]) + dot(other[:, 256:], w3[...])
    second = joined((p0, p1, p2, p3)) + total.astype(jnp.bfloat16).astype(jnp.float32)
    second = second.astype(jnp.bfloat16).astype(jnp.float32)
    xn = normalize(second)
    h0 = gelu(dot(xn, u0[...])).astype(jnp.bfloat16)
    h1 = gelu(dot(xn, u1[...])).astype(jnp.bfloat16)
    held[...] = 0.5 * second + dot(h0, d0[...]) + dot(h1, d1[...])
    member = lax.axis_index("mp")
    for step in range(4):
        start = pl.multiple_of(owned(member ^ step) * ROWS, 8)
        outs[step][...] = held[pl.ds(start, ROWS), :].astype(jnp.bfloat16)


def sum_kernel(own, far, near_sib, far_sib, out):
    mine = own[...].astype(jnp.float32) + far[...].astype(jnp.float32)
    sib = near_sib[...].astype(jnp.float32) + far_sib[...].astype(jnp.float32)
    first = core_index() == 0
    out[...] = jnp.concatenate([jnp.where(first, mine, sib), jnp.where(first, sib, mine)], axis=0).astype(
        jnp.bfloat16
    )


def place_kernel(r0, r1, r2, r3, out):
    member = lax.axis_index("mp")
    index = iota((1, 2 * ROWS), 1)
    core = jnp.where(index >= ROWS, 1, 0)
    slot = index - core * ROWS
    level, row, col = piece_place(slot)
    total = None
    for step, part in enumerate((r0, r1, r2, r3)):
        prow, pcol = patch_place(owned(member ^ step), row, col)
        place = (prow * 12 + pcol) * 4 + real_level(level, core)
        place = jnp.where(slot < USED, place, -1)
        term = dot(one_hot(iota((PATCH, 2 * ROWS), 0) == place), part[...])
        total = term if total is None else total + term
    out[...] = total.reshape(out.shape).astype(jnp.bfloat16)


def call(kernel, outs, operands, flops, limit, tables=(), scratch=()):
    shapes = [jax.ShapeDtypeStruct(s, jnp.bfloat16) for s in outs]
    moved = sum(o.size * o.dtype.itemsize for o in operands) + sum(2 * s.size for s in shapes)
    vmem = pl.BlockSpec(memory_space=pltpu.VMEM)
    smem = pl.BlockSpec(memory_space=pltpu.SMEM)
    result = pl.pallas_call(
        kernel,
        out_shape=shapes,
        in_specs=[vmem] * len(operands) + [smem] * len(tables),
        out_specs=[vmem] * len(shapes),
        scratch_shapes=scratch,
        compiler_params=pltpu.CompilerParams(vmem_limit_bytes=limit * MIB),
        cost_estimate=pl.CostEstimate(flops=flops, bytes_accessed=moved, transcendentals=0),
    )(*operands, *tables)
    return result if len(result) > 1 else result[0]


def tied(values, after):
    return lax.optimization_barrier((tuple(values), tuple(after)))[0]


def body(counts, tokens, qkv_first, qkv_second, out_first, out_second, rel_tables, up_weight, down_weight):
    levels, rows, cols, width = tokens.shape
    half = out_first.shape[0] // 2
    turn = counts[1] // 2

    def move(value, target):
        return lax.ppermute(value, AXES, pairs(counts, target))

    def core_swap(value):
        return move(value, lambda a, b, m: (a, b, m ^ 1))

    def chip_swap(value):
        return move(value, lambda a, b, m: (a, b, m ^ 2))

    def far_swap(value):
        return move(value, lambda a, b, m: (a, b, m ^ 3))

    def side_swap(value):
        return move(value, lambda a, b, m: (a, b + turn, m ^ 2))

    offsets = ((0, 0), (1, 0), (0, 1), (1, 1))
    pieces = [(ROWS, width)] * 4
    halves = [(KEPT, 256)] * 2

    tok = tokens.transpose(1, 2, 0, 3).reshape(rows * cols, levels, width)
    w_first = qkv_first.transpose(1, 0, 2)
    w_second = qkv_second.transpose(1, 0, 2)

    f2a = chip_swap(out_first[:half])
    f2b = side_swap(out_first[half:])
    f1 = core_swap(out_first)
    keep, give, base = call(
        first_kernel, halves + [(KEPT, width)], (tok, w_first), 10**9, 24, tables=(rel_tables,)
    )
    from_far = far_swap(give)
    from_chip = chip_swap(keep)
    from_core = core_swap(give)
    f3a = core_swap(f2a)
    f3b = core_swap(f2b)
    s_table = core_swap(rel_tables)
    w_sib = core_swap(w_second)

    firsts = call(
        residual_kernel,
        pieces,
        (keep, from_core, from_chip, from_far, out_first, f1, f2a, f2b, f3a, f3b, base),
        5 * 10**8,
        24,
    )
    *firsts, w_sib, s_table = tied((*firsts, w_sib, s_table), ())
    shifted = {0: firsts[0]}
    for q in (3, 2, 1):
        dy, dx = offsets[q]

        def target(a, b, m, dy=dy, dx=dx):
            return a - dy, b - dx, m ^ 2 if dx and b % turn == 0 else m

        shifted[q] = move(firsts[q], target)
    shifted = [shifted[q] for q in range(4)]
    out_second, up_weight, down_weight = tied((out_second, up_weight, down_weight), (w_sib,))
    s2 = chip_swap(out_second)
    s1 = core_swap(out_second)
    u1 = core_swap(up_weight)
    d1 = core_swap(down_weight)

    mixed = call(
        second_kernel,
        [(KEPT, 512)],
        (*shifted, w_second, w_sib),
        10**9,
        24,
        tables=(rel_tables, s_table),
    )
    other = chip_swap(mixed)
    s3 = core_swap(s2)
    own, to_core, to_chip, to_far = call(
        mlp_kernel,
        pieces,
        (mixed, other, out_second, s1, s2, s3, *shifted, up_weight, u1, down_weight, d1),
        2 * 10**9,
        40,
        scratch=[pltpu.VMEM((KEPT, width), jnp.float32)],
    )
    at_far = far_swap(to_far)
    at_chip = chip_swap(to_chip)
    at_core = core_swap(to_core)
    done = call(sum_kernel, [(2 * ROWS, width)], (own, at_chip, at_core, at_far), 10**6, 16)

    def home(flip):
        def target(a, b, m):
            dy, dx = offsets[(0, 3, 1, 2)[m]]
            return a + dy, b + dx, m ^ flip

        return target

    here = move(done, home(0))
    there = move(done, home(2))
    result = call(
        place_kernel,
        [(rows * cols, levels, width)],
        (here, core_swap(here), there, core_swap(there)),
        2 * 10**8,
        16,
    )
    return result.reshape(rows, cols, levels, width).transpose(2, 0, 1, 3)


def solution(mesh):
    counts = tuple(mesh.shape[name] for name in AXES)
    return jax.shard_map(
        functools.partial(body, counts),
        mesh=mesh,
        in_specs=(
            P(None, "lat", "lon", None),
            P(None, None, "mp"),
            P(None, None, "mp"),
            P("mp", None),
            P("mp", None),
            P(None, "mp", None),
            P(None, "mp"),
            P("mp", None),
        ),
        out_specs=P(None, "lat", "lon", None),
        check_vma=False,
    )
```

time: 280 us -> 106 us (0.38)
  waiting for transfers between devices: 164 us -> 51.1 us
  local copies, waits for them, and re-layouts: 46 us -> 5.65 us
  matrix products: 31.4 us -> 0 us
  starting transfers between devices: 10.8 us -> 36.5 us
  between operations: 13.5 us -> 0.15 us
  other arithmetic: 12.7 us -> 0 us
  Pallas kernels: 0 us -> 12.6 us
    psum x3 -> x0, waiting for transfers between devices: 131 us -> none  [reduce_rows(): return lax.psum(terms.astype(jnp.bfloat16), 'mp')]
    dot_general x15 -> x0, matrix products: 29.9 us -> none  [the longest x6 7.24 us: bias_matrix(): jnp.einsum('hk,ijk->hij', table[:, offset:offset + span], onehot, precisi...]
    ppermute x4 -> x26, starting transfers between devices: 10.5 us -> 36.5 us  [move(): return lax.ppermute(value, AXES, pairs(counts, target))]
    ppermute x4 -> x26, waiting for transfers between devices: 33.1 us -> 51.1 us  [move(): return lax.ppermute(value, AXES, pairs(counts, target))]
    pallas_call x0 -> x6, Pallas kernels: none -> 12.6 us  [call(): pl.pallas_call(kernel, out_shape=shapes, in_specs=[vmem] * len(operands)...]
    unnamed x37 -> x16, local copies, waits for them, and re-layouts: 15.5 us -> 4.59 us
    slice x8 -> x1, local copies, waits for them, and re-layouts: 9.35 us -> 1.06 us  [body(): f2b = side_swap(out_first[half:])]
    convert_element_type x6 -> x0, local copies, waits for them, and re-layouts: 7 us -> none  [the longest x2 3.9 us: add_branch(): residual.astype(jnp.float32) + branch.astype(jnp.float32)]
  transfers between devices with their start and end apart: 7 -> 26, of which waited for: 7 -> 14; matrix products, arithmetic and copies ran while one was open for 5% -> 1% of each run, Pallas kernels for 0% -> 8%
where the time goes in v2:
time: 106 us
  waiting for transfers between devices  51.1 us (48%)
  starting transfers between devices  36.5 us (34%)
  Pallas kernels  12.6 us (12%)
  local copies, waits for them, and re-layouts  5.65 us (5%)
    ppermute x26, waiting for transfers between devices, move(): return lax.ppermute(value, AXES, pairs(counts, target))  51.1 us
    ppermute x26, starting transfers between devices, move(): return lax.ppermute(value, AXES, pairs(counts, target))  36.5 us
    pallas_call x6, Pallas kernels, call(): pl.pallas_call(kernel, out_shape=shapes, in_specs=[vmem] * len(operands)...  12.6 us
    unnamed x16, local copies, waits for them, and re-layouts  4.59 us
  transfers between devices with their start and end apart: 26, of which 14 were waited for; matrix products, arithmetic and copies ran while one was open for 1% of the time, Pallas kernels for 8%

profile of v2, /device:TPU:1, one launch (start us, length us, event | category | flops | bytes accessed | tf_op | source)
XLA Modules:
  0.0 106.1 jit_solution(2338823206549037316)
XLA Ops:
  0.0 3.2 %collective-permute-start.8 = (bf16[3,1024,256]{2,1,0:T(8,128)(2,1)}, bf16[3,1024,256]{2,1,0:T(8,128)(2,1)S(1)}, u32[]{:S(2)}, u32[]{:S(2)}) collective-permute-start(bf16[3,1024,256]{2,1,0:T(8,128)(2,1)} %bitcast.9), channel_id=1, source_target_pairs={{0,1},{1,0},{2,3},{3,2},{4,5},{5,4},{6,7},{7,6},{8,9},{9,8},{10,11... | collective-permute-start | bytes 4718600 | tf_op jit(solution)/shard_map/ppermute | solution.py:280
  3.2 1.1 %fusion = (bf16[128,1024]{1,0:T(8,128)(2,1)S(1)}, bf16[128,1024]{1,0:T(8,128)(2,1)S(1)}) fusion(bf16[256,1024]{1,0:T(8,128)(2,1)} %w0.1), kind=kLoop, calls=%fused_computation | loop fusion | bytes 1048576 | tf_op jit(solution)/shard_map/slice | solution.py:303
  4.3 0.8 collective-permute-start.5
  5.7 7.9 %collective-permute-done.5.w2b = bf16[128,1024]{1,0:T(8,128)(2,1)S(1)} collective-permute-done((bf16[128,1024]{1,0:T(8,128)(2,1)S(1)}, bf16[128,1024]{1,0:T(8,128)(2,1)S(1)}, u32[]{:S(2)}, u32[]{:S(2)}) %collective-permute-start.5) | collective-permute-done | bytes 262176 | tf_op jit(solution)/shard_map/ppermute | solution.py:280
  14.4 1.4 %copy-done.4 = bf16[1024,3,256]{2,0,1:T(8,128)(2,1)S(1)} copy-done((bf16[1024,3,256]{2,0,1:T(8,128)(2,1)S(1)}, bf16[1024,3,256]{2,0,1:T(8,128)(2,1)}, u32[]{:S(2)}) %copy-start.4) | copy-done | bytes 1572888
  15.8 1.1 %copy-done.6 = bf16[4,6,12,1024]{3,0,2,1:T(4,128)(2,1)S(1)} copy-done((bf16[4,6,12,1024]{3,0,2,1:T(4,128)(2,1)S(1)}, bf16[4,6,12,1024]{3,0,2,1:T(4,128)(2,1)}, u32[]{:S(2)}) %copy-start.6) | copy-done | bytes 589848
  17.5 3.7 %shard_map.82 = (bf16[160,256]{1,0:T(8,128)(2,1)S(1)}, bf16[160,256]{1,0:T(8,128)(2,1)S(1)}, bf16[160,1024]{1,0:T(8,128)(2,1)S(1)}) custom-call(bf16[72,4,1024]{2,1,0:T(4,128)(2,1)S(1)} %bitcast.11, bf16[3,1024,256]{2,1,0:T(8,128)(2,1)S(1)} %bitcast.8, f32[2,4,37]{2,1,0:T(4,128)S(1)} %copy-done.7), custom_call_target="tpu_custom_call" | custom-call | flops 1000000000 | bytes 2654208 | tf_op jit(solution)/shard_map/pallas_call | solution.py:258
  21.3 3.3 %collective-permute-done.1.o2 = bf16[160,256]{1,0:T(8,128)(2,1)S(1)} collective-permute-done((bf16[160,256]{1,0:T(8,128)(2,1)S(1)}, bf16[160,256]{1,0:T(8,128)(2,1)S(1)}, u32[]{:S(2)}, u32[]{:S(2)}) %collective-permute-start.1) | collective-permute-done | bytes 81952 | tf_op jit(solution)/shard_map/ppermute | solution.py:280
  24.6 1.5 %collective-permute-start.2 = (bf16[160,256]{1,0:T(8,128)(2,1)S(1)}, bf16[160,256]{1,0:T(8,128)(2,1)S(1)}, u32[]{:S(2)}, u32[]{:S(2)}) collective-permute-start(bf16[160,256]{1,0:T(8,128)(2,1)S(1)} %get-tuple-element.26), channel_id=1, source_target_pairs={{0,3},{1,2},{2,1},{3,0},{4,7},{5,6},{6,5},{7,4},{8,11},{9,10},{10,... | collective-permute-start | bytes 245768 | tf_op jit(solution)/shard_map/ppermute | solution.py:280
  26.1 2.4 %collective-permute-done.2.o3 = bf16[160,256]{1,0:T(8,128)(2,1)S(1)} collective-permute-done((bf16[160,256]{1,0:T(8,128)(2,1)S(1)}, bf16[160,256]{1,0:T(8,128)(2,1)S(1)}, u32[]{:S(2)}, u32[]{:S(2)}) %collective-permute-start.2) | collective-permute-done | bytes 81952 | tf_op jit(solution)/shard_map/ppermute | solution.py:280
  28.5 1.7 %collective-permute-start = (bf16[160,256]{1,0:T(8,128)(2,1)S(1)}, bf16[160,256]{1,0:T(8,128)(2,1)S(1)}, u32[]{:S(2)}, u32[]{:S(2)}) collective-permute-start(bf16[160,256]{1,0:T(8,128)(2,1)S(1)} %get-tuple-element.26), channel_id=1, source_target_pairs={{0,1},{1,0},{2,3},{3,2},{4,5},{5,4},{6,7},{7,6},{8,9},{9,8},{10,11... | collective-permute-start | bytes 245768 | tf_op jit(solution)/shard_map/ppermute | solution.py:280
  30.1 0.9 collective-permute-done.o1
  33.9 12.1 %collective-permute-done.15.w2 = bf16[256,1024]{1,0:T(8,128)(2,1)S(1)} collective-permute-done((bf16[256,1024]{1,0:T(8,128)(2,1)S(1)}, bf16[256,1024]{1,0:T(8,128)(2,1)S(1)}, u32[]{:S(2)}, u32[]{:S(2)}) %collective-permute-start.15) | collective-permute-done | bytes 524320 | tf_op jit(solution)/shard_map/ppermute | solution.py:280
  46.0 1.1 %collective-permute-start.16 = (bf16[256,1024]{1,0:T(8,128)(2,1)S(1)}, bf16[256,1024]{1,0:T(8,128)(2,1)S(1)}, u32[]{:S(2)}, u32[]{:S(2)}) collective-permute-start(bf16[256,1024]{1,0:T(8,128)(2,1)S(1)} %collective-permute-done.15.w2), channel_id=1, source_target_pairs={{0,1},{1,0},{2,3},{3,2},{4,5},{5,4},{6,7},{7,6},{8,9},{9,8},{10,11... | collective-permute-start | bytes 1572872 | tf_op jit(solution)/shard_map/ppermute | solution.py:280
  47.1 5.8 %collective-permute-start.10 = (bf16[40,1024]{1,0:T(8,128)(2,1)S(1)}, bf16[40,1024]{1,0:T(8,128)(2,1)S(1)}, u32[]{:S(2)}, u32[]{:S(2)}) collective-permute-start(bf16[40,1024]{1,0:T(8,128)(2,1)S(1)} %get-tuple-element.33), channel_id=1, source_target_pairs={{0,224},{1,225},{2,226},{3,227},{4,228},{5,229},{6,230},{7,231},{8... | collective-permute-start | bytes 245768 | tf_op jit(solution)/shard_map/ppermute | solution.py:280
  52.9 1.9 %collective-permute-done.10.p1 = bf16[40,1024]{1,0:T(8,128)(2,1)S(1)} collective-permute-done((bf16[40,1024]{1,0:T(8,128)(2,1)S(1)}, bf16[40,1024]{1,0:T(8,128)(2,1)S(1)}, u32[]{:S(2)}, u32[]{:S(2)}) %collective-permute-start.10) | collective-permute-done | bytes 81952 | tf_op jit(solution)/shard_map/ppermute | solution.py:280
  54.8 3.0 %collective-permute-start.11 = (bf16[40,1024]{1,0:T(8,128)(2,1)S(1)}, bf16[40,1024]{1,0:T(8,128)(2,1)S(1)}, u32[]{:S(2)}, u32[]{:S(2)}) collective-permute-start(bf16[40,1024]{1,0:T(8,128)(2,1)S(1)} %get-tuple-element.34), channel_id=1, source_target_pairs={{0,30},{1,31},{2,28},{3,29},{4,0},{5,1},{6,2},{7,3},{8,4},{9,5},{1... | collective-permute-start | bytes 245768 | tf_op jit(solution)/shard_map/ppermute | solution.py:280
  57.8 1.5 %collective-permute-done.11.p2 = bf16[40,1024]{1,0:T(8,128)(2,1)S(1)} collective-permute-done((bf16[40,1024]{1,0:T(8,128)(2,1)S(1)}, bf16[40,1024]{1,0:T(8,128)(2,1)S(1)}, u32[]{:S(2)}, u32[]{:S(2)}) %collective-permute-start.11) | collective-permute-done | bytes 81952 | tf_op jit(solution)/shard_map/ppermute | solution.py:280
  59.3 8.3 %collective-permute-start.12 = (bf16[40,1024]{1,0:T(8,128)(2,1)S(1)}, bf16[40,1024]{1,0:T(8,128)(2,1)S(1)}, u32[]{:S(2)}, u32[]{:S(2)}) collective-permute-start(bf16[40,1024]{1,0:T(8,128)(2,1)S(1)} %get-tuple-element.35), channel_id=1, source_target_pairs={{0,254},{1,255},{2,252},{3,253},{4,224},{5,225},{6,226},{7,227},{8... | collective-permute-start | bytes 245768 | tf_op jit(solution)/shard_map/ppermute | solution.py:280
  67.5 1.5 %collective-permute-done.12.p3 = bf16[40,1024]{1,0:T(8,128)(2,1)S(1)} collective-permute-done((bf16[40,1024]{1,0:T(8,128)(2,1)S(1)}, bf16[40,1024]{1,0:T(8,128)(2,1)S(1)}, u32[]{:S(2)}, u32[]{:S(2)}) %collective-permute-start.12) | collective-permute-done | bytes 81952 | tf_op jit(solution)/shard_map/ppermute | solution.py:280
  69.0 1.4 %copy-done.5 = bf16[1024,3,256]{2,0,1:T(8,128)(2,1)S(1)} copy-done((bf16[1024,3,256]{2,0,1:T(8,128)(2,1)S(1)}, bf16[1024,3,256]{2,0,1:T(8,128)(2,1)}, u32[]{:S(2)}) %copy-start.5) | copy-done | bytes 1572888
  70.4 4.3 %shard_map.84.mine = bf16[160,512]{1,0:T(8,128)(2,1)S(1)} custom-call(bf16[40,1024]{1,0:T(8,128)(2,1)S(1)} %get-tuple-element.32.p0, bf16[40,1024]{1,0:T(8,128)(2,1)S(1)} %collective-permute-done.10.p1, bf16[40,1024]{1,0:T(8,128)(2,1)S(1)} %collective-permute-done.11.p2, bf16[40,1024]{1,0:T(8,128)(2,1)S(1)} %collective-permute-done.12.p3, ...), custom_call_target="tpu_custom_call" | custom-call | flops 1000000000 | bytes 3637248 | tf_op jit(solution)/shard_map/pallas_call | solution.py:258
  74.8 4.2 %collective-permute-done.13.other = bf16[160,512]{1,0:T(8,128)(2,1)S(1)} collective-permute-done((bf16[160,512]{1,0:T(8,128)(2,1)S(1)}, bf16[160,512]{1,0:T(8,128)(2,1)S(1)}, u32[]{:S(2)}, u32[]{:S(2)}) %collective-permute-start.13) | collective-permute-done | bytes 163872 | tf_op jit(solution)/shard_map/ppermute | solution.py:280
  79.0 2.3 %shard_map.85 = (bf16[40,1024]{1,0:T(8,128)(2,1)S(1)}, bf16[40,1024]{1,0:T(8,128)(2,1)S(1)}, bf16[40,1024]{1,0:T(8,128)(2,1)S(1)}, bf16[40,1024]{1,0:T(8,128)(2,1)S(1)}) custom-call(bf16[160,512]{1,0:T(8,128)(2,1)S(1)} %shard_map.84.mine, bf16[160,512]{1,0:T(8,128)(2,1)S(1)} %collective-permute-done.13.other, bf16[256,1024]{1,0:T(8,128)(2,1)S(1)} %copy-done.3, ...), custom_call_target="tpu_custom_call" | custom-call | flops 2000000000 | bytes 11468800 | tf_op jit(solution)/shard_map/pallas_call | solution.py:258
  81.4 4.0 %collective-permute-start.20 = (bf16[40,1024]{1,0:T(8,128)(2,1)S(1)}, bf16[40,1024]{1,0:T(8,128)(2,1)S(1)}, u32[]{:S(2)}, u32[]{:S(2)}) collective-permute-start(bf16[40,1024]{1,0:T(8,128)(2,1)S(1)} %get-tuple-element.43), channel_id=1, source_target_pairs={{0,1},{1,0},{2,3},{3,2},{4,5},{5,4},{6,7},{7,6},{8,9},{9,8},{10,11... | collective-permute-start | bytes 245768 | tf_op jit(solution)/shard_map/ppermute | solution.py:280
  85.4 1.5 %collective-permute-start.21 = (bf16[40,1024]{1,0:T(8,128)(2,1)S(1)}, bf16[40,1024]{1,0:T(8,128)(2,1)S(1)}, u32[]{:S(2)}, u32[]{:S(2)}) collective-permute-start(bf16[40,1024]{1,0:T(8,128)(2,1)S(1)} %get-tuple-element.44), channel_id=1, source_target_pairs={{0,3},{1,2},{2,1},{3,0},{4,7},{5,6},{6,5},{7,4},{8,11},{9,10},{10,... | collective-permute-start | bytes 245768 | tf_op jit(solution)/shard_map/ppermute | solution.py:280
  86.9 3.7 %collective-permute-done.21.far_sib = bf16[40,1024]{1,0:T(8,128)(2,1)S(1)} collective-permute-done((bf16[40,1024]{1,0:T(8,128)(2,1)S(1)}, bf16[40,1024]{1,0:T(8,128)(2,1)S(1)}, u32[]{:S(2)}, u32[]{:S(2)}) %collective-permute-start.21) | collective-permute-done | bytes 81952 | tf_op jit(solution)/shard_map/ppermute | solution.py:280
  90.8 2.0 %collective-permute-start.22 = (bf16[80,1024]{1,0:T(8,128)(2,1)S(1)}, bf16[80,1024]{1,0:T(8,128)(2,1)S(1)}, u32[]{:S(2)}, u32[]{:S(2)}) collective-permute-start(bf16[80,1024]{1,0:T(8,128)(2,1)S(1)} %shard_map.86), channel_id=1, source_target_pairs={{0,0},{1,37},{2,34},{3,7},{4,4},{5,41},{6,38},{7,11},{8,8},{9,45},... | collective-permute-start | bytes 491528 | tf_op jit(solution)/shard_map/ppermute | solution.py:280
  92.8 5.5 %collective-permute-done.24.r2 = bf16[80,1024]{1,0:T(8,128)(2,1)S(1)} collective-permute-done((bf16[80,1024]{1,0:T(8,128)(2,1)S(1)}, bf16[80,1024]{1,0:T(8,128)(2,1)S(1)}, u32[]{:S(2)}, u32[]{:S(2)}) %collective-permute-start.24) | collective-permute-done | bytes 163872 | tf_op jit(solution)/shard_map/ppermute | solution.py:280
  98.2 4.8 %collective-permute-done.22.r0 = bf16[80,1024]{1,0:T(8,128)(2,1)S(1)} collective-permute-done((bf16[80,1024]{1,0:T(8,128)(2,1)S(1)}, bf16[80,1024]{1,0:T(8,128)(2,1)S(1)}, u32[]{:S(2)}, u32[]{:S(2)}) %collective-permute-start.22) | collective-permute-done | bytes 163872 | tf_op jit(solution)/shard_map/ppermute | solution.py:280
  103.1 1.4 %collective-permute-done.23.r1 = bf16[80,1024]{1,0:T(8,128)(2,1)S(1)} collective-permute-done((bf16[80,1024]{1,0:T(8,128)(2,1)S(1)}, bf16[80,1024]{1,0:T(8,128)(2,1)S(1)}, u32[]{:S(2)}, u32[]{:S(2)}) %collective-permute-start.23) | collective-permute-done | bytes 163872 | tf_op jit(solution)/shard_map/ppermute | solution.py:280
  104.5 1.6 %shard_map.87 = bf16[72,4,1024]{2,1,0:T(4,128)(2,1)} custom-call(bf16[80,1024]{1,0:T(8,128)(2,1)S(1)} %collective-permute-done.22.r0, bf16[80,1024]{1,0:T(8,128)(2,1)S(1)} %collective-permute-done.23.r1, bf16[80,1024]{1,0:T(8,128)(2,1)S(1)} %collective-permute-done.24.r2, bf16[80,1024]{1,0:T(8,128)(2,1)S(1)} %collective-permute-done.25.r3), custom_call_target="tpu_custom_call" | custom-call | flops 200000000 | bytes 1245184 | tf_op jit(solution)/shard_map/pallas_call | solution.py:258
  (43 shorter events, 5.2 us)
Async XLA Ops:
  0.0 32.2 %collective-permute-start.8 = (bf16[3,1024,256]{2,1,0:T(8,128)(2,1)}, bf16[3,1024,256]{2,1,0:T(8,128)(2,1)S(1)}, u32[]{:S(2)}, u32[]{:S(2)}) collective-permute-start(bf16[3,1024,256]{2,1,0:T(8,128)(2,1)} %bitcast.9), channel_id=1, source_target_pairs={{0,1},{1,0},{2,3},{3,2},{4,5},{5,4},{6,7},{7,6},{8,9},{9,8},{10,11... | collective-permute-start | bytes 4718600 | tf_op jit(solution)/shard_map/ppermute | solution.py:280
  4.3 27.1 %copy-start = (bf16[256,1024]{1,0:T(8,128)(2,1)S(1)}, bf16[256,1024]{1,0:T(8,128)(2,1)}, u32[]{:S(2)}) copy-start(bf16[256,1024]{1,0:T(8,128)(2,1)} %w0.1) | copy-start | bytes 1572868
  4.3 9.2 %collective-permute-start.5 = (bf16[128,1024]{1,0:T(8,128)(2,1)S(1)}, bf16[128,1024]{1,0:T(8,128)(2,1)S(1)}, u32[]{:S(2)}, u32[]{:S(2)}) collective-permute-start(bf16[128,1024]{1,0:T(8,128)(2,1)S(1)} %get-tuple-element.45), channel_id=1, source_target_pairs={{0,18},{1,19},{2,16},{3,17},{4,22},{5,23},{6,20},{7,21},{8,26},{9,... | collective-permute-start | bytes 786440 | tf_op jit(solution)/shard_map/ppermute | solution.py:280
  5.2 9.2 %collective-permute-start.4 = (bf16[128,1024]{1,0:T(8,128)(2,1)S(1)}, bf16[128,1024]{1,0:T(8,128)(2,1)S(1)}, u32[]{:S(2)}, u32[]{:S(2)}) collective-permute-start(bf16[128,1024]{1,0:T(8,128)(2,1)S(1)} %get-tuple-element.46), channel_id=1, source_target_pairs={{0,2},{1,3},{2,0},{3,1},{4,6},{5,7},{6,4},{7,5},{8,10},{9,11},{10,... | collective-permute-start | bytes 786440 | tf_op jit(solution)/shard_map/ppermute | solution.py:280
  5.2 26.3 %collective-permute-start.3 = (bf16[256,1024]{1,0:T(8,128)(2,1)}, bf16[256,1024]{1,0:T(8,128)(2,1)S(1)}, u32[]{:S(2)}, u32[]{:S(2)}) collective-permute-start(bf16[256,1024]{1,0:T(8,128)(2,1)} %w0.1), channel_id=1, source_target_pairs={{0,1},{1,0},{2,3},{3,2},{4,5},{5,4},{6,7},{7,6},{8,9},{9,8},{10,11... | collective-permute-start | bytes 1572872 | tf_op jit(solution)/shard_map/ppermute | solution.py:280
  13.6 17.9 %collective-permute-start.7 = (bf16[128,1024]{1,0:T(8,128)(2,1)S(1)}, bf16[128,1024]{1,0:T(8,128)(2,1)S(1)}, u32[]{:S(2)}, u32[]{:S(2)}) collective-permute-start(bf16[128,1024]{1,0:T(8,128)(2,1)S(1)} %collective-permute-done.5.w2b), channel_id=1, source_target_pairs={{0,1},{1,0},{2,3},{3,2},{4,5},{5,4},{6,7},{7,6},{8,9},{9,8},{10,11... | collective-permute-start | bytes 786440 | tf_op jit(solution)/shard_map/ppermute | solution.py:280
  14.3 17.1 %collective-permute-start.6 = (bf16[128,1024]{1,0:T(8,128)(2,1)S(1)}, bf16[128,1024]{1,0:T(8,128)(2,1)S(1)}, u32[]{:S(2)}, u32[]{:S(2)}) collective-permute-start(bf16[128,1024]{1,0:T(8,128)(2,1)S(1)} %collective-permute-done.4.w2a), channel_id=1, source_target_pairs={{0,1},{1,0},{2,3},{3,2},{4,5},{5,4},{6,7},{7,6},{8,9},{9,8},{10,11... | collective-permute-start | bytes 786440 | tf_op jit(solution)/shard_map/ppermute | solution.py:280
  14.3 1.4 %copy-start.4 = (bf16[1024,3,256]{2,0,1:T(8,128)(2,1)S(1)}, bf16[1024,3,256]{2,0,1:T(8,128)(2,1)}, u32[]{:S(2)}) copy-start(bf16[1024,3,256]{2,0,1:T(8,128)(2,1)} %param.9) | copy-start | bytes 4718596
  17.5 15.1 %copy-start.2 = (bf16[1024,1024]{1,0:T(8,128)(2,1)S(1)}, bf16[1024,1024]{1,0:T(8,128)(2,1)}, u32[]{:S(2)}) copy-start(bf16[1024,1024]{1,0:T(8,128)(2,1)} %d0) | copy-start | bytes 6291460
  21.2 11.0 %copy-start.1 = (bf16[1024,1024]{1,0:T(8,128)(2,1)S(1)}, bf16[1024,1024]{1,0:T(8,128)(2,1)}, u32[]{:S(2)}) copy-start(bf16[1024,1024]{1,0:T(8,128)(2,1)} %u0) | copy-start | bytes 6291460
  21.2 11.6 %copy-start.3 = (bf16[256,1024]{1,0:T(8,128)(2,1)S(1)}, bf16[256,1024]{1,0:T(8,128)(2,1)}, u32[]{:S(2)}) copy-start(bf16[256,1024]{1,0:T(8,128)(2,1)} %w0.2) | copy-start | bytes 1572868
  21.2 3.4 %collective-permute-start.1 = (bf16[160,256]{1,0:T(8,128)(2,1)S(1)}, bf16[160,256]{1,0:T(8,128)(2,1)S(1)}, u32[]{:S(2)}, u32[]{:S(2)}) collective-permute-start(bf16[160,256]{1,0:T(8,128)(2,1)S(1)} %get-tuple-element.25.o0), channel_id=1, source_target_pairs={{0,2},{1,3},{2,0},{3,1},{4,6},{5,7},{6,4},{7,5},{8,10},{9,11},{10,... | collective-permute-start | bytes 245768 | tf_op jit(solution)/shard_map/ppermute | solution.py:280
  24.6 3.9 %collective-permute-start.2 = (bf16[160,256]{1,0:T(8,128)(2,1)S(1)}, bf16[160,256]{1,0:T(8,128)(2,1)S(1)}, u32[]{:S(2)}, u32[]{:S(2)}) collective-permute-start(bf16[160,256]{1,0:T(8,128)(2,1)S(1)} %get-tuple-element.26), channel_id=1, source_target_pairs={{0,3},{1,2},{2,1},{3,0},{4,7},{5,6},{6,5},{7,4},{8,11},{9,10},{10,... | collective-permute-start | bytes 245768 | tf_op jit(solution)/shard_map/ppermute | solution.py:280
  28.5 2.6 %collective-permute-start = (bf16[160,256]{1,0:T(8,128)(2,1)S(1)}, bf16[160,256]{1,0:T(8,128)(2,1)S(1)}, u32[]{:S(2)}, u32[]{:S(2)}) collective-permute-start(bf16[160,256]{1,0:T(8,128)(2,1)S(1)} %get-tuple-element.26), channel_id=1, source_target_pairs={{0,1},{1,0},{2,3},{3,2},{4,5},{5,4},{6,7},{7,6},{8,9},{9,8},{10,11... | collective-permute-start | bytes 245768 | tf_op jit(solution)/shard_map/ppermute | solution.py:280
  31.1 1.2 %collective-permute-start.9 = (f32[2,4,37]{2,1,0:T(4,128)S(1)}, f32[2,4,37]{2,1,0:T(4,128)S(1)}, u32[]{:S(2)}, u32[]{:S(2)}) collective-permute-start(f32[2,4,37]{2,1,0:T(4,128)S(1)} %copy-done.7), channel_id=1, source_target_pairs={{0,1},{1,0},{2,3},{3,2},{4,5},{5,4},{6,7},{7,6},{8,9},{9,8},{10,11... | collective-permute-start | bytes 3560 | tf_op jit(solution)/shard_map/ppermute | solution.py:280
  32.3 46.7 %collective-permute-start.17 = (bf16[1024,1024]{1,0:T(8,128)(2,1)S(1)}, bf16[1024,1024]{1,0:T(8,128)(2,1)S(1)}, u32[]{:S(2)}, u32[]{:S(2)}) collective-permute-start(bf16[1024,1024]{1,0:T(8,128)(2,1)S(1)} %copy-done.1), channel_id=1, source_target_pairs={{0,1},{1,0},{2,3},{3,2},{4,5},{5,4},{6,7},{7,6},{8,9},{9,8},{10,11... | collective-permute-start | bytes 6291464 | tf_op jit(solution)/shard_map/ppermute | solution.py:280
  32.6 46.4 %collective-permute-start.18 = (bf16[1024,1024]{1,0:T(8,128)(2,1)S(1)}, bf16[1024,1024]{1,0:T(8,128)(2,1)S(1)}, u32[]{:S(2)}, u32[]{:S(2)}) collective-permute-start(bf16[1024,1024]{1,0:T(8,128)(2,1)S(1)} %copy-done.2), channel_id=1, source_target_pairs={{0,1},{1,0},{2,3},{3,2},{4,5},{5,4},{6,7},{7,6},{8,9},{9,8},{10,11... | collective-permute-start | bytes 6291464 | tf_op jit(solution)/shard_map/ppermute | solution.py:280
  32.8 13.2 %collective-permute-start.15 = (bf16[256,1024]{1,0:T(8,128)(2,1)S(1)}, bf16[256,1024]{1,0:T(8,128)(2,1)S(1)}, u32[]{:S(2)}, u32[]{:S(2)}) collective-permute-start(bf16[256,1024]{1,0:T(8,128)(2,1)S(1)} %copy-done.3), channel_id=1, source_target_pairs={{0,2},{1,3},{2,0},{3,1},{4,6},{5,7},{6,4},{7,5},{8,10},{9,11},{10,... | collective-permute-start | bytes 1572872 | tf_op jit(solution)/shard_map/ppermute | solution.py:280
  33.3 45.7 %collective-permute-start.14 = (bf16[256,1024]{1,0:T(8,128)(2,1)S(1)}, bf16[256,1024]{1,0:T(8,128)(2,1)S(1)}, u32[]{:S(2)}, u32[]{:S(2)}) collective-permute-start(bf16[256,1024]{1,0:T(8,128)(2,1)S(1)} %copy-done.3), channel_id=1, source_target_pairs={{0,1},{1,0},{2,3},{3,2},{4,5},{5,4},{6,7},{7,6},{8,9},{9,8},{10,11... | collective-permute-start | bytes 1572872 | tf_op jit(solution)/shard_map/ppermute | solution.py:280
  46.0 33.0 %collective-permute-start.16 = (bf16[256,1024]{1,0:T(8,128)(2,1)S(1)}, bf16[256,1024]{1,0:T(8,128)(2,1)S(1)}, u32[]{:S(2)}, u32[]{:S(2)}) collective-permute-start(bf16[256,1024]{1,0:T(8,128)(2,1)S(1)} %collective-permute-done.15.w2), channel_id=1, source_target_pairs={{0,1},{1,0},{2,3},{3,2},{4,5},{5,4},{6,7},{7,6},{8,9},{9,8},{10,11... | collective-permute-start | bytes 1572872 | tf_op jit(solution)/shard_map/ppermute | solution.py:280
  47.1 7.7 %collective-permute-start.10 = (bf16[40,1024]{1,0:T(8,128)(2,1)S(1)}, bf16[40,1024]{1,0:T(8,128)(2,1)S(1)}, u32[]{:S(2)}, u32[]{:S(2)}) collective-permute-start(bf16[40,1024]{1,0:T(8,128)(2,1)S(1)} %get-tuple-element.33), channel_id=1, source_target_pairs={{0,224},{1,225},{2,226},{3,227},{4,228},{5,229},{6,230},{7,231},{8... | collective-permute-start | bytes 245768 | tf_op jit(solution)/shard_map/ppermute | solution.py:280
  54.8 4.5 %collective-permute-start.11 = (bf16[40,1024]{1,0:T(8,128)(2,1)S(1)}, bf16[40,1024]{1,0:T(8,128)(2,1)S(1)}, u32[]{:S(2)}, u32[]{:S(2)}) collective-permute-start(bf16[40,1024]{1,0:T(8,128)(2,1)S(1)} %get-tuple-element.34), channel_id=1, source_target_pairs={{0,30},{1,31},{2,28},{3,29},{4,0},{5,1},{6,2},{7,3},{8,4},{9,5},{1... | collective-permute-start | bytes 245768 | tf_op jit(solution)/shard_map/ppermute | solution.py:280
  59.3 9.7 %collective-permute-start.12 = (bf16[40,1024]{1,0:T(8,128)(2,1)S(1)}, bf16[40,1024]{1,0:T(8,128)(2,1)S(1)}, u32[]{:S(2)}, u32[]{:S(2)}) collective-permute-start(bf16[40,1024]{1,0:T(8,128)(2,1)S(1)} %get-tuple-element.35), channel_id=1, source_target_pairs={{0,254},{1,255},{2,252},{3,253},{4,224},{5,225},{6,226},{7,227},{8... | collective-permute-start | bytes 245768 | tf_op jit(solution)/shard_map/ppermute | solution.py:280
  69.0 1.4 %copy-start.5 = (bf16[1024,3,256]{2,0,1:T(8,128)(2,1)S(1)}, bf16[1024,3,256]{2,0,1:T(8,128)(2,1)}, u32[]{:S(2)}) copy-start(bf16[1024,3,256]{2,0,1:T(8,128)(2,1)} %param.10) | copy-start | bytes 4718596
  74.7 4.3 %collective-permute-start.13 = (bf16[160,512]{1,0:T(8,128)(2,1)S(1)}, bf16[160,512]{1,0:T(8,128)(2,1)S(1)}, u32[]{:S(2)}, u32[]{:S(2)}) collective-permute-start(bf16[160,512]{1,0:T(8,128)(2,1)S(1)} %shard_map.84.mine), channel_id=1, source_target_pairs={{0,2},{1,3},{2,0},{3,1},{4,6},{5,7},{6,4},{7,5},{8,10},{9,11},{10,... | collective-permute-start | bytes 491528 | tf_op jit(solution)/shard_map/ppermute | solution.py:280
  81.3 5.7 %collective-permute-start.19 = (bf16[40,1024]{1,0:T(8,128)(2,1)S(1)}, bf16[40,1024]{1,0:T(8,128)(2,1)S(1)}, u32[]{:S(2)}, u32[]{:S(2)}) collective-permute-start(bf16[40,1024]{1,0:T(8,128)(2,1)S(1)} %get-tuple-element.42), channel_id=1, source_target_pairs={{0,2},{1,3},{2,0},{3,1},{4,6},{5,7},{6,4},{7,5},{8,10},{9,11},{10,... | collective-permute-start | bytes 245768 | tf_op jit(solution)/shard_map/ppermute | solution.py:280
  81.4 5.6 %collective-permute-start.20 = (bf16[40,1024]{1,0:T(8,128)(2,1)S(1)}, bf16[40,1024]{1,0:T(8,128)(2,1)S(1)}, u32[]{:S(2)}, u32[]{:S(2)}) collective-permute-start(bf16[40,1024]{1,0:T(8,128)(2,1)S(1)} %get-tuple-element.43), channel_id=1, source_target_pairs={{0,1},{1,0},{2,3},{3,2},{4,5},{5,4},{6,7},{7,6},{8,9},{9,8},{10,11... | collective-permute-start | bytes 245768 | tf_op jit(solution)/shard_map/ppermute | solution.py:280
  85.4 5.2 %collective-permute-start.21 = (bf16[40,1024]{1,0:T(8,128)(2,1)S(1)}, bf16[40,1024]{1,0:T(8,128)(2,1)S(1)}, u32[]{:S(2)}, u32[]{:S(2)}) collective-permute-start(bf16[40,1024]{1,0:T(8,128)(2,1)S(1)} %get-tuple-element.44), channel_id=1, source_target_pairs={{0,3},{1,2},{2,1},{3,0},{4,7},{5,6},{6,5},{7,4},{8,11},{9,10},{10,... | collective-permute-start | bytes 245768 | tf_op jit(solution)/shard_map/ppermute | solution.py:280
  90.7 7.6 %collective-permute-start.24 = (bf16[80,1024]{1,0:T(8,128)(2,1)S(1)}, bf16[80,1024]{1,0:T(8,128)(2,1)S(1)}, u32[]{:S(2)}, u32[]{:S(2)}) collective-permute-start(bf16[80,1024]{1,0:T(8,128)(2,1)S(1)} %shard_map.86), channel_id=1, source_target_pairs={{0,2},{1,39},{2,32},{3,5},{4,6},{5,43},{6,36},{7,9},{8,10},{9,47},... | collective-permute-start | bytes 491528 | tf_op jit(solution)/shard_map/ppermute | solution.py:280
  90.8 12.3 %collective-permute-start.22 = (bf16[80,1024]{1,0:T(8,128)(2,1)S(1)}, bf16[80,1024]{1,0:T(8,128)(2,1)S(1)}, u32[]{:S(2)}, u32[]{:S(2)}) collective-permute-start(bf16[80,1024]{1,0:T(8,128)(2,1)S(1)} %shard_map.86), channel_id=1, source_target_pairs={{0,0},{1,37},{2,34},{3,7},{4,4},{5,41},{6,38},{7,11},{8,8},{9,45},... | collective-permute-start | bytes 491528 | tf_op jit(solution)/shard_map/ppermute | solution.py:280
  98.2 4.8 %collective-permute-start.25 = (bf16[80,1024]{1,0:T(8,128)(2,1)S(1)}, bf16[80,1024]{1,0:T(8,128)(2,1)S(1)}, u32[]{:S(2)}, u32[]{:S(2)}) collective-permute-start(bf16[80,1024]{1,0:T(8,128)(2,1)S(1)} %collective-permute-done.24.r2), channel_id=1, source_target_pairs={{0,1},{1,0},{2,3},{3,2},{4,5},{5,4},{6,7},{7,6},{8,9},{9,8},{10,11... | collective-permute-start | bytes 491528 | tf_op jit(solution)/shard_map/ppermute | solution.py:280
  103.1 1.4 %collective-permute-start.23 = (bf16[80,1024]{1,0:T(8,128)(2,1)S(1)}, bf16[80,1024]{1,0:T(8,128)(2,1)S(1)}, u32[]{:S(2)}, u32[]{:S(2)}) collective-permute-start(bf16[80,1024]{1,0:T(8,128)(2,1)S(1)} %collective-permute-done.22.r0), channel_id=1, source_target_pairs={{0,1},{1,0},{2,3},{3,2},{4,5},{5,4},{6,7},{7,6},{8,9},{9,8},{10,11... | collective-permute-start | bytes 491528 | tf_op jit(solution)/shard_map/ppermute | solution.py:280
  (2 other events, 1.8 us)

commit v3 on v2

--- a/solution.py
+++ b/solution.py
@@ -125,10 +125,25 @@
     return jnp.where(low_q, outs[0], outs[1]).astype(jnp.bfloat16)
 
 
-def first_kernel(tokens, weight, table, keep, give, base):
+def fetch(source, held, sems):
+    copies = [pltpu.make_async_copy(source.at[p], held.at[p], sems.at[p]) for p in range(3)]
+    for copy in copies:
+        copy.start()
+    return copies
+
+
+def first_kernel(tokens_ref, weight_ref, table_ref, keep, give, base, weight, sems, tokens, table, more):
     core = core_index()
+    load = pltpu.make_async_copy(tokens_ref, tokens, more.at[0])
+    load.start()
+    copies = fetch(weight_ref, weight, sems)
+    copies.append(pltpu.make_async_copy(table_ref, table, more.at[1]))
+    copies[-1].start()
+    load.wait()
     floats = tokens[...].astype(jnp.float32).reshape(PATCH, -1)
     xn = normalize(floats)
+    for copy in copies:
+        copy.wait()
     q = (dot(xn, weight[0]) * HD**-0.5).astype(jnp.bfloat16)
     k = dot(xn, weight[1]).astype(jnp.bfloat16)
     v = dot(xn, weight[2]).astype(jnp.bfloat16)
@@ -163,11 +178,24 @@
     base[...] = dot(one_hot(lanes == place), floats.astype(jnp.bfloat16)).astype(jnp.bfloat16)
 
 
-def residual_kernel(o0, o1, o2, o3, w0, w1, w2a, w2b, w3a, w3b, base, *outs):
-    total = dot(o0[...], w0[...]) + dot(o1[...], w1[...])
-    total = total + dot(o2[:, :128], w2a[...]) + dot(o2[:, 128:], w2b[...])
-    total = total + dot(o3[:, :128], w3a[...]) + dot(o3[:, 128:], w3b[...])
-    first = base[...].astype(jnp.float32) + total.astype(jnp.bfloat16).astype(jnp.float32)
+def partial_kernel(o1, w0, w1, o0_ref, base_ref, out, base_out, o0, base, sems):
+    loads = [pltpu.make_async_copy(o0_ref, o0, sems.at[0]), pltpu.make_async_copy(base_ref, base, sems.at[1])]
+    for load in loads:
+        load.start()
+    total = dot(o1[...], w1[...])
+    loads[0].wait()
+    out[...] = (total + dot(o0[...], w0[...])).astype(jnp.bfloat16)
+    loads[1].wait()
+    base_out[...] = base[...]
+
+
+def branch_sum(mine, other):
+    total = mine[...].astype(jnp.float32) + other[...].astype(jnp.float32)
+    return total.astype(jnp.bfloat16).astype(jnp.float32)
+
+
+def residual_kernel(mine, other, base, *outs):
+    first = base[...].astype(jnp.float32) + branch_sum(mine, other)
     for q in range(4):
         outs[q][...] = first[q * ROWS : (q + 1) * ROWS].astype(jnp.bfloat16)
 
@@ -176,7 +204,14 @@
     return jnp.concatenate([p[...].astype(jnp.float32) for p in pieces], axis=0)
 
 
-def second_kernel(p0, p1, p2, p3, w_own, w_sib, t_own, t_sib, out):
+def second_kernel(p0, p1, p2, p3, w_sib, o0, o1, w_ref, t_own_ref, t_sib_ref, out, w_own, sems, t_own, t_sib, more):
+    copies = fetch(w_ref, w_own, sems)
+    loads = [
+        pltpu.make_async_copy(t_own_ref, t_own, more.at[0]),
+        pltpu.make_async_copy(t_sib_ref, t_sib, more.at[1]),
+    ]
+    for load in loads:
+        load.start()
     xn = normalize(joined((p0, p1, p2, p3)))
     quad, slot, level, row, col = kept_place(iota((KEPT, 1), 0))
     row, col = row + 3 * (quad & 1), col + 3 * (quad & 2)
@@ -189,7 +224,13 @@
     ban_row = (j >= F_Y) & (j < F_Y + WY) & ((j >= F_Y + SY) != (row >= SY))
     ban = jnp.where(ban_level, split_levels.astype(jnp.int32), jnp.where(ban_row, split_rows.astype(jnp.int32), 0))
     ban = jnp.where((lane & FEAT) == 0, ban, 0) == 1
-    for part, (weight, table) in enumerate(((w_own, t_own), (w_sib, t_sib))):
+    for load in loads:
+        load.wait()
+    total = None
+    for weight, table, project in ((w_sib, t_sib, o1), (w_own, t_own, o0)):
+        if weight is w_own:
+            for copy in copies:
+                copy.wait()
         q = (dot(xn, weight[0]) * HD**-0.5).astype(jnp.bfloat16)
         k = dot(xn, weight[1]).astype(jnp.bfloat16)
         v = dot(xn, weight[2]).astype(jnp.bfloat16)
@@ -197,8 +238,10 @@
             cols = slice(pair * 128, pair * 128 + 128)
             extra = dot(feat[:, :FEAT], bias_rows(table, 1, pair))
             extra = jnp.where(ban, NEG, extra).astype(jnp.bfloat16)
-            start = part * 256 + pair * 128
-            out[:, start : start + 128] = pair_heads(q[:, cols], k[:, cols], v[:, cols], extra, feat)
+            mixed = pair_heads(q[:, cols], k[:, cols], v[:, cols], extra, feat)
+            term = dot(mixed, project[cols, :])
+            total = term if total is None else total + term
+    out[...] = total.astype(jnp.bfloat16)
 
 
 def gelu(x):
@@ -209,11 +252,9 @@
     return jnp.where(member == 0, 0, jnp.where(member == 1, 3, member - 1))
 
 
-def mlp_kernel(mine, other, w0, w1, w2, w3, p0, p1, p2, p3, u0, u1, d0, d1, *refs):
+def mlp_kernel(mine, other, p0, p1, p2, p3, u0, u1, d0, d1, *refs):
     outs, held = refs[:4], refs[4]
-    total = dot(mine[:, :256], w0[...]) + dot(mine[:, 256:], w1[...])
-    total = total + dot(other[:, :256], w2[...]) + dot(other[:, 256:], w3[...])
-    second = joined((p0, p1, p2, p3)) + total.astype(jnp.bfloat16).astype(jnp.float32)
+    second = joined((p0, p1, p2, p3)) + branch_sum(mine, other)
     second = second.astype(jnp.bfloat16).astype(jnp.float32)
     xn = normalize(second)
     h0 = gelu(dot(xn, u0[...])).astype(jnp.bfloat16)
@@ -250,30 +291,30 @@
     out[...] = total.reshape(out.shape).astype(jnp.bfloat16)
 
 
-def call(kernel, outs, operands, flops, limit, tables=(), scratch=()):
+def call(kernel, outs, operands, flops, limit, large=(), scratch=()):
     shapes = [jax.ShapeDtypeStruct(s, jnp.bfloat16) for s in outs]
+    operands = (*operands, *large)
     moved = sum(o.size * o.dtype.itemsize for o in operands) + sum(2 * s.size for s in shapes)
     vmem = pl.BlockSpec(memory_space=pltpu.VMEM)
-    smem = pl.BlockSpec(memory_space=pltpu.SMEM)
+    plain = len(operands) - len(large)
     result = pl.pallas_call(
         kernel,
         out_shape=shapes,
-        in_specs=[vmem] * len(operands) + [smem] * len(tables),
+        in_specs=[vmem] * plain + [pl.BlockSpec(memory_space=pltpu.HBM)] * len(large),
         out_specs=[vmem] * len(shapes),
         scratch_shapes=scratch,
         compiler_params=pltpu.CompilerParams(vmem_limit_bytes=limit * MIB),
         cost_estimate=pl.CostEstimate(flops=flops, bytes_accessed=moved, transcendentals=0),
-    )(*operands, *tables)
+    )(*operands)
     return result if len(result) > 1 else result[0]
 
 
-def tied(values, after):
-    return lax.optimization_barrier((tuple(values), tuple(after)))[0]
+def tied(*values):
+    return lax.optimization_barrier(values)
 
 
 def body(counts, tokens, qkv_first, qkv_second, out_first, out_second, rel_tables, up_weight, down_weight):
     levels, rows, cols, width = tokens.shape
-    half = out_first.shape[0] // 2
     turn = counts[1] // 2
 
     def move(value, target):
@@ -287,40 +328,42 @@
 
     def far_swap(value):
         return move(value, lambda a, b, m: (a, b, m ^ 3))
-
-    def side_swap(value):
-        return move(value, lambda a, b, m: (a, b + turn, m ^ 2))
 
     offsets = ((0, 0), (1, 0), (0, 1), (1, 1))
     pieces = [(ROWS, width)] * 4
     halves = [(KEPT, 256)] * 2
+    own_qkv = [pltpu.VMEM((3, width, 256), jnp.bfloat16), pltpu.SemaphoreType.DMA((3,))]
+    table = pltpu.SMEM(rel_tables.shape, jnp.float32)
+    two = pltpu.SemaphoreType.DMA((2,))
 
     tok = tokens.transpose(1, 2, 0, 3).reshape(rows * cols, levels, width)
     w_first = qkv_first.transpose(1, 0, 2)
     w_second = qkv_second.transpose(1, 0, 2)
 
-    f2a = chip_swap(out_first[:half])
-    f2b = side_swap(out_first[half:])
     f1 = core_swap(out_first)
+    s1 = core_swap(out_second)
+    w_sib = core_swap(w_second)
+    s_table = core_swap(rel_tables)
     keep, give, base = call(
-        first_kernel, halves + [(KEPT, width)], (tok, w_first), 10**9, 24, tables=(rel_tables,)
-    )
-    from_far = far_swap(give)
-    from_chip = chip_swap(keep)
-    from_core = core_swap(give)
-    f3a = core_swap(f2a)
-    f3b = core_swap(f2b)
-    s_table = core_swap(rel_tables)
-    w_sib = core_swap(w_second)
-
-    firsts = call(
-        residual_kernel,
-        pieces,
-        (keep, from_core, from_chip, from_far, out_first, f1, f2a, f2b, f3a, f3b, base),
-        5 * 10**8,
-        24,
-    )
-    *firsts, w_sib, s_table = tied((*firsts, w_sib, s_table), ())
+        first_kernel,
+        halves + [(KEPT, width)],
+        (),
+        10**9,
+        57,
+        large=(tok, w_first, rel_tables),
+        scratch=own_qkv + [pltpu.VMEM(tok.shape, jnp.bfloat16), table, two],
+    )
+    keep, give, f1, s1, w_sib, s_table = tied(keep, give, f1, s1, w_sib, s_table)
+    part, base = call(
+        partial_kernel,
+        [(KEPT, width)] * 2,
+        (core_swap(give), out_first, f1),
+        2 * 10**8,
+        8,
+        large=(keep, base),
+        scratch=[pltpu.VMEM((KEPT, 256), jnp.bfloat16), pltpu.VMEM((KEPT, width), jnp.bfloat16), two],
+    )
+    firsts = call(residual_kernel, pieces, (part, chip_swap(part), base), 10**6, 8)
     shifted = {0: firsts[0]}
     for q in (3, 2, 1):
         dy, dx = offsets[q]
@@ -330,34 +373,31 @@
 
         shifted[q] = move(firsts[q], target)
     shifted = [shifted[q] for q in range(4)]
-    out_second, up_weight, down_weight = tied((out_second, up_weight, down_weight), (w_sib,))
-    s2 = chip_swap(out_second)
-    s1 = core_swap(out_second)
+
+    part = call(
+        second_kernel,
+        [(KEPT, width)],
+        (*shifted, w_sib, out_second, s1),
+        10**9,
+        16,
+        large=(w_second, rel_tables, s_table),
+        scratch=own_qkv + [table, table, two],
+    )
+    part, up_weight, down_weight = tied(part, up_weight, down_weight)
     u1 = core_swap(up_weight)
     d1 = core_swap(down_weight)
-
-    mixed = call(
-        second_kernel,
-        [(KEPT, 512)],
-        (*shifted, w_second, w_sib),
-        10**9,
-        24,
-        tables=(rel_tables, s_table),
-    )
-    other = chip_swap(mixed)
-    s3 = core_swap(s2)
     own, to_core, to_chip, to_far = call(
         mlp_kernel,
         pieces,
-        (mixed, other, out_second, s1, s2, s3, *shifted, up_weight, u1, down_weight, d1),
+        (part, chip_swap(part), *shifted, up_weight, u1, down_weight, d1),
         2 * 10**9,
-        40,
+        24,
         scratch=[pltpu.VMEM((KEPT, width), jnp.float32)],
     )
     at_far = far_swap(to_far)
     at_chip = chip_swap(to_chip)
     at_core = core_swap(to_core)
-    done = call(sum_kernel, [(2 * ROWS, width)], (own, at_chip, at_core, at_far), 10**6, 16)
+    done = call(sum_kernel, [(2 * ROWS, width)], (own, at_chip, at_core, at_far), 10**6, 8)
 
     def home(flip):
         def target(a, b, m):
@@ -373,7 +413,7 @@
         [(rows * cols, levels, width)],
         (here, core_swap(here), there, core_swap(there)),
         2 * 10**8,
-        16,
+        12,
     )
     return result.reshape(rows, cols, levels, width).transpose(2, 0, 1, 3)
 

time: 106 us -> 76.5 us (0.72)
  starting transfers between devices: 36.5 us -> 22.4 us
  waiting for transfers between devices: 51.1 us -> 37.2 us
  local copies, waits for them, and re-layouts: 5.65 us -> 1.89 us
  Pallas kernels: 12.6 us -> 14.6 us
    ppermute x26 -> x19, starting transfers between devices: 36.5 us -> 22.4 us  [move(): return lax.ppermute(value, AXES, pairs(counts, target))]
    ppermute x26 -> x19, waiting for transfers between devices: 51.1 us -> 37.2 us  [move(): return lax.ppermute(value, AXES, pairs(counts, target))]
    unnamed x16, local copies, waits for them, and re-layouts: 4.59 us -> 1.89 us
    pallas_call x6 -> x7, Pallas kernels: 12.6 us -> 14.6 us  [call(): pl.pallas_call(kernel, out_shape=shapes, in_specs=[vmem] * plain + [pl.Bl...]
    slice x1 -> x0, local copies, waits for them, and re-layouts: 1.06 us -> none  [body(): f2b = side_swap(out_first[half:])]
  transfers between devices with their start and end apart: 26 -> 19, of which waited for: 14 -> 10; matrix products, arithmetic and copies ran while one was open for 1% -> 0% of each run, Pallas kernels for 8% -> 7%
where the time goes in v3:
time: 76.5 us; the launch traced here: 76.3 us
  waiting for transfers between devices  37.2 us (49%)
  starting transfers between devices  22.4 us (29%)
  Pallas kernels  14.6 us (19%)
  local copies, waits for them, and re-layouts  1.89 us (2%)
    ppermute x19, waiting for transfers between devices, move(): return lax.ppermute(value, AXES, pairs(counts, target))  37.2 us
    ppermute x19, starting transfers between devices, move(): return lax.ppermute(value, AXES, pairs(counts, target))  22.4 us
    pallas_call x7, Pallas kernels, call(): pl.pallas_call(kernel, out_shape=shapes, in_specs=[vmem] * plain + [pl.Bl...  14.6 us
    unnamed x16, local copies, waits for them, and re-layouts  1.89 us
  transfers between devices with their start and end apart: 19, of which 10 were waited for; matrix products, arithmetic and copies ran while one was open for 0% of the time, Pallas kernels for 7%

profile of v3, /device:TPU:1, one launch (start us, length us, event | category | flops | bytes accessed | tf_op | source)
XLA Modules:
  0.0 76.3 jit_solution(5769755386889705989)
XLA Ops:
  0.0 3.2 %collective-permute-start.2 = (bf16[3,1024,256]{2,1,0:T(8,128)(2,1)}, bf16[3,1024,256]{2,1,0:T(8,128)(2,1)S(1)}, u32[]{:S(2)}, u32[]{:S(2)}) collective-permute-start(bf16[3,1024,256]{2,1,0:T(8,128)(2,1)} %bitcast.8), channel_id=1, source_target_pairs={{0,1},{1,0},{2,3},{3,2},{4,5},{5,4},{6,7},{7,6},{8,9},{9,8},{10,11... | collective-permute-start | bytes 4718600 | tf_op jit(solution)/shard_map/ppermute | solution.py:321
  3.2 0.5 collective-permute-start.1
  3.8 5.3 %shard_map.82 = (bf16[160,256]{1,0:T(8,128)(2,1)}, bf16[160,256]{1,0:T(8,128)(2,1)}, bf16[160,1024]{1,0:T(8,128)(2,1)}) custom-call(bf16[72,4,1024]{2,1,0:T(4,128)(2,1)} %bitcast.11, bf16[3,1024,256]{2,1,0:T(8,128)(2,1)} %bitcast.10, f32[2,4,37]{2,1,0:T(4,128)} %t_own_ref.1), custom_call_target="tpu_custom_call" | custom-call | flops 1000000000 | bytes 2655392 | tf_op jit(solution)/shard_map/pallas_call | solution.py:300
  9.1 0.6 collective-permute-start.4
  9.7 1.1 %collective-permute-done.4.o1 = bf16[160,256]{1,0:T(8,128)(2,1)S(1)} collective-permute-done((bf16[160,256]{1,0:T(8,128)(2,1)}, bf16[160,256]{1,0:T(8,128)(2,1)S(1)}, u32[]{:S(2)}, u32[]{:S(2)}) %collective-permute-start.4) | collective-permute-done | bytes 81952 | tf_op jit(solution)/shard_map/ppermute | solution.py:321
  10.8 1.0 %copy-done.5 = bf16[160,1024]{1,0:T(8,128)(2,1)S(1)} copy-done((bf16[160,1024]{1,0:T(8,128)(2,1)S(1)}, bf16[160,1024]{1,0:T(8,128)(2,1)}, u32[]{:S(2)}) %copy-start.5) | copy-done | bytes 327704
  11.8 0.9 %copy-done.6 = bf16[160,256]{1,0:T(8,128)(2,1)S(1)} copy-done((bf16[160,256]{1,0:T(8,128)(2,1)S(1)}, bf16[160,256]{1,0:T(8,128)(2,1)}, u32[]{:S(2)}) %copy-start.6) | copy-done | bytes 81944
  12.7 0.6 shard_map.83
  13.3 0.1 collective-permute-start.5
  13.4 8.9 %collective-permute-done.5.other = bf16[160,1024]{1,0:T(8,128)(2,1)S(1)} collective-permute-done((bf16[160,1024]{1,0:T(8,128)(2,1)S(1)}, bf16[160,1024]{1,0:T(8,128)(2,1)S(1)}, u32[]{:S(2)}, u32[]{:S(2)}) %collective-permute-start.5) | collective-permute-done | bytes 327712 | tf_op jit(solution)/shard_map/ppermute | solution.py:321
  22.3 0.2 shard_map.84
  22.5 3.9 %collective-permute-start.6 = (bf16[40,1024]{1,0:T(8,128)(2,1)S(1)}, bf16[40,1024]{1,0:T(8,128)(2,1)S(1)}, u32[]{:S(2)}, u32[]{:S(2)}) collective-permute-start(bf16[40,1024]{1,0:T(8,128)(2,1)S(1)} %get-tuple-element.36), channel_id=1, source_target_pairs={{0,224},{1,225},{2,226},{3,227},{4,228},{5,229},{6,230},{7,231},{8... | collective-permute-start | bytes 245768 | tf_op jit(solution)/shard_map/ppermute | solution.py:321
  26.4 4.9 %collective-permute-start.7 = (bf16[40,1024]{1,0:T(8,128)(2,1)S(1)}, bf16[40,1024]{1,0:T(8,128)(2,1)S(1)}, u32[]{:S(2)}, u32[]{:S(2)}) collective-permute-start(bf16[40,1024]{1,0:T(8,128)(2,1)S(1)} %get-tuple-element.37), channel_id=1, source_target_pairs={{0,30},{1,31},{2,28},{3,29},{4,0},{5,1},{6,2},{7,3},{8,4},{9,5},{1... | collective-permute-start | bytes 245768 | tf_op jit(solution)/shard_map/ppermute | solution.py:321
  31.3 0.9 %collective-permute-start.8 = (bf16[40,1024]{1,0:T(8,128)(2,1)S(1)}, bf16[40,1024]{1,0:T(8,128)(2,1)S(1)}, u32[]{:S(2)}, u32[]{:S(2)}) collective-permute-start(bf16[40,1024]{1,0:T(8,128)(2,1)S(1)} %get-tuple-element.38), channel_id=1, source_target_pairs={{0,254},{1,255},{2,252},{3,253},{4,224},{5,225},{6,226},{7,227},{8... | collective-permute-start | bytes 245768 | tf_op jit(solution)/shard_map/ppermute | solution.py:321
  32.2 0.6 collective-permute-done.7.p2
  32.8 2.7 %collective-permute-done.8.p3 = bf16[40,1024]{1,0:T(8,128)(2,1)S(1)} collective-permute-done((bf16[40,1024]{1,0:T(8,128)(2,1)S(1)}, bf16[40,1024]{1,0:T(8,128)(2,1)S(1)}, u32[]{:S(2)}, u32[]{:S(2)}) %collective-permute-start.8) | collective-permute-done | bytes 81952 | tf_op jit(solution)/shard_map/ppermute | solution.py:321
  35.5 5.0 %shard_map.85.mine = bf16[160,1024]{1,0:T(8,128)(2,1)S(1)} custom-call(bf16[40,1024]{1,0:T(8,128)(2,1)S(1)} %get-tuple-element.35.p0, bf16[40,1024]{1,0:T(8,128)(2,1)S(1)} %collective-permute-done.6.p1, bf16[40,1024]{1,0:T(8,128)(2,1)S(1)} %collective-permute-done.7.p2, bf16[40,1024]{1,0:T(8,128)(2,1)S(1)} %collective-permute-done.8.p3, ...), custom_call_target="tpu_custom_call" | custom-call | flops 1000000000 | bytes 4852032 | tf_op jit(solution)/shard_map/pallas_call | solution.py:300
  40.6 3.2 %collective-permute-start.10 = (bf16[1024,1024]{1,0:T(8,128)(2,1)S(1)}, bf16[1024,1024]{1,0:T(8,128)(2,1)S(1)}, u32[]{:S(2)}, u32[]{:S(2)}) collective-permute-start(bf16[1024,1024]{1,0:T(8,128)(2,1)S(1)} %copy-done), channel_id=1, source_target_pairs={{0,1},{1,0},{2,3},{3,2},{4,5},{5,4},{6,7},{7,6},{8,9},{9,8},{10,11... | collective-permute-start | bytes 6291464 | tf_op jit(solution)/shard_map/ppermute | solution.py:321
  43.8 0.1 collective-permute-start.11
  43.9 8.9 %collective-permute-done.9.other = bf16[160,1024]{1,0:T(8,128)(2,1)S(1)} collective-permute-done((bf16[160,1024]{1,0:T(8,128)(2,1)S(1)}, bf16[160,1024]{1,0:T(8,128)(2,1)S(1)}, u32[]{:S(2)}, u32[]{:S(2)}) %collective-permute-start.9) | collective-permute-done | bytes 327712 | tf_op jit(solution)/shard_map/ppermute | solution.py:321
  52.8 1.9 %shard_map.86 = (bf16[40,1024]{1,0:T(8,128)(2,1)S(1)}, bf16[40,1024]{1,0:T(8,128)(2,1)S(1)}, bf16[40,1024]{1,0:T(8,128)(2,1)S(1)}, bf16[40,1024]{1,0:T(8,128)(2,1)S(1)}) custom-call(bf16[160,1024]{1,0:T(8,128)(2,1)S(1)} %shard_map.85.mine, bf16[160,1024]{1,0:T(8,128)(2,1)S(1)} %collective-permute-done.9.other, bf16[40,1024]{1,0:T(8,128)(2,1)S(1)} %get-tuple-element.35.p0, ...), custom_call_target="tpu_custom_call" | custom-call | flops 2000000000 | bytes 9699328 | tf_op jit(solution)/shard_map/pallas_call | solution.py:300
  54.7 0.2 collective-permute-start.12
  54.8 1.4 %collective-permute-start.13 = (bf16[40,1024]{1,0:T(8,128)(2,1)S(1)}, bf16[40,1024]{1,0:T(8,128)(2,1)S(1)}, u32[]{:S(2)}, u32[]{:S(2)}) collective-permute-start(bf16[40,1024]{1,0:T(8,128)(2,1)S(1)} %get-tuple-element.47), channel_id=1, source_target_pairs={{0,1},{1,0},{2,3},{3,2},{4,5},{5,4},{6,7},{7,6},{8,9},{9,8},{10,11... | collective-permute-start | bytes 245768 | tf_op jit(solution)/shard_map/ppermute | solution.py:321
  56.3 1.4 %collective-permute-start.14 = (bf16[40,1024]{1,0:T(8,128)(2,1)S(1)}, bf16[40,1024]{1,0:T(8,128)(2,1)S(1)}, u32[]{:S(2)}, u32[]{:S(2)}) collective-permute-start(bf16[40,1024]{1,0:T(8,128)(2,1)S(1)} %get-tuple-element.48), channel_id=1, source_target_pairs={{0,3},{1,2},{2,1},{3,0},{4,7},{5,6},{6,5},{7,4},{8,11},{9,10},{10,... | collective-permute-start | bytes 245768 | tf_op jit(solution)/shard_map/ppermute | solution.py:321
  57.6 0.4 collective-permute-done.12.far
  58.1 3.3 %collective-permute-done.14.far_sib = bf16[40,1024]{1,0:T(8,128)(2,1)S(1)} collective-permute-done((bf16[40,1024]{1,0:T(8,128)(2,1)S(1)}, bf16[40,1024]{1,0:T(8,128)(2,1)S(1)}, u32[]{:S(2)}, u32[]{:S(2)}) %collective-permute-start.14) | collective-permute-done | bytes 81952 | tf_op jit(solution)/shard_map/ppermute | solution.py:321
  61.4 0.1 collective-permute-start.17
  61.5 1.9 %collective-permute-start.15 = (bf16[80,1024]{1,0:T(8,128)(2,1)S(1)}, bf16[80,1024]{1,0:T(8,128)(2,1)S(1)}, u32[]{:S(2)}, u32[]{:S(2)}) collective-permute-start(bf16[80,1024]{1,0:T(8,128)(2,1)S(1)} %shard_map.87), channel_id=1, source_target_pairs={{0,0},{1,37},{2,34},{3,7},{4,4},{5,41},{6,38},{7,11},{8,8},{9,45},... | collective-permute-start | bytes 491528 | tf_op jit(solution)/shard_map/ppermute | solution.py:321
  63.4 5.5 %collective-permute-done.17.r2 = bf16[80,1024]{1,0:T(8,128)(2,1)S(1)} collective-permute-done((bf16[80,1024]{1,0:T(8,128)(2,1)S(1)}, bf16[80,1024]{1,0:T(8,128)(2,1)S(1)}, u32[]{:S(2)}, u32[]{:S(2)}) %collective-permute-start.17) | collective-permute-done | bytes 163872 | tf_op jit(solution)/shard_map/ppermute | solution.py:321
  69.0 4.3 %collective-permute-done.15.r0 = bf16[80,1024]{1,0:T(8,128)(2,1)S(1)} collective-permute-done((bf16[80,1024]{1,0:T(8,128)(2,1)S(1)}, bf16[80,1024]{1,0:T(8,128)(2,1)S(1)}, u32[]{:S(2)}, u32[]{:S(2)}) %collective-permute-start.15) | collective-permute-done | bytes 163872 | tf_op jit(solution)/shard_map/ppermute | solution.py:321
  73.3 1.4 %collective-permute-done.16.r1 = bf16[80,1024]{1,0:T(8,128)(2,1)S(1)} collective-permute-done((bf16[80,1024]{1,0:T(8,128)(2,1)S(1)}, bf16[80,1024]{1,0:T(8,128)(2,1)S(1)}, u32[]{:S(2)}, u32[]{:S(2)}) %collective-permute-start.16) | collective-permute-done | bytes 163872 | tf_op jit(solution)/shard_map/ppermute | solution.py:321
  74.7 1.6 %shard_map.88 = bf16[72,4,1024]{2,1,0:T(4,128)(2,1)} custom-call(bf16[80,1024]{1,0:T(8,128)(2,1)S(1)} %collective-permute-done.15.r0, bf16[80,1024]{1,0:T(8,128)(2,1)S(1)} %collective-permute-done.16.r1, bf16[80,1024]{1,0:T(8,128)(2,1)S(1)} %collective-permute-done.17.r2, bf16[80,1024]{1,0:T(8,128)(2,1)S(1)} %collective-permute-done.18.r3), custom_call_target="tpu_custom_call" | custom-call | flops 200000000 | bytes 1245184 | tf_op jit(solution)/shard_map/pallas_call | solution.py:300
  (29 shorter events, 0.1 us)
Async XLA Ops:
  0.0 10.8 %copy-start.3 = (bf16[256,1024]{1,0:T(8,128)(2,1)S(1)}, bf16[256,1024]{1,0:T(8,128)(2,1)}, u32[]{:S(2)}) copy-start(bf16[256,1024]{1,0:T(8,128)(2,1)} %w0.1) | copy-start | bytes 1572868
  0.0 9.1 %collective-permute-start.2 = (bf16[3,1024,256]{2,1,0:T(8,128)(2,1)}, bf16[3,1024,256]{2,1,0:T(8,128)(2,1)S(1)}, u32[]{:S(2)}, u32[]{:S(2)}) collective-permute-start(bf16[3,1024,256]{2,1,0:T(8,128)(2,1)} %bitcast.8), channel_id=1, source_target_pairs={{0,1},{1,0},{2,3},{3,2},{4,5},{5,4},{6,7},{7,6},{8,9},{9,8},{10,11... | collective-permute-start | bytes 4718600 | tf_op jit(solution)/shard_map/ppermute | solution.py:321
  3.2 5.8 %collective-permute-start = (bf16[256,1024]{1,0:T(8,128)(2,1)}, bf16[256,1024]{1,0:T(8,128)(2,1)S(1)}, u32[]{:S(2)}, u32[]{:S(2)}) collective-permute-start(bf16[256,1024]{1,0:T(8,128)(2,1)} %w0.1), channel_id=1, source_target_pairs={{0,1},{1,0},{2,3},{3,2},{4,5},{5,4},{6,7},{7,6},{8,9},{9,8},{10,11... | collective-permute-start | bytes 1572872 | tf_op jit(solution)/shard_map/ppermute | solution.py:321
  3.2 5.8 %collective-permute-start.1 = (bf16[256,1024]{1,0:T(8,128)(2,1)}, bf16[256,1024]{1,0:T(8,128)(2,1)S(1)}, u32[]{:S(2)}, u32[]{:S(2)}) collective-permute-start(bf16[256,1024]{1,0:T(8,128)(2,1)} %o0.1), channel_id=1, source_target_pairs={{0,1},{1,0},{2,3},{3,2},{4,5},{5,4},{6,7},{7,6},{8,9},{9,8},{10,11... | collective-permute-start | bytes 1572872 | tf_op jit(solution)/shard_map/ppermute | solution.py:321
  3.8 5.3 %collective-permute-start.3 = (f32[2,4,37]{2,1,0:T(4,128)}, f32[2,4,37]{2,1,0:T(4,128)S(1)}, u32[]{:S(2)}, u32[]{:S(2)}) collective-permute-start(f32[2,4,37]{2,1,0:T(4,128)} %t_own_ref.1), channel_id=1, source_target_pairs={{0,1},{1,0},{2,3},{3,2},{4,5},{5,4},{6,7},{7,6},{8,9},{9,8},{10,11... | collective-permute-start | bytes 3560 | tf_op jit(solution)/shard_map/ppermute | solution.py:321
  3.8 31.8 %copy-start.7 = (f32[2,4,37]{2,1,0:T(4,128)S(1)}, f32[2,4,37]{2,1,0:T(4,128)}, u32[]{:S(2)}) copy-start(f32[2,4,37]{2,1,0:T(4,128)} %t_own_ref.1) | copy-start | bytes 3556
  9.0 26.5 %copy-start.2 = (bf16[1024,3,256]{2,0,1:T(8,128)(2,1)S(1)}, bf16[1024,3,256]{2,0,1:T(8,128)(2,1)}, u32[]{:S(2)}) copy-start(bf16[1024,3,256]{2,0,1:T(8,128)(2,1)} %param.10) | copy-start | bytes 4718596
  9.0 26.5 %copy-start.4 = (bf16[256,1024]{1,0:T(8,128)(2,1)S(1)}, bf16[256,1024]{1,0:T(8,128)(2,1)}, u32[]{:S(2)}) copy-start(bf16[256,1024]{1,0:T(8,128)(2,1)} %o0.1) | copy-start | bytes 1572868
  9.1 1.7 %collective-permute-start.4 = (bf16[160,256]{1,0:T(8,128)(2,1)}, bf16[160,256]{1,0:T(8,128)(2,1)S(1)}, u32[]{:S(2)}, u32[]{:S(2)}) collective-permute-start(bf16[160,256]{1,0:T(8,128)(2,1)} %get-tuple-element.29), channel_id=1, source_target_pairs={{0,1},{1,0},{2,3},{3,2},{4,5},{5,4},{6,7},{7,6},{8,9},{9,8},{10,11... | collective-permute-start | bytes 245768 | tf_op jit(solution)/shard_map/ppermute | solution.py:321
  10.8 1.0 %copy-start.5 = (bf16[160,1024]{1,0:T(8,128)(2,1)S(1)}, bf16[160,1024]{1,0:T(8,128)(2,1)}, u32[]{:S(2)}) copy-start(bf16[160,1024]{1,0:T(8,128)(2,1)} %get-tuple-element.32.base_ref) | copy-start | bytes 983044
  11.8 0.9 %copy-start.6 = (bf16[160,256]{1,0:T(8,128)(2,1)S(1)}, bf16[160,256]{1,0:T(8,128)(2,1)}, u32[]{:S(2)}) copy-start(bf16[160,256]{1,0:T(8,128)(2,1)} %get-tuple-element.31.o0_ref) | copy-start | bytes 245764
  13.3 9.0 %collective-permute-start.5 = (bf16[160,1024]{1,0:T(8,128)(2,1)S(1)}, bf16[160,1024]{1,0:T(8,128)(2,1)S(1)}, u32[]{:S(2)}, u32[]{:S(2)}) collective-permute-start(bf16[160,1024]{1,0:T(8,128)(2,1)S(1)} %get-tuple-element.33.mine), channel_id=1, source_target_pairs={{0,2},{1,3},{2,0},{3,1},{4,6},{5,7},{6,4},{7,5},{8,10},{9,11},{10,... | collective-permute-start | bytes 983048 | tf_op jit(solution)/shard_map/ppermute | solution.py:321
  22.5 9.8 %collective-permute-start.6 = (bf16[40,1024]{1,0:T(8,128)(2,1)S(1)}, bf16[40,1024]{1,0:T(8,128)(2,1)S(1)}, u32[]{:S(2)}, u32[]{:S(2)}) collective-permute-start(bf16[40,1024]{1,0:T(8,128)(2,1)S(1)} %get-tuple-element.36), channel_id=1, source_target_pairs={{0,224},{1,225},{2,226},{3,227},{4,228},{5,229},{6,230},{7,231},{8... | collective-permute-start | bytes 245768 | tf_op jit(solution)/shard_map/ppermute | solution.py:321
  26.4 6.4 %collective-permute-start.7 = (bf16[40,1024]{1,0:T(8,128)(2,1)S(1)}, bf16[40,1024]{1,0:T(8,128)(2,1)S(1)}, u32[]{:S(2)}, u32[]{:S(2)}) collective-permute-start(bf16[40,1024]{1,0:T(8,128)(2,1)S(1)} %get-tuple-element.37), channel_id=1, source_target_pairs={{0,30},{1,31},{2,28},{3,29},{4,0},{5,1},{6,2},{7,3},{8,4},{9,5},{1... | collective-permute-start | bytes 245768 | tf_op jit(solution)/shard_map/ppermute | solution.py:321
  31.3 4.2 %collective-permute-start.8 = (bf16[40,1024]{1,0:T(8,128)(2,1)S(1)}, bf16[40,1024]{1,0:T(8,128)(2,1)S(1)}, u32[]{:S(2)}, u32[]{:S(2)}) collective-permute-start(bf16[40,1024]{1,0:T(8,128)(2,1)S(1)} %get-tuple-element.38), channel_id=1, source_target_pairs={{0,254},{1,255},{2,252},{3,253},{4,224},{5,225},{6,226},{7,227},{8... | collective-permute-start | bytes 245768 | tf_op jit(solution)/shard_map/ppermute | solution.py:321
  35.5 5.1 %copy-start = (bf16[1024,1024]{1,0:T(8,128)(2,1)S(1)}, bf16[1024,1024]{1,0:T(8,128)(2,1)}, u32[]{:S(2)}) copy-start(bf16[1024,1024]{1,0:T(8,128)(2,1)} %u0) | copy-start | bytes 6291460
  35.5 8.2 %copy-start.1 = (bf16[1024,1024]{1,0:T(8,128)(2,1)S(1)}, bf16[1024,1024]{1,0:T(8,128)(2,1)}, u32[]{:S(2)}) copy-start(bf16[1024,1024]{1,0:T(8,128)(2,1)} %d0) | copy-start | bytes 6291460
  40.6 12.2 %collective-permute-start.10 = (bf16[1024,1024]{1,0:T(8,128)(2,1)S(1)}, bf16[1024,1024]{1,0:T(8,128)(2,1)S(1)}, u32[]{:S(2)}, u32[]{:S(2)}) collective-permute-start(bf16[1024,1024]{1,0:T(8,128)(2,1)S(1)} %copy-done), channel_id=1, source_target_pairs={{0,1},{1,0},{2,3},{3,2},{4,5},{5,4},{6,7},{7,6},{8,9},{9,8},{10,11... | collective-permute-start | bytes 6291464 | tf_op jit(solution)/shard_map/ppermute | solution.py:321
  43.8 9.0 %collective-permute-start.11 = (bf16[1024,1024]{1,0:T(8,128)(2,1)S(1)}, bf16[1024,1024]{1,0:T(8,128)(2,1)S(1)}, u32[]{:S(2)}, u32[]{:S(2)}) collective-permute-start(bf16[1024,1024]{1,0:T(8,128)(2,1)S(1)} %copy-done.1), channel_id=1, source_target_pairs={{0,1},{1,0},{2,3},{3,2},{4,5},{5,4},{6,7},{7,6},{8,9},{9,8},{10,11... | collective-permute-start | bytes 6291464 | tf_op jit(solution)/shard_map/ppermute | solution.py:321
  43.9 8.9 %collective-permute-start.9 = (bf16[160,1024]{1,0:T(8,128)(2,1)S(1)}, bf16[160,1024]{1,0:T(8,128)(2,1)S(1)}, u32[]{:S(2)}, u32[]{:S(2)}) collective-permute-start(bf16[160,1024]{1,0:T(8,128)(2,1)S(1)} %shard_map.85.mine), channel_id=1, source_target_pairs={{0,2},{1,3},{2,0},{3,1},{4,6},{5,7},{6,4},{7,5},{8,10},{9,11},{10,... | collective-permute-start | bytes 983048 | tf_op jit(solution)/shard_map/ppermute | solution.py:321
  54.7 3.4 %collective-permute-start.12 = (bf16[40,1024]{1,0:T(8,128)(2,1)S(1)}, bf16[40,1024]{1,0:T(8,128)(2,1)S(1)}, u32[]{:S(2)}, u32[]{:S(2)}) collective-permute-start(bf16[40,1024]{1,0:T(8,128)(2,1)S(1)} %get-tuple-element.46), channel_id=1, source_target_pairs={{0,2},{1,3},{2,0},{3,1},{4,6},{5,7},{6,4},{7,5},{8,10},{9,11},{10,... | collective-permute-start | bytes 245768 | tf_op jit(solution)/shard_map/ppermute | solution.py:321
  54.8 3.2 %collective-permute-start.13 = (bf16[40,1024]{1,0:T(8,128)(2,1)S(1)}, bf16[40,1024]{1,0:T(8,128)(2,1)S(1)}, u32[]{:S(2)}, u32[]{:S(2)}) collective-permute-start(bf16[40,1024]{1,0:T(8,128)(2,1)S(1)} %get-tuple-element.47), channel_id=1, source_target_pairs={{0,1},{1,0},{2,3},{3,2},{4,5},{5,4},{6,7},{7,6},{8,9},{9,8},{10,11... | collective-permute-start | bytes 245768 | tf_op jit(solution)/shard_map/ppermute | solution.py:321
  56.3 5.0 %collective-permute-start.14 = (bf16[40,1024]{1,0:T(8,128)(2,1)S(1)}, bf16[40,1024]{1,0:T(8,128)(2,1)S(1)}, u32[]{:S(2)}, u32[]{:S(2)}) collective-permute-start(bf16[40,1024]{1,0:T(8,128)(2,1)S(1)} %get-tuple-element.48), channel_id=1, source_target_pairs={{0,3},{1,2},{2,1},{3,0},{4,7},{5,6},{6,5},{7,4},{8,11},{9,10},{10,... | collective-permute-start | bytes 245768 | tf_op jit(solution)/shard_map/ppermute | solution.py:321
  61.4 7.6 %collective-permute-start.17 = (bf16[80,1024]{1,0:T(8,128)(2,1)S(1)}, bf16[80,1024]{1,0:T(8,128)(2,1)S(1)}, u32[]{:S(2)}, u32[]{:S(2)}) collective-permute-start(bf16[80,1024]{1,0:T(8,128)(2,1)S(1)} %shard_map.87), channel_id=1, source_target_pairs={{0,2},{1,39},{2,32},{3,5},{4,6},{5,43},{6,36},{7,9},{8,10},{9,47},... | collective-permute-start | bytes 491528 | tf_op jit(solution)/shard_map/ppermute | solution.py:321
  61.5 11.8 %collective-permute-start.15 = (bf16[80,1024]{1,0:T(8,128)(2,1)S(1)}, bf16[80,1024]{1,0:T(8,128)(2,1)S(1)}, u32[]{:S(2)}, u32[]{:S(2)}) collective-permute-start(bf16[80,1024]{1,0:T(8,128)(2,1)S(1)} %shard_map.87), channel_id=1, source_target_pairs={{0,0},{1,37},{2,34},{3,7},{4,4},{5,41},{6,38},{7,11},{8,8},{9,45},... | collective-permute-start | bytes 491528 | tf_op jit(solution)/shard_map/ppermute | solution.py:321
  69.0 4.3 %collective-permute-start.18 = (bf16[80,1024]{1,0:T(8,128)(2,1)S(1)}, bf16[80,1024]{1,0:T(8,128)(2,1)S(1)}, u32[]{:S(2)}, u32[]{:S(2)}) collective-permute-start(bf16[80,1024]{1,0:T(8,128)(2,1)S(1)} %collective-permute-done.17.r2), channel_id=1, source_target_pairs={{0,1},{1,0},{2,3},{3,2},{4,5},{5,4},{6,7},{7,6},{8,9},{9,8},{10,11... | collective-permute-start | bytes 491528 | tf_op jit(solution)/shard_map/ppermute | solution.py:321
  73.3 1.4 %collective-permute-start.16 = (bf16[80,1024]{1,0:T(8,128)(2,1)S(1)}, bf16[80,1024]{1,0:T(8,128)(2,1)S(1)}, u32[]{:S(2)}, u32[]{:S(2)}) collective-permute-start(bf16[80,1024]{1,0:T(8,128)(2,1)S(1)} %collective-permute-done.15.r0), channel_id=1, source_target_pairs={{0,1},{1,0},{2,3},{3,2},{4,5},{5,4},{6,7},{7,6},{8,9},{9,8},{10,11... | collective-permute-start | bytes 491528 | tf_op jit(solution)/shard_map/ppermute | solution.py:321

commit v4 on v2

v4 whole, which is shorter than its diff:
```python
import functools

import jax
import jax.numpy as jnp
import numpy as np
from jax import lax
from jax.experimental import pallas as pl
from jax.experimental.pallas import tpu as pltpu
from jax.sharding import PartitionSpec as P

WL = 2
WY = 6
WX = 12
SY = 3
SX = 6
HD = 64
NEG = -1000000000.0
AXES = ("lat", "lon", "mp")
MIB = 1024 * 1024

USED = 36
ROWS = 40
KEPT = 4 * ROWS
HALF = 2 * ROWS
PATCH = 4 * WY * WX
WINDOW = WL * WY * WX
FEAT = 32
F_Y = 4
F_X = 10
F_PAD = 22


def pairs(counts, target):
    lats, lons, mps = counts
    result = []
    for a in range(lats):
        for b in range(lons):
            for m in range(mps):
                ta, tb, tm = target(a, b, m)
                dest = ((ta % lats) * lons + tb % lons) * mps + tm
                result.append(((a * lons + b) * mps + m, dest))
    return result


def dot(left, right):
    return jnp.dot(left, right, preferred_element_type=jnp.float32)


def dot_t(left, right):
    return lax.dot_general(left, right, (((1,), (1,)), ((), ())), preferred_element_type=jnp.float32)


def normalize(floats):
    center = floats - jnp.mean(floats, axis=-1, keepdims=True)
    spread = jnp.mean(center * center, axis=-1, keepdims=True)
    return (center * lax.rsqrt(spread + 1e-05)).astype(jnp.bfloat16)


def core_index():
    return lax.rem(lax.axis_index("mp"), 2)


def iota(shape, axis):
    return lax.broadcasted_iota(jnp.int32, shape, axis)


def one_hot(condition):
    return jnp.where(condition, 1.0, 0.0).astype(jnp.bfloat16)


def piece_place(slot):
    level = (slot * 57) >> 10
    rest = slot - level * 18
    row = (rest * 43) >> 8
    return level, row, rest - row * 6


def kept_place(index):
    piece = (index * 205) >> 13
    slot = index - piece * ROWS
    return ((piece + 2) & 3, slot) + piece_place(slot)


def real_level(level, core):
    return jnp.where(core == 0, 1 + level, 3 - 3 * level)


def patch_place(q, row, col):
    return row + 3 - 3 * (q & 1), col + 6 - 3 * (q & 2)


def bias_rows(table, block, pair):
    shape = (FEAT, 4 * FEAT)
    i, lane = iota(shape, 0), iota(shape, 1)
    j = lane & (FEAT - 1)
    kind = jnp.full(shape, 37, jnp.int32)
    kind = jnp.where((i < WL) & (j < WL), i - j + 1, kind)
    kind = jnp.where((i < WL) & (j == F_PAD), 38, kind)
    in_y = (i >= F_Y) & (i < F_Y + WY) & (j >= F_Y) & (j < F_Y + WY)
    kind = jnp.where(in_y, 3 + i - j + 5, kind)
    in_x = (i >= F_X) & (i < F_X + WX) & (j >= F_X) & (j < F_X + WX)
    kind = jnp.where(in_x, 14 + i - j + 11, kind)
    total = jnp.where(kind == 38, NEG, 0.0)
    for k in range(37):
        value = jnp.where(lane < HD, table[block, 2 * pair + 1, k], table[block, 2 * pair, k])
        total = jnp.where(kind == k, value, total)
    high = total.astype(jnp.bfloat16).astype(jnp.float32)
    return jnp.where((lane & FEAT) != 0, total - high, high).astype(jnp.bfloat16)


def bias_kernel(table, first, second):
    for block, out in enumerate((first, second)):
        for pair in range(2):
            out[:, pair * 128 : pair * 128 + 128] = bias_rows(table, block, pair)


def features(level, row, col, used, count):
    j = iota((count, 128), 1) & (FEAT - 1)
    hit = (j == level) | (j == F_Y + row) | (j == F_X + col)
    return one_hot(jnp.where(used, jnp.where(hit, 1, 0), jnp.where(j == F_PAD, 1, 0)) == 1)


def pair_heads(query, key, value, extra, key_feat):
    low_q = iota(query.shape, 1) < HD
    low_k = iota(key.shape, 1) < HD
    outs = []
    for head in range(2):
        mine_q, mine_k = (low_q, low_k) if head == 0 else (~low_q, ~low_k)
        scores = dot_t(jnp.where(mine_q, query, extra), jnp.where(mine_k, key, key_feat))
        expo = jnp.exp(scores - jnp.max(scores, axis=-1, keepdims=True))
        probs = (expo / jnp.sum(expo, axis=-1, keepdims=True)).astype(jnp.bfloat16)
        outs.append(dot(probs, value))
    return jnp.where(low_q, outs[0], outs[1]).astype(jnp.bfloat16)


def first_kernel(tokens, weight, bias, keep, give, *bases):
    core = core_index()
    floats = tokens[...].astype(jnp.float32).reshape(PATCH, -1)
    xn = normalize(floats)
    q = (dot(xn, weight[0]) * HD**-0.5).astype(jnp.bfloat16)
    k = dot(xn, weight[1]).astype(jnp.bfloat16)
    v = dot(xn, weight[2]).astype(jnp.bfloat16)
    index = iota((PATCH, 1), 0)
    level = (index * 911) >> 16
    order = one_hot(iota((PATCH, PATCH), 1) == (index - 72 * level) * 4 + level)
    q, k, v = (dot(order, part).astype(jnp.bfloat16) for part in (q, k, v))
    index = iota((WINDOW, 1), 0)
    level = (index * 911) >> 16
    rest = index - 72 * level
    row = (rest * 171) >> 11
    feat = features(level, row, rest - 12 * row, index >= 0, WINDOW)
    parts = []
    for pair in range(2):
        cols = slice(pair * 128, pair * 128 + 128)
        extra = dot(feat[:, :FEAT], bias[:, cols]).astype(jnp.bfloat16)
        halves = []
        for w in range(2):
            rows = slice(w * WINDOW, (w + 1) * WINDOW)
            halves.append(pair_heads(q[rows, cols], k[rows, cols], v[rows, cols], extra, feat))
        parts.append(jnp.concatenate(halves, axis=0))
    mixed = jnp.concatenate(parts, axis=1)
    quad, slot, level, row, col = kept_place(iota((KEPT, 1), 0))
    row, col = patch_place(quad, row, col)
    lanes = iota((KEPT, PATCH), 1)
    for out, chosen in ((keep, core), (give, 1 - core)):
        place = real_level(level, chosen) * 72 + row * 12 + col
        place = jnp.where(slot < USED, place, -1)
        out[...] = dot(one_hot(lanes == place), mixed).astype(jnp.bfloat16)
    place = (row * 12 + col) * 4 + real_level(level, core)
    place = jnp.where(slot < USED, place, -1)
    base = dot(one_hot(lanes == place), floats.astype(jnp.bfloat16)).astype(jnp.bfloat16)
    for h in range(2):
        bases[h][...] = base[h * HALF : (h + 1) * HALF]


def store_halves(total, outs):
    for h in range(2):
        outs[h][...] = total[h * HALF : (h + 1) * HALF].astype(jnp.bfloat16)


def partial_kernel(o0, o1, w0, w1, *outs):
    store_halves(dot(o0[...], w0[...]) + dot(o1[...], w1[...]), outs)


def branch_sum(mine, other):
    total = mine[...].astype(jnp.float32) + other[...].astype(jnp.float32)
    return total.astype(jnp.bfloat16).astype(jnp.float32)


def residual_kernel(mine, other, base, *outs):
    first = base[...].astype(jnp.float32) + branch_sum(mine, other)
    for p in range(2):
        outs[p][...] = first[p * ROWS : (p + 1) * ROWS].astype(jnp.bfloat16)


def joined(pieces):
    return jnp.concatenate([p[...].astype(jnp.float32) for p in pieces], axis=0)


def norm_kernel(p0, p1, out):
    out[...] = normalize(joined((p0, p1)))


def second_kernel(xn_a, p2, p3, w_own, w_sib, o_own, o_sib, b_own, b_sib, *outs):
    xn_b = normalize(joined((p2, p3))).astype(jnp.float32)
    xn = jnp.concatenate([xn_a[...].astype(jnp.float32), xn_b], axis=0).astype(jnp.bfloat16)
    quad, slot, level, row, col = kept_place(iota((KEPT, 1), 0))
    row, col = row + 3 * (quad & 1), col + 3 * (quad & 2)
    feat = features(level, row, col, slot < USED, KEPT)
    lane = iota((KEPT, 128), 1)
    j = lane & (FEAT - 1)
    split_levels = core_index() == 1
    split_rows = lax.axis_index("lat") == lax.axis_size("lat") - 1
    ban_level = (j < WL) & (j != level)
    ban_row = (j >= F_Y) & (j < F_Y + WY) & ((j >= F_Y + SY) != (row >= SY))
    ban = jnp.where(ban_level, split_levels.astype(jnp.int32), jnp.where(ban_row, split_rows.astype(jnp.int32), 0))
    ban = jnp.where((lane & FEAT) == 0, ban, 0) == 1
    total = None
    for weight, bias, project in ((w_own, b_own, o_own), (w_sib, b_sib, o_sib)):
        q = (dot(xn, weight[0]) * HD**-0.5).astype(jnp.bfloat16)
        k = dot(xn, weight[1]).astype(jnp.bfloat16)
        v = dot(xn, weight[2]).astype(jnp.bfloat16)
        for pair in range(2):
            cols = slice(pair * 128, pair * 128 + 128)
            extra = dot(feat[:, :FEAT], bias[:, cols])
            extra = jnp.where(ban, NEG, extra).astype(jnp.bfloat16)
            mixed = pair_heads(q[:, cols], k[:, cols], v[:, cols], extra, feat)
            term = dot(mixed, project[cols, :])
            total = term if total is None else total + term
    store_halves(total, outs)


def gelu(x):
    return 0.5 * x * (1.0 + lax.erf(x * np.float32(np.sqrt(0.5))))


def mlp_kernel(mine, other, p0, p1, u0, u1, d0, d1, out):
    second = joined((p0, p1)) + branch_sum(mine, other)
    second = second.astype(jnp.bfloat16).astype(jnp.float32)
    xn = normalize(second)
    h0 = gelu(dot(xn, u0[...])).astype(jnp.bfloat16)
    h1 = gelu(dot(xn, u1[...])).astype(jnp.bfloat16)
    out[...] = (0.5 * second + dot(h0, d0[...]) + dot(h1, d1[...])).astype(jnp.bfloat16)


def sum_kernel(mine, other, *outs):
    total = mine[...].astype(jnp.float32) + other[...].astype(jnp.float32)
    for p in range(2):
        outs[p][...] = total[p * ROWS : (p + 1) * ROWS].astype(jnp.bfloat16)


def place_kernel(half, m0, m1, s0, s1, *refs):
    out, held, sems = refs[-3:]
    core = core_index()
    index = iota((1, HALF), 1)
    slot = jnp.where(index >= ROWS, index - ROWS, index)
    level, row, col = piece_place(slot)
    row = jnp.where(index >= ROWS, row, row + SY)
    total = None
    for chosen, pieces in ((core, (m0, m1)), (1 - core, (s0, s1))):
        place = (row * SX + col) * 4 + real_level(level, chosen)
        place = jnp.where(slot < USED, place, -1)
        term = dot(one_hot(iota((PATCH // 2, HALF), 0) == place), joined(pieces).astype(jnp.bfloat16))
        total = term if total is None else total + term
    held[...] = total.reshape(held.shape).astype(jnp.bfloat16)
    copies = []
    for y in range(WY):
        target = out.at[pl.ds(y * WX + half * SX, SX)]
        copies.append(pltpu.make_async_copy(held.at[pl.ds(y * SX, SX)], target, sems.at[y]))
        copies[-1].start()
    for copy in copies:
        copy.wait()


def place(half, pieces, shape, held):
    vmem, large = pl.BlockSpec(memory_space=pltpu.VMEM), pl.BlockSpec(memory_space=pl.ANY)
    return pl.pallas_call(
        functools.partial(place_kernel, half),
        out_shape=jax.ShapeDtypeStruct(shape, jnp.bfloat16),
        in_specs=[vmem] * 4 + [large] * len(held),
        out_specs=large,
        scratch_shapes=[
            pltpu.VMEM((shape[0] // 2,) + shape[1:], jnp.bfloat16),
            pltpu.SemaphoreType.DMA((WY,)),
        ],
        input_output_aliases={4: 0} if held else {},
        compiler_params=pltpu.CompilerParams(vmem_limit_bytes=12 * MIB),
        cost_estimate=pl.CostEstimate(flops=10**10, bytes_accessed=10**6, transcendentals=0),
    )(*pieces, *held)


def call(kernel, outs, operands, flops, limit, table=False):
    shapes = [jax.ShapeDtypeStruct(s, jnp.bfloat16) for s in outs]
    moved = sum(o.size * o.dtype.itemsize for o in operands) + sum(2 * s.size for s in shapes)
    result = pl.pallas_call(
        kernel,
        out_shape=shapes,
        in_specs=[pl.BlockSpec(memory_space=pltpu.SMEM if table else pltpu.VMEM)] * len(operands),
        out_specs=[pl.BlockSpec(memory_space=pltpu.VMEM)] * len(shapes),
        compiler_params=pltpu.CompilerParams(vmem_limit_bytes=limit * MIB),
        cost_estimate=pl.CostEstimate(flops=flops, bytes_accessed=moved, transcendentals=0),
    )(*operands)
    return result if len(result) > 1 else result[0]


def tied(*values):
    return lax.optimization_barrier(values)


def body(counts, tokens, qkv_first, qkv_second, out_first, out_second, rel_tables, up_weight, down_weight):
    levels, rows, cols, width = tokens.shape
    turn = counts[1] // 2

    def move(value, target):
        return lax.ppermute(value, AXES, pairs(counts, target))

    def core_swap(value):
        return move(value, lambda a, b, m: (a, b, m ^ 1))

    def chip_swap(value):
        return move(value, lambda a, b, m: (a, b, m ^ 2))

    def out_to(value, dy, dx):
        return move(value, lambda a, b, m: (a - dy, b - dx, m ^ 2 if dx and b % turn == 0 else m))

    def home(value, dy, dx):
        return move(value, lambda a, b, m: (a + dy, b + dx, m ^ 2 if dx and (b + 1) % turn == 0 else m))

    full, half, piece = [(KEPT, width)], [(HALF, width)], [(ROWS, width)]
    heads, features = [(KEPT, 256)], [(FEAT, 256)]

    tok = tokens.transpose(1, 2, 0, 3).reshape(rows * cols, levels, width)
    w_first = qkv_first.transpose(1, 0, 2)
    w_second = qkv_second.transpose(1, 0, 2)

    f1 = core_swap(out_first)
    s1 = core_swap(out_second)
    w_sib = core_swap(w_second)
    bias1, bias2 = call(bias_kernel, features * 2, (rel_tables,), 5 * 10**9, 4, table=True)
    bias2_sib = core_swap(bias2)
    keep, give, base_a, base_b = call(first_kernel, heads * 2 + half * 2, (tok, w_first, bias1), 10**9, 16)
    keep, give, f1, s1, w_sib, bias2_sib = tied(keep, give, f1, s1, w_sib, bias2_sib)
    given, up_late, down_late = tied(core_swap(give), up_weight, down_weight)
    u1 = core_swap(up_late)
    d1 = core_swap(down_late)
    part_a, part_b = call(partial_kernel, half * 2, (keep, given, out_first, f1), 2 * 10**8, 8)
    other_a = chip_swap(part_a)
    other_b = chip_swap(part_b)
    lon, diag = call(residual_kernel, piece * 2, (part_a, other_a, base_a), 10**6, 8)
    lon, diag, part_b = tied(lon, diag, part_b)
    own, lat = call(residual_kernel, piece * 2, (part_b, other_b, base_b), 10**10, 8)
    lon = out_to(lon, 0, 1)
    diag = out_to(diag, 1, 1)
    lat = out_to(lat, 1, 0)

    xn_a = call(norm_kernel, half, (lon, diag), 10**10, 8)
    part_a, part_b = call(
        second_kernel,
        half * 2,
        (xn_a, own, lat, w_second, w_sib, out_second, s1, bias2, bias2_sib),
        10**9,
        16,
    )
    other_a = chip_swap(part_a)
    other_b = chip_swap(part_b)
    mlp = (up_weight, u1, down_weight, d1)
    part_a = call(mlp_kernel, half, (part_a, other_a, lon, diag, *mlp), 10**9, 20)
    part_a, part_b = tied(part_a, part_b)
    other_a = chip_swap(part_a)
    part_b = call(mlp_kernel, half, (part_b, other_b, own, lat, *mlp), 10**9, 20)
    other_b = chip_swap(part_b)
    lon, diag = call(sum_kernel, piece * 2, (part_a, other_a), 10**6, 8)
    lon, diag, part_b = tied(lon, diag, part_b)
    lon = home(lon, 0, 1)
    diag = home(diag, 1, 1)
    own, lat = call(sum_kernel, piece * 2, (part_b, other_b), 10**10, 8)
    lat = home(lat, 1, 0)
    shape = (rows * cols, levels, width)
    result = place(0, (lon, diag, core_swap(lon), core_swap(diag)), shape, ())
    result = place(1, (own, lat, core_swap(own), core_swap(lat)), shape, (result,))
    return result.reshape(rows, cols, levels, width).transpose(2, 0, 1, 3)


def solution(mesh):
    counts = tuple(mesh.shape[name] for name in AXES)
    return jax.shard_map(
        functools.partial(body, counts),
        mesh=mesh,
        in_specs=(
            P(None, "lat", "lon", None),
            P(None, None, "mp"),
            P(None, None, "mp"),
            P("mp", None),
            P("mp", None),
            P(None, "mp", None),
            P(None, "mp"),
            P("mp", None),
        ),
        out_specs=P(None, "lat", "lon", None),
        check_vma=False,
    )
```

time: 106 us -> 63.9 us (0.60)
  waiting for transfers between devices: 51.1 us -> 17.2 us
  starting transfers between devices: 36.5 us -> 30.7 us
  local copies, waits for them, and re-layouts: 5.65 us -> 0.72 us
  Pallas kernels: 12.6 us -> 14.7 us
    ppermute x26 -> x23, waiting for transfers between devices: 51.1 us -> 17.2 us  [move(): return lax.ppermute(value, AXES, pairs(counts, target))]
    ppermute x26 -> x23, starting transfers between devices: 36.5 us -> 30.7 us  [move(): return lax.ppermute(value, AXES, pairs(counts, target))]
    unnamed x16, local copies, waits for them, and re-layouts: 4.59 us -> 0.72 us
    pallas_call x6 -> x13, Pallas kernels: 12.6 us -> 14.7 us  [the longest x11 12.6 us: call(): pl.pallas_call(kernel, out_shape=shapes, in_specs=[pl.BlockSpec(memory_sp...]
    slice x1 -> x0, local copies, waits for them, and re-layouts: 1.06 us -> none  [body(): f2b = side_swap(out_first[half:])]
  transfers between devices with their start and end apart: 26 -> 23, of which waited for: 14 -> 9; matrix products, arithmetic and copies ran while one was open for 1% -> 0% of each run, Pallas kernels for 8% -> 21%
where the time goes in v4:
time: 63.9 us; the launch traced here: 63.8 us
  starting transfers between devices  30.7 us (48%)
  waiting for transfers between devices  17.2 us (27%)
  Pallas kernels  14.7 us (23%)
  local copies, waits for them, and re-layouts  0.72 us (1%)
    ppermute x23, starting transfers between devices, move(): return lax.ppermute(value, AXES, pairs(counts, target))  30.7 us
    ppermute x23, waiting for transfers between devices, move(): return lax.ppermute(value, AXES, pairs(counts, target))  17.2 us
    pallas_call x11, Pallas kernels, call(): pl.pallas_call(kernel, out_shape=shapes, in_specs=[pl.BlockSpec(memory_sp...  12.6 us
    pallas_call x2, Pallas kernels, place(): pl.pallas_call(functools.partial(place_kernel, half), out_shape=jax.Shape...  2.14 us
  transfers between devices with their start and end apart: 23, of which 9 were waited for; matrix products, arithmetic and copies ran while one was open for 0% of the time, Pallas kernels for 21%

profile of v4, /device:TPU:1, one launch (start us, length us, event | category | flops | bytes accessed | tf_op | source)
XLA Modules:
  0.0 63.8 jit_solution(14515178194789372097)
XLA Ops:
  0.0 3.2 %collective-permute-start.2 = (bf16[3,1024,256]{2,1,0:T(8,128)(2,1)}, bf16[3,1024,256]{2,1,0:T(8,128)(2,1)S(1)}, u32[]{:S(2)}, u32[]{:S(2)}) collective-permute-start(bf16[3,1024,256]{2,1,0:T(8,128)(2,1)} %bitcast.8), channel_id=1, source_target_pairs={{0,1},{1,0},{2,3},{3,2},{4,5},{5,4},{6,7},{7,6},{8,9},{9,8},{10,11... | collective-permute-start | bytes 4718600 | tf_op jit(solution)/shard_map/ppermute | solution.py:315
  3.2 0.5 collective-permute-start.1
  3.8 0.7 %copy-done.7 = f32[2,4,37]{2,1,0:T(4,128)S(1)} copy-done((f32[2,4,37]{2,1,0:T(4,128)S(1)}, f32[2,4,37]{2,1,0:T(4,128)}, u32[]{:S(2)}) %copy-start.7) | copy-done | bytes 1208
  4.4 0.8 %shard_map.82 = (bf16[32,256]{1,0:T(8,128)(2,1)S(1)}, bf16[32,256]{1,0:T(8,128)(2,1)S(1)}) custom-call(f32[2,4,37]{2,1,0:T(4,128)S(1)} %copy-done.7), custom_call_target="tpu_custom_call" | custom-call | flops 5000000000 | bytes 33952 | tf_op jit(solution)/shard_map/pallas_call | solution.py:295
  5.5 3.1 %shard_map.83 = (bf16[160,256]{1,0:T(8,128)(2,1)S(1)}, bf16[160,256]{1,0:T(8,128)(2,1)S(1)}, bf16[80,1024]{1,0:T(8,128)(2,1)S(1)}, bf16[80,1024]{1,0:T(8,128)(2,1)S(1)}) custom-call(bf16[72,4,1024]{2,1,0:T(4,128)(2,1)S(1)} %bitcast.11, bf16[3,1024,256]{2,1,0:T(8,128)(2,1)S(1)} %bitcast.10, bf16[32,256]{1,0:T(8,128)(2,1)S(1)} %get-tuple-element.40.bias), custom_call_target="tpu_custom_call" | custom-call | flops 1000000000 | bytes 2670592 | tf_op jit(solution)/shard_map/pallas_call | solution.py:295
  8.6 0.5 collective-permute-start.4
  9.1 0.9 %collective-permute-done.4.o1 = bf16[160,256]{1,0:T(8,128)(2,1)S(1)} collective-permute-done((bf16[160,256]{1,0:T(8,128)(2,1)S(1)}, bf16[160,256]{1,0:T(8,128)(2,1)S(1)}, u32[]{:S(2)}, u32[]{:S(2)}) %collective-permute-start.4) | collective-permute-done | bytes 81952 | tf_op jit(solution)/shard_map/ppermute | solution.py:315
  10.0 0.3 shard_map.84
  10.5 1.5 %collective-permute-start.8 = (bf16[80,1024]{1,0:T(8,128)(2,1)S(1)}, bf16[80,1024]{1,0:T(8,128)(2,1)S(1)}, u32[]{:S(2)}, u32[]{:S(2)}) collective-permute-start(bf16[80,1024]{1,0:T(8,128)(2,1)S(1)} %get-tuple-element.55.mine), channel_id=1, source_target_pairs={{0,2},{1,3},{2,0},{3,1},{4,6},{5,7},{6,4},{7,5},{8,10},{9,11},{10,... | collective-permute-start | bytes 491528 | tf_op jit(solution)/shard_map/ppermute | solution.py:315
  11.9 0.9 %collective-permute-start.11 = (bf16[1024,1024]{1,0:T(8,128)(2,1)S(1)}, bf16[1024,1024]{1,0:T(8,128)(2,1)S(1)}, u32[]{:S(2)}, u32[]{:S(2)}) collective-permute-start(bf16[1024,1024]{1,0:T(8,128)(2,1)S(1)} %copy-done), channel_id=1, source_target_pairs={{0,1},{1,0},{2,3},{3,2},{4,5},{5,4},{6,7},{7,6},{8,9},{9,8},{10,11... | collective-permute-start | bytes 6291464 | tf_op jit(solution)/shard_map/ppermute | solution.py:315
  12.9 3.0 %collective-permute-done.5.other = bf16[80,1024]{1,0:T(8,128)(2,1)S(1)} collective-permute-done((bf16[80,1024]{1,0:T(8,128)(2,1)S(1)}, bf16[80,1024]{1,0:T(8,128)(2,1)S(1)}, u32[]{:S(2)}, u32[]{:S(2)}) %collective-permute-start.5) | collective-permute-done | bytes 163872 | tf_op jit(solution)/shard_map/ppermute | solution.py:315
  16.0 3.3 %collective-permute-start.6 = (bf16[40,1024]{1,0:T(8,128)(2,1)S(1)}, bf16[40,1024]{1,0:T(8,128)(2,1)S(1)}, u32[]{:S(2)}, u32[]{:S(2)}) collective-permute-start(bf16[40,1024]{1,0:T(8,128)(2,1)S(1)} %get-tuple-element.53), channel_id=1, source_target_pairs={{0,30},{1,31},{2,28},{3,29},{4,0},{5,1},{6,2},{7,3},{8,4},{9,5},{1... | collective-permute-start | bytes 245768 | tf_op jit(solution)/shard_map/ppermute | solution.py:315
  19.2 5.8 %collective-permute-start.7 = (bf16[40,1024]{1,0:T(8,128)(2,1)S(1)}, bf16[40,1024]{1,0:T(8,128)(2,1)S(1)}, u32[]{:S(2)}, u32[]{:S(2)}) collective-permute-start(bf16[40,1024]{1,0:T(8,128)(2,1)S(1)} %get-tuple-element.54), channel_id=1, source_target_pairs={{0,254},{1,255},{2,252},{3,253},{4,224},{5,225},{6,226},{7,227},{8... | collective-permute-start | bytes 245768 | tf_op jit(solution)/shard_map/ppermute | solution.py:315
  25.1 1.0 %collective-permute-start.9 = (bf16[40,1024]{1,0:T(8,128)(2,1)S(1)}, bf16[40,1024]{1,0:T(8,128)(2,1)S(1)}, u32[]{:S(2)}, u32[]{:S(2)}) collective-permute-start(bf16[40,1024]{1,0:T(8,128)(2,1)S(1)} %get-tuple-element.58), channel_id=1, source_target_pairs={{0,224},{1,225},{2,226},{3,227},{4,228},{5,229},{6,230},{7,231},{8... | collective-permute-start | bytes 245768 | tf_op jit(solution)/shard_map/ppermute | solution.py:315
  26.1 0.4 collective-permute-done.7.p1
  26.7 1.9 %collective-permute-done.9.p3.p1 = bf16[40,1024]{1,0:T(8,128)(2,1)S(1)} collective-permute-done((bf16[40,1024]{1,0:T(8,128)(2,1)S(1)}, bf16[40,1024]{1,0:T(8,128)(2,1)S(1)}, u32[]{:S(2)}, u32[]{:S(2)}) %collective-permute-start.9) | collective-permute-done | bytes 81952 | tf_op jit(solution)/shard_map/ppermute | solution.py:315
  28.6 4.3 %shard_map.88 = (bf16[80,1024]{1,0:T(8,128)(2,1)S(1)}, bf16[80,1024]{1,0:T(8,128)(2,1)S(1)}) custom-call(bf16[80,1024]{1,0:T(8,128)(2,1)S(1)} %shard_map.86.xn_a, bf16[40,1024]{1,0:T(8,128)(2,1)S(1)} %get-tuple-element.57.p2.p0, bf16[40,1024]{1,0:T(8,128)(2,1)S(1)} %collective-permute-done.9.p3.p1, bf16[3,1024,256]{2,1,0:T(8,128)(2,1)S(1)} %bitcast.9, ...), custom_call_target="tpu_custom_call" | custom-call | flops 1000000000 | bytes 4882432 | tf_op jit(solution)/shard_map/pallas_call | solution.py:295
  33.0 1.5 %collective-permute-start.14 = (bf16[80,1024]{1,0:T(8,128)(2,1)S(1)}, bf16[80,1024]{1,0:T(8,128)(2,1)S(1)}, u32[]{:S(2)}, u32[]{:S(2)}) collective-permute-start(bf16[80,1024]{1,0:T(8,128)(2,1)S(1)} %get-tuple-element.69.mine), channel_id=1, source_target_pairs={{0,2},{1,3},{2,0},{3,1},{4,6},{5,7},{6,4},{7,5},{8,10},{9,11},{10,... | collective-permute-start | bytes 491528 | tf_op jit(solution)/shard_map/ppermute | solution.py:315
  34.5 2.7 %collective-permute-done.10.other = bf16[80,1024]{1,0:T(8,128)(2,1)S(1)} collective-permute-done((bf16[80,1024]{1,0:T(8,128)(2,1)S(1)}, bf16[80,1024]{1,0:T(8,128)(2,1)S(1)}, u32[]{:S(2)}, u32[]{:S(2)}) %collective-permute-start.10) | collective-permute-done | bytes 163872 | tf_op jit(solution)/shard_map/ppermute | solution.py:315
  37.2 1.8 %shard_map.89.mine = bf16[80,1024]{1,0:T(8,128)(2,1)S(1)} custom-call(bf16[80,1024]{1,0:T(8,128)(2,1)S(1)} %get-tuple-element.62.mine, bf16[80,1024]{1,0:T(8,128)(2,1)S(1)} %collective-permute-done.10.other, bf16[40,1024]{1,0:T(8,128)(2,1)S(1)} %collective-permute-done.6.p0, bf16[40,1024]{1,0:T(8,128)(2,1)S(1)} %collective-permute-done.7.p1, ...), custom_call_target="tpu_custom_call" | custom-call | flops 1000000000 | bytes 9043968 | tf_op jit(solution)/shard_map/pallas_call | solution.py:295
  39.1 1.8 %shard_map.91.mine = bf16[80,1024]{1,0:T(8,128)(2,1)S(1)} custom-call(bf16[80,1024]{1,0:T(8,128)(2,1)S(1)} %get-tuple-element.69.mine, bf16[80,1024]{1,0:T(8,128)(2,1)S(1)} %collective-permute-done.14.other, bf16[40,1024]{1,0:T(8,128)(2,1)S(1)} %get-tuple-element.57.p2.p0, bf16[40,1024]{1,0:T(8,128)(2,1)S(1)} %collective-permute-done.9.p3.p1, ...), custom_call_target="tpu_custom_call" | custom-call | flops 1000000000 | bytes 9043968 | tf_op jit(solution)/shard_map/pallas_call | solution.py:295
  41.0 1.5 %collective-permute-start.15 = (bf16[80,1024]{1,0:T(8,128)(2,1)S(1)}, bf16[80,1024]{1,0:T(8,128)(2,1)S(1)}, u32[]{:S(2)}, u32[]{:S(2)}) collective-permute-start(bf16[80,1024]{1,0:T(8,128)(2,1)S(1)} %shard_map.91.mine), channel_id=1, source_target_pairs={{0,2},{1,3},{2,0},{3,1},{4,6},{5,7},{6,4},{7,5},{8,10},{9,11},{10,... | collective-permute-start | bytes 491528 | tf_op jit(solution)/shard_map/ppermute | solution.py:315
  42.5 2.4 %collective-permute-done.13.other = bf16[80,1024]{1,0:T(8,128)(2,1)S(1)} collective-permute-done((bf16[80,1024]{1,0:T(8,128)(2,1)S(1)}, bf16[80,1024]{1,0:T(8,128)(2,1)S(1)}, u32[]{:S(2)}, u32[]{:S(2)}) %collective-permute-start.13) | collective-permute-done | bytes 163872 | tf_op jit(solution)/shard_map/ppermute | solution.py:315
  44.9 1.1 %collective-permute-start.19 = (bf16[40,1024]{1,0:T(8,128)(2,1)S(1)}, bf16[40,1024]{1,0:T(8,128)(2,1)S(1)}, u32[]{:S(2)}, u32[]{:S(2)}) collective-permute-start(bf16[40,1024]{1,0:T(8,128)(2,1)S(1)} %get-tuple-element.73), channel_id=1, source_target_pairs={{0,4},{1,5},{2,6},{3,7},{4,8},{5,9},{6,10},{7,11},{8,12},{9,13},{1... | collective-permute-start | bytes 245768 | tf_op jit(solution)/shard_map/ppermute | solution.py:315
  46.0 0.6 collective-permute-done.15.other
  46.7 4.9 %collective-permute-done.19.m0 = bf16[40,1024]{1,0:T(8,128)(2,1)S(1)} collective-permute-done((bf16[40,1024]{1,0:T(8,128)(2,1)S(1)}, bf16[40,1024]{1,0:T(8,128)(2,1)S(1)}, u32[]{:S(2)}, u32[]{:S(2)}) %collective-permute-start.19) | collective-permute-done | bytes 81952 | tf_op jit(solution)/shard_map/ppermute | solution.py:315
  51.6 5.5 %collective-permute-start.21 = (bf16[40,1024]{1,0:T(8,128)(2,1)S(1)}, bf16[40,1024]{1,0:T(8,128)(2,1)S(1)}, u32[]{:S(2)}, u32[]{:S(2)}) collective-permute-start(bf16[40,1024]{1,0:T(8,128)(2,1)S(1)} %collective-permute-done.19.m0), channel_id=1, source_target_pairs={{0,1},{1,0},{2,3},{3,2},{4,5},{5,4},{6,7},{7,6},{8,9},{9,8},{10,11... | collective-permute-start | bytes 245768 | tf_op jit(solution)/shard_map/ppermute | solution.py:315
  57.1 3.4 %collective-permute-start.22 = (bf16[40,1024]{1,0:T(8,128)(2,1)S(1)}, bf16[40,1024]{1,0:T(8,128)(2,1)S(1)}, u32[]{:S(2)}, u32[]{:S(2)}) collective-permute-start(bf16[40,1024]{1,0:T(8,128)(2,1)S(1)} %collective-permute-done.20.m1), channel_id=1, source_target_pairs={{0,1},{1,0},{2,3},{3,2},{4,5},{5,4},{6,7},{7,6},{8,9},{9,8},{10,11... | collective-permute-start | bytes 245768 | tf_op jit(solution)/shard_map/ppermute | solution.py:315
  60.5 0.5 collective-permute-start.18
  61.1 0.4 collective-permute-done.22.s1
  61.5 1.1 %shard_map.93.refs_0_ = bf16[72,4,1024]{2,1,0:T(4,128)(2,1)} custom-call(bf16[40,1024]{1,0:T(8,128)(2,1)S(1)} %collective-permute-done.19.m0, bf16[40,1024]{1,0:T(8,128)(2,1)S(1)} %collective-permute-done.20.m1, bf16[40,1024]{1,0:T(8,128)(2,1)S(1)} %collective-permute-done.21.s0, bf16[40,1024]{1,0:T(8,128)(2,1)S(1)} %collective-permute-done.22.s1), custom_call_target="tpu_custom_call" | custom-call | flops 10000000000 | bytes 1000000 | tf_op jit(solution)/shard_map/pallas_call | solution.py:277
  62.6 1.1 %shard_map.94 = bf16[72,4,1024]{2,1,0:T(4,128)(2,1)} custom-call(bf16[40,1024]{1,0:T(8,128)(2,1)S(1)} %get-tuple-element.71.m0, bf16[40,1024]{1,0:T(8,128)(2,1)S(1)} %collective-permute-done.16.m1, bf16[40,1024]{1,0:T(8,128)(2,1)S(1)} %collective-permute-done.17.s0, bf16[40,1024]{1,0:T(8,128)(2,1)S(1)} %collective-permute-done.18.s1, ...), custom_call_target="tpu_custom_call", output_to_operand_aliasing={{}: (4, {})} | custom-call | flops 10000000000 | bytes 1000000 | tf_op jit(solution)/shard_map/pallas_call | solution.py:277
  (43 shorter events, 1.2 us)
Async XLA Ops:
  0.0 5.5 %copy-start.5 = (bf16[1024,3,256]{2,0,1:T(8,128)(2,1)S(1)}, bf16[1024,3,256]{2,0,1:T(8,128)(2,1)}, u32[]{:S(2)}) copy-start(bf16[1024,3,256]{2,0,1:T(8,128)(2,1)} %param.9) | copy-start | bytes 4718596
  0.0 5.5 %copy-start.6 = (bf16[4,6,12,1024]{3,0,2,1:T(4,128)(2,1)S(1)}, bf16[4,6,12,1024]{3,0,2,1:T(4,128)(2,1)}, u32[]{:S(2)}) copy-start(bf16[4,6,12,1024]{3,0,2,1:T(4,128)(2,1)} %param.8) | copy-start | bytes 1769476
  0.0 8.6 %collective-permute-start.2 = (bf16[3,1024,256]{2,1,0:T(8,128)(2,1)}, bf16[3,1024,256]{2,1,0:T(8,128)(2,1)S(1)}, u32[]{:S(2)}, u32[]{:S(2)}) collective-permute-start(bf16[3,1024,256]{2,1,0:T(8,128)(2,1)} %bitcast.8), channel_id=1, source_target_pairs={{0,1},{1,0},{2,3},{3,2},{4,5},{5,4},{6,7},{7,6},{8,9},{9,8},{10,11... | collective-permute-start | bytes 4718600 | tf_op jit(solution)/shard_map/ppermute | solution.py:315
  3.2 5.4 %collective-permute-start = (bf16[256,1024]{1,0:T(8,128)(2,1)}, bf16[256,1024]{1,0:T(8,128)(2,1)S(1)}, u32[]{:S(2)}, u32[]{:S(2)}) collective-permute-start(bf16[256,1024]{1,0:T(8,128)(2,1)} %w0.1), channel_id=1, source_target_pairs={{0,1},{1,0},{2,3},{3,2},{4,5},{5,4},{6,7},{7,6},{8,9},{9,8},{10,11... | collective-permute-start | bytes 1572872 | tf_op jit(solution)/shard_map/ppermute | solution.py:315
  3.2 5.4 %collective-permute-start.1 = (bf16[256,1024]{1,0:T(8,128)(2,1)}, bf16[256,1024]{1,0:T(8,128)(2,1)S(1)}, u32[]{:S(2)}, u32[]{:S(2)}) collective-permute-start(bf16[256,1024]{1,0:T(8,128)(2,1)} %o_own.1), channel_id=1, source_target_pairs={{0,1},{1,0},{2,3},{3,2},{4,5},{5,4},{6,7},{7,6},{8,9},{9,8},{10,11... | collective-permute-start | bytes 1572872 | tf_op jit(solution)/shard_map/ppermute | solution.py:315
  3.8 0.7 %copy-start.7 = (f32[2,4,37]{2,1,0:T(4,128)S(1)}, f32[2,4,37]{2,1,0:T(4,128)}, u32[]{:S(2)}) copy-start(f32[2,4,37]{2,1,0:T(4,128)} %table.1) | copy-start | bytes 3556
  5.3 4.8 %copy-start.4 = (bf16[256,1024]{1,0:T(8,128)(2,1)S(1)}, bf16[256,1024]{1,0:T(8,128)(2,1)}, u32[]{:S(2)}) copy-start(bf16[256,1024]{1,0:T(8,128)(2,1)} %w0.1) | copy-start | bytes 1572868
  5.3 3.3 %collective-permute-start.3 = (bf16[32,256]{1,0:T(8,128)(2,1)S(1)}, bf16[32,256]{1,0:T(8,128)(2,1)S(1)}, u32[]{:S(2)}, u32[]{:S(2)}) collective-permute-start(bf16[32,256]{1,0:T(8,128)(2,1)S(1)} %get-tuple-element.43.b_own), channel_id=1, source_target_pairs={{0,1},{1,0},{2,3},{3,2},{4,5},{5,4},{6,7},{7,6},{8,9},{9,8},{10,11... | collective-permute-start | bytes 49160 | tf_op jit(solution)/shard_map/ppermute | solution.py:315
  5.5 6.4 %copy-start = (bf16[1024,1024]{1,0:T(8,128)(2,1)S(1)}, bf16[1024,1024]{1,0:T(8,128)(2,1)}, u32[]{:S(2)}) copy-start(bf16[1024,1024]{1,0:T(8,128)(2,1)} %u0.3) | copy-start | bytes 6291460
  5.5 7.3 %copy-start.1 = (bf16[1024,1024]{1,0:T(8,128)(2,1)S(1)}, bf16[1024,1024]{1,0:T(8,128)(2,1)}, u32[]{:S(2)}) copy-start(bf16[1024,1024]{1,0:T(8,128)(2,1)} %d0.3) | copy-start | bytes 6291460
  8.6 1.4 %collective-permute-start.4 = (bf16[160,256]{1,0:T(8,128)(2,1)S(1)}, bf16[160,256]{1,0:T(8,128)(2,1)S(1)}, u32[]{:S(2)}, u32[]{:S(2)}) collective-permute-start(bf16[160,256]{1,0:T(8,128)(2,1)S(1)} %get-tuple-element.45), channel_id=1, source_target_pairs={{0,1},{1,0},{2,3},{3,2},{4,5},{5,4},{6,7},{7,6},{8,9},{9,8},{10,11... | collective-permute-start | bytes 245768 | tf_op jit(solution)/shard_map/ppermute | solution.py:315
  10.4 5.5 %collective-permute-start.5 = (bf16[80,1024]{1,0:T(8,128)(2,1)S(1)}, bf16[80,1024]{1,0:T(8,128)(2,1)S(1)}, u32[]{:S(2)}, u32[]{:S(2)}) collective-permute-start(bf16[80,1024]{1,0:T(8,128)(2,1)S(1)} %get-tuple-element.48.mine), channel_id=1, source_target_pairs={{0,2},{1,3},{2,0},{3,1},{4,6},{5,7},{6,4},{7,5},{8,10},{9,11},{10,... | collective-permute-start | bytes 491528 | tf_op jit(solution)/shard_map/ppermute | solution.py:315
  10.5 14.5 %collective-permute-start.8 = (bf16[80,1024]{1,0:T(8,128)(2,1)S(1)}, bf16[80,1024]{1,0:T(8,128)(2,1)S(1)}, u32[]{:S(2)}, u32[]{:S(2)}) collective-permute-start(bf16[80,1024]{1,0:T(8,128)(2,1)S(1)} %get-tuple-element.55.mine), channel_id=1, source_target_pairs={{0,2},{1,3},{2,0},{3,1},{4,6},{5,7},{6,4},{7,5},{8,10},{9,11},{10,... | collective-permute-start | bytes 491528 | tf_op jit(solution)/shard_map/ppermute | solution.py:315
  11.9 25.3 %collective-permute-start.11 = (bf16[1024,1024]{1,0:T(8,128)(2,1)S(1)}, bf16[1024,1024]{1,0:T(8,128)(2,1)S(1)}, u32[]{:S(2)}, u32[]{:S(2)}) collective-permute-start(bf16[1024,1024]{1,0:T(8,128)(2,1)S(1)} %copy-done), channel_id=1, source_target_pairs={{0,1},{1,0},{2,3},{3,2},{4,5},{5,4},{6,7},{7,6},{8,9},{9,8},{10,11... | collective-permute-start | bytes 6291464 | tf_op jit(solution)/shard_map/ppermute | solution.py:315
  12.8 24.4 %collective-permute-start.12 = (bf16[1024,1024]{1,0:T(8,128)(2,1)S(1)}, bf16[1024,1024]{1,0:T(8,128)(2,1)S(1)}, u32[]{:S(2)}, u32[]{:S(2)}) collective-permute-start(bf16[1024,1024]{1,0:T(8,128)(2,1)S(1)} %copy-done.1), channel_id=1, source_target_pairs={{0,1},{1,0},{2,3},{3,2},{4,5},{5,4},{6,7},{7,6},{8,9},{9,8},{10,11... | collective-permute-start | bytes 6291464 | tf_op jit(solution)/shard_map/ppermute | solution.py:315
  16.0 10.1 %collective-permute-start.6 = (bf16[40,1024]{1,0:T(8,128)(2,1)S(1)}, bf16[40,1024]{1,0:T(8,128)(2,1)S(1)}, u32[]{:S(2)}, u32[]{:S(2)}) collective-permute-start(bf16[40,1024]{1,0:T(8,128)(2,1)S(1)} %get-tuple-element.53), channel_id=1, source_target_pairs={{0,30},{1,31},{2,28},{3,29},{4,0},{5,1},{6,2},{7,3},{8,4},{9,5},{1... | collective-permute-start | bytes 245768 | tf_op jit(solution)/shard_map/ppermute | solution.py:315
  19.2 7.2 %collective-permute-start.7 = (bf16[40,1024]{1,0:T(8,128)(2,1)S(1)}, bf16[40,1024]{1,0:T(8,128)(2,1)S(1)}, u32[]{:S(2)}, u32[]{:S(2)}) collective-permute-start(bf16[40,1024]{1,0:T(8,128)(2,1)S(1)} %get-tuple-element.54), channel_id=1, source_target_pairs={{0,254},{1,255},{2,252},{3,253},{4,224},{5,225},{6,226},{7,227},{8... | collective-permute-start | bytes 245768 | tf_op jit(solution)/shard_map/ppermute | solution.py:315
  25.1 3.6 %copy-start.2 = (bf16[1024,3,256]{2,0,1:T(8,128)(2,1)S(1)}, bf16[1024,3,256]{2,0,1:T(8,128)(2,1)}, u32[]{:S(2)}) copy-start(bf16[1024,3,256]{2,0,1:T(8,128)(2,1)} %param.10) | copy-start | bytes 4718596
  25.1 3.6 %copy-start.3 = (bf16[256,1024]{1,0:T(8,128)(2,1)S(1)}, bf16[256,1024]{1,0:T(8,128)(2,1)}, u32[]{:S(2)}) copy-start(bf16[256,1024]{1,0:T(8,128)(2,1)} %o_own.1) | copy-start | bytes 1572868
  25.1 3.5 %collective-permute-start.9 = (bf16[40,1024]{1,0:T(8,128)(2,1)S(1)}, bf16[40,1024]{1,0:T(8,128)(2,1)S(1)}, u32[]{:S(2)}, u32[]{:S(2)}) collective-permute-start(bf16[40,1024]{1,0:T(8,128)(2,1)S(1)} %get-tuple-element.58), channel_id=1, source_target_pairs={{0,224},{1,225},{2,226},{3,227},{4,228},{5,229},{6,230},{7,231},{8... | collective-permute-start | bytes 245768 | tf_op jit(solution)/shard_map/ppermute | solution.py:315
  32.9 4.3 %collective-permute-start.10 = (bf16[80,1024]{1,0:T(8,128)(2,1)S(1)}, bf16[80,1024]{1,0:T(8,128)(2,1)S(1)}, u32[]{:S(2)}, u32[]{:S(2)}) collective-permute-start(bf16[80,1024]{1,0:T(8,128)(2,1)S(1)} %get-tuple-element.62.mine), channel_id=1, source_target_pairs={{0,2},{1,3},{2,0},{3,1},{4,6},{5,7},{6,4},{7,5},{8,10},{9,11},{10,... | collective-permute-start | bytes 491528 | tf_op jit(solution)/shard_map/ppermute | solution.py:315
  33.0 6.1 %collective-permute-start.14 = (bf16[80,1024]{1,0:T(8,128)(2,1)S(1)}, bf16[80,1024]{1,0:T(8,128)(2,1)S(1)}, u32[]{:S(2)}, u32[]{:S(2)}) collective-permute-start(bf16[80,1024]{1,0:T(8,128)(2,1)S(1)} %get-tuple-element.69.mine), channel_id=1, source_target_pairs={{0,2},{1,3},{2,0},{3,1},{4,6},{5,7},{6,4},{7,5},{8,10},{9,11},{10,... | collective-permute-start | bytes 491528 | tf_op jit(solution)/shard_map/ppermute | solution.py:315
  39.0 5.9 %collective-permute-start.13 = (bf16[80,1024]{1,0:T(8,128)(2,1)S(1)}, bf16[80,1024]{1,0:T(8,128)(2,1)S(1)}, u32[]{:S(2)}, u32[]{:S(2)}) collective-permute-start(bf16[80,1024]{1,0:T(8,128)(2,1)S(1)} %shard_map.89.mine), channel_id=1, source_target_pairs={{0,2},{1,3},{2,0},{3,1},{4,6},{5,7},{6,4},{7,5},{8,10},{9,11},{10,... | collective-permute-start | bytes 491528 | tf_op jit(solution)/shard_map/ppermute | solution.py:315
  41.0 5.7 %collective-permute-start.15 = (bf16[80,1024]{1,0:T(8,128)(2,1)S(1)}, bf16[80,1024]{1,0:T(8,128)(2,1)S(1)}, u32[]{:S(2)}, u32[]{:S(2)}) collective-permute-start(bf16[80,1024]{1,0:T(8,128)(2,1)S(1)} %shard_map.91.mine), channel_id=1, source_target_pairs={{0,2},{1,3},{2,0},{3,1},{4,6},{5,7},{6,4},{7,5},{8,10},{9,11},{10,... | collective-permute-start | bytes 491528 | tf_op jit(solution)/shard_map/ppermute | solution.py:315
  44.9 6.7 %collective-permute-start.19 = (bf16[40,1024]{1,0:T(8,128)(2,1)S(1)}, bf16[40,1024]{1,0:T(8,128)(2,1)S(1)}, u32[]{:S(2)}, u32[]{:S(2)}) collective-permute-start(bf16[40,1024]{1,0:T(8,128)(2,1)S(1)} %get-tuple-element.73), channel_id=1, source_target_pairs={{0,4},{1,5},{2,6},{3,7},{4,8},{5,9},{6,10},{7,11},{8,12},{9,13},{1... | collective-permute-start | bytes 245768 | tf_op jit(solution)/shard_map/ppermute | solution.py:315
  46.0 11.1 %collective-permute-start.20 = (bf16[40,1024]{1,0:T(8,128)(2,1)S(1)}, bf16[40,1024]{1,0:T(8,128)(2,1)S(1)}, u32[]{:S(2)}, u32[]{:S(2)}) collective-permute-start(bf16[40,1024]{1,0:T(8,128)(2,1)S(1)} %get-tuple-element.74), channel_id=1, source_target_pairs={{0,36},{1,37},{2,38},{3,39},{4,40},{5,41},{6,42},{7,43},{8,44},{9,... | collective-permute-start | bytes 245768 | tf_op jit(solution)/shard_map/ppermute | solution.py:315
  46.7 13.9 %collective-permute-start.16 = (bf16[40,1024]{1,0:T(8,128)(2,1)S(1)}, bf16[40,1024]{1,0:T(8,128)(2,1)S(1)}, u32[]{:S(2)}, u32[]{:S(2)}) collective-permute-start(bf16[40,1024]{1,0:T(8,128)(2,1)S(1)} %get-tuple-element.72), channel_id=1, source_target_pairs={{0,32},{1,33},{2,34},{3,35},{4,36},{5,37},{6,38},{7,39},{8,40},{9,... | collective-permute-start | bytes 245768 | tf_op jit(solution)/shard_map/ppermute | solution.py:315
  51.6 9.4 %collective-permute-start.21 = (bf16[40,1024]{1,0:T(8,128)(2,1)S(1)}, bf16[40,1024]{1,0:T(8,128)(2,1)S(1)}, u32[]{:S(2)}, u32[]{:S(2)}) collective-permute-start(bf16[40,1024]{1,0:T(8,128)(2,1)S(1)} %collective-permute-done.19.m0), channel_id=1, source_target_pairs={{0,1},{1,0},{2,3},{3,2},{4,5},{5,4},{6,7},{7,6},{8,9},{9,8},{10,11... | collective-permute-start | bytes 245768 | tf_op jit(solution)/shard_map/ppermute | solution.py:315
  57.1 4.3 %collective-permute-start.22 = (bf16[40,1024]{1,0:T(8,128)(2,1)S(1)}, bf16[40,1024]{1,0:T(8,128)(2,1)S(1)}, u32[]{:S(2)}, u32[]{:S(2)}) collective-permute-start(bf16[40,1024]{1,0:T(8,128)(2,1)S(1)} %collective-permute-done.20.m1), channel_id=1, source_target_pairs={{0,1},{1,0},{2,3},{3,2},{4,5},{5,4},{6,7},{7,6},{8,9},{9,8},{10,11... | collective-permute-start | bytes 245768 | tf_op jit(solution)/shard_map/ppermute | solution.py:315
  60.5 2.0 %collective-permute-start.17 = (bf16[40,1024]{1,0:T(8,128)(2,1)S(1)}, bf16[40,1024]{1,0:T(8,128)(2,1)S(1)}, u32[]{:S(2)}, u32[]{:S(2)}) collective-permute-start(bf16[40,1024]{1,0:T(8,128)(2,1)S(1)} %get-tuple-element.71.m0), channel_id=1, source_target_pairs={{0,1},{1,0},{2,3},{3,2},{4,5},{5,4},{6,7},{7,6},{8,9},{9,8},{10,11... | collective-permute-start | bytes 245768 | tf_op jit(solution)/shard_map/ppermute | solution.py:315
  60.5 2.0 %collective-permute-start.18 = (bf16[40,1024]{1,0:T(8,128)(2,1)S(1)}, bf16[40,1024]{1,0:T(8,128)(2,1)S(1)}, u32[]{:S(2)}, u32[]{:S(2)}) collective-permute-start(bf16[40,1024]{1,0:T(8,128)(2,1)S(1)} %collective-permute-done.16.m1), channel_id=1, source_target_pairs={{0,1},{1,0},{2,3},{3,2},{4,5},{5,4},{6,7},{7,6},{8,9},{9,8},{10,11... | collective-permute-start | bytes 245768 | tf_op jit(solution)/shard_map/ppermute | solution.py:315

commit v5 on v4

--- a/solution.py
+++ b/solution.py
@@ -76,9 +76,9 @@
 
 
 def kept_place(index):
-    piece = (index * 205) >> 13
-    slot = index - piece * ROWS
-    return ((piece + 2) & 3, slot) + piece_place(slot)
+    quad = (index * 205) >> 13
+    slot = index - quad * ROWS
+    return (quad, slot) + piece_place(slot)
 
 
 def real_level(level, core):
@@ -210,7 +210,7 @@
     lane = iota((KEPT, 128), 1)
     j = lane & (FEAT - 1)
     split_levels = core_index() == 1
-    split_rows = lax.axis_index("lat") == lax.axis_size("lat") - 1
+    split_rows = lax.axis_index("lat") == 0
     ban_level = (j < WL) & (j != level)
     ban_row = (j >= F_Y) & (j < F_Y + WY) & ((j >= F_Y + SY) != (row >= SY))
     ban = jnp.where(ban_level, split_levels.astype(jnp.int32), jnp.where(ban_row, split_rows.astype(jnp.int32), 0))
@@ -321,12 +321,12 @@
         return move(value, lambda a, b, m: (a, b, m ^ 2))
 
     def out_to(value, dy, dx):
+        return move(value, lambda a, b, m: (a + dy, b + dx, m ^ 2 if dx and (b + 1) % turn == 0 else m))
+
+    def home(value, dy, dx):
         return move(value, lambda a, b, m: (a - dy, b - dx, m ^ 2 if dx and b % turn == 0 else m))
 
-    def home(value, dy, dx):
-        return move(value, lambda a, b, m: (a + dy, b + dx, m ^ 2 if dx and (b + 1) % turn == 0 else m))
-
-    full, half, piece = [(KEPT, width)], [(HALF, width)], [(ROWS, width)]
+    half, piece = [(HALF, width)], [(ROWS, width)]
     heads, features = [(KEPT, 256)], [(FEAT, 256)]
 
     tok = tokens.transpose(1, 2, 0, 3).reshape(rows * cols, levels, width)
@@ -346,38 +346,38 @@
     part_a, part_b = call(partial_kernel, half * 2, (keep, given, out_first, f1), 2 * 10**8, 8)
     other_a = chip_swap(part_a)
     other_b = chip_swap(part_b)
-    lon, diag = call(residual_kernel, piece * 2, (part_a, other_a, base_a), 10**6, 8)
-    lon, diag, part_b = tied(lon, diag, part_b)
-    own, lat = call(residual_kernel, piece * 2, (part_b, other_b, base_b), 10**10, 8)
+    diag, lon = call(residual_kernel, piece * 2, (part_a, other_a, base_a), 10**6, 8)
+    diag, lon, part_b = tied(diag, lon, part_b)
+    lat, own = call(residual_kernel, piece * 2, (part_b, other_b, base_b), 10**10, 8)
+    diag = out_to(diag, 1, 1)
     lon = out_to(lon, 0, 1)
-    diag = out_to(diag, 1, 1)
     lat = out_to(lat, 1, 0)
 
-    xn_a = call(norm_kernel, half, (lon, diag), 10**10, 8)
+    xn_a = call(norm_kernel, half, (diag, lon), 10**10, 8)
     part_a, part_b = call(
         second_kernel,
         half * 2,
-        (xn_a, own, lat, w_second, w_sib, out_second, s1, bias2, bias2_sib),
+        (xn_a, lat, own, w_second, w_sib, out_second, s1, bias2, bias2_sib),
         10**9,
         16,
     )
     other_a = chip_swap(part_a)
     other_b = chip_swap(part_b)
     mlp = (up_weight, u1, down_weight, d1)
-    part_a = call(mlp_kernel, half, (part_a, other_a, lon, diag, *mlp), 10**9, 20)
+    part_a = call(mlp_kernel, half, (part_a, other_a, diag, lon, *mlp), 10**9, 20)
     part_a, part_b = tied(part_a, part_b)
     other_a = chip_swap(part_a)
-    part_b = call(mlp_kernel, half, (part_b, other_b, own, lat, *mlp), 10**9, 20)
+    part_b = call(mlp_kernel, half, (part_b, other_b, lat, own, *mlp), 10**9, 20)
     other_b = chip_swap(part_b)
-    lon, diag = call(sum_kernel, piece * 2, (part_a, other_a), 10**6, 8)
-    lon, diag, part_b = tied(lon, diag, part_b)
+    diag, lon = call(sum_kernel, piece * 2, (part_a, other_a), 10**6, 8)
+    diag, lon, part_b = tied(diag, lon, part_b)
+    diag = home(diag, 1, 1)
     lon = home(lon, 0, 1)
-    diag = home(diag, 1, 1)
-    own, lat = call(sum_kernel, piece * 2, (part_b, other_b), 10**10, 8)
+    lat, own = call(sum_kernel, piece * 2, (part_b, other_b), 10**10, 8)
     lat = home(lat, 1, 0)
     shape = (rows * cols, levels, width)
-    result = place(0, (lon, diag, core_swap(lon), core_swap(diag)), shape, ())
-    result = place(1, (own, lat, core_swap(own), core_swap(lat)), shape, (result,))
+    result = place(1, (diag, lon, core_swap(diag), core_swap(lon)), shape, ())
+    result = place(0, (lat, own, core_swap(lat), core_swap(own)), shape, (result,))
     return result.reshape(rows, cols, levels, width).transpose(2, 0, 1, 3)
 
 

time: 63.9 us -> 60.5 us (0.947)
  starting transfers between devices: 30.7 us -> 28.7 us
  waiting for transfers between devices: 17.2 us -> 15.9 us
    ppermute x23, starting transfers between devices: 30.7 us -> 28.7 us  [move(): return lax.ppermute(value, AXES, pairs(counts, target))]
    ppermute x23, waiting for transfers between devices: 17.2 us -> 15.9 us  [move(): return lax.ppermute(value, AXES, pairs(counts, target))]
  transfers between devices with their start and end apart: 23 -> 23, of which waited for: 9 -> 7; matrix products, arithmetic and copies ran while one was open for 0% -> 0% of each run, Pallas kernels for 21% -> 22%
where the time goes in v5:
time: 60.5 us; the launch traced here: 60.4 us
  starting transfers between devices  28.7 us (47%)
  waiting for transfers between devices  15.9 us (26%)
  Pallas kernels  14.7 us (24%)
  local copies, waits for them, and re-layouts  0.72 us (1%)
    ppermute x23, starting transfers between devices, move(): return lax.ppermute(value, AXES, pairs(counts, target))  28.7 us
    ppermute x23, waiting for transfers between devices, move(): return lax.ppermute(value, AXES, pairs(counts, target))  15.9 us
    pallas_call x11, Pallas kernels, call(): pl.pallas_call(kernel, out_shape=shapes, in_specs=[pl.BlockSpec(memory_sp...  12.6 us
    pallas_call x2, Pallas kernels, place(): pl.pallas_call(functools.partial(place_kernel, half), out_shape=jax.Shape...  2.14 us
  transfers between devices with their start and end apart: 23, of which 7 were waited for; matrix products, arithmetic and copies ran while one was open for 0% of the time, Pallas kernels for 22%

profile of v5, /device:TPU:1, one launch (start us, length us, event | category | flops | bytes accessed | tf_op | source)
XLA Modules:
  0.0 60.4 jit_solution(3228484350558896466)
XLA Ops:
  0.0 3.2 %collective-permute-start.2 = (bf16[3,1024,256]{2,1,0:T(8,128)(2,1)}, bf16[3,1024,256]{2,1,0:T(8,128)(2,1)S(1)}, u32[]{:S(2)}, u32[]{:S(2)}) collective-permute-start(bf16[3,1024,256]{2,1,0:T(8,128)(2,1)} %bitcast.8), channel_id=1, source_target_pairs={{0,1},{1,0},{2,3},{3,2},{4,5},{5,4},{6,7},{7,6},{8,9},{9,8},{10,11... | collective-permute-start | bytes 4718600 | tf_op jit(solution)/shard_map/ppermute | solution.py:315
  3.2 0.5 collective-permute-start.1
  3.8 0.7 %copy-done.7 = f32[2,4,37]{2,1,0:T(4,128)S(1)} copy-done((f32[2,4,37]{2,1,0:T(4,128)S(1)}, f32[2,4,37]{2,1,0:T(4,128)}, u32[]{:S(2)}) %copy-start.7) | copy-done | bytes 1208
  4.4 0.8 %shard_map.82 = (bf16[32,256]{1,0:T(8,128)(2,1)S(1)}, bf16[32,256]{1,0:T(8,128)(2,1)S(1)}) custom-call(f32[2,4,37]{2,1,0:T(4,128)S(1)} %copy-done.7), custom_call_target="tpu_custom_call" | custom-call | flops 5000000000 | bytes 33952 | tf_op jit(solution)/shard_map/pallas_call | solution.py:295
  5.5 3.1 %shard_map.83 = (bf16[160,256]{1,0:T(8,128)(2,1)S(1)}, bf16[160,256]{1,0:T(8,128)(2,1)S(1)}, bf16[80,1024]{1,0:T(8,128)(2,1)S(1)}, bf16[80,1024]{1,0:T(8,128)(2,1)S(1)}) custom-call(bf16[72,4,1024]{2,1,0:T(4,128)(2,1)S(1)} %bitcast.11, bf16[3,1024,256]{2,1,0:T(8,128)(2,1)S(1)} %bitcast.10, bf16[32,256]{1,0:T(8,128)(2,1)S(1)} %get-tuple-element.40.bias), custom_call_target="tpu_custom_call" | custom-call | flops 1000000000 | bytes 2670592 | tf_op jit(solution)/shard_map/pallas_call | solution.py:295
  8.6 0.5 collective-permute-start.4
  9.1 0.9 %collective-permute-done.4.o1 = bf16[160,256]{1,0:T(8,128)(2,1)S(1)} collective-permute-done((bf16[160,256]{1,0:T(8,128)(2,1)S(1)}, bf16[160,256]{1,0:T(8,128)(2,1)S(1)}, u32[]{:S(2)}, u32[]{:S(2)}) %collective-permute-start.4) | collective-permute-done | bytes 81952 | tf_op jit(solution)/shard_map/ppermute | solution.py:315
  10.0 0.3 shard_map.84
  10.5 1.5 %collective-permute-start.8 = (bf16[80,1024]{1,0:T(8,128)(2,1)S(1)}, bf16[80,1024]{1,0:T(8,128)(2,1)S(1)}, u32[]{:S(2)}, u32[]{:S(2)}) collective-permute-start(bf16[80,1024]{1,0:T(8,128)(2,1)S(1)} %get-tuple-element.55.mine), channel_id=1, source_target_pairs={{0,2},{1,3},{2,0},{3,1},{4,6},{5,7},{6,4},{7,5},{8,10},{9,11},{10,... | collective-permute-start | bytes 491528 | tf_op jit(solution)/shard_map/ppermute | solution.py:315
  11.9 0.9 %collective-permute-start.11 = (bf16[1024,1024]{1,0:T(8,128)(2,1)S(1)}, bf16[1024,1024]{1,0:T(8,128)(2,1)S(1)}, u32[]{:S(2)}, u32[]{:S(2)}) collective-permute-start(bf16[1024,1024]{1,0:T(8,128)(2,1)S(1)} %copy-done), channel_id=1, source_target_pairs={{0,1},{1,0},{2,3},{3,2},{4,5},{5,4},{6,7},{7,6},{8,9},{9,8},{10,11... | collective-permute-start | bytes 6291464 | tf_op jit(solution)/shard_map/ppermute | solution.py:315
  12.9 3.0 %collective-permute-done.5.other = bf16[80,1024]{1,0:T(8,128)(2,1)S(1)} collective-permute-done((bf16[80,1024]{1,0:T(8,128)(2,1)S(1)}, bf16[80,1024]{1,0:T(8,128)(2,1)S(1)}, u32[]{:S(2)}, u32[]{:S(2)}) %collective-permute-start.5) | collective-permute-done | bytes 163872 | tf_op jit(solution)/shard_map/ppermute | solution.py:315
  16.0 1.0 %collective-permute-start.6 = (bf16[40,1024]{1,0:T(8,128)(2,1)S(1)}, bf16[40,1024]{1,0:T(8,128)(2,1)S(1)}, u32[]{:S(2)}, u32[]{:S(2)}) collective-permute-start(bf16[40,1024]{1,0:T(8,128)(2,1)S(1)} %get-tuple-element.53), channel_id=1, source_target_pairs={{0,36},{1,37},{2,38},{3,39},{4,40},{5,41},{6,42},{7,43},{8,44},{9,... | collective-permute-start | bytes 245768 | tf_op jit(solution)/shard_map/ppermute | solution.py:315
  17.0 1.3 %collective-permute-start.7 = (bf16[40,1024]{1,0:T(8,128)(2,1)S(1)}, bf16[40,1024]{1,0:T(8,128)(2,1)S(1)}, u32[]{:S(2)}, u32[]{:S(2)}) collective-permute-start(bf16[40,1024]{1,0:T(8,128)(2,1)S(1)} %get-tuple-element.54), channel_id=1, source_target_pairs={{0,4},{1,5},{2,6},{3,7},{4,8},{5,9},{6,10},{7,11},{8,12},{9,13},{1... | collective-permute-start | bytes 245768 | tf_op jit(solution)/shard_map/ppermute | solution.py:315
  18.3 1.1 %collective-permute-done.8.other = bf16[80,1024]{1,0:T(8,128)(2,1)S(1)} collective-permute-done((bf16[80,1024]{1,0:T(8,128)(2,1)S(1)}, bf16[80,1024]{1,0:T(8,128)(2,1)S(1)}, u32[]{:S(2)}, u32[]{:S(2)}) %collective-permute-start.8) | collective-permute-done | bytes 163872 | tf_op jit(solution)/shard_map/ppermute | solution.py:315
  19.5 0.8 %collective-permute-start.9 = (bf16[40,1024]{1,0:T(8,128)(2,1)S(1)}, bf16[40,1024]{1,0:T(8,128)(2,1)S(1)}, u32[]{:S(2)}, u32[]{:S(2)}) collective-permute-start(bf16[40,1024]{1,0:T(8,128)(2,1)S(1)} %get-tuple-element.57), channel_id=1, source_target_pairs={{0,32},{1,33},{2,34},{3,35},{4,36},{5,37},{6,38},{7,39},{8,40},{9,... | collective-permute-start | bytes 245768 | tf_op jit(solution)/shard_map/ppermute | solution.py:315
  20.3 6.2 %collective-permute-done.6.p0 = bf16[40,1024]{1,0:T(8,128)(2,1)S(1)} collective-permute-done((bf16[40,1024]{1,0:T(8,128)(2,1)S(1)}, bf16[40,1024]{1,0:T(8,128)(2,1)S(1)}, u32[]{:S(2)}, u32[]{:S(2)}) %collective-permute-start.6) | collective-permute-done | bytes 81952 | tf_op jit(solution)/shard_map/ppermute | solution.py:315
  26.7 4.3 %shard_map.88 = (bf16[80,1024]{1,0:T(8,128)(2,1)S(1)}, bf16[80,1024]{1,0:T(8,128)(2,1)S(1)}) custom-call(bf16[80,1024]{1,0:T(8,128)(2,1)S(1)} %shard_map.86.xn_a, bf16[40,1024]{1,0:T(8,128)(2,1)S(1)} %collective-permute-done.9.p2.p0, bf16[40,1024]{1,0:T(8,128)(2,1)S(1)} %get-tuple-element.58.p3.p1, bf16[3,1024,256]{2,1,0:T(8,128)(2,1)S(1)} %bitcast.9, ...), custom_call_target="tpu_custom_call" | custom-call | flops 1000000000 | bytes 4882432 | tf_op jit(solution)/shard_map/pallas_call | solution.py:295
  31.0 0.3 collective-permute-start.10
  31.3 1.2 %collective-permute-start.14 = (bf16[80,1024]{1,0:T(8,128)(2,1)S(1)}, bf16[80,1024]{1,0:T(8,128)(2,1)S(1)}, u32[]{:S(2)}, u32[]{:S(2)}) collective-permute-start(bf16[80,1024]{1,0:T(8,128)(2,1)S(1)} %get-tuple-element.69.mine), channel_id=1, source_target_pairs={{0,2},{1,3},{2,0},{3,1},{4,6},{5,7},{6,4},{7,5},{8,10},{9,11},{10,... | collective-permute-start | bytes 491528 | tf_op jit(solution)/shard_map/ppermute | solution.py:315
  32.6 2.7 %collective-permute-done.10.other = bf16[80,1024]{1,0:T(8,128)(2,1)S(1)} collective-permute-done((bf16[80,1024]{1,0:T(8,128)(2,1)S(1)}, bf16[80,1024]{1,0:T(8,128)(2,1)S(1)}, u32[]{:S(2)}, u32[]{:S(2)}) %collective-permute-start.10) | collective-permute-done | bytes 163872 | tf_op jit(solution)/shard_map/ppermute | solution.py:315
  35.3 1.8 %shard_map.89.mine = bf16[80,1024]{1,0:T(8,128)(2,1)S(1)} custom-call(bf16[80,1024]{1,0:T(8,128)(2,1)S(1)} %get-tuple-element.62.mine, bf16[80,1024]{1,0:T(8,128)(2,1)S(1)} %collective-permute-done.10.other, bf16[40,1024]{1,0:T(8,128)(2,1)S(1)} %collective-permute-done.6.p0, bf16[40,1024]{1,0:T(8,128)(2,1)S(1)} %collective-permute-done.7.p1, ...), custom_call_target="tpu_custom_call" | custom-call | flops 1000000000 | bytes 9043968 | tf_op jit(solution)/shard_map/pallas_call | solution.py:295
  37.6 1.8 %shard_map.91.mine = bf16[80,1024]{1,0:T(8,128)(2,1)S(1)} custom-call(bf16[80,1024]{1,0:T(8,128)(2,1)S(1)} %get-tuple-element.69.mine, bf16[80,1024]{1,0:T(8,128)(2,1)S(1)} %collective-permute-done.14.other, bf16[40,1024]{1,0:T(8,128)(2,1)S(1)} %collective-permute-done.9.p2.p0, bf16[40,1024]{1,0:T(8,128)(2,1)S(1)} %get-tuple-element.58.p3.p1, ...), custom_call_target="tpu_custom_call" | custom-call | flops 1000000000 | bytes 9043968 | tf_op jit(solution)/shard_map/pallas_call | solution.py:295
  39.4 1.2 %collective-permute-start.15 = (bf16[80,1024]{1,0:T(8,128)(2,1)S(1)}, bf16[80,1024]{1,0:T(8,128)(2,1)S(1)}, u32[]{:S(2)}, u32[]{:S(2)}) collective-permute-start(bf16[80,1024]{1,0:T(8,128)(2,1)S(1)} %shard_map.91.mine), channel_id=1, source_target_pairs={{0,2},{1,3},{2,0},{3,1},{4,6},{5,7},{6,4},{7,5},{8,10},{9,11},{10,... | collective-permute-start | bytes 491528 | tf_op jit(solution)/shard_map/ppermute | solution.py:315
  40.6 1.7 %collective-permute-done.13.other = bf16[80,1024]{1,0:T(8,128)(2,1)S(1)} collective-permute-done((bf16[80,1024]{1,0:T(8,128)(2,1)S(1)}, bf16[80,1024]{1,0:T(8,128)(2,1)S(1)}, u32[]{:S(2)}, u32[]{:S(2)}) %collective-permute-start.13) | collective-permute-done | bytes 163872 | tf_op jit(solution)/shard_map/ppermute | solution.py:315
  42.3 5.2 %collective-permute-start.19 = (bf16[40,1024]{1,0:T(8,128)(2,1)S(1)}, bf16[40,1024]{1,0:T(8,128)(2,1)S(1)}, u32[]{:S(2)}, u32[]{:S(2)}) collective-permute-start(bf16[40,1024]{1,0:T(8,128)(2,1)S(1)} %get-tuple-element.73), channel_id=1, source_target_pairs={{0,254},{1,255},{2,252},{3,253},{4,224},{5,225},{6,226},{7,227},{8... | collective-permute-start | bytes 245768 | tf_op jit(solution)/shard_map/ppermute | solution.py:315
  47.5 0.7 %collective-permute-start.20 = (bf16[40,1024]{1,0:T(8,128)(2,1)S(1)}, bf16[40,1024]{1,0:T(8,128)(2,1)S(1)}, u32[]{:S(2)}, u32[]{:S(2)}) collective-permute-start(bf16[40,1024]{1,0:T(8,128)(2,1)S(1)} %get-tuple-element.74), channel_id=1, source_target_pairs={{0,30},{1,31},{2,28},{3,29},{4,0},{5,1},{6,2},{7,3},{8,4},{9,5},{1... | collective-permute-start | bytes 245768 | tf_op jit(solution)/shard_map/ppermute | solution.py:315
  48.3 0.9 %collective-permute-start.16 = (bf16[40,1024]{1,0:T(8,128)(2,1)S(1)}, bf16[40,1024]{1,0:T(8,128)(2,1)S(1)}, u32[]{:S(2)}, u32[]{:S(2)}) collective-permute-start(bf16[40,1024]{1,0:T(8,128)(2,1)S(1)} %get-tuple-element.71), channel_id=1, source_target_pairs={{0,224},{1,225},{2,226},{3,227},{4,228},{5,229},{6,230},{7,231},{8... | collective-permute-start | bytes 245768 | tf_op jit(solution)/shard_map/ppermute | solution.py:315
  49.2 5.6 %collective-permute-start.21 = (bf16[40,1024]{1,0:T(8,128)(2,1)S(1)}, bf16[40,1024]{1,0:T(8,128)(2,1)S(1)}, u32[]{:S(2)}, u32[]{:S(2)}) collective-permute-start(bf16[40,1024]{1,0:T(8,128)(2,1)S(1)} %collective-permute-done.19.m0), channel_id=1, source_target_pairs={{0,1},{1,0},{2,3},{3,2},{4,5},{5,4},{6,7},{7,6},{8,9},{9,8},{10,11... | collective-permute-start | bytes 245768 | tf_op jit(solution)/shard_map/ppermute | solution.py:315
  54.8 1.9 %collective-permute-start.22 = (bf16[40,1024]{1,0:T(8,128)(2,1)S(1)}, bf16[40,1024]{1,0:T(8,128)(2,1)S(1)}, u32[]{:S(2)}, u32[]{:S(2)}) collective-permute-start(bf16[40,1024]{1,0:T(8,128)(2,1)S(1)} %collective-permute-done.20.m1), channel_id=1, source_target_pairs={{0,1},{1,0},{2,3},{3,2},{4,5},{5,4},{6,7},{7,6},{8,9},{9,8},{10,11... | collective-permute-start | bytes 245768 | tf_op jit(solution)/shard_map/ppermute | solution.py:315
  56.7 1.3 %collective-permute-start.17 = (bf16[40,1024]{1,0:T(8,128)(2,1)S(1)}, bf16[40,1024]{1,0:T(8,128)(2,1)S(1)}, u32[]{:S(2)}, u32[]{:S(2)}) collective-permute-start(bf16[40,1024]{1,0:T(8,128)(2,1)S(1)} %collective-permute-done.16.m0), channel_id=1, source_target_pairs={{0,1},{1,0},{2,3},{3,2},{4,5},{5,4},{6,7},{7,6},{8,9},{9,8},{10,11... | collective-permute-start | bytes 245768 | tf_op jit(solution)/shard_map/ppermute | solution.py:315
  58.0 1.1 %shard_map.93.refs_0_ = bf16[72,4,1024]{2,1,0:T(4,128)(2,1)} custom-call(bf16[40,1024]{1,0:T(8,128)(2,1)S(1)} %collective-permute-done.19.m0, bf16[40,1024]{1,0:T(8,128)(2,1)S(1)} %collective-permute-done.20.m1, bf16[40,1024]{1,0:T(8,128)(2,1)S(1)} %collective-permute-done.21.s0, bf16[40,1024]{1,0:T(8,128)(2,1)S(1)} %collective-permute-done.22.s1), custom_call_target="tpu_custom_call" | custom-call | flops 10000000000 | bytes 1000000 | tf_op jit(solution)/shard_map/pallas_call | solution.py:277
  59.1 1.1 %shard_map.94 = bf16[72,4,1024]{2,1,0:T(4,128)(2,1)} custom-call(bf16[40,1024]{1,0:T(8,128)(2,1)S(1)} %collective-permute-done.16.m0, bf16[40,1024]{1,0:T(8,128)(2,1)S(1)} %get-tuple-element.72.m1, bf16[40,1024]{1,0:T(8,128)(2,1)S(1)} %collective-permute-done.17.s0, bf16[40,1024]{1,0:T(8,128)(2,1)S(1)} %collective-permute-done.18.s1, ...), custom_call_target="tpu_custom_call", output_to_operand_aliasing={{}: (4, {})} | custom-call | flops 10000000000 | bytes 1000000 | tf_op jit(solution)/shard_map/pallas_call | solution.py:277
  (43 shorter events, 1.4 us)
Async XLA Ops:
  0.0 5.5 %copy-start.5 = (bf16[1024,3,256]{2,0,1:T(8,128)(2,1)S(1)}, bf16[1024,3,256]{2,0,1:T(8,128)(2,1)}, u32[]{:S(2)}) copy-start(bf16[1024,3,256]{2,0,1:T(8,128)(2,1)} %param.9) | copy-start | bytes 4718596
  0.0 5.5 %copy-start.6 = (bf16[4,6,12,1024]{3,0,2,1:T(4,128)(2,1)S(1)}, bf16[4,6,12,1024]{3,0,2,1:T(4,128)(2,1)}, u32[]{:S(2)}) copy-start(bf16[4,6,12,1024]{3,0,2,1:T(4,128)(2,1)} %param.8) | copy-start | bytes 1769476
  0.0 8.6 %collective-permute-start.2 = (bf16[3,1024,256]{2,1,0:T(8,128)(2,1)}, bf16[3,1024,256]{2,1,0:T(8,128)(2,1)S(1)}, u32[]{:S(2)}, u32[]{:S(2)}) collective-permute-start(bf16[3,1024,256]{2,1,0:T(8,128)(2,1)} %bitcast.8), channel_id=1, source_target_pairs={{0,1},{1,0},{2,3},{3,2},{4,5},{5,4},{6,7},{7,6},{8,9},{9,8},{10,11... | collective-permute-start | bytes 4718600 | tf_op jit(solution)/shard_map/ppermute | solution.py:315
  3.2 5.4 %collective-permute-start = (bf16[256,1024]{1,0:T(8,128)(2,1)}, bf16[256,1024]{1,0:T(8,128)(2,1)S(1)}, u32[]{:S(2)}, u32[]{:S(2)}) collective-permute-start(bf16[256,1024]{1,0:T(8,128)(2,1)} %w0.1), channel_id=1, source_target_pairs={{0,1},{1,0},{2,3},{3,2},{4,5},{5,4},{6,7},{7,6},{8,9},{9,8},{10,11... | collective-permute-start | bytes 1572872 | tf_op jit(solution)/shard_map/ppermute | solution.py:315
  3.2 5.4 %collective-permute-start.1 = (bf16[256,1024]{1,0:T(8,128)(2,1)}, bf16[256,1024]{1,0:T(8,128)(2,1)S(1)}, u32[]{:S(2)}, u32[]{:S(2)}) collective-permute-start(bf16[256,1024]{1,0:T(8,128)(2,1)} %o_own.1), channel_id=1, source_target_pairs={{0,1},{1,0},{2,3},{3,2},{4,5},{5,4},{6,7},{7,6},{8,9},{9,8},{10,11... | collective-permute-start | bytes 1572872 | tf_op jit(solution)/shard_map/ppermute | solution.py:315
  3.8 0.7 %copy-start.7 = (f32[2,4,37]{2,1,0:T(4,128)S(1)}, f32[2,4,37]{2,1,0:T(4,128)}, u32[]{:S(2)}) copy-start(f32[2,4,37]{2,1,0:T(4,128)} %table.1) | copy-start | bytes 3556
  5.3 4.8 %copy-start.4 = (bf16[256,1024]{1,0:T(8,128)(2,1)S(1)}, bf16[256,1024]{1,0:T(8,128)(2,1)}, u32[]{:S(2)}) copy-start(bf16[256,1024]{1,0:T(8,128)(2,1)} %w0.1) | copy-start | bytes 1572868
  5.3 3.3 %collective-permute-start.3 = (bf16[32,256]{1,0:T(8,128)(2,1)S(1)}, bf16[32,256]{1,0:T(8,128)(2,1)S(1)}, u32[]{:S(2)}, u32[]{:S(2)}) collective-permute-start(bf16[32,256]{1,0:T(8,128)(2,1)S(1)} %get-tuple-element.43.b_own), channel_id=1, source_target_pairs={{0,1},{1,0},{2,3},{3,2},{4,5},{5,4},{6,7},{7,6},{8,9},{9,8},{10,11... | collective-permute-start | bytes 49160 | tf_op jit(solution)/shard_map/ppermute | solution.py:315
  5.5 6.4 %copy-start = (bf16[1024,1024]{1,0:T(8,128)(2,1)S(1)}, bf16[1024,1024]{1,0:T(8,128)(2,1)}, u32[]{:S(2)}) copy-start(bf16[1024,1024]{1,0:T(8,128)(2,1)} %u0.3) | copy-start | bytes 6291460
  5.5 7.4 %copy-start.1 = (bf16[1024,1024]{1,0:T(8,128)(2,1)S(1)}, bf16[1024,1024]{1,0:T(8,128)(2,1)}, u32[]{:S(2)}) copy-start(bf16[1024,1024]{1,0:T(8,128)(2,1)} %d0.3) | copy-start | bytes 6291460
  8.6 1.4 %collective-permute-start.4 = (bf16[160,256]{1,0:T(8,128)(2,1)S(1)}, bf16[160,256]{1,0:T(8,128)(2,1)S(1)}, u32[]{:S(2)}, u32[]{:S(2)}) collective-permute-start(bf16[160,256]{1,0:T(8,128)(2,1)S(1)} %get-tuple-element.45), channel_id=1, source_target_pairs={{0,1},{1,0},{2,3},{3,2},{4,5},{5,4},{6,7},{7,6},{8,9},{9,8},{10,11... | collective-permute-start | bytes 245768 | tf_op jit(solution)/shard_map/ppermute | solution.py:315
  10.4 5.5 %collective-permute-start.5 = (bf16[80,1024]{1,0:T(8,128)(2,1)S(1)}, bf16[80,1024]{1,0:T(8,128)(2,1)S(1)}, u32[]{:S(2)}, u32[]{:S(2)}) collective-permute-start(bf16[80,1024]{1,0:T(8,128)(2,1)S(1)} %get-tuple-element.48.mine), channel_id=1, source_target_pairs={{0,2},{1,3},{2,0},{3,1},{4,6},{5,7},{6,4},{7,5},{8,10},{9,11},{10,... | collective-permute-start | bytes 491528 | tf_op jit(solution)/shard_map/ppermute | solution.py:315
  10.5 8.9 %collective-permute-start.8 = (bf16[80,1024]{1,0:T(8,128)(2,1)S(1)}, bf16[80,1024]{1,0:T(8,128)(2,1)S(1)}, u32[]{:S(2)}, u32[]{:S(2)}) collective-permute-start(bf16[80,1024]{1,0:T(8,128)(2,1)S(1)} %get-tuple-element.55.mine), channel_id=1, source_target_pairs={{0,2},{1,3},{2,0},{3,1},{4,6},{5,7},{6,4},{7,5},{8,10},{9,11},{10,... | collective-permute-start | bytes 491528 | tf_op jit(solution)/shard_map/ppermute | solution.py:315
  11.9 23.3 %collective-permute-start.11 = (bf16[1024,1024]{1,0:T(8,128)(2,1)S(1)}, bf16[1024,1024]{1,0:T(8,128)(2,1)S(1)}, u32[]{:S(2)}, u32[]{:S(2)}) collective-permute-start(bf16[1024,1024]{1,0:T(8,128)(2,1)S(1)} %copy-done), channel_id=1, source_target_pairs={{0,1},{1,0},{2,3},{3,2},{4,5},{5,4},{6,7},{7,6},{8,9},{9,8},{10,11... | collective-permute-start | bytes 6291464 | tf_op jit(solution)/shard_map/ppermute | solution.py:315
  12.8 22.4 %collective-permute-start.12 = (bf16[1024,1024]{1,0:T(8,128)(2,1)S(1)}, bf16[1024,1024]{1,0:T(8,128)(2,1)S(1)}, u32[]{:S(2)}, u32[]{:S(2)}) collective-permute-start(bf16[1024,1024]{1,0:T(8,128)(2,1)S(1)} %copy-done.1), channel_id=1, source_target_pairs={{0,1},{1,0},{2,3},{3,2},{4,5},{5,4},{6,7},{7,6},{8,9},{9,8},{10,11... | collective-permute-start | bytes 6291464 | tf_op jit(solution)/shard_map/ppermute | solution.py:315
  16.0 10.5 %collective-permute-start.6 = (bf16[40,1024]{1,0:T(8,128)(2,1)S(1)}, bf16[40,1024]{1,0:T(8,128)(2,1)S(1)}, u32[]{:S(2)}, u32[]{:S(2)}) collective-permute-start(bf16[40,1024]{1,0:T(8,128)(2,1)S(1)} %get-tuple-element.53), channel_id=1, source_target_pairs={{0,36},{1,37},{2,38},{3,39},{4,40},{5,41},{6,42},{7,43},{8,44},{9,... | collective-permute-start | bytes 245768 | tf_op jit(solution)/shard_map/ppermute | solution.py:315
  17.0 9.5 %collective-permute-start.7 = (bf16[40,1024]{1,0:T(8,128)(2,1)S(1)}, bf16[40,1024]{1,0:T(8,128)(2,1)S(1)}, u32[]{:S(2)}, u32[]{:S(2)}) collective-permute-start(bf16[40,1024]{1,0:T(8,128)(2,1)S(1)} %get-tuple-element.54), channel_id=1, source_target_pairs={{0,4},{1,5},{2,6},{3,7},{4,8},{5,9},{6,10},{7,11},{8,12},{9,13},{1... | collective-permute-start | bytes 245768 | tf_op jit(solution)/shard_map/ppermute | solution.py:315
  19.5 7.2 %copy-start.2 = (bf16[1024,3,256]{2,0,1:T(8,128)(2,1)S(1)}, bf16[1024,3,256]{2,0,1:T(8,128)(2,1)}, u32[]{:S(2)}) copy-start(bf16[1024,3,256]{2,0,1:T(8,128)(2,1)} %param.10) | copy-start | bytes 4718596
  19.5 7.2 %copy-start.3 = (bf16[256,1024]{1,0:T(8,128)(2,1)S(1)}, bf16[256,1024]{1,0:T(8,128)(2,1)}, u32[]{:S(2)}) copy-start(bf16[256,1024]{1,0:T(8,128)(2,1)} %o_own.1) | copy-start | bytes 1572868
  19.5 7.2 %collective-permute-start.9 = (bf16[40,1024]{1,0:T(8,128)(2,1)S(1)}, bf16[40,1024]{1,0:T(8,128)(2,1)S(1)}, u32[]{:S(2)}, u32[]{:S(2)}) collective-permute-start(bf16[40,1024]{1,0:T(8,128)(2,1)S(1)} %get-tuple-element.57), channel_id=1, source_target_pairs={{0,32},{1,33},{2,34},{3,35},{4,36},{5,37},{6,38},{7,39},{8,40},{9,... | collective-permute-start | bytes 245768 | tf_op jit(solution)/shard_map/ppermute | solution.py:315
  31.0 4.3 %collective-permute-start.10 = (bf16[80,1024]{1,0:T(8,128)(2,1)S(1)}, bf16[80,1024]{1,0:T(8,128)(2,1)S(1)}, u32[]{:S(2)}, u32[]{:S(2)}) collective-permute-start(bf16[80,1024]{1,0:T(8,128)(2,1)S(1)} %get-tuple-element.62.mine), channel_id=1, source_target_pairs={{0,2},{1,3},{2,0},{3,1},{4,6},{5,7},{6,4},{7,5},{8,10},{9,11},{10,... | collective-permute-start | bytes 491528 | tf_op jit(solution)/shard_map/ppermute | solution.py:315
  31.3 6.2 %collective-permute-start.14 = (bf16[80,1024]{1,0:T(8,128)(2,1)S(1)}, bf16[80,1024]{1,0:T(8,128)(2,1)S(1)}, u32[]{:S(2)}, u32[]{:S(2)}) collective-permute-start(bf16[80,1024]{1,0:T(8,128)(2,1)S(1)} %get-tuple-element.69.mine), channel_id=1, source_target_pairs={{0,2},{1,3},{2,0},{3,1},{4,6},{5,7},{6,4},{7,5},{8,10},{9,11},{10,... | collective-permute-start | bytes 491528 | tf_op jit(solution)/shard_map/ppermute | solution.py:315
  37.1 5.2 %collective-permute-start.13 = (bf16[80,1024]{1,0:T(8,128)(2,1)S(1)}, bf16[80,1024]{1,0:T(8,128)(2,1)S(1)}, u32[]{:S(2)}, u32[]{:S(2)}) collective-permute-start(bf16[80,1024]{1,0:T(8,128)(2,1)S(1)} %shard_map.89.mine), channel_id=1, source_target_pairs={{0,2},{1,3},{2,0},{3,1},{4,6},{5,7},{6,4},{7,5},{8,10},{9,11},{10,... | collective-permute-start | bytes 491528 | tf_op jit(solution)/shard_map/ppermute | solution.py:315
  39.4 8.8 %collective-permute-start.15 = (bf16[80,1024]{1,0:T(8,128)(2,1)S(1)}, bf16[80,1024]{1,0:T(8,128)(2,1)S(1)}, u32[]{:S(2)}, u32[]{:S(2)}) collective-permute-start(bf16[80,1024]{1,0:T(8,128)(2,1)S(1)} %shard_map.91.mine), channel_id=1, source_target_pairs={{0,2},{1,3},{2,0},{3,1},{4,6},{5,7},{6,4},{7,5},{8,10},{9,11},{10,... | collective-permute-start | bytes 491528 | tf_op jit(solution)/shard_map/ppermute | solution.py:315
  42.3 6.8 %collective-permute-start.19 = (bf16[40,1024]{1,0:T(8,128)(2,1)S(1)}, bf16[40,1024]{1,0:T(8,128)(2,1)S(1)}, u32[]{:S(2)}, u32[]{:S(2)}) collective-permute-start(bf16[40,1024]{1,0:T(8,128)(2,1)S(1)} %get-tuple-element.73), channel_id=1, source_target_pairs={{0,254},{1,255},{2,252},{3,253},{4,224},{5,225},{6,226},{7,227},{8... | collective-permute-start | bytes 245768 | tf_op jit(solution)/shard_map/ppermute | solution.py:315
  47.5 7.3 %collective-permute-start.20 = (bf16[40,1024]{1,0:T(8,128)(2,1)S(1)}, bf16[40,1024]{1,0:T(8,128)(2,1)S(1)}, u32[]{:S(2)}, u32[]{:S(2)}) collective-permute-start(bf16[40,1024]{1,0:T(8,128)(2,1)S(1)} %get-tuple-element.74), channel_id=1, source_target_pairs={{0,30},{1,31},{2,28},{3,29},{4,0},{5,1},{6,2},{7,3},{8,4},{9,5},{1... | collective-permute-start | bytes 245768 | tf_op jit(solution)/shard_map/ppermute | solution.py:315
  48.3 8.4 %collective-permute-start.16 = (bf16[40,1024]{1,0:T(8,128)(2,1)S(1)}, bf16[40,1024]{1,0:T(8,128)(2,1)S(1)}, u32[]{:S(2)}, u32[]{:S(2)}) collective-permute-start(bf16[40,1024]{1,0:T(8,128)(2,1)S(1)} %get-tuple-element.71), channel_id=1, source_target_pairs={{0,224},{1,225},{2,226},{3,227},{4,228},{5,229},{6,230},{7,231},{8... | collective-permute-start | bytes 245768 | tf_op jit(solution)/shard_map/ppermute | solution.py:315
  49.2 8.9 %collective-permute-start.21 = (bf16[40,1024]{1,0:T(8,128)(2,1)S(1)}, bf16[40,1024]{1,0:T(8,128)(2,1)S(1)}, u32[]{:S(2)}, u32[]{:S(2)}) collective-permute-start(bf16[40,1024]{1,0:T(8,128)(2,1)S(1)} %collective-permute-done.19.m0), channel_id=1, source_target_pairs={{0,1},{1,0},{2,3},{3,2},{4,5},{5,4},{6,7},{7,6},{8,9},{9,8},{10,11... | collective-permute-start | bytes 245768 | tf_op jit(solution)/shard_map/ppermute | solution.py:315
  54.8 3.2 %collective-permute-start.22 = (bf16[40,1024]{1,0:T(8,128)(2,1)S(1)}, bf16[40,1024]{1,0:T(8,128)(2,1)S(1)}, u32[]{:S(2)}, u32[]{:S(2)}) collective-permute-start(bf16[40,1024]{1,0:T(8,128)(2,1)S(1)} %collective-permute-done.20.m1), channel_id=1, source_target_pairs={{0,1},{1,0},{2,3},{3,2},{4,5},{5,4},{6,7},{7,6},{8,9},{9,8},{10,11... | collective-permute-start | bytes 245768 | tf_op jit(solution)/shard_map/ppermute | solution.py:315
  56.7 2.4 %collective-permute-start.18 = (bf16[40,1024]{1,0:T(8,128)(2,1)S(1)}, bf16[40,1024]{1,0:T(8,128)(2,1)S(1)}, u32[]{:S(2)}, u32[]{:S(2)}) collective-permute-start(bf16[40,1024]{1,0:T(8,128)(2,1)S(1)} %get-tuple-element.72.m1), channel_id=1, source_target_pairs={{0,1},{1,0},{2,3},{3,2},{4,5},{5,4},{6,7},{7,6},{8,9},{9,8},{10,11... | collective-permute-start | bytes 245768 | tf_op jit(solution)/shard_map/ppermute | solution.py:315
  56.7 2.4 %collective-permute-start.17 = (bf16[40,1024]{1,0:T(8,128)(2,1)S(1)}, bf16[40,1024]{1,0:T(8,128)(2,1)S(1)}, u32[]{:S(2)}, u32[]{:S(2)}) collective-permute-start(bf16[40,1024]{1,0:T(8,128)(2,1)S(1)} %collective-permute-done.16.m0), channel_id=1, source_target_pairs={{0,1},{1,0},{2,3},{3,2},{4,5},{5,4},{6,7},{7,6},{8,9},{9,8},{10,11... | collective-permute-start | bytes 245768 | tf_op jit(solution)/shard_map/ppermute | solution.py:315

commit v6 on v5

--- a/solution.py
+++ b/solution.py
@@ -121,16 +121,16 @@
 
 
 def pair_heads(query, key, value, extra, key_feat):
-    low_q = iota(query.shape, 1) < HD
-    low_k = iota(key.shape, 1) < HD
-    outs = []
-    for head in range(2):
-        mine_q, mine_k = (low_q, low_k) if head == 0 else (~low_q, ~low_k)
-        scores = dot_t(jnp.where(mine_q, query, extra), jnp.where(mine_k, key, key_feat))
-        expo = jnp.exp(scores - jnp.max(scores, axis=-1, keepdims=True))
-        probs = (expo / jnp.sum(expo, axis=-1, keepdims=True)).astype(jnp.bfloat16)
-        outs.append(dot(probs, value))
-    return jnp.where(low_q, outs[0], outs[1]).astype(jnp.bfloat16)
+    count = query.shape[0]
+    low = iota(query.shape, 1) < HD
+    none = jnp.zeros_like(query)
+    upper = jnp.concatenate([jnp.where(low, query, none), jnp.where(low, none, extra)], axis=1)
+    lower = jnp.concatenate([jnp.where(low, none, query), jnp.where(low, extra, none)], axis=1)
+    scores = dot_t(jnp.concatenate([upper, lower], axis=0), jnp.concatenate([key, key_feat], axis=1))
+    expo = jnp.exp(scores - jnp.max(scores, axis=-1, keepdims=True))
+    scale = 1.0 / jnp.sum(expo, axis=-1, keepdims=True)
+    mixed = dot(expo.astype(jnp.bfloat16), value) * scale
+    return jnp.where(low, mixed[:count], mixed[count:]).astype(jnp.bfloat16)
 
 
 def first_kernel(tokens, weight, bias, keep, give, *bases):
@@ -249,44 +249,22 @@
         outs[p][...] = total[p * ROWS : (p + 1) * ROWS].astype(jnp.bfloat16)
 
 
-def place_kernel(half, m0, m1, s0, s1, *refs):
-    out, held, sems = refs[-3:]
+def join_kernel(p0, p1, out):
+    out[...] = joined((p0, p1)).astype(jnp.bfloat16)
+
+
+def place_kernel(m0, m1, s0, s1, out):
     core = core_index()
-    index = iota((1, HALF), 1)
-    slot = jnp.where(index >= ROWS, index - ROWS, index)
-    level, row, col = piece_place(slot)
-    row = jnp.where(index >= ROWS, row, row + SY)
+    quad, slot, level, row, col = kept_place(iota((1, KEPT), 1))
+    row, col = patch_place(quad, row, col)
     total = None
-    for chosen, pieces in ((core, (m0, m1)), (1 - core, (s0, s1))):
-        place = (row * SX + col) * 4 + real_level(level, chosen)
+    for chosen, parts in ((core, (m0, m1)), (1 - core, (s0, s1))):
+        place = (row * 12 + col) * 4 + real_level(level, chosen)
         place = jnp.where(slot < USED, place, -1)
-        term = dot(one_hot(iota((PATCH // 2, HALF), 0) == place), joined(pieces).astype(jnp.bfloat16))
+        source = jnp.concatenate([part[...] for part in parts], axis=0)
+        term = dot(one_hot(iota((PATCH, KEPT), 0) == place), source)
         total = term if total is None else total + term
-    held[...] = total.reshape(held.shape).astype(jnp.bfloat16)
-    copies = []
-    for y in range(WY):
-        target = out.at[pl.ds(y * WX + half * SX, SX)]
-        copies.append(pltpu.make_async_copy(held.at[pl.ds(y * SX, SX)], target, sems.at[y]))
-        copies[-1].start()
-    for copy in copies:
-        copy.wait()
-
-
-def place(half, pieces, shape, held):
-    vmem, large = pl.BlockSpec(memory_space=pltpu.VMEM), pl.BlockSpec(memory_space=pl.ANY)
-    return pl.pallas_call(
-        functools.partial(place_kernel, half),
-        out_shape=jax.ShapeDtypeStruct(shape, jnp.bfloat16),
-        in_specs=[vmem] * 4 + [large] * len(held),
-        out_specs=large,
-        scratch_shapes=[
-            pltpu.VMEM((shape[0] // 2,) + shape[1:], jnp.bfloat16),
-            pltpu.SemaphoreType.DMA((WY,)),
-        ],
-        input_output_aliases={4: 0} if held else {},
-        compiler_params=pltpu.CompilerParams(vmem_limit_bytes=12 * MIB),
-        cost_estimate=pl.CostEstimate(flops=10**10, bytes_accessed=10**6, transcendentals=0),
-    )(*pieces, *held)
+    out[...] = total.reshape(out.shape).astype(jnp.bfloat16)
 
 
 def call(kernel, outs, operands, flops, limit, table=False):
@@ -375,9 +353,15 @@
     lon = home(lon, 0, 1)
     lat, own = call(sum_kernel, piece * 2, (part_b, other_b), 10**10, 8)
     lat = home(lat, 1, 0)
-    shape = (rows * cols, levels, width)
-    result = place(1, (diag, lon, core_swap(diag), core_swap(lon)), shape, ())
-    result = place(0, (lat, own, core_swap(lat), core_swap(own)), shape, (result,))
+    mine_a = call(join_kernel, half, (diag, lon), 10**10, 8)
+    mine_b = call(join_kernel, half, (lat, own), 10**6, 8)
+    result = call(
+        place_kernel,
+        [(rows * cols, levels, width)],
+        (mine_a, mine_b, core_swap(mine_a), core_swap(mine_b)),
+        2 * 10**8,
+        12,
+    )
     return result.reshape(rows, cols, levels, width).transpose(2, 0, 1, 3)
 
 

time: 60.5 us -> 60.7 us (level)
  Pallas kernels: 14.7 us -> 11.6 us
  waiting for transfers between devices: 15.9 us -> 18.7 us
    ppermute x23 -> x21, waiting for transfers between devices: 15.9 us -> 18.7 us  [move(): return lax.ppermute(value, AXES, pairs(counts, target))]
    pallas_call x2 -> x0, Pallas kernels: 2.14 us -> none  [place(): pl.pallas_call(functools.partial(place_kernel, half), out_shape=jax.Shape...]
    pallas_call x11 -> x14, Pallas kernels: 12.6 us -> 11.6 us  [call(): pl.pallas_call(kernel, out_shape=shapes, in_specs=[pl.BlockSpec(memory_sp...]
    ppermute x23 -> x21, starting transfers between devices: 28.7 us -> 29.3 us  [move(): return lax.ppermute(value, AXES, pairs(counts, target))]
  transfers between devices with their start and end apart: 23 -> 21, of which waited for: 7 -> 10; matrix products, arithmetic and copies ran while one was open for 0% -> 0% of each run, Pallas kernels for 22% -> 16%
where the time goes in v6:
time: 60.7 us; the launch traced here: 60.5 us
  starting transfers between devices  29.3 us (48%)
  waiting for transfers between devices  18.7 us (31%)
  Pallas kernels  11.6 us (19%)
  local copies, waits for them, and re-layouts  0.72 us (1%)
    ppermute x21, starting transfers between devices, move(): return lax.ppermute(value, AXES, pairs(counts, target))  29.3 us
    ppermute x21, waiting for transfers between devices, move(): return lax.ppermute(value, AXES, pairs(counts, target))  18.7 us
    pallas_call x14, Pallas kernels, call(): pl.pallas_call(kernel, out_shape=shapes, in_specs=[pl.BlockSpec(memory_sp...  11.6 us
  transfers between devices with their start and end apart: 21, of which 10 were waited for; matrix products, arithmetic and copies ran while one was open for 0% of the time, Pallas kernels for 16%

profile of v6, /device:TPU:1, one launch (start us, length us, event | category | flops | bytes accessed | tf_op | source)
XLA Modules:
  0.0 60.5 jit_solution(14863438667076744402)
XLA Ops:
  0.0 3.2 %collective-permute-start.2 = (bf16[3,1024,256]{2,1,0:T(8,128)(2,1)}, bf16[3,1024,256]{2,1,0:T(8,128)(2,1)S(1)}, u32[]{:S(2)}, u32[]{:S(2)}) collective-permute-start(bf16[3,1024,256]{2,1,0:T(8,128)(2,1)} %bitcast.8), channel_id=1, source_target_pairs={{0,1},{1,0},{2,3},{3,2},{4,5},{5,4},{6,7},{7,6},{8,9},{9,8},{10,11... | collective-permute-start | bytes 4718600 | tf_op jit(solution)/shard_map/ppermute | solution.py:293
  3.2 0.5 collective-permute-start.1
  3.8 0.7 %copy-done.7 = f32[2,4,37]{2,1,0:T(4,128)S(1)} copy-done((f32[2,4,37]{2,1,0:T(4,128)S(1)}, f32[2,4,37]{2,1,0:T(4,128)}, u32[]{:S(2)}) %copy-start.7) | copy-done | bytes 1208
  4.4 0.8 %shard_map.82 = (bf16[32,256]{1,0:T(8,128)(2,1)S(1)}, bf16[32,256]{1,0:T(8,128)(2,1)S(1)}) custom-call(f32[2,4,37]{2,1,0:T(4,128)S(1)} %copy-done.7), custom_call_target="tpu_custom_call" | custom-call | flops 5000000000 | bytes 33952 | tf_op jit(solution)/shard_map/pallas_call | solution.py:273
  5.5 2.4 %shard_map.83 = (bf16[160,256]{1,0:T(8,128)(2,1)S(1)}, bf16[160,256]{1,0:T(8,128)(2,1)S(1)}, bf16[80,1024]{1,0:T(8,128)(2,1)S(1)}, bf16[80,1024]{1,0:T(8,128)(2,1)S(1)}) custom-call(bf16[72,4,1024]{2,1,0:T(4,128)(2,1)S(1)} %bitcast.11, bf16[3,1024,256]{2,1,0:T(8,128)(2,1)S(1)} %bitcast.10, bf16[32,256]{1,0:T(8,128)(2,1)S(1)} %get-tuple-element.40.bias), custom_call_target="tpu_custom_call" | custom-call | flops 1000000000 | bytes 2670592 | tf_op jit(solution)/shard_map/pallas_call | solution.py:273
  8.0 0.4 collective-permute-start.4
  8.4 0.9 %collective-permute-done.4.o1 = bf16[160,256]{1,0:T(8,128)(2,1)S(1)} collective-permute-done((bf16[160,256]{1,0:T(8,128)(2,1)S(1)}, bf16[160,256]{1,0:T(8,128)(2,1)S(1)}, u32[]{:S(2)}, u32[]{:S(2)}) %collective-permute-start.4) | collective-permute-done | bytes 81952 | tf_op jit(solution)/shard_map/ppermute | solution.py:293
  9.3 0.3 shard_map.84
  9.8 1.5 %collective-permute-start.8 = (bf16[80,1024]{1,0:T(8,128)(2,1)S(1)}, bf16[80,1024]{1,0:T(8,128)(2,1)S(1)}, u32[]{:S(2)}, u32[]{:S(2)}) collective-permute-start(bf16[80,1024]{1,0:T(8,128)(2,1)S(1)} %get-tuple-element.55.mine), channel_id=1, source_target_pairs={{0,2},{1,3},{2,0},{3,1},{4,6},{5,7},{6,4},{7,5},{8,10},{9,11},{10,... | collective-permute-start | bytes 491528 | tf_op jit(solution)/shard_map/ppermute | solution.py:293
  11.2 0.9 %collective-permute-start.11 = (bf16[1024,1024]{1,0:T(8,128)(2,1)S(1)}, bf16[1024,1024]{1,0:T(8,128)(2,1)S(1)}, u32[]{:S(2)}, u32[]{:S(2)}) collective-permute-start(bf16[1024,1024]{1,0:T(8,128)(2,1)S(1)} %copy-done), channel_id=1, source_target_pairs={{0,1},{1,0},{2,3},{3,2},{4,5},{5,4},{6,7},{7,6},{8,9},{9,8},{10,11... | collective-permute-start | bytes 6291464 | tf_op jit(solution)/shard_map/ppermute | solution.py:293
  12.2 2.9 %collective-permute-done.5.other = bf16[80,1024]{1,0:T(8,128)(2,1)S(1)} collective-permute-done((bf16[80,1024]{1,0:T(8,128)(2,1)S(1)}, bf16[80,1024]{1,0:T(8,128)(2,1)S(1)}, u32[]{:S(2)}, u32[]{:S(2)}) %collective-permute-start.5) | collective-permute-done | bytes 163872 | tf_op jit(solution)/shard_map/ppermute | solution.py:293
  15.3 1.0 %collective-permute-start.6 = (bf16[40,1024]{1,0:T(8,128)(2,1)S(1)}, bf16[40,1024]{1,0:T(8,128)(2,1)S(1)}, u32[]{:S(2)}, u32[]{:S(2)}) collective-permute-start(bf16[40,1024]{1,0:T(8,128)(2,1)S(1)} %get-tuple-element.53), channel_id=1, source_target_pairs={{0,36},{1,37},{2,38},{3,39},{4,40},{5,41},{6,42},{7,43},{8,44},{9,... | collective-permute-start | bytes 245768 | tf_op jit(solution)/shard_map/ppermute | solution.py:293
  16.3 1.3 %collective-permute-start.7 = (bf16[40,1024]{1,0:T(8,128)(2,1)S(1)}, bf16[40,1024]{1,0:T(8,128)(2,1)S(1)}, u32[]{:S(2)}, u32[]{:S(2)}) collective-permute-start(bf16[40,1024]{1,0:T(8,128)(2,1)S(1)} %get-tuple-element.54), channel_id=1, source_target_pairs={{0,4},{1,5},{2,6},{3,7},{4,8},{5,9},{6,10},{7,11},{8,12},{9,13},{1... | collective-permute-start | bytes 245768 | tf_op jit(solution)/shard_map/ppermute | solution.py:293
  17.6 1.1 %collective-permute-done.8.other = bf16[80,1024]{1,0:T(8,128)(2,1)S(1)} collective-permute-done((bf16[80,1024]{1,0:T(8,128)(2,1)S(1)}, bf16[80,1024]{1,0:T(8,128)(2,1)S(1)}, u32[]{:S(2)}, u32[]{:S(2)}) %collective-permute-start.8) | collective-permute-done | bytes 163872 | tf_op jit(solution)/shard_map/ppermute | solution.py:293
  18.8 0.8 %collective-permute-start.9 = (bf16[40,1024]{1,0:T(8,128)(2,1)S(1)}, bf16[40,1024]{1,0:T(8,128)(2,1)S(1)}, u32[]{:S(2)}, u32[]{:S(2)}) collective-permute-start(bf16[40,1024]{1,0:T(8,128)(2,1)S(1)} %get-tuple-element.57), channel_id=1, source_target_pairs={{0,32},{1,33},{2,34},{3,35},{4,36},{5,37},{6,38},{7,39},{8,40},{9,... | collective-permute-start | bytes 245768 | tf_op jit(solution)/shard_map/ppermute | solution.py:293
  19.6 6.2 %collective-permute-done.6.p0 = bf16[40,1024]{1,0:T(8,128)(2,1)S(1)} collective-permute-done((bf16[40,1024]{1,0:T(8,128)(2,1)S(1)}, bf16[40,1024]{1,0:T(8,128)(2,1)S(1)}, u32[]{:S(2)}, u32[]{:S(2)}) %collective-permute-start.6) | collective-permute-done | bytes 81952 | tf_op jit(solution)/shard_map/ppermute | solution.py:293
  26.0 2.7 %shard_map.88 = (bf16[80,1024]{1,0:T(8,128)(2,1)S(1)}, bf16[80,1024]{1,0:T(8,128)(2,1)S(1)}) custom-call(bf16[80,1024]{1,0:T(8,128)(2,1)S(1)} %shard_map.86.xn_a, bf16[40,1024]{1,0:T(8,128)(2,1)S(1)} %collective-permute-done.9.p2.p0, bf16[40,1024]{1,0:T(8,128)(2,1)S(1)} %get-tuple-element.58.p3.p1, bf16[3,1024,256]{2,1,0:T(8,128)(2,1)S(1)} %bitcast.9, ...), custom_call_target="tpu_custom_call" | custom-call | flops 1000000000 | bytes 4882432 | tf_op jit(solution)/shard_map/pallas_call | solution.py:273
  28.7 0.3 collective-permute-start.10
  29.0 1.3 %collective-permute-start.14 = (bf16[80,1024]{1,0:T(8,128)(2,1)S(1)}, bf16[80,1024]{1,0:T(8,128)(2,1)S(1)}, u32[]{:S(2)}, u32[]{:S(2)}) collective-permute-start(bf16[80,1024]{1,0:T(8,128)(2,1)S(1)} %get-tuple-element.69.mine), channel_id=1, source_target_pairs={{0,2},{1,3},{2,0},{3,1},{4,6},{5,7},{6,4},{7,5},{8,10},{9,11},{10,... | collective-permute-start | bytes 491528 | tf_op jit(solution)/shard_map/ppermute | solution.py:293
  30.3 2.7 %collective-permute-done.10.other = bf16[80,1024]{1,0:T(8,128)(2,1)S(1)} collective-permute-done((bf16[80,1024]{1,0:T(8,128)(2,1)S(1)}, bf16[80,1024]{1,0:T(8,128)(2,1)S(1)}, u32[]{:S(2)}, u32[]{:S(2)}) %collective-permute-start.10) | collective-permute-done | bytes 163872 | tf_op jit(solution)/shard_map/ppermute | solution.py:293
  33.0 1.8 %shard_map.89.mine = bf16[80,1024]{1,0:T(8,128)(2,1)S(1)} custom-call(bf16[80,1024]{1,0:T(8,128)(2,1)S(1)} %get-tuple-element.62.mine, bf16[80,1024]{1,0:T(8,128)(2,1)S(1)} %collective-permute-done.10.other, bf16[40,1024]{1,0:T(8,128)(2,1)S(1)} %collective-permute-done.6.p0, bf16[40,1024]{1,0:T(8,128)(2,1)S(1)} %collective-permute-done.7.p1, ...), custom_call_target="tpu_custom_call" | custom-call | flops 1000000000 | bytes 9043968 | tf_op jit(solution)/shard_map/pallas_call | solution.py:273
  35.3 1.8 %shard_map.91.mine = bf16[80,1024]{1,0:T(8,128)(2,1)S(1)} custom-call(bf16[80,1024]{1,0:T(8,128)(2,1)S(1)} %get-tuple-element.69.mine, bf16[80,1024]{1,0:T(8,128)(2,1)S(1)} %collective-permute-done.14.other, bf16[40,1024]{1,0:T(8,128)(2,1)S(1)} %collective-permute-done.9.p2.p0, bf16[40,1024]{1,0:T(8,128)(2,1)S(1)} %get-tuple-element.58.p3.p1, ...), custom_call_target="tpu_custom_call" | custom-call | flops 1000000000 | bytes 9043968 | tf_op jit(solution)/shard_map/pallas_call | solution.py:273
  37.1 1.2 %collective-permute-start.17 = (bf16[80,1024]{1,0:T(8,128)(2,1)S(1)}, bf16[80,1024]{1,0:T(8,128)(2,1)S(1)}, u32[]{:S(2)}, u32[]{:S(2)}) collective-permute-start(bf16[80,1024]{1,0:T(8,128)(2,1)S(1)} %shard_map.91.mine), channel_id=1, source_target_pairs={{0,2},{1,3},{2,0},{3,1},{4,6},{5,7},{6,4},{7,5},{8,10},{9,11},{10,... | collective-permute-start | bytes 491528 | tf_op jit(solution)/shard_map/ppermute | solution.py:293
  38.3 1.7 %collective-permute-done.13.other = bf16[80,1024]{1,0:T(8,128)(2,1)S(1)} collective-permute-done((bf16[80,1024]{1,0:T(8,128)(2,1)S(1)}, bf16[80,1024]{1,0:T(8,128)(2,1)S(1)}, u32[]{:S(2)}, u32[]{:S(2)}) %collective-permute-start.13) | collective-permute-done | bytes 163872 | tf_op jit(solution)/shard_map/ppermute | solution.py:293
  40.1 1.7 %collective-permute-done.17.other = bf16[80,1024]{1,0:T(8,128)(2,1)S(1)} collective-permute-done((bf16[80,1024]{1,0:T(8,128)(2,1)S(1)}, bf16[80,1024]{1,0:T(8,128)(2,1)S(1)}, u32[]{:S(2)}, u32[]{:S(2)}) %collective-permute-start.17) | collective-permute-done | bytes 163872 | tf_op jit(solution)/shard_map/ppermute | solution.py:293
  41.8 1.9 %collective-permute-start.18 = (bf16[40,1024]{1,0:T(8,128)(2,1)S(1)}, bf16[40,1024]{1,0:T(8,128)(2,1)S(1)}, u32[]{:S(2)}, u32[]{:S(2)}) collective-permute-start(bf16[40,1024]{1,0:T(8,128)(2,1)S(1)} %get-tuple-element.73), channel_id=1, source_target_pairs={{0,224},{1,225},{2,226},{3,227},{4,228},{5,229},{6,230},{7,231},{8... | collective-permute-start | bytes 245768 | tf_op jit(solution)/shard_map/ppermute | solution.py:293
  43.8 4.6 %collective-permute-start.15 = (bf16[40,1024]{1,0:T(8,128)(2,1)S(1)}, bf16[40,1024]{1,0:T(8,128)(2,1)S(1)}, u32[]{:S(2)}, u32[]{:S(2)}) collective-permute-start(bf16[40,1024]{1,0:T(8,128)(2,1)S(1)} %get-tuple-element.70), channel_id=1, source_target_pairs={{0,254},{1,255},{2,252},{3,253},{4,224},{5,225},{6,226},{7,227},{8... | collective-permute-start | bytes 245768 | tf_op jit(solution)/shard_map/ppermute | solution.py:293
  48.4 1.4 %collective-permute-start.16 = (bf16[40,1024]{1,0:T(8,128)(2,1)S(1)}, bf16[40,1024]{1,0:T(8,128)(2,1)S(1)}, u32[]{:S(2)}, u32[]{:S(2)}) collective-permute-start(bf16[40,1024]{1,0:T(8,128)(2,1)S(1)} %get-tuple-element.71), channel_id=1, source_target_pairs={{0,30},{1,31},{2,28},{3,29},{4,0},{5,1},{6,2},{7,3},{8,4},{9,5},{1... | collective-permute-start | bytes 245768 | tf_op jit(solution)/shard_map/ppermute | solution.py:293
  49.8 5.1 %collective-permute-start.20 = (bf16[80,1024]{1,0:T(8,128)(2,1)S(1)}, bf16[80,1024]{1,0:T(8,128)(2,1)S(1)}, u32[]{:S(2)}, u32[]{:S(2)}) collective-permute-start(bf16[80,1024]{1,0:T(8,128)(2,1)S(1)} %shard_map.94.m1), channel_id=1, source_target_pairs={{0,1},{1,0},{2,3},{3,2},{4,5},{5,4},{6,7},{7,6},{8,9},{9,8},{10,11... | collective-permute-start | bytes 491528 | tf_op jit(solution)/shard_map/ppermute | solution.py:293
  54.8 3.4 %collective-permute-start.19 = (bf16[80,1024]{1,0:T(8,128)(2,1)S(1)}, bf16[80,1024]{1,0:T(8,128)(2,1)S(1)}, u32[]{:S(2)}, u32[]{:S(2)}) collective-permute-start(bf16[80,1024]{1,0:T(8,128)(2,1)S(1)} %shard_map.92.m0), channel_id=1, source_target_pairs={{0,1},{1,0},{2,3},{3,2},{4,5},{5,4},{6,7},{7,6},{8,9},{9,8},{10,11... | collective-permute-start | bytes 491528 | tf_op jit(solution)/shard_map/ppermute | solution.py:293
  58.2 1.0 %collective-permute-done.19.s0 = bf16[80,1024]{1,0:T(8,128)(2,1)S(1)} collective-permute-done((bf16[80,1024]{1,0:T(8,128)(2,1)S(1)}, bf16[80,1024]{1,0:T(8,128)(2,1)S(1)}, u32[]{:S(2)}, u32[]{:S(2)}) %collective-permute-start.19) | collective-permute-done | bytes 163872 | tf_op jit(solution)/shard_map/ppermute | solution.py:293
  59.2 1.3 %shard_map.95 = bf16[72,4,1024]{2,1,0:T(4,128)(2,1)} custom-call(bf16[80,1024]{1,0:T(8,128)(2,1)S(1)} %shard_map.92.m0, bf16[80,1024]{1,0:T(8,128)(2,1)S(1)} %shard_map.94.m1, bf16[80,1024]{1,0:T(8,128)(2,1)S(1)} %collective-permute-done.19.s0, bf16[80,1024]{1,0:T(8,128)(2,1)S(1)} %collective-permute-done.20.s1), custom_call_target="tpu_custom_call" | custom-call | flops 200000000 | bytes 1245184 | tf_op jit(solution)/shard_map/pallas_call | solution.py:273
  (40 shorter events, 1.5 us)
Async XLA Ops:
  0.0 5.5 %copy-start.5 = (bf16[1024,3,256]{2,0,1:T(8,128)(2,1)S(1)}, bf16[1024,3,256]{2,0,1:T(8,128)(2,1)}, u32[]{:S(2)}) copy-start(bf16[1024,3,256]{2,0,1:T(8,128)(2,1)} %param.9) | copy-start | bytes 4718596
  0.0 5.5 %copy-start.6 = (bf16[4,6,12,1024]{3,0,2,1:T(4,128)(2,1)S(1)}, bf16[4,6,12,1024]{3,0,2,1:T(4,128)(2,1)}, u32[]{:S(2)}) copy-start(bf16[4,6,12,1024]{3,0,2,1:T(4,128)(2,1)} %param.8) | copy-start | bytes 1769476
  0.0 8.0 %collective-permute-start.2 = (bf16[3,1024,256]{2,1,0:T(8,128)(2,1)}, bf16[3,1024,256]{2,1,0:T(8,128)(2,1)S(1)}, u32[]{:S(2)}, u32[]{:S(2)}) collective-permute-start(bf16[3,1024,256]{2,1,0:T(8,128)(2,1)} %bitcast.8), channel_id=1, source_target_pairs={{0,1},{1,0},{2,3},{3,2},{4,5},{5,4},{6,7},{7,6},{8,9},{9,8},{10,11... | collective-permute-start | bytes 4718600 | tf_op jit(solution)/shard_map/ppermute | solution.py:293
  3.2 4.7 %collective-permute-start = (bf16[256,1024]{1,0:T(8,128)(2,1)}, bf16[256,1024]{1,0:T(8,128)(2,1)S(1)}, u32[]{:S(2)}, u32[]{:S(2)}) collective-permute-start(bf16[256,1024]{1,0:T(8,128)(2,1)} %w0.1), channel_id=1, source_target_pairs={{0,1},{1,0},{2,3},{3,2},{4,5},{5,4},{6,7},{7,6},{8,9},{9,8},{10,11... | collective-permute-start | bytes 1572872 | tf_op jit(solution)/shard_map/ppermute | solution.py:293
  3.2 4.8 %collective-permute-start.1 = (bf16[256,1024]{1,0:T(8,128)(2,1)}, bf16[256,1024]{1,0:T(8,128)(2,1)S(1)}, u32[]{:S(2)}, u32[]{:S(2)}) collective-permute-start(bf16[256,1024]{1,0:T(8,128)(2,1)} %o_own.1), channel_id=1, source_target_pairs={{0,1},{1,0},{2,3},{3,2},{4,5},{5,4},{6,7},{7,6},{8,9},{9,8},{10,11... | collective-permute-start | bytes 1572872 | tf_op jit(solution)/shard_map/ppermute | solution.py:293
  3.8 0.7 %copy-start.7 = (f32[2,4,37]{2,1,0:T(4,128)S(1)}, f32[2,4,37]{2,1,0:T(4,128)}, u32[]{:S(2)}) copy-start(f32[2,4,37]{2,1,0:T(4,128)} %table.1) | copy-start | bytes 3556
  5.3 4.1 %copy-start.4 = (bf16[256,1024]{1,0:T(8,128)(2,1)S(1)}, bf16[256,1024]{1,0:T(8,128)(2,1)}, u32[]{:S(2)}) copy-start(bf16[256,1024]{1,0:T(8,128)(2,1)} %w0.1) | copy-start | bytes 1572868
  5.3 2.6 %collective-permute-start.3 = (bf16[32,256]{1,0:T(8,128)(2,1)S(1)}, bf16[32,256]{1,0:T(8,128)(2,1)S(1)}, u32[]{:S(2)}, u32[]{:S(2)}) collective-permute-start(bf16[32,256]{1,0:T(8,128)(2,1)S(1)} %get-tuple-element.43.b_own), channel_id=1, source_target_pairs={{0,1},{1,0},{2,3},{3,2},{4,5},{5,4},{6,7},{7,6},{8,9},{9,8},{10,11... | collective-permute-start | bytes 49160 | tf_op jit(solution)/shard_map/ppermute | solution.py:293
  5.5 5.7 %copy-start = (bf16[1024,1024]{1,0:T(8,128)(2,1)S(1)}, bf16[1024,1024]{1,0:T(8,128)(2,1)}, u32[]{:S(2)}) copy-start(bf16[1024,1024]{1,0:T(8,128)(2,1)} %u0.3) | copy-start | bytes 6291460
  5.5 6.7 %copy-start.1 = (bf16[1024,1024]{1,0:T(8,128)(2,1)S(1)}, bf16[1024,1024]{1,0:T(8,128)(2,1)}, u32[]{:S(2)}) copy-start(bf16[1024,1024]{1,0:T(8,128)(2,1)} %d0.3) | copy-start | bytes 6291460
  8.0 1.3 %collective-permute-start.4 = (bf16[160,256]{1,0:T(8,128)(2,1)S(1)}, bf16[160,256]{1,0:T(8,128)(2,1)S(1)}, u32[]{:S(2)}, u32[]{:S(2)}) collective-permute-start(bf16[160,256]{1,0:T(8,128)(2,1)S(1)} %get-tuple-element.45), channel_id=1, source_target_pairs={{0,1},{1,0},{2,3},{3,2},{4,5},{5,4},{6,7},{7,6},{8,9},{9,8},{10,11... | collective-permute-start | bytes 245768 | tf_op jit(solution)/shard_map/ppermute | solution.py:293
  9.7 5.5 %collective-permute-start.5 = (bf16[80,1024]{1,0:T(8,128)(2,1)S(1)}, bf16[80,1024]{1,0:T(8,128)(2,1)S(1)}, u32[]{:S(2)}, u32[]{:S(2)}) collective-permute-start(bf16[80,1024]{1,0:T(8,128)(2,1)S(1)} %get-tuple-element.48.mine), channel_id=1, source_target_pairs={{0,2},{1,3},{2,0},{3,1},{4,6},{5,7},{6,4},{7,5},{8,10},{9,11},{10,... | collective-permute-start | bytes 491528 | tf_op jit(solution)/shard_map/ppermute | solution.py:293
  9.8 8.9 %collective-permute-start.8 = (bf16[80,1024]{1,0:T(8,128)(2,1)S(1)}, bf16[80,1024]{1,0:T(8,128)(2,1)S(1)}, u32[]{:S(2)}, u32[]{:S(2)}) collective-permute-start(bf16[80,1024]{1,0:T(8,128)(2,1)S(1)} %get-tuple-element.55.mine), channel_id=1, source_target_pairs={{0,2},{1,3},{2,0},{3,1},{4,6},{5,7},{6,4},{7,5},{8,10},{9,11},{10,... | collective-permute-start | bytes 491528 | tf_op jit(solution)/shard_map/ppermute | solution.py:293
  11.2 21.8 %collective-permute-start.11 = (bf16[1024,1024]{1,0:T(8,128)(2,1)S(1)}, bf16[1024,1024]{1,0:T(8,128)(2,1)S(1)}, u32[]{:S(2)}, u32[]{:S(2)}) collective-permute-start(bf16[1024,1024]{1,0:T(8,128)(2,1)S(1)} %copy-done), channel_id=1, source_target_pairs={{0,1},{1,0},{2,3},{3,2},{4,5},{5,4},{6,7},{7,6},{8,9},{9,8},{10,11... | collective-permute-start | bytes 6291464 | tf_op jit(solution)/shard_map/ppermute | solution.py:293
  12.1 20.9 %collective-permute-start.12 = (bf16[1024,1024]{1,0:T(8,128)(2,1)S(1)}, bf16[1024,1024]{1,0:T(8,128)(2,1)S(1)}, u32[]{:S(2)}, u32[]{:S(2)}) collective-permute-start(bf16[1024,1024]{1,0:T(8,128)(2,1)S(1)} %copy-done.1), channel_id=1, source_target_pairs={{0,1},{1,0},{2,3},{3,2},{4,5},{5,4},{6,7},{7,6},{8,9},{9,8},{10,11... | collective-permute-start | bytes 6291464 | tf_op jit(solution)/shard_map/ppermute | solution.py:293
  15.3 10.5 %collective-permute-start.6 = (bf16[40,1024]{1,0:T(8,128)(2,1)S(1)}, bf16[40,1024]{1,0:T(8,128)(2,1)S(1)}, u32[]{:S(2)}, u32[]{:S(2)}) collective-permute-start(bf16[40,1024]{1,0:T(8,128)(2,1)S(1)} %get-tuple-element.53), channel_id=1, source_target_pairs={{0,36},{1,37},{2,38},{3,39},{4,40},{5,41},{6,42},{7,43},{8,44},{9,... | collective-permute-start | bytes 245768 | tf_op jit(solution)/shard_map/ppermute | solution.py:293
  16.3 9.5 %collective-permute-start.7 = (bf16[40,1024]{1,0:T(8,128)(2,1)S(1)}, bf16[40,1024]{1,0:T(8,128)(2,1)S(1)}, u32[]{:S(2)}, u32[]{:S(2)}) collective-permute-start(bf16[40,1024]{1,0:T(8,128)(2,1)S(1)} %get-tuple-element.54), channel_id=1, source_target_pairs={{0,4},{1,5},{2,6},{3,7},{4,8},{5,9},{6,10},{7,11},{8,12},{9,13},{1... | collective-permute-start | bytes 245768 | tf_op jit(solution)/shard_map/ppermute | solution.py:293
  18.8 7.2 %copy-start.2 = (bf16[1024,3,256]{2,0,1:T(8,128)(2,1)S(1)}, bf16[1024,3,256]{2,0,1:T(8,128)(2,1)}, u32[]{:S(2)}) copy-start(bf16[1024,3,256]{2,0,1:T(8,128)(2,1)} %param.10) | copy-start | bytes 4718596
  18.8 7.2 %copy-start.3 = (bf16[256,1024]{1,0:T(8,128)(2,1)S(1)}, bf16[256,1024]{1,0:T(8,128)(2,1)}, u32[]{:S(2)}) copy-start(bf16[256,1024]{1,0:T(8,128)(2,1)} %o_own.1) | copy-start | bytes 1572868
  18.8 7.2 %collective-permute-start.9 = (bf16[40,1024]{1,0:T(8,128)(2,1)S(1)}, bf16[40,1024]{1,0:T(8,128)(2,1)S(1)}, u32[]{:S(2)}, u32[]{:S(2)}) collective-permute-start(bf16[40,1024]{1,0:T(8,128)(2,1)S(1)} %get-tuple-element.57), channel_id=1, source_target_pairs={{0,32},{1,33},{2,34},{3,35},{4,36},{5,37},{6,38},{7,39},{8,40},{9,... | collective-permute-start | bytes 245768 | tf_op jit(solution)/shard_map/ppermute | solution.py:293
  28.7 4.3 %collective-permute-start.10 = (bf16[80,1024]{1,0:T(8,128)(2,1)S(1)}, bf16[80,1024]{1,0:T(8,128)(2,1)S(1)}, u32[]{:S(2)}, u32[]{:S(2)}) collective-permute-start(bf16[80,1024]{1,0:T(8,128)(2,1)S(1)} %get-tuple-element.62.mine), channel_id=1, source_target_pairs={{0,2},{1,3},{2,0},{3,1},{4,6},{5,7},{6,4},{7,5},{8,10},{9,11},{10,... | collective-permute-start | bytes 491528 | tf_op jit(solution)/shard_map/ppermute | solution.py:293
  29.0 6.2 %collective-permute-start.14 = (bf16[80,1024]{1,0:T(8,128)(2,1)S(1)}, bf16[80,1024]{1,0:T(8,128)(2,1)S(1)}, u32[]{:S(2)}, u32[]{:S(2)}) collective-permute-start(bf16[80,1024]{1,0:T(8,128)(2,1)S(1)} %get-tuple-element.69.mine), channel_id=1, source_target_pairs={{0,2},{1,3},{2,0},{3,1},{4,6},{5,7},{6,4},{7,5},{8,10},{9,11},{10,... | collective-permute-start | bytes 491528 | tf_op jit(solution)/shard_map/ppermute | solution.py:293
  34.8 5.2 %collective-permute-start.13 = (bf16[80,1024]{1,0:T(8,128)(2,1)S(1)}, bf16[80,1024]{1,0:T(8,128)(2,1)S(1)}, u32[]{:S(2)}, u32[]{:S(2)}) collective-permute-start(bf16[80,1024]{1,0:T(8,128)(2,1)S(1)} %shard_map.89.mine), channel_id=1, source_target_pairs={{0,2},{1,3},{2,0},{3,1},{4,6},{5,7},{6,4},{7,5},{8,10},{9,11},{10,... | collective-permute-start | bytes 491528 | tf_op jit(solution)/shard_map/ppermute | solution.py:293
  37.1 4.7 %collective-permute-start.17 = (bf16[80,1024]{1,0:T(8,128)(2,1)S(1)}, bf16[80,1024]{1,0:T(8,128)(2,1)S(1)}, u32[]{:S(2)}, u32[]{:S(2)}) collective-permute-start(bf16[80,1024]{1,0:T(8,128)(2,1)S(1)} %shard_map.91.mine), channel_id=1, source_target_pairs={{0,2},{1,3},{2,0},{3,1},{4,6},{5,7},{6,4},{7,5},{8,10},{9,11},{10,... | collective-permute-start | bytes 491528 | tf_op jit(solution)/shard_map/ppermute | solution.py:293
  41.8 7.9 %collective-permute-start.18 = (bf16[40,1024]{1,0:T(8,128)(2,1)S(1)}, bf16[40,1024]{1,0:T(8,128)(2,1)S(1)}, u32[]{:S(2)}, u32[]{:S(2)}) collective-permute-start(bf16[40,1024]{1,0:T(8,128)(2,1)S(1)} %get-tuple-element.73), channel_id=1, source_target_pairs={{0,224},{1,225},{2,226},{3,227},{4,228},{5,229},{6,230},{7,231},{8... | collective-permute-start | bytes 245768 | tf_op jit(solution)/shard_map/ppermute | solution.py:293
  43.8 11.1 %collective-permute-start.15 = (bf16[40,1024]{1,0:T(8,128)(2,1)S(1)}, bf16[40,1024]{1,0:T(8,128)(2,1)S(1)}, u32[]{:S(2)}, u32[]{:S(2)}) collective-permute-start(bf16[40,1024]{1,0:T(8,128)(2,1)S(1)} %get-tuple-element.70), channel_id=1, source_target_pairs={{0,254},{1,255},{2,252},{3,253},{4,224},{5,225},{6,226},{7,227},{8... | collective-permute-start | bytes 245768 | tf_op jit(solution)/shard_map/ppermute | solution.py:293
  48.4 6.5 %collective-permute-start.16 = (bf16[40,1024]{1,0:T(8,128)(2,1)S(1)}, bf16[40,1024]{1,0:T(8,128)(2,1)S(1)}, u32[]{:S(2)}, u32[]{:S(2)}) collective-permute-start(bf16[40,1024]{1,0:T(8,128)(2,1)S(1)} %get-tuple-element.71), channel_id=1, source_target_pairs={{0,30},{1,31},{2,28},{3,29},{4,0},{5,1},{6,2},{7,3},{8,4},{9,5},{1... | collective-permute-start | bytes 245768 | tf_op jit(solution)/shard_map/ppermute | solution.py:293
  49.8 8.5 %collective-permute-start.20 = (bf16[80,1024]{1,0:T(8,128)(2,1)S(1)}, bf16[80,1024]{1,0:T(8,128)(2,1)S(1)}, u32[]{:S(2)}, u32[]{:S(2)}) collective-permute-start(bf16[80,1024]{1,0:T(8,128)(2,1)S(1)} %shard_map.94.m1), channel_id=1, source_target_pairs={{0,1},{1,0},{2,3},{3,2},{4,5},{5,4},{6,7},{7,6},{8,9},{9,8},{10,11... | collective-permute-start | bytes 491528 | tf_op jit(solution)/shard_map/ppermute | solution.py:293
  54.8 4.4 %collective-permute-start.19 = (bf16[80,1024]{1,0:T(8,128)(2,1)S(1)}, bf16[80,1024]{1,0:T(8,128)(2,1)S(1)}, u32[]{:S(2)}, u32[]{:S(2)}) collective-permute-start(bf16[80,1024]{1,0:T(8,128)(2,1)S(1)} %shard_map.92.m0), channel_id=1, source_target_pairs={{0,1},{1,0},{2,3},{3,2},{4,5},{5,4},{6,7},{7,6},{8,9},{9,8},{10,11... | collective-permute-start | bytes 491528 | tf_op jit(solution)/shard_map/ppermute | solution.py:293

commit v7 on v6

--- a/solution.py
+++ b/solution.py
@@ -354,6 +354,7 @@
     lat, own = call(sum_kernel, piece * 2, (part_b, other_b), 10**10, 8)
     lat = home(lat, 1, 0)
     mine_a = call(join_kernel, half, (diag, lon), 10**10, 8)
+    mine_a, lat, own = tied(mine_a, lat, own)
     mine_b = call(join_kernel, half, (lat, own), 10**6, 8)
     result = call(
         place_kernel,

time: 60.7 us -> 58.7 us (0.967)
  starting transfers between devices: 29.3 us -> 26 us
  waiting for transfers between devices: 18.7 us -> 20 us
    ppermute x21, starting transfers between devices: 29.3 us -> 26 us  [move(): return lax.ppermute(value, AXES, pairs(counts, target))]
    ppermute x21, waiting for transfers between devices: 18.7 us -> 20 us  [move(): return lax.ppermute(value, AXES, pairs(counts, target))]
  transfers between devices with their start and end apart: 21 -> 21, of which waited for: 10 -> 11; matrix products, arithmetic and copies ran while one was open for 0% -> 0% of each run, Pallas kernels for 16% -> 17%
where the time goes in v7:
time: 58.7 us; the launch traced here: 58.6 us
  starting transfers between devices  26 us (44%)
  waiting for transfers between devices  20 us (34%)
  Pallas kernels  11.6 us (20%)
  local copies, waits for them, and re-layouts  0.72 us (1%)
    ppermute x21, starting transfers between devices, move(): return lax.ppermute(value, AXES, pairs(counts, target))  26 us
    ppermute x21, waiting for transfers between devices, move(): return lax.ppermute(value, AXES, pairs(counts, target))  20 us
    pallas_call x14, Pallas kernels, call(): pl.pallas_call(kernel, out_shape=shapes, in_specs=[pl.BlockSpec(memory_sp...  11.6 us
  transfers between devices with their start and end apart: 21, of which 11 were waited for; matrix products, arithmetic and copies ran while one was open for 0% of the time, Pallas kernels for 17%

profile of v7, /device:TPU:1, one launch (start us, length us, event | category | flops | bytes accessed | tf_op | source)
XLA Modules:
  0.0 58.6 jit_solution(5811714042944521190)
XLA Ops:
  0.0 3.2 %collective-permute-start.2 = (bf16[3,1024,256]{2,1,0:T(8,128)(2,1)}, bf16[3,1024,256]{2,1,0:T(8,128)(2,1)S(1)}, u32[]{:S(2)}, u32[]{:S(2)}) collective-permute-start(bf16[3,1024,256]{2,1,0:T(8,128)(2,1)} %bitcast.8), channel_id=1, source_target_pairs={{0,1},{1,0},{2,3},{3,2},{4,5},{5,4},{6,7},{7,6},{8,9},{9,8},{10,11... | collective-permute-start | bytes 4718600 | tf_op jit(solution)/shard_map/ppermute | solution.py:293
  3.2 0.5 collective-permute-start.1
  3.8 0.7 %copy-done.7 = f32[2,4,37]{2,1,0:T(4,128)S(1)} copy-done((f32[2,4,37]{2,1,0:T(4,128)S(1)}, f32[2,4,37]{2,1,0:T(4,128)}, u32[]{:S(2)}) %copy-start.7) | copy-done | bytes 1208
  4.4 0.8 %shard_map.82 = (bf16[32,256]{1,0:T(8,128)(2,1)S(1)}, bf16[32,256]{1,0:T(8,128)(2,1)S(1)}) custom-call(f32[2,4,37]{2,1,0:T(4,128)S(1)} %copy-done.7), custom_call_target="tpu_custom_call" | custom-call | flops 5000000000 | bytes 33952 | tf_op jit(solution)/shard_map/pallas_call | solution.py:273
  5.5 2.4 %shard_map.83 = (bf16[160,256]{1,0:T(8,128)(2,1)S(1)}, bf16[160,256]{1,0:T(8,128)(2,1)S(1)}, bf16[80,1024]{1,0:T(8,128)(2,1)S(1)}, bf16[80,1024]{1,0:T(8,128)(2,1)S(1)}) custom-call(bf16[72,4,1024]{2,1,0:T(4,128)(2,1)S(1)} %bitcast.11, bf16[3,1024,256]{2,1,0:T(8,128)(2,1)S(1)} %bitcast.10, bf16[32,256]{1,0:T(8,128)(2,1)S(1)} %get-tuple-element.43.bias), custom_call_target="tpu_custom_call" | custom-call | flops 1000000000 | bytes 2670592 | tf_op jit(solution)/shard_map/pallas_call | solution.py:273
  8.0 0.4 collective-permute-start.4
  8.4 0.9 %collective-permute-done.4.o1 = bf16[160,256]{1,0:T(8,128)(2,1)S(1)} collective-permute-done((bf16[160,256]{1,0:T(8,128)(2,1)S(1)}, bf16[160,256]{1,0:T(8,128)(2,1)S(1)}, u32[]{:S(2)}, u32[]{:S(2)}) %collective-permute-start.4) | collective-permute-done | bytes 81952 | tf_op jit(solution)/shard_map/ppermute | solution.py:293
  9.3 0.3 shard_map.84
  9.8 1.5 %collective-permute-start.8 = (bf16[80,1024]{1,0:T(8,128)(2,1)S(1)}, bf16[80,1024]{1,0:T(8,128)(2,1)S(1)}, u32[]{:S(2)}, u32[]{:S(2)}) collective-permute-start(bf16[80,1024]{1,0:T(8,128)(2,1)S(1)} %get-tuple-element.58.mine), channel_id=1, source_target_pairs={{0,2},{1,3},{2,0},{3,1},{4,6},{5,7},{6,4},{7,5},{8,10},{9,11},{10,... | collective-permute-start | bytes 491528 | tf_op jit(solution)/shard_map/ppermute | solution.py:293
  11.2 0.9 %collective-permute-start.11 = (bf16[1024,1024]{1,0:T(8,128)(2,1)S(1)}, bf16[1024,1024]{1,0:T(8,128)(2,1)S(1)}, u32[]{:S(2)}, u32[]{:S(2)}) collective-permute-start(bf16[1024,1024]{1,0:T(8,128)(2,1)S(1)} %copy-done), channel_id=1, source_target_pairs={{0,1},{1,0},{2,3},{3,2},{4,5},{5,4},{6,7},{7,6},{8,9},{9,8},{10,11... | collective-permute-start | bytes 6291464 | tf_op jit(solution)/shard_map/ppermute | solution.py:293
  12.2 2.9 %collective-permute-done.5.other = bf16[80,1024]{1,0:T(8,128)(2,1)S(1)} collective-permute-done((bf16[80,1024]{1,0:T(8,128)(2,1)S(1)}, bf16[80,1024]{1,0:T(8,128)(2,1)S(1)}, u32[]{:S(2)}, u32[]{:S(2)}) %collective-permute-start.5) | collective-permute-done | bytes 163872 | tf_op jit(solution)/shard_map/ppermute | solution.py:293
  15.3 1.0 %collective-permute-start.6 = (bf16[40,1024]{1,0:T(8,128)(2,1)S(1)}, bf16[40,1024]{1,0:T(8,128)(2,1)S(1)}, u32[]{:S(2)}, u32[]{:S(2)}) collective-permute-start(bf16[40,1024]{1,0:T(8,128)(2,1)S(1)} %get-tuple-element.56), channel_id=1, source_target_pairs={{0,36},{1,37},{2,38},{3,39},{4,40},{5,41},{6,42},{7,43},{8,44},{9,... | collective-permute-start | bytes 245768 | tf_op jit(solution)/shard_map/ppermute | solution.py:293
  16.3 1.3 %collective-permute-start.7 = (bf16[40,1024]{1,0:T(8,128)(2,1)S(1)}, bf16[40,1024]{1,0:T(8,128)(2,1)S(1)}, u32[]{:S(2)}, u32[]{:S(2)}) collective-permute-start(bf16[40,1024]{1,0:T(8,128)(2,1)S(1)} %get-tuple-element.57), channel_id=1, source_target_pairs={{0,4},{1,5},{2,6},{3,7},{4,8},{5,9},{6,10},{7,11},{8,12},{9,13},{1... | collective-permute-start | bytes 245768 | tf_op jit(solution)/shard_map/ppermute | solution.py:293
  17.6 1.1 %collective-permute-done.8.other = bf16[80,1024]{1,0:T(8,128)(2,1)S(1)} collective-permute-done((bf16[80,1024]{1,0:T(8,128)(2,1)S(1)}, bf16[80,1024]{1,0:T(8,128)(2,1)S(1)}, u32[]{:S(2)}, u32[]{:S(2)}) %collective-permute-start.8) | collective-permute-done | bytes 163872 | tf_op jit(solution)/shard_map/ppermute | solution.py:293
  18.8 0.8 %collective-permute-start.9 = (bf16[40,1024]{1,0:T(8,128)(2,1)S(1)}, bf16[40,1024]{1,0:T(8,128)(2,1)S(1)}, u32[]{:S(2)}, u32[]{:S(2)}) collective-permute-start(bf16[40,1024]{1,0:T(8,128)(2,1)S(1)} %get-tuple-element.60), channel_id=1, source_target_pairs={{0,32},{1,33},{2,34},{3,35},{4,36},{5,37},{6,38},{7,39},{8,40},{9,... | collective-permute-start | bytes 245768 | tf_op jit(solution)/shard_map/ppermute | solution.py:293
  19.6 6.2 %collective-permute-done.6.p0 = bf16[40,1024]{1,0:T(8,128)(2,1)S(1)} collective-permute-done((bf16[40,1024]{1,0:T(8,128)(2,1)S(1)}, bf16[40,1024]{1,0:T(8,128)(2,1)S(1)}, u32[]{:S(2)}, u32[]{:S(2)}) %collective-permute-start.6) | collective-permute-done | bytes 81952 | tf_op jit(solution)/shard_map/ppermute | solution.py:293
  26.0 2.7 %shard_map.88 = (bf16[80,1024]{1,0:T(8,128)(2,1)S(1)}, bf16[80,1024]{1,0:T(8,128)(2,1)S(1)}) custom-call(bf16[80,1024]{1,0:T(8,128)(2,1)S(1)} %shard_map.86.xn_a, bf16[40,1024]{1,0:T(8,128)(2,1)S(1)} %collective-permute-done.9.p2.p0, bf16[40,1024]{1,0:T(8,128)(2,1)S(1)} %get-tuple-element.61.p3.p1, bf16[3,1024,256]{2,1,0:T(8,128)(2,1)S(1)} %bitcast.9, ...), custom_call_target="tpu_custom_call" | custom-call | flops 1000000000 | bytes 4882432 | tf_op jit(solution)/shard_map/pallas_call | solution.py:273
  28.7 0.3 collective-permute-start.10
  29.0 1.3 %collective-permute-start.14 = (bf16[80,1024]{1,0:T(8,128)(2,1)S(1)}, bf16[80,1024]{1,0:T(8,128)(2,1)S(1)}, u32[]{:S(2)}, u32[]{:S(2)}) collective-permute-start(bf16[80,1024]{1,0:T(8,128)(2,1)S(1)} %get-tuple-element.72.mine), channel_id=1, source_target_pairs={{0,2},{1,3},{2,0},{3,1},{4,6},{5,7},{6,4},{7,5},{8,10},{9,11},{10,... | collective-permute-start | bytes 491528 | tf_op jit(solution)/shard_map/ppermute | solution.py:293
  30.3 2.7 %collective-permute-done.10.other = bf16[80,1024]{1,0:T(8,128)(2,1)S(1)} collective-permute-done((bf16[80,1024]{1,0:T(8,128)(2,1)S(1)}, bf16[80,1024]{1,0:T(8,128)(2,1)S(1)}, u32[]{:S(2)}, u32[]{:S(2)}) %collective-permute-start.10) | collective-permute-done | bytes 163872 | tf_op jit(solution)/shard_map/ppermute | solution.py:293
  33.0 1.8 %shard_map.89.mine = bf16[80,1024]{1,0:T(8,128)(2,1)S(1)} custom-call(bf16[80,1024]{1,0:T(8,128)(2,1)S(1)} %get-tuple-element.65.mine, bf16[80,1024]{1,0:T(8,128)(2,1)S(1)} %collective-permute-done.10.other, bf16[40,1024]{1,0:T(8,128)(2,1)S(1)} %collective-permute-done.6.p0, bf16[40,1024]{1,0:T(8,128)(2,1)S(1)} %collective-permute-done.7.p1, ...), custom_call_target="tpu_custom_call" | custom-call | flops 1000000000 | bytes 9043968 | tf_op jit(solution)/shard_map/pallas_call | solution.py:273
  35.3 1.8 %shard_map.91.mine = bf16[80,1024]{1,0:T(8,128)(2,1)S(1)} custom-call(bf16[80,1024]{1,0:T(8,128)(2,1)S(1)} %get-tuple-element.72.mine, bf16[80,1024]{1,0:T(8,128)(2,1)S(1)} %collective-permute-done.14.other, bf16[40,1024]{1,0:T(8,128)(2,1)S(1)} %collective-permute-done.9.p2.p0, bf16[40,1024]{1,0:T(8,128)(2,1)S(1)} %get-tuple-element.61.p3.p1, ...), custom_call_target="tpu_custom_call" | custom-call | flops 1000000000 | bytes 9043968 | tf_op jit(solution)/shard_map/pallas_call | solution.py:273
  37.1 1.2 %collective-permute-start.17 = (bf16[80,1024]{1,0:T(8,128)(2,1)S(1)}, bf16[80,1024]{1,0:T(8,128)(2,1)S(1)}, u32[]{:S(2)}, u32[]{:S(2)}) collective-permute-start(bf16[80,1024]{1,0:T(8,128)(2,1)S(1)} %shard_map.91.mine), channel_id=1, source_target_pairs={{0,2},{1,3},{2,0},{3,1},{4,6},{5,7},{6,4},{7,5},{8,10},{9,11},{10,... | collective-permute-start | bytes 491528 | tf_op jit(solution)/shard_map/ppermute | solution.py:293
  38.3 1.7 %collective-permute-done.13.other = bf16[80,1024]{1,0:T(8,128)(2,1)S(1)} collective-permute-done((bf16[80,1024]{1,0:T(8,128)(2,1)S(1)}, bf16[80,1024]{1,0:T(8,128)(2,1)S(1)}, u32[]{:S(2)}, u32[]{:S(2)}) %collective-permute-start.13) | collective-permute-done | bytes 163872 | tf_op jit(solution)/shard_map/ppermute | solution.py:293
  40.1 5.2 %collective-permute-start.15 = (bf16[40,1024]{1,0:T(8,128)(2,1)S(1)}, bf16[40,1024]{1,0:T(8,128)(2,1)S(1)}, u32[]{:S(2)}, u32[]{:S(2)}) collective-permute-start(bf16[40,1024]{1,0:T(8,128)(2,1)S(1)} %get-tuple-element.73), channel_id=1, source_target_pairs={{0,254},{1,255},{2,252},{3,253},{4,224},{5,225},{6,226},{7,227},{8... | collective-permute-start | bytes 245768 | tf_op jit(solution)/shard_map/ppermute | solution.py:293
  45.2 0.7 %collective-permute-start.16 = (bf16[40,1024]{1,0:T(8,128)(2,1)S(1)}, bf16[40,1024]{1,0:T(8,128)(2,1)S(1)}, u32[]{:S(2)}, u32[]{:S(2)}) collective-permute-start(bf16[40,1024]{1,0:T(8,128)(2,1)S(1)} %get-tuple-element.74), channel_id=1, source_target_pairs={{0,30},{1,31},{2,28},{3,29},{4,0},{5,1},{6,2},{7,3},{8,4},{9,5},{1... | collective-permute-start | bytes 245768 | tf_op jit(solution)/shard_map/ppermute | solution.py:293
  46.0 0.9 %collective-permute-start.18 = (bf16[40,1024]{1,0:T(8,128)(2,1)S(1)}, bf16[40,1024]{1,0:T(8,128)(2,1)S(1)}, u32[]{:S(2)}, u32[]{:S(2)}) collective-permute-start(bf16[40,1024]{1,0:T(8,128)(2,1)S(1)} %get-tuple-element.76), channel_id=1, source_target_pairs={{0,224},{1,225},{2,226},{3,227},{4,228},{5,229},{6,230},{7,231},{8... | collective-permute-start | bytes 245768 | tf_op jit(solution)/shard_map/ppermute | solution.py:293
  46.9 2.7 %collective-permute-done.16.p1 = bf16[40,1024]{1,0:T(8,128)(2,1)S(1)} collective-permute-done((bf16[40,1024]{1,0:T(8,128)(2,1)S(1)}, bf16[40,1024]{1,0:T(8,128)(2,1)S(1)}, u32[]{:S(2)}, u32[]{:S(2)}) %collective-permute-start.16) | collective-permute-done | bytes 81952 | tf_op jit(solution)/shard_map/ppermute | solution.py:293
  49.7 6.2 %collective-permute-start.20 = (bf16[80,1024]{1,0:T(8,128)(2,1)S(1)}, bf16[80,1024]{1,0:T(8,128)(2,1)S(1)}, u32[]{:S(2)}, u32[]{:S(2)}) collective-permute-start(bf16[80,1024]{1,0:T(8,128)(2,1)S(1)} %shard_map.94.m1), channel_id=1, source_target_pairs={{0,1},{1,0},{2,3},{3,2},{4,5},{5,4},{6,7},{7,6},{8,9},{9,8},{10,11... | collective-permute-start | bytes 491528 | tf_op jit(solution)/shard_map/ppermute | solution.py:293
  56.0 0.9 %collective-permute-done.20.s1 = bf16[80,1024]{1,0:T(8,128)(2,1)S(1)} collective-permute-done((bf16[80,1024]{1,0:T(8,128)(2,1)S(1)}, bf16[80,1024]{1,0:T(8,128)(2,1)S(1)}, u32[]{:S(2)}, u32[]{:S(2)}) %collective-permute-start.20) | collective-permute-done | bytes 163872 | tf_op jit(solution)/shard_map/ppermute | solution.py:293
  56.9 0.4 collective-permute-done.19.s0
  57.3 1.3 %shard_map.95 = bf16[72,4,1024]{2,1,0:T(4,128)(2,1)} custom-call(bf16[80,1024]{1,0:T(8,128)(2,1)S(1)} %shard_map.92.m0, bf16[80,1024]{1,0:T(8,128)(2,1)S(1)} %shard_map.94.m1, bf16[80,1024]{1,0:T(8,128)(2,1)S(1)} %collective-permute-done.19.s0, bf16[80,1024]{1,0:T(8,128)(2,1)S(1)} %collective-permute-done.20.s1), custom_call_target="tpu_custom_call" | custom-call | flops 200000000 | bytes 1245184 | tf_op jit(solution)/shard_map/pallas_call | solution.py:273
  (40 shorter events, 1.6 us)
Async XLA Ops:
  0.0 5.5 %copy-start.5 = (bf16[1024,3,256]{2,0,1:T(8,128)(2,1)S(1)}, bf16[1024,3,256]{2,0,1:T(8,128)(2,1)}, u32[]{:S(2)}) copy-start(bf16[1024,3,256]{2,0,1:T(8,128)(2,1)} %param.9) | copy-start | bytes 4718596
  0.0 5.5 %copy-start.6 = (bf16[4,6,12,1024]{3,0,2,1:T(4,128)(2,1)S(1)}, bf16[4,6,12,1024]{3,0,2,1:T(4,128)(2,1)}, u32[]{:S(2)}) copy-start(bf16[4,6,12,1024]{3,0,2,1:T(4,128)(2,1)} %param.8) | copy-start | bytes 1769476
  0.0 8.0 %collective-permute-start.2 = (bf16[3,1024,256]{2,1,0:T(8,128)(2,1)}, bf16[3,1024,256]{2,1,0:T(8,128)(2,1)S(1)}, u32[]{:S(2)}, u32[]{:S(2)}) collective-permute-start(bf16[3,1024,256]{2,1,0:T(8,128)(2,1)} %bitcast.8), channel_id=1, source_target_pairs={{0,1},{1,0},{2,3},{3,2},{4,5},{5,4},{6,7},{7,6},{8,9},{9,8},{10,11... | collective-permute-start | bytes 4718600 | tf_op jit(solution)/shard_map/ppermute | solution.py:293
  3.2 4.7 %collective-permute-start = (bf16[256,1024]{1,0:T(8,128)(2,1)}, bf16[256,1024]{1,0:T(8,128)(2,1)S(1)}, u32[]{:S(2)}, u32[]{:S(2)}) collective-permute-start(bf16[256,1024]{1,0:T(8,128)(2,1)} %w0.1), channel_id=1, source_target_pairs={{0,1},{1,0},{2,3},{3,2},{4,5},{5,4},{6,7},{7,6},{8,9},{9,8},{10,11... | collective-permute-start | bytes 1572872 | tf_op jit(solution)/shard_map/ppermute | solution.py:293
  3.2 4.8 %collective-permute-start.1 = (bf16[256,1024]{1,0:T(8,128)(2,1)}, bf16[256,1024]{1,0:T(8,128)(2,1)S(1)}, u32[]{:S(2)}, u32[]{:S(2)}) collective-permute-start(bf16[256,1024]{1,0:T(8,128)(2,1)} %o_own.1), channel_id=1, source_target_pairs={{0,1},{1,0},{2,3},{3,2},{4,5},{5,4},{6,7},{7,6},{8,9},{9,8},{10,11... | collective-permute-start | bytes 1572872 | tf_op jit(solution)/shard_map/ppermute | solution.py:293
  3.8 0.7 %copy-start.7 = (f32[2,4,37]{2,1,0:T(4,128)S(1)}, f32[2,4,37]{2,1,0:T(4,128)}, u32[]{:S(2)}) copy-start(f32[2,4,37]{2,1,0:T(4,128)} %table.1) | copy-start | bytes 3556
  5.3 4.1 %copy-start.4 = (bf16[256,1024]{1,0:T(8,128)(2,1)S(1)}, bf16[256,1024]{1,0:T(8,128)(2,1)}, u32[]{:S(2)}) copy-start(bf16[256,1024]{1,0:T(8,128)(2,1)} %w0.1) | copy-start | bytes 1572868
  5.3 2.6 %collective-permute-start.3 = (bf16[32,256]{1,0:T(8,128)(2,1)S(1)}, bf16[32,256]{1,0:T(8,128)(2,1)S(1)}, u32[]{:S(2)}, u32[]{:S(2)}) collective-permute-start(bf16[32,256]{1,0:T(8,128)(2,1)S(1)} %get-tuple-element.46.b_own), channel_id=1, source_target_pairs={{0,1},{1,0},{2,3},{3,2},{4,5},{5,4},{6,7},{7,6},{8,9},{9,8},{10,11... | collective-permute-start | bytes 49160 | tf_op jit(solution)/shard_map/ppermute | solution.py:293
  5.5 5.7 %copy-start = (bf16[1024,1024]{1,0:T(8,128)(2,1)S(1)}, bf16[1024,1024]{1,0:T(8,128)(2,1)}, u32[]{:S(2)}) copy-start(bf16[1024,1024]{1,0:T(8,128)(2,1)} %u0.3) | copy-start | bytes 6291460
  5.5 6.7 %copy-start.1 = (bf16[1024,1024]{1,0:T(8,128)(2,1)S(1)}, bf16[1024,1024]{1,0:T(8,128)(2,1)}, u32[]{:S(2)}) copy-start(bf16[1024,1024]{1,0:T(8,128)(2,1)} %d0.3) | copy-start | bytes 6291460
  8.0 1.3 %collective-permute-start.4 = (bf16[160,256]{1,0:T(8,128)(2,1)S(1)}, bf16[160,256]{1,0:T(8,128)(2,1)S(1)}, u32[]{:S(2)}, u32[]{:S(2)}) collective-permute-start(bf16[160,256]{1,0:T(8,128)(2,1)S(1)} %get-tuple-element.48), channel_id=1, source_target_pairs={{0,1},{1,0},{2,3},{3,2},{4,5},{5,4},{6,7},{7,6},{8,9},{9,8},{10,11... | collective-permute-start | bytes 245768 | tf_op jit(solution)/shard_map/ppermute | solution.py:293
  9.7 5.5 %collective-permute-start.5 = (bf16[80,1024]{1,0:T(8,128)(2,1)S(1)}, bf16[80,1024]{1,0:T(8,128)(2,1)S(1)}, u32[]{:S(2)}, u32[]{:S(2)}) collective-permute-start(bf16[80,1024]{1,0:T(8,128)(2,1)S(1)} %get-tuple-element.51.mine), channel_id=1, source_target_pairs={{0,2},{1,3},{2,0},{3,1},{4,6},{5,7},{6,4},{7,5},{8,10},{9,11},{10,... | collective-permute-start | bytes 491528 | tf_op jit(solution)/shard_map/ppermute | solution.py:293
  9.8 8.9 %collective-permute-start.8 = (bf16[80,1024]{1,0:T(8,128)(2,1)S(1)}, bf16[80,1024]{1,0:T(8,128)(2,1)S(1)}, u32[]{:S(2)}, u32[]{:S(2)}) collective-permute-start(bf16[80,1024]{1,0:T(8,128)(2,1)S(1)} %get-tuple-element.58.mine), channel_id=1, source_target_pairs={{0,2},{1,3},{2,0},{3,1},{4,6},{5,7},{6,4},{7,5},{8,10},{9,11},{10,... | collective-permute-start | bytes 491528 | tf_op jit(solution)/shard_map/ppermute | solution.py:293
  11.2 21.8 %collective-permute-start.11 = (bf16[1024,1024]{1,0:T(8,128)(2,1)S(1)}, bf16[1024,1024]{1,0:T(8,128)(2,1)S(1)}, u32[]{:S(2)}, u32[]{:S(2)}) collective-permute-start(bf16[1024,1024]{1,0:T(8,128)(2,1)S(1)} %copy-done), channel_id=1, source_target_pairs={{0,1},{1,0},{2,3},{3,2},{4,5},{5,4},{6,7},{7,6},{8,9},{9,8},{10,11... | collective-permute-start | bytes 6291464 | tf_op jit(solution)/shard_map/ppermute | solution.py:293
  12.1 20.9 %collective-permute-start.12 = (bf16[1024,1024]{1,0:T(8,128)(2,1)S(1)}, bf16[1024,1024]{1,0:T(8,128)(2,1)S(1)}, u32[]{:S(2)}, u32[]{:S(2)}) collective-permute-start(bf16[1024,1024]{1,0:T(8,128)(2,1)S(1)} %copy-done.1), channel_id=1, source_target_pairs={{0,1},{1,0},{2,3},{3,2},{4,5},{5,4},{6,7},{7,6},{8,9},{9,8},{10,11... | collective-permute-start | bytes 6291464 | tf_op jit(solution)/shard_map/ppermute | solution.py:293
  15.3 10.5 %collective-permute-start.6 = (bf16[40,1024]{1,0:T(8,128)(2,1)S(1)}, bf16[40,1024]{1,0:T(8,128)(2,1)S(1)}, u32[]{:S(2)}, u32[]{:S(2)}) collective-permute-start(bf16[40,1024]{1,0:T(8,128)(2,1)S(1)} %get-tuple-element.56), channel_id=1, source_target_pairs={{0,36},{1,37},{2,38},{3,39},{4,40},{5,41},{6,42},{7,43},{8,44},{9,... | collective-permute-start | bytes 245768 | tf_op jit(solution)/shard_map/ppermute | solution.py:293
  16.3 9.5 %collective-permute-start.7 = (bf16[40,1024]{1,0:T(8,128)(2,1)S(1)}, bf16[40,1024]{1,0:T(8,128)(2,1)S(1)}, u32[]{:S(2)}, u32[]{:S(2)}) collective-permute-start(bf16[40,1024]{1,0:T(8,128)(2,1)S(1)} %get-tuple-element.57), channel_id=1, source_target_pairs={{0,4},{1,5},{2,6},{3,7},{4,8},{5,9},{6,10},{7,11},{8,12},{9,13},{1... | collective-permute-start | bytes 245768 | tf_op jit(solution)/shard_map/ppermute | solution.py:293
  18.8 7.2 %copy-start.2 = (bf16[1024,3,256]{2,0,1:T(8,128)(2,1)S(1)}, bf16[1024,3,256]{2,0,1:T(8,128)(2,1)}, u32[]{:S(2)}) copy-start(bf16[1024,3,256]{2,0,1:T(8,128)(2,1)} %param.10) | copy-start | bytes 4718596
  18.8 7.2 %copy-start.3 = (bf16[256,1024]{1,0:T(8,128)(2,1)S(1)}, bf16[256,1024]{1,0:T(8,128)(2,1)}, u32[]{:S(2)}) copy-start(bf16[256,1024]{1,0:T(8,128)(2,1)} %o_own.1) | copy-start | bytes 1572868
  18.8 7.2 %collective-permute-start.9 = (bf16[40,1024]{1,0:T(8,128)(2,1)S(1)}, bf16[40,1024]{1,0:T(8,128)(2,1)S(1)}, u32[]{:S(2)}, u32[]{:S(2)}) collective-permute-start(bf16[40,1024]{1,0:T(8,128)(2,1)S(1)} %get-tuple-element.60), channel_id=1, source_target_pairs={{0,32},{1,33},{2,34},{3,35},{4,36},{5,37},{6,38},{7,39},{8,40},{9,... | collective-permute-start | bytes 245768 | tf_op jit(solution)/shard_map/ppermute | solution.py:293
  28.7 4.3 %collective-permute-start.10 = (bf16[80,1024]{1,0:T(8,128)(2,1)S(1)}, bf16[80,1024]{1,0:T(8,128)(2,1)S(1)}, u32[]{:S(2)}, u32[]{:S(2)}) collective-permute-start(bf16[80,1024]{1,0:T(8,128)(2,1)S(1)} %get-tuple-element.65.mine), channel_id=1, source_target_pairs={{0,2},{1,3},{2,0},{3,1},{4,6},{5,7},{6,4},{7,5},{8,10},{9,11},{10,... | collective-permute-start | bytes 491528 | tf_op jit(solution)/shard_map/ppermute | solution.py:293
  29.0 6.2 %collective-permute-start.14 = (bf16[80,1024]{1,0:T(8,128)(2,1)S(1)}, bf16[80,1024]{1,0:T(8,128)(2,1)S(1)}, u32[]{:S(2)}, u32[]{:S(2)}) collective-permute-start(bf16[80,1024]{1,0:T(8,128)(2,1)S(1)} %get-tuple-element.72.mine), channel_id=1, source_target_pairs={{0,2},{1,3},{2,0},{3,1},{4,6},{5,7},{6,4},{7,5},{8,10},{9,11},{10,... | collective-permute-start | bytes 491528 | tf_op jit(solution)/shard_map/ppermute | solution.py:293
  34.8 5.2 %collective-permute-start.13 = (bf16[80,1024]{1,0:T(8,128)(2,1)S(1)}, bf16[80,1024]{1,0:T(8,128)(2,1)S(1)}, u32[]{:S(2)}, u32[]{:S(2)}) collective-permute-start(bf16[80,1024]{1,0:T(8,128)(2,1)S(1)} %shard_map.89.mine), channel_id=1, source_target_pairs={{0,2},{1,3},{2,0},{3,1},{4,6},{5,7},{6,4},{7,5},{8,10},{9,11},{10,... | collective-permute-start | bytes 491528 | tf_op jit(solution)/shard_map/ppermute | solution.py:293
  37.1 8.8 %collective-permute-start.17 = (bf16[80,1024]{1,0:T(8,128)(2,1)S(1)}, bf16[80,1024]{1,0:T(8,128)(2,1)S(1)}, u32[]{:S(2)}, u32[]{:S(2)}) collective-permute-start(bf16[80,1024]{1,0:T(8,128)(2,1)S(1)} %shard_map.91.mine), channel_id=1, source_target_pairs={{0,2},{1,3},{2,0},{3,1},{4,6},{5,7},{6,4},{7,5},{8,10},{9,11},{10,... | collective-permute-start | bytes 491528 | tf_op jit(solution)/shard_map/ppermute | solution.py:293
  40.1 6.8 %collective-permute-start.15 = (bf16[40,1024]{1,0:T(8,128)(2,1)S(1)}, bf16[40,1024]{1,0:T(8,128)(2,1)S(1)}, u32[]{:S(2)}, u32[]{:S(2)}) collective-permute-start(bf16[40,1024]{1,0:T(8,128)(2,1)S(1)} %get-tuple-element.73), channel_id=1, source_target_pairs={{0,254},{1,255},{2,252},{3,253},{4,224},{5,225},{6,226},{7,227},{8... | collective-permute-start | bytes 245768 | tf_op jit(solution)/shard_map/ppermute | solution.py:293
  45.2 4.4 %collective-permute-start.16 = (bf16[40,1024]{1,0:T(8,128)(2,1)S(1)}, bf16[40,1024]{1,0:T(8,128)(2,1)S(1)}, u32[]{:S(2)}, u32[]{:S(2)}) collective-permute-start(bf16[40,1024]{1,0:T(8,128)(2,1)S(1)} %get-tuple-element.74), channel_id=1, source_target_pairs={{0,30},{1,31},{2,28},{3,29},{4,0},{5,1},{6,2},{7,3},{8,4},{9,5},{1... | collective-permute-start | bytes 245768 | tf_op jit(solution)/shard_map/ppermute | solution.py:293
  46.0 3.7 %collective-permute-start.18 = (bf16[40,1024]{1,0:T(8,128)(2,1)S(1)}, bf16[40,1024]{1,0:T(8,128)(2,1)S(1)}, u32[]{:S(2)}, u32[]{:S(2)}) collective-permute-start(bf16[40,1024]{1,0:T(8,128)(2,1)S(1)} %get-tuple-element.76), channel_id=1, source_target_pairs={{0,224},{1,225},{2,226},{3,227},{4,228},{5,229},{6,230},{7,231},{8... | collective-permute-start | bytes 245768 | tf_op jit(solution)/shard_map/ppermute | solution.py:293
  49.7 7.2 %collective-permute-start.20 = (bf16[80,1024]{1,0:T(8,128)(2,1)S(1)}, bf16[80,1024]{1,0:T(8,128)(2,1)S(1)}, u32[]{:S(2)}, u32[]{:S(2)}) collective-permute-start(bf16[80,1024]{1,0:T(8,128)(2,1)S(1)} %shard_map.94.m1), channel_id=1, source_target_pairs={{0,1},{1,0},{2,3},{3,2},{4,5},{5,4},{6,7},{7,6},{8,9},{9,8},{10,11... | collective-permute-start | bytes 491528 | tf_op jit(solution)/shard_map/ppermute | solution.py:293
  55.9 1.4 %collective-permute-start.19 = (bf16[80,1024]{1,0:T(8,128)(2,1)S(1)}, bf16[80,1024]{1,0:T(8,128)(2,1)S(1)}, u32[]{:S(2)}, u32[]{:S(2)}) collective-permute-start(bf16[80,1024]{1,0:T(8,128)(2,1)S(1)} %shard_map.92.m0), channel_id=1, source_target_pairs={{0,1},{1,0},{2,3},{3,2},{4,5},{5,4},{6,7},{7,6},{8,9},{9,8},{10,11... | collective-permute-start | bytes 491528 | tf_op jit(solution)/shard_map/ppermute | solution.py:293

commit v8 on v7

--- a/solution.py
+++ b/solution.py
@@ -75,10 +75,10 @@
     return level, row, rest - row * 6
 
 
-def kept_place(index):
-    quad = (index * 205) >> 13
-    slot = index - quad * ROWS
-    return (quad, slot) + piece_place(slot)
+def kept_place(index, core):
+    piece = (index * 205) >> 13
+    slot = index - piece * ROWS
+    return (jnp.where(core == 0, piece, 3 - piece), slot) + piece_place(slot)
 
 
 def real_level(level, core):
@@ -159,15 +159,14 @@
             halves.append(pair_heads(q[rows, cols], k[rows, cols], v[rows, cols], extra, feat))
         parts.append(jnp.concatenate(halves, axis=0))
     mixed = jnp.concatenate(parts, axis=1)
-    quad, slot, level, row, col = kept_place(iota((KEPT, 1), 0))
-    row, col = patch_place(quad, row, col)
     lanes = iota((KEPT, PATCH), 1)
-    for out, chosen in ((keep, core), (give, 1 - core)):
-        place = real_level(level, chosen) * 72 + row * 12 + col
-        place = jnp.where(slot < USED, place, -1)
+    for out, chosen in ((give, 1 - core), (keep, core)):
+        quad, slot, level, row, col = kept_place(iota((KEPT, 1), 0), chosen)
+        row, col = patch_place(quad, row, col)
+        level = real_level(level, chosen)
+        place = jnp.where(slot < USED, level * 72 + row * 12 + col, -1)
         out[...] = dot(one_hot(lanes == place), mixed).astype(jnp.bfloat16)
-    place = (row * 12 + col) * 4 + real_level(level, core)
-    place = jnp.where(slot < USED, place, -1)
+    place = jnp.where(slot < USED, (row * 12 + col) * 4 + level, -1)
     base = dot(one_hot(lanes == place), floats.astype(jnp.bfloat16)).astype(jnp.bfloat16)
     for h in range(2):
         bases[h][...] = base[h * HALF : (h + 1) * HALF]
@@ -204,13 +203,14 @@
 def second_kernel(xn_a, p2, p3, w_own, w_sib, o_own, o_sib, b_own, b_sib, *outs):
     xn_b = normalize(joined((p2, p3))).astype(jnp.float32)
     xn = jnp.concatenate([xn_a[...].astype(jnp.float32), xn_b], axis=0).astype(jnp.bfloat16)
-    quad, slot, level, row, col = kept_place(iota((KEPT, 1), 0))
+    core = core_index()
+    quad, slot, level, row, col = kept_place(iota((KEPT, 1), 0), core)
     row, col = row + 3 * (quad & 1), col + 3 * (quad & 2)
     feat = features(level, row, col, slot < USED, KEPT)
     lane = iota((KEPT, 128), 1)
     j = lane & (FEAT - 1)
-    split_levels = core_index() == 1
-    split_rows = lax.axis_index("lat") == 0
+    split_levels = core == 1
+    split_rows = lax.axis_index("lat") == jnp.where(core == 0, 0, lax.axis_size("lat") - 1)
     ban_level = (j < WL) & (j != level)
     ban_row = (j >= F_Y) & (j < F_Y + WY) & ((j >= F_Y + SY) != (row >= SY))
     ban = jnp.where(ban_level, split_levels.astype(jnp.int32), jnp.where(ban_row, split_rows.astype(jnp.int32), 0))
@@ -255,10 +255,10 @@
 
 def place_kernel(m0, m1, s0, s1, out):
     core = core_index()
-    quad, slot, level, row, col = kept_place(iota((1, KEPT), 1))
-    row, col = patch_place(quad, row, col)
     total = None
     for chosen, parts in ((core, (m0, m1)), (1 - core, (s0, s1))):
+        quad, slot, level, row, col = kept_place(iota((1, KEPT), 1), chosen)
+        row, col = patch_place(quad, row, col)
         place = (row * 12 + col) * 4 + real_level(level, chosen)
         place = jnp.where(slot < USED, place, -1)
         source = jnp.concatenate([part[...] for part in parts], axis=0)
@@ -298,11 +298,19 @@
     def chip_swap(value):
         return move(value, lambda a, b, m: (a, b, m ^ 2))
 
+    def shift(value, dy, dx):
+        def target(a, b, m):
+            way = 1 - 2 * (m % 2)
+            seam = dx and (b if way * dx < 0 else b + 1) % turn == 0
+            return a + way * dy, b + way * dx, m ^ 2 if seam else m
+
+        return move(value, target)
+
     def out_to(value, dy, dx):
-        return move(value, lambda a, b, m: (a + dy, b + dx, m ^ 2 if dx and (b + 1) % turn == 0 else m))
+        return shift(value, dy, dx)
 
     def home(value, dy, dx):
-        return move(value, lambda a, b, m: (a - dy, b - dx, m ^ 2 if dx and b % turn == 0 else m))
+        return shift(value, -dy, -dx)
 
     half, piece = [(HALF, width)], [(ROWS, width)]
     heads, features = [(KEPT, 256)], [(FEAT, 256)]

time: 58.7 us -> 60.1 us (1.024)
  starting transfers between devices: 26 us -> 27.8 us
    ppermute x21, starting transfers between devices: 26 us -> 27.8 us  [move(): return lax.ppermute(value, AXES, pairs(counts, target))]
  transfers between devices with their start and end apart: 21 -> 21, of which waited for: 11 -> 14; matrix products, arithmetic and copies ran while one was open for 0% -> 0% of each run, Pallas kernels for 17% -> 17%
where the time goes in v8:
time: 60.1 us; the launch traced here: 60 us
  starting transfers between devices  27.8 us (46%)
  waiting for transfers between devices  19.6 us (33%)
  Pallas kernels  11.7 us (19%)
  local copies, waits for them, and re-layouts  0.72 us (1%)
    ppermute x21, starting transfers between devices, move(): return lax.ppermute(value, AXES, pairs(counts, target))  27.8 us
    ppermute x21, waiting for transfers between devices, move(): return lax.ppermute(value, AXES, pairs(counts, target))  19.6 us
    pallas_call x14, Pallas kernels, call(): pl.pallas_call(kernel, out_shape=shapes, in_specs=[pl.BlockSpec(memory_sp...  11.7 us
  transfers between devices with their start and end apart: 21, of which 14 were waited for; matrix products, arithmetic and copies ran while one was open for 0% of the time, Pallas kernels for 17%

profile of v8, /device:TPU:1, one launch (start us, length us, event | category | flops | bytes accessed | tf_op | source)
XLA Modules:
  0.0 60.0 jit_solution(12187921456043797608)
XLA Ops:
  0.0 3.2 %collective-permute-start.2 = (bf16[3,1024,256]{2,1,0:T(8,128)(2,1)}, bf16[3,1024,256]{2,1,0:T(8,128)(2,1)S(1)}, u32[]{:S(2)}, u32[]{:S(2)}) collective-permute-start(bf16[3,1024,256]{2,1,0:T(8,128)(2,1)} %bitcast.8), channel_id=1, source_target_pairs={{0,1},{1,0},{2,3},{3,2},{4,5},{5,4},{6,7},{7,6},{8,9},{9,8},{10,11... | collective-permute-start | bytes 4718600 | tf_op jit(solution)/shard_map/ppermute | solution.py:293
  3.2 0.5 collective-permute-start.1
  3.8 0.7 %copy-done.7 = f32[2,4,37]{2,1,0:T(4,128)S(1)} copy-done((f32[2,4,37]{2,1,0:T(4,128)S(1)}, f32[2,4,37]{2,1,0:T(4,128)}, u32[]{:S(2)}) %copy-start.7) | copy-done | bytes 1208
  4.4 0.8 %shard_map.82 = (bf16[32,256]{1,0:T(8,128)(2,1)S(1)}, bf16[32,256]{1,0:T(8,128)(2,1)S(1)}) custom-call(f32[2,4,37]{2,1,0:T(4,128)S(1)} %copy-done.7), custom_call_target="tpu_custom_call" | custom-call | flops 5000000000 | bytes 33952 | tf_op jit(solution)/shard_map/pallas_call | solution.py:273
  5.5 2.4 %shard_map.83 = (bf16[160,256]{1,0:T(8,128)(2,1)S(1)}, bf16[160,256]{1,0:T(8,128)(2,1)S(1)}, bf16[80,1024]{1,0:T(8,128)(2,1)S(1)}, bf16[80,1024]{1,0:T(8,128)(2,1)S(1)}) custom-call(bf16[72,4,1024]{2,1,0:T(4,128)(2,1)S(1)} %bitcast.11, bf16[3,1024,256]{2,1,0:T(8,128)(2,1)S(1)} %bitcast.10, bf16[32,256]{1,0:T(8,128)(2,1)S(1)} %get-tuple-element.43.bias), custom_call_target="tpu_custom_call" | custom-call | flops 1000000000 | bytes 2670592 | tf_op jit(solution)/shard_map/pallas_call | solution.py:273
  8.0 0.4 collective-permute-start.4
  8.4 0.9 %collective-permute-done.4.o1 = bf16[160,256]{1,0:T(8,128)(2,1)S(1)} collective-permute-done((bf16[160,256]{1,0:T(8,128)(2,1)S(1)}, bf16[160,256]{1,0:T(8,128)(2,1)S(1)}, u32[]{:S(2)}, u32[]{:S(2)}) %collective-permute-start.4) | collective-permute-done | bytes 81952 | tf_op jit(solution)/shard_map/ppermute | solution.py:293
  9.8 1.5 %collective-permute-start.8 = (bf16[80,1024]{1,0:T(8,128)(2,1)S(1)}, bf16[80,1024]{1,0:T(8,128)(2,1)S(1)}, u32[]{:S(2)}, u32[]{:S(2)}) collective-permute-start(bf16[80,1024]{1,0:T(8,128)(2,1)S(1)} %get-tuple-element.58.mine), channel_id=1, source_target_pairs={{0,2},{1,3},{2,0},{3,1},{4,6},{5,7},{6,4},{7,5},{8,10},{9,11},{10,... | collective-permute-start | bytes 491528 | tf_op jit(solution)/shard_map/ppermute | solution.py:293
  11.3 0.9 %collective-permute-start.11 = (bf16[1024,1024]{1,0:T(8,128)(2,1)S(1)}, bf16[1024,1024]{1,0:T(8,128)(2,1)S(1)}, u32[]{:S(2)}, u32[]{:S(2)}) collective-permute-start(bf16[1024,1024]{1,0:T(8,128)(2,1)S(1)} %copy-done), channel_id=1, source_target_pairs={{0,1},{1,0},{2,3},{3,2},{4,5},{5,4},{6,7},{7,6},{8,9},{9,8},{10,11... | collective-permute-start | bytes 6291464 | tf_op jit(solution)/shard_map/ppermute | solution.py:293
  12.3 3.0 %collective-permute-done.5.other = bf16[80,1024]{1,0:T(8,128)(2,1)S(1)} collective-permute-done((bf16[80,1024]{1,0:T(8,128)(2,1)S(1)}, bf16[80,1024]{1,0:T(8,128)(2,1)S(1)}, u32[]{:S(2)}, u32[]{:S(2)}) %collective-permute-start.5) | collective-permute-done | bytes 163872 | tf_op jit(solution)/shard_map/ppermute | solution.py:293
  15.3 8.6 %collective-permute-start.6 = (bf16[40,1024]{1,0:T(8,128)(2,1)S(1)}, bf16[40,1024]{1,0:T(8,128)(2,1)S(1)}, u32[]{:S(2)}, u32[]{:S(2)}) collective-permute-start(bf16[40,1024]{1,0:T(8,128)(2,1)S(1)} %get-tuple-element.56), channel_id=1, source_target_pairs={{0,36},{1,255},{2,38},{3,253},{4,40},{5,225},{6,42},{7,227},{8,44}... | collective-permute-start | bytes 245768 | tf_op jit(solution)/shard_map/ppermute | solution.py:293
  23.9 0.5 collective-permute-start.7
  24.4 1.0 %collective-permute-start.9 = (bf16[40,1024]{1,0:T(8,128)(2,1)S(1)}, bf16[40,1024]{1,0:T(8,128)(2,1)S(1)}, u32[]{:S(2)}, u32[]{:S(2)}) collective-permute-start(bf16[40,1024]{1,0:T(8,128)(2,1)S(1)} %get-tuple-element.60), channel_id=1, source_target_pairs={{0,32},{1,225},{2,34},{3,227},{4,36},{5,229},{6,38},{7,231},{8,40}... | collective-permute-start | bytes 245768 | tf_op jit(solution)/shard_map/ppermute | solution.py:293
  25.4 2.0 %collective-permute-done.7.p1 = bf16[40,1024]{1,0:T(8,128)(2,1)S(1)} collective-permute-done((bf16[40,1024]{1,0:T(8,128)(2,1)S(1)}, bf16[40,1024]{1,0:T(8,128)(2,1)S(1)}, u32[]{:S(2)}, u32[]{:S(2)}) %collective-permute-start.7) | collective-permute-done | bytes 81952 | tf_op jit(solution)/shard_map/ppermute | solution.py:293
  27.7 0.5 collective-permute-done.9.p2.p0
  28.1 2.7 %shard_map.88 = (bf16[80,1024]{1,0:T(8,128)(2,1)S(1)}, bf16[80,1024]{1,0:T(8,128)(2,1)S(1)}) custom-call(bf16[80,1024]{1,0:T(8,128)(2,1)S(1)} %shard_map.86.xn_a, bf16[40,1024]{1,0:T(8,128)(2,1)S(1)} %collective-permute-done.9.p2.p0, bf16[40,1024]{1,0:T(8,128)(2,1)S(1)} %get-tuple-element.61.p3.p1, bf16[3,1024,256]{2,1,0:T(8,128)(2,1)S(1)} %bitcast.9, ...), custom_call_target="tpu_custom_call" | custom-call | flops 1000000000 | bytes 4882432 | tf_op jit(solution)/shard_map/pallas_call | solution.py:273
  31.0 1.5 %collective-permute-start.14 = (bf16[80,1024]{1,0:T(8,128)(2,1)S(1)}, bf16[80,1024]{1,0:T(8,128)(2,1)S(1)}, u32[]{:S(2)}, u32[]{:S(2)}) collective-permute-start(bf16[80,1024]{1,0:T(8,128)(2,1)S(1)} %get-tuple-element.72.mine), channel_id=1, source_target_pairs={{0,2},{1,3},{2,0},{3,1},{4,6},{5,7},{6,4},{7,5},{8,10},{9,11},{10,... | collective-permute-start | bytes 491528 | tf_op jit(solution)/shard_map/ppermute | solution.py:293
  32.4 3.6 %collective-permute-done.10.other = bf16[80,1024]{1,0:T(8,128)(2,1)S(1)} collective-permute-done((bf16[80,1024]{1,0:T(8,128)(2,1)S(1)}, bf16[80,1024]{1,0:T(8,128)(2,1)S(1)}, u32[]{:S(2)}, u32[]{:S(2)}) %collective-permute-start.10) | collective-permute-done | bytes 163872 | tf_op jit(solution)/shard_map/ppermute | solution.py:293
  36.0 1.8 %shard_map.89.mine = bf16[80,1024]{1,0:T(8,128)(2,1)S(1)} custom-call(bf16[80,1024]{1,0:T(8,128)(2,1)S(1)} %get-tuple-element.65.mine, bf16[80,1024]{1,0:T(8,128)(2,1)S(1)} %collective-permute-done.10.other, bf16[40,1024]{1,0:T(8,128)(2,1)S(1)} %collective-permute-done.6.p0, bf16[40,1024]{1,0:T(8,128)(2,1)S(1)} %collective-permute-done.7.p1, ...), custom_call_target="tpu_custom_call" | custom-call | flops 1000000000 | bytes 9043968 | tf_op jit(solution)/shard_map/pallas_call | solution.py:273
  38.0 1.5 %collective-permute-done.14.other = bf16[80,1024]{1,0:T(8,128)(2,1)S(1)} collective-permute-done((bf16[80,1024]{1,0:T(8,128)(2,1)S(1)}, bf16[80,1024]{1,0:T(8,128)(2,1)S(1)}, u32[]{:S(2)}, u32[]{:S(2)}) %collective-permute-start.14) | collective-permute-done | bytes 163872 | tf_op jit(solution)/shard_map/ppermute | solution.py:293
  39.6 1.8 %shard_map.91.mine = bf16[80,1024]{1,0:T(8,128)(2,1)S(1)} custom-call(bf16[80,1024]{1,0:T(8,128)(2,1)S(1)} %get-tuple-element.72.mine, bf16[80,1024]{1,0:T(8,128)(2,1)S(1)} %collective-permute-done.14.other, bf16[40,1024]{1,0:T(8,128)(2,1)S(1)} %collective-permute-done.9.p2.p0, bf16[40,1024]{1,0:T(8,128)(2,1)S(1)} %get-tuple-element.61.p3.p1, ...), custom_call_target="tpu_custom_call" | custom-call | flops 1000000000 | bytes 9043968 | tf_op jit(solution)/shard_map/pallas_call | solution.py:273
  41.5 0.6 %collective-permute-done.13.other = bf16[80,1024]{1,0:T(8,128)(2,1)S(1)} collective-permute-done((bf16[80,1024]{1,0:T(8,128)(2,1)S(1)}, bf16[80,1024]{1,0:T(8,128)(2,1)S(1)}, u32[]{:S(2)}, u32[]{:S(2)}) %collective-permute-start.13) | collective-permute-done | bytes 163872 | tf_op jit(solution)/shard_map/ppermute | solution.py:293
  42.2 2.8 %collective-permute-start.15 = (bf16[40,1024]{1,0:T(8,128)(2,1)S(1)}, bf16[40,1024]{1,0:T(8,128)(2,1)S(1)}, u32[]{:S(2)}, u32[]{:S(2)}) collective-permute-start(bf16[40,1024]{1,0:T(8,128)(2,1)S(1)} %get-tuple-element.73), channel_id=1, source_target_pairs={{0,254},{1,37},{2,252},{3,39},{4,224},{5,41},{6,226},{7,43},{8,228... | collective-permute-start | bytes 245768 | tf_op jit(solution)/shard_map/ppermute | solution.py:293
  45.0 1.1 %collective-permute-start.16 = (bf16[40,1024]{1,0:T(8,128)(2,1)S(1)}, bf16[40,1024]{1,0:T(8,128)(2,1)S(1)}, u32[]{:S(2)}, u32[]{:S(2)}) collective-permute-start(bf16[40,1024]{1,0:T(8,128)(2,1)S(1)} %get-tuple-element.74), channel_id=1, source_target_pairs={{0,30},{1,5},{2,28},{3,7},{4,0},{5,9},{6,2},{7,11},{8,4},{9,13},{1... | collective-permute-start | bytes 245768 | tf_op jit(solution)/shard_map/ppermute | solution.py:293
  46.1 1.5 %collective-permute-done.17.other = bf16[80,1024]{1,0:T(8,128)(2,1)S(1)} collective-permute-done((bf16[80,1024]{1,0:T(8,128)(2,1)S(1)}, bf16[80,1024]{1,0:T(8,128)(2,1)S(1)}, u32[]{:S(2)}, u32[]{:S(2)}) %collective-permute-start.17) | collective-permute-done | bytes 163872 | tf_op jit(solution)/shard_map/ppermute | solution.py:293
  47.7 3.3 %collective-permute-done.15.p0 = bf16[40,1024]{1,0:T(8,128)(2,1)S(1)} collective-permute-done((bf16[40,1024]{1,0:T(8,128)(2,1)S(1)}, bf16[40,1024]{1,0:T(8,128)(2,1)S(1)}, u32[]{:S(2)}, u32[]{:S(2)}) %collective-permute-start.15) | collective-permute-done | bytes 81952 | tf_op jit(solution)/shard_map/ppermute | solution.py:293
  51.0 0.9 %collective-permute-done.16.p1 = bf16[40,1024]{1,0:T(8,128)(2,1)S(1)} collective-permute-done((bf16[40,1024]{1,0:T(8,128)(2,1)S(1)}, bf16[40,1024]{1,0:T(8,128)(2,1)S(1)}, u32[]{:S(2)}, u32[]{:S(2)}) %collective-permute-start.16) | collective-permute-done | bytes 81952 | tf_op jit(solution)/shard_map/ppermute | solution.py:293
  51.9 0.5 collective-permute-done.18.p0
  52.4 4.9 %collective-permute-start.20 = (bf16[80,1024]{1,0:T(8,128)(2,1)S(1)}, bf16[80,1024]{1,0:T(8,128)(2,1)S(1)}, u32[]{:S(2)}, u32[]{:S(2)}) collective-permute-start(bf16[80,1024]{1,0:T(8,128)(2,1)S(1)} %shard_map.94.m1), channel_id=1, source_target_pairs={{0,1},{1,0},{2,3},{3,2},{4,5},{5,4},{6,7},{7,6},{8,9},{9,8},{10,11... | collective-permute-start | bytes 491528 | tf_op jit(solution)/shard_map/ppermute | solution.py:293
  57.4 0.9 %collective-permute-done.20.s1 = bf16[80,1024]{1,0:T(8,128)(2,1)S(1)} collective-permute-done((bf16[80,1024]{1,0:T(8,128)(2,1)S(1)}, bf16[80,1024]{1,0:T(8,128)(2,1)S(1)}, u32[]{:S(2)}, u32[]{:S(2)}) %collective-permute-start.20) | collective-permute-done | bytes 163872 | tf_op jit(solution)/shard_map/ppermute | solution.py:293
  58.3 0.4 collective-permute-done.19.s0
  58.7 1.3 %shard_map.95 = bf16[72,4,1024]{2,1,0:T(4,128)(2,1)} custom-call(bf16[80,1024]{1,0:T(8,128)(2,1)S(1)} %shard_map.92.m0, bf16[80,1024]{1,0:T(8,128)(2,1)S(1)} %shard_map.94.m1, bf16[80,1024]{1,0:T(8,128)(2,1)S(1)} %collective-permute-done.19.s0, bf16[80,1024]{1,0:T(8,128)(2,1)S(1)} %collective-permute-done.20.s1), custom_call_target="tpu_custom_call" | custom-call | flops 200000000 | bytes 1245184 | tf_op jit(solution)/shard_map/pallas_call | solution.py:273
  (40 shorter events, 1.9 us)
Async XLA Ops:
  0.0 5.5 %copy-start.5 = (bf16[1024,3,256]{2,0,1:T(8,128)(2,1)S(1)}, bf16[1024,3,256]{2,0,1:T(8,128)(2,1)}, u32[]{:S(2)}) copy-start(bf16[1024,3,256]{2,0,1:T(8,128)(2,1)} %param.9) | copy-start | bytes 4718596
  0.0 5.5 %copy-start.6 = (bf16[4,6,12,1024]{3,0,2,1:T(4,128)(2,1)S(1)}, bf16[4,6,12,1024]{3,0,2,1:T(4,128)(2,1)}, u32[]{:S(2)}) copy-start(bf16[4,6,12,1024]{3,0,2,1:T(4,128)(2,1)} %param.8) | copy-start | bytes 1769476
  0.0 8.0 %collective-permute-start.2 = (bf16[3,1024,256]{2,1,0:T(8,128)(2,1)}, bf16[3,1024,256]{2,1,0:T(8,128)(2,1)S(1)}, u32[]{:S(2)}, u32[]{:S(2)}) collective-permute-start(bf16[3,1024,256]{2,1,0:T(8,128)(2,1)} %bitcast.8), channel_id=1, source_target_pairs={{0,1},{1,0},{2,3},{3,2},{4,5},{5,4},{6,7},{7,6},{8,9},{9,8},{10,11... | collective-permute-start | bytes 4718600 | tf_op jit(solution)/shard_map/ppermute | solution.py:293
  3.2 4.7 %collective-permute-start = (bf16[256,1024]{1,0:T(8,128)(2,1)}, bf16[256,1024]{1,0:T(8,128)(2,1)S(1)}, u32[]{:S(2)}, u32[]{:S(2)}) collective-permute-start(bf16[256,1024]{1,0:T(8,128)(2,1)} %w0.1), channel_id=1, source_target_pairs={{0,1},{1,0},{2,3},{3,2},{4,5},{5,4},{6,7},{7,6},{8,9},{9,8},{10,11... | collective-permute-start | bytes 1572872 | tf_op jit(solution)/shard_map/ppermute | solution.py:293
  3.2 4.8 %collective-permute-start.1 = (bf16[256,1024]{1,0:T(8,128)(2,1)}, bf16[256,1024]{1,0:T(8,128)(2,1)S(1)}, u32[]{:S(2)}, u32[]{:S(2)}) collective-permute-start(bf16[256,1024]{1,0:T(8,128)(2,1)} %o_own.1), channel_id=1, source_target_pairs={{0,1},{1,0},{2,3},{3,2},{4,5},{5,4},{6,7},{7,6},{8,9},{9,8},{10,11... | collective-permute-start | bytes 1572872 | tf_op jit(solution)/shard_map/ppermute | solution.py:293
  3.8 0.7 %copy-start.7 = (f32[2,4,37]{2,1,0:T(4,128)S(1)}, f32[2,4,37]{2,1,0:T(4,128)}, u32[]{:S(2)}) copy-start(f32[2,4,37]{2,1,0:T(4,128)} %table.1) | copy-start | bytes 3556
  5.3 4.1 %copy-start.4 = (bf16[256,1024]{1,0:T(8,128)(2,1)S(1)}, bf16[256,1024]{1,0:T(8,128)(2,1)}, u32[]{:S(2)}) copy-start(bf16[256,1024]{1,0:T(8,128)(2,1)} %w0.1) | copy-start | bytes 1572868
  5.3 2.7 %collective-permute-start.3 = (bf16[32,256]{1,0:T(8,128)(2,1)S(1)}, bf16[32,256]{1,0:T(8,128)(2,1)S(1)}, u32[]{:S(2)}, u32[]{:S(2)}) collective-permute-start(bf16[32,256]{1,0:T(8,128)(2,1)S(1)} %get-tuple-element.46.b_own), channel_id=1, source_target_pairs={{0,1},{1,0},{2,3},{3,2},{4,5},{5,4},{6,7},{7,6},{8,9},{9,8},{10,11... | collective-permute-start | bytes 49160 | tf_op jit(solution)/shard_map/ppermute | solution.py:293
  5.5 5.8 %copy-start = (bf16[1024,1024]{1,0:T(8,128)(2,1)S(1)}, bf16[1024,1024]{1,0:T(8,128)(2,1)}, u32[]{:S(2)}) copy-start(bf16[1024,1024]{1,0:T(8,128)(2,1)} %u0.3) | copy-start | bytes 6291460
  5.5 6.7 %copy-start.1 = (bf16[1024,1024]{1,0:T(8,128)(2,1)S(1)}, bf16[1024,1024]{1,0:T(8,128)(2,1)}, u32[]{:S(2)}) copy-start(bf16[1024,1024]{1,0:T(8,128)(2,1)} %d0.3) | copy-start | bytes 6291460
  8.0 1.3 %collective-permute-start.4 = (bf16[160,256]{1,0:T(8,128)(2,1)S(1)}, bf16[160,256]{1,0:T(8,128)(2,1)S(1)}, u32[]{:S(2)}, u32[]{:S(2)}) collective-permute-start(bf16[160,256]{1,0:T(8,128)(2,1)S(1)} %get-tuple-element.48), channel_id=1, source_target_pairs={{0,1},{1,0},{2,3},{3,2},{4,5},{5,4},{6,7},{7,6},{8,9},{9,8},{10,11... | collective-permute-start | bytes 245768 | tf_op jit(solution)/shard_map/ppermute | solution.py:293
  9.7 5.5 %collective-permute-start.5 = (bf16[80,1024]{1,0:T(8,128)(2,1)S(1)}, bf16[80,1024]{1,0:T(8,128)(2,1)S(1)}, u32[]{:S(2)}, u32[]{:S(2)}) collective-permute-start(bf16[80,1024]{1,0:T(8,128)(2,1)S(1)} %get-tuple-element.51.mine), channel_id=1, source_target_pairs={{0,2},{1,3},{2,0},{3,1},{4,6},{5,7},{6,4},{7,5},{8,10},{9,11},{10,... | collective-permute-start | bytes 491528 | tf_op jit(solution)/shard_map/ppermute | solution.py:293
  9.8 14.5 %collective-permute-start.8 = (bf16[80,1024]{1,0:T(8,128)(2,1)S(1)}, bf16[80,1024]{1,0:T(8,128)(2,1)S(1)}, u32[]{:S(2)}, u32[]{:S(2)}) collective-permute-start(bf16[80,1024]{1,0:T(8,128)(2,1)S(1)} %get-tuple-element.58.mine), channel_id=1, source_target_pairs={{0,2},{1,3},{2,0},{3,1},{4,6},{5,7},{6,4},{7,5},{8,10},{9,11},{10,... | collective-permute-start | bytes 491528 | tf_op jit(solution)/shard_map/ppermute | solution.py:293
  11.3 24.8 %collective-permute-start.11 = (bf16[1024,1024]{1,0:T(8,128)(2,1)S(1)}, bf16[1024,1024]{1,0:T(8,128)(2,1)S(1)}, u32[]{:S(2)}, u32[]{:S(2)}) collective-permute-start(bf16[1024,1024]{1,0:T(8,128)(2,1)S(1)} %copy-done), channel_id=1, source_target_pairs={{0,1},{1,0},{2,3},{3,2},{4,5},{5,4},{6,7},{7,6},{8,9},{9,8},{10,11... | collective-permute-start | bytes 6291464 | tf_op jit(solution)/shard_map/ppermute | solution.py:293
  12.2 23.9 %collective-permute-start.12 = (bf16[1024,1024]{1,0:T(8,128)(2,1)S(1)}, bf16[1024,1024]{1,0:T(8,128)(2,1)S(1)}, u32[]{:S(2)}, u32[]{:S(2)}) collective-permute-start(bf16[1024,1024]{1,0:T(8,128)(2,1)S(1)} %copy-done.1), channel_id=1, source_target_pairs={{0,1},{1,0},{2,3},{3,2},{4,5},{5,4},{6,7},{7,6},{8,9},{9,8},{10,11... | collective-permute-start | bytes 6291464 | tf_op jit(solution)/shard_map/ppermute | solution.py:293
  15.3 10.1 %collective-permute-start.6 = (bf16[40,1024]{1,0:T(8,128)(2,1)S(1)}, bf16[40,1024]{1,0:T(8,128)(2,1)S(1)}, u32[]{:S(2)}, u32[]{:S(2)}) collective-permute-start(bf16[40,1024]{1,0:T(8,128)(2,1)S(1)} %get-tuple-element.56), channel_id=1, source_target_pairs={{0,36},{1,255},{2,38},{3,253},{4,40},{5,225},{6,42},{7,227},{8,44}... | collective-permute-start | bytes 245768 | tf_op jit(solution)/shard_map/ppermute | solution.py:293
  23.9 3.6 %collective-permute-start.7 = (bf16[40,1024]{1,0:T(8,128)(2,1)S(1)}, bf16[40,1024]{1,0:T(8,128)(2,1)S(1)}, u32[]{:S(2)}, u32[]{:S(2)}) collective-permute-start(bf16[40,1024]{1,0:T(8,128)(2,1)S(1)} %get-tuple-element.57), channel_id=1, source_target_pairs={{0,4},{1,31},{2,6},{3,29},{4,8},{5,1},{6,10},{7,3},{8,12},{9,5},{1... | collective-permute-start | bytes 245768 | tf_op jit(solution)/shard_map/ppermute | solution.py:293
  24.4 3.7 %copy-start.2 = (bf16[1024,3,256]{2,0,1:T(8,128)(2,1)S(1)}, bf16[1024,3,256]{2,0,1:T(8,128)(2,1)}, u32[]{:S(2)}) copy-start(bf16[1024,3,256]{2,0,1:T(8,128)(2,1)} %param.10) | copy-start | bytes 4718596
  24.4 3.7 %copy-start.3 = (bf16[256,1024]{1,0:T(8,128)(2,1)S(1)}, bf16[256,1024]{1,0:T(8,128)(2,1)}, u32[]{:S(2)}) copy-start(bf16[256,1024]{1,0:T(8,128)(2,1)} %o_own.1) | copy-start | bytes 1572868
  24.4 3.7 %collective-permute-start.9 = (bf16[40,1024]{1,0:T(8,128)(2,1)S(1)}, bf16[40,1024]{1,0:T(8,128)(2,1)S(1)}, u32[]{:S(2)}, u32[]{:S(2)}) collective-permute-start(bf16[40,1024]{1,0:T(8,128)(2,1)S(1)} %get-tuple-element.60), channel_id=1, source_target_pairs={{0,32},{1,225},{2,34},{3,227},{4,36},{5,229},{6,38},{7,231},{8,40}... | collective-permute-start | bytes 245768 | tf_op jit(solution)/shard_map/ppermute | solution.py:293
  30.9 5.2 %collective-permute-start.10 = (bf16[80,1024]{1,0:T(8,128)(2,1)S(1)}, bf16[80,1024]{1,0:T(8,128)(2,1)S(1)}, u32[]{:S(2)}, u32[]{:S(2)}) collective-permute-start(bf16[80,1024]{1,0:T(8,128)(2,1)S(1)} %get-tuple-element.65.mine), channel_id=1, source_target_pairs={{0,2},{1,3},{2,0},{3,1},{4,6},{5,7},{6,4},{7,5},{8,10},{9,11},{10,... | collective-permute-start | bytes 491528 | tf_op jit(solution)/shard_map/ppermute | solution.py:293
  31.0 8.6 %collective-permute-start.14 = (bf16[80,1024]{1,0:T(8,128)(2,1)S(1)}, bf16[80,1024]{1,0:T(8,128)(2,1)S(1)}, u32[]{:S(2)}, u32[]{:S(2)}) collective-permute-start(bf16[80,1024]{1,0:T(8,128)(2,1)S(1)} %get-tuple-element.72.mine), channel_id=1, source_target_pairs={{0,2},{1,3},{2,0},{3,1},{4,6},{5,7},{6,4},{7,5},{8,10},{9,11},{10,... | collective-permute-start | bytes 491528 | tf_op jit(solution)/shard_map/ppermute | solution.py:293
  37.9 4.3 %collective-permute-start.13 = (bf16[80,1024]{1,0:T(8,128)(2,1)S(1)}, bf16[80,1024]{1,0:T(8,128)(2,1)S(1)}, u32[]{:S(2)}, u32[]{:S(2)}) collective-permute-start(bf16[80,1024]{1,0:T(8,128)(2,1)S(1)} %shard_map.89.mine), channel_id=1, source_target_pairs={{0,2},{1,3},{2,0},{3,1},{4,6},{5,7},{6,4},{7,5},{8,10},{9,11},{10,... | collective-permute-start | bytes 491528 | tf_op jit(solution)/shard_map/ppermute | solution.py:293
  41.4 6.2 %collective-permute-start.17 = (bf16[80,1024]{1,0:T(8,128)(2,1)S(1)}, bf16[80,1024]{1,0:T(8,128)(2,1)S(1)}, u32[]{:S(2)}, u32[]{:S(2)}) collective-permute-start(bf16[80,1024]{1,0:T(8,128)(2,1)S(1)} %shard_map.91.mine), channel_id=1, source_target_pairs={{0,2},{1,3},{2,0},{3,1},{4,6},{5,7},{6,4},{7,5},{8,10},{9,11},{10,... | collective-permute-start | bytes 491528 | tf_op jit(solution)/shard_map/ppermute | solution.py:293
  42.2 8.8 %collective-permute-start.15 = (bf16[40,1024]{1,0:T(8,128)(2,1)S(1)}, bf16[40,1024]{1,0:T(8,128)(2,1)S(1)}, u32[]{:S(2)}, u32[]{:S(2)}) collective-permute-start(bf16[40,1024]{1,0:T(8,128)(2,1)S(1)} %get-tuple-element.73), channel_id=1, source_target_pairs={{0,254},{1,37},{2,252},{3,39},{4,224},{5,41},{6,226},{7,43},{8,228... | collective-permute-start | bytes 245768 | tf_op jit(solution)/shard_map/ppermute | solution.py:293
  45.0 6.8 %collective-permute-start.16 = (bf16[40,1024]{1,0:T(8,128)(2,1)S(1)}, bf16[40,1024]{1,0:T(8,128)(2,1)S(1)}, u32[]{:S(2)}, u32[]{:S(2)}) collective-permute-start(bf16[40,1024]{1,0:T(8,128)(2,1)S(1)} %get-tuple-element.74), channel_id=1, source_target_pairs={{0,30},{1,5},{2,28},{3,7},{4,0},{5,9},{6,2},{7,11},{8,4},{9,13},{1... | collective-permute-start | bytes 245768 | tf_op jit(solution)/shard_map/ppermute | solution.py:293
  47.6 4.7 %collective-permute-start.18 = (bf16[40,1024]{1,0:T(8,128)(2,1)S(1)}, bf16[40,1024]{1,0:T(8,128)(2,1)S(1)}, u32[]{:S(2)}, u32[]{:S(2)}) collective-permute-start(bf16[40,1024]{1,0:T(8,128)(2,1)S(1)} %get-tuple-element.76), channel_id=1, source_target_pairs={{0,224},{1,33},{2,226},{3,35},{4,228},{5,37},{6,230},{7,39},{8,232... | collective-permute-start | bytes 245768 | tf_op jit(solution)/shard_map/ppermute | solution.py:293
  52.4 6.0 %collective-permute-start.20 = (bf16[80,1024]{1,0:T(8,128)(2,1)S(1)}, bf16[80,1024]{1,0:T(8,128)(2,1)S(1)}, u32[]{:S(2)}, u32[]{:S(2)}) collective-permute-start(bf16[80,1024]{1,0:T(8,128)(2,1)S(1)} %shard_map.94.m1), channel_id=1, source_target_pairs={{0,1},{1,0},{2,3},{3,2},{4,5},{5,4},{6,7},{7,6},{8,9},{9,8},{10,11... | collective-permute-start | bytes 491528 | tf_op jit(solution)/shard_map/ppermute | solution.py:293
  57.3 1.4 %collective-permute-start.19 = (bf16[80,1024]{1,0:T(8,128)(2,1)S(1)}, bf16[80,1024]{1,0:T(8,128)(2,1)S(1)}, u32[]{:S(2)}, u32[]{:S(2)}) collective-permute-start(bf16[80,1024]{1,0:T(8,128)(2,1)S(1)} %shard_map.92.m0), channel_id=1, source_target_pairs={{0,1},{1,0},{2,3},{3,2},{4,5},{5,4},{6,7},{7,6},{8,9},{9,8},{10,11... | collective-permute-start | bytes 491528 | tf_op jit(solution)/shard_map/ppermute | solution.py:293

commit v9 on v7

--- a/solution.py
+++ b/solution.py
@@ -201,33 +201,52 @@
     out[...] = normalize(joined((p0, p1)))
 
 
-def second_kernel(xn_a, p2, p3, w_own, w_sib, o_own, o_sib, b_own, b_sib, *outs):
-    xn_b = normalize(joined((p2, p3))).astype(jnp.float32)
-    xn = jnp.concatenate([xn_a[...].astype(jnp.float32), xn_b], axis=0).astype(jnp.bfloat16)
+def shifted_features(half):
     quad, slot, level, row, col = kept_place(iota((KEPT, 1), 0))
     row, col = row + 3 * (quad & 1), col + 3 * (quad & 2)
     feat = features(level, row, col, slot < USED, KEPT)
-    lane = iota((KEPT, 128), 1)
+    rows = slice(half * HALF, (half + 1) * HALF)
+    level, row = level[rows], row[rows]
+    lane = iota((HALF, 128), 1)
     j = lane & (FEAT - 1)
     split_levels = core_index() == 1
     split_rows = lax.axis_index("lat") == 0
     ban_level = (j < WL) & (j != level)
     ban_row = (j >= F_Y) & (j < F_Y + WY) & ((j >= F_Y + SY) != (row >= SY))
     ban = jnp.where(ban_level, split_levels.astype(jnp.int32), jnp.where(ban_row, split_rows.astype(jnp.int32), 0))
-    ban = jnp.where((lane & FEAT) == 0, ban, 0) == 1
+    return feat, feat[rows], jnp.where((lane & FEAT) == 0, ban, 0) == 1
+
+
+def half_attention(half, xn, keys, values, weights, projections, biases):
+    feat, mine, ban = shifted_features(half)
     total = None
-    for weight, bias, project in ((w_own, b_own, o_own), (w_sib, b_sib, o_sib)):
-        q = (dot(xn, weight[0]) * HD**-0.5).astype(jnp.bfloat16)
-        k = dot(xn, weight[1]).astype(jnp.bfloat16)
-        v = dot(xn, weight[2]).astype(jnp.bfloat16)
+    for part in range(2):
+        q = (dot(xn, weights[part][0]) * HD**-0.5).astype(jnp.bfloat16)
         for pair in range(2):
             cols = slice(pair * 128, pair * 128 + 128)
-            extra = dot(feat[:, :FEAT], bias[:, cols])
+            extra = dot(mine[:, :FEAT], biases[part][:, cols])
             extra = jnp.where(ban, NEG, extra).astype(jnp.bfloat16)
-            mixed = pair_heads(q[:, cols], k[:, cols], v[:, cols], extra, feat)
-            term = dot(mixed, project[cols, :])
+            mixed = pair_heads(q[:, cols], keys[part][:, cols], values[part][:, cols], extra, feat)
+            term = dot(mixed, projections[part][cols, :])
             total = term if total is None else total + term
-    store_halves(total, outs)
+    return total.astype(jnp.bfloat16)
+
+
+def second_kernel(xn_a, p2, p3, w_own, w_sib, o_own, o_sib, b_own, b_sib, out, xn_out, k_out, v_out):
+    xn_b = normalize(joined((p2, p3)))
+    xn_out[...] = xn_b
+    xn = jnp.concatenate([xn_a[...], xn_b], axis=0)
+    keys, values = [], []
+    for part, weight in enumerate((w_own, w_sib)):
+        keys.append(dot(xn, weight[1]).astype(jnp.bfloat16))
+        values.append(dot(xn, weight[2]).astype(jnp.bfloat16))
+        k_out[part] = keys[part]
+        v_out[part] = values[part]
+    out[...] = half_attention(0, xn_a[...], keys, values, (w_own, w_sib), (o_own, o_sib), (b_own, b_sib))
+
+
+def rest_kernel(xn_b, keys, values, w_own, w_sib, o_own, o_sib, b_own, b_sib, out):
+    out[...] = half_attention(1, xn_b[...], keys, values, (w_own, w_sib), (o_own, o_sib), (b_own, b_sib))
 
 
 def gelu(x):
@@ -332,14 +351,12 @@
     lat = out_to(lat, 1, 0)
 
     xn_a = call(norm_kernel, half, (diag, lon), 10**10, 8)
-    part_a, part_b = call(
-        second_kernel,
-        half * 2,
-        (xn_a, lat, own, w_second, w_sib, out_second, s1, bias2, bias2_sib),
-        10**9,
-        16,
+    own_sib = (w_second, w_sib, out_second, s1, bias2, bias2_sib)
+    part_a, xn_b, keys, values = call(
+        second_kernel, half * 2 + [(2, KEPT, 256)] * 2, (xn_a, lat, own, *own_sib), 10**9, 16
     )
     other_a = chip_swap(part_a)
+    part_b = call(rest_kernel, half, (xn_b, keys, values, *own_sib), 10**10, 16)
     other_b = chip_swap(part_b)
     mlp = (up_weight, u1, down_weight, d1)
     part_a = call(mlp_kernel, half, (part_a, other_a, diag, lon, *mlp), 10**9, 20)

time: 58.7 us -> 59.4 us (1.012)
  Pallas kernels: 11.6 us -> 14 us
  waiting for transfers between devices: 20 us -> 18.5 us
    pallas_call x14 -> x15, Pallas kernels: 11.6 us -> 14 us  [call(): pl.pallas_call(kernel, out_shape=shapes, in_specs=[pl.BlockSpec(memory_sp...]
    ppermute x21, waiting for transfers between devices: 20 us -> 18.5 us  [move(): return lax.ppermute(value, AXES, pairs(counts, target))]
  transfers between devices with their start and end apart: 21 -> 21, of which waited for: 11 -> 12; matrix products, arithmetic and copies ran while one was open for 0% -> 0% of each run, Pallas kernels for 17% -> 21%
where the time goes in v9:
time: 59.4 us; the launch traced here: 59.3 us
  starting transfers between devices  25.9 us (44%)
  waiting for transfers between devices  18.5 us (31%)
  Pallas kernels  14 us (24%)
  local copies, waits for them, and re-layouts  0.72 us (1%)
    ppermute x21, starting transfers between devices, move(): return lax.ppermute(value, AXES, pairs(counts, target))  25.9 us
    ppermute x21, waiting for transfers between devices, move(): return lax.ppermute(value, AXES, pairs(counts, target))  18.5 us
    pallas_call x15, Pallas kernels, call(): pl.pallas_call(kernel, out_shape=shapes, in_specs=[pl.BlockSpec(memory_sp...  14 us
  transfers between devices with their start and end apart: 21, of which 12 were waited for; matrix products, arithmetic and copies ran while one was open for 0% of the time, Pallas kernels for 21%

profile of v9, /device:TPU:1, one launch (start us, length us, event | category | flops | bytes accessed | tf_op | source)
XLA Modules:
  0.0 59.3 jit_solution(6727729563977061551)
XLA Ops:
  0.0 3.2 %collective-permute-start.2 = (bf16[3,1024,256]{2,1,0:T(8,128)(2,1)}, bf16[3,1024,256]{2,1,0:T(8,128)(2,1)S(1)}, u32[]{:S(2)}, u32[]{:S(2)}) collective-permute-start(bf16[3,1024,256]{2,1,0:T(8,128)(2,1)} %bitcast.8), channel_id=1, source_target_pairs={{0,1},{1,0},{2,3},{3,2},{4,5},{5,4},{6,7},{7,6},{8,9},{9,8},{10,11... | collective-permute-start | bytes 4718600 | tf_op jit(solution)/shard_map/ppermute | solution.py:312
  3.2 0.5 collective-permute-start.1
  3.8 0.7 %copy-done.7 = f32[2,4,37]{2,1,0:T(4,128)S(1)} copy-done((f32[2,4,37]{2,1,0:T(4,128)S(1)}, f32[2,4,37]{2,1,0:T(4,128)}, u32[]{:S(2)}) %copy-start.7) | copy-done | bytes 1208
  4.4 0.8 %shard_map.82 = (bf16[32,256]{1,0:T(8,128)(2,1)S(1)}, bf16[32,256]{1,0:T(8,128)(2,1)S(1)}) custom-call(f32[2,4,37]{2,1,0:T(4,128)S(1)} %copy-done.7), custom_call_target="tpu_custom_call" | custom-call | flops 5000000000 | bytes 33952 | tf_op jit(solution)/shard_map/pallas_call | solution.py:292
  5.5 2.4 %shard_map.83 = (bf16[160,256]{1,0:T(8,128)(2,1)S(1)}, bf16[160,256]{1,0:T(8,128)(2,1)S(1)}, bf16[80,1024]{1,0:T(8,128)(2,1)S(1)}, bf16[80,1024]{1,0:T(8,128)(2,1)S(1)}) custom-call(bf16[72,4,1024]{2,1,0:T(4,128)(2,1)S(1)} %bitcast.12, bf16[3,1024,256]{2,1,0:T(8,128)(2,1)S(1)} %bitcast.11, bf16[32,256]{1,0:T(8,128)(2,1)S(1)} %get-tuple-element.45.bias), custom_call_target="tpu_custom_call" | custom-call | flops 1000000000 | bytes 2670592 | tf_op jit(solution)/shard_map/pallas_call | solution.py:292
  8.0 0.4 collective-permute-start.4
  8.4 0.9 %collective-permute-done.4.o1 = bf16[160,256]{1,0:T(8,128)(2,1)S(1)} collective-permute-done((bf16[160,256]{1,0:T(8,128)(2,1)S(1)}, bf16[160,256]{1,0:T(8,128)(2,1)S(1)}, u32[]{:S(2)}, u32[]{:S(2)}) %collective-permute-start.4) | collective-permute-done | bytes 81952 | tf_op jit(solution)/shard_map/ppermute | solution.py:312
  9.8 1.5 %collective-permute-start.8 = (bf16[80,1024]{1,0:T(8,128)(2,1)S(1)}, bf16[80,1024]{1,0:T(8,128)(2,1)S(1)}, u32[]{:S(2)}, u32[]{:S(2)}) collective-permute-start(bf16[80,1024]{1,0:T(8,128)(2,1)S(1)} %get-tuple-element.60.mine), channel_id=1, source_target_pairs={{0,2},{1,3},{2,0},{3,1},{4,6},{5,7},{6,4},{7,5},{8,10},{9,11},{10,... | collective-permute-start | bytes 491528 | tf_op jit(solution)/shard_map/ppermute | solution.py:312
  11.2 0.9 %collective-permute-start.11 = (bf16[1024,1024]{1,0:T(8,128)(2,1)S(1)}, bf16[1024,1024]{1,0:T(8,128)(2,1)S(1)}, u32[]{:S(2)}, u32[]{:S(2)}) collective-permute-start(bf16[1024,1024]{1,0:T(8,128)(2,1)S(1)} %copy-done), channel_id=1, source_target_pairs={{0,1},{1,0},{2,3},{3,2},{4,5},{5,4},{6,7},{7,6},{8,9},{9,8},{10,11... | collective-permute-start | bytes 6291464 | tf_op jit(solution)/shard_map/ppermute | solution.py:312
  12.2 2.9 %collective-permute-done.5.other = bf16[80,1024]{1,0:T(8,128)(2,1)S(1)} collective-permute-done((bf16[80,1024]{1,0:T(8,128)(2,1)S(1)}, bf16[80,1024]{1,0:T(8,128)(2,1)S(1)}, u32[]{:S(2)}, u32[]{:S(2)}) %collective-permute-start.5) | collective-permute-done | bytes 163872 | tf_op jit(solution)/shard_map/ppermute | solution.py:312
  15.3 1.0 %collective-permute-start.6 = (bf16[40,1024]{1,0:T(8,128)(2,1)S(1)}, bf16[40,1024]{1,0:T(8,128)(2,1)S(1)}, u32[]{:S(2)}, u32[]{:S(2)}) collective-permute-start(bf16[40,1024]{1,0:T(8,128)(2,1)S(1)} %get-tuple-element.58), channel_id=1, source_target_pairs={{0,36},{1,37},{2,38},{3,39},{4,40},{5,41},{6,42},{7,43},{8,44},{9,... | collective-permute-start | bytes 245768 | tf_op jit(solution)/shard_map/ppermute | solution.py:312
  16.3 1.3 %collective-permute-start.7 = (bf16[40,1024]{1,0:T(8,128)(2,1)S(1)}, bf16[40,1024]{1,0:T(8,128)(2,1)S(1)}, u32[]{:S(2)}, u32[]{:S(2)}) collective-permute-start(bf16[40,1024]{1,0:T(8,128)(2,1)S(1)} %get-tuple-element.59), channel_id=1, source_target_pairs={{0,4},{1,5},{2,6},{3,7},{4,8},{5,9},{6,10},{7,11},{8,12},{9,13},{1... | collective-permute-start | bytes 245768 | tf_op jit(solution)/shard_map/ppermute | solution.py:312
  17.6 1.1 %collective-permute-done.8.other = bf16[80,1024]{1,0:T(8,128)(2,1)S(1)} collective-permute-done((bf16[80,1024]{1,0:T(8,128)(2,1)S(1)}, bf16[80,1024]{1,0:T(8,128)(2,1)S(1)}, u32[]{:S(2)}, u32[]{:S(2)}) %collective-permute-start.8) | collective-permute-done | bytes 163872 | tf_op jit(solution)/shard_map/ppermute | solution.py:312
  18.8 0.6 collective-permute-start.9
  19.4 6.4 %collective-permute-done.6.p0 = bf16[40,1024]{1,0:T(8,128)(2,1)S(1)} collective-permute-done((bf16[40,1024]{1,0:T(8,128)(2,1)S(1)}, bf16[40,1024]{1,0:T(8,128)(2,1)S(1)}, u32[]{:S(2)}, u32[]{:S(2)}) %collective-permute-start.6) | collective-permute-done | bytes 81952 | tf_op jit(solution)/shard_map/ppermute | solution.py:312
  26.0 2.7 %shard_map.88 = (bf16[80,1024]{1,0:T(8,128)(2,1)S(1)}, bf16[80,1024]{1,0:T(8,128)(2,1)S(1)}, bf16[2,160,256]{2,1,0:T(8,128)(2,1)S(1)}, bf16[2,160,256]{2,1,0:T(8,128)(2,1)S(1)}) custom-call(bf16[80,1024]{1,0:T(8,128)(2,1)S(1)} %shard_map.86.xn_a, bf16[40,1024]{1,0:T(8,128)(2,1)S(1)} %collective-permute-done.9.p2.p0, ...), custom_call_target="tpu_custom_call" | custom-call | flops 1000000000 | bytes 5210112 | tf_op jit(solution)/shard_map/pallas_call | solution.py:292
  29.1 2.3 %shard_map.90.mine = bf16[80,1024]{1,0:T(8,128)(2,1)S(1)} custom-call(bf16[80,1024]{1,0:T(8,128)(2,1)S(1)} %get-tuple-element.70.xn_b, bf16[2,160,256]{2,1,0:T(8,128)(2,1)S(1)} %get-tuple-element.71.keys, bf16[2,160,256]{2,1,0:T(8,128)(2,1)S(1)} %get-tuple-element.72.values, bf16[3,1024,256]{2,1,0:T(8,128)(2,1)S(1)} %bitcast.10, ...), custom_call_target="tpu_custom_call" | custom-call | flops 10000000000 | bytes 4882432 | tf_op jit(solution)/shard_map/pallas_call | solution.py:292
  31.4 1.5 %collective-permute-start.14 = (bf16[80,1024]{1,0:T(8,128)(2,1)S(1)}, bf16[80,1024]{1,0:T(8,128)(2,1)S(1)}, u32[]{:S(2)}, u32[]{:S(2)}) collective-permute-start(bf16[80,1024]{1,0:T(8,128)(2,1)S(1)} %shard_map.90.mine), channel_id=1, source_target_pairs={{0,2},{1,3},{2,0},{3,1},{4,6},{5,7},{6,4},{7,5},{8,10},{9,11},{10,... | collective-permute-start | bytes 491528 | tf_op jit(solution)/shard_map/ppermute | solution.py:312
  33.2 1.8 %shard_map.89.mine = bf16[80,1024]{1,0:T(8,128)(2,1)S(1)} custom-call(bf16[80,1024]{1,0:T(8,128)(2,1)S(1)} %get-tuple-element.67.mine, bf16[80,1024]{1,0:T(8,128)(2,1)S(1)} %collective-permute-done.10.other, bf16[40,1024]{1,0:T(8,128)(2,1)S(1)} %collective-permute-done.6.p0, bf16[40,1024]{1,0:T(8,128)(2,1)S(1)} %collective-permute-done.7.p1, ...), custom_call_target="tpu_custom_call" | custom-call | flops 1000000000 | bytes 9043968 | tf_op jit(solution)/shard_map/pallas_call | solution.py:292
  35.2 1.9 %collective-permute-done.14.other = bf16[80,1024]{1,0:T(8,128)(2,1)S(1)} collective-permute-done((bf16[80,1024]{1,0:T(8,128)(2,1)S(1)}, bf16[80,1024]{1,0:T(8,128)(2,1)S(1)}, u32[]{:S(2)}, u32[]{:S(2)}) %collective-permute-start.14) | collective-permute-done | bytes 163872 | tf_op jit(solution)/shard_map/ppermute | solution.py:312
  37.1 1.8 %shard_map.92.mine = bf16[80,1024]{1,0:T(8,128)(2,1)S(1)} custom-call(bf16[80,1024]{1,0:T(8,128)(2,1)S(1)} %shard_map.90.mine, bf16[80,1024]{1,0:T(8,128)(2,1)S(1)} %collective-permute-done.14.other, bf16[40,1024]{1,0:T(8,128)(2,1)S(1)} %collective-permute-done.9.p2.p0, bf16[40,1024]{1,0:T(8,128)(2,1)S(1)} %get-tuple-element.63.p3.p1, ...), custom_call_target="tpu_custom_call" | custom-call | flops 1000000000 | bytes 9043968 | tf_op jit(solution)/shard_map/pallas_call | solution.py:292
  38.9 1.1 %collective-permute-start.17 = (bf16[80,1024]{1,0:T(8,128)(2,1)S(1)}, bf16[80,1024]{1,0:T(8,128)(2,1)S(1)}, u32[]{:S(2)}, u32[]{:S(2)}) collective-permute-start(bf16[80,1024]{1,0:T(8,128)(2,1)S(1)} %shard_map.92.mine), channel_id=1, source_target_pairs={{0,2},{1,3},{2,0},{3,1},{4,6},{5,7},{6,4},{7,5},{8,10},{9,11},{10,... | collective-permute-start | bytes 491528 | tf_op jit(solution)/shard_map/ppermute | solution.py:312
  40.0 1.1 %collective-permute-done.13.other = bf16[80,1024]{1,0:T(8,128)(2,1)S(1)} collective-permute-done((bf16[80,1024]{1,0:T(8,128)(2,1)S(1)}, bf16[80,1024]{1,0:T(8,128)(2,1)S(1)}, u32[]{:S(2)}, u32[]{:S(2)}) %collective-permute-start.13) | collective-permute-done | bytes 163872 | tf_op jit(solution)/shard_map/ppermute | solution.py:312
  41.1 5.0 %collective-permute-start.15 = (bf16[40,1024]{1,0:T(8,128)(2,1)S(1)}, bf16[40,1024]{1,0:T(8,128)(2,1)S(1)}, u32[]{:S(2)}, u32[]{:S(2)}) collective-permute-start(bf16[40,1024]{1,0:T(8,128)(2,1)S(1)} %get-tuple-element.77), channel_id=1, source_target_pairs={{0,254},{1,255},{2,252},{3,253},{4,224},{5,225},{6,226},{7,227},{8... | collective-permute-start | bytes 245768 | tf_op jit(solution)/shard_map/ppermute | solution.py:312
  46.1 0.4 collective-permute-start.16
  46.5 1.2 %collective-permute-start.18 = (bf16[40,1024]{1,0:T(8,128)(2,1)S(1)}, bf16[40,1024]{1,0:T(8,128)(2,1)S(1)}, u32[]{:S(2)}, u32[]{:S(2)}) collective-permute-start(bf16[40,1024]{1,0:T(8,128)(2,1)S(1)} %get-tuple-element.80), channel_id=1, source_target_pairs={{0,224},{1,225},{2,226},{3,227},{4,228},{5,229},{6,230},{7,231},{8... | collective-permute-start | bytes 245768 | tf_op jit(solution)/shard_map/ppermute | solution.py:312
  47.8 1.6 %collective-permute-done.16.p1 = bf16[40,1024]{1,0:T(8,128)(2,1)S(1)} collective-permute-done((bf16[40,1024]{1,0:T(8,128)(2,1)S(1)}, bf16[40,1024]{1,0:T(8,128)(2,1)S(1)}, u32[]{:S(2)}, u32[]{:S(2)}) %collective-permute-start.16) | collective-permute-done | bytes 81952 | tf_op jit(solution)/shard_map/ppermute | solution.py:312
  49.4 0.8 %collective-permute-done.18.p0 = bf16[40,1024]{1,0:T(8,128)(2,1)S(1)} collective-permute-done((bf16[40,1024]{1,0:T(8,128)(2,1)S(1)}, bf16[40,1024]{1,0:T(8,128)(2,1)S(1)}, u32[]{:S(2)}, u32[]{:S(2)}) %collective-permute-start.18) | collective-permute-done | bytes 81952 | tf_op jit(solution)/shard_map/ppermute | solution.py:312
  50.2 6.4 %collective-permute-start.20 = (bf16[80,1024]{1,0:T(8,128)(2,1)S(1)}, bf16[80,1024]{1,0:T(8,128)(2,1)S(1)}, u32[]{:S(2)}, u32[]{:S(2)}) collective-permute-start(bf16[80,1024]{1,0:T(8,128)(2,1)S(1)} %shard_map.95.m1), channel_id=1, source_target_pairs={{0,1},{1,0},{2,3},{3,2},{4,5},{5,4},{6,7},{7,6},{8,9},{9,8},{10,11... | collective-permute-start | bytes 491528 | tf_op jit(solution)/shard_map/ppermute | solution.py:312
  56.7 0.9 %collective-permute-done.20.s1 = bf16[80,1024]{1,0:T(8,128)(2,1)S(1)} collective-permute-done((bf16[80,1024]{1,0:T(8,128)(2,1)S(1)}, bf16[80,1024]{1,0:T(8,128)(2,1)S(1)}, u32[]{:S(2)}, u32[]{:S(2)}) %collective-permute-start.20) | collective-permute-done | bytes 163872 | tf_op jit(solution)/shard_map/ppermute | solution.py:312
  57.6 0.4 collective-permute-done.19.s0
  58.0 1.3 %shard_map.96 = bf16[72,4,1024]{2,1,0:T(4,128)(2,1)} custom-call(bf16[80,1024]{1,0:T(8,128)(2,1)S(1)} %shard_map.93.m0, bf16[80,1024]{1,0:T(8,128)(2,1)S(1)} %shard_map.95.m1, bf16[80,1024]{1,0:T(8,128)(2,1)S(1)} %collective-permute-done.19.s0, bf16[80,1024]{1,0:T(8,128)(2,1)S(1)} %collective-permute-done.20.s1), custom_call_target="tpu_custom_call" | custom-call | flops 200000000 | bytes 1245184 | tf_op jit(solution)/shard_map/pallas_call | solution.py:292
  (41 shorter events, 2.2 us)
Async XLA Ops:
  0.0 5.5 %copy-start.5 = (bf16[1024,3,256]{2,0,1:T(8,128)(2,1)S(1)}, bf16[1024,3,256]{2,0,1:T(8,128)(2,1)}, u32[]{:S(2)}) copy-start(bf16[1024,3,256]{2,0,1:T(8,128)(2,1)} %param.9) | copy-start | bytes 4718596
  0.0 5.5 %copy-start.6 = (bf16[4,6,12,1024]{3,0,2,1:T(4,128)(2,1)S(1)}, bf16[4,6,12,1024]{3,0,2,1:T(4,128)(2,1)}, u32[]{:S(2)}) copy-start(bf16[4,6,12,1024]{3,0,2,1:T(4,128)(2,1)} %param.8) | copy-start | bytes 1769476
  0.0 8.0 %collective-permute-start.2 = (bf16[3,1024,256]{2,1,0:T(8,128)(2,1)}, bf16[3,1024,256]{2,1,0:T(8,128)(2,1)S(1)}, u32[]{:S(2)}, u32[]{:S(2)}) collective-permute-start(bf16[3,1024,256]{2,1,0:T(8,128)(2,1)} %bitcast.8), channel_id=1, source_target_pairs={{0,1},{1,0},{2,3},{3,2},{4,5},{5,4},{6,7},{7,6},{8,9},{9,8},{10,11... | collective-permute-start | bytes 4718600 | tf_op jit(solution)/shard_map/ppermute | solution.py:312
  3.2 4.7 %collective-permute-start = (bf16[256,1024]{1,0:T(8,128)(2,1)}, bf16[256,1024]{1,0:T(8,128)(2,1)S(1)}, u32[]{:S(2)}, u32[]{:S(2)}) collective-permute-start(bf16[256,1024]{1,0:T(8,128)(2,1)} %w0.1), channel_id=1, source_target_pairs={{0,1},{1,0},{2,3},{3,2},{4,5},{5,4},{6,7},{7,6},{8,9},{9,8},{10,11... | collective-permute-start | bytes 1572872 | tf_op jit(solution)/shard_map/ppermute | solution.py:312
  3.2 4.8 %collective-permute-start.1 = (bf16[256,1024]{1,0:T(8,128)(2,1)}, bf16[256,1024]{1,0:T(8,128)(2,1)S(1)}, u32[]{:S(2)}, u32[]{:S(2)}) collective-permute-start(bf16[256,1024]{1,0:T(8,128)(2,1)} %o_own.3), channel_id=1, source_target_pairs={{0,1},{1,0},{2,3},{3,2},{4,5},{5,4},{6,7},{7,6},{8,9},{9,8},{10,11... | collective-permute-start | bytes 1572872 | tf_op jit(solution)/shard_map/ppermute | solution.py:312
  3.8 0.7 %copy-start.7 = (f32[2,4,37]{2,1,0:T(4,128)S(1)}, f32[2,4,37]{2,1,0:T(4,128)}, u32[]{:S(2)}) copy-start(f32[2,4,37]{2,1,0:T(4,128)} %table.1) | copy-start | bytes 3556
  5.3 4.1 %copy-start.4 = (bf16[256,1024]{1,0:T(8,128)(2,1)S(1)}, bf16[256,1024]{1,0:T(8,128)(2,1)}, u32[]{:S(2)}) copy-start(bf16[256,1024]{1,0:T(8,128)(2,1)} %w0.1) | copy-start | bytes 1572868
  5.3 2.6 %collective-permute-start.3 = (bf16[32,256]{1,0:T(8,128)(2,1)S(1)}, bf16[32,256]{1,0:T(8,128)(2,1)S(1)}, u32[]{:S(2)}, u32[]{:S(2)}) collective-permute-start(bf16[32,256]{1,0:T(8,128)(2,1)S(1)} %get-tuple-element.48.b_own), channel_id=1, source_target_pairs={{0,1},{1,0},{2,3},{3,2},{4,5},{5,4},{6,7},{7,6},{8,9},{9,8},{10,11... | collective-permute-start | bytes 49160 | tf_op jit(solution)/shard_map/ppermute | solution.py:312
  5.5 5.7 %copy-start = (bf16[1024,1024]{1,0:T(8,128)(2,1)S(1)}, bf16[1024,1024]{1,0:T(8,128)(2,1)}, u32[]{:S(2)}) copy-start(bf16[1024,1024]{1,0:T(8,128)(2,1)} %u0.3) | copy-start | bytes 6291460
  5.5 6.7 %copy-start.1 = (bf16[1024,1024]{1,0:T(8,128)(2,1)S(1)}, bf16[1024,1024]{1,0:T(8,128)(2,1)}, u32[]{:S(2)}) copy-start(bf16[1024,1024]{1,0:T(8,128)(2,1)} %d0.3) | copy-start | bytes 6291460
  8.0 1.3 %collective-permute-start.4 = (bf16[160,256]{1,0:T(8,128)(2,1)S(1)}, bf16[160,256]{1,0:T(8,128)(2,1)S(1)}, u32[]{:S(2)}, u32[]{:S(2)}) collective-permute-start(bf16[160,256]{1,0:T(8,128)(2,1)S(1)} %get-tuple-element.50), channel_id=1, source_target_pairs={{0,1},{1,0},{2,3},{3,2},{4,5},{5,4},{6,7},{7,6},{8,9},{9,8},{10,11... | collective-permute-start | bytes 245768 | tf_op jit(solution)/shard_map/ppermute | solution.py:312
  9.7 5.5 %collective-permute-start.5 = (bf16[80,1024]{1,0:T(8,128)(2,1)S(1)}, bf16[80,1024]{1,0:T(8,128)(2,1)S(1)}, u32[]{:S(2)}, u32[]{:S(2)}) collective-permute-start(bf16[80,1024]{1,0:T(8,128)(2,1)S(1)} %get-tuple-element.53.mine), channel_id=1, source_target_pairs={{0,2},{1,3},{2,0},{3,1},{4,6},{5,7},{6,4},{7,5},{8,10},{9,11},{10,... | collective-permute-start | bytes 491528 | tf_op jit(solution)/shard_map/ppermute | solution.py:312
  9.8 8.9 %collective-permute-start.8 = (bf16[80,1024]{1,0:T(8,128)(2,1)S(1)}, bf16[80,1024]{1,0:T(8,128)(2,1)S(1)}, u32[]{:S(2)}, u32[]{:S(2)}) collective-permute-start(bf16[80,1024]{1,0:T(8,128)(2,1)S(1)} %get-tuple-element.60.mine), channel_id=1, source_target_pairs={{0,2},{1,3},{2,0},{3,1},{4,6},{5,7},{6,4},{7,5},{8,10},{9,11},{10,... | collective-permute-start | bytes 491528 | tf_op jit(solution)/shard_map/ppermute | solution.py:312
  11.2 22.0 %collective-permute-start.11 = (bf16[1024,1024]{1,0:T(8,128)(2,1)S(1)}, bf16[1024,1024]{1,0:T(8,128)(2,1)S(1)}, u32[]{:S(2)}, u32[]{:S(2)}) collective-permute-start(bf16[1024,1024]{1,0:T(8,128)(2,1)S(1)} %copy-done), channel_id=1, source_target_pairs={{0,1},{1,0},{2,3},{3,2},{4,5},{5,4},{6,7},{7,6},{8,9},{9,8},{10,11... | collective-permute-start | bytes 6291464 | tf_op jit(solution)/shard_map/ppermute | solution.py:312
  12.1 21.1 %collective-permute-start.12 = (bf16[1024,1024]{1,0:T(8,128)(2,1)S(1)}, bf16[1024,1024]{1,0:T(8,128)(2,1)S(1)}, u32[]{:S(2)}, u32[]{:S(2)}) collective-permute-start(bf16[1024,1024]{1,0:T(8,128)(2,1)S(1)} %copy-done.1), channel_id=1, source_target_pairs={{0,1},{1,0},{2,3},{3,2},{4,5},{5,4},{6,7},{7,6},{8,9},{9,8},{10,11... | collective-permute-start | bytes 6291464 | tf_op jit(solution)/shard_map/ppermute | solution.py:312
  15.3 10.5 %collective-permute-start.6 = (bf16[40,1024]{1,0:T(8,128)(2,1)S(1)}, bf16[40,1024]{1,0:T(8,128)(2,1)S(1)}, u32[]{:S(2)}, u32[]{:S(2)}) collective-permute-start(bf16[40,1024]{1,0:T(8,128)(2,1)S(1)} %get-tuple-element.58), channel_id=1, source_target_pairs={{0,36},{1,37},{2,38},{3,39},{4,40},{5,41},{6,42},{7,43},{8,44},{9,... | collective-permute-start | bytes 245768 | tf_op jit(solution)/shard_map/ppermute | solution.py:312
  16.3 9.5 %collective-permute-start.7 = (bf16[40,1024]{1,0:T(8,128)(2,1)S(1)}, bf16[40,1024]{1,0:T(8,128)(2,1)S(1)}, u32[]{:S(2)}, u32[]{:S(2)}) collective-permute-start(bf16[40,1024]{1,0:T(8,128)(2,1)S(1)} %get-tuple-element.59), channel_id=1, source_target_pairs={{0,4},{1,5},{2,6},{3,7},{4,8},{5,9},{6,10},{7,11},{8,12},{9,13},{1... | collective-permute-start | bytes 245768 | tf_op jit(solution)/shard_map/ppermute | solution.py:312
  18.8 7.2 %copy-start.2 = (bf16[1024,3,256]{2,0,1:T(8,128)(2,1)S(1)}, bf16[1024,3,256]{2,0,1:T(8,128)(2,1)}, u32[]{:S(2)}) copy-start(bf16[1024,3,256]{2,0,1:T(8,128)(2,1)} %param.10) | copy-start | bytes 4718596
  18.8 7.2 %copy-start.3 = (bf16[256,1024]{1,0:T(8,128)(2,1)S(1)}, bf16[256,1024]{1,0:T(8,128)(2,1)}, u32[]{:S(2)}) copy-start(bf16[256,1024]{1,0:T(8,128)(2,1)} %o_own.3) | copy-start | bytes 1572868
  18.8 7.2 %collective-permute-start.9 = (bf16[40,1024]{1,0:T(8,128)(2,1)S(1)}, bf16[40,1024]{1,0:T(8,128)(2,1)S(1)}, u32[]{:S(2)}, u32[]{:S(2)}) collective-permute-start(bf16[40,1024]{1,0:T(8,128)(2,1)S(1)} %get-tuple-element.62), channel_id=1, source_target_pairs={{0,32},{1,33},{2,34},{3,35},{4,36},{5,37},{6,38},{7,39},{8,40},{9,... | collective-permute-start | bytes 245768 | tf_op jit(solution)/shard_map/ppermute | solution.py:312
  28.8 4.4 %collective-permute-start.10 = (bf16[80,1024]{1,0:T(8,128)(2,1)S(1)}, bf16[80,1024]{1,0:T(8,128)(2,1)S(1)}, u32[]{:S(2)}, u32[]{:S(2)}) collective-permute-start(bf16[80,1024]{1,0:T(8,128)(2,1)S(1)} %get-tuple-element.67.mine), channel_id=1, source_target_pairs={{0,2},{1,3},{2,0},{3,1},{4,6},{5,7},{6,4},{7,5},{8,10},{9,11},{10,... | collective-permute-start | bytes 491528 | tf_op jit(solution)/shard_map/ppermute | solution.py:312
  31.4 5.6 %collective-permute-start.14 = (bf16[80,1024]{1,0:T(8,128)(2,1)S(1)}, bf16[80,1024]{1,0:T(8,128)(2,1)S(1)}, u32[]{:S(2)}, u32[]{:S(2)}) collective-permute-start(bf16[80,1024]{1,0:T(8,128)(2,1)S(1)} %shard_map.90.mine), channel_id=1, source_target_pairs={{0,2},{1,3},{2,0},{3,1},{4,6},{5,7},{6,4},{7,5},{8,10},{9,11},{10,... | collective-permute-start | bytes 491528 | tf_op jit(solution)/shard_map/ppermute | solution.py:312
  35.0 6.1 %collective-permute-start.13 = (bf16[80,1024]{1,0:T(8,128)(2,1)S(1)}, bf16[80,1024]{1,0:T(8,128)(2,1)S(1)}, u32[]{:S(2)}, u32[]{:S(2)}) collective-permute-start(bf16[80,1024]{1,0:T(8,128)(2,1)S(1)} %shard_map.89.mine), channel_id=1, source_target_pairs={{0,2},{1,3},{2,0},{3,1},{4,6},{5,7},{6,4},{7,5},{8,10},{9,11},{10,... | collective-permute-start | bytes 491528 | tf_op jit(solution)/shard_map/ppermute | solution.py:312
  38.9 7.6 %collective-permute-start.17 = (bf16[80,1024]{1,0:T(8,128)(2,1)S(1)}, bf16[80,1024]{1,0:T(8,128)(2,1)S(1)}, u32[]{:S(2)}, u32[]{:S(2)}) collective-permute-start(bf16[80,1024]{1,0:T(8,128)(2,1)S(1)} %shard_map.92.mine), channel_id=1, source_target_pairs={{0,2},{1,3},{2,0},{3,1},{4,6},{5,7},{6,4},{7,5},{8,10},{9,11},{10,... | collective-permute-start | bytes 491528 | tf_op jit(solution)/shard_map/ppermute | solution.py:312
  41.1 6.6 %collective-permute-start.15 = (bf16[40,1024]{1,0:T(8,128)(2,1)S(1)}, bf16[40,1024]{1,0:T(8,128)(2,1)S(1)}, u32[]{:S(2)}, u32[]{:S(2)}) collective-permute-start(bf16[40,1024]{1,0:T(8,128)(2,1)S(1)} %get-tuple-element.77), channel_id=1, source_target_pairs={{0,254},{1,255},{2,252},{3,253},{4,224},{5,225},{6,226},{7,227},{8... | collective-permute-start | bytes 245768 | tf_op jit(solution)/shard_map/ppermute | solution.py:312
  46.1 3.3 %collective-permute-start.16 = (bf16[40,1024]{1,0:T(8,128)(2,1)S(1)}, bf16[40,1024]{1,0:T(8,128)(2,1)S(1)}, u32[]{:S(2)}, u32[]{:S(2)}) collective-permute-start(bf16[40,1024]{1,0:T(8,128)(2,1)S(1)} %get-tuple-element.78), channel_id=1, source_target_pairs={{0,30},{1,31},{2,28},{3,29},{4,0},{5,1},{6,2},{7,3},{8,4},{9,5},{1... | collective-permute-start | bytes 245768 | tf_op jit(solution)/shard_map/ppermute | solution.py:312
  46.5 3.7 %collective-permute-start.18 = (bf16[40,1024]{1,0:T(8,128)(2,1)S(1)}, bf16[40,1024]{1,0:T(8,128)(2,1)S(1)}, u32[]{:S(2)}, u32[]{:S(2)}) collective-permute-start(bf16[40,1024]{1,0:T(8,128)(2,1)S(1)} %get-tuple-element.80), channel_id=1, source_target_pairs={{0,224},{1,225},{2,226},{3,227},{4,228},{5,229},{6,230},{7,231},{8... | collective-permute-start | bytes 245768 | tf_op jit(solution)/shard_map/ppermute | solution.py:312
  50.2 7.4 %collective-permute-start.20 = (bf16[80,1024]{1,0:T(8,128)(2,1)S(1)}, bf16[80,1024]{1,0:T(8,128)(2,1)S(1)}, u32[]{:S(2)}, u32[]{:S(2)}) collective-permute-start(bf16[80,1024]{1,0:T(8,128)(2,1)S(1)} %shard_map.95.m1), channel_id=1, source_target_pairs={{0,1},{1,0},{2,3},{3,2},{4,5},{5,4},{6,7},{7,6},{8,9},{9,8},{10,11... | collective-permute-start | bytes 491528 | tf_op jit(solution)/shard_map/ppermute | solution.py:312
  56.6 1.4 %collective-permute-start.19 = (bf16[80,1024]{1,0:T(8,128)(2,1)S(1)}, bf16[80,1024]{1,0:T(8,128)(2,1)S(1)}, u32[]{:S(2)}, u32[]{:S(2)}) collective-permute-start(bf16[80,1024]{1,0:T(8,128)(2,1)S(1)} %shard_map.93.m0), channel_id=1, source_target_pairs={{0,1},{1,0},{2,3},{3,2},{4,5},{5,4},{6,7},{7,6},{8,9},{9,8},{10,11... | collective-permute-start | bytes 491528 | tf_op jit(solution)/shard_map/ppermute | solution.py:312

commit v10 on v6

--- a/solution.py
+++ b/solution.py
@@ -120,17 +120,30 @@
     return one_hot(jnp.where(used, jnp.where(hit, 1, 0), jnp.where(j == F_PAD, 1, 0)) == 1)
 
 
-def pair_heads(query, key, value, extra, key_feat):
-    count = query.shape[0]
-    low = iota(query.shape, 1) < HD
-    none = jnp.zeros_like(query)
-    upper = jnp.concatenate([jnp.where(low, query, none), jnp.where(low, none, extra)], axis=1)
-    lower = jnp.concatenate([jnp.where(low, none, query), jnp.where(low, extra, none)], axis=1)
-    scores = dot_t(jnp.concatenate([upper, lower], axis=0), jnp.concatenate([key, key_feat], axis=1))
-    expo = jnp.exp(scores - jnp.max(scores, axis=-1, keepdims=True))
-    scale = 1.0 / jnp.sum(expo, axis=-1, keepdims=True)
-    mixed = dot(expo.astype(jnp.bfloat16), value) * scale
-    return jnp.where(low, mixed[:count], mixed[count:]).astype(jnp.bfloat16)
+def attend(parts, key_feat):
+    low = iota(parts[0][0].shape, 1) < HD
+    none = jnp.zeros_like(parts[0][0])
+    count = none.shape[0]
+    scores = []
+    for query, key, _, extra in parts:
+        upper = jnp.concatenate([jnp.where(low, query, none), jnp.where(low, none, extra)], axis=1)
+        lower = jnp.concatenate([jnp.where(low, none, query), jnp.where(low, extra, none)], axis=1)
+        both = jnp.concatenate([upper, lower], axis=0)
+        scores.append(dot_t(both, jnp.concatenate([key, key_feat], axis=1)))
+    expos, scales = [], []
+    for score in scores:
+        expo = jnp.exp(score - jnp.max(score, axis=-1, keepdims=True))
+        expos.append(expo.astype(jnp.bfloat16))
+        scales.append(1.0 / jnp.sum(expo, axis=-1, keepdims=True))
+    results = []
+    for (_, _, value, _), expo, scale in zip(parts, expos, scales):
+        mixed = dot(expo, value) * scale
+        results.append(jnp.where(low, mixed[:count], mixed[count:]).astype(jnp.bfloat16))
+    return results
+
+
+def pair_cols(pair):
+    return slice(pair * 128, pair * 128 + 128)
 
 
 def first_kernel(tokens, weight, bias, keep, give, *bases):
@@ -149,16 +162,16 @@
     rest = index - 72 * level
     row = (rest * 171) >> 11
     feat = features(level, row, rest - 12 * row, index >= 0, WINDOW)
+    extra = dot(feat[:, :FEAT], bias[...]).astype(jnp.bfloat16)
     parts = []
-    for pair in range(2):
-        cols = slice(pair * 128, pair * 128 + 128)
-        extra = dot(feat[:, :FEAT], bias[:, cols]).astype(jnp.bfloat16)
-        halves = []
-        for w in range(2):
-            rows = slice(w * WINDOW, (w + 1) * WINDOW)
-            halves.append(pair_heads(q[rows, cols], k[rows, cols], v[rows, cols], extra, feat))
-        parts.append(jnp.concatenate(halves, axis=0))
-    mixed = jnp.concatenate(parts, axis=1)
+    for w in range(2):
+        rows = slice(w * WINDOW, (w + 1) * WINDOW)
+        for pair in range(2):
+            cols = pair_cols(pair)
+            parts.append((q[rows, cols], k[rows, cols], v[rows, cols], extra[:, cols]))
+    heads = attend(parts, feat)
+    windows = [jnp.concatenate(heads[2 * w : 2 * w + 2], axis=1) for w in range(2)]
+    mixed = jnp.concatenate(windows, axis=0)
     quad, slot, level, row, col = kept_place(iota((KEPT, 1), 0))
     row, col = patch_place(quad, row, col)
     lanes = iota((KEPT, PATCH), 1)
@@ -215,19 +228,20 @@
     ban_row = (j >= F_Y) & (j < F_Y + WY) & ((j >= F_Y + SY) != (row >= SY))
     ban = jnp.where(ban_level, split_levels.astype(jnp.int32), jnp.where(ban_row, split_rows.astype(jnp.int32), 0))
     ban = jnp.where((lane & FEAT) == 0, ban, 0) == 1
-    total = None
-    for weight, bias, project in ((w_own, b_own, o_own), (w_sib, b_sib, o_sib)):
+    parts = []
+    for weight, bias in ((w_own, b_own), (w_sib, b_sib)):
         q = (dot(xn, weight[0]) * HD**-0.5).astype(jnp.bfloat16)
         k = dot(xn, weight[1]).astype(jnp.bfloat16)
         v = dot(xn, weight[2]).astype(jnp.bfloat16)
+        extra = dot(feat[:, :FEAT], bias[...])
         for pair in range(2):
-            cols = slice(pair * 128, pair * 128 + 128)
-            extra = dot(feat[:, :FEAT], bias[:, cols])
-            extra = jnp.where(ban, NEG, extra).astype(jnp.bfloat16)
-            mixed = pair_heads(q[:, cols], k[:, cols], v[:, cols], extra, feat)
-            term = dot(mixed, project[cols, :])
-            total = term if total is None else total + term
-    store_halves(total, outs)
+            cols = pair_cols(pair)
+            parts.append((q[:, cols], k[:, cols], v[:, cols], jnp.where(ban, NEG, extra[:, cols]).astype(jnp.bfloat16)))
+    heads = attend(parts, feat)
+    total = dot(jnp.concatenate(heads[:2], axis=1), o_own[...])
+    total = total + dot(jnp.concatenate(heads[2:], axis=1), o_sib[...])
+    outs[0][...] = total[ROWS : 3 * ROWS].astype(jnp.bfloat16)
+    outs[1][...] = jnp.concatenate([total[:ROWS], total[3 * ROWS :]], axis=0).astype(jnp.bfloat16)
 
 
 def gelu(x):
@@ -255,7 +269,8 @@
 
 def place_kernel(m0, m1, s0, s1, out):
     core = core_index()
-    quad, slot, level, row, col = kept_place(iota((1, KEPT), 1))
+    piece, slot, level, row, col = kept_place(iota((1, KEPT), 1))
+    quad = jnp.where(piece < 2, piece + 1, jnp.where(piece == 2, 0, piece))
     row, col = patch_place(quad, row, col)
     total = None
     for chosen, parts in ((core, (m0, m1)), (1 - core, (s0, s1))):
@@ -342,19 +357,20 @@
     other_a = chip_swap(part_a)
     other_b = chip_swap(part_b)
     mlp = (up_weight, u1, down_weight, d1)
-    part_a = call(mlp_kernel, half, (part_a, other_a, diag, lon, *mlp), 10**9, 20)
+    part_a = call(mlp_kernel, half, (part_a, other_a, lon, lat, *mlp), 10**9, 20)
     part_a, part_b = tied(part_a, part_b)
     other_a = chip_swap(part_a)
-    part_b = call(mlp_kernel, half, (part_b, other_b, lat, own, *mlp), 10**9, 20)
+    part_b = call(mlp_kernel, half, (part_b, other_b, diag, own, *mlp), 10**9, 20)
     other_b = chip_swap(part_b)
-    diag, lon = call(sum_kernel, piece * 2, (part_a, other_a), 10**6, 8)
-    diag, lon, part_b = tied(diag, lon, part_b)
+    lon, lat = call(sum_kernel, piece * 2, (part_a, other_a), 10**6, 8)
+    lon, lat, part_b = tied(lon, lat, part_b)
+    lon = home(lon, 0, 1)
+    lat = home(lat, 1, 0)
+    diag, own = call(sum_kernel, piece * 2, (part_b, other_b), 10**10, 8)
     diag = home(diag, 1, 1)
-    lon = home(lon, 0, 1)
-    lat, own = call(sum_kernel, piece * 2, (part_b, other_b), 10**10, 8)
-    lat = home(lat, 1, 0)
-    mine_a = call(join_kernel, half, (diag, lon), 10**10, 8)
-    mine_b = call(join_kernel, half, (lat, own), 10**6, 8)
+    mine_a = call(join_kernel, half, (lon, lat), 10**10, 8)
+    mine_a, diag, own = tied(mine_a, diag, own)
+    mine_b = call(join_kernel, half, (diag, own), 10**6, 8)
     result = call(
         place_kernel,
         [(rows * cols, levels, width)],

time: 60.7 us -> 57.7 us (0.951)
  starting transfers between devices: 29.3 us -> 25.5 us
  waiting for transfers between devices: 18.7 us -> 20.8 us
  Pallas kernels: 11.6 us -> 10.4 us
    ppermute x21, starting transfers between devices: 29.3 us -> 25.5 us  [move(): return lax.ppermute(value, AXES, pairs(counts, target))]
    ppermute x21, waiting for transfers between devices: 18.7 us -> 20.8 us  [move(): return lax.ppermute(value, AXES, pairs(counts, target))]
    pallas_call x14, Pallas kernels: 11.6 us -> 10.4 us  [call(): pl.pallas_call(kernel, out_shape=shapes, in_specs=[pl.BlockSpec(memory_sp...]
  transfers between devices with their start and end apart: 21 -> 21, of which waited for: 10 -> 11; matrix products, arithmetic and copies ran while one was open for 0% -> 0% of each run, Pallas kernels for 16% -> 15%
where the time goes in v10:
time: 57.7 us; the launch traced here: 57.5 us
  starting transfers between devices  25.5 us (44%)
  waiting for transfers between devices  20.8 us (36%)
  Pallas kernels  10.4 us (18%)
  local copies, waits for them, and re-layouts  0.72 us (1%)
    ppermute x21, starting transfers between devices, move(): return lax.ppermute(value, AXES, pairs(counts, target))  25.5 us
    ppermute x21, waiting for transfers between devices, move(): return lax.ppermute(value, AXES, pairs(counts, target))  20.8 us
    pallas_call x14, Pallas kernels, call(): pl.pallas_call(kernel, out_shape=shapes, in_specs=[pl.BlockSpec(memory_sp...  10.4 us
  transfers between devices with their start and end apart: 21, of which 11 were waited for; matrix products, arithmetic and copies ran while one was open for 0% of the time, Pallas kernels for 15%

profile of v10, /device:TPU:1, one launch (start us, length us, event | category | flops | bytes accessed | tf_op | source)
XLA Modules:
  0.0 57.5 jit_solution(8998244862473092169)
XLA Ops:
  0.0 3.2 %collective-permute-start.2 = (bf16[3,1024,256]{2,1,0:T(8,128)(2,1)}, bf16[3,1024,256]{2,1,0:T(8,128)(2,1)S(1)}, u32[]{:S(2)}, u32[]{:S(2)}) collective-permute-start(bf16[3,1024,256]{2,1,0:T(8,128)(2,1)} %bitcast.8), channel_id=1, source_target_pairs={{0,1},{1,0},{2,3},{3,2},{4,5},{5,4},{6,7},{7,6},{8,9},{9,8},{10,11... | collective-permute-start | bytes 4718600 | tf_op jit(solution)/shard_map/ppermute | solution.py:308
  3.2 0.5 collective-permute-start.1
  3.8 0.7 %copy-done.7 = f32[2,4,37]{2,1,0:T(4,128)S(1)} copy-done((f32[2,4,37]{2,1,0:T(4,128)S(1)}, f32[2,4,37]{2,1,0:T(4,128)}, u32[]{:S(2)}) %copy-start.7) | copy-done | bytes 1208
  4.4 0.8 %shard_map.82 = (bf16[32,256]{1,0:T(8,128)(2,1)S(1)}, bf16[32,256]{1,0:T(8,128)(2,1)S(1)}) custom-call(f32[2,4,37]{2,1,0:T(4,128)S(1)} %copy-done.7), custom_call_target="tpu_custom_call" | custom-call | flops 5000000000 | bytes 33952 | tf_op jit(solution)/shard_map/pallas_call | solution.py:288
  5.5 2.3 %shard_map.83 = (bf16[160,256]{1,0:T(8,128)(2,1)S(1)}, bf16[160,256]{1,0:T(8,128)(2,1)S(1)}, bf16[80,1024]{1,0:T(8,128)(2,1)S(1)}, bf16[80,1024]{1,0:T(8,128)(2,1)S(1)}) custom-call(bf16[72,4,1024]{2,1,0:T(4,128)(2,1)S(1)} %bitcast.11, bf16[3,1024,256]{2,1,0:T(8,128)(2,1)S(1)} %bitcast.10, bf16[32,256]{1,0:T(8,128)(2,1)S(1)} %get-tuple-element.43.bias), custom_call_target="tpu_custom_call" | custom-call | flops 1000000000 | bytes 2670592 | tf_op jit(solution)/shard_map/pallas_call | solution.py:288
  8.0 0.4 collective-permute-start.4
  8.4 0.9 %collective-permute-done.4.o1 = bf16[160,256]{1,0:T(8,128)(2,1)S(1)} collective-permute-done((bf16[160,256]{1,0:T(8,128)(2,1)S(1)}, bf16[160,256]{1,0:T(8,128)(2,1)S(1)}, u32[]{:S(2)}, u32[]{:S(2)}) %collective-permute-start.4) | collective-permute-done | bytes 81952 | tf_op jit(solution)/shard_map/ppermute | solution.py:308
  9.3 0.3 shard_map.84
  9.8 1.5 %collective-permute-start.8 = (bf16[80,1024]{1,0:T(8,128)(2,1)S(1)}, bf16[80,1024]{1,0:T(8,128)(2,1)S(1)}, u32[]{:S(2)}, u32[]{:S(2)}) collective-permute-start(bf16[80,1024]{1,0:T(8,128)(2,1)S(1)} %get-tuple-element.58.mine), channel_id=1, source_target_pairs={{0,2},{1,3},{2,0},{3,1},{4,6},{5,7},{6,4},{7,5},{8,10},{9,11},{10,... | collective-permute-start | bytes 491528 | tf_op jit(solution)/shard_map/ppermute | solution.py:308
  11.2 0.9 %collective-permute-start.11 = (bf16[1024,1024]{1,0:T(8,128)(2,1)S(1)}, bf16[1024,1024]{1,0:T(8,128)(2,1)S(1)}, u32[]{:S(2)}, u32[]{:S(2)}) collective-permute-start(bf16[1024,1024]{1,0:T(8,128)(2,1)S(1)} %copy-done), channel_id=1, source_target_pairs={{0,1},{1,0},{2,3},{3,2},{4,5},{5,4},{6,7},{7,6},{8,9},{9,8},{10,11... | collective-permute-start | bytes 6291464 | tf_op jit(solution)/shard_map/ppermute | solution.py:308
  12.2 3.0 %collective-permute-done.5.other = bf16[80,1024]{1,0:T(8,128)(2,1)S(1)} collective-permute-done((bf16[80,1024]{1,0:T(8,128)(2,1)S(1)}, bf16[80,1024]{1,0:T(8,128)(2,1)S(1)}, u32[]{:S(2)}, u32[]{:S(2)}) %collective-permute-start.5) | collective-permute-done | bytes 163872 | tf_op jit(solution)/shard_map/ppermute | solution.py:308
  15.3 1.0 %collective-permute-start.6 = (bf16[40,1024]{1,0:T(8,128)(2,1)S(1)}, bf16[40,1024]{1,0:T(8,128)(2,1)S(1)}, u32[]{:S(2)}, u32[]{:S(2)}) collective-permute-start(bf16[40,1024]{1,0:T(8,128)(2,1)S(1)} %get-tuple-element.56), channel_id=1, source_target_pairs={{0,36},{1,37},{2,38},{3,39},{4,40},{5,41},{6,42},{7,43},{8,44},{9,... | collective-permute-start | bytes 245768 | tf_op jit(solution)/shard_map/ppermute | solution.py:308
  16.3 1.3 %collective-permute-start.7 = (bf16[40,1024]{1,0:T(8,128)(2,1)S(1)}, bf16[40,1024]{1,0:T(8,128)(2,1)S(1)}, u32[]{:S(2)}, u32[]{:S(2)}) collective-permute-start(bf16[40,1024]{1,0:T(8,128)(2,1)S(1)} %get-tuple-element.57), channel_id=1, source_target_pairs={{0,4},{1,5},{2,6},{3,7},{4,8},{5,9},{6,10},{7,11},{8,12},{9,13},{1... | collective-permute-start | bytes 245768 | tf_op jit(solution)/shard_map/ppermute | solution.py:308
  17.6 1.1 %collective-permute-done.8.other = bf16[80,1024]{1,0:T(8,128)(2,1)S(1)} collective-permute-done((bf16[80,1024]{1,0:T(8,128)(2,1)S(1)}, bf16[80,1024]{1,0:T(8,128)(2,1)S(1)}, u32[]{:S(2)}, u32[]{:S(2)}) %collective-permute-start.8) | collective-permute-done | bytes 163872 | tf_op jit(solution)/shard_map/ppermute | solution.py:308
  18.8 0.6 %collective-permute-start.9 = (bf16[40,1024]{1,0:T(8,128)(2,1)S(1)}, bf16[40,1024]{1,0:T(8,128)(2,1)S(1)}, u32[]{:S(2)}, u32[]{:S(2)}) collective-permute-start(bf16[40,1024]{1,0:T(8,128)(2,1)S(1)} %get-tuple-element.60), channel_id=1, source_target_pairs={{0,32},{1,33},{2,34},{3,35},{4,36},{5,37},{6,38},{7,39},{8,40},{9,... | collective-permute-start | bytes 245768 | tf_op jit(solution)/shard_map/ppermute | solution.py:308
  19.4 6.4 %collective-permute-done.6.p0 = bf16[40,1024]{1,0:T(8,128)(2,1)S(1)} collective-permute-done((bf16[40,1024]{1,0:T(8,128)(2,1)S(1)}, bf16[40,1024]{1,0:T(8,128)(2,1)S(1)}, u32[]{:S(2)}, u32[]{:S(2)}) %collective-permute-start.6) | collective-permute-done | bytes 81952 | tf_op jit(solution)/shard_map/ppermute | solution.py:308
  26.0 1.6 %shard_map.88 = (bf16[80,1024]{1,0:T(8,128)(2,1)S(1)}, bf16[80,1024]{1,0:T(8,128)(2,1)S(1)}) custom-call(bf16[80,1024]{1,0:T(8,128)(2,1)S(1)} %shard_map.86.xn_a, bf16[40,1024]{1,0:T(8,128)(2,1)S(1)} %collective-permute-done.9.p2.p1, bf16[40,1024]{1,0:T(8,128)(2,1)S(1)} %get-tuple-element.61.p3.p1, bf16[3,1024,256]{2,1,0:T(8,128)(2,1)S(1)} %bitcast.9, ...), custom_call_target="tpu_custom_call" | custom-call | flops 1000000000 | bytes 4882432 | tf_op jit(solution)/shard_map/pallas_call | solution.py:288
  27.7 1.4 %collective-permute-start.14 = (bf16[80,1024]{1,0:T(8,128)(2,1)S(1)}, bf16[80,1024]{1,0:T(8,128)(2,1)S(1)}, u32[]{:S(2)}, u32[]{:S(2)}) collective-permute-start(bf16[80,1024]{1,0:T(8,128)(2,1)S(1)} %get-tuple-element.72.mine), channel_id=1, source_target_pairs={{0,2},{1,3},{2,0},{3,1},{4,6},{5,7},{6,4},{7,5},{8,10},{9,11},{10,... | collective-permute-start | bytes 491528 | tf_op jit(solution)/shard_map/ppermute | solution.py:308
  29.2 2.7 %collective-permute-done.10.other = bf16[80,1024]{1,0:T(8,128)(2,1)S(1)} collective-permute-done((bf16[80,1024]{1,0:T(8,128)(2,1)S(1)}, bf16[80,1024]{1,0:T(8,128)(2,1)S(1)}, u32[]{:S(2)}, u32[]{:S(2)}) %collective-permute-start.10) | collective-permute-done | bytes 163872 | tf_op jit(solution)/shard_map/ppermute | solution.py:308
  31.9 1.8 %shard_map.89.mine = bf16[80,1024]{1,0:T(8,128)(2,1)S(1)} custom-call(bf16[80,1024]{1,0:T(8,128)(2,1)S(1)} %get-tuple-element.65.mine, bf16[80,1024]{1,0:T(8,128)(2,1)S(1)} %collective-permute-done.10.other, bf16[40,1024]{1,0:T(8,128)(2,1)S(1)} %collective-permute-done.7.p1.p0, bf16[40,1024]{1,0:T(8,128)(2,1)S(1)} %collective-permute-done.9.p2.p1, ...), custom_call_target="tpu_custom_call" | custom-call | flops 1000000000 | bytes 9043968 | tf_op jit(solution)/shard_map/pallas_call | solution.py:288
  33.8 0.4 collective-permute-done.14.other
  34.2 1.8 %shard_map.91.mine = bf16[80,1024]{1,0:T(8,128)(2,1)S(1)} custom-call(bf16[80,1024]{1,0:T(8,128)(2,1)S(1)} %get-tuple-element.72.mine, bf16[80,1024]{1,0:T(8,128)(2,1)S(1)} %collective-permute-done.14.other, bf16[40,1024]{1,0:T(8,128)(2,1)S(1)} %collective-permute-done.6.p0, bf16[40,1024]{1,0:T(8,128)(2,1)S(1)} %get-tuple-element.61.p3.p1, ...), custom_call_target="tpu_custom_call" | custom-call | flops 1000000000 | bytes 9043968 | tf_op jit(solution)/shard_map/pallas_call | solution.py:288
  36.0 1.2 %collective-permute-start.17 = (bf16[80,1024]{1,0:T(8,128)(2,1)S(1)}, bf16[80,1024]{1,0:T(8,128)(2,1)S(1)}, u32[]{:S(2)}, u32[]{:S(2)}) collective-permute-start(bf16[80,1024]{1,0:T(8,128)(2,1)S(1)} %shard_map.91.mine), channel_id=1, source_target_pairs={{0,2},{1,3},{2,0},{3,1},{4,6},{5,7},{6,4},{7,5},{8,10},{9,11},{10,... | collective-permute-start | bytes 491528 | tf_op jit(solution)/shard_map/ppermute | solution.py:308
  37.1 1.7 %collective-permute-done.13.other = bf16[80,1024]{1,0:T(8,128)(2,1)S(1)} collective-permute-done((bf16[80,1024]{1,0:T(8,128)(2,1)S(1)}, bf16[80,1024]{1,0:T(8,128)(2,1)S(1)}, u32[]{:S(2)}, u32[]{:S(2)}) %collective-permute-start.13) | collective-permute-done | bytes 163872 | tf_op jit(solution)/shard_map/ppermute | solution.py:308
  38.9 3.5 %collective-permute-start.15 = (bf16[40,1024]{1,0:T(8,128)(2,1)S(1)}, bf16[40,1024]{1,0:T(8,128)(2,1)S(1)}, u32[]{:S(2)}, u32[]{:S(2)}) collective-permute-start(bf16[40,1024]{1,0:T(8,128)(2,1)S(1)} %get-tuple-element.73), channel_id=1, source_target_pairs={{0,30},{1,31},{2,28},{3,29},{4,0},{5,1},{6,2},{7,3},{8,4},{9,5},{1... | collective-permute-start | bytes 245768 | tf_op jit(solution)/shard_map/ppermute | solution.py:308
  42.5 1.8 %collective-permute-start.16 = (bf16[40,1024]{1,0:T(8,128)(2,1)S(1)}, bf16[40,1024]{1,0:T(8,128)(2,1)S(1)}, u32[]{:S(2)}, u32[]{:S(2)}) collective-permute-start(bf16[40,1024]{1,0:T(8,128)(2,1)S(1)} %get-tuple-element.74), channel_id=1, source_target_pairs={{0,224},{1,225},{2,226},{3,227},{4,228},{5,229},{6,230},{7,231},{8... | collective-permute-start | bytes 245768 | tf_op jit(solution)/shard_map/ppermute | solution.py:308
  44.3 2.0 %collective-permute-start.18 = (bf16[40,1024]{1,0:T(8,128)(2,1)S(1)}, bf16[40,1024]{1,0:T(8,128)(2,1)S(1)}, u32[]{:S(2)}, u32[]{:S(2)}) collective-permute-start(bf16[40,1024]{1,0:T(8,128)(2,1)S(1)} %get-tuple-element.76), channel_id=1, source_target_pairs={{0,254},{1,255},{2,252},{3,253},{4,224},{5,225},{6,226},{7,227},{8... | collective-permute-start | bytes 245768 | tf_op jit(solution)/shard_map/ppermute | solution.py:308
  46.3 3.0 %collective-permute-done.18.p0 = bf16[40,1024]{1,0:T(8,128)(2,1)S(1)} collective-permute-done((bf16[40,1024]{1,0:T(8,128)(2,1)S(1)}, bf16[40,1024]{1,0:T(8,128)(2,1)S(1)}, u32[]{:S(2)}, u32[]{:S(2)}) %collective-permute-start.18) | collective-permute-done | bytes 81952 | tf_op jit(solution)/shard_map/ppermute | solution.py:308
  49.3 5.5 %collective-permute-start.20 = (bf16[80,1024]{1,0:T(8,128)(2,1)S(1)}, bf16[80,1024]{1,0:T(8,128)(2,1)S(1)}, u32[]{:S(2)}, u32[]{:S(2)}) collective-permute-start(bf16[80,1024]{1,0:T(8,128)(2,1)S(1)} %shard_map.94.m1), channel_id=1, source_target_pairs={{0,1},{1,0},{2,3},{3,2},{4,5},{5,4},{6,7},{7,6},{8,9},{9,8},{10,11... | collective-permute-start | bytes 491528 | tf_op jit(solution)/shard_map/ppermute | solution.py:308
  54.9 0.9 %collective-permute-done.20.s1 = bf16[80,1024]{1,0:T(8,128)(2,1)S(1)} collective-permute-done((bf16[80,1024]{1,0:T(8,128)(2,1)S(1)}, bf16[80,1024]{1,0:T(8,128)(2,1)S(1)}, u32[]{:S(2)}, u32[]{:S(2)}) %collective-permute-start.20) | collective-permute-done | bytes 163872 | tf_op jit(solution)/shard_map/ppermute | solution.py:308
  55.9 0.4 collective-permute-done.19.s0
  56.2 1.3 %shard_map.95 = bf16[72,4,1024]{2,1,0:T(4,128)(2,1)} custom-call(bf16[80,1024]{1,0:T(8,128)(2,1)S(1)} %shard_map.92.m0, bf16[80,1024]{1,0:T(8,128)(2,1)S(1)} %shard_map.94.m1, bf16[80,1024]{1,0:T(8,128)(2,1)S(1)} %collective-permute-done.19.s0, bf16[80,1024]{1,0:T(8,128)(2,1)S(1)} %collective-permute-done.20.s1), custom_call_target="tpu_custom_call" | custom-call | flops 200000000 | bytes 1245184 | tf_op jit(solution)/shard_map/pallas_call | solution.py:288
  (40 shorter events, 1.5 us)
Async XLA Ops:
  0.0 5.5 %copy-start.5 = (bf16[1024,3,256]{2,0,1:T(8,128)(2,1)S(1)}, bf16[1024,3,256]{2,0,1:T(8,128)(2,1)}, u32[]{:S(2)}) copy-start(bf16[1024,3,256]{2,0,1:T(8,128)(2,1)} %param.9) | copy-start | bytes 4718596
  0.0 5.5 %copy-start.6 = (bf16[4,6,12,1024]{3,0,2,1:T(4,128)(2,1)S(1)}, bf16[4,6,12,1024]{3,0,2,1:T(4,128)(2,1)}, u32[]{:S(2)}) copy-start(bf16[4,6,12,1024]{3,0,2,1:T(4,128)(2,1)} %param.8) | copy-start | bytes 1769476
  0.0 8.0 %collective-permute-start.2 = (bf16[3,1024,256]{2,1,0:T(8,128)(2,1)}, bf16[3,1024,256]{2,1,0:T(8,128)(2,1)S(1)}, u32[]{:S(2)}, u32[]{:S(2)}) collective-permute-start(bf16[3,1024,256]{2,1,0:T(8,128)(2,1)} %bitcast.8), channel_id=1, source_target_pairs={{0,1},{1,0},{2,3},{3,2},{4,5},{5,4},{6,7},{7,6},{8,9},{9,8},{10,11... | collective-permute-start | bytes 4718600 | tf_op jit(solution)/shard_map/ppermute | solution.py:308
  3.2 4.5 %collective-permute-start = (bf16[256,1024]{1,0:T(8,128)(2,1)}, bf16[256,1024]{1,0:T(8,128)(2,1)S(1)}, u32[]{:S(2)}, u32[]{:S(2)}) collective-permute-start(bf16[256,1024]{1,0:T(8,128)(2,1)} %w0.1), channel_id=1, source_target_pairs={{0,1},{1,0},{2,3},{3,2},{4,5},{5,4},{6,7},{7,6},{8,9},{9,8},{10,11... | collective-permute-start | bytes 1572872 | tf_op jit(solution)/shard_map/ppermute | solution.py:308
  3.2 4.8 %collective-permute-start.1 = (bf16[256,1024]{1,0:T(8,128)(2,1)}, bf16[256,1024]{1,0:T(8,128)(2,1)S(1)}, u32[]{:S(2)}, u32[]{:S(2)}) collective-permute-start(bf16[256,1024]{1,0:T(8,128)(2,1)} %o_own.1), channel_id=1, source_target_pairs={{0,1},{1,0},{2,3},{3,2},{4,5},{5,4},{6,7},{7,6},{8,9},{9,8},{10,11... | collective-permute-start | bytes 1572872 | tf_op jit(solution)/shard_map/ppermute | solution.py:308
  3.8 0.7 %copy-start.7 = (f32[2,4,37]{2,1,0:T(4,128)S(1)}, f32[2,4,37]{2,1,0:T(4,128)}, u32[]{:S(2)}) copy-start(f32[2,4,37]{2,1,0:T(4,128)} %table.1) | copy-start | bytes 3556
  5.3 4.1 %copy-start.4 = (bf16[256,1024]{1,0:T(8,128)(2,1)S(1)}, bf16[256,1024]{1,0:T(8,128)(2,1)}, u32[]{:S(2)}) copy-start(bf16[256,1024]{1,0:T(8,128)(2,1)} %w0.1) | copy-start | bytes 1572868
  5.3 2.5 %collective-permute-start.3 = (bf16[32,256]{1,0:T(8,128)(2,1)S(1)}, bf16[32,256]{1,0:T(8,128)(2,1)S(1)}, u32[]{:S(2)}, u32[]{:S(2)}) collective-permute-start(bf16[32,256]{1,0:T(8,128)(2,1)S(1)} %get-tuple-element.46.b_own), channel_id=1, source_target_pairs={{0,1},{1,0},{2,3},{3,2},{4,5},{5,4},{6,7},{7,6},{8,9},{9,8},{10,11... | collective-permute-start | bytes 49160 | tf_op jit(solution)/shard_map/ppermute | solution.py:308
  5.5 5.7 %copy-start = (bf16[1024,1024]{1,0:T(8,128)(2,1)S(1)}, bf16[1024,1024]{1,0:T(8,128)(2,1)}, u32[]{:S(2)}) copy-start(bf16[1024,1024]{1,0:T(8,128)(2,1)} %u0.3) | copy-start | bytes 6291460
  5.5 6.6 %copy-start.1 = (bf16[1024,1024]{1,0:T(8,128)(2,1)S(1)}, bf16[1024,1024]{1,0:T(8,128)(2,1)}, u32[]{:S(2)}) copy-start(bf16[1024,1024]{1,0:T(8,128)(2,1)} %d0.3) | copy-start | bytes 6291460
  8.0 1.3 %collective-permute-start.4 = (bf16[160,256]{1,0:T(8,128)(2,1)S(1)}, bf16[160,256]{1,0:T(8,128)(2,1)S(1)}, u32[]{:S(2)}, u32[]{:S(2)}) collective-permute-start(bf16[160,256]{1,0:T(8,128)(2,1)S(1)} %get-tuple-element.48), channel_id=1, source_target_pairs={{0,1},{1,0},{2,3},{3,2},{4,5},{5,4},{6,7},{7,6},{8,9},{9,8},{10,11... | collective-permute-start | bytes 245768 | tf_op jit(solution)/shard_map/ppermute | solution.py:308
  9.7 5.5 %collective-permute-start.5 = (bf16[80,1024]{1,0:T(8,128)(2,1)S(1)}, bf16[80,1024]{1,0:T(8,128)(2,1)S(1)}, u32[]{:S(2)}, u32[]{:S(2)}) collective-permute-start(bf16[80,1024]{1,0:T(8,128)(2,1)S(1)} %get-tuple-element.51.mine), channel_id=1, source_target_pairs={{0,2},{1,3},{2,0},{3,1},{4,6},{5,7},{6,4},{7,5},{8,10},{9,11},{10,... | collective-permute-start | bytes 491528 | tf_op jit(solution)/shard_map/ppermute | solution.py:308
  9.8 8.9 %collective-permute-start.8 = (bf16[80,1024]{1,0:T(8,128)(2,1)S(1)}, bf16[80,1024]{1,0:T(8,128)(2,1)S(1)}, u32[]{:S(2)}, u32[]{:S(2)}) collective-permute-start(bf16[80,1024]{1,0:T(8,128)(2,1)S(1)} %get-tuple-element.58.mine), channel_id=1, source_target_pairs={{0,2},{1,3},{2,0},{3,1},{4,6},{5,7},{6,4},{7,5},{8,10},{9,11},{10,... | collective-permute-start | bytes 491528 | tf_op jit(solution)/shard_map/ppermute | solution.py:308
  11.2 20.6 %collective-permute-start.11 = (bf16[1024,1024]{1,0:T(8,128)(2,1)S(1)}, bf16[1024,1024]{1,0:T(8,128)(2,1)S(1)}, u32[]{:S(2)}, u32[]{:S(2)}) collective-permute-start(bf16[1024,1024]{1,0:T(8,128)(2,1)S(1)} %copy-done), channel_id=1, source_target_pairs={{0,1},{1,0},{2,3},{3,2},{4,5},{5,4},{6,7},{7,6},{8,9},{9,8},{10,11... | collective-permute-start | bytes 6291464 | tf_op jit(solution)/shard_map/ppermute | solution.py:308
  12.1 19.7 %collective-permute-start.12 = (bf16[1024,1024]{1,0:T(8,128)(2,1)S(1)}, bf16[1024,1024]{1,0:T(8,128)(2,1)S(1)}, u32[]{:S(2)}, u32[]{:S(2)}) collective-permute-start(bf16[1024,1024]{1,0:T(8,128)(2,1)S(1)} %copy-done.1), channel_id=1, source_target_pairs={{0,1},{1,0},{2,3},{3,2},{4,5},{5,4},{6,7},{7,6},{8,9},{9,8},{10,11... | collective-permute-start | bytes 6291464 | tf_op jit(solution)/shard_map/ppermute | solution.py:308
  15.3 10.5 %collective-permute-start.6 = (bf16[40,1024]{1,0:T(8,128)(2,1)S(1)}, bf16[40,1024]{1,0:T(8,128)(2,1)S(1)}, u32[]{:S(2)}, u32[]{:S(2)}) collective-permute-start(bf16[40,1024]{1,0:T(8,128)(2,1)S(1)} %get-tuple-element.56), channel_id=1, source_target_pairs={{0,36},{1,37},{2,38},{3,39},{4,40},{5,41},{6,42},{7,43},{8,44},{9,... | collective-permute-start | bytes 245768 | tf_op jit(solution)/shard_map/ppermute | solution.py:308
  16.3 9.5 %collective-permute-start.7 = (bf16[40,1024]{1,0:T(8,128)(2,1)S(1)}, bf16[40,1024]{1,0:T(8,128)(2,1)S(1)}, u32[]{:S(2)}, u32[]{:S(2)}) collective-permute-start(bf16[40,1024]{1,0:T(8,128)(2,1)S(1)} %get-tuple-element.57), channel_id=1, source_target_pairs={{0,4},{1,5},{2,6},{3,7},{4,8},{5,9},{6,10},{7,11},{8,12},{9,13},{1... | collective-permute-start | bytes 245768 | tf_op jit(solution)/shard_map/ppermute | solution.py:308
  18.8 7.2 %copy-start.2 = (bf16[1024,3,256]{2,0,1:T(8,128)(2,1)S(1)}, bf16[1024,3,256]{2,0,1:T(8,128)(2,1)}, u32[]{:S(2)}) copy-start(bf16[1024,3,256]{2,0,1:T(8,128)(2,1)} %param.10) | copy-start | bytes 4718596
  18.8 7.2 %copy-start.3 = (bf16[256,1024]{1,0:T(8,128)(2,1)S(1)}, bf16[256,1024]{1,0:T(8,128)(2,1)}, u32[]{:S(2)}) copy-start(bf16[256,1024]{1,0:T(8,128)(2,1)} %o_own.1) | copy-start | bytes 1572868
  18.8 7.2 %collective-permute-start.9 = (bf16[40,1024]{1,0:T(8,128)(2,1)S(1)}, bf16[40,1024]{1,0:T(8,128)(2,1)S(1)}, u32[]{:S(2)}, u32[]{:S(2)}) collective-permute-start(bf16[40,1024]{1,0:T(8,128)(2,1)S(1)} %get-tuple-element.60), channel_id=1, source_target_pairs={{0,32},{1,33},{2,34},{3,35},{4,36},{5,37},{6,38},{7,39},{8,40},{9,... | collective-permute-start | bytes 245768 | tf_op jit(solution)/shard_map/ppermute | solution.py:308
  27.6 4.3 %collective-permute-start.10 = (bf16[80,1024]{1,0:T(8,128)(2,1)S(1)}, bf16[80,1024]{1,0:T(8,128)(2,1)S(1)}, u32[]{:S(2)}, u32[]{:S(2)}) collective-permute-start(bf16[80,1024]{1,0:T(8,128)(2,1)S(1)} %get-tuple-element.65.mine), channel_id=1, source_target_pairs={{0,2},{1,3},{2,0},{3,1},{4,6},{5,7},{6,4},{7,5},{8,10},{9,11},{10,... | collective-permute-start | bytes 491528 | tf_op jit(solution)/shard_map/ppermute | solution.py:308
  27.7 6.4 %collective-permute-start.14 = (bf16[80,1024]{1,0:T(8,128)(2,1)S(1)}, bf16[80,1024]{1,0:T(8,128)(2,1)S(1)}, u32[]{:S(2)}, u32[]{:S(2)}) collective-permute-start(bf16[80,1024]{1,0:T(8,128)(2,1)S(1)} %get-tuple-element.72.mine), channel_id=1, source_target_pairs={{0,2},{1,3},{2,0},{3,1},{4,6},{5,7},{6,4},{7,5},{8,10},{9,11},{10,... | collective-permute-start | bytes 491528 | tf_op jit(solution)/shard_map/ppermute | solution.py:308
  33.7 5.2 %collective-permute-start.13 = (bf16[80,1024]{1,0:T(8,128)(2,1)S(1)}, bf16[80,1024]{1,0:T(8,128)(2,1)S(1)}, u32[]{:S(2)}, u32[]{:S(2)}) collective-permute-start(bf16[80,1024]{1,0:T(8,128)(2,1)S(1)} %shard_map.89.mine), channel_id=1, source_target_pairs={{0,2},{1,3},{2,0},{3,1},{4,6},{5,7},{6,4},{7,5},{8,10},{9,11},{10,... | collective-permute-start | bytes 491528 | tf_op jit(solution)/shard_map/ppermute | solution.py:308
  36.0 8.2 %collective-permute-start.17 = (bf16[80,1024]{1,0:T(8,128)(2,1)S(1)}, bf16[80,1024]{1,0:T(8,128)(2,1)S(1)}, u32[]{:S(2)}, u32[]{:S(2)}) collective-permute-start(bf16[80,1024]{1,0:T(8,128)(2,1)S(1)} %shard_map.91.mine), channel_id=1, source_target_pairs={{0,2},{1,3},{2,0},{3,1},{4,6},{5,7},{6,4},{7,5},{8,10},{9,11},{10,... | collective-permute-start | bytes 491528 | tf_op jit(solution)/shard_map/ppermute | solution.py:308
  38.9 7.4 %collective-permute-start.15 = (bf16[40,1024]{1,0:T(8,128)(2,1)S(1)}, bf16[40,1024]{1,0:T(8,128)(2,1)S(1)}, u32[]{:S(2)}, u32[]{:S(2)}) collective-permute-start(bf16[40,1024]{1,0:T(8,128)(2,1)S(1)} %get-tuple-element.73), channel_id=1, source_target_pairs={{0,30},{1,31},{2,28},{3,29},{4,0},{5,1},{6,2},{7,3},{8,4},{9,5},{1... | collective-permute-start | bytes 245768 | tf_op jit(solution)/shard_map/ppermute | solution.py:308
  42.5 3.8 %collective-permute-start.16 = (bf16[40,1024]{1,0:T(8,128)(2,1)S(1)}, bf16[40,1024]{1,0:T(8,128)(2,1)S(1)}, u32[]{:S(2)}, u32[]{:S(2)}) collective-permute-start(bf16[40,1024]{1,0:T(8,128)(2,1)S(1)} %get-tuple-element.74), channel_id=1, source_target_pairs={{0,224},{1,225},{2,226},{3,227},{4,228},{5,229},{6,230},{7,231},{8... | collective-permute-start | bytes 245768 | tf_op jit(solution)/shard_map/ppermute | solution.py:308
  44.3 5.0 %collective-permute-start.18 = (bf16[40,1024]{1,0:T(8,128)(2,1)S(1)}, bf16[40,1024]{1,0:T(8,128)(2,1)S(1)}, u32[]{:S(2)}, u32[]{:S(2)}) collective-permute-start(bf16[40,1024]{1,0:T(8,128)(2,1)S(1)} %get-tuple-element.76), channel_id=1, source_target_pairs={{0,254},{1,255},{2,252},{3,253},{4,224},{5,225},{6,226},{7,227},{8... | collective-permute-start | bytes 245768 | tf_op jit(solution)/shard_map/ppermute | solution.py:308
  49.3 6.5 %collective-permute-start.20 = (bf16[80,1024]{1,0:T(8,128)(2,1)S(1)}, bf16[80,1024]{1,0:T(8,128)(2,1)S(1)}, u32[]{:S(2)}, u32[]{:S(2)}) collective-permute-start(bf16[80,1024]{1,0:T(8,128)(2,1)S(1)} %shard_map.94.m1), channel_id=1, source_target_pairs={{0,1},{1,0},{2,3},{3,2},{4,5},{5,4},{6,7},{7,6},{8,9},{9,8},{10,11... | collective-permute-start | bytes 491528 | tf_op jit(solution)/shard_map/ppermute | solution.py:308
  54.8 1.4 %collective-permute-start.19 = (bf16[80,1024]{1,0:T(8,128)(2,1)S(1)}, bf16[80,1024]{1,0:T(8,128)(2,1)S(1)}, u32[]{:S(2)}, u32[]{:S(2)}) collective-permute-start(bf16[80,1024]{1,0:T(8,128)(2,1)S(1)} %shard_map.92.m0), channel_id=1, source_target_pairs={{0,1},{1,0},{2,3},{3,2},{4,5},{5,4},{6,7},{7,6},{8,9},{9,8},{10,11... | collective-permute-start | bytes 491528 | tf_op jit(solution)/shard_map/ppermute | solution.py:308

commit v11 on v10

--- a/solution.py
+++ b/solution.py
@@ -108,8 +108,8 @@
     return jnp.where((lane & FEAT) != 0, total - high, high).astype(jnp.bfloat16)
 
 
-def bias_kernel(table, first, second):
-    for block, out in enumerate((first, second)):
+def bias_kernel(block, *refs):
+    for table, out in zip(refs[: len(refs) // 2], refs[len(refs) // 2 :]):
         for pair in range(2):
             out[:, pair * 128 : pair * 128 + 128] = bias_rows(table, block, pair)
 
@@ -146,7 +146,7 @@
     return slice(pair * 128, pair * 128 + 128)
 
 
-def first_kernel(tokens, weight, bias, keep, give, *bases):
+def first_kernel(tokens, weight, bias, keep, give):
     core = core_index()
     floats = tokens[...].astype(jnp.float32).reshape(PATCH, -1)
     xn = normalize(floats)
@@ -179,11 +179,15 @@
         place = real_level(level, chosen) * 72 + row * 12 + col
         place = jnp.where(slot < USED, place, -1)
         out[...] = dot(one_hot(lanes == place), mixed).astype(jnp.bfloat16)
-    place = (row * 12 + col) * 4 + real_level(level, core)
+
+
+def base_kernel(tokens, *outs):
+    values = tokens[...].astype(jnp.float32).reshape(PATCH, -1).astype(jnp.bfloat16)
+    quad, slot, level, row, col = kept_place(iota((KEPT, 1), 0))
+    row, col = patch_place(quad, row, col)
+    place = (row * 12 + col) * 4 + real_level(level, core_index())
     place = jnp.where(slot < USED, place, -1)
-    base = dot(one_hot(lanes == place), floats.astype(jnp.bfloat16)).astype(jnp.bfloat16)
-    for h in range(2):
-        bases[h][...] = base[h * HALF : (h + 1) * HALF]
+    store_halves(dot(one_hot(iota((KEPT, PATCH), 1) == place), values), outs)
 
 
 def store_halves(total, outs):
@@ -329,10 +333,15 @@
     f1 = core_swap(out_first)
     s1 = core_swap(out_second)
     w_sib = core_swap(w_second)
-    bias1, bias2 = call(bias_kernel, features * 2, (rel_tables,), 5 * 10**9, 4, table=True)
-    bias2_sib = core_swap(bias2)
-    keep, give, base_a, base_b = call(first_kernel, heads * 2 + half * 2, (tok, w_first, bias1), 10**9, 16)
-    keep, give, f1, s1, w_sib, bias2_sib = tied(keep, give, f1, s1, w_sib, bias2_sib)
+    s_table = core_swap(rel_tables)
+    bias1 = call(functools.partial(bias_kernel, 0), features, (rel_tables,), 5 * 10**9, 4, table=True)
+    keep, give = call(first_kernel, heads * 2, (tok, w_first, bias1), 10**9, 16)
+    keep, give, f1, s1, w_sib, s_table = tied(keep, give, f1, s1, w_sib, s_table)
+    keep, tok, rel_tables = tied(keep, tok, rel_tables)
+    base_a, base_b = call(base_kernel, half * 2, (tok,), 10**9, 8)
+    bias2, bias2_sib = call(
+        functools.partial(bias_kernel, 1), features * 2, (rel_tables, s_table), 10**9, 4, table=True
+    )
     given, up_late, down_late = tied(core_swap(give), up_weight, down_weight)
     u1 = core_swap(up_late)
     d1 = core_swap(down_late)

time: 57.7 us -> 57.9 us (level)
  waiting for transfers between devices: 20.8 us -> 19.2 us
  Pallas kernels: 10.4 us -> 11.4 us
  local copies, waits for them, and re-layouts: 0.72 us -> 1.63 us
    ppermute x21, waiting for transfers between devices: 20.8 us -> 19.2 us  [move(): return lax.ppermute(value, AXES, pairs(counts, target))]
    pallas_call x14 -> x16, Pallas kernels: 10.4 us -> 11.4 us  [call(): pl.pallas_call(kernel, out_shape=shapes, in_specs=[pl.BlockSpec(memory_sp...]
    unnamed x16 -> x18, local copies, waits for them, and re-layouts: 0.72 us -> 1.63 us
  transfers between devices with their start and end apart: 21 -> 21, of which waited for: 11 -> 11; matrix products, arithmetic and copies ran while one was open for 0% -> 0% of each run, Pallas kernels for 15% -> 17%
where the time goes in v11:
time: 57.9 us; the launch traced here: 57.8 us
  starting transfers between devices  25.5 us (44%)
  waiting for transfers between devices  19.2 us (33%)
  Pallas kernels  11.4 us (20%)
  local copies, waits for them, and re-layouts  1.63 us (3%)
    ppermute x21, starting transfers between devices, move(): return lax.ppermute(value, AXES, pairs(counts, target))  25.5 us
    ppermute x21, waiting for transfers between devices, move(): return lax.ppermute(value, AXES, pairs(counts, target))  19.2 us
    pallas_call x16, Pallas kernels, call(): pl.pallas_call(kernel, out_shape=shapes, in_specs=[pl.BlockSpec(memory_sp...  11.4 us
    unnamed x18, local copies, waits for them, and re-layouts  1.63 us
  transfers between devices with their start and end apart: 21, of which 11 were waited for; matrix products, arithmetic and copies ran while one was open for 0% of the time, Pallas kernels for 17%

profile of v11, /device:TPU:1, one launch (start us, length us, event | category | flops | bytes accessed | tf_op | source)
XLA Modules:
  0.0 57.8 jit_solution(16705914691020402388)
XLA Ops:
  0.0 3.2 %collective-permute-start.2 = (bf16[3,1024,256]{2,1,0:T(8,128)(2,1)}, bf16[3,1024,256]{2,1,0:T(8,128)(2,1)S(1)}, u32[]{:S(2)}, u32[]{:S(2)}) collective-permute-start(bf16[3,1024,256]{2,1,0:T(8,128)(2,1)} %bitcast.8), channel_id=1, source_target_pairs={{0,1},{1,0},{2,3},{3,2},{4,5},{5,4},{6,7},{7,6},{8,9},{9,8},{10,11... | collective-permute-start | bytes 4718600 | tf_op jit(solution)/shard_map/ppermute | solution.py:312
  3.2 0.5 collective-permute-start.1
  3.8 0.7 %copy-done.7 = f32[2,4,37]{2,1,0:T(4,128)S(1)} copy-done((f32[2,4,37]{2,1,0:T(4,128)S(1)}, f32[2,4,37]{2,1,0:T(4,128)}, u32[]{:S(2)}) %copy-start.7) | copy-done | bytes 1208
  4.4 0.7 %shard_map.82.bias = bf16[32,256]{1,0:T(8,128)(2,1)S(1)} custom-call(f32[2,4,37]{2,1,0:T(4,128)S(1)} %copy-done.7), custom_call_target="tpu_custom_call" | custom-call | flops 5000000000 | bytes 17568 | tf_op jit(solution)/shard_map/pallas_call | solution.py:292
  5.2 2.1 %shard_map.83 = (bf16[160,256]{1,0:T(8,128)(2,1)S(1)}, bf16[160,256]{1,0:T(8,128)(2,1)S(1)}) custom-call(bf16[72,4,1024]{2,1,0:T(4,128)(2,1)S(1)} %bitcast.11, bf16[3,1024,256]{2,1,0:T(8,128)(2,1)S(1)} %bitcast.10, bf16[32,256]{1,0:T(8,128)(2,1)S(1)} %shard_map.82.bias), custom_call_target="tpu_custom_call" | custom-call | flops 1000000000 | bytes 2342912 | tf_op jit(solution)/shard_map/pallas_call | solution.py:292
  7.3 0.7 %collective-permute-done.3.refs_1_ = f32[2,4,37]{2,1,0:T(4,128)S(1)} collective-permute-done((f32[2,4,37]{2,1,0:T(4,128)}, f32[2,4,37]{2,1,0:T(4,128)S(1)}, u32[]{:S(2)}, u32[]{:S(2)}) %collective-permute-start.3) | collective-permute-done | bytes 1216 | tf_op jit(solution)/shard_map/ppermute | solution.py:312
  8.0 0.5 collective-permute-start.4
  8.5 0.9 %collective-permute-done.4.o1 = bf16[160,256]{1,0:T(8,128)(2,1)S(1)} collective-permute-done((bf16[160,256]{1,0:T(8,128)(2,1)S(1)}, bf16[160,256]{1,0:T(8,128)(2,1)S(1)}, u32[]{:S(2)}, u32[]{:S(2)}) %collective-permute-start.4) | collective-permute-done | bytes 81952 | tf_op jit(solution)/shard_map/ppermute | solution.py:312
  9.9 1.5 %collective-permute-start.8 = (bf16[80,1024]{1,0:T(8,128)(2,1)S(1)}, bf16[80,1024]{1,0:T(8,128)(2,1)S(1)}, u32[]{:S(2)}, u32[]{:S(2)}) collective-permute-start(bf16[80,1024]{1,0:T(8,128)(2,1)S(1)} %get-tuple-element.61.mine), channel_id=1, source_target_pairs={{0,2},{1,3},{2,0},{3,1},{4,6},{5,7},{6,4},{7,5},{8,10},{9,11},{10,... | collective-permute-start | bytes 491528 | tf_op jit(solution)/shard_map/ppermute | solution.py:312
  11.8 0.9 %shard_map.89 = (bf16[32,256]{1,0:T(8,128)(2,1)S(1)}, bf16[32,256]{1,0:T(8,128)(2,1)S(1)}) custom-call(f32[2,4,37]{2,1,0:T(4,128)S(1)} %copy-done.8, f32[2,4,37]{2,1,0:T(4,128)S(1)} %collective-permute-done.3.refs_1_), custom_call_target="tpu_custom_call" | custom-call | flops 1000000000 | bytes 35136 | tf_op jit(solution)/shard_map/pallas_call | solution.py:292
  12.6 0.9 %copy-done = bf16[1024,1024]{1,0:T(8,128)(2,1)S(1)} copy-done((bf16[1024,1024]{1,0:T(8,128)(2,1)S(1)}, bf16[1024,1024]{1,0:T(8,128)(2,1)}, u32[]{:S(2)}) %copy-start) | copy-done | bytes 2097176
  13.5 0.9 %collective-permute-start.11 = (bf16[1024,1024]{1,0:T(8,128)(2,1)S(1)}, bf16[1024,1024]{1,0:T(8,128)(2,1)S(1)}, u32[]{:S(2)}, u32[]{:S(2)}) collective-permute-start(bf16[1024,1024]{1,0:T(8,128)(2,1)S(1)} %copy-done), channel_id=1, source_target_pairs={{0,1},{1,0},{2,3},{3,2},{4,5},{5,4},{6,7},{7,6},{8,9},{9,8},{10,11... | collective-permute-start | bytes 6291464 | tf_op jit(solution)/shard_map/ppermute | solution.py:312
  14.5 0.8 %collective-permute-done.5.other = bf16[80,1024]{1,0:T(8,128)(2,1)S(1)} collective-permute-done((bf16[80,1024]{1,0:T(8,128)(2,1)S(1)}, bf16[80,1024]{1,0:T(8,128)(2,1)S(1)}, u32[]{:S(2)}, u32[]{:S(2)}) %collective-permute-start.5) | collective-permute-done | bytes 163872 | tf_op jit(solution)/shard_map/ppermute | solution.py:312
  15.4 1.0 %collective-permute-start.6 = (bf16[40,1024]{1,0:T(8,128)(2,1)S(1)}, bf16[40,1024]{1,0:T(8,128)(2,1)S(1)}, u32[]{:S(2)}, u32[]{:S(2)}) collective-permute-start(bf16[40,1024]{1,0:T(8,128)(2,1)S(1)} %get-tuple-element.59), channel_id=1, source_target_pairs={{0,36},{1,37},{2,38},{3,39},{4,40},{5,41},{6,42},{7,43},{8,44},{9,... | collective-permute-start | bytes 245768 | tf_op jit(solution)/shard_map/ppermute | solution.py:312
  16.3 1.3 %collective-permute-start.7 = (bf16[40,1024]{1,0:T(8,128)(2,1)S(1)}, bf16[40,1024]{1,0:T(8,128)(2,1)S(1)}, u32[]{:S(2)}, u32[]{:S(2)}) collective-permute-start(bf16[40,1024]{1,0:T(8,128)(2,1)S(1)} %get-tuple-element.60), channel_id=1, source_target_pairs={{0,4},{1,5},{2,6},{3,7},{4,8},{5,9},{6,10},{7,11},{8,12},{9,13},{1... | collective-permute-start | bytes 245768 | tf_op jit(solution)/shard_map/ppermute | solution.py:312
  17.6 1.1 %collective-permute-done.8.other = bf16[80,1024]{1,0:T(8,128)(2,1)S(1)} collective-permute-done((bf16[80,1024]{1,0:T(8,128)(2,1)S(1)}, bf16[80,1024]{1,0:T(8,128)(2,1)S(1)}, u32[]{:S(2)}, u32[]{:S(2)}) %collective-permute-start.8) | collective-permute-done | bytes 163872 | tf_op jit(solution)/shard_map/ppermute | solution.py:312
  18.9 0.6 collective-permute-start.9
  19.5 6.4 %collective-permute-done.6.p0 = bf16[40,1024]{1,0:T(8,128)(2,1)S(1)} collective-permute-done((bf16[40,1024]{1,0:T(8,128)(2,1)S(1)}, bf16[40,1024]{1,0:T(8,128)(2,1)S(1)}, u32[]{:S(2)}, u32[]{:S(2)}) %collective-permute-start.6) | collective-permute-done | bytes 81952 | tf_op jit(solution)/shard_map/ppermute | solution.py:312
  26.1 1.6 %shard_map.90 = (bf16[80,1024]{1,0:T(8,128)(2,1)S(1)}, bf16[80,1024]{1,0:T(8,128)(2,1)S(1)}) custom-call(bf16[80,1024]{1,0:T(8,128)(2,1)S(1)} %shard_map.87.xn_a, bf16[40,1024]{1,0:T(8,128)(2,1)S(1)} %collective-permute-done.9.p2.p1, bf16[40,1024]{1,0:T(8,128)(2,1)S(1)} %get-tuple-element.64.p3.p1, bf16[3,1024,256]{2,1,0:T(8,128)(2,1)S(1)} %bitcast.9, ...), custom_call_target="tpu_custom_call" | custom-call | flops 1000000000 | bytes 4882432 | tf_op jit(solution)/shard_map/pallas_call | solution.py:292
  28.0 1.4 %collective-permute-start.14 = (bf16[80,1024]{1,0:T(8,128)(2,1)S(1)}, bf16[80,1024]{1,0:T(8,128)(2,1)S(1)}, u32[]{:S(2)}, u32[]{:S(2)}) collective-permute-start(bf16[80,1024]{1,0:T(8,128)(2,1)S(1)} %get-tuple-element.78.mine), channel_id=1, source_target_pairs={{0,2},{1,3},{2,0},{3,1},{4,6},{5,7},{6,4},{7,5},{8,10},{9,11},{10,... | collective-permute-start | bytes 491528 | tf_op jit(solution)/shard_map/ppermute | solution.py:312
  29.4 2.7 %collective-permute-done.10.other = bf16[80,1024]{1,0:T(8,128)(2,1)S(1)} collective-permute-done((bf16[80,1024]{1,0:T(8,128)(2,1)S(1)}, bf16[80,1024]{1,0:T(8,128)(2,1)S(1)}, u32[]{:S(2)}, u32[]{:S(2)}) %collective-permute-start.10) | collective-permute-done | bytes 163872 | tf_op jit(solution)/shard_map/ppermute | solution.py:312
  32.1 1.8 %shard_map.91.mine = bf16[80,1024]{1,0:T(8,128)(2,1)S(1)} custom-call(bf16[80,1024]{1,0:T(8,128)(2,1)S(1)} %get-tuple-element.71.mine, bf16[80,1024]{1,0:T(8,128)(2,1)S(1)} %collective-permute-done.10.other, bf16[40,1024]{1,0:T(8,128)(2,1)S(1)} %collective-permute-done.7.p1.p0, bf16[40,1024]{1,0:T(8,128)(2,1)S(1)} %collective-permute-done.9.p2.p1, ...), custom_call_target="tpu_custom_call" | custom-call | flops 1000000000 | bytes 9043968 | tf_op jit(solution)/shard_map/pallas_call | solution.py:292
  34.4 1.8 %shard_map.93.mine = bf16[80,1024]{1,0:T(8,128)(2,1)S(1)} custom-call(bf16[80,1024]{1,0:T(8,128)(2,1)S(1)} %get-tuple-element.78.mine, bf16[80,1024]{1,0:T(8,128)(2,1)S(1)} %collective-permute-done.14.other, bf16[40,1024]{1,0:T(8,128)(2,1)S(1)} %collective-permute-done.6.p0, bf16[40,1024]{1,0:T(8,128)(2,1)S(1)} %get-tuple-element.64.p3.p1, ...), custom_call_target="tpu_custom_call" | custom-call | flops 1000000000 | bytes 9043968 | tf_op jit(solution)/shard_map/pallas_call | solution.py:292
  36.2 1.2 %collective-permute-start.17 = (bf16[80,1024]{1,0:T(8,128)(2,1)S(1)}, bf16[80,1024]{1,0:T(8,128)(2,1)S(1)}, u32[]{:S(2)}, u32[]{:S(2)}) collective-permute-start(bf16[80,1024]{1,0:T(8,128)(2,1)S(1)} %shard_map.93.mine), channel_id=1, source_target_pairs={{0,2},{1,3},{2,0},{3,1},{4,6},{5,7},{6,4},{7,5},{8,10},{9,11},{10,... | collective-permute-start | bytes 491528 | tf_op jit(solution)/shard_map/ppermute | solution.py:312
  37.4 1.7 %collective-permute-done.13.other = bf16[80,1024]{1,0:T(8,128)(2,1)S(1)} collective-permute-done((bf16[80,1024]{1,0:T(8,128)(2,1)S(1)}, bf16[80,1024]{1,0:T(8,128)(2,1)S(1)}, u32[]{:S(2)}, u32[]{:S(2)}) %collective-permute-start.13) | collective-permute-done | bytes 163872 | tf_op jit(solution)/shard_map/ppermute | solution.py:312
  39.2 3.5 %collective-permute-start.15 = (bf16[40,1024]{1,0:T(8,128)(2,1)S(1)}, bf16[40,1024]{1,0:T(8,128)(2,1)S(1)}, u32[]{:S(2)}, u32[]{:S(2)}) collective-permute-start(bf16[40,1024]{1,0:T(8,128)(2,1)S(1)} %get-tuple-element.79), channel_id=1, source_target_pairs={{0,30},{1,31},{2,28},{3,29},{4,0},{5,1},{6,2},{7,3},{8,4},{9,5},{1... | collective-permute-start | bytes 245768 | tf_op jit(solution)/shard_map/ppermute | solution.py:312
  42.7 1.8 %collective-permute-start.16 = (bf16[40,1024]{1,0:T(8,128)(2,1)S(1)}, bf16[40,1024]{1,0:T(8,128)(2,1)S(1)}, u32[]{:S(2)}, u32[]{:S(2)}) collective-permute-start(bf16[40,1024]{1,0:T(8,128)(2,1)S(1)} %get-tuple-element.80), channel_id=1, source_target_pairs={{0,224},{1,225},{2,226},{3,227},{4,228},{5,229},{6,230},{7,231},{8... | collective-permute-start | bytes 245768 | tf_op jit(solution)/shard_map/ppermute | solution.py:312
  44.5 2.0 %collective-permute-start.18 = (bf16[40,1024]{1,0:T(8,128)(2,1)S(1)}, bf16[40,1024]{1,0:T(8,128)(2,1)S(1)}, u32[]{:S(2)}, u32[]{:S(2)}) collective-permute-start(bf16[40,1024]{1,0:T(8,128)(2,1)S(1)} %get-tuple-element.82), channel_id=1, source_target_pairs={{0,254},{1,255},{2,252},{3,253},{4,224},{5,225},{6,226},{7,227},{8... | collective-permute-start | bytes 245768 | tf_op jit(solution)/shard_map/ppermute | solution.py:312
  46.5 3.0 %collective-permute-done.18.p0 = bf16[40,1024]{1,0:T(8,128)(2,1)S(1)} collective-permute-done((bf16[40,1024]{1,0:T(8,128)(2,1)S(1)}, bf16[40,1024]{1,0:T(8,128)(2,1)S(1)}, u32[]{:S(2)}, u32[]{:S(2)}) %collective-permute-start.18) | collective-permute-done | bytes 81952 | tf_op jit(solution)/shard_map/ppermute | solution.py:312
  49.6 5.5 %collective-permute-start.20 = (bf16[80,1024]{1,0:T(8,128)(2,1)S(1)}, bf16[80,1024]{1,0:T(8,128)(2,1)S(1)}, u32[]{:S(2)}, u32[]{:S(2)}) collective-permute-start(bf16[80,1024]{1,0:T(8,128)(2,1)S(1)} %shard_map.96.m1), channel_id=1, source_target_pairs={{0,1},{1,0},{2,3},{3,2},{4,5},{5,4},{6,7},{7,6},{8,9},{9,8},{10,11... | collective-permute-start | bytes 491528 | tf_op jit(solution)/shard_map/ppermute | solution.py:312
  55.2 0.9 %collective-permute-done.20.s1 = bf16[80,1024]{1,0:T(8,128)(2,1)S(1)} collective-permute-done((bf16[80,1024]{1,0:T(8,128)(2,1)S(1)}, bf16[80,1024]{1,0:T(8,128)(2,1)S(1)}, u32[]{:S(2)}, u32[]{:S(2)}) %collective-permute-start.20) | collective-permute-done | bytes 163872 | tf_op jit(solution)/shard_map/ppermute | solution.py:312
  56.5 1.3 %shard_map.97 = bf16[72,4,1024]{2,1,0:T(4,128)(2,1)} custom-call(bf16[80,1024]{1,0:T(8,128)(2,1)S(1)} %shard_map.94.m0, bf16[80,1024]{1,0:T(8,128)(2,1)S(1)} %shard_map.96.m1, bf16[80,1024]{1,0:T(8,128)(2,1)S(1)} %collective-permute-done.19.s0, bf16[80,1024]{1,0:T(8,128)(2,1)S(1)} %collective-permute-done.20.s1), custom_call_target="tpu_custom_call" | custom-call | flops 200000000 | bytes 1245184 | tf_op jit(solution)/shard_map/pallas_call | solution.py:292
  (44 shorter events, 2.7 us)
Async XLA Ops:
  0.0 5.2 %copy-start.5 = (bf16[1024,3,256]{2,0,1:T(8,128)(2,1)S(1)}, bf16[1024,3,256]{2,0,1:T(8,128)(2,1)}, u32[]{:S(2)}) copy-start(bf16[1024,3,256]{2,0,1:T(8,128)(2,1)} %param.9) | copy-start | bytes 4718596
  0.0 5.2 %copy-start.6 = (bf16[4,6,12,1024]{3,0,2,1:T(4,128)(2,1)S(1)}, bf16[4,6,12,1024]{3,0,2,1:T(4,128)(2,1)}, u32[]{:S(2)}) copy-start(bf16[4,6,12,1024]{3,0,2,1:T(4,128)(2,1)} %param.8) | copy-start | bytes 1769476
  0.0 8.0 %collective-permute-start.2 = (bf16[3,1024,256]{2,1,0:T(8,128)(2,1)}, bf16[3,1024,256]{2,1,0:T(8,128)(2,1)S(1)}, u32[]{:S(2)}, u32[]{:S(2)}) collective-permute-start(bf16[3,1024,256]{2,1,0:T(8,128)(2,1)} %bitcast.8), channel_id=1, source_target_pairs={{0,1},{1,0},{2,3},{3,2},{4,5},{5,4},{6,7},{7,6},{8,9},{9,8},{10,11... | collective-permute-start | bytes 4718600 | tf_op jit(solution)/shard_map/ppermute | solution.py:312
  3.2 4.8 %collective-permute-start = (bf16[256,1024]{1,0:T(8,128)(2,1)}, bf16[256,1024]{1,0:T(8,128)(2,1)S(1)}, u32[]{:S(2)}, u32[]{:S(2)}) collective-permute-start(bf16[256,1024]{1,0:T(8,128)(2,1)} %w0.1), channel_id=1, source_target_pairs={{0,1},{1,0},{2,3},{3,2},{4,5},{5,4},{6,7},{7,6},{8,9},{9,8},{10,11... | collective-permute-start | bytes 1572872 | tf_op jit(solution)/shard_map/ppermute | solution.py:312
  3.2 4.8 %collective-permute-start.1 = (bf16[256,1024]{1,0:T(8,128)(2,1)}, bf16[256,1024]{1,0:T(8,128)(2,1)S(1)}, u32[]{:S(2)}, u32[]{:S(2)}) collective-permute-start(bf16[256,1024]{1,0:T(8,128)(2,1)} %o_own.1), channel_id=1, source_target_pairs={{0,1},{1,0},{2,3},{3,2},{4,5},{5,4},{6,7},{7,6},{8,9},{9,8},{10,11... | collective-permute-start | bytes 1572872 | tf_op jit(solution)/shard_map/ppermute | solution.py:312
  3.8 4.2 %collective-permute-start.3 = (f32[2,4,37]{2,1,0:T(4,128)}, f32[2,4,37]{2,1,0:T(4,128)S(1)}, u32[]{:S(2)}, u32[]{:S(2)}) collective-permute-start(f32[2,4,37]{2,1,0:T(4,128)} %refs_0_.2), channel_id=1, source_target_pairs={{0,1},{1,0},{2,3},{3,2},{4,5},{5,4},{6,7},{7,6},{8,9},{9,8},{10,11... | collective-permute-start | bytes 3560 | tf_op jit(solution)/shard_map/ppermute | solution.py:312
  3.8 0.7 %copy-start.7 = (f32[2,4,37]{2,1,0:T(4,128)S(1)}, f32[2,4,37]{2,1,0:T(4,128)}, u32[]{:S(2)}) copy-start(f32[2,4,37]{2,1,0:T(4,128)} %refs_0_.2) | copy-start | bytes 3556
  5.2 4.2 %copy-start.4 = (bf16[256,1024]{1,0:T(8,128)(2,1)S(1)}, bf16[256,1024]{1,0:T(8,128)(2,1)}, u32[]{:S(2)}) copy-start(bf16[256,1024]{1,0:T(8,128)(2,1)} %w0.1) | copy-start | bytes 1572868
  8.0 1.4 %collective-permute-start.4 = (bf16[160,256]{1,0:T(8,128)(2,1)S(1)}, bf16[160,256]{1,0:T(8,128)(2,1)S(1)}, u32[]{:S(2)}, u32[]{:S(2)}) collective-permute-start(bf16[160,256]{1,0:T(8,128)(2,1)S(1)} %get-tuple-element.50), channel_id=1, source_target_pairs={{0,1},{1,0},{2,3},{3,2},{4,5},{5,4},{6,7},{7,6},{8,9},{9,8},{10,11... | collective-permute-start | bytes 245768 | tf_op jit(solution)/shard_map/ppermute | solution.py:312
  9.7 2.0 %copy-start.8 = (f32[2,4,37]{2,1,0:T(4,128)S(1)}, f32[2,4,37]{2,1,0:T(4,128)}, u32[]{:S(2)}) copy-start(f32[2,4,37]{2,1,0:T(4,128)} %refs_0_.2) | copy-start | bytes 3556
  9.8 5.5 %collective-permute-start.5 = (bf16[80,1024]{1,0:T(8,128)(2,1)S(1)}, bf16[80,1024]{1,0:T(8,128)(2,1)S(1)}, u32[]{:S(2)}, u32[]{:S(2)}) collective-permute-start(bf16[80,1024]{1,0:T(8,128)(2,1)S(1)} %get-tuple-element.53.mine), channel_id=1, source_target_pairs={{0,2},{1,3},{2,0},{3,1},{4,6},{5,7},{6,4},{7,5},{8,10},{9,11},{10,... | collective-permute-start | bytes 491528 | tf_op jit(solution)/shard_map/ppermute | solution.py:312
  9.9 8.9 %collective-permute-start.8 = (bf16[80,1024]{1,0:T(8,128)(2,1)S(1)}, bf16[80,1024]{1,0:T(8,128)(2,1)S(1)}, u32[]{:S(2)}, u32[]{:S(2)}) collective-permute-start(bf16[80,1024]{1,0:T(8,128)(2,1)S(1)} %get-tuple-element.61.mine), channel_id=1, source_target_pairs={{0,2},{1,3},{2,0},{3,1},{4,6},{5,7},{6,4},{7,5},{8,10},{9,11},{10,... | collective-permute-start | bytes 491528 | tf_op jit(solution)/shard_map/ppermute | solution.py:312
  11.3 3.1 %copy-start.1 = (bf16[1024,1024]{1,0:T(8,128)(2,1)S(1)}, bf16[1024,1024]{1,0:T(8,128)(2,1)}, u32[]{:S(2)}) copy-start(bf16[1024,1024]{1,0:T(8,128)(2,1)} %d0.3) | copy-start | bytes 6291460
  11.7 1.8 %copy-start = (bf16[1024,1024]{1,0:T(8,128)(2,1)S(1)}, bf16[1024,1024]{1,0:T(8,128)(2,1)}, u32[]{:S(2)}) copy-start(bf16[1024,1024]{1,0:T(8,128)(2,1)} %u0.3) | copy-start | bytes 6291460
  13.5 18.6 %collective-permute-start.11 = (bf16[1024,1024]{1,0:T(8,128)(2,1)S(1)}, bf16[1024,1024]{1,0:T(8,128)(2,1)S(1)}, u32[]{:S(2)}, u32[]{:S(2)}) collective-permute-start(bf16[1024,1024]{1,0:T(8,128)(2,1)S(1)} %copy-done), channel_id=1, source_target_pairs={{0,1},{1,0},{2,3},{3,2},{4,5},{5,4},{6,7},{7,6},{8,9},{9,8},{10,11... | collective-permute-start | bytes 6291464 | tf_op jit(solution)/shard_map/ppermute | solution.py:312
  14.5 17.7 %collective-permute-start.12 = (bf16[1024,1024]{1,0:T(8,128)(2,1)S(1)}, bf16[1024,1024]{1,0:T(8,128)(2,1)S(1)}, u32[]{:S(2)}, u32[]{:S(2)}) collective-permute-start(bf16[1024,1024]{1,0:T(8,128)(2,1)S(1)} %copy-done.1), channel_id=1, source_target_pairs={{0,1},{1,0},{2,3},{3,2},{4,5},{5,4},{6,7},{7,6},{8,9},{9,8},{10,11... | collective-permute-start | bytes 6291464 | tf_op jit(solution)/shard_map/ppermute | solution.py:312
  15.4 10.5 %collective-permute-start.6 = (bf16[40,1024]{1,0:T(8,128)(2,1)S(1)}, bf16[40,1024]{1,0:T(8,128)(2,1)S(1)}, u32[]{:S(2)}, u32[]{:S(2)}) collective-permute-start(bf16[40,1024]{1,0:T(8,128)(2,1)S(1)} %get-tuple-element.59), channel_id=1, source_target_pairs={{0,36},{1,37},{2,38},{3,39},{4,40},{5,41},{6,42},{7,43},{8,44},{9,... | collective-permute-start | bytes 245768 | tf_op jit(solution)/shard_map/ppermute | solution.py:312
  16.3 9.5 %collective-permute-start.7 = (bf16[40,1024]{1,0:T(8,128)(2,1)S(1)}, bf16[40,1024]{1,0:T(8,128)(2,1)S(1)}, u32[]{:S(2)}, u32[]{:S(2)}) collective-permute-start(bf16[40,1024]{1,0:T(8,128)(2,1)S(1)} %get-tuple-element.60), channel_id=1, source_target_pairs={{0,4},{1,5},{2,6},{3,7},{4,8},{5,9},{6,10},{7,11},{8,12},{9,13},{1... | collective-permute-start | bytes 245768 | tf_op jit(solution)/shard_map/ppermute | solution.py:312
  18.9 7.2 %copy-start.2 = (bf16[1024,3,256]{2,0,1:T(8,128)(2,1)S(1)}, bf16[1024,3,256]{2,0,1:T(8,128)(2,1)}, u32[]{:S(2)}) copy-start(bf16[1024,3,256]{2,0,1:T(8,128)(2,1)} %param.10) | copy-start | bytes 4718596
  18.9 7.2 %copy-start.3 = (bf16[256,1024]{1,0:T(8,128)(2,1)S(1)}, bf16[256,1024]{1,0:T(8,128)(2,1)}, u32[]{:S(2)}) copy-start(bf16[256,1024]{1,0:T(8,128)(2,1)} %o_own.1) | copy-start | bytes 1572868
  18.9 7.2 %collective-permute-start.9 = (bf16[40,1024]{1,0:T(8,128)(2,1)S(1)}, bf16[40,1024]{1,0:T(8,128)(2,1)S(1)}, u32[]{:S(2)}, u32[]{:S(2)}) collective-permute-start(bf16[40,1024]{1,0:T(8,128)(2,1)S(1)} %get-tuple-element.63), channel_id=1, source_target_pairs={{0,32},{1,33},{2,34},{3,35},{4,36},{5,37},{6,38},{7,39},{8,40},{9,... | collective-permute-start | bytes 245768 | tf_op jit(solution)/shard_map/ppermute | solution.py:312
  27.7 4.4 %collective-permute-start.10 = (bf16[80,1024]{1,0:T(8,128)(2,1)S(1)}, bf16[80,1024]{1,0:T(8,128)(2,1)S(1)}, u32[]{:S(2)}, u32[]{:S(2)}) collective-permute-start(bf16[80,1024]{1,0:T(8,128)(2,1)S(1)} %get-tuple-element.71.mine), channel_id=1, source_target_pairs={{0,2},{1,3},{2,0},{3,1},{4,6},{5,7},{6,4},{7,5},{8,10},{9,11},{10,... | collective-permute-start | bytes 491528 | tf_op jit(solution)/shard_map/ppermute | solution.py:312
  28.0 6.4 %collective-permute-start.14 = (bf16[80,1024]{1,0:T(8,128)(2,1)S(1)}, bf16[80,1024]{1,0:T(8,128)(2,1)S(1)}, u32[]{:S(2)}, u32[]{:S(2)}) collective-permute-start(bf16[80,1024]{1,0:T(8,128)(2,1)S(1)} %get-tuple-element.78.mine), channel_id=1, source_target_pairs={{0,2},{1,3},{2,0},{3,1},{4,6},{5,7},{6,4},{7,5},{8,10},{9,11},{10,... | collective-permute-start | bytes 491528 | tf_op jit(solution)/shard_map/ppermute | solution.py:312
  33.9 5.2 %collective-permute-start.13 = (bf16[80,1024]{1,0:T(8,128)(2,1)S(1)}, bf16[80,1024]{1,0:T(8,128)(2,1)S(1)}, u32[]{:S(2)}, u32[]{:S(2)}) collective-permute-start(bf16[80,1024]{1,0:T(8,128)(2,1)S(1)} %shard_map.91.mine), channel_id=1, source_target_pairs={{0,2},{1,3},{2,0},{3,1},{4,6},{5,7},{6,4},{7,5},{8,10},{9,11},{10,... | collective-permute-start | bytes 491528 | tf_op jit(solution)/shard_map/ppermute | solution.py:312
  36.2 8.3 %collective-permute-start.17 = (bf16[80,1024]{1,0:T(8,128)(2,1)S(1)}, bf16[80,1024]{1,0:T(8,128)(2,1)S(1)}, u32[]{:S(2)}, u32[]{:S(2)}) collective-permute-start(bf16[80,1024]{1,0:T(8,128)(2,1)S(1)} %shard_map.93.mine), channel_id=1, source_target_pairs={{0,2},{1,3},{2,0},{3,1},{4,6},{5,7},{6,4},{7,5},{8,10},{9,11},{10,... | collective-permute-start | bytes 491528 | tf_op jit(solution)/shard_map/ppermute | solution.py:312
  39.2 7.3 %collective-permute-start.15 = (bf16[40,1024]{1,0:T(8,128)(2,1)S(1)}, bf16[40,1024]{1,0:T(8,128)(2,1)S(1)}, u32[]{:S(2)}, u32[]{:S(2)}) collective-permute-start(bf16[40,1024]{1,0:T(8,128)(2,1)S(1)} %get-tuple-element.79), channel_id=1, source_target_pairs={{0,30},{1,31},{2,28},{3,29},{4,0},{5,1},{6,2},{7,3},{8,4},{9,5},{1... | collective-permute-start | bytes 245768 | tf_op jit(solution)/shard_map/ppermute | solution.py:312
  42.7 3.8 %collective-permute-start.16 = (bf16[40,1024]{1,0:T(8,128)(2,1)S(1)}, bf16[40,1024]{1,0:T(8,128)(2,1)S(1)}, u32[]{:S(2)}, u32[]{:S(2)}) collective-permute-start(bf16[40,1024]{1,0:T(8,128)(2,1)S(1)} %get-tuple-element.80), channel_id=1, source_target_pairs={{0,224},{1,225},{2,226},{3,227},{4,228},{5,229},{6,230},{7,231},{8... | collective-permute-start | bytes 245768 | tf_op jit(solution)/shard_map/ppermute | solution.py:312
  44.5 5.1 %collective-permute-start.18 = (bf16[40,1024]{1,0:T(8,128)(2,1)S(1)}, bf16[40,1024]{1,0:T(8,128)(2,1)S(1)}, u32[]{:S(2)}, u32[]{:S(2)}) collective-permute-start(bf16[40,1024]{1,0:T(8,128)(2,1)S(1)} %get-tuple-element.82), channel_id=1, source_target_pairs={{0,254},{1,255},{2,252},{3,253},{4,224},{5,225},{6,226},{7,227},{8... | collective-permute-start | bytes 245768 | tf_op jit(solution)/shard_map/ppermute | solution.py:312
  49.6 6.5 %collective-permute-start.20 = (bf16[80,1024]{1,0:T(8,128)(2,1)S(1)}, bf16[80,1024]{1,0:T(8,128)(2,1)S(1)}, u32[]{:S(2)}, u32[]{:S(2)}) collective-permute-start(bf16[80,1024]{1,0:T(8,128)(2,1)S(1)} %shard_map.96.m1), channel_id=1, source_target_pairs={{0,1},{1,0},{2,3},{3,2},{4,5},{5,4},{6,7},{7,6},{8,9},{9,8},{10,11... | collective-permute-start | bytes 491528 | tf_op jit(solution)/shard_map/ppermute | solution.py:312
  55.1 1.4 %collective-permute-start.19 = (bf16[80,1024]{1,0:T(8,128)(2,1)S(1)}, bf16[80,1024]{1,0:T(8,128)(2,1)S(1)}, u32[]{:S(2)}, u32[]{:S(2)}) collective-permute-start(bf16[80,1024]{1,0:T(8,128)(2,1)S(1)} %shard_map.94.m0), channel_id=1, source_target_pairs={{0,1},{1,0},{2,3},{3,2},{4,5},{5,4},{6,7},{7,6},{8,9},{9,8},{10,11... | collective-permute-start | bytes 491528 | tf_op jit(solution)/shard_map/ppermute | solution.py:312

commit v12 on v11

--- a/solution.py
+++ b/solution.py
@@ -36,9 +36,11 @@
     for a in range(lats):
         for b in range(lons):
             for m in range(mps):
-                ta, tb, tm = target(a, b, m)
-                dest = ((ta % lats) * lons + tb % lons) * mps + tm
-                result.append(((a * lons + b) * mps + m, dest))
+                found = target(a, b, m)
+                if found is not None:
+                    ta, tb, tm = found
+                    dest = ((ta % lats) * lons + tb % lons) * mps + tm
+                    result.append(((a * lons + b) * mps + m, dest))
     return result
 
 
@@ -267,21 +269,26 @@
         outs[p][...] = total[p * ROWS : (p + 1) * ROWS].astype(jnp.bfloat16)
 
 
-def join_kernel(p0, p1, out):
-    out[...] = joined((p0, p1)).astype(jnp.bfloat16)
-
-
-def place_kernel(m0, m1, s0, s1, out):
+def join_kernel(lon, lat, out):
+    out[...] = joined((lon, lat)).astype(jnp.bfloat16)
+
+
+def join_rest_kernel(pair, diag, lon_around, lat_around, diag_around, own, out):
+    around = joined((lon_around, lat_around, diag_around))
+    total = jnp.concatenate([pair[...].astype(jnp.float32), joined((diag,))], axis=0) + around
+    out[...] = jnp.concatenate([total, joined((own,))], axis=0).astype(jnp.bfloat16)
+
+
+def place_kernel(mine, other, out):
     core = core_index()
     piece, slot, level, row, col = kept_place(iota((1, KEPT), 1))
     quad = jnp.where(piece < 2, piece + 1, jnp.where(piece == 2, 0, piece))
     row, col = patch_place(quad, row, col)
     total = None
-    for chosen, parts in ((core, (m0, m1)), (1 - core, (s0, s1))):
+    for chosen, rows in ((core, mine), (1 - core, other)):
         place = (row * 12 + col) * 4 + real_level(level, chosen)
         place = jnp.where(slot < USED, place, -1)
-        source = jnp.concatenate([part[...] for part in parts], axis=0)
-        term = dot(one_hot(iota((PATCH, KEPT), 0) == place), source)
+        term = dot(one_hot(iota((PATCH, KEPT), 0) == place), rows[...])
         total = term if total is None else total + term
     out[...] = total.reshape(out.shape).astype(jnp.bfloat16)
 
@@ -321,7 +328,15 @@
         return move(value, lambda a, b, m: (a + dy, b + dx, m ^ 2 if dx and (b + 1) % turn == 0 else m))
 
     def home(value, dy, dx):
-        return move(value, lambda a, b, m: (a - dy, b - dx, m ^ 2 if dx and b % turn == 0 else m))
+        def edges(around):
+            def target(a, b, m):
+                if ((dy and a == 0) or (dx and b == 0)) != around:
+                    return None
+                return a - dy, b - dx, m ^ 2 if dx and b % turn == 0 else m
+
+            return move(value, target)
+
+        return edges(False), edges(True)
 
     half, piece = [(HALF, width)], [(ROWS, width)]
     heads, features = [(KEPT, 256)], [(FEAT, 256)]
@@ -336,7 +351,7 @@
     s_table = core_swap(rel_tables)
     bias1 = call(functools.partial(bias_kernel, 0), features, (rel_tables,), 5 * 10**9, 4, table=True)
     keep, give = call(first_kernel, heads * 2, (tok, w_first, bias1), 10**9, 16)
-    keep, give, f1, s1, w_sib, s_table = tied(keep, give, f1, s1, w_sib, s_table)
+    keep, give, f1, s1, w_sib = tied(keep, give, f1, s1, w_sib)
     keep, tok, rel_tables = tied(keep, tok, rel_tables)
     base_a, base_b = call(base_kernel, half * 2, (tok,), 10**9, 8)
     bias2, bias2_sib = call(
@@ -377,15 +392,11 @@
     lat = home(lat, 1, 0)
     diag, own = call(sum_kernel, piece * 2, (part_b, other_b), 10**10, 8)
     diag = home(diag, 1, 1)
-    mine_a = call(join_kernel, half, (lon, lat), 10**10, 8)
-    mine_a, diag, own = tied(mine_a, diag, own)
-    mine_b = call(join_kernel, half, (diag, own), 10**6, 8)
+    pair = call(join_kernel, half, (lon[0], lat[0]), 10**10, 8)
+    pair, own, diag_in, *around = tied(pair, own, diag[0], lon[1], lat[1], diag[1])
+    mine = call(join_rest_kernel, [(KEPT, width)], (pair, diag_in, *around, own), 10**6, 8)
     result = call(
-        place_kernel,
-        [(rows * cols, levels, width)],
-        (mine_a, mine_b, core_swap(mine_a), core_swap(mine_b)),
-        2 * 10**8,
-        12,
+        place_kernel, [(rows * cols, levels, width)], (mine, core_swap(mine)), 2 * 10**8, 12
     )
     return result.reshape(rows, cols, levels, width).transpose(2, 0, 1, 3)
 

time: 57.9 us -> 70.1 us (1.21)
  starting transfers between devices: 25.5 us -> 39.2 us
  waiting for transfers between devices: 19.2 us -> 17.3 us
    ppermute x21 -> x23, starting transfers between devices: 25.5 us -> 39.2 us  [move(): return lax.ppermute(value, AXES, pairs(counts, target))]
    ppermute x21 -> x23, waiting for transfers between devices: 19.2 us -> 17.3 us  [move(): return lax.ppermute(value, AXES, pairs(counts, target))]
  transfers between devices with their start and end apart: 21 -> 23, of which waited for: 11 -> 10; matrix products, arithmetic and copies ran while one was open for 0% -> 0% of each run, Pallas kernels for 17% -> 14%
where the time goes in v12:
time: 70.1 us; the launch traced here: 69.9 us
  starting transfers between devices  39.2 us (56%)
  waiting for transfers between devices  17.3 us (25%)
  Pallas kernels  11.4 us (16%)
  local copies, waits for them, and re-layouts  1.63 us (2%)
    ppermute x23, starting transfers between devices, move(): return lax.ppermute(value, AXES, pairs(counts, target))  39.2 us
    ppermute x23, waiting for transfers between devices, move(): return lax.ppermute(value, AXES, pairs(counts, target))  17.3 us
    pallas_call x16, Pallas kernels, call(): pl.pallas_call(kernel, out_shape=shapes, in_specs=[pl.BlockSpec(memory_sp...  11.4 us
    unnamed x18, local copies, waits for them, and re-layouts  1.63 us
  transfers between devices with their start and end apart: 23, of which 10 were waited for; matrix products, arithmetic and copies ran while one was open for 0% of the time, Pallas kernels for 14%

profile of v12, /device:TPU:1, one launch (start us, length us, event | category | flops | bytes accessed | tf_op | source)
XLA Modules:
  0.0 69.9 jit_solution(16317962973306568363)
XLA Ops:
  0.0 3.2 %collective-permute-start.2 = (bf16[3,1024,256]{2,1,0:T(8,128)(2,1)}, bf16[3,1024,256]{2,1,0:T(8,128)(2,1)S(1)}, u32[]{:S(2)}, u32[]{:S(2)}) collective-permute-start(bf16[3,1024,256]{2,1,0:T(8,128)(2,1)} %bitcast.8), channel_id=1, source_target_pairs={{0,1},{1,0},{2,3},{3,2},{4,5},{5,4},{6,7},{7,6},{8,9},{9,8},{10,11... | collective-permute-start | bytes 4718600 | tf_op jit(solution)/shard_map/ppermute | solution.py:319
  3.8 0.7 copy-done.7
  4.4 0.7 %shard_map.82.bias = bf16[32,256]{1,0:T(8,128)(2,1)S(1)} custom-call(f32[2,4,37]{2,1,0:T(4,128)S(1)} %copy-done.7), custom_call_target="tpu_custom_call" | custom-call | flops 5000000000 | bytes 17568 | tf_op jit(solution)/shard_map/pallas_call | solution.py:299
  5.2 2.1 %shard_map.83 = (bf16[160,256]{1,0:T(8,128)(2,1)S(1)}, bf16[160,256]{1,0:T(8,128)(2,1)S(1)}) custom-call(bf16[72,4,1024]{2,1,0:T(4,128)(2,1)S(1)} %bitcast.11, bf16[3,1024,256]{2,1,0:T(8,128)(2,1)S(1)} %bitcast.10, bf16[32,256]{1,0:T(8,128)(2,1)S(1)} %shard_map.82.bias), custom_call_target="tpu_custom_call" | custom-call | flops 1000000000 | bytes 2342912 | tf_op jit(solution)/shard_map/pallas_call | solution.py:299
  7.3 0.7 %collective-permute-done.1.o_sib = bf16[256,1024]{1,0:T(8,128)(2,1)S(1)} collective-permute-done((bf16[256,1024]{1,0:T(8,128)(2,1)}, bf16[256,1024]{1,0:T(8,128)(2,1)S(1)}, u32[]{:S(2)}, u32[]{:S(2)}) %collective-permute-start.1) | collective-permute-done | bytes 524320 | tf_op jit(solution)/shard_map/ppermute | solution.py:319
  8.5 0.8 %collective-permute-done.3.o1 = bf16[160,256]{1,0:T(8,128)(2,1)S(1)} collective-permute-done((bf16[160,256]{1,0:T(8,128)(2,1)S(1)}, bf16[160,256]{1,0:T(8,128)(2,1)S(1)}, u32[]{:S(2)}, u32[]{:S(2)}) %collective-permute-start.3) | collective-permute-done | bytes 81952 | tf_op jit(solution)/shard_map/ppermute | solution.py:319
  9.7 1.5 %collective-permute-start.7 = (bf16[80,1024]{1,0:T(8,128)(2,1)S(1)}, bf16[80,1024]{1,0:T(8,128)(2,1)S(1)}, u32[]{:S(2)}, u32[]{:S(2)}) collective-permute-start(bf16[80,1024]{1,0:T(8,128)(2,1)S(1)} %get-tuple-element.63.mine), channel_id=1, source_target_pairs={{0,2},{1,3},{2,0},{3,1},{4,6},{5,7},{6,4},{7,5},{8,10},{9,11},{10,... | collective-permute-start | bytes 491528 | tf_op jit(solution)/shard_map/ppermute | solution.py:319
  11.6 0.9 %shard_map.89 = (bf16[32,256]{1,0:T(8,128)(2,1)S(1)}, bf16[32,256]{1,0:T(8,128)(2,1)S(1)}) custom-call(f32[2,4,37]{2,1,0:T(4,128)S(1)} %copy-done.8, f32[2,4,37]{2,1,0:T(4,128)S(1)} %collective-permute-done.9.refs_1_), custom_call_target="tpu_custom_call" | custom-call | flops 1000000000 | bytes 35136 | tf_op jit(solution)/shard_map/pallas_call | solution.py:299
  12.5 0.9 %copy-done = bf16[1024,1024]{1,0:T(8,128)(2,1)S(1)} copy-done((bf16[1024,1024]{1,0:T(8,128)(2,1)S(1)}, bf16[1024,1024]{1,0:T(8,128)(2,1)}, u32[]{:S(2)}) %copy-start) | copy-done | bytes 2097176
  13.4 0.9 %collective-permute-start.11 = (bf16[1024,1024]{1,0:T(8,128)(2,1)S(1)}, bf16[1024,1024]{1,0:T(8,128)(2,1)S(1)}, u32[]{:S(2)}, u32[]{:S(2)}) collective-permute-start(bf16[1024,1024]{1,0:T(8,128)(2,1)S(1)} %copy-done), channel_id=1, source_target_pairs={{0,1},{1,0},{2,3},{3,2},{4,5},{5,4},{6,7},{7,6},{8,9},{9,8},{10,11... | collective-permute-start | bytes 6291464 | tf_op jit(solution)/shard_map/ppermute | solution.py:319
  14.3 0.8 %collective-permute-done.4.other = bf16[80,1024]{1,0:T(8,128)(2,1)S(1)} collective-permute-done((bf16[80,1024]{1,0:T(8,128)(2,1)S(1)}, bf16[80,1024]{1,0:T(8,128)(2,1)S(1)}, u32[]{:S(2)}, u32[]{:S(2)}) %collective-permute-start.4) | collective-permute-done | bytes 163872 | tf_op jit(solution)/shard_map/ppermute | solution.py:319
  15.2 1.0 %collective-permute-start.5 = (bf16[40,1024]{1,0:T(8,128)(2,1)S(1)}, bf16[40,1024]{1,0:T(8,128)(2,1)S(1)}, u32[]{:S(2)}, u32[]{:S(2)}) collective-permute-start(bf16[40,1024]{1,0:T(8,128)(2,1)S(1)} %get-tuple-element.61), channel_id=1, source_target_pairs={{0,36},{1,37},{2,38},{3,39},{4,40},{5,41},{6,42},{7,43},{8,44},{9,... | collective-permute-start | bytes 245768 | tf_op jit(solution)/shard_map/ppermute | solution.py:319
  16.2 1.3 %collective-permute-start.6 = (bf16[40,1024]{1,0:T(8,128)(2,1)S(1)}, bf16[40,1024]{1,0:T(8,128)(2,1)S(1)}, u32[]{:S(2)}, u32[]{:S(2)}) collective-permute-start(bf16[40,1024]{1,0:T(8,128)(2,1)S(1)} %get-tuple-element.62), channel_id=1, source_target_pairs={{0,4},{1,5},{2,6},{3,7},{4,8},{5,9},{6,10},{7,11},{8,12},{9,13},{1... | collective-permute-start | bytes 245768 | tf_op jit(solution)/shard_map/ppermute | solution.py:319
  17.5 1.1 %collective-permute-done.7.other = bf16[80,1024]{1,0:T(8,128)(2,1)S(1)} collective-permute-done((bf16[80,1024]{1,0:T(8,128)(2,1)S(1)}, bf16[80,1024]{1,0:T(8,128)(2,1)S(1)}, u32[]{:S(2)}, u32[]{:S(2)}) %collective-permute-start.7) | collective-permute-done | bytes 163872 | tf_op jit(solution)/shard_map/ppermute | solution.py:319
  19.4 6.4 %collective-permute-done.5.p0 = bf16[40,1024]{1,0:T(8,128)(2,1)S(1)} collective-permute-done((bf16[40,1024]{1,0:T(8,128)(2,1)S(1)}, bf16[40,1024]{1,0:T(8,128)(2,1)S(1)}, u32[]{:S(2)}, u32[]{:S(2)}) %collective-permute-start.5) | collective-permute-done | bytes 81952 | tf_op jit(solution)/shard_map/ppermute | solution.py:319
  26.0 1.6 %shard_map.90 = (bf16[80,1024]{1,0:T(8,128)(2,1)S(1)}, bf16[80,1024]{1,0:T(8,128)(2,1)S(1)}) custom-call(bf16[80,1024]{1,0:T(8,128)(2,1)S(1)} %shard_map.87.xn_a, bf16[40,1024]{1,0:T(8,128)(2,1)S(1)} %collective-permute-done.8.p2.p1, bf16[40,1024]{1,0:T(8,128)(2,1)S(1)} %get-tuple-element.66.p3.p1, bf16[3,1024,256]{2,1,0:T(8,128)(2,1)S(1)} %bitcast.9, ...), custom_call_target="tpu_custom_call" | custom-call | flops 1000000000 | bytes 4882432 | tf_op jit(solution)/shard_map/pallas_call | solution.py:299
  27.9 1.4 %collective-permute-start.14 = (bf16[80,1024]{1,0:T(8,128)(2,1)S(1)}, bf16[80,1024]{1,0:T(8,128)(2,1)S(1)}, u32[]{:S(2)}, u32[]{:S(2)}) collective-permute-start(bf16[80,1024]{1,0:T(8,128)(2,1)S(1)} %get-tuple-element.79.mine), channel_id=1, source_target_pairs={{0,2},{1,3},{2,0},{3,1},{4,6},{5,7},{6,4},{7,5},{8,10},{9,11},{10,... | collective-permute-start | bytes 491528 | tf_op jit(solution)/shard_map/ppermute | solution.py:319
  29.3 2.7 %collective-permute-done.10.other = bf16[80,1024]{1,0:T(8,128)(2,1)S(1)} collective-permute-done((bf16[80,1024]{1,0:T(8,128)(2,1)S(1)}, bf16[80,1024]{1,0:T(8,128)(2,1)S(1)}, u32[]{:S(2)}, u32[]{:S(2)}) %collective-permute-start.10) | collective-permute-done | bytes 163872 | tf_op jit(solution)/shard_map/ppermute | solution.py:319
  32.0 1.8 %shard_map.91.mine = bf16[80,1024]{1,0:T(8,128)(2,1)S(1)} custom-call(bf16[80,1024]{1,0:T(8,128)(2,1)S(1)} %get-tuple-element.72.mine, bf16[80,1024]{1,0:T(8,128)(2,1)S(1)} %collective-permute-done.10.other, bf16[40,1024]{1,0:T(8,128)(2,1)S(1)} %collective-permute-done.6.p1.p0, bf16[40,1024]{1,0:T(8,128)(2,1)S(1)} %collective-permute-done.8.p2.p1, ...), custom_call_target="tpu_custom_call" | custom-call | flops 1000000000 | bytes 9043968 | tf_op jit(solution)/shard_map/pallas_call | solution.py:299
  34.3 1.8 %shard_map.93.mine = bf16[80,1024]{1,0:T(8,128)(2,1)S(1)} custom-call(bf16[80,1024]{1,0:T(8,128)(2,1)S(1)} %get-tuple-element.79.mine, bf16[80,1024]{1,0:T(8,128)(2,1)S(1)} %collective-permute-done.14.other, bf16[40,1024]{1,0:T(8,128)(2,1)S(1)} %collective-permute-done.5.p0, bf16[40,1024]{1,0:T(8,128)(2,1)S(1)} %get-tuple-element.66.p3.p1, ...), custom_call_target="tpu_custom_call" | custom-call | flops 1000000000 | bytes 9043968 | tf_op jit(solution)/shard_map/pallas_call | solution.py:299
  36.1 1.2 %collective-permute-start.17 = (bf16[80,1024]{1,0:T(8,128)(2,1)S(1)}, bf16[80,1024]{1,0:T(8,128)(2,1)S(1)}, u32[]{:S(2)}, u32[]{:S(2)}) collective-permute-start(bf16[80,1024]{1,0:T(8,128)(2,1)S(1)} %shard_map.93.mine), channel_id=1, source_target_pairs={{0,2},{1,3},{2,0},{3,1},{4,6},{5,7},{6,4},{7,5},{8,10},{9,11},{10,... | collective-permute-start | bytes 491528 | tf_op jit(solution)/shard_map/ppermute | solution.py:319
  37.3 1.7 %collective-permute-done.13.other = bf16[80,1024]{1,0:T(8,128)(2,1)S(1)} collective-permute-done((bf16[80,1024]{1,0:T(8,128)(2,1)S(1)}, bf16[80,1024]{1,0:T(8,128)(2,1)S(1)}, u32[]{:S(2)}, u32[]{:S(2)}) %collective-permute-start.13) | collective-permute-done | bytes 163872 | tf_op jit(solution)/shard_map/ppermute | solution.py:319
  39.1 1.3 %collective-permute-start.15 = (bf16[40,1024]{1,0:T(8,128)(2,1)S(1)}, bf16[40,1024]{1,0:T(8,128)(2,1)S(1)}, u32[]{:S(2)}, u32[]{:S(2)}) collective-permute-start(bf16[40,1024]{1,0:T(8,128)(2,1)S(1)} %get-tuple-element.80), channel_id=1, source_target_pairs={{4,0},{5,1},{6,2},{7,3},{8,4},{9,5},{10,6},{11,7},{12,8},{13,9},{1... | collective-permute-start | bytes 245768 | tf_op jit(solution)/shard_map/ppermute | solution.py:319
  40.4 1.3 %collective-permute-start.16 = (bf16[40,1024]{1,0:T(8,128)(2,1)S(1)}, bf16[40,1024]{1,0:T(8,128)(2,1)S(1)}, u32[]{:S(2)}, u32[]{:S(2)}) collective-permute-start(bf16[40,1024]{1,0:T(8,128)(2,1)S(1)} %get-tuple-element.81), channel_id=1, source_target_pairs={{32,0},{33,1},{34,2},{35,3},{36,4},{37,5},{38,6},{39,7},{40,8},{41... | collective-permute-start | bytes 245768 | tf_op jit(solution)/shard_map/ppermute | solution.py:319
  41.7 1.3 %collective-permute-start.18 = (bf16[40,1024]{1,0:T(8,128)(2,1)S(1)}, bf16[40,1024]{1,0:T(8,128)(2,1)S(1)}, u32[]{:S(2)}, u32[]{:S(2)}) collective-permute-start(bf16[40,1024]{1,0:T(8,128)(2,1)S(1)} %get-tuple-element.84), channel_id=1, source_target_pairs={{36,0},{37,1},{38,2},{39,3},{40,4},{41,5},{42,6},{43,7},{44,8},{45... | collective-permute-start | bytes 245768 | tf_op jit(solution)/shard_map/ppermute | solution.py:319
  43.0 11.3 %collective-permute-start.21 = (bf16[40,1024]{1,0:T(8,128)(2,1)S(1)}, bf16[40,1024]{1,0:T(8,128)(2,1)S(1)}, u32[]{:S(2)}, u32[]{:S(2)}) collective-permute-start(bf16[40,1024]{1,0:T(8,128)(2,1)S(1)} %get-tuple-element.84), channel_id=1, source_target_pairs={{0,254},{1,255},{2,252},{3,253},{4,224},{5,225},{6,226},{7,227},{8... | collective-permute-start | bytes 245768 | tf_op jit(solution)/shard_map/ppermute | solution.py:319
  54.3 3.5 %collective-permute-start.19 = (bf16[40,1024]{1,0:T(8,128)(2,1)S(1)}, bf16[40,1024]{1,0:T(8,128)(2,1)S(1)}, u32[]{:S(2)}, u32[]{:S(2)}) collective-permute-start(bf16[40,1024]{1,0:T(8,128)(2,1)S(1)} %get-tuple-element.80), channel_id=1, source_target_pairs={{0,30},{1,31},{2,28},{3,29},{32,62},{33,63},{34,60},{35,61},{64,94... | collective-permute-start | bytes 245768 | tf_op jit(solution)/shard_map/ppermute | solution.py:319
  57.8 1.4 %collective-permute-start.20 = (bf16[40,1024]{1,0:T(8,128)(2,1)S(1)}, bf16[40,1024]{1,0:T(8,128)(2,1)S(1)}, u32[]{:S(2)}, u32[]{:S(2)}) collective-permute-start(bf16[40,1024]{1,0:T(8,128)(2,1)S(1)} %get-tuple-element.81), channel_id=1, source_target_pairs={{0,224},{1,225},{2,226},{3,227},{4,228},{5,229},{6,230},{7,231},{8... | collective-permute-start | bytes 245768 | tf_op jit(solution)/shard_map/ppermute | solution.py:319
  59.3 1.4 %collective-permute-done.20.lat_around = bf16[40,1024]{1,0:T(8,128)(2,1)S(1)} collective-permute-done((bf16[40,1024]{1,0:T(8,128)(2,1)S(1)}, bf16[40,1024]{1,0:T(8,128)(2,1)S(1)}, u32[]{:S(2)}, u32[]{:S(2)}) %collective-permute-start.20) | collective-permute-done | bytes 81952 | tf_op jit(solution)/shard_map/ppermute | solution.py:319
  60.8 6.5 %collective-permute-start.22 = (bf16[160,1024]{1,0:T(8,128)(2,1)S(1)}, bf16[160,1024]{1,0:T(8,128)(2,1)S(1)}, u32[]{:S(2)}, u32[]{:S(2)}) collective-permute-start(bf16[160,1024]{1,0:T(8,128)(2,1)S(1)} %shard_map.96.mine), channel_id=1, source_target_pairs={{0,1},{1,0},{2,3},{3,2},{4,5},{5,4},{6,7},{7,6},{8,9},{9,8},{10,11... | collective-permute-start | bytes 983048 | tf_op jit(solution)/shard_map/ppermute | solution.py:319
  67.3 1.3 %collective-permute-done.22.other = bf16[160,1024]{1,0:T(8,128)(2,1)S(1)} collective-permute-done((bf16[160,1024]{1,0:T(8,128)(2,1)S(1)}, bf16[160,1024]{1,0:T(8,128)(2,1)S(1)}, u32[]{:S(2)}, u32[]{:S(2)}) %collective-permute-start.22) | collective-permute-done | bytes 327712 | tf_op jit(solution)/shard_map/ppermute | solution.py:319
  68.6 1.3 %shard_map.97 = bf16[72,4,1024]{2,1,0:T(4,128)(2,1)} custom-call(bf16[160,1024]{1,0:T(8,128)(2,1)S(1)} %shard_map.96.mine, bf16[160,1024]{1,0:T(8,128)(2,1)S(1)} %collective-permute-done.22.other), custom_call_target="tpu_custom_call" | custom-call | flops 200000000 | bytes 1245184 | tf_op jit(solution)/shard_map/pallas_call | solution.py:299
  (48 shorter events, 3.8 us)
Async XLA Ops:
  0.0 5.2 %copy-start.5 = (bf16[1024,3,256]{2,0,1:T(8,128)(2,1)S(1)}, bf16[1024,3,256]{2,0,1:T(8,128)(2,1)}, u32[]{:S(2)}) copy-start(bf16[1024,3,256]{2,0,1:T(8,128)(2,1)} %param.9) | copy-start | bytes 4718596
  0.0 5.2 %copy-start.6 = (bf16[4,6,12,1024]{3,0,2,1:T(4,128)(2,1)S(1)}, bf16[4,6,12,1024]{3,0,2,1:T(4,128)(2,1)}, u32[]{:S(2)}) copy-start(bf16[4,6,12,1024]{3,0,2,1:T(4,128)(2,1)} %param.8) | copy-start | bytes 1769476
  0.0 8.0 %collective-permute-start.2 = (bf16[3,1024,256]{2,1,0:T(8,128)(2,1)}, bf16[3,1024,256]{2,1,0:T(8,128)(2,1)S(1)}, u32[]{:S(2)}, u32[]{:S(2)}) collective-permute-start(bf16[3,1024,256]{2,1,0:T(8,128)(2,1)} %bitcast.8), channel_id=1, source_target_pairs={{0,1},{1,0},{2,3},{3,2},{4,5},{5,4},{6,7},{7,6},{8,9},{9,8},{10,11... | collective-permute-start | bytes 4718600 | tf_op jit(solution)/shard_map/ppermute | solution.py:319
  3.2 4.0 %collective-permute-start = (bf16[256,1024]{1,0:T(8,128)(2,1)}, bf16[256,1024]{1,0:T(8,128)(2,1)S(1)}, u32[]{:S(2)}, u32[]{:S(2)}) collective-permute-start(bf16[256,1024]{1,0:T(8,128)(2,1)} %w0.1), channel_id=1, source_target_pairs={{0,1},{1,0},{2,3},{3,2},{4,5},{5,4},{6,7},{7,6},{8,9},{9,8},{10,11... | collective-permute-start | bytes 1572872 | tf_op jit(solution)/shard_map/ppermute | solution.py:319
  3.2 4.7 %collective-permute-start.1 = (bf16[256,1024]{1,0:T(8,128)(2,1)}, bf16[256,1024]{1,0:T(8,128)(2,1)S(1)}, u32[]{:S(2)}, u32[]{:S(2)}) collective-permute-start(bf16[256,1024]{1,0:T(8,128)(2,1)} %o_own.1), channel_id=1, source_target_pairs={{0,1},{1,0},{2,3},{3,2},{4,5},{5,4},{6,7},{7,6},{8,9},{9,8},{10,11... | collective-permute-start | bytes 1572872 | tf_op jit(solution)/shard_map/ppermute | solution.py:319
  3.8 0.7 copy-start.7
  5.2 3.2 %copy-start.8 = (f32[2,4,37]{2,1,0:T(4,128)S(1)}, f32[2,4,37]{2,1,0:T(4,128)}, u32[]{:S(2)}) copy-start(f32[2,4,37]{2,1,0:T(4,128)} %refs_0_.2) | copy-start | bytes 3556
  5.2 4.1 %copy-start.4 = (bf16[256,1024]{1,0:T(8,128)(2,1)S(1)}, bf16[256,1024]{1,0:T(8,128)(2,1)}, u32[]{:S(2)}) copy-start(bf16[256,1024]{1,0:T(8,128)(2,1)} %w0.1) | copy-start | bytes 1572868
  8.0 1.3 %collective-permute-start.3 = (bf16[160,256]{1,0:T(8,128)(2,1)S(1)}, bf16[160,256]{1,0:T(8,128)(2,1)S(1)}, u32[]{:S(2)}, u32[]{:S(2)}) collective-permute-start(bf16[160,256]{1,0:T(8,128)(2,1)S(1)} %get-tuple-element.52), channel_id=1, source_target_pairs={{0,1},{1,0},{2,3},{3,2},{4,5},{5,4},{6,7},{7,6},{8,9},{9,8},{10,11... | collective-permute-start | bytes 245768 | tf_op jit(solution)/shard_map/ppermute | solution.py:319
  8.4 3.3 %collective-permute-start.9 = (f32[2,4,37]{2,1,0:T(4,128)S(1)}, f32[2,4,37]{2,1,0:T(4,128)S(1)}, u32[]{:S(2)}, u32[]{:S(2)}) collective-permute-start(f32[2,4,37]{2,1,0:T(4,128)S(1)} %copy-done.8), channel_id=1, source_target_pairs={{0,1},{1,0},{2,3},{3,2},{4,5},{5,4},{6,7},{7,6},{8,9},{9,8},{10,11... | collective-permute-start | bytes 3560 | tf_op jit(solution)/shard_map/ppermute | solution.py:319
  9.6 5.5 %collective-permute-start.4 = (bf16[80,1024]{1,0:T(8,128)(2,1)S(1)}, bf16[80,1024]{1,0:T(8,128)(2,1)S(1)}, u32[]{:S(2)}, u32[]{:S(2)}) collective-permute-start(bf16[80,1024]{1,0:T(8,128)(2,1)S(1)} %get-tuple-element.55.mine), channel_id=1, source_target_pairs={{0,2},{1,3},{2,0},{3,1},{4,6},{5,7},{6,4},{7,5},{8,10},{9,11},{10,... | collective-permute-start | bytes 491528 | tf_op jit(solution)/shard_map/ppermute | solution.py:319
  9.7 8.9 %collective-permute-start.7 = (bf16[80,1024]{1,0:T(8,128)(2,1)S(1)}, bf16[80,1024]{1,0:T(8,128)(2,1)S(1)}, u32[]{:S(2)}, u32[]{:S(2)}) collective-permute-start(bf16[80,1024]{1,0:T(8,128)(2,1)S(1)} %get-tuple-element.63.mine), channel_id=1, source_target_pairs={{0,2},{1,3},{2,0},{3,1},{4,6},{5,7},{6,4},{7,5},{8,10},{9,11},{10,... | collective-permute-start | bytes 491528 | tf_op jit(solution)/shard_map/ppermute | solution.py:319
  11.2 3.1 %copy-start.1 = (bf16[1024,1024]{1,0:T(8,128)(2,1)S(1)}, bf16[1024,1024]{1,0:T(8,128)(2,1)}, u32[]{:S(2)}) copy-start(bf16[1024,1024]{1,0:T(8,128)(2,1)} %d0.3) | copy-start | bytes 6291460
  11.6 1.8 %copy-start = (bf16[1024,1024]{1,0:T(8,128)(2,1)S(1)}, bf16[1024,1024]{1,0:T(8,128)(2,1)}, u32[]{:S(2)}) copy-start(bf16[1024,1024]{1,0:T(8,128)(2,1)} %u0.3) | copy-start | bytes 6291460
  13.4 18.6 %collective-permute-start.11 = (bf16[1024,1024]{1,0:T(8,128)(2,1)S(1)}, bf16[1024,1024]{1,0:T(8,128)(2,1)S(1)}, u32[]{:S(2)}, u32[]{:S(2)}) collective-permute-start(bf16[1024,1024]{1,0:T(8,128)(2,1)S(1)} %copy-done), channel_id=1, source_target_pairs={{0,1},{1,0},{2,3},{3,2},{4,5},{5,4},{6,7},{7,6},{8,9},{9,8},{10,11... | collective-permute-start | bytes 6291464 | tf_op jit(solution)/shard_map/ppermute | solution.py:319
  14.3 17.7 %collective-permute-start.12 = (bf16[1024,1024]{1,0:T(8,128)(2,1)S(1)}, bf16[1024,1024]{1,0:T(8,128)(2,1)S(1)}, u32[]{:S(2)}, u32[]{:S(2)}) collective-permute-start(bf16[1024,1024]{1,0:T(8,128)(2,1)S(1)} %copy-done.1), channel_id=1, source_target_pairs={{0,1},{1,0},{2,3},{3,2},{4,5},{5,4},{6,7},{7,6},{8,9},{9,8},{10,11... | collective-permute-start | bytes 6291464 | tf_op jit(solution)/shard_map/ppermute | solution.py:319
  15.2 10.5 %collective-permute-start.5 = (bf16[40,1024]{1,0:T(8,128)(2,1)S(1)}, bf16[40,1024]{1,0:T(8,128)(2,1)S(1)}, u32[]{:S(2)}, u32[]{:S(2)}) collective-permute-start(bf16[40,1024]{1,0:T(8,128)(2,1)S(1)} %get-tuple-element.61), channel_id=1, source_target_pairs={{0,36},{1,37},{2,38},{3,39},{4,40},{5,41},{6,42},{7,43},{8,44},{9,... | collective-permute-start | bytes 245768 | tf_op jit(solution)/shard_map/ppermute | solution.py:319
  16.2 9.5 %collective-permute-start.6 = (bf16[40,1024]{1,0:T(8,128)(2,1)S(1)}, bf16[40,1024]{1,0:T(8,128)(2,1)S(1)}, u32[]{:S(2)}, u32[]{:S(2)}) collective-permute-start(bf16[40,1024]{1,0:T(8,128)(2,1)S(1)} %get-tuple-element.62), channel_id=1, source_target_pairs={{0,4},{1,5},{2,6},{3,7},{4,8},{5,9},{6,10},{7,11},{8,12},{9,13},{1... | collective-permute-start | bytes 245768 | tf_op jit(solution)/shard_map/ppermute | solution.py:319
  18.8 7.2 %copy-start.2 = (bf16[1024,3,256]{2,0,1:T(8,128)(2,1)S(1)}, bf16[1024,3,256]{2,0,1:T(8,128)(2,1)}, u32[]{:S(2)}) copy-start(bf16[1024,3,256]{2,0,1:T(8,128)(2,1)} %param.10) | copy-start | bytes 4718596
  18.8 7.2 %copy-start.3 = (bf16[256,1024]{1,0:T(8,128)(2,1)S(1)}, bf16[256,1024]{1,0:T(8,128)(2,1)}, u32[]{:S(2)}) copy-start(bf16[256,1024]{1,0:T(8,128)(2,1)} %o_own.1) | copy-start | bytes 1572868
  18.8 7.2 %collective-permute-start.8 = (bf16[40,1024]{1,0:T(8,128)(2,1)S(1)}, bf16[40,1024]{1,0:T(8,128)(2,1)S(1)}, u32[]{:S(2)}, u32[]{:S(2)}) collective-permute-start(bf16[40,1024]{1,0:T(8,128)(2,1)S(1)} %get-tuple-element.65), channel_id=1, source_target_pairs={{0,32},{1,33},{2,34},{3,35},{4,36},{5,37},{6,38},{7,39},{8,40},{9,... | collective-permute-start | bytes 245768 | tf_op jit(solution)/shard_map/ppermute | solution.py:319
  27.6 4.4 %collective-permute-start.10 = (bf16[80,1024]{1,0:T(8,128)(2,1)S(1)}, bf16[80,1024]{1,0:T(8,128)(2,1)S(1)}, u32[]{:S(2)}, u32[]{:S(2)}) collective-permute-start(bf16[80,1024]{1,0:T(8,128)(2,1)S(1)} %get-tuple-element.72.mine), channel_id=1, source_target_pairs={{0,2},{1,3},{2,0},{3,1},{4,6},{5,7},{6,4},{7,5},{8,10},{9,11},{10,... | collective-permute-start | bytes 491528 | tf_op jit(solution)/shard_map/ppermute | solution.py:319
  27.9 6.4 %collective-permute-start.14 = (bf16[80,1024]{1,0:T(8,128)(2,1)S(1)}, bf16[80,1024]{1,0:T(8,128)(2,1)S(1)}, u32[]{:S(2)}, u32[]{:S(2)}) collective-permute-start(bf16[80,1024]{1,0:T(8,128)(2,1)S(1)} %get-tuple-element.79.mine), channel_id=1, source_target_pairs={{0,2},{1,3},{2,0},{3,1},{4,6},{5,7},{6,4},{7,5},{8,10},{9,11},{10,... | collective-permute-start | bytes 491528 | tf_op jit(solution)/shard_map/ppermute | solution.py:319
  33.8 5.2 %collective-permute-start.13 = (bf16[80,1024]{1,0:T(8,128)(2,1)S(1)}, bf16[80,1024]{1,0:T(8,128)(2,1)S(1)}, u32[]{:S(2)}, u32[]{:S(2)}) collective-permute-start(bf16[80,1024]{1,0:T(8,128)(2,1)S(1)} %shard_map.91.mine), channel_id=1, source_target_pairs={{0,2},{1,3},{2,0},{3,1},{4,6},{5,7},{6,4},{7,5},{8,10},{9,11},{10,... | collective-permute-start | bytes 491528 | tf_op jit(solution)/shard_map/ppermute | solution.py:319
  36.1 5.6 %collective-permute-start.17 = (bf16[80,1024]{1,0:T(8,128)(2,1)S(1)}, bf16[80,1024]{1,0:T(8,128)(2,1)S(1)}, u32[]{:S(2)}, u32[]{:S(2)}) collective-permute-start(bf16[80,1024]{1,0:T(8,128)(2,1)S(1)} %shard_map.93.mine), channel_id=1, source_target_pairs={{0,2},{1,3},{2,0},{3,1},{4,6},{5,7},{6,4},{7,5},{8,10},{9,11},{10,... | collective-permute-start | bytes 491528 | tf_op jit(solution)/shard_map/ppermute | solution.py:319
  39.1 18.8 %collective-permute-start.15 = (bf16[40,1024]{1,0:T(8,128)(2,1)S(1)}, bf16[40,1024]{1,0:T(8,128)(2,1)S(1)}, u32[]{:S(2)}, u32[]{:S(2)}) collective-permute-start(bf16[40,1024]{1,0:T(8,128)(2,1)S(1)} %get-tuple-element.80), channel_id=1, source_target_pairs={{4,0},{5,1},{6,2},{7,3},{8,4},{9,5},{10,6},{11,7},{12,8},{13,9},{1... | collective-permute-start | bytes 245768 | tf_op jit(solution)/shard_map/ppermute | solution.py:319
  40.4 18.9 %collective-permute-start.16 = (bf16[40,1024]{1,0:T(8,128)(2,1)S(1)}, bf16[40,1024]{1,0:T(8,128)(2,1)S(1)}, u32[]{:S(2)}, u32[]{:S(2)}) collective-permute-start(bf16[40,1024]{1,0:T(8,128)(2,1)S(1)} %get-tuple-element.81), channel_id=1, source_target_pairs={{32,0},{33,1},{34,2},{35,3},{36,4},{37,5},{38,6},{39,7},{40,8},{41... | collective-permute-start | bytes 245768 | tf_op jit(solution)/shard_map/ppermute | solution.py:319
  41.7 17.6 %collective-permute-start.18 = (bf16[40,1024]{1,0:T(8,128)(2,1)S(1)}, bf16[40,1024]{1,0:T(8,128)(2,1)S(1)}, u32[]{:S(2)}, u32[]{:S(2)}) collective-permute-start(bf16[40,1024]{1,0:T(8,128)(2,1)S(1)} %get-tuple-element.84), channel_id=1, source_target_pairs={{36,0},{37,1},{38,2},{39,3},{40,4},{41,5},{42,6},{43,7},{44,8},{45... | collective-permute-start | bytes 245768 | tf_op jit(solution)/shard_map/ppermute | solution.py:319
  43.0 16.3 %collective-permute-start.21 = (bf16[40,1024]{1,0:T(8,128)(2,1)S(1)}, bf16[40,1024]{1,0:T(8,128)(2,1)S(1)}, u32[]{:S(2)}, u32[]{:S(2)}) collective-permute-start(bf16[40,1024]{1,0:T(8,128)(2,1)S(1)} %get-tuple-element.84), channel_id=1, source_target_pairs={{0,254},{1,255},{2,252},{3,253},{4,224},{5,225},{6,226},{7,227},{8... | collective-permute-start | bytes 245768 | tf_op jit(solution)/shard_map/ppermute | solution.py:319
  54.3 5.0 %collective-permute-start.19 = (bf16[40,1024]{1,0:T(8,128)(2,1)S(1)}, bf16[40,1024]{1,0:T(8,128)(2,1)S(1)}, u32[]{:S(2)}, u32[]{:S(2)}) collective-permute-start(bf16[40,1024]{1,0:T(8,128)(2,1)S(1)} %get-tuple-element.80), channel_id=1, source_target_pairs={{0,30},{1,31},{2,28},{3,29},{32,62},{33,63},{34,60},{35,61},{64,94... | collective-permute-start | bytes 245768 | tf_op jit(solution)/shard_map/ppermute | solution.py:319
  57.8 2.9 %collective-permute-start.20 = (bf16[40,1024]{1,0:T(8,128)(2,1)S(1)}, bf16[40,1024]{1,0:T(8,128)(2,1)S(1)}, u32[]{:S(2)}, u32[]{:S(2)}) collective-permute-start(bf16[40,1024]{1,0:T(8,128)(2,1)S(1)} %get-tuple-element.81), channel_id=1, source_target_pairs={{0,224},{1,225},{2,226},{3,227},{4,228},{5,229},{6,230},{7,231},{8... | collective-permute-start | bytes 245768 | tf_op jit(solution)/shard_map/ppermute | solution.py:319
  60.8 7.8 %collective-permute-start.22 = (bf16[160,1024]{1,0:T(8,128)(2,1)S(1)}, bf16[160,1024]{1,0:T(8,128)(2,1)S(1)}, u32[]{:S(2)}, u32[]{:S(2)}) collective-permute-start(bf16[160,1024]{1,0:T(8,128)(2,1)S(1)} %shard_map.96.mine), channel_id=1, source_target_pairs={{0,1},{1,0},{2,3},{3,2},{4,5},{5,4},{6,7},{7,6},{8,9},{9,8},{10,11... | collective-permute-start | bytes 983048 | tf_op jit(solution)/shard_map/ppermute | solution.py:319

commit v13 on v11

--- a/solution.py
+++ b/solution.py
@@ -76,9 +76,9 @@
 
 
 def kept_place(index):
-    quad = (index * 205) >> 13
-    slot = index - quad * ROWS
-    return (quad, slot) + piece_place(slot)
+    piece = (index * 205) >> 13
+    slot = index - piece * ROWS
+    return (piece ^ 2, slot) + piece_place(slot)
 
 
 def real_level(level, core):
@@ -273,8 +273,8 @@
 
 def place_kernel(m0, m1, s0, s1, out):
     core = core_index()
-    piece, slot, level, row, col = kept_place(iota((1, KEPT), 1))
-    quad = jnp.where(piece < 2, piece + 1, jnp.where(piece == 2, 0, piece))
+    quad, slot, level, row, col = kept_place(iota((1, KEPT), 1))
+    quad = jnp.where(quad == 2, 3, jnp.where(quad == 3, 0, jnp.where(quad == 0, 2, 1)))
     row, col = patch_place(quad, row, col)
     total = None
     for chosen, parts in ((core, (m0, m1)), (1 - core, (s0, s1))):
@@ -318,10 +318,10 @@
         return move(value, lambda a, b, m: (a, b, m ^ 2))
 
     def out_to(value, dy, dx):
-        return move(value, lambda a, b, m: (a + dy, b + dx, m ^ 2 if dx and (b + 1) % turn == 0 else m))
+        return move(value, lambda a, b, m: (a + dy, b - dx, m ^ 2 if dx and b % turn == 0 else m))
 
     def home(value, dy, dx):
-        return move(value, lambda a, b, m: (a - dy, b - dx, m ^ 2 if dx and b % turn == 0 else m))
+        return move(value, lambda a, b, m: (a - dy, b + dx, m ^ 2 if dx and (b + 1) % turn == 0 else m))
 
     half, piece = [(HALF, width)], [(ROWS, width)]
     heads, features = [(KEPT, 256)], [(FEAT, 256)]
@@ -336,7 +336,7 @@
     s_table = core_swap(rel_tables)
     bias1 = call(functools.partial(bias_kernel, 0), features, (rel_tables,), 5 * 10**9, 4, table=True)
     keep, give = call(first_kernel, heads * 2, (tok, w_first, bias1), 10**9, 16)
-    keep, give, f1, s1, w_sib, s_table = tied(keep, give, f1, s1, w_sib, s_table)
+    keep, give, f1, s1, w_sib = tied(keep, give, f1, s1, w_sib)
     keep, tok, rel_tables = tied(keep, tok, rel_tables)
     base_a, base_b = call(base_kernel, half * 2, (tok,), 10**9, 8)
     bias2, bias2_sib = call(

time: 57.9 us -> 58.9 us (1.017)
  starting transfers between devices: 25.5 us -> 27.7 us
  waiting for transfers between devices: 19.2 us -> 17.9 us
    ppermute x21, starting transfers between devices: 25.5 us -> 27.7 us  [move(): return lax.ppermute(value, AXES, pairs(counts, target))]
    ppermute x21, waiting for transfers between devices: 19.2 us -> 17.9 us  [move(): return lax.ppermute(value, AXES, pairs(counts, target))]
where the time goes in v13:
time: 58.9 us; the launch traced here: 58.8 us
  starting transfers between devices  27.7 us (47%)
  waiting for transfers between devices  17.9 us (30%)
  Pallas kernels  11.4 us (19%)
  local copies, waits for them, and re-layouts  1.63 us (3%)
    ppermute x21, starting transfers between devices, move(): return lax.ppermute(value, AXES, pairs(counts, target))  27.7 us
    ppermute x21, waiting for transfers between devices, move(): return lax.ppermute(value, AXES, pairs(counts, target))  17.9 us
    pallas_call x16, Pallas kernels, call(): pl.pallas_call(kernel, out_shape=shapes, in_specs=[pl.BlockSpec(memory_sp...  11.4 us
    unnamed x18, local copies, waits for them, and re-layouts  1.63 us
  transfers between devices with their start and end apart: 21, of which 11 were waited for; matrix products, arithmetic and copies ran while one was open for 0% of the time, Pallas kernels for 17%

profile of v13, /device:TPU:1, one launch (start us, length us, event | category | flops | bytes accessed | tf_op | source)
XLA Modules:
  0.0 58.8 jit_solution(6070874111687349773)
XLA Ops:
  0.0 3.2 %collective-permute-start.2 = (bf16[3,1024,256]{2,1,0:T(8,128)(2,1)}, bf16[3,1024,256]{2,1,0:T(8,128)(2,1)S(1)}, u32[]{:S(2)}, u32[]{:S(2)}) collective-permute-start(bf16[3,1024,256]{2,1,0:T(8,128)(2,1)} %bitcast.8), channel_id=1, source_target_pairs={{0,1},{1,0},{2,3},{3,2},{4,5},{5,4},{6,7},{7,6},{8,9},{9,8},{10,11... | collective-permute-start | bytes 4718600 | tf_op jit(solution)/shard_map/ppermute | solution.py:312
  3.2 0.5 collective-permute-start.1
  3.8 0.7 %copy-done.7 = f32[2,4,37]{2,1,0:T(4,128)S(1)} copy-done((f32[2,4,37]{2,1,0:T(4,128)S(1)}, f32[2,4,37]{2,1,0:T(4,128)}, u32[]{:S(2)}) %copy-start.7) | copy-done | bytes 1208
  4.4 0.7 %shard_map.82.bias = bf16[32,256]{1,0:T(8,128)(2,1)S(1)} custom-call(f32[2,4,37]{2,1,0:T(4,128)S(1)} %copy-done.7), custom_call_target="tpu_custom_call" | custom-call | flops 5000000000 | bytes 17568 | tf_op jit(solution)/shard_map/pallas_call | solution.py:292
  5.2 2.0 %shard_map.83 = (bf16[160,256]{1,0:T(8,128)(2,1)S(1)}, bf16[160,256]{1,0:T(8,128)(2,1)S(1)}) custom-call(bf16[72,4,1024]{2,1,0:T(4,128)(2,1)S(1)} %bitcast.11, bf16[3,1024,256]{2,1,0:T(8,128)(2,1)S(1)} %bitcast.10, bf16[32,256]{1,0:T(8,128)(2,1)S(1)} %shard_map.82.bias), custom_call_target="tpu_custom_call" | custom-call | flops 1000000000 | bytes 2342912 | tf_op jit(solution)/shard_map/pallas_call | solution.py:292
  7.3 0.7 %collective-permute-done.1.o_sib = bf16[256,1024]{1,0:T(8,128)(2,1)S(1)} collective-permute-done((bf16[256,1024]{1,0:T(8,128)(2,1)}, bf16[256,1024]{1,0:T(8,128)(2,1)S(1)}, u32[]{:S(2)}, u32[]{:S(2)}) %collective-permute-start.1) | collective-permute-done | bytes 524320 | tf_op jit(solution)/shard_map/ppermute | solution.py:312
  8.5 0.8 %collective-permute-done.3.o1 = bf16[160,256]{1,0:T(8,128)(2,1)S(1)} collective-permute-done((bf16[160,256]{1,0:T(8,128)(2,1)S(1)}, bf16[160,256]{1,0:T(8,128)(2,1)S(1)}, u32[]{:S(2)}, u32[]{:S(2)}) %collective-permute-start.3) | collective-permute-done | bytes 81952 | tf_op jit(solution)/shard_map/ppermute | solution.py:312
  9.7 1.5 %collective-permute-start.7 = (bf16[80,1024]{1,0:T(8,128)(2,1)S(1)}, bf16[80,1024]{1,0:T(8,128)(2,1)S(1)}, u32[]{:S(2)}, u32[]{:S(2)}) collective-permute-start(bf16[80,1024]{1,0:T(8,128)(2,1)S(1)} %get-tuple-element.60.mine), channel_id=1, source_target_pairs={{0,2},{1,3},{2,0},{3,1},{4,6},{5,7},{6,4},{7,5},{8,10},{9,11},{10,... | collective-permute-start | bytes 491528 | tf_op jit(solution)/shard_map/ppermute | solution.py:312
  11.6 0.9 %shard_map.89 = (bf16[32,256]{1,0:T(8,128)(2,1)S(1)}, bf16[32,256]{1,0:T(8,128)(2,1)S(1)}) custom-call(f32[2,4,37]{2,1,0:T(4,128)S(1)} %copy-done.8, f32[2,4,37]{2,1,0:T(4,128)S(1)} %collective-permute-done.9.refs_1_), custom_call_target="tpu_custom_call" | custom-call | flops 1000000000 | bytes 35136 | tf_op jit(solution)/shard_map/pallas_call | solution.py:292
  12.5 0.9 %copy-done = bf16[1024,1024]{1,0:T(8,128)(2,1)S(1)} copy-done((bf16[1024,1024]{1,0:T(8,128)(2,1)S(1)}, bf16[1024,1024]{1,0:T(8,128)(2,1)}, u32[]{:S(2)}) %copy-start) | copy-done | bytes 2097176
  13.4 0.9 %collective-permute-start.11 = (bf16[1024,1024]{1,0:T(8,128)(2,1)S(1)}, bf16[1024,1024]{1,0:T(8,128)(2,1)S(1)}, u32[]{:S(2)}, u32[]{:S(2)}) collective-permute-start(bf16[1024,1024]{1,0:T(8,128)(2,1)S(1)} %copy-done), channel_id=1, source_target_pairs={{0,1},{1,0},{2,3},{3,2},{4,5},{5,4},{6,7},{7,6},{8,9},{9,8},{10,11... | collective-permute-start | bytes 6291464 | tf_op jit(solution)/shard_map/ppermute | solution.py:312
  14.3 0.8 %collective-permute-done.4.other = bf16[80,1024]{1,0:T(8,128)(2,1)S(1)} collective-permute-done((bf16[80,1024]{1,0:T(8,128)(2,1)S(1)}, bf16[80,1024]{1,0:T(8,128)(2,1)S(1)}, u32[]{:S(2)}, u32[]{:S(2)}) %collective-permute-start.4) | collective-permute-done | bytes 163872 | tf_op jit(solution)/shard_map/ppermute | solution.py:312
  15.2 4.6 %collective-permute-start.5 = (bf16[40,1024]{1,0:T(8,128)(2,1)S(1)}, bf16[40,1024]{1,0:T(8,128)(2,1)S(1)}, u32[]{:S(2)}, u32[]{:S(2)}) collective-permute-start(bf16[40,1024]{1,0:T(8,128)(2,1)S(1)} %get-tuple-element.58), channel_id=1, source_target_pairs={{0,62},{1,63},{2,60},{3,61},{4,32},{5,33},{6,34},{7,35},{8,36},{9,... | collective-permute-start | bytes 245768 | tf_op jit(solution)/shard_map/ppermute | solution.py:312
  19.9 0.5 collective-permute-start.6
  20.4 1.7 %collective-permute-start.8 = (bf16[40,1024]{1,0:T(8,128)(2,1)S(1)}, bf16[40,1024]{1,0:T(8,128)(2,1)S(1)}, u32[]{:S(2)}, u32[]{:S(2)}) collective-permute-start(bf16[40,1024]{1,0:T(8,128)(2,1)S(1)} %get-tuple-element.62), channel_id=1, source_target_pairs={{0,32},{1,33},{2,34},{3,35},{4,36},{5,37},{6,38},{7,39},{8,40},{9,... | collective-permute-start | bytes 245768 | tf_op jit(solution)/shard_map/ppermute | solution.py:312
  22.2 1.3 %collective-permute-done.6.p1.p0 = bf16[40,1024]{1,0:T(8,128)(2,1)S(1)} collective-permute-done((bf16[40,1024]{1,0:T(8,128)(2,1)S(1)}, bf16[40,1024]{1,0:T(8,128)(2,1)S(1)}, u32[]{:S(2)}, u32[]{:S(2)}) %collective-permute-start.6) | collective-permute-done | bytes 81952 | tf_op jit(solution)/shard_map/ppermute | solution.py:312
  23.7 2.5 %collective-permute-done.8.p2.p1 = bf16[40,1024]{1,0:T(8,128)(2,1)S(1)} collective-permute-done((bf16[40,1024]{1,0:T(8,128)(2,1)S(1)}, bf16[40,1024]{1,0:T(8,128)(2,1)S(1)}, u32[]{:S(2)}, u32[]{:S(2)}) %collective-permute-start.8) | collective-permute-done | bytes 81952 | tf_op jit(solution)/shard_map/ppermute | solution.py:312
  26.2 1.6 %shard_map.90 = (bf16[80,1024]{1,0:T(8,128)(2,1)S(1)}, bf16[80,1024]{1,0:T(8,128)(2,1)S(1)}) custom-call(bf16[80,1024]{1,0:T(8,128)(2,1)S(1)} %shard_map.87.xn_a, bf16[40,1024]{1,0:T(8,128)(2,1)S(1)} %collective-permute-done.8.p2.p1, bf16[40,1024]{1,0:T(8,128)(2,1)S(1)} %get-tuple-element.63.p3.p1, bf16[3,1024,256]{2,1,0:T(8,128)(2,1)S(1)} %bitcast.9, ...), custom_call_target="tpu_custom_call" | custom-call | flops 1000000000 | bytes 4882432 | tf_op jit(solution)/shard_map/pallas_call | solution.py:292
  28.1 1.5 %collective-permute-start.14 = (bf16[80,1024]{1,0:T(8,128)(2,1)S(1)}, bf16[80,1024]{1,0:T(8,128)(2,1)S(1)}, u32[]{:S(2)}, u32[]{:S(2)}) collective-permute-start(bf16[80,1024]{1,0:T(8,128)(2,1)S(1)} %get-tuple-element.76.mine), channel_id=1, source_target_pairs={{0,2},{1,3},{2,0},{3,1},{4,6},{5,7},{6,4},{7,5},{8,10},{9,11},{10,... | collective-permute-start | bytes 491528 | tf_op jit(solution)/shard_map/ppermute | solution.py:312
  29.5 2.7 %collective-permute-done.10.other = bf16[80,1024]{1,0:T(8,128)(2,1)S(1)} collective-permute-done((bf16[80,1024]{1,0:T(8,128)(2,1)S(1)}, bf16[80,1024]{1,0:T(8,128)(2,1)S(1)}, u32[]{:S(2)}, u32[]{:S(2)}) %collective-permute-start.10) | collective-permute-done | bytes 163872 | tf_op jit(solution)/shard_map/ppermute | solution.py:312
  32.2 1.8 %shard_map.91.mine = bf16[80,1024]{1,0:T(8,128)(2,1)S(1)} custom-call(bf16[80,1024]{1,0:T(8,128)(2,1)S(1)} %get-tuple-element.69.mine, bf16[80,1024]{1,0:T(8,128)(2,1)S(1)} %collective-permute-done.10.other, bf16[40,1024]{1,0:T(8,128)(2,1)S(1)} %collective-permute-done.6.p1.p0, bf16[40,1024]{1,0:T(8,128)(2,1)S(1)} %collective-permute-done.8.p2.p1, ...), custom_call_target="tpu_custom_call" | custom-call | flops 1000000000 | bytes 9043968 | tf_op jit(solution)/shard_map/pallas_call | solution.py:292
  34.1 1.8 %shard_map.93.mine = bf16[80,1024]{1,0:T(8,128)(2,1)S(1)} custom-call(bf16[80,1024]{1,0:T(8,128)(2,1)S(1)} %get-tuple-element.76.mine, bf16[80,1024]{1,0:T(8,128)(2,1)S(1)} %collective-permute-done.14.other, bf16[40,1024]{1,0:T(8,128)(2,1)S(1)} %collective-permute-done.5.p0, bf16[40,1024]{1,0:T(8,128)(2,1)S(1)} %get-tuple-element.63.p3.p1, ...), custom_call_target="tpu_custom_call" | custom-call | flops 1000000000 | bytes 9043968 | tf_op jit(solution)/shard_map/pallas_call | solution.py:292
  36.0 1.5 %collective-permute-start.17 = (bf16[80,1024]{1,0:T(8,128)(2,1)S(1)}, bf16[80,1024]{1,0:T(8,128)(2,1)S(1)}, u32[]{:S(2)}, u32[]{:S(2)}) collective-permute-start(bf16[80,1024]{1,0:T(8,128)(2,1)S(1)} %shard_map.93.mine), channel_id=1, source_target_pairs={{0,2},{1,3},{2,0},{3,1},{4,6},{5,7},{6,4},{7,5},{8,10},{9,11},{10,... | collective-permute-start | bytes 491528 | tf_op jit(solution)/shard_map/ppermute | solution.py:312
  37.5 1.8 %collective-permute-done.13.other = bf16[80,1024]{1,0:T(8,128)(2,1)S(1)} collective-permute-done((bf16[80,1024]{1,0:T(8,128)(2,1)S(1)}, bf16[80,1024]{1,0:T(8,128)(2,1)S(1)}, u32[]{:S(2)}, u32[]{:S(2)}) %collective-permute-start.13) | collective-permute-done | bytes 163872 | tf_op jit(solution)/shard_map/ppermute | solution.py:312
  39.3 0.5 collective-permute-start.15
  39.8 2.4 %collective-permute-start.16 = (bf16[40,1024]{1,0:T(8,128)(2,1)S(1)}, bf16[40,1024]{1,0:T(8,128)(2,1)S(1)}, u32[]{:S(2)}, u32[]{:S(2)}) collective-permute-start(bf16[40,1024]{1,0:T(8,128)(2,1)S(1)} %get-tuple-element.78), channel_id=1, source_target_pairs={{0,224},{1,225},{2,226},{3,227},{4,228},{5,229},{6,230},{7,231},{8... | collective-permute-start | bytes 245768 | tf_op jit(solution)/shard_map/ppermute | solution.py:312
  42.3 1.6 %collective-permute-start.18 = (bf16[40,1024]{1,0:T(8,128)(2,1)S(1)}, bf16[40,1024]{1,0:T(8,128)(2,1)S(1)}, u32[]{:S(2)}, u32[]{:S(2)}) collective-permute-start(bf16[40,1024]{1,0:T(8,128)(2,1)S(1)} %get-tuple-element.80), channel_id=1, source_target_pairs={{0,228},{1,229},{2,230},{3,231},{4,232},{5,233},{6,234},{7,235},{8... | collective-permute-start | bytes 245768 | tf_op jit(solution)/shard_map/ppermute | solution.py:312
  44.0 2.1 %collective-permute-done.15.p0 = bf16[40,1024]{1,0:T(8,128)(2,1)S(1)} collective-permute-done((bf16[40,1024]{1,0:T(8,128)(2,1)S(1)}, bf16[40,1024]{1,0:T(8,128)(2,1)S(1)}, u32[]{:S(2)}, u32[]{:S(2)}) %collective-permute-start.15) | collective-permute-done | bytes 81952 | tf_op jit(solution)/shard_map/ppermute | solution.py:312
  46.1 3.9 %collective-permute-done.18.p0 = bf16[40,1024]{1,0:T(8,128)(2,1)S(1)} collective-permute-done((bf16[40,1024]{1,0:T(8,128)(2,1)S(1)}, bf16[40,1024]{1,0:T(8,128)(2,1)S(1)}, u32[]{:S(2)}, u32[]{:S(2)}) %collective-permute-start.18) | collective-permute-done | bytes 81952 | tf_op jit(solution)/shard_map/ppermute | solution.py:312
  49.9 6.2 %collective-permute-start.20 = (bf16[80,1024]{1,0:T(8,128)(2,1)S(1)}, bf16[80,1024]{1,0:T(8,128)(2,1)S(1)}, u32[]{:S(2)}, u32[]{:S(2)}) collective-permute-start(bf16[80,1024]{1,0:T(8,128)(2,1)S(1)} %shard_map.96.m1), channel_id=1, source_target_pairs={{0,1},{1,0},{2,3},{3,2},{4,5},{5,4},{6,7},{7,6},{8,9},{9,8},{10,11... | collective-permute-start | bytes 491528 | tf_op jit(solution)/shard_map/ppermute | solution.py:312
  56.2 0.9 %collective-permute-done.20.s1 = bf16[80,1024]{1,0:T(8,128)(2,1)S(1)} collective-permute-done((bf16[80,1024]{1,0:T(8,128)(2,1)S(1)}, bf16[80,1024]{1,0:T(8,128)(2,1)S(1)}, u32[]{:S(2)}, u32[]{:S(2)}) %collective-permute-start.20) | collective-permute-done | bytes 163872 | tf_op jit(solution)/shard_map/ppermute | solution.py:312
  57.5 1.3 %shard_map.97 = bf16[72,4,1024]{2,1,0:T(4,128)(2,1)} custom-call(bf16[80,1024]{1,0:T(8,128)(2,1)S(1)} %shard_map.94.m0, bf16[80,1024]{1,0:T(8,128)(2,1)S(1)} %shard_map.96.m1, bf16[80,1024]{1,0:T(8,128)(2,1)S(1)} %collective-permute-done.19.s0, bf16[80,1024]{1,0:T(8,128)(2,1)S(1)} %collective-permute-done.20.s1), custom_call_target="tpu_custom_call" | custom-call | flops 200000000 | bytes 1245184 | tf_op jit(solution)/shard_map/pallas_call | solution.py:292
  (44 shorter events, 2.7 us)
Async XLA Ops:
  0.0 5.2 %copy-start.5 = (bf16[1024,3,256]{2,0,1:T(8,128)(2,1)S(1)}, bf16[1024,3,256]{2,0,1:T(8,128)(2,1)}, u32[]{:S(2)}) copy-start(bf16[1024,3,256]{2,0,1:T(8,128)(2,1)} %param.9) | copy-start | bytes 4718596
  0.0 5.2 %copy-start.6 = (bf16[4,6,12,1024]{3,0,2,1:T(4,128)(2,1)S(1)}, bf16[4,6,12,1024]{3,0,2,1:T(4,128)(2,1)}, u32[]{:S(2)}) copy-start(bf16[4,6,12,1024]{3,0,2,1:T(4,128)(2,1)} %param.8) | copy-start | bytes 1769476
  0.0 8.0 %collective-permute-start.2 = (bf16[3,1024,256]{2,1,0:T(8,128)(2,1)}, bf16[3,1024,256]{2,1,0:T(8,128)(2,1)S(1)}, u32[]{:S(2)}, u32[]{:S(2)}) collective-permute-start(bf16[3,1024,256]{2,1,0:T(8,128)(2,1)} %bitcast.8), channel_id=1, source_target_pairs={{0,1},{1,0},{2,3},{3,2},{4,5},{5,4},{6,7},{7,6},{8,9},{9,8},{10,11... | collective-permute-start | bytes 4718600 | tf_op jit(solution)/shard_map/ppermute | solution.py:312
  3.2 4.0 %collective-permute-start = (bf16[256,1024]{1,0:T(8,128)(2,1)}, bf16[256,1024]{1,0:T(8,128)(2,1)S(1)}, u32[]{:S(2)}, u32[]{:S(2)}) collective-permute-start(bf16[256,1024]{1,0:T(8,128)(2,1)} %w0.1), channel_id=1, source_target_pairs={{0,1},{1,0},{2,3},{3,2},{4,5},{5,4},{6,7},{7,6},{8,9},{9,8},{10,11... | collective-permute-start | bytes 1572872 | tf_op jit(solution)/shard_map/ppermute | solution.py:312
  3.2 4.7 %collective-permute-start.1 = (bf16[256,1024]{1,0:T(8,128)(2,1)}, bf16[256,1024]{1,0:T(8,128)(2,1)S(1)}, u32[]{:S(2)}, u32[]{:S(2)}) collective-permute-start(bf16[256,1024]{1,0:T(8,128)(2,1)} %o_own.1), channel_id=1, source_target_pairs={{0,1},{1,0},{2,3},{3,2},{4,5},{5,4},{6,7},{7,6},{8,9},{9,8},{10,11... | collective-permute-start | bytes 1572872 | tf_op jit(solution)/shard_map/ppermute | solution.py:312
  3.8 0.7 %copy-start.7 = (f32[2,4,37]{2,1,0:T(4,128)S(1)}, f32[2,4,37]{2,1,0:T(4,128)}, u32[]{:S(2)}) copy-start(f32[2,4,37]{2,1,0:T(4,128)} %refs_0_.2) | copy-start | bytes 3556
  5.2 3.2 %copy-start.8 = (f32[2,4,37]{2,1,0:T(4,128)S(1)}, f32[2,4,37]{2,1,0:T(4,128)}, u32[]{:S(2)}) copy-start(f32[2,4,37]{2,1,0:T(4,128)} %refs_0_.2) | copy-start | bytes 3556
  5.2 4.1 %copy-start.4 = (bf16[256,1024]{1,0:T(8,128)(2,1)S(1)}, bf16[256,1024]{1,0:T(8,128)(2,1)}, u32[]{:S(2)}) copy-start(bf16[256,1024]{1,0:T(8,128)(2,1)} %w0.1) | copy-start | bytes 1572868
  8.0 1.3 %collective-permute-start.3 = (bf16[160,256]{1,0:T(8,128)(2,1)S(1)}, bf16[160,256]{1,0:T(8,128)(2,1)S(1)}, u32[]{:S(2)}, u32[]{:S(2)}) collective-permute-start(bf16[160,256]{1,0:T(8,128)(2,1)S(1)} %get-tuple-element.49), channel_id=1, source_target_pairs={{0,1},{1,0},{2,3},{3,2},{4,5},{5,4},{6,7},{7,6},{8,9},{9,8},{10,11... | collective-permute-start | bytes 245768 | tf_op jit(solution)/shard_map/ppermute | solution.py:312
  8.4 3.3 %collective-permute-start.9 = (f32[2,4,37]{2,1,0:T(4,128)S(1)}, f32[2,4,37]{2,1,0:T(4,128)S(1)}, u32[]{:S(2)}, u32[]{:S(2)}) collective-permute-start(f32[2,4,37]{2,1,0:T(4,128)S(1)} %copy-done.8), channel_id=1, source_target_pairs={{0,1},{1,0},{2,3},{3,2},{4,5},{5,4},{6,7},{7,6},{8,9},{9,8},{10,11... | collective-permute-start | bytes 3560 | tf_op jit(solution)/shard_map/ppermute | solution.py:312
  9.6 5.5 %collective-permute-start.4 = (bf16[80,1024]{1,0:T(8,128)(2,1)S(1)}, bf16[80,1024]{1,0:T(8,128)(2,1)S(1)}, u32[]{:S(2)}, u32[]{:S(2)}) collective-permute-start(bf16[80,1024]{1,0:T(8,128)(2,1)S(1)} %get-tuple-element.52.mine), channel_id=1, source_target_pairs={{0,2},{1,3},{2,0},{3,1},{4,6},{5,7},{6,4},{7,5},{8,10},{9,11},{10,... | collective-permute-start | bytes 491528 | tf_op jit(solution)/shard_map/ppermute | solution.py:312
  9.7 10.6 %collective-permute-start.7 = (bf16[80,1024]{1,0:T(8,128)(2,1)S(1)}, bf16[80,1024]{1,0:T(8,128)(2,1)S(1)}, u32[]{:S(2)}, u32[]{:S(2)}) collective-permute-start(bf16[80,1024]{1,0:T(8,128)(2,1)S(1)} %get-tuple-element.60.mine), channel_id=1, source_target_pairs={{0,2},{1,3},{2,0},{3,1},{4,6},{5,7},{6,4},{7,5},{8,10},{9,11},{10,... | collective-permute-start | bytes 491528 | tf_op jit(solution)/shard_map/ppermute | solution.py:312
  11.2 3.1 %copy-start.1 = (bf16[1024,1024]{1,0:T(8,128)(2,1)S(1)}, bf16[1024,1024]{1,0:T(8,128)(2,1)}, u32[]{:S(2)}) copy-start(bf16[1024,1024]{1,0:T(8,128)(2,1)} %d0.3) | copy-start | bytes 6291460
  11.6 1.8 %copy-start = (bf16[1024,1024]{1,0:T(8,128)(2,1)S(1)}, bf16[1024,1024]{1,0:T(8,128)(2,1)}, u32[]{:S(2)}) copy-start(bf16[1024,1024]{1,0:T(8,128)(2,1)} %u0.3) | copy-start | bytes 6291460
  13.4 18.8 %collective-permute-start.11 = (bf16[1024,1024]{1,0:T(8,128)(2,1)S(1)}, bf16[1024,1024]{1,0:T(8,128)(2,1)S(1)}, u32[]{:S(2)}, u32[]{:S(2)}) collective-permute-start(bf16[1024,1024]{1,0:T(8,128)(2,1)S(1)} %copy-done), channel_id=1, source_target_pairs={{0,1},{1,0},{2,3},{3,2},{4,5},{5,4},{6,7},{7,6},{8,9},{9,8},{10,11... | collective-permute-start | bytes 6291464 | tf_op jit(solution)/shard_map/ppermute | solution.py:312
  14.3 17.9 %collective-permute-start.12 = (bf16[1024,1024]{1,0:T(8,128)(2,1)S(1)}, bf16[1024,1024]{1,0:T(8,128)(2,1)S(1)}, u32[]{:S(2)}, u32[]{:S(2)}) collective-permute-start(bf16[1024,1024]{1,0:T(8,128)(2,1)S(1)} %copy-done.1), channel_id=1, source_target_pairs={{0,1},{1,0},{2,3},{3,2},{4,5},{5,4},{6,7},{7,6},{8,9},{9,8},{10,11... | collective-permute-start | bytes 6291464 | tf_op jit(solution)/shard_map/ppermute | solution.py:312
  15.2 6.9 %collective-permute-start.5 = (bf16[40,1024]{1,0:T(8,128)(2,1)S(1)}, bf16[40,1024]{1,0:T(8,128)(2,1)S(1)}, u32[]{:S(2)}, u32[]{:S(2)}) collective-permute-start(bf16[40,1024]{1,0:T(8,128)(2,1)S(1)} %get-tuple-element.58), channel_id=1, source_target_pairs={{0,62},{1,63},{2,60},{3,61},{4,32},{5,33},{6,34},{7,35},{8,36},{9,... | collective-permute-start | bytes 245768 | tf_op jit(solution)/shard_map/ppermute | solution.py:312
  19.9 3.6 %collective-permute-start.6 = (bf16[40,1024]{1,0:T(8,128)(2,1)S(1)}, bf16[40,1024]{1,0:T(8,128)(2,1)S(1)}, u32[]{:S(2)}, u32[]{:S(2)}) collective-permute-start(bf16[40,1024]{1,0:T(8,128)(2,1)S(1)} %get-tuple-element.59), channel_id=1, source_target_pairs={{0,30},{1,31},{2,28},{3,29},{4,0},{5,1},{6,2},{7,3},{8,4},{9,5},{1... | collective-permute-start | bytes 245768 | tf_op jit(solution)/shard_map/ppermute | solution.py:312
  20.4 5.8 %copy-start.2 = (bf16[1024,3,256]{2,0,1:T(8,128)(2,1)S(1)}, bf16[1024,3,256]{2,0,1:T(8,128)(2,1)}, u32[]{:S(2)}) copy-start(bf16[1024,3,256]{2,0,1:T(8,128)(2,1)} %param.10) | copy-start | bytes 4718596
  20.4 5.8 %copy-start.3 = (bf16[256,1024]{1,0:T(8,128)(2,1)S(1)}, bf16[256,1024]{1,0:T(8,128)(2,1)}, u32[]{:S(2)}) copy-start(bf16[256,1024]{1,0:T(8,128)(2,1)} %o_own.1) | copy-start | bytes 1572868
  20.4 5.8 %collective-permute-start.8 = (bf16[40,1024]{1,0:T(8,128)(2,1)S(1)}, bf16[40,1024]{1,0:T(8,128)(2,1)S(1)}, u32[]{:S(2)}, u32[]{:S(2)}) collective-permute-start(bf16[40,1024]{1,0:T(8,128)(2,1)S(1)} %get-tuple-element.62), channel_id=1, source_target_pairs={{0,32},{1,33},{2,34},{3,35},{4,36},{5,37},{6,38},{7,39},{8,40},{9,... | collective-permute-start | bytes 245768 | tf_op jit(solution)/shard_map/ppermute | solution.py:312
  27.8 4.4 %collective-permute-start.10 = (bf16[80,1024]{1,0:T(8,128)(2,1)S(1)}, bf16[80,1024]{1,0:T(8,128)(2,1)S(1)}, u32[]{:S(2)}, u32[]{:S(2)}) collective-permute-start(bf16[80,1024]{1,0:T(8,128)(2,1)S(1)} %get-tuple-element.69.mine), channel_id=1, source_target_pairs={{0,2},{1,3},{2,0},{3,1},{4,6},{5,7},{6,4},{7,5},{8,10},{9,11},{10,... | collective-permute-start | bytes 491528 | tf_op jit(solution)/shard_map/ppermute | solution.py:312
  28.1 6.1 %collective-permute-start.14 = (bf16[80,1024]{1,0:T(8,128)(2,1)S(1)}, bf16[80,1024]{1,0:T(8,128)(2,1)S(1)}, u32[]{:S(2)}, u32[]{:S(2)}) collective-permute-start(bf16[80,1024]{1,0:T(8,128)(2,1)S(1)} %get-tuple-element.76.mine), channel_id=1, source_target_pairs={{0,2},{1,3},{2,0},{3,1},{4,6},{5,7},{6,4},{7,5},{8,10},{9,11},{10,... | collective-permute-start | bytes 491528 | tf_op jit(solution)/shard_map/ppermute | solution.py:312
  34.0 5.3 %collective-permute-start.13 = (bf16[80,1024]{1,0:T(8,128)(2,1)S(1)}, bf16[80,1024]{1,0:T(8,128)(2,1)S(1)}, u32[]{:S(2)}, u32[]{:S(2)}) collective-permute-start(bf16[80,1024]{1,0:T(8,128)(2,1)S(1)} %shard_map.91.mine), channel_id=1, source_target_pairs={{0,2},{1,3},{2,0},{3,1},{4,6},{5,7},{6,4},{7,5},{8,10},{9,11},{10,... | collective-permute-start | bytes 491528 | tf_op jit(solution)/shard_map/ppermute | solution.py:312
  36.0 6.3 %collective-permute-start.17 = (bf16[80,1024]{1,0:T(8,128)(2,1)S(1)}, bf16[80,1024]{1,0:T(8,128)(2,1)S(1)}, u32[]{:S(2)}, u32[]{:S(2)}) collective-permute-start(bf16[80,1024]{1,0:T(8,128)(2,1)S(1)} %shard_map.93.mine), channel_id=1, source_target_pairs={{0,2},{1,3},{2,0},{3,1},{4,6},{5,7},{6,4},{7,5},{8,10},{9,11},{10,... | collective-permute-start | bytes 491528 | tf_op jit(solution)/shard_map/ppermute | solution.py:312
  39.3 6.7 %collective-permute-start.15 = (bf16[40,1024]{1,0:T(8,128)(2,1)S(1)}, bf16[40,1024]{1,0:T(8,128)(2,1)S(1)}, u32[]{:S(2)}, u32[]{:S(2)}) collective-permute-start(bf16[40,1024]{1,0:T(8,128)(2,1)S(1)} %get-tuple-element.77), channel_id=1, source_target_pairs={{0,4},{1,5},{2,6},{3,7},{4,8},{5,9},{6,10},{7,11},{8,12},{9,13},{1... | collective-permute-start | bytes 245768 | tf_op jit(solution)/shard_map/ppermute | solution.py:312
  39.8 6.2 %collective-permute-start.16 = (bf16[40,1024]{1,0:T(8,128)(2,1)S(1)}, bf16[40,1024]{1,0:T(8,128)(2,1)S(1)}, u32[]{:S(2)}, u32[]{:S(2)}) collective-permute-start(bf16[40,1024]{1,0:T(8,128)(2,1)S(1)} %get-tuple-element.78), channel_id=1, source_target_pairs={{0,224},{1,225},{2,226},{3,227},{4,228},{5,229},{6,230},{7,231},{8... | collective-permute-start | bytes 245768 | tf_op jit(solution)/shard_map/ppermute | solution.py:312
  42.3 7.6 %collective-permute-start.18 = (bf16[40,1024]{1,0:T(8,128)(2,1)S(1)}, bf16[40,1024]{1,0:T(8,128)(2,1)S(1)}, u32[]{:S(2)}, u32[]{:S(2)}) collective-permute-start(bf16[40,1024]{1,0:T(8,128)(2,1)S(1)} %get-tuple-element.80), channel_id=1, source_target_pairs={{0,228},{1,229},{2,230},{3,231},{4,232},{5,233},{6,234},{7,235},{8... | collective-permute-start | bytes 245768 | tf_op jit(solution)/shard_map/ppermute | solution.py:312
  49.9 7.2 %collective-permute-start.20 = (bf16[80,1024]{1,0:T(8,128)(2,1)S(1)}, bf16[80,1024]{1,0:T(8,128)(2,1)S(1)}, u32[]{:S(2)}, u32[]{:S(2)}) collective-permute-start(bf16[80,1024]{1,0:T(8,128)(2,1)S(1)} %shard_map.96.m1), channel_id=1, source_target_pairs={{0,1},{1,0},{2,3},{3,2},{4,5},{5,4},{6,7},{7,6},{8,9},{9,8},{10,11... | collective-permute-start | bytes 491528 | tf_op jit(solution)/shard_map/ppermute | solution.py:312
  56.1 1.4 %collective-permute-start.19 = (bf16[80,1024]{1,0:T(8,128)(2,1)S(1)}, bf16[80,1024]{1,0:T(8,128)(2,1)S(1)}, u32[]{:S(2)}, u32[]{:S(2)}) collective-permute-start(bf16[80,1024]{1,0:T(8,128)(2,1)S(1)} %shard_map.94.m0), channel_id=1, source_target_pairs={{0,1},{1,0},{2,3},{3,2},{4,5},{5,4},{6,7},{7,6},{8,9},{9,8},{10,11... | collective-permute-start | bytes 491528 | tf_op jit(solution)/shard_map/ppermute | solution.py:312

commit v14 on v11

--- a/solution.py
+++ b/solution.py
@@ -108,10 +108,9 @@
     return jnp.where((lane & FEAT) != 0, total - high, high).astype(jnp.bfloat16)
 
 
-def bias_kernel(block, *refs):
-    for table, out in zip(refs[: len(refs) // 2], refs[len(refs) // 2 :]):
-        for pair in range(2):
-            out[:, pair * 128 : pair * 128 + 128] = bias_rows(table, block, pair)
+def bias_kernel(block, table, out):
+    for pair in range(2):
+        out[:, pair * 128 : pair * 128 + 128] = bias_rows(table, block, pair)
 
 
 def features(level, row, col, used, count):
@@ -244,8 +243,7 @@
     heads = attend(parts, feat)
     total = dot(jnp.concatenate(heads[:2], axis=1), o_own[...])
     total = total + dot(jnp.concatenate(heads[2:], axis=1), o_sib[...])
-    outs[0][...] = total[ROWS : 3 * ROWS].astype(jnp.bfloat16)
-    outs[1][...] = jnp.concatenate([total[:ROWS], total[3 * ROWS :]], axis=0).astype(jnp.bfloat16)
+    store_halves(total, outs)
 
 
 def gelu(x):
@@ -273,8 +271,7 @@
 
 def place_kernel(m0, m1, s0, s1, out):
     core = core_index()
-    piece, slot, level, row, col = kept_place(iota((1, KEPT), 1))
-    quad = jnp.where(piece < 2, piece + 1, jnp.where(piece == 2, 0, piece))
+    quad, slot, level, row, col = kept_place(iota((1, KEPT), 1))
     row, col = patch_place(quad, row, col)
     total = None
     for chosen, parts in ((core, (m0, m1)), (1 - core, (s0, s1))):
@@ -333,21 +330,20 @@
     f1 = core_swap(out_first)
     s1 = core_swap(out_second)
     w_sib = core_swap(w_second)
-    s_table = core_swap(rel_tables)
     bias1 = call(functools.partial(bias_kernel, 0), features, (rel_tables,), 5 * 10**9, 4, table=True)
     keep, give = call(first_kernel, heads * 2, (tok, w_first, bias1), 10**9, 16)
-    keep, give, f1, s1, w_sib, s_table = tied(keep, give, f1, s1, w_sib, s_table)
+    keep, give, f1, s1, w_sib = tied(keep, give, f1, s1, w_sib)
     keep, tok, rel_tables = tied(keep, tok, rel_tables)
     base_a, base_b = call(base_kernel, half * 2, (tok,), 10**9, 8)
-    bias2, bias2_sib = call(
-        functools.partial(bias_kernel, 1), features * 2, (rel_tables, s_table), 10**9, 4, table=True
-    )
+    bias2 = call(functools.partial(bias_kernel, 1), features, (rel_tables,), 10**9, 4, table=True)
+    bias2_sib = core_swap(bias2)
     given, up_late, down_late = tied(core_swap(give), up_weight, down_weight)
     u1 = core_swap(up_late)
     d1 = core_swap(down_late)
     part_a, part_b = call(partial_kernel, half * 2, (keep, given, out_first, f1), 2 * 10**8, 8)
     other_a = chip_swap(part_a)
     other_b = chip_swap(part_b)
+    other_a, bias2_sib = tied(other_a, bias2_sib)
     diag, lon = call(residual_kernel, piece * 2, (part_a, other_a, base_a), 10**6, 8)
     diag, lon, part_b = tied(diag, lon, part_b)
     lat, own = call(residual_kernel, piece * 2, (part_b, other_b, base_b), 10**10, 8)
@@ -366,20 +362,20 @@
     other_a = chip_swap(part_a)
     other_b = chip_swap(part_b)
     mlp = (up_weight, u1, down_weight, d1)
-    part_a = call(mlp_kernel, half, (part_a, other_a, lon, lat, *mlp), 10**9, 20)
+    part_a = call(mlp_kernel, half, (part_a, other_a, diag, lon, *mlp), 10**9, 20)
     part_a, part_b = tied(part_a, part_b)
     other_a = chip_swap(part_a)
-    part_b = call(mlp_kernel, half, (part_b, other_b, diag, own, *mlp), 10**9, 20)
+    part_b = call(mlp_kernel, half, (part_b, other_b, lat, own, *mlp), 10**9, 20)
     other_b = chip_swap(part_b)
-    lon, lat = call(sum_kernel, piece * 2, (part_a, other_a), 10**6, 8)
-    lon, lat, part_b = tied(lon, lat, part_b)
+    diag, lon = call(sum_kernel, piece * 2, (part_a, other_a), 10**6, 8)
+    diag, lon, part_b = tied(diag, lon, part_b)
+    diag = home(diag, 1, 1)
     lon = home(lon, 0, 1)
+    lat, own = call(sum_kernel, piece * 2, (part_b, other_b), 10**10, 8)
     lat = home(lat, 1, 0)
-    diag, own = call(sum_kernel, piece * 2, (part_b, other_b), 10**10, 8)
-    diag = home(diag, 1, 1)
-    mine_a = call(join_kernel, half, (lon, lat), 10**10, 8)
-    mine_a, diag, own = tied(mine_a, diag, own)
-    mine_b = call(join_kernel, half, (diag, own), 10**6, 8)
+    mine_a = call(join_kernel, half, (diag, lon), 10**10, 8)
+    mine_a, lat, own = tied(mine_a, lat, own)
+    mine_b = call(join_kernel, half, (lat, own), 10**6, 8)
     result = call(
         place_kernel,
         [(rows * cols, levels, width)],

time: 57.9 us -> 58 us (level)
  starting transfers between devices: 25.5 us -> 26.8 us
  local copies, waits for them, and re-layouts: 1.63 us -> 0.88 us
    ppermute x21, starting transfers between devices: 25.5 us -> 26.8 us  [move(): return lax.ppermute(value, AXES, pairs(counts, target))]
    unnamed x18, local copies, waits for them, and re-layouts: 1.63 us -> 0.88 us
  transfers between devices with their start and end apart: 21 -> 21, of which waited for: 11 -> 12; matrix products, arithmetic and copies ran while one was open for 0% -> 0% of each run, Pallas kernels for 17% -> 17%
where the time goes in v14:
time: 58 us; the launch traced here: 57.9 us
  starting transfers between devices  26.8 us (46%)
  waiting for transfers between devices  18.8 us (32%)
  Pallas kernels  11.2 us (19%)
  local copies, waits for them, and re-layouts  0.88 us (2%)
    ppermute x21, starting transfers between devices, move(): return lax.ppermute(value, AXES, pairs(counts, target))  26.8 us
    ppermute x21, waiting for transfers between devices, move(): return lax.ppermute(value, AXES, pairs(counts, target))  18.8 us
    pallas_call x16, Pallas kernels, call(): pl.pallas_call(kernel, out_shape=shapes, in_specs=[pl.BlockSpec(memory_sp...  11.2 us
  transfers between devices with their start and end apart: 21, of which 12 were waited for; matrix products, arithmetic and copies ran while one was open for 0% of the time, Pallas kernels for 17%

profile of v14, /device:TPU:1, one launch (start us, length us, event | category | flops | bytes accessed | tf_op | source)
XLA Modules:
  0.0 57.9 jit_solution(15310623468252866008)
XLA Ops:
  0.0 3.2 %collective-permute-start.2 = (bf16[3,1024,256]{2,1,0:T(8,128)(2,1)}, bf16[3,1024,256]{2,1,0:T(8,128)(2,1)S(1)}, u32[]{:S(2)}, u32[]{:S(2)}) collective-permute-start(bf16[3,1024,256]{2,1,0:T(8,128)(2,1)} %bitcast.8), channel_id=1, source_target_pairs={{0,1},{1,0},{2,3},{3,2},{4,5},{5,4},{6,7},{7,6},{8,9},{9,8},{10,11... | collective-permute-start | bytes 4718600 | tf_op jit(solution)/shard_map/ppermute | solution.py:309
  3.2 0.5 collective-permute-start.1
  3.8 0.7 %copy-done.7 = f32[2,4,37]{2,1,0:T(4,128)S(1)} copy-done((f32[2,4,37]{2,1,0:T(4,128)S(1)}, f32[2,4,37]{2,1,0:T(4,128)}, u32[]{:S(2)}) %copy-start.7) | copy-done | bytes 1208
  4.4 0.7 %shard_map.82.bias = bf16[32,256]{1,0:T(8,128)(2,1)S(1)} custom-call(f32[2,4,37]{2,1,0:T(4,128)S(1)} %copy-done.7), custom_call_target="tpu_custom_call" | custom-call | flops 5000000000 | bytes 17568 | tf_op jit(solution)/shard_map/pallas_call | solution.py:289
  5.2 2.1 %shard_map.83 = (bf16[160,256]{1,0:T(8,128)(2,1)S(1)}, bf16[160,256]{1,0:T(8,128)(2,1)S(1)}) custom-call(bf16[72,4,1024]{2,1,0:T(4,128)(2,1)S(1)} %bitcast.11, bf16[3,1024,256]{2,1,0:T(8,128)(2,1)S(1)} %bitcast.10, bf16[32,256]{1,0:T(8,128)(2,1)S(1)} %shard_map.82.bias), custom_call_target="tpu_custom_call" | custom-call | flops 1000000000 | bytes 2342912 | tf_op jit(solution)/shard_map/pallas_call | solution.py:289
  7.3 0.7 %collective-permute-done.1.o_sib = bf16[256,1024]{1,0:T(8,128)(2,1)S(1)} collective-permute-done((bf16[256,1024]{1,0:T(8,128)(2,1)}, bf16[256,1024]{1,0:T(8,128)(2,1)S(1)}, u32[]{:S(2)}, u32[]{:S(2)}) %collective-permute-start.1) | collective-permute-done | bytes 524320 | tf_op jit(solution)/shard_map/ppermute | solution.py:309
  8.4 0.9 %collective-permute-done.3.o1 = bf16[160,256]{1,0:T(8,128)(2,1)S(1)} collective-permute-done((bf16[160,256]{1,0:T(8,128)(2,1)S(1)}, bf16[160,256]{1,0:T(8,128)(2,1)S(1)}, u32[]{:S(2)}, u32[]{:S(2)}) %collective-permute-start.3) | collective-permute-done | bytes 81952 | tf_op jit(solution)/shard_map/ppermute | solution.py:309
  9.7 1.5 %collective-permute-start.8 = (bf16[80,1024]{1,0:T(8,128)(2,1)S(1)}, bf16[80,1024]{1,0:T(8,128)(2,1)S(1)}, u32[]{:S(2)}, u32[]{:S(2)}) collective-permute-start(bf16[80,1024]{1,0:T(8,128)(2,1)S(1)} %get-tuple-element.62.mine), channel_id=1, source_target_pairs={{0,2},{1,3},{2,0},{3,1},{4,6},{5,7},{6,4},{7,5},{8,10},{9,11},{10,... | collective-permute-start | bytes 491528 | tf_op jit(solution)/shard_map/ppermute | solution.py:309
  11.2 0.7 %shard_map.85.b_own = bf16[32,256]{1,0:T(8,128)(2,1)S(1)} custom-call(f32[2,4,37]{2,1,0:T(4,128)S(1)} %copy-done.8), custom_call_target="tpu_custom_call" | custom-call | flops 1000000000 | bytes 17568 | tf_op jit(solution)/shard_map/pallas_call | solution.py:289
  11.9 1.0 %collective-permute-start.5 = (bf16[32,256]{1,0:T(8,128)(2,1)S(1)}, bf16[32,256]{1,0:T(8,128)(2,1)S(1)}, u32[]{:S(2)}, u32[]{:S(2)}) collective-permute-start(bf16[32,256]{1,0:T(8,128)(2,1)S(1)} %shard_map.85.b_own), channel_id=1, source_target_pairs={{0,1},{1,0},{2,3},{3,2},{4,5},{5,4},{6,7},{7,6},{8,9},{9,8},{10,11... | collective-permute-start | bytes 49160 | tf_op jit(solution)/shard_map/ppermute | solution.py:309
  13.5 0.9 %collective-permute-start.11 = (bf16[1024,1024]{1,0:T(8,128)(2,1)S(1)}, bf16[1024,1024]{1,0:T(8,128)(2,1)S(1)}, u32[]{:S(2)}, u32[]{:S(2)}) collective-permute-start(bf16[1024,1024]{1,0:T(8,128)(2,1)S(1)} %copy-done), channel_id=1, source_target_pairs={{0,1},{1,0},{2,3},{3,2},{4,5},{5,4},{6,7},{7,6},{8,9},{9,8},{10,11... | collective-permute-start | bytes 6291464 | tf_op jit(solution)/shard_map/ppermute | solution.py:309
  14.4 0.7 %collective-permute-done.4.other = bf16[80,1024]{1,0:T(8,128)(2,1)S(1)} collective-permute-done((bf16[80,1024]{1,0:T(8,128)(2,1)S(1)}, bf16[80,1024]{1,0:T(8,128)(2,1)S(1)}, u32[]{:S(2)}, u32[]{:S(2)}) %collective-permute-start.4) | collective-permute-done | bytes 163872 | tf_op jit(solution)/shard_map/ppermute | solution.py:309
  15.2 1.0 %collective-permute-start.6 = (bf16[40,1024]{1,0:T(8,128)(2,1)S(1)}, bf16[40,1024]{1,0:T(8,128)(2,1)S(1)}, u32[]{:S(2)}, u32[]{:S(2)}) collective-permute-start(bf16[40,1024]{1,0:T(8,128)(2,1)S(1)} %get-tuple-element.60), channel_id=1, source_target_pairs={{0,36},{1,37},{2,38},{3,39},{4,40},{5,41},{6,42},{7,43},{8,44},{9,... | collective-permute-start | bytes 245768 | tf_op jit(solution)/shard_map/ppermute | solution.py:309
  16.2 1.3 %collective-permute-start.7 = (bf16[40,1024]{1,0:T(8,128)(2,1)S(1)}, bf16[40,1024]{1,0:T(8,128)(2,1)S(1)}, u32[]{:S(2)}, u32[]{:S(2)}) collective-permute-start(bf16[40,1024]{1,0:T(8,128)(2,1)S(1)} %get-tuple-element.61), channel_id=1, source_target_pairs={{0,4},{1,5},{2,6},{3,7},{4,8},{5,9},{6,10},{7,11},{8,12},{9,13},{1... | collective-permute-start | bytes 245768 | tf_op jit(solution)/shard_map/ppermute | solution.py:309
  17.5 1.1 %collective-permute-done.8.other = bf16[80,1024]{1,0:T(8,128)(2,1)S(1)} collective-permute-done((bf16[80,1024]{1,0:T(8,128)(2,1)S(1)}, bf16[80,1024]{1,0:T(8,128)(2,1)S(1)}, u32[]{:S(2)}, u32[]{:S(2)}) %collective-permute-start.8) | collective-permute-done | bytes 163872 | tf_op jit(solution)/shard_map/ppermute | solution.py:309
  18.8 0.6 collective-permute-start.9
  19.4 6.4 %collective-permute-done.6.p0 = bf16[40,1024]{1,0:T(8,128)(2,1)S(1)} collective-permute-done((bf16[40,1024]{1,0:T(8,128)(2,1)S(1)}, bf16[40,1024]{1,0:T(8,128)(2,1)S(1)}, u32[]{:S(2)}, u32[]{:S(2)}) %collective-permute-start.6) | collective-permute-done | bytes 81952 | tf_op jit(solution)/shard_map/ppermute | solution.py:309
  26.0 1.6 %shard_map.90 = (bf16[80,1024]{1,0:T(8,128)(2,1)S(1)}, bf16[80,1024]{1,0:T(8,128)(2,1)S(1)}) custom-call(bf16[80,1024]{1,0:T(8,128)(2,1)S(1)} %shard_map.88.xn_a, bf16[40,1024]{1,0:T(8,128)(2,1)S(1)} %collective-permute-done.9.p2.p0, bf16[40,1024]{1,0:T(8,128)(2,1)S(1)} %get-tuple-element.65.p3.p1, bf16[3,1024,256]{2,1,0:T(8,128)(2,1)S(1)} %bitcast.9, ...), custom_call_target="tpu_custom_call" | custom-call | flops 1000000000 | bytes 4882432 | tf_op jit(solution)/shard_map/pallas_call | solution.py:289
  27.9 1.4 %collective-permute-start.14 = (bf16[80,1024]{1,0:T(8,128)(2,1)S(1)}, bf16[80,1024]{1,0:T(8,128)(2,1)S(1)}, u32[]{:S(2)}, u32[]{:S(2)}) collective-permute-start(bf16[80,1024]{1,0:T(8,128)(2,1)S(1)} %get-tuple-element.76.mine), channel_id=1, source_target_pairs={{0,2},{1,3},{2,0},{3,1},{4,6},{5,7},{6,4},{7,5},{8,10},{9,11},{10,... | collective-permute-start | bytes 491528 | tf_op jit(solution)/shard_map/ppermute | solution.py:309
  29.3 2.7 %collective-permute-done.10.other = bf16[80,1024]{1,0:T(8,128)(2,1)S(1)} collective-permute-done((bf16[80,1024]{1,0:T(8,128)(2,1)S(1)}, bf16[80,1024]{1,0:T(8,128)(2,1)S(1)}, u32[]{:S(2)}, u32[]{:S(2)}) %collective-permute-start.10) | collective-permute-done | bytes 163872 | tf_op jit(solution)/shard_map/ppermute | solution.py:309
  32.0 1.8 %shard_map.91.mine = bf16[80,1024]{1,0:T(8,128)(2,1)S(1)} custom-call(bf16[80,1024]{1,0:T(8,128)(2,1)S(1)} %get-tuple-element.69.mine, bf16[80,1024]{1,0:T(8,128)(2,1)S(1)} %collective-permute-done.10.other, bf16[40,1024]{1,0:T(8,128)(2,1)S(1)} %collective-permute-done.6.p0, bf16[40,1024]{1,0:T(8,128)(2,1)S(1)} %collective-permute-done.7.p1, ...), custom_call_target="tpu_custom_call" | custom-call | flops 1000000000 | bytes 9043968 | tf_op jit(solution)/shard_map/pallas_call | solution.py:289
  34.3 1.8 %shard_map.93.mine = bf16[80,1024]{1,0:T(8,128)(2,1)S(1)} custom-call(bf16[80,1024]{1,0:T(8,128)(2,1)S(1)} %get-tuple-element.76.mine, bf16[80,1024]{1,0:T(8,128)(2,1)S(1)} %collective-permute-done.14.other, bf16[40,1024]{1,0:T(8,128)(2,1)S(1)} %collective-permute-done.9.p2.p0, bf16[40,1024]{1,0:T(8,128)(2,1)S(1)} %get-tuple-element.65.p3.p1, ...), custom_call_target="tpu_custom_call" | custom-call | flops 1000000000 | bytes 9043968 | tf_op jit(solution)/shard_map/pallas_call | solution.py:289
  36.1 1.2 %collective-permute-start.17 = (bf16[80,1024]{1,0:T(8,128)(2,1)S(1)}, bf16[80,1024]{1,0:T(8,128)(2,1)S(1)}, u32[]{:S(2)}, u32[]{:S(2)}) collective-permute-start(bf16[80,1024]{1,0:T(8,128)(2,1)S(1)} %shard_map.93.mine), channel_id=1, source_target_pairs={{0,2},{1,3},{2,0},{3,1},{4,6},{5,7},{6,4},{7,5},{8,10},{9,11},{10,... | collective-permute-start | bytes 491528 | tf_op jit(solution)/shard_map/ppermute | solution.py:309
  37.3 1.7 %collective-permute-done.13.other = bf16[80,1024]{1,0:T(8,128)(2,1)S(1)} collective-permute-done((bf16[80,1024]{1,0:T(8,128)(2,1)S(1)}, bf16[80,1024]{1,0:T(8,128)(2,1)S(1)}, u32[]{:S(2)}, u32[]{:S(2)}) %collective-permute-start.13) | collective-permute-done | bytes 163872 | tf_op jit(solution)/shard_map/ppermute | solution.py:309
  39.1 5.0 %collective-permute-start.15 = (bf16[40,1024]{1,0:T(8,128)(2,1)S(1)}, bf16[40,1024]{1,0:T(8,128)(2,1)S(1)}, u32[]{:S(2)}, u32[]{:S(2)}) collective-permute-start(bf16[40,1024]{1,0:T(8,128)(2,1)S(1)} %get-tuple-element.77), channel_id=1, source_target_pairs={{0,254},{1,255},{2,252},{3,253},{4,224},{5,225},{6,226},{7,227},{8... | collective-permute-start | bytes 245768 | tf_op jit(solution)/shard_map/ppermute | solution.py:309
  44.1 1.0 %collective-permute-start.16 = (bf16[40,1024]{1,0:T(8,128)(2,1)S(1)}, bf16[40,1024]{1,0:T(8,128)(2,1)S(1)}, u32[]{:S(2)}, u32[]{:S(2)}) collective-permute-start(bf16[40,1024]{1,0:T(8,128)(2,1)S(1)} %get-tuple-element.78), channel_id=1, source_target_pairs={{0,30},{1,31},{2,28},{3,29},{4,0},{5,1},{6,2},{7,3},{8,4},{9,5},{1... | collective-permute-start | bytes 245768 | tf_op jit(solution)/shard_map/ppermute | solution.py:309
  45.1 0.8 %collective-permute-start.18 = (bf16[40,1024]{1,0:T(8,128)(2,1)S(1)}, bf16[40,1024]{1,0:T(8,128)(2,1)S(1)}, u32[]{:S(2)}, u32[]{:S(2)}) collective-permute-start(bf16[40,1024]{1,0:T(8,128)(2,1)S(1)} %get-tuple-element.80), channel_id=1, source_target_pairs={{0,224},{1,225},{2,226},{3,227},{4,228},{5,229},{6,230},{7,231},{8... | collective-permute-start | bytes 245768 | tf_op jit(solution)/shard_map/ppermute | solution.py:309
  45.9 1.8 %collective-permute-done.16.p1 = bf16[40,1024]{1,0:T(8,128)(2,1)S(1)} collective-permute-done((bf16[40,1024]{1,0:T(8,128)(2,1)S(1)}, bf16[40,1024]{1,0:T(8,128)(2,1)S(1)}, u32[]{:S(2)}, u32[]{:S(2)}) %collective-permute-start.16) | collective-permute-done | bytes 81952 | tf_op jit(solution)/shard_map/ppermute | solution.py:309
  47.7 1.1 %collective-permute-done.18.p0 = bf16[40,1024]{1,0:T(8,128)(2,1)S(1)} collective-permute-done((bf16[40,1024]{1,0:T(8,128)(2,1)S(1)}, bf16[40,1024]{1,0:T(8,128)(2,1)S(1)}, u32[]{:S(2)}, u32[]{:S(2)}) %collective-permute-start.18) | collective-permute-done | bytes 81952 | tf_op jit(solution)/shard_map/ppermute | solution.py:309
  48.8 6.5 %collective-permute-start.20 = (bf16[80,1024]{1,0:T(8,128)(2,1)S(1)}, bf16[80,1024]{1,0:T(8,128)(2,1)S(1)}, u32[]{:S(2)}, u32[]{:S(2)}) collective-permute-start(bf16[80,1024]{1,0:T(8,128)(2,1)S(1)} %shard_map.96.m1), channel_id=1, source_target_pairs={{0,1},{1,0},{2,3},{3,2},{4,5},{5,4},{6,7},{7,6},{8,9},{9,8},{10,11... | collective-permute-start | bytes 491528 | tf_op jit(solution)/shard_map/ppermute | solution.py:309
  55.3 0.9 %collective-permute-done.20.s1 = bf16[80,1024]{1,0:T(8,128)(2,1)S(1)} collective-permute-done((bf16[80,1024]{1,0:T(8,128)(2,1)S(1)}, bf16[80,1024]{1,0:T(8,128)(2,1)S(1)}, u32[]{:S(2)}, u32[]{:S(2)}) %collective-permute-start.20) | collective-permute-done | bytes 163872 | tf_op jit(solution)/shard_map/ppermute | solution.py:309
  56.6 1.3 %shard_map.97 = bf16[72,4,1024]{2,1,0:T(4,128)(2,1)} custom-call(bf16[80,1024]{1,0:T(8,128)(2,1)S(1)} %shard_map.94.m0, bf16[80,1024]{1,0:T(8,128)(2,1)S(1)} %shard_map.96.m1, bf16[80,1024]{1,0:T(8,128)(2,1)S(1)} %collective-permute-done.19.s0, bf16[80,1024]{1,0:T(8,128)(2,1)S(1)} %collective-permute-done.20.s1), custom_call_target="tpu_custom_call" | custom-call | flops 200000000 | bytes 1245184 | tf_op jit(solution)/shard_map/pallas_call | solution.py:289
  (44 shorter events, 3.2 us)
Async XLA Ops:
  0.0 5.2 %copy-start.5 = (bf16[1024,3,256]{2,0,1:T(8,128)(2,1)S(1)}, bf16[1024,3,256]{2,0,1:T(8,128)(2,1)}, u32[]{:S(2)}) copy-start(bf16[1024,3,256]{2,0,1:T(8,128)(2,1)} %param.9) | copy-start | bytes 4718596
  0.0 5.2 %copy-start.6 = (bf16[4,6,12,1024]{3,0,2,1:T(4,128)(2,1)S(1)}, bf16[4,6,12,1024]{3,0,2,1:T(4,128)(2,1)}, u32[]{:S(2)}) copy-start(bf16[4,6,12,1024]{3,0,2,1:T(4,128)(2,1)} %param.8) | copy-start | bytes 1769476
  0.0 8.0 %collective-permute-start.2 = (bf16[3,1024,256]{2,1,0:T(8,128)(2,1)}, bf16[3,1024,256]{2,1,0:T(8,128)(2,1)S(1)}, u32[]{:S(2)}, u32[]{:S(2)}) collective-permute-start(bf16[3,1024,256]{2,1,0:T(8,128)(2,1)} %bitcast.8), channel_id=1, source_target_pairs={{0,1},{1,0},{2,3},{3,2},{4,5},{5,4},{6,7},{7,6},{8,9},{9,8},{10,11... | collective-permute-start | bytes 4718600 | tf_op jit(solution)/shard_map/ppermute | solution.py:309
  3.2 4.0 %collective-permute-start = (bf16[256,1024]{1,0:T(8,128)(2,1)}, bf16[256,1024]{1,0:T(8,128)(2,1)S(1)}, u32[]{:S(2)}, u32[]{:S(2)}) collective-permute-start(bf16[256,1024]{1,0:T(8,128)(2,1)} %w0.1), channel_id=1, source_target_pairs={{0,1},{1,0},{2,3},{3,2},{4,5},{5,4},{6,7},{7,6},{8,9},{9,8},{10,11... | collective-permute-start | bytes 1572872 | tf_op jit(solution)/shard_map/ppermute | solution.py:309
  3.2 4.7 %collective-permute-start.1 = (bf16[256,1024]{1,0:T(8,128)(2,1)}, bf16[256,1024]{1,0:T(8,128)(2,1)S(1)}, u32[]{:S(2)}, u32[]{:S(2)}) collective-permute-start(bf16[256,1024]{1,0:T(8,128)(2,1)} %o_own.1), channel_id=1, source_target_pairs={{0,1},{1,0},{2,3},{3,2},{4,5},{5,4},{6,7},{7,6},{8,9},{9,8},{10,11... | collective-permute-start | bytes 1572872 | tf_op jit(solution)/shard_map/ppermute | solution.py:309
  3.8 0.7 %copy-start.7 = (f32[2,4,37]{2,1,0:T(4,128)S(1)}, f32[2,4,37]{2,1,0:T(4,128)}, u32[]{:S(2)}) copy-start(f32[2,4,37]{2,1,0:T(4,128)} %table.2) | copy-start | bytes 3556
  5.2 4.1 %copy-start.4 = (bf16[256,1024]{1,0:T(8,128)(2,1)S(1)}, bf16[256,1024]{1,0:T(8,128)(2,1)}, u32[]{:S(2)}) copy-start(bf16[256,1024]{1,0:T(8,128)(2,1)} %w0.1) | copy-start | bytes 1572868
  5.2 6.0 %copy-start.8 = (f32[2,4,37]{2,1,0:T(4,128)S(1)}, f32[2,4,37]{2,1,0:T(4,128)}, u32[]{:S(2)}) copy-start(f32[2,4,37]{2,1,0:T(4,128)} %table.2) | copy-start | bytes 3556
  8.0 1.3 %collective-permute-start.3 = (bf16[160,256]{1,0:T(8,128)(2,1)S(1)}, bf16[160,256]{1,0:T(8,128)(2,1)S(1)}, u32[]{:S(2)}, u32[]{:S(2)}) collective-permute-start(bf16[160,256]{1,0:T(8,128)(2,1)S(1)} %get-tuple-element.49), channel_id=1, source_target_pairs={{0,1},{1,0},{2,3},{3,2},{4,5},{5,4},{6,7},{7,6},{8,9},{9,8},{10,11... | collective-permute-start | bytes 245768 | tf_op jit(solution)/shard_map/ppermute | solution.py:309
  9.6 5.5 %collective-permute-start.4 = (bf16[80,1024]{1,0:T(8,128)(2,1)S(1)}, bf16[80,1024]{1,0:T(8,128)(2,1)S(1)}, u32[]{:S(2)}, u32[]{:S(2)}) collective-permute-start(bf16[80,1024]{1,0:T(8,128)(2,1)S(1)} %get-tuple-element.52.mine), channel_id=1, source_target_pairs={{0,2},{1,3},{2,0},{3,1},{4,6},{5,7},{6,4},{7,5},{8,10},{9,11},{10,... | collective-permute-start | bytes 491528 | tf_op jit(solution)/shard_map/ppermute | solution.py:309
  9.7 8.9 %collective-permute-start.8 = (bf16[80,1024]{1,0:T(8,128)(2,1)S(1)}, bf16[80,1024]{1,0:T(8,128)(2,1)S(1)}, u32[]{:S(2)}, u32[]{:S(2)}) collective-permute-start(bf16[80,1024]{1,0:T(8,128)(2,1)S(1)} %get-tuple-element.62.mine), channel_id=1, source_target_pairs={{0,2},{1,3},{2,0},{3,1},{4,6},{5,7},{6,4},{7,5},{8,10},{9,11},{10,... | collective-permute-start | bytes 491528 | tf_op jit(solution)/shard_map/ppermute | solution.py:309
  11.2 3.2 %copy-start.1 = (bf16[1024,1024]{1,0:T(8,128)(2,1)S(1)}, bf16[1024,1024]{1,0:T(8,128)(2,1)}, u32[]{:S(2)}) copy-start(bf16[1024,1024]{1,0:T(8,128)(2,1)} %d0.3) | copy-start | bytes 6291460
  11.9 1.6 %copy-start = (bf16[1024,1024]{1,0:T(8,128)(2,1)S(1)}, bf16[1024,1024]{1,0:T(8,128)(2,1)}, u32[]{:S(2)}) copy-start(bf16[1024,1024]{1,0:T(8,128)(2,1)} %u0.3) | copy-start | bytes 6291460
  11.9 2.5 %collective-permute-start.5 = (bf16[32,256]{1,0:T(8,128)(2,1)S(1)}, bf16[32,256]{1,0:T(8,128)(2,1)S(1)}, u32[]{:S(2)}, u32[]{:S(2)}) collective-permute-start(bf16[32,256]{1,0:T(8,128)(2,1)S(1)} %shard_map.85.b_own), channel_id=1, source_target_pairs={{0,1},{1,0},{2,3},{3,2},{4,5},{5,4},{6,7},{7,6},{8,9},{9,8},{10,11... | collective-permute-start | bytes 49160 | tf_op jit(solution)/shard_map/ppermute | solution.py:309
  13.5 18.5 %collective-permute-start.11 = (bf16[1024,1024]{1,0:T(8,128)(2,1)S(1)}, bf16[1024,1024]{1,0:T(8,128)(2,1)S(1)}, u32[]{:S(2)}, u32[]{:S(2)}) collective-permute-start(bf16[1024,1024]{1,0:T(8,128)(2,1)S(1)} %copy-done), channel_id=1, source_target_pairs={{0,1},{1,0},{2,3},{3,2},{4,5},{5,4},{6,7},{7,6},{8,9},{9,8},{10,11... | collective-permute-start | bytes 6291464 | tf_op jit(solution)/shard_map/ppermute | solution.py:309
  14.4 17.6 %collective-permute-start.12 = (bf16[1024,1024]{1,0:T(8,128)(2,1)S(1)}, bf16[1024,1024]{1,0:T(8,128)(2,1)S(1)}, u32[]{:S(2)}, u32[]{:S(2)}) collective-permute-start(bf16[1024,1024]{1,0:T(8,128)(2,1)S(1)} %copy-done.1), channel_id=1, source_target_pairs={{0,1},{1,0},{2,3},{3,2},{4,5},{5,4},{6,7},{7,6},{8,9},{9,8},{10,11... | collective-permute-start | bytes 6291464 | tf_op jit(solution)/shard_map/ppermute | solution.py:309
  15.2 10.5 %collective-permute-start.6 = (bf16[40,1024]{1,0:T(8,128)(2,1)S(1)}, bf16[40,1024]{1,0:T(8,128)(2,1)S(1)}, u32[]{:S(2)}, u32[]{:S(2)}) collective-permute-start(bf16[40,1024]{1,0:T(8,128)(2,1)S(1)} %get-tuple-element.60), channel_id=1, source_target_pairs={{0,36},{1,37},{2,38},{3,39},{4,40},{5,41},{6,42},{7,43},{8,44},{9,... | collective-permute-start | bytes 245768 | tf_op jit(solution)/shard_map/ppermute | solution.py:309
  16.2 9.5 %collective-permute-start.7 = (bf16[40,1024]{1,0:T(8,128)(2,1)S(1)}, bf16[40,1024]{1,0:T(8,128)(2,1)S(1)}, u32[]{:S(2)}, u32[]{:S(2)}) collective-permute-start(bf16[40,1024]{1,0:T(8,128)(2,1)S(1)} %get-tuple-element.61), channel_id=1, source_target_pairs={{0,4},{1,5},{2,6},{3,7},{4,8},{5,9},{6,10},{7,11},{8,12},{9,13},{1... | collective-permute-start | bytes 245768 | tf_op jit(solution)/shard_map/ppermute | solution.py:309
  18.8 7.2 %copy-start.2 = (bf16[1024,3,256]{2,0,1:T(8,128)(2,1)S(1)}, bf16[1024,3,256]{2,0,1:T(8,128)(2,1)}, u32[]{:S(2)}) copy-start(bf16[1024,3,256]{2,0,1:T(8,128)(2,1)} %param.10) | copy-start | bytes 4718596
  18.8 7.2 %copy-start.3 = (bf16[256,1024]{1,0:T(8,128)(2,1)S(1)}, bf16[256,1024]{1,0:T(8,128)(2,1)}, u32[]{:S(2)}) copy-start(bf16[256,1024]{1,0:T(8,128)(2,1)} %o_own.1) | copy-start | bytes 1572868
  18.8 7.2 %collective-permute-start.9 = (bf16[40,1024]{1,0:T(8,128)(2,1)S(1)}, bf16[40,1024]{1,0:T(8,128)(2,1)S(1)}, u32[]{:S(2)}, u32[]{:S(2)}) collective-permute-start(bf16[40,1024]{1,0:T(8,128)(2,1)S(1)} %get-tuple-element.64), channel_id=1, source_target_pairs={{0,32},{1,33},{2,34},{3,35},{4,36},{5,37},{6,38},{7,39},{8,40},{9,... | collective-permute-start | bytes 245768 | tf_op jit(solution)/shard_map/ppermute | solution.py:309
  27.6 4.4 %collective-permute-start.10 = (bf16[80,1024]{1,0:T(8,128)(2,1)S(1)}, bf16[80,1024]{1,0:T(8,128)(2,1)S(1)}, u32[]{:S(2)}, u32[]{:S(2)}) collective-permute-start(bf16[80,1024]{1,0:T(8,128)(2,1)S(1)} %get-tuple-element.69.mine), channel_id=1, source_target_pairs={{0,2},{1,3},{2,0},{3,1},{4,6},{5,7},{6,4},{7,5},{8,10},{9,11},{10,... | collective-permute-start | bytes 491528 | tf_op jit(solution)/shard_map/ppermute | solution.py:309
  27.9 6.4 %collective-permute-start.14 = (bf16[80,1024]{1,0:T(8,128)(2,1)S(1)}, bf16[80,1024]{1,0:T(8,128)(2,1)S(1)}, u32[]{:S(2)}, u32[]{:S(2)}) collective-permute-start(bf16[80,1024]{1,0:T(8,128)(2,1)S(1)} %get-tuple-element.76.mine), channel_id=1, source_target_pairs={{0,2},{1,3},{2,0},{3,1},{4,6},{5,7},{6,4},{7,5},{8,10},{9,11},{10,... | collective-permute-start | bytes 491528 | tf_op jit(solution)/shard_map/ppermute | solution.py:309
  33.8 5.2 %collective-permute-start.13 = (bf16[80,1024]{1,0:T(8,128)(2,1)S(1)}, bf16[80,1024]{1,0:T(8,128)(2,1)S(1)}, u32[]{:S(2)}, u32[]{:S(2)}) collective-permute-start(bf16[80,1024]{1,0:T(8,128)(2,1)S(1)} %shard_map.91.mine), channel_id=1, source_target_pairs={{0,2},{1,3},{2,0},{3,1},{4,6},{5,7},{6,4},{7,5},{8,10},{9,11},{10,... | collective-permute-start | bytes 491528 | tf_op jit(solution)/shard_map/ppermute | solution.py:309
  36.1 8.9 %collective-permute-start.17 = (bf16[80,1024]{1,0:T(8,128)(2,1)S(1)}, bf16[80,1024]{1,0:T(8,128)(2,1)S(1)}, u32[]{:S(2)}, u32[]{:S(2)}) collective-permute-start(bf16[80,1024]{1,0:T(8,128)(2,1)S(1)} %shard_map.93.mine), channel_id=1, source_target_pairs={{0,2},{1,3},{2,0},{3,1},{4,6},{5,7},{6,4},{7,5},{8,10},{9,11},{10,... | collective-permute-start | bytes 491528 | tf_op jit(solution)/shard_map/ppermute | solution.py:309
  39.1 6.8 %collective-permute-start.15 = (bf16[40,1024]{1,0:T(8,128)(2,1)S(1)}, bf16[40,1024]{1,0:T(8,128)(2,1)S(1)}, u32[]{:S(2)}, u32[]{:S(2)}) collective-permute-start(bf16[40,1024]{1,0:T(8,128)(2,1)S(1)} %get-tuple-element.77), channel_id=1, source_target_pairs={{0,254},{1,255},{2,252},{3,253},{4,224},{5,225},{6,226},{7,227},{8... | collective-permute-start | bytes 245768 | tf_op jit(solution)/shard_map/ppermute | solution.py:309
  44.1 3.6 %collective-permute-start.16 = (bf16[40,1024]{1,0:T(8,128)(2,1)S(1)}, bf16[40,1024]{1,0:T(8,128)(2,1)S(1)}, u32[]{:S(2)}, u32[]{:S(2)}) collective-permute-start(bf16[40,1024]{1,0:T(8,128)(2,1)S(1)} %get-tuple-element.78), channel_id=1, source_target_pairs={{0,30},{1,31},{2,28},{3,29},{4,0},{5,1},{6,2},{7,3},{8,4},{9,5},{1... | collective-permute-start | bytes 245768 | tf_op jit(solution)/shard_map/ppermute | solution.py:309
  45.1 3.7 %collective-permute-start.18 = (bf16[40,1024]{1,0:T(8,128)(2,1)S(1)}, bf16[40,1024]{1,0:T(8,128)(2,1)S(1)}, u32[]{:S(2)}, u32[]{:S(2)}) collective-permute-start(bf16[40,1024]{1,0:T(8,128)(2,1)S(1)} %get-tuple-element.80), channel_id=1, source_target_pairs={{0,224},{1,225},{2,226},{3,227},{4,228},{5,229},{6,230},{7,231},{8... | collective-permute-start | bytes 245768 | tf_op jit(solution)/shard_map/ppermute | solution.py:309
  48.8 7.5 %collective-permute-start.20 = (bf16[80,1024]{1,0:T(8,128)(2,1)S(1)}, bf16[80,1024]{1,0:T(8,128)(2,1)S(1)}, u32[]{:S(2)}, u32[]{:S(2)}) collective-permute-start(bf16[80,1024]{1,0:T(8,128)(2,1)S(1)} %shard_map.96.m1), channel_id=1, source_target_pairs={{0,1},{1,0},{2,3},{3,2},{4,5},{5,4},{6,7},{7,6},{8,9},{9,8},{10,11... | collective-permute-start | bytes 491528 | tf_op jit(solution)/shard_map/ppermute | solution.py:309
  55.2 1.4 %collective-permute-start.19 = (bf16[80,1024]{1,0:T(8,128)(2,1)S(1)}, bf16[80,1024]{1,0:T(8,128)(2,1)S(1)}, u32[]{:S(2)}, u32[]{:S(2)}) collective-permute-start(bf16[80,1024]{1,0:T(8,128)(2,1)S(1)} %shard_map.94.m0), channel_id=1, source_target_pairs={{0,1},{1,0},{2,3},{3,2},{4,5},{5,4},{6,7},{7,6},{8,9},{9,8},{10,11... | collective-permute-start | bytes 491528 | tf_op jit(solution)/shard_map/ppermute | solution.py:309

commit v15 on v14

--- a/solution.py
+++ b/solution.py
@@ -269,18 +269,38 @@
     out[...] = joined((p0, p1)).astype(jnp.bfloat16)
 
 
-def place_kernel(m0, m1, s0, s1, out):
+def place_kernel(m0, m1, s0, s1, out, held, sems):
     core = core_index()
     quad, slot, level, row, col = kept_place(iota((1, KEPT), 1))
     row, col = patch_place(quad, row, col)
-    total = None
+    places, sources = [], []
     for chosen, parts in ((core, (m0, m1)), (1 - core, (s0, s1))):
         place = (row * 12 + col) * 4 + real_level(level, chosen)
-        place = jnp.where(slot < USED, place, -1)
-        source = jnp.concatenate([part[...] for part in parts], axis=0)
-        term = dot(one_hot(iota((PATCH, KEPT), 0) == place), source)
-        total = term if total is None else total + term
-    out[...] = total.reshape(out.shape).astype(jnp.bfloat16)
+        places.append(jnp.where(slot < USED, place, -1))
+        sources.append(jnp.concatenate([part[...] for part in parts], axis=0))
+    count = PATCH // 2
+    copies = []
+    for h in range(2):
+        index = iota((count, KEPT), 0) + h * count
+        total = dot(one_hot(index == places[0]), sources[0]) + dot(one_hot(index == places[1]), sources[1])
+        rows = pl.ds(h * count // 4, count // 4)
+        held[rows] = total.reshape(count // 4, 4, -1).astype(jnp.bfloat16)
+        copies.append(pltpu.make_async_copy(held.at[rows], out.at[rows], sems.at[h]))
+        copies[h].start()
+    for copy in copies:
+        copy.wait()
+
+
+def place_rows(shape, operands):
+    return pl.pallas_call(
+        place_kernel,
+        out_shape=jax.ShapeDtypeStruct(shape, jnp.bfloat16),
+        in_specs=[pl.BlockSpec(memory_space=pltpu.VMEM)] * 4,
+        out_specs=pl.BlockSpec(memory_space=pl.ANY),
+        scratch_shapes=[pltpu.VMEM(shape, jnp.bfloat16), pltpu.SemaphoreType.DMA((2,))],
+        compiler_params=pltpu.CompilerParams(vmem_limit_bytes=12 * MIB),
+        cost_estimate=pl.CostEstimate(flops=2 * 10**8, bytes_accessed=2 * 10**6, transcendentals=0),
+    )(*operands)
 
 
 def call(kernel, outs, operands, flops, limit, table=False):
@@ -332,12 +352,12 @@
     w_sib = core_swap(w_second)
     bias1 = call(functools.partial(bias_kernel, 0), features, (rel_tables,), 5 * 10**9, 4, table=True)
     keep, give = call(first_kernel, heads * 2, (tok, w_first, bias1), 10**9, 16)
-    keep, give, f1, s1, w_sib = tied(keep, give, f1, s1, w_sib)
+    keep, give, f1 = tied(keep, give, f1)
     keep, tok, rel_tables = tied(keep, tok, rel_tables)
     base_a, base_b = call(base_kernel, half * 2, (tok,), 10**9, 8)
     bias2 = call(functools.partial(bias_kernel, 1), features, (rel_tables,), 10**9, 4, table=True)
     bias2_sib = core_swap(bias2)
-    given, up_late, down_late = tied(core_swap(give), up_weight, down_weight)
+    given, up_late, down_late, s1, w_sib = tied(core_swap(give), up_weight, down_weight, s1, w_sib)
     u1 = core_swap(up_late)
     d1 = core_swap(down_late)
     part_a, part_b = call(partial_kernel, half * 2, (keep, given, out_first, f1), 2 * 10**8, 8)
@@ -376,13 +396,8 @@
     mine_a = call(join_kernel, half, (diag, lon), 10**10, 8)
     mine_a, lat, own = tied(mine_a, lat, own)
     mine_b = call(join_kernel, half, (lat, own), 10**6, 8)
-    result = call(
-        place_kernel,
-        [(rows * cols, levels, width)],
-        (mine_a, mine_b, core_swap(mine_a), core_swap(mine_b)),
-        2 * 10**8,
-        12,
-    )
+    operands = (mine_a, mine_b, core_swap(mine_a), core_swap(mine_b))
+    result = place_rows((rows * cols, levels, width), operands)
     return result.reshape(rows, cols, levels, width).transpose(2, 0, 1, 3)
 
 

time: 58 us -> 57 us (0.983)
  starting transfers between devices: 26.8 us -> 25.9 us
    pallas_call x16 -> x15, Pallas kernels: 11.2 us -> 9.91 us  [call(): pl.pallas_call(kernel, out_shape=shapes, in_specs=[pl.BlockSpec(memory_sp...]
    pallas_call x0 -> x1, Pallas kernels: none -> 1.24 us  [place_rows(): pl.pallas_call(place_kernel, out_shape=jax.ShapeDtypeStruct(shape, jnp.bf...]
    ppermute x21, starting transfers between devices: 26.8 us -> 25.9 us  [move(): return lax.ppermute(value, AXES, pairs(counts, target))]
where the time goes in v15:
time: 57 us; the launch traced here: 56.9 us
  starting transfers between devices  25.9 us (45%)
  waiting for transfers between devices  18.5 us (32%)
  Pallas kernels  11.2 us (20%)
  local copies, waits for them, and re-layouts  0.98 us (2%)
    ppermute x21, starting transfers between devices, move(): return lax.ppermute(value, AXES, pairs(counts, target))  25.9 us
    ppermute x21, waiting for transfers between devices, move(): return lax.ppermute(value, AXES, pairs(counts, target))  18.5 us
    pallas_call x15, Pallas kernels, call(): pl.pallas_call(kernel, out_shape=shapes, in_specs=[pl.BlockSpec(memory_sp...  9.91 us
    pallas_call x1, Pallas kernels, place_rows(): pl.pallas_call(place_kernel, out_shape=jax.ShapeDtypeStruct(shape, jnp.bf...  1.24 us
  transfers between devices with their start and end apart: 21, of which 12 were waited for; matrix products, arithmetic and copies ran while one was open for 0% of the time, Pallas kernels for 17%

profile of v15, /device:TPU:1, one launch (start us, length us, event | category | flops | bytes accessed | tf_op | source)
XLA Modules:
  0.0 56.9 jit_solution(17485487817097841968)
XLA Ops:
  0.0 3.2 %collective-permute-start.3 = (bf16[3,1024,256]{2,1,0:T(8,128)(2,1)}, bf16[3,1024,256]{2,1,0:T(8,128)(2,1)S(1)}, u32[]{:S(2)}, u32[]{:S(2)}) collective-permute-start(bf16[3,1024,256]{2,1,0:T(8,128)(2,1)} %bitcast.8), channel_id=1, source_target_pairs={{0,1},{1,0},{2,3},{3,2},{4,5},{5,4},{6,7},{7,6},{8,9},{9,8},{10,11... | collective-permute-start | bytes 4718600 | tf_op jit(solution)/shard_map/ppermute | solution.py:329
  3.2 0.5 collective-permute-start.2
  3.8 0.7 %copy-done.7 = f32[2,4,37]{2,1,0:T(4,128)S(1)} copy-done((f32[2,4,37]{2,1,0:T(4,128)S(1)}, f32[2,4,37]{2,1,0:T(4,128)}, u32[]{:S(2)}) %copy-start.7) | copy-done | bytes 1208
  4.4 0.7 %shard_map.82.bias = bf16[32,256]{1,0:T(8,128)(2,1)S(1)} custom-call(f32[2,4,37]{2,1,0:T(4,128)S(1)} %copy-done.7), custom_call_target="tpu_custom_call" | custom-call | flops 5000000000 | bytes 17568 | tf_op jit(solution)/shard_map/pallas_call | solution.py:309
  5.2 2.1 %shard_map.83 = (bf16[160,256]{1,0:T(8,128)(2,1)S(1)}, bf16[160,256]{1,0:T(8,128)(2,1)S(1)}) custom-call(bf16[72,4,1024]{2,1,0:T(4,128)(2,1)S(1)} %bitcast.11, bf16[3,1024,256]{2,1,0:T(8,128)(2,1)S(1)} %bitcast.10, bf16[32,256]{1,0:T(8,128)(2,1)S(1)} %shard_map.82.bias), custom_call_target="tpu_custom_call" | custom-call | flops 1000000000 | bytes 2342912 | tf_op jit(solution)/shard_map/pallas_call | solution.py:309
  8.0 0.6 %collective-permute-done.1.o1 = bf16[160,256]{1,0:T(8,128)(2,1)S(1)} collective-permute-done((bf16[160,256]{1,0:T(8,128)(2,1)S(1)}, bf16[160,256]{1,0:T(8,128)(2,1)S(1)}, u32[]{:S(2)}, u32[]{:S(2)}) %collective-permute-start.1) | collective-permute-done | bytes 81952 | tf_op jit(solution)/shard_map/ppermute | solution.py:329
  9.1 1.5 %collective-permute-start.8 = (bf16[80,1024]{1,0:T(8,128)(2,1)S(1)}, bf16[80,1024]{1,0:T(8,128)(2,1)S(1)}, u32[]{:S(2)}, u32[]{:S(2)}) collective-permute-start(bf16[80,1024]{1,0:T(8,128)(2,1)S(1)} %get-tuple-element.62.mine), channel_id=1, source_target_pairs={{0,2},{1,3},{2,0},{3,1},{4,6},{5,7},{6,4},{7,5},{8,10},{9,11},{10,... | collective-permute-start | bytes 491528 | tf_op jit(solution)/shard_map/ppermute | solution.py:329
  10.5 0.7 %shard_map.85.b_own = bf16[32,256]{1,0:T(8,128)(2,1)S(1)} custom-call(f32[2,4,37]{2,1,0:T(4,128)S(1)} %copy-done.8), custom_call_target="tpu_custom_call" | custom-call | flops 1000000000 | bytes 17568 | tf_op jit(solution)/shard_map/pallas_call | solution.py:309
  11.3 0.9 %collective-permute-start.5 = (bf16[32,256]{1,0:T(8,128)(2,1)S(1)}, bf16[32,256]{1,0:T(8,128)(2,1)S(1)}, u32[]{:S(2)}, u32[]{:S(2)}) collective-permute-start(bf16[32,256]{1,0:T(8,128)(2,1)S(1)} %shard_map.85.b_own), channel_id=1, source_target_pairs={{0,1},{1,0},{2,3},{3,2},{4,5},{5,4},{6,7},{7,6},{8,9},{9,8},{10,11... | collective-permute-start | bytes 49160 | tf_op jit(solution)/shard_map/ppermute | solution.py:329
  12.9 0.8 %collective-permute-start.11 = (bf16[1024,1024]{1,0:T(8,128)(2,1)S(1)}, bf16[1024,1024]{1,0:T(8,128)(2,1)S(1)}, u32[]{:S(2)}, u32[]{:S(2)}) collective-permute-start(bf16[1024,1024]{1,0:T(8,128)(2,1)S(1)} %copy-done), channel_id=1, source_target_pairs={{0,1},{1,0},{2,3},{3,2},{4,5},{5,4},{6,7},{7,6},{8,9},{9,8},{10,11... | collective-permute-start | bytes 6291464 | tf_op jit(solution)/shard_map/ppermute | solution.py:329
  13.7 0.9 %collective-permute-done.4.other = bf16[80,1024]{1,0:T(8,128)(2,1)S(1)} collective-permute-done((bf16[80,1024]{1,0:T(8,128)(2,1)S(1)}, bf16[80,1024]{1,0:T(8,128)(2,1)S(1)}, u32[]{:S(2)}, u32[]{:S(2)}) %collective-permute-start.4) | collective-permute-done | bytes 163872 | tf_op jit(solution)/shard_map/ppermute | solution.py:329
  14.7 1.0 %collective-permute-start.6 = (bf16[40,1024]{1,0:T(8,128)(2,1)S(1)}, bf16[40,1024]{1,0:T(8,128)(2,1)S(1)}, u32[]{:S(2)}, u32[]{:S(2)}) collective-permute-start(bf16[40,1024]{1,0:T(8,128)(2,1)S(1)} %get-tuple-element.60), channel_id=1, source_target_pairs={{0,36},{1,37},{2,38},{3,39},{4,40},{5,41},{6,42},{7,43},{8,44},{9,... | collective-permute-start | bytes 245768 | tf_op jit(solution)/shard_map/ppermute | solution.py:329
  15.7 1.3 %collective-permute-start.7 = (bf16[40,1024]{1,0:T(8,128)(2,1)S(1)}, bf16[40,1024]{1,0:T(8,128)(2,1)S(1)}, u32[]{:S(2)}, u32[]{:S(2)}) collective-permute-start(bf16[40,1024]{1,0:T(8,128)(2,1)S(1)} %get-tuple-element.61), channel_id=1, source_target_pairs={{0,4},{1,5},{2,6},{3,7},{4,8},{5,9},{6,10},{7,11},{8,12},{9,13},{1... | collective-permute-start | bytes 245768 | tf_op jit(solution)/shard_map/ppermute | solution.py:329
  17.0 1.1 %collective-permute-done.8.other = bf16[80,1024]{1,0:T(8,128)(2,1)S(1)} collective-permute-done((bf16[80,1024]{1,0:T(8,128)(2,1)S(1)}, bf16[80,1024]{1,0:T(8,128)(2,1)S(1)}, u32[]{:S(2)}, u32[]{:S(2)}) %collective-permute-start.8) | collective-permute-done | bytes 163872 | tf_op jit(solution)/shard_map/ppermute | solution.py:329
  18.2 0.6 collective-permute-start.9
  18.8 6.4 %collective-permute-done.6.p0 = bf16[40,1024]{1,0:T(8,128)(2,1)S(1)} collective-permute-done((bf16[40,1024]{1,0:T(8,128)(2,1)S(1)}, bf16[40,1024]{1,0:T(8,128)(2,1)S(1)}, u32[]{:S(2)}, u32[]{:S(2)}) %collective-permute-start.6) | collective-permute-done | bytes 81952 | tf_op jit(solution)/shard_map/ppermute | solution.py:329
  25.4 1.6 %shard_map.90 = (bf16[80,1024]{1,0:T(8,128)(2,1)S(1)}, bf16[80,1024]{1,0:T(8,128)(2,1)S(1)}) custom-call(bf16[80,1024]{1,0:T(8,128)(2,1)S(1)} %shard_map.88.xn_a, bf16[40,1024]{1,0:T(8,128)(2,1)S(1)} %collective-permute-done.9.p2.p0, bf16[40,1024]{1,0:T(8,128)(2,1)S(1)} %get-tuple-element.65.p3.p1, bf16[3,1024,256]{2,1,0:T(8,128)(2,1)S(1)} %bitcast.9, ...), custom_call_target="tpu_custom_call" | custom-call | flops 1000000000 | bytes 4882432 | tf_op jit(solution)/shard_map/pallas_call | solution.py:309
  27.3 1.4 %collective-permute-start.14 = (bf16[80,1024]{1,0:T(8,128)(2,1)S(1)}, bf16[80,1024]{1,0:T(8,128)(2,1)S(1)}, u32[]{:S(2)}, u32[]{:S(2)}) collective-permute-start(bf16[80,1024]{1,0:T(8,128)(2,1)S(1)} %get-tuple-element.76.mine), channel_id=1, source_target_pairs={{0,2},{1,3},{2,0},{3,1},{4,6},{5,7},{6,4},{7,5},{8,10},{9,11},{10,... | collective-permute-start | bytes 491528 | tf_op jit(solution)/shard_map/ppermute | solution.py:329
  28.8 2.7 %collective-permute-done.10.other = bf16[80,1024]{1,0:T(8,128)(2,1)S(1)} collective-permute-done((bf16[80,1024]{1,0:T(8,128)(2,1)S(1)}, bf16[80,1024]{1,0:T(8,128)(2,1)S(1)}, u32[]{:S(2)}, u32[]{:S(2)}) %collective-permute-start.10) | collective-permute-done | bytes 163872 | tf_op jit(solution)/shard_map/ppermute | solution.py:329
  31.5 1.8 %shard_map.91.mine = bf16[80,1024]{1,0:T(8,128)(2,1)S(1)} custom-call(bf16[80,1024]{1,0:T(8,128)(2,1)S(1)} %get-tuple-element.69.mine, bf16[80,1024]{1,0:T(8,128)(2,1)S(1)} %collective-permute-done.10.other, bf16[40,1024]{1,0:T(8,128)(2,1)S(1)} %collective-permute-done.6.p0, bf16[40,1024]{1,0:T(8,128)(2,1)S(1)} %collective-permute-done.7.p1, ...), custom_call_target="tpu_custom_call" | custom-call | flops 1000000000 | bytes 9043968 | tf_op jit(solution)/shard_map/pallas_call | solution.py:309
  33.4 0.6 collective-permute-done.14.other
  34.0 1.8 %shard_map.93.mine = bf16[80,1024]{1,0:T(8,128)(2,1)S(1)} custom-call(bf16[80,1024]{1,0:T(8,128)(2,1)S(1)} %get-tuple-element.76.mine, bf16[80,1024]{1,0:T(8,128)(2,1)S(1)} %collective-permute-done.14.other, bf16[40,1024]{1,0:T(8,128)(2,1)S(1)} %collective-permute-done.9.p2.p0, bf16[40,1024]{1,0:T(8,128)(2,1)S(1)} %get-tuple-element.65.p3.p1, ...), custom_call_target="tpu_custom_call" | custom-call | flops 1000000000 | bytes 9043968 | tf_op jit(solution)/shard_map/pallas_call | solution.py:309
  35.8 0.9 %collective-permute-start.17 = (bf16[80,1024]{1,0:T(8,128)(2,1)S(1)}, bf16[80,1024]{1,0:T(8,128)(2,1)S(1)}, u32[]{:S(2)}, u32[]{:S(2)}) collective-permute-start(bf16[80,1024]{1,0:T(8,128)(2,1)S(1)} %shard_map.93.mine), channel_id=1, source_target_pairs={{0,2},{1,3},{2,0},{3,1},{4,6},{5,7},{6,4},{7,5},{8,10},{9,11},{10,... | collective-permute-start | bytes 491528 | tf_op jit(solution)/shard_map/ppermute | solution.py:329
  36.7 1.7 %collective-permute-done.13.other = bf16[80,1024]{1,0:T(8,128)(2,1)S(1)} collective-permute-done((bf16[80,1024]{1,0:T(8,128)(2,1)S(1)}, bf16[80,1024]{1,0:T(8,128)(2,1)S(1)}, u32[]{:S(2)}, u32[]{:S(2)}) %collective-permute-start.13) | collective-permute-done | bytes 163872 | tf_op jit(solution)/shard_map/ppermute | solution.py:329
  38.5 4.9 %collective-permute-start.15 = (bf16[40,1024]{1,0:T(8,128)(2,1)S(1)}, bf16[40,1024]{1,0:T(8,128)(2,1)S(1)}, u32[]{:S(2)}, u32[]{:S(2)}) collective-permute-start(bf16[40,1024]{1,0:T(8,128)(2,1)S(1)} %get-tuple-element.77), channel_id=1, source_target_pairs={{0,254},{1,255},{2,252},{3,253},{4,224},{5,225},{6,226},{7,227},{8... | collective-permute-start | bytes 245768 | tf_op jit(solution)/shard_map/ppermute | solution.py:329
  43.4 0.7 %collective-permute-start.16 = (bf16[40,1024]{1,0:T(8,128)(2,1)S(1)}, bf16[40,1024]{1,0:T(8,128)(2,1)S(1)}, u32[]{:S(2)}, u32[]{:S(2)}) collective-permute-start(bf16[40,1024]{1,0:T(8,128)(2,1)S(1)} %get-tuple-element.78), channel_id=1, source_target_pairs={{0,30},{1,31},{2,28},{3,29},{4,0},{5,1},{6,2},{7,3},{8,4},{9,5},{1... | collective-permute-start | bytes 245768 | tf_op jit(solution)/shard_map/ppermute | solution.py:329
  44.2 1.0 %collective-permute-start.18 = (bf16[40,1024]{1,0:T(8,128)(2,1)S(1)}, bf16[40,1024]{1,0:T(8,128)(2,1)S(1)}, u32[]{:S(2)}, u32[]{:S(2)}) collective-permute-start(bf16[40,1024]{1,0:T(8,128)(2,1)S(1)} %get-tuple-element.80), channel_id=1, source_target_pairs={{0,224},{1,225},{2,226},{3,227},{4,228},{5,229},{6,230},{7,231},{8... | collective-permute-start | bytes 245768 | tf_op jit(solution)/shard_map/ppermute | solution.py:329
  45.1 1.6 %collective-permute-done.16.p1 = bf16[40,1024]{1,0:T(8,128)(2,1)S(1)} collective-permute-done((bf16[40,1024]{1,0:T(8,128)(2,1)S(1)}, bf16[40,1024]{1,0:T(8,128)(2,1)S(1)}, u32[]{:S(2)}, u32[]{:S(2)}) %collective-permute-start.16) | collective-permute-done | bytes 81952 | tf_op jit(solution)/shard_map/ppermute | solution.py:329
  46.7 1.1 %collective-permute-done.18.p0 = bf16[40,1024]{1,0:T(8,128)(2,1)S(1)} collective-permute-done((bf16[40,1024]{1,0:T(8,128)(2,1)S(1)}, bf16[40,1024]{1,0:T(8,128)(2,1)S(1)}, u32[]{:S(2)}, u32[]{:S(2)}) %collective-permute-start.18) | collective-permute-done | bytes 81952 | tf_op jit(solution)/shard_map/ppermute | solution.py:329
  47.9 6.2 %collective-permute-start.20 = (bf16[80,1024]{1,0:T(8,128)(2,1)S(1)}, bf16[80,1024]{1,0:T(8,128)(2,1)S(1)}, u32[]{:S(2)}, u32[]{:S(2)}) collective-permute-start(bf16[80,1024]{1,0:T(8,128)(2,1)S(1)} %shard_map.96.m1), channel_id=1, source_target_pairs={{0,1},{1,0},{2,3},{3,2},{4,5},{5,4},{6,7},{7,6},{8,9},{9,8},{10,11... | collective-permute-start | bytes 491528 | tf_op jit(solution)/shard_map/ppermute | solution.py:329
  54.2 0.9 %collective-permute-done.20.s1 = bf16[80,1024]{1,0:T(8,128)(2,1)S(1)} collective-permute-done((bf16[80,1024]{1,0:T(8,128)(2,1)S(1)}, bf16[80,1024]{1,0:T(8,128)(2,1)S(1)}, u32[]{:S(2)}, u32[]{:S(2)}) %collective-permute-start.20) | collective-permute-done | bytes 163872 | tf_op jit(solution)/shard_map/ppermute | solution.py:329
  55.5 1.2 %shard_map.97 = bf16[72,4,1024]{2,1,0:T(4,128)(2,1)} custom-call(bf16[80,1024]{1,0:T(8,128)(2,1)S(1)} %shard_map.94.m0, bf16[80,1024]{1,0:T(8,128)(2,1)S(1)} %shard_map.96.m1, bf16[80,1024]{1,0:T(8,128)(2,1)S(1)} %collective-permute-done.19.s0, bf16[80,1024]{1,0:T(8,128)(2,1)S(1)} %collective-permute-done.20.s1), custom_call_target="tpu_custom_call" | custom-call | flops 200000000 | bytes 2000000 | tf_op jit(solution)/shard_map/pallas_call | solution.py:295
  (44 shorter events, 3.3 us)
Async XLA Ops:
  0.0 5.2 %copy-start.5 = (bf16[1024,3,256]{2,0,1:T(8,128)(2,1)S(1)}, bf16[1024,3,256]{2,0,1:T(8,128)(2,1)}, u32[]{:S(2)}) copy-start(bf16[1024,3,256]{2,0,1:T(8,128)(2,1)} %param.9) | copy-start | bytes 4718596
  0.0 5.2 %copy-start.6 = (bf16[4,6,12,1024]{3,0,2,1:T(4,128)(2,1)S(1)}, bf16[4,6,12,1024]{3,0,2,1:T(4,128)(2,1)}, u32[]{:S(2)}) copy-start(bf16[4,6,12,1024]{3,0,2,1:T(4,128)(2,1)} %param.8) | copy-start | bytes 1769476
  0.0 8.6 %collective-permute-start.3 = (bf16[3,1024,256]{2,1,0:T(8,128)(2,1)}, bf16[3,1024,256]{2,1,0:T(8,128)(2,1)S(1)}, u32[]{:S(2)}, u32[]{:S(2)}) collective-permute-start(bf16[3,1024,256]{2,1,0:T(8,128)(2,1)} %bitcast.8), channel_id=1, source_target_pairs={{0,1},{1,0},{2,3},{3,2},{4,5},{5,4},{6,7},{7,6},{8,9},{9,8},{10,11... | collective-permute-start | bytes 4718600 | tf_op jit(solution)/shard_map/ppermute | solution.py:329
  3.2 4.0 %collective-permute-start = (bf16[256,1024]{1,0:T(8,128)(2,1)}, bf16[256,1024]{1,0:T(8,128)(2,1)S(1)}, u32[]{:S(2)}, u32[]{:S(2)}) collective-permute-start(bf16[256,1024]{1,0:T(8,128)(2,1)} %w0.1), channel_id=1, source_target_pairs={{0,1},{1,0},{2,3},{3,2},{4,5},{5,4},{6,7},{7,6},{8,9},{9,8},{10,11... | collective-permute-start | bytes 1572872 | tf_op jit(solution)/shard_map/ppermute | solution.py:329
  3.2 4.7 %collective-permute-start.2 = (bf16[256,1024]{1,0:T(8,128)(2,1)}, bf16[256,1024]{1,0:T(8,128)(2,1)S(1)}, u32[]{:S(2)}, u32[]{:S(2)}) collective-permute-start(bf16[256,1024]{1,0:T(8,128)(2,1)} %o_own.1), channel_id=1, source_target_pairs={{0,1},{1,0},{2,3},{3,2},{4,5},{5,4},{6,7},{7,6},{8,9},{9,8},{10,11... | collective-permute-start | bytes 1572872 | tf_op jit(solution)/shard_map/ppermute | solution.py:329
  3.8 0.7 %copy-start.7 = (f32[2,4,37]{2,1,0:T(4,128)S(1)}, f32[2,4,37]{2,1,0:T(4,128)}, u32[]{:S(2)}) copy-start(f32[2,4,37]{2,1,0:T(4,128)} %table.2) | copy-start | bytes 3556
  5.2 3.5 %copy-start.4 = (bf16[256,1024]{1,0:T(8,128)(2,1)S(1)}, bf16[256,1024]{1,0:T(8,128)(2,1)}, u32[]{:S(2)}) copy-start(bf16[256,1024]{1,0:T(8,128)(2,1)} %w0.1) | copy-start | bytes 1572868
  5.2 5.4 %copy-start.8 = (f32[2,4,37]{2,1,0:T(4,128)S(1)}, f32[2,4,37]{2,1,0:T(4,128)}, u32[]{:S(2)}) copy-start(f32[2,4,37]{2,1,0:T(4,128)} %table.2) | copy-start | bytes 3556
  7.3 1.4 %collective-permute-start.1 = (bf16[160,256]{1,0:T(8,128)(2,1)S(1)}, bf16[160,256]{1,0:T(8,128)(2,1)S(1)}, u32[]{:S(2)}, u32[]{:S(2)}) collective-permute-start(bf16[160,256]{1,0:T(8,128)(2,1)S(1)} %get-tuple-element.49), channel_id=1, source_target_pairs={{0,1},{1,0},{2,3},{3,2},{4,5},{5,4},{6,7},{7,6},{8,9},{9,8},{10,11... | collective-permute-start | bytes 245768 | tf_op jit(solution)/shard_map/ppermute | solution.py:329
  9.0 5.6 %collective-permute-start.4 = (bf16[80,1024]{1,0:T(8,128)(2,1)S(1)}, bf16[80,1024]{1,0:T(8,128)(2,1)S(1)}, u32[]{:S(2)}, u32[]{:S(2)}) collective-permute-start(bf16[80,1024]{1,0:T(8,128)(2,1)S(1)} %get-tuple-element.52.mine), channel_id=1, source_target_pairs={{0,2},{1,3},{2,0},{3,1},{4,6},{5,7},{6,4},{7,5},{8,10},{9,11},{10,... | collective-permute-start | bytes 491528 | tf_op jit(solution)/shard_map/ppermute | solution.py:329
  9.1 9.0 %collective-permute-start.8 = (bf16[80,1024]{1,0:T(8,128)(2,1)S(1)}, bf16[80,1024]{1,0:T(8,128)(2,1)S(1)}, u32[]{:S(2)}, u32[]{:S(2)}) collective-permute-start(bf16[80,1024]{1,0:T(8,128)(2,1)S(1)} %get-tuple-element.62.mine), channel_id=1, source_target_pairs={{0,2},{1,3},{2,0},{3,1},{4,6},{5,7},{6,4},{7,5},{8,10},{9,11},{10,... | collective-permute-start | bytes 491528 | tf_op jit(solution)/shard_map/ppermute | solution.py:329
  10.5 3.1 %copy-start.1 = (bf16[1024,1024]{1,0:T(8,128)(2,1)S(1)}, bf16[1024,1024]{1,0:T(8,128)(2,1)}, u32[]{:S(2)}) copy-start(bf16[1024,1024]{1,0:T(8,128)(2,1)} %d0.3) | copy-start | bytes 6291460
  11.3 1.6 %copy-start = (bf16[1024,1024]{1,0:T(8,128)(2,1)S(1)}, bf16[1024,1024]{1,0:T(8,128)(2,1)}, u32[]{:S(2)}) copy-start(bf16[1024,1024]{1,0:T(8,128)(2,1)} %u0.3) | copy-start | bytes 6291460
  11.3 2.4 %collective-permute-start.5 = (bf16[32,256]{1,0:T(8,128)(2,1)S(1)}, bf16[32,256]{1,0:T(8,128)(2,1)S(1)}, u32[]{:S(2)}, u32[]{:S(2)}) collective-permute-start(bf16[32,256]{1,0:T(8,128)(2,1)S(1)} %shard_map.85.b_own), channel_id=1, source_target_pairs={{0,1},{1,0},{2,3},{3,2},{4,5},{5,4},{6,7},{7,6},{8,9},{9,8},{10,11... | collective-permute-start | bytes 49160 | tf_op jit(solution)/shard_map/ppermute | solution.py:329
  12.9 18.6 %collective-permute-start.11 = (bf16[1024,1024]{1,0:T(8,128)(2,1)S(1)}, bf16[1024,1024]{1,0:T(8,128)(2,1)S(1)}, u32[]{:S(2)}, u32[]{:S(2)}) collective-permute-start(bf16[1024,1024]{1,0:T(8,128)(2,1)S(1)} %copy-done), channel_id=1, source_target_pairs={{0,1},{1,0},{2,3},{3,2},{4,5},{5,4},{6,7},{7,6},{8,9},{9,8},{10,11... | collective-permute-start | bytes 6291464 | tf_op jit(solution)/shard_map/ppermute | solution.py:329
  13.7 17.8 %collective-permute-start.12 = (bf16[1024,1024]{1,0:T(8,128)(2,1)S(1)}, bf16[1024,1024]{1,0:T(8,128)(2,1)S(1)}, u32[]{:S(2)}, u32[]{:S(2)}) collective-permute-start(bf16[1024,1024]{1,0:T(8,128)(2,1)S(1)} %copy-done.1), channel_id=1, source_target_pairs={{0,1},{1,0},{2,3},{3,2},{4,5},{5,4},{6,7},{7,6},{8,9},{9,8},{10,11... | collective-permute-start | bytes 6291464 | tf_op jit(solution)/shard_map/ppermute | solution.py:329
  14.7 10.5 %collective-permute-start.6 = (bf16[40,1024]{1,0:T(8,128)(2,1)S(1)}, bf16[40,1024]{1,0:T(8,128)(2,1)S(1)}, u32[]{:S(2)}, u32[]{:S(2)}) collective-permute-start(bf16[40,1024]{1,0:T(8,128)(2,1)S(1)} %get-tuple-element.60), channel_id=1, source_target_pairs={{0,36},{1,37},{2,38},{3,39},{4,40},{5,41},{6,42},{7,43},{8,44},{9,... | collective-permute-start | bytes 245768 | tf_op jit(solution)/shard_map/ppermute | solution.py:329
  15.7 9.5 %collective-permute-start.7 = (bf16[40,1024]{1,0:T(8,128)(2,1)S(1)}, bf16[40,1024]{1,0:T(8,128)(2,1)S(1)}, u32[]{:S(2)}, u32[]{:S(2)}) collective-permute-start(bf16[40,1024]{1,0:T(8,128)(2,1)S(1)} %get-tuple-element.61), channel_id=1, source_target_pairs={{0,4},{1,5},{2,6},{3,7},{4,8},{5,9},{6,10},{7,11},{8,12},{9,13},{1... | collective-permute-start | bytes 245768 | tf_op jit(solution)/shard_map/ppermute | solution.py:329
  18.2 7.2 %copy-start.2 = (bf16[1024,3,256]{2,0,1:T(8,128)(2,1)S(1)}, bf16[1024,3,256]{2,0,1:T(8,128)(2,1)}, u32[]{:S(2)}) copy-start(bf16[1024,3,256]{2,0,1:T(8,128)(2,1)} %param.10) | copy-start | bytes 4718596
  18.2 7.2 %copy-start.3 = (bf16[256,1024]{1,0:T(8,128)(2,1)S(1)}, bf16[256,1024]{1,0:T(8,128)(2,1)}, u32[]{:S(2)}) copy-start(bf16[256,1024]{1,0:T(8,128)(2,1)} %o_own.1) | copy-start | bytes 1572868
  18.2 7.2 %collective-permute-start.9 = (bf16[40,1024]{1,0:T(8,128)(2,1)S(1)}, bf16[40,1024]{1,0:T(8,128)(2,1)S(1)}, u32[]{:S(2)}, u32[]{:S(2)}) collective-permute-start(bf16[40,1024]{1,0:T(8,128)(2,1)S(1)} %get-tuple-element.64), channel_id=1, source_target_pairs={{0,32},{1,33},{2,34},{3,35},{4,36},{5,37},{6,38},{7,39},{8,40},{9,... | collective-permute-start | bytes 245768 | tf_op jit(solution)/shard_map/ppermute | solution.py:329
  27.0 4.4 %collective-permute-start.10 = (bf16[80,1024]{1,0:T(8,128)(2,1)S(1)}, bf16[80,1024]{1,0:T(8,128)(2,1)S(1)}, u32[]{:S(2)}, u32[]{:S(2)}) collective-permute-start(bf16[80,1024]{1,0:T(8,128)(2,1)S(1)} %get-tuple-element.69.mine), channel_id=1, source_target_pairs={{0,2},{1,3},{2,0},{3,1},{4,6},{5,7},{6,4},{7,5},{8,10},{9,11},{10,... | collective-permute-start | bytes 491528 | tf_op jit(solution)/shard_map/ppermute | solution.py:329
  27.3 6.6 %collective-permute-start.14 = (bf16[80,1024]{1,0:T(8,128)(2,1)S(1)}, bf16[80,1024]{1,0:T(8,128)(2,1)S(1)}, u32[]{:S(2)}, u32[]{:S(2)}) collective-permute-start(bf16[80,1024]{1,0:T(8,128)(2,1)S(1)} %get-tuple-element.76.mine), channel_id=1, source_target_pairs={{0,2},{1,3},{2,0},{3,1},{4,6},{5,7},{6,4},{7,5},{8,10},{9,11},{10,... | collective-permute-start | bytes 491528 | tf_op jit(solution)/shard_map/ppermute | solution.py:329
  33.3 5.2 %collective-permute-start.13 = (bf16[80,1024]{1,0:T(8,128)(2,1)S(1)}, bf16[80,1024]{1,0:T(8,128)(2,1)S(1)}, u32[]{:S(2)}, u32[]{:S(2)}) collective-permute-start(bf16[80,1024]{1,0:T(8,128)(2,1)S(1)} %shard_map.91.mine), channel_id=1, source_target_pairs={{0,2},{1,3},{2,0},{3,1},{4,6},{5,7},{6,4},{7,5},{8,10},{9,11},{10,... | collective-permute-start | bytes 491528 | tf_op jit(solution)/shard_map/ppermute | solution.py:329
  35.8 8.3 %collective-permute-start.17 = (bf16[80,1024]{1,0:T(8,128)(2,1)S(1)}, bf16[80,1024]{1,0:T(8,128)(2,1)S(1)}, u32[]{:S(2)}, u32[]{:S(2)}) collective-permute-start(bf16[80,1024]{1,0:T(8,128)(2,1)S(1)} %shard_map.93.mine), channel_id=1, source_target_pairs={{0,2},{1,3},{2,0},{3,1},{4,6},{5,7},{6,4},{7,5},{8,10},{9,11},{10,... | collective-permute-start | bytes 491528 | tf_op jit(solution)/shard_map/ppermute | solution.py:329
  38.5 6.6 %collective-permute-start.15 = (bf16[40,1024]{1,0:T(8,128)(2,1)S(1)}, bf16[40,1024]{1,0:T(8,128)(2,1)S(1)}, u32[]{:S(2)}, u32[]{:S(2)}) collective-permute-start(bf16[40,1024]{1,0:T(8,128)(2,1)S(1)} %get-tuple-element.77), channel_id=1, source_target_pairs={{0,254},{1,255},{2,252},{3,253},{4,224},{5,225},{6,226},{7,227},{8... | collective-permute-start | bytes 245768 | tf_op jit(solution)/shard_map/ppermute | solution.py:329
  43.4 3.3 %collective-permute-start.16 = (bf16[40,1024]{1,0:T(8,128)(2,1)S(1)}, bf16[40,1024]{1,0:T(8,128)(2,1)S(1)}, u32[]{:S(2)}, u32[]{:S(2)}) collective-permute-start(bf16[40,1024]{1,0:T(8,128)(2,1)S(1)} %get-tuple-element.78), channel_id=1, source_target_pairs={{0,30},{1,31},{2,28},{3,29},{4,0},{5,1},{6,2},{7,3},{8,4},{9,5},{1... | collective-permute-start | bytes 245768 | tf_op jit(solution)/shard_map/ppermute | solution.py:329
  44.2 3.7 %collective-permute-start.18 = (bf16[40,1024]{1,0:T(8,128)(2,1)S(1)}, bf16[40,1024]{1,0:T(8,128)(2,1)S(1)}, u32[]{:S(2)}, u32[]{:S(2)}) collective-permute-start(bf16[40,1024]{1,0:T(8,128)(2,1)S(1)} %get-tuple-element.80), channel_id=1, source_target_pairs={{0,224},{1,225},{2,226},{3,227},{4,228},{5,229},{6,230},{7,231},{8... | collective-permute-start | bytes 245768 | tf_op jit(solution)/shard_map/ppermute | solution.py:329
  47.9 7.3 %collective-permute-start.20 = (bf16[80,1024]{1,0:T(8,128)(2,1)S(1)}, bf16[80,1024]{1,0:T(8,128)(2,1)S(1)}, u32[]{:S(2)}, u32[]{:S(2)}) collective-permute-start(bf16[80,1024]{1,0:T(8,128)(2,1)S(1)} %shard_map.96.m1), channel_id=1, source_target_pairs={{0,1},{1,0},{2,3},{3,2},{4,5},{5,4},{6,7},{7,6},{8,9},{9,8},{10,11... | collective-permute-start | bytes 491528 | tf_op jit(solution)/shard_map/ppermute | solution.py:329
  54.1 1.4 %collective-permute-start.19 = (bf16[80,1024]{1,0:T(8,128)(2,1)S(1)}, bf16[80,1024]{1,0:T(8,128)(2,1)S(1)}, u32[]{:S(2)}, u32[]{:S(2)}) collective-permute-start(bf16[80,1024]{1,0:T(8,128)(2,1)S(1)} %shard_map.94.m0), channel_id=1, source_target_pairs={{0,1},{1,0},{2,3},{3,2},{4,5},{5,4},{6,7},{7,6},{8,9},{9,8},{10,11... | collective-permute-start | bytes 491528 | tf_op jit(solution)/shard_map/ppermute | solution.py:329

commit v16 on v15

--- a/solution.py
+++ b/solution.py
@@ -265,11 +265,11 @@
         outs[p][...] = total[p * ROWS : (p + 1) * ROWS].astype(jnp.bfloat16)
 
 
-def join_kernel(p0, p1, out):
-    out[...] = joined((p0, p1)).astype(jnp.bfloat16)
-
-
-def place_kernel(m0, m1, s0, s1, out, held, sems):
+def join_kernel(second, first, out):
+    out[...] = joined((first, second)).astype(jnp.bfloat16)
+
+
+def place_kernel(m1, m0, s1, s0, out, held, sems):
     core = core_index()
     quad, slot, level, row, col = kept_place(iota((1, KEPT), 1))
     row, col = patch_place(quad, row, col)
@@ -393,10 +393,11 @@
     lon = home(lon, 0, 1)
     lat, own = call(sum_kernel, piece * 2, (part_b, other_b), 10**10, 8)
     lat = home(lat, 1, 0)
-    mine_a = call(join_kernel, half, (diag, lon), 10**10, 8)
+    mine_a = call(join_kernel, half, (lon, diag), 10**10, 8)
     mine_a, lat, own = tied(mine_a, lat, own)
-    mine_b = call(join_kernel, half, (lat, own), 10**6, 8)
-    operands = (mine_a, mine_b, core_swap(mine_a), core_swap(mine_b))
+    mine_b = call(join_kernel, half, (own, lat), 10**6, 8)
+    sib_b = core_swap(mine_b)
+    operands = (mine_b, mine_a, sib_b, core_swap(mine_a))
     result = place_rows((rows * cols, levels, width), operands)
     return result.reshape(rows, cols, levels, width).transpose(2, 0, 1, 3)
 

time: 57 us -> 57 us (level)
  no operation moved by 1% of the time
where the time goes in v16:
time: 57 us; the launch traced here: 56.9 us
  starting transfers between devices  26.2 us (46%)
  waiting for transfers between devices  18.2 us (32%)
  Pallas kernels  11.2 us (20%)
  local copies, waits for them, and re-layouts  0.98 us (2%)
    ppermute x21, starting transfers between devices, move(): return lax.ppermute(value, AXES, pairs(counts, target))  26.2 us
    ppermute x21, waiting for transfers between devices, move(): return lax.ppermute(value, AXES, pairs(counts, target))  18.2 us
    pallas_call x15, Pallas kernels, call(): pl.pallas_call(kernel, out_shape=shapes, in_specs=[pl.BlockSpec(memory_sp...  9.91 us
    pallas_call x1, Pallas kernels, place_rows(): pl.pallas_call(place_kernel, out_shape=jax.ShapeDtypeStruct(shape, jnp.bf...  1.24 us
  transfers between devices with their start and end apart: 21, of which 12 were waited for; matrix products, arithmetic and copies ran while one was open for 0% of the time, Pallas kernels for 17%

profile of v16, /device:TPU:1, one launch (start us, length us, event | category | flops | bytes accessed | tf_op | source)
XLA Modules:
  0.0 56.9 jit_solution(5939936996382394412)
XLA Ops:
  0.0 3.2 %collective-permute-start.3 = (bf16[3,1024,256]{2,1,0:T(8,128)(2,1)}, bf16[3,1024,256]{2,1,0:T(8,128)(2,1)S(1)}, u32[]{:S(2)}, u32[]{:S(2)}) collective-permute-start(bf16[3,1024,256]{2,1,0:T(8,128)(2,1)} %bitcast.8), channel_id=1, source_target_pairs={{0,1},{1,0},{2,3},{3,2},{4,5},{5,4},{6,7},{7,6},{8,9},{9,8},{10,11... | collective-permute-start | bytes 4718600 | tf_op jit(solution)/shard_map/ppermute | solution.py:329
  3.2 0.5 collective-permute-start.2
  3.8 0.7 %copy-done.7 = f32[2,4,37]{2,1,0:T(4,128)S(1)} copy-done((f32[2,4,37]{2,1,0:T(4,128)S(1)}, f32[2,4,37]{2,1,0:T(4,128)}, u32[]{:S(2)}) %copy-start.7) | copy-done | bytes 1208
  4.4 0.7 %shard_map.82.bias = bf16[32,256]{1,0:T(8,128)(2,1)S(1)} custom-call(f32[2,4,37]{2,1,0:T(4,128)S(1)} %copy-done.7), custom_call_target="tpu_custom_call" | custom-call | flops 5000000000 | bytes 17568 | tf_op jit(solution)/shard_map/pallas_call | solution.py:309
  5.2 2.1 %shard_map.83 = (bf16[160,256]{1,0:T(8,128)(2,1)S(1)}, bf16[160,256]{1,0:T(8,128)(2,1)S(1)}) custom-call(bf16[72,4,1024]{2,1,0:T(4,128)(2,1)S(1)} %bitcast.11, bf16[3,1024,256]{2,1,0:T(8,128)(2,1)S(1)} %bitcast.10, bf16[32,256]{1,0:T(8,128)(2,1)S(1)} %shard_map.82.bias), custom_call_target="tpu_custom_call" | custom-call | flops 1000000000 | bytes 2342912 | tf_op jit(solution)/shard_map/pallas_call | solution.py:309
  8.0 0.6 %collective-permute-done.1.o1 = bf16[160,256]{1,0:T(8,128)(2,1)S(1)} collective-permute-done((bf16[160,256]{1,0:T(8,128)(2,1)S(1)}, bf16[160,256]{1,0:T(8,128)(2,1)S(1)}, u32[]{:S(2)}, u32[]{:S(2)}) %collective-permute-start.1) | collective-permute-done | bytes 81952 | tf_op jit(solution)/shard_map/ppermute | solution.py:329
  9.1 1.5 %collective-permute-start.8 = (bf16[80,1024]{1,0:T(8,128)(2,1)S(1)}, bf16[80,1024]{1,0:T(8,128)(2,1)S(1)}, u32[]{:S(2)}, u32[]{:S(2)}) collective-permute-start(bf16[80,1024]{1,0:T(8,128)(2,1)S(1)} %get-tuple-element.62.mine), channel_id=1, source_target_pairs={{0,2},{1,3},{2,0},{3,1},{4,6},{5,7},{6,4},{7,5},{8,10},{9,11},{10,... | collective-permute-start | bytes 491528 | tf_op jit(solution)/shard_map/ppermute | solution.py:329
  10.5 0.7 %shard_map.85.b_own = bf16[32,256]{1,0:T(8,128)(2,1)S(1)} custom-call(f32[2,4,37]{2,1,0:T(4,128)S(1)} %copy-done.8), custom_call_target="tpu_custom_call" | custom-call | flops 1000000000 | bytes 17568 | tf_op jit(solution)/shard_map/pallas_call | solution.py:309
  11.3 0.9 %collective-permute-start.5 = (bf16[32,256]{1,0:T(8,128)(2,1)S(1)}, bf16[32,256]{1,0:T(8,128)(2,1)S(1)}, u32[]{:S(2)}, u32[]{:S(2)}) collective-permute-start(bf16[32,256]{1,0:T(8,128)(2,1)S(1)} %shard_map.85.b_own), channel_id=1, source_target_pairs={{0,1},{1,0},{2,3},{3,2},{4,5},{5,4},{6,7},{7,6},{8,9},{9,8},{10,11... | collective-permute-start | bytes 49160 | tf_op jit(solution)/shard_map/ppermute | solution.py:329
  12.9 0.8 %collective-permute-start.11 = (bf16[1024,1024]{1,0:T(8,128)(2,1)S(1)}, bf16[1024,1024]{1,0:T(8,128)(2,1)S(1)}, u32[]{:S(2)}, u32[]{:S(2)}) collective-permute-start(bf16[1024,1024]{1,0:T(8,128)(2,1)S(1)} %copy-done), channel_id=1, source_target_pairs={{0,1},{1,0},{2,3},{3,2},{4,5},{5,4},{6,7},{7,6},{8,9},{9,8},{10,11... | collective-permute-start | bytes 6291464 | tf_op jit(solution)/shard_map/ppermute | solution.py:329
  13.7 0.9 %collective-permute-done.4.other = bf16[80,1024]{1,0:T(8,128)(2,1)S(1)} collective-permute-done((bf16[80,1024]{1,0:T(8,128)(2,1)S(1)}, bf16[80,1024]{1,0:T(8,128)(2,1)S(1)}, u32[]{:S(2)}, u32[]{:S(2)}) %collective-permute-start.4) | collective-permute-done | bytes 163872 | tf_op jit(solution)/shard_map/ppermute | solution.py:329
  14.7 1.0 %collective-permute-start.6 = (bf16[40,1024]{1,0:T(8,128)(2,1)S(1)}, bf16[40,1024]{1,0:T(8,128)(2,1)S(1)}, u32[]{:S(2)}, u32[]{:S(2)}) collective-permute-start(bf16[40,1024]{1,0:T(8,128)(2,1)S(1)} %get-tuple-element.60), channel_id=1, source_target_pairs={{0,36},{1,37},{2,38},{3,39},{4,40},{5,41},{6,42},{7,43},{8,44},{9,... | collective-permute-start | bytes 245768 | tf_op jit(solution)/shard_map/ppermute | solution.py:329
  15.7 1.3 %collective-permute-start.7 = (bf16[40,1024]{1,0:T(8,128)(2,1)S(1)}, bf16[40,1024]{1,0:T(8,128)(2,1)S(1)}, u32[]{:S(2)}, u32[]{:S(2)}) collective-permute-start(bf16[40,1024]{1,0:T(8,128)(2,1)S(1)} %get-tuple-element.61), channel_id=1, source_target_pairs={{0,4},{1,5},{2,6},{3,7},{4,8},{5,9},{6,10},{7,11},{8,12},{9,13},{1... | collective-permute-start | bytes 245768 | tf_op jit(solution)/shard_map/ppermute | solution.py:329
  17.0 1.1 %collective-permute-done.8.other = bf16[80,1024]{1,0:T(8,128)(2,1)S(1)} collective-permute-done((bf16[80,1024]{1,0:T(8,128)(2,1)S(1)}, bf16[80,1024]{1,0:T(8,128)(2,1)S(1)}, u32[]{:S(2)}, u32[]{:S(2)}) %collective-permute-start.8) | collective-permute-done | bytes 163872 | tf_op jit(solution)/shard_map/ppermute | solution.py:329
  18.2 0.6 collective-permute-start.9
  18.8 6.4 %collective-permute-done.6.p0 = bf16[40,1024]{1,0:T(8,128)(2,1)S(1)} collective-permute-done((bf16[40,1024]{1,0:T(8,128)(2,1)S(1)}, bf16[40,1024]{1,0:T(8,128)(2,1)S(1)}, u32[]{:S(2)}, u32[]{:S(2)}) %collective-permute-start.6) | collective-permute-done | bytes 81952 | tf_op jit(solution)/shard_map/ppermute | solution.py:329
  25.4 1.6 %shard_map.90 = (bf16[80,1024]{1,0:T(8,128)(2,1)S(1)}, bf16[80,1024]{1,0:T(8,128)(2,1)S(1)}) custom-call(bf16[80,1024]{1,0:T(8,128)(2,1)S(1)} %shard_map.88.xn_a, bf16[40,1024]{1,0:T(8,128)(2,1)S(1)} %collective-permute-done.9.p2.p0, bf16[40,1024]{1,0:T(8,128)(2,1)S(1)} %get-tuple-element.65.p3.p1, bf16[3,1024,256]{2,1,0:T(8,128)(2,1)S(1)} %bitcast.9, ...), custom_call_target="tpu_custom_call" | custom-call | flops 1000000000 | bytes 4882432 | tf_op jit(solution)/shard_map/pallas_call | solution.py:309
  27.3 1.4 %collective-permute-start.14 = (bf16[80,1024]{1,0:T(8,128)(2,1)S(1)}, bf16[80,1024]{1,0:T(8,128)(2,1)S(1)}, u32[]{:S(2)}, u32[]{:S(2)}) collective-permute-start(bf16[80,1024]{1,0:T(8,128)(2,1)S(1)} %get-tuple-element.76.mine), channel_id=1, source_target_pairs={{0,2},{1,3},{2,0},{3,1},{4,6},{5,7},{6,4},{7,5},{8,10},{9,11},{10,... | collective-permute-start | bytes 491528 | tf_op jit(solution)/shard_map/ppermute | solution.py:329
  28.8 2.7 %collective-permute-done.10.other = bf16[80,1024]{1,0:T(8,128)(2,1)S(1)} collective-permute-done((bf16[80,1024]{1,0:T(8,128)(2,1)S(1)}, bf16[80,1024]{1,0:T(8,128)(2,1)S(1)}, u32[]{:S(2)}, u32[]{:S(2)}) %collective-permute-start.10) | collective-permute-done | bytes 163872 | tf_op jit(solution)/shard_map/ppermute | solution.py:329
  31.5 1.8 %shard_map.91.mine = bf16[80,1024]{1,0:T(8,128)(2,1)S(1)} custom-call(bf16[80,1024]{1,0:T(8,128)(2,1)S(1)} %get-tuple-element.69.mine, bf16[80,1024]{1,0:T(8,128)(2,1)S(1)} %collective-permute-done.10.other, bf16[40,1024]{1,0:T(8,128)(2,1)S(1)} %collective-permute-done.6.p0, bf16[40,1024]{1,0:T(8,128)(2,1)S(1)} %collective-permute-done.7.p1, ...), custom_call_target="tpu_custom_call" | custom-call | flops 1000000000 | bytes 9043968 | tf_op jit(solution)/shard_map/pallas_call | solution.py:309
  33.4 0.6 collective-permute-done.14.other
  34.0 1.8 %shard_map.93.mine = bf16[80,1024]{1,0:T(8,128)(2,1)S(1)} custom-call(bf16[80,1024]{1,0:T(8,128)(2,1)S(1)} %get-tuple-element.76.mine, bf16[80,1024]{1,0:T(8,128)(2,1)S(1)} %collective-permute-done.14.other, bf16[40,1024]{1,0:T(8,128)(2,1)S(1)} %collective-permute-done.9.p2.p0, bf16[40,1024]{1,0:T(8,128)(2,1)S(1)} %get-tuple-element.65.p3.p1, ...), custom_call_target="tpu_custom_call" | custom-call | flops 1000000000 | bytes 9043968 | tf_op jit(solution)/shard_map/pallas_call | solution.py:309
  35.8 0.9 %collective-permute-start.17 = (bf16[80,1024]{1,0:T(8,128)(2,1)S(1)}, bf16[80,1024]{1,0:T(8,128)(2,1)S(1)}, u32[]{:S(2)}, u32[]{:S(2)}) collective-permute-start(bf16[80,1024]{1,0:T(8,128)(2,1)S(1)} %shard_map.93.mine), channel_id=1, source_target_pairs={{0,2},{1,3},{2,0},{3,1},{4,6},{5,7},{6,4},{7,5},{8,10},{9,11},{10,... | collective-permute-start | bytes 491528 | tf_op jit(solution)/shard_map/ppermute | solution.py:329
  36.7 1.7 %collective-permute-done.13.other = bf16[80,1024]{1,0:T(8,128)(2,1)S(1)} collective-permute-done((bf16[80,1024]{1,0:T(8,128)(2,1)S(1)}, bf16[80,1024]{1,0:T(8,128)(2,1)S(1)}, u32[]{:S(2)}, u32[]{:S(2)}) %collective-permute-start.13) | collective-permute-done | bytes 163872 | tf_op jit(solution)/shard_map/ppermute | solution.py:329
  38.5 3.5 %collective-permute-start.15 = (bf16[40,1024]{1,0:T(8,128)(2,1)S(1)}, bf16[40,1024]{1,0:T(8,128)(2,1)S(1)}, u32[]{:S(2)}, u32[]{:S(2)}) collective-permute-start(bf16[40,1024]{1,0:T(8,128)(2,1)S(1)} %get-tuple-element.77), channel_id=1, source_target_pairs={{0,30},{1,31},{2,28},{3,29},{4,0},{5,1},{6,2},{7,3},{8,4},{9,5},{1... | collective-permute-start | bytes 245768 | tf_op jit(solution)/shard_map/ppermute | solution.py:329
  42.1 2.1 %collective-permute-start.16 = (bf16[40,1024]{1,0:T(8,128)(2,1)S(1)}, bf16[40,1024]{1,0:T(8,128)(2,1)S(1)}, u32[]{:S(2)}, u32[]{:S(2)}) collective-permute-start(bf16[40,1024]{1,0:T(8,128)(2,1)S(1)} %get-tuple-element.78), channel_id=1, source_target_pairs={{0,254},{1,255},{2,252},{3,253},{4,224},{5,225},{6,226},{7,227},{8... | collective-permute-start | bytes 245768 | tf_op jit(solution)/shard_map/ppermute | solution.py:329
  44.2 1.0 %collective-permute-start.18 = (bf16[40,1024]{1,0:T(8,128)(2,1)S(1)}, bf16[40,1024]{1,0:T(8,128)(2,1)S(1)}, u32[]{:S(2)}, u32[]{:S(2)}) collective-permute-start(bf16[40,1024]{1,0:T(8,128)(2,1)S(1)} %get-tuple-element.80), channel_id=1, source_target_pairs={{0,224},{1,225},{2,226},{3,227},{4,228},{5,229},{6,230},{7,231},{8... | collective-permute-start | bytes 245768 | tf_op jit(solution)/shard_map/ppermute | solution.py:329
  45.1 1.2 %collective-permute-done.16.first = bf16[40,1024]{1,0:T(8,128)(2,1)S(1)} collective-permute-done((bf16[40,1024]{1,0:T(8,128)(2,1)S(1)}, bf16[40,1024]{1,0:T(8,128)(2,1)S(1)}, u32[]{:S(2)}, u32[]{:S(2)}) %collective-permute-start.16) | collective-permute-done | bytes 81952 | tf_op jit(solution)/shard_map/ppermute | solution.py:329
  46.3 1.2 %collective-permute-done.18.first = bf16[40,1024]{1,0:T(8,128)(2,1)S(1)} collective-permute-done((bf16[40,1024]{1,0:T(8,128)(2,1)S(1)}, bf16[40,1024]{1,0:T(8,128)(2,1)S(1)}, u32[]{:S(2)}, u32[]{:S(2)}) %collective-permute-start.18) | collective-permute-done | bytes 81952 | tf_op jit(solution)/shard_map/ppermute | solution.py:329
  47.6 6.5 %collective-permute-start.19 = (bf16[80,1024]{1,0:T(8,128)(2,1)S(1)}, bf16[80,1024]{1,0:T(8,128)(2,1)S(1)}, u32[]{:S(2)}, u32[]{:S(2)}) collective-permute-start(bf16[80,1024]{1,0:T(8,128)(2,1)S(1)} %shard_map.96.m1), channel_id=1, source_target_pairs={{0,1},{1,0},{2,3},{3,2},{4,5},{5,4},{6,7},{7,6},{8,9},{9,8},{10,11... | collective-permute-start | bytes 491528 | tf_op jit(solution)/shard_map/ppermute | solution.py:329
  54.2 0.9 %collective-permute-done.19.s1 = bf16[80,1024]{1,0:T(8,128)(2,1)S(1)} collective-permute-done((bf16[80,1024]{1,0:T(8,128)(2,1)S(1)}, bf16[80,1024]{1,0:T(8,128)(2,1)S(1)}, u32[]{:S(2)}, u32[]{:S(2)}) %collective-permute-start.19) | collective-permute-done | bytes 163872 | tf_op jit(solution)/shard_map/ppermute | solution.py:329
  55.5 1.2 %shard_map.97 = bf16[72,4,1024]{2,1,0:T(4,128)(2,1)} custom-call(bf16[80,1024]{1,0:T(8,128)(2,1)S(1)} %shard_map.96.m1, bf16[80,1024]{1,0:T(8,128)(2,1)S(1)} %shard_map.94.m0, bf16[80,1024]{1,0:T(8,128)(2,1)S(1)} %collective-permute-done.19.s1, bf16[80,1024]{1,0:T(8,128)(2,1)S(1)} %collective-permute-done.20.s0), custom_call_target="tpu_custom_call" | custom-call | flops 200000000 | bytes 2000000 | tf_op jit(solution)/shard_map/pallas_call | solution.py:295
  (44 shorter events, 3.3 us)
Async XLA Ops:
  0.0 5.2 %copy-start.5 = (bf16[1024,3,256]{2,0,1:T(8,128)(2,1)S(1)}, bf16[1024,3,256]{2,0,1:T(8,128)(2,1)}, u32[]{:S(2)}) copy-start(bf16[1024,3,256]{2,0,1:T(8,128)(2,1)} %param.9) | copy-start | bytes 4718596
  0.0 5.2 %copy-start.6 = (bf16[4,6,12,1024]{3,0,2,1:T(4,128)(2,1)S(1)}, bf16[4,6,12,1024]{3,0,2,1:T(4,128)(2,1)}, u32[]{:S(2)}) copy-start(bf16[4,6,12,1024]{3,0,2,1:T(4,128)(2,1)} %param.8) | copy-start | bytes 1769476
  0.0 8.6 %collective-permute-start.3 = (bf16[3,1024,256]{2,1,0:T(8,128)(2,1)}, bf16[3,1024,256]{2,1,0:T(8,128)(2,1)S(1)}, u32[]{:S(2)}, u32[]{:S(2)}) collective-permute-start(bf16[3,1024,256]{2,1,0:T(8,128)(2,1)} %bitcast.8), channel_id=1, source_target_pairs={{0,1},{1,0},{2,3},{3,2},{4,5},{5,4},{6,7},{7,6},{8,9},{9,8},{10,11... | collective-permute-start | bytes 4718600 | tf_op jit(solution)/shard_map/ppermute | solution.py:329
  3.2 4.0 %collective-permute-start = (bf16[256,1024]{1,0:T(8,128)(2,1)}, bf16[256,1024]{1,0:T(8,128)(2,1)S(1)}, u32[]{:S(2)}, u32[]{:S(2)}) collective-permute-start(bf16[256,1024]{1,0:T(8,128)(2,1)} %w0.1), channel_id=1, source_target_pairs={{0,1},{1,0},{2,3},{3,2},{4,5},{5,4},{6,7},{7,6},{8,9},{9,8},{10,11... | collective-permute-start | bytes 1572872 | tf_op jit(solution)/shard_map/ppermute | solution.py:329
  3.2 4.7 %collective-permute-start.2 = (bf16[256,1024]{1,0:T(8,128)(2,1)}, bf16[256,1024]{1,0:T(8,128)(2,1)S(1)}, u32[]{:S(2)}, u32[]{:S(2)}) collective-permute-start(bf16[256,1024]{1,0:T(8,128)(2,1)} %o_own.1), channel_id=1, source_target_pairs={{0,1},{1,0},{2,3},{3,2},{4,5},{5,4},{6,7},{7,6},{8,9},{9,8},{10,11... | collective-permute-start | bytes 1572872 | tf_op jit(solution)/shard_map/ppermute | solution.py:329
  3.8 0.7 %copy-start.7 = (f32[2,4,37]{2,1,0:T(4,128)S(1)}, f32[2,4,37]{2,1,0:T(4,128)}, u32[]{:S(2)}) copy-start(f32[2,4,37]{2,1,0:T(4,128)} %table.2) | copy-start | bytes 3556
  5.2 3.5 %copy-start.4 = (bf16[256,1024]{1,0:T(8,128)(2,1)S(1)}, bf16[256,1024]{1,0:T(8,128)(2,1)}, u32[]{:S(2)}) copy-start(bf16[256,1024]{1,0:T(8,128)(2,1)} %w0.1) | copy-start | bytes 1572868
  5.2 5.4 %copy-start.8 = (f32[2,4,37]{2,1,0:T(4,128)S(1)}, f32[2,4,37]{2,1,0:T(4,128)}, u32[]{:S(2)}) copy-start(f32[2,4,37]{2,1,0:T(4,128)} %table.2) | copy-start | bytes 3556
  7.3 1.4 %collective-permute-start.1 = (bf16[160,256]{1,0:T(8,128)(2,1)S(1)}, bf16[160,256]{1,0:T(8,128)(2,1)S(1)}, u32[]{:S(2)}, u32[]{:S(2)}) collective-permute-start(bf16[160,256]{1,0:T(8,128)(2,1)S(1)} %get-tuple-element.49), channel_id=1, source_target_pairs={{0,1},{1,0},{2,3},{3,2},{4,5},{5,4},{6,7},{7,6},{8,9},{9,8},{10,11... | collective-permute-start | bytes 245768 | tf_op jit(solution)/shard_map/ppermute | solution.py:329
  9.0 5.6 %collective-permute-start.4 = (bf16[80,1024]{1,0:T(8,128)(2,1)S(1)}, bf16[80,1024]{1,0:T(8,128)(2,1)S(1)}, u32[]{:S(2)}, u32[]{:S(2)}) collective-permute-start(bf16[80,1024]{1,0:T(8,128)(2,1)S(1)} %get-tuple-element.52.mine), channel_id=1, source_target_pairs={{0,2},{1,3},{2,0},{3,1},{4,6},{5,7},{6,4},{7,5},{8,10},{9,11},{10,... | collective-permute-start | bytes 491528 | tf_op jit(solution)/shard_map/ppermute | solution.py:329
  9.1 9.0 %collective-permute-start.8 = (bf16[80,1024]{1,0:T(8,128)(2,1)S(1)}, bf16[80,1024]{1,0:T(8,128)(2,1)S(1)}, u32[]{:S(2)}, u32[]{:S(2)}) collective-permute-start(bf16[80,1024]{1,0:T(8,128)(2,1)S(1)} %get-tuple-element.62.mine), channel_id=1, source_target_pairs={{0,2},{1,3},{2,0},{3,1},{4,6},{5,7},{6,4},{7,5},{8,10},{9,11},{10,... | collective-permute-start | bytes 491528 | tf_op jit(solution)/shard_map/ppermute | solution.py:329
  10.5 3.1 %copy-start.1 = (bf16[1024,1024]{1,0:T(8,128)(2,1)S(1)}, bf16[1024,1024]{1,0:T(8,128)(2,1)}, u32[]{:S(2)}) copy-start(bf16[1024,1024]{1,0:T(8,128)(2,1)} %d0.3) | copy-start | bytes 6291460
  11.3 1.6 %copy-start = (bf16[1024,1024]{1,0:T(8,128)(2,1)S(1)}, bf16[1024,1024]{1,0:T(8,128)(2,1)}, u32[]{:S(2)}) copy-start(bf16[1024,1024]{1,0:T(8,128)(2,1)} %u0.3) | copy-start | bytes 6291460
  11.3 2.4 %collective-permute-start.5 = (bf16[32,256]{1,0:T(8,128)(2,1)S(1)}, bf16[32,256]{1,0:T(8,128)(2,1)S(1)}, u32[]{:S(2)}, u32[]{:S(2)}) collective-permute-start(bf16[32,256]{1,0:T(8,128)(2,1)S(1)} %shard_map.85.b_own), channel_id=1, source_target_pairs={{0,1},{1,0},{2,3},{3,2},{4,5},{5,4},{6,7},{7,6},{8,9},{9,8},{10,11... | collective-permute-start | bytes 49160 | tf_op jit(solution)/shard_map/ppermute | solution.py:329
  12.9 18.6 %collective-permute-start.11 = (bf16[1024,1024]{1,0:T(8,128)(2,1)S(1)}, bf16[1024,1024]{1,0:T(8,128)(2,1)S(1)}, u32[]{:S(2)}, u32[]{:S(2)}) collective-permute-start(bf16[1024,1024]{1,0:T(8,128)(2,1)S(1)} %copy-done), channel_id=1, source_target_pairs={{0,1},{1,0},{2,3},{3,2},{4,5},{5,4},{6,7},{7,6},{8,9},{9,8},{10,11... | collective-permute-start | bytes 6291464 | tf_op jit(solution)/shard_map/ppermute | solution.py:329
  13.7 17.8 %collective-permute-start.12 = (bf16[1024,1024]{1,0:T(8,128)(2,1)S(1)}, bf16[1024,1024]{1,0:T(8,128)(2,1)S(1)}, u32[]{:S(2)}, u32[]{:S(2)}) collective-permute-start(bf16[1024,1024]{1,0:T(8,128)(2,1)S(1)} %copy-done.1), channel_id=1, source_target_pairs={{0,1},{1,0},{2,3},{3,2},{4,5},{5,4},{6,7},{7,6},{8,9},{9,8},{10,11... | collective-permute-start | bytes 6291464 | tf_op jit(solution)/shard_map/ppermute | solution.py:329
  14.7 10.5 %collective-permute-start.6 = (bf16[40,1024]{1,0:T(8,128)(2,1)S(1)}, bf16[40,1024]{1,0:T(8,128)(2,1)S(1)}, u32[]{:S(2)}, u32[]{:S(2)}) collective-permute-start(bf16[40,1024]{1,0:T(8,128)(2,1)S(1)} %get-tuple-element.60), channel_id=1, source_target_pairs={{0,36},{1,37},{2,38},{3,39},{4,40},{5,41},{6,42},{7,43},{8,44},{9,... | collective-permute-start | bytes 245768 | tf_op jit(solution)/shard_map/ppermute | solution.py:329
  15.7 9.5 %collective-permute-start.7 = (bf16[40,1024]{1,0:T(8,128)(2,1)S(1)}, bf16[40,1024]{1,0:T(8,128)(2,1)S(1)}, u32[]{:S(2)}, u32[]{:S(2)}) collective-permute-start(bf16[40,1024]{1,0:T(8,128)(2,1)S(1)} %get-tuple-element.61), channel_id=1, source_target_pairs={{0,4},{1,5},{2,6},{3,7},{4,8},{5,9},{6,10},{7,11},{8,12},{9,13},{1... | collective-permute-start | bytes 245768 | tf_op jit(solution)/shard_map/ppermute | solution.py:329
  18.2 7.2 %copy-start.2 = (bf16[1024,3,256]{2,0,1:T(8,128)(2,1)S(1)}, bf16[1024,3,256]{2,0,1:T(8,128)(2,1)}, u32[]{:S(2)}) copy-start(bf16[1024,3,256]{2,0,1:T(8,128)(2,1)} %param.10) | copy-start | bytes 4718596
  18.2 7.2 %copy-start.3 = (bf16[256,1024]{1,0:T(8,128)(2,1)S(1)}, bf16[256,1024]{1,0:T(8,128)(2,1)}, u32[]{:S(2)}) copy-start(bf16[256,1024]{1,0:T(8,128)(2,1)} %o_own.1) | copy-start | bytes 1572868
  18.2 7.2 %collective-permute-start.9 = (bf16[40,1024]{1,0:T(8,128)(2,1)S(1)}, bf16[40,1024]{1,0:T(8,128)(2,1)S(1)}, u32[]{:S(2)}, u32[]{:S(2)}) collective-permute-start(bf16[40,1024]{1,0:T(8,128)(2,1)S(1)} %get-tuple-element.64), channel_id=1, source_target_pairs={{0,32},{1,33},{2,34},{3,35},{4,36},{5,37},{6,38},{7,39},{8,40},{9,... | collective-permute-start | bytes 245768 | tf_op jit(solution)/shard_map/ppermute | solution.py:329
  27.0 4.4 %collective-permute-start.10 = (bf16[80,1024]{1,0:T(8,128)(2,1)S(1)}, bf16[80,1024]{1,0:T(8,128)(2,1)S(1)}, u32[]{:S(2)}, u32[]{:S(2)}) collective-permute-start(bf16[80,1024]{1,0:T(8,128)(2,1)S(1)} %get-tuple-element.69.mine), channel_id=1, source_target_pairs={{0,2},{1,3},{2,0},{3,1},{4,6},{5,7},{6,4},{7,5},{8,10},{9,11},{10,... | collective-permute-start | bytes 491528 | tf_op jit(solution)/shard_map/ppermute | solution.py:329
  27.3 6.6 %collective-permute-start.14 = (bf16[80,1024]{1,0:T(8,128)(2,1)S(1)}, bf16[80,1024]{1,0:T(8,128)(2,1)S(1)}, u32[]{:S(2)}, u32[]{:S(2)}) collective-permute-start(bf16[80,1024]{1,0:T(8,128)(2,1)S(1)} %get-tuple-element.76.mine), channel_id=1, source_target_pairs={{0,2},{1,3},{2,0},{3,1},{4,6},{5,7},{6,4},{7,5},{8,10},{9,11},{10,... | collective-permute-start | bytes 491528 | tf_op jit(solution)/shard_map/ppermute | solution.py:329
  33.3 5.2 %collective-permute-start.13 = (bf16[80,1024]{1,0:T(8,128)(2,1)S(1)}, bf16[80,1024]{1,0:T(8,128)(2,1)S(1)}, u32[]{:S(2)}, u32[]{:S(2)}) collective-permute-start(bf16[80,1024]{1,0:T(8,128)(2,1)S(1)} %shard_map.91.mine), channel_id=1, source_target_pairs={{0,2},{1,3},{2,0},{3,1},{4,6},{5,7},{6,4},{7,5},{8,10},{9,11},{10,... | collective-permute-start | bytes 491528 | tf_op jit(solution)/shard_map/ppermute | solution.py:329
  35.8 8.3 %collective-permute-start.17 = (bf16[80,1024]{1,0:T(8,128)(2,1)S(1)}, bf16[80,1024]{1,0:T(8,128)(2,1)S(1)}, u32[]{:S(2)}, u32[]{:S(2)}) collective-permute-start(bf16[80,1024]{1,0:T(8,128)(2,1)S(1)} %shard_map.93.mine), channel_id=1, source_target_pairs={{0,2},{1,3},{2,0},{3,1},{4,6},{5,7},{6,4},{7,5},{8,10},{9,11},{10,... | collective-permute-start | bytes 491528 | tf_op jit(solution)/shard_map/ppermute | solution.py:329
  38.5 6.6 %collective-permute-start.15 = (bf16[40,1024]{1,0:T(8,128)(2,1)S(1)}, bf16[40,1024]{1,0:T(8,128)(2,1)S(1)}, u32[]{:S(2)}, u32[]{:S(2)}) collective-permute-start(bf16[40,1024]{1,0:T(8,128)(2,1)S(1)} %get-tuple-element.77), channel_id=1, source_target_pairs={{0,30},{1,31},{2,28},{3,29},{4,0},{5,1},{6,2},{7,3},{8,4},{9,5},{1... | collective-permute-start | bytes 245768 | tf_op jit(solution)/shard_map/ppermute | solution.py:329
  42.1 4.2 %collective-permute-start.16 = (bf16[40,1024]{1,0:T(8,128)(2,1)S(1)}, bf16[40,1024]{1,0:T(8,128)(2,1)S(1)}, u32[]{:S(2)}, u32[]{:S(2)}) collective-permute-start(bf16[40,1024]{1,0:T(8,128)(2,1)S(1)} %get-tuple-element.78), channel_id=1, source_target_pairs={{0,254},{1,255},{2,252},{3,253},{4,224},{5,225},{6,226},{7,227},{8... | collective-permute-start | bytes 245768 | tf_op jit(solution)/shard_map/ppermute | solution.py:329
  44.2 3.4 %collective-permute-start.18 = (bf16[40,1024]{1,0:T(8,128)(2,1)S(1)}, bf16[40,1024]{1,0:T(8,128)(2,1)S(1)}, u32[]{:S(2)}, u32[]{:S(2)}) collective-permute-start(bf16[40,1024]{1,0:T(8,128)(2,1)S(1)} %get-tuple-element.80), channel_id=1, source_target_pairs={{0,224},{1,225},{2,226},{3,227},{4,228},{5,229},{6,230},{7,231},{8... | collective-permute-start | bytes 245768 | tf_op jit(solution)/shard_map/ppermute | solution.py:329
  47.6 7.6 %collective-permute-start.19 = (bf16[80,1024]{1,0:T(8,128)(2,1)S(1)}, bf16[80,1024]{1,0:T(8,128)(2,1)S(1)}, u32[]{:S(2)}, u32[]{:S(2)}) collective-permute-start(bf16[80,1024]{1,0:T(8,128)(2,1)S(1)} %shard_map.96.m1), channel_id=1, source_target_pairs={{0,1},{1,0},{2,3},{3,2},{4,5},{5,4},{6,7},{7,6},{8,9},{9,8},{10,11... | collective-permute-start | bytes 491528 | tf_op jit(solution)/shard_map/ppermute | solution.py:329
  54.1 1.4 %collective-permute-start.20 = (bf16[80,1024]{1,0:T(8,128)(2,1)S(1)}, bf16[80,1024]{1,0:T(8,128)(2,1)S(1)}, u32[]{:S(2)}, u32[]{:S(2)}) collective-permute-start(bf16[80,1024]{1,0:T(8,128)(2,1)S(1)} %shard_map.94.m0), channel_id=1, source_target_pairs={{0,1},{1,0},{2,3},{3,2},{4,5},{5,4},{6,7},{7,6},{8,9},{9,8},{10,11... | collective-permute-start | bytes 491528 | tf_op jit(solution)/shard_map/ppermute | solution.py:329

commit v17 on v15

--- a/solution.py
+++ b/solution.py
@@ -186,7 +186,7 @@
     row, col = patch_place(quad, row, col)
     place = (row * 12 + col) * 4 + real_level(level, core_index())
     place = jnp.where(slot < USED, place, -1)
-    store_halves(dot(one_hot(iota((KEPT, PATCH), 1) == place), values), outs)
+    store_three(dot(one_hot(iota((KEPT, PATCH), 1) == place), values), outs)
 
 
 def store_halves(total, outs):
@@ -194,8 +194,13 @@
         outs[h][...] = total[h * HALF : (h + 1) * HALF].astype(jnp.bfloat16)
 
 
+def store_three(total, outs):
+    for out, start, stop in zip(outs, (0, 2 * ROWS, 3 * ROWS), (2 * ROWS, 3 * ROWS, KEPT)):
+        out[...] = total[start:stop].astype(jnp.bfloat16)
+
+
 def partial_kernel(o0, o1, w0, w1, *outs):
-    store_halves(dot(o0[...], w0[...]) + dot(o1[...], w1[...]), outs)
+    store_three(dot(o0[...], w0[...]) + dot(o1[...], w1[...]), outs)
 
 
 def branch_sum(mine, other):
@@ -205,8 +210,8 @@
 
 def residual_kernel(mine, other, base, *outs):
     first = base[...].astype(jnp.float32) + branch_sum(mine, other)
-    for p in range(2):
-        outs[p][...] = first[p * ROWS : (p + 1) * ROWS].astype(jnp.bfloat16)
+    for p, out in enumerate(outs):
+        out[...] = first[p * ROWS : (p + 1) * ROWS].astype(jnp.bfloat16)
 
 
 def joined(pieces):
@@ -354,19 +359,21 @@
     keep, give = call(first_kernel, heads * 2, (tok, w_first, bias1), 10**9, 16)
     keep, give, f1 = tied(keep, give, f1)
     keep, tok, rel_tables = tied(keep, tok, rel_tables)
-    base_a, base_b = call(base_kernel, half * 2, (tok,), 10**9, 8)
+    base_a, base_lat, base_own = call(base_kernel, half + piece * 2, (tok,), 10**9, 8)
     bias2 = call(functools.partial(bias_kernel, 1), features, (rel_tables,), 10**9, 4, table=True)
     bias2_sib = core_swap(bias2)
-    given, up_late, down_late, s1, w_sib = tied(core_swap(give), up_weight, down_weight, s1, w_sib)
+    given, up_late, s1, w_sib = tied(core_swap(give), up_weight, s1, w_sib)
     u1 = core_swap(up_late)
-    d1 = core_swap(down_late)
-    part_a, part_b = call(partial_kernel, half * 2, (keep, given, out_first, f1), 2 * 10**8, 8)
+    part_a, part_lat, part_own = call(partial_kernel, half + piece * 2, (keep, given, out_first, f1), 2 * 10**8, 8)
     other_a = chip_swap(part_a)
-    other_b = chip_swap(part_b)
+    other_lat = chip_swap(part_lat)
+    other_own = chip_swap(part_own)
     other_a, bias2_sib = tied(other_a, bias2_sib)
     diag, lon = call(residual_kernel, piece * 2, (part_a, other_a, base_a), 10**6, 8)
-    diag, lon, part_b = tied(diag, lon, part_b)
-    lat, own = call(residual_kernel, piece * 2, (part_b, other_b, base_b), 10**10, 8)
+    diag, lon, part_lat = tied(diag, lon, part_lat)
+    lat = call(residual_kernel, piece, (part_lat, other_lat, base_lat), 10**10, 8)
+    lat, part_own = tied(lat, part_own)
+    own = call(residual_kernel, piece, (part_own, other_own, base_own), 10**6, 8)
     diag = out_to(diag, 1, 1)
     lon = out_to(lon, 0, 1)
     lat = out_to(lat, 1, 0)
@@ -379,8 +386,10 @@
         10**9,
         16,
     )
+    part_b, down_late = tied(part_b, down_weight)
     other_a = chip_swap(part_a)
     other_b = chip_swap(part_b)
+    d1 = core_swap(down_late)
     mlp = (up_weight, u1, down_weight, d1)
     part_a = call(mlp_kernel, half, (part_a, other_a, diag, lon, *mlp), 10**9, 20)
     part_a, part_b = tied(part_a, part_b)

time: 57 us -> 56.1 us (0.984)
  starting transfers between devices: 25.9 us -> 23.2 us
  waiting for transfers between devices: 18.5 us -> 20.5 us
    ppermute x21 -> x22, starting transfers between devices: 25.9 us -> 23.2 us  [move(): return lax.ppermute(value, AXES, pairs(counts, target))]
    ppermute x21 -> x22, waiting for transfers between devices: 18.5 us -> 20.5 us  [move(): return lax.ppermute(value, AXES, pairs(counts, target))]
    pallas_call x15 -> x16, Pallas kernels: 9.91 us -> 9.91 us  [call(): pl.pallas_call(kernel, out_shape=shapes, in_specs=[pl.BlockSpec(memory_sp...]
  transfers between devices with their start and end apart: 21 -> 22, of which waited for: 12 -> 12; matrix products, arithmetic and copies ran while one was open for 0% -> 0% of each run, Pallas kernels for 17% -> 17%
where the time goes in v17:
time: 56.1 us; the launch traced here: 56 us
  starting transfers between devices  23.2 us (41%)
  waiting for transfers between devices  20.5 us (37%)
  Pallas kernels  11.1 us (20%)
  local copies, waits for them, and re-layouts  0.73 us (1%)
    ppermute x22, starting transfers between devices, move(): return lax.ppermute(value, AXES, pairs(counts, target))  23.2 us
    ppermute x22, waiting for transfers between devices, move(): return lax.ppermute(value, AXES, pairs(counts, target))  20.5 us
    pallas_call x16, Pallas kernels, call(): pl.pallas_call(kernel, out_shape=shapes, in_specs=[pl.BlockSpec(memory_sp...  9.91 us
    pallas_call x1, Pallas kernels, place_rows(): pl.pallas_call(place_kernel, out_shape=jax.ShapeDtypeStruct(shape, jnp.bf...  1.24 us
  transfers between devices with their start and end apart: 22, of which 12 were waited for; matrix products, arithmetic and copies ran while one was open for 0% of the time, Pallas kernels for 17%

profile of v17, /device:TPU:1, one launch (start us, length us, event | category | flops | bytes accessed | tf_op | source)
XLA Modules:
  0.0 56.0 jit_solution(10868364207377309687)
XLA Ops:
  0.0 3.2 %collective-permute-start.3 = (bf16[3,1024,256]{2,1,0:T(8,128)(2,1)}, bf16[3,1024,256]{2,1,0:T(8,128)(2,1)S(1)}, u32[]{:S(2)}, u32[]{:S(2)}) collective-permute-start(bf16[3,1024,256]{2,1,0:T(8,128)(2,1)} %bitcast.8), channel_id=1, source_target_pairs={{0,1},{1,0},{2,3},{3,2},{4,5},{5,4},{6,7},{7,6},{8,9},{9,8},{10,11... | collective-permute-start | bytes 4718600 | tf_op jit(solution)/shard_map/ppermute | solution.py:334
  3.2 0.5 collective-permute-start.2
  3.8 0.7 %copy-done.7 = f32[2,4,37]{2,1,0:T(4,128)S(1)} copy-done((f32[2,4,37]{2,1,0:T(4,128)S(1)}, f32[2,4,37]{2,1,0:T(4,128)}, u32[]{:S(2)}) %copy-start.7) | copy-done | bytes 1208
  4.4 0.7 %shard_map.82.bias = bf16[32,256]{1,0:T(8,128)(2,1)S(1)} custom-call(f32[2,4,37]{2,1,0:T(4,128)S(1)} %copy-done.7), custom_call_target="tpu_custom_call" | custom-call | flops 5000000000 | bytes 17568 | tf_op jit(solution)/shard_map/pallas_call | solution.py:314
  5.2 2.1 %shard_map.83 = (bf16[160,256]{1,0:T(8,128)(2,1)S(1)}, bf16[160,256]{1,0:T(8,128)(2,1)S(1)}) custom-call(bf16[72,4,1024]{2,1,0:T(4,128)(2,1)S(1)} %bitcast.11, bf16[3,1024,256]{2,1,0:T(8,128)(2,1)S(1)} %bitcast.10, bf16[32,256]{1,0:T(8,128)(2,1)S(1)} %shard_map.82.bias), custom_call_target="tpu_custom_call" | custom-call | flops 1000000000 | bytes 2342912 | tf_op jit(solution)/shard_map/pallas_call | solution.py:314
  7.6 0.4 collective-permute-done.2.o_sib
  8.0 0.6 %collective-permute-done.1.o1 = bf16[160,256]{1,0:T(8,128)(2,1)S(1)} collective-permute-done((bf16[160,256]{1,0:T(8,128)(2,1)S(1)}, bf16[160,256]{1,0:T(8,128)(2,1)S(1)}, u32[]{:S(2)}, u32[]{:S(2)}) %collective-permute-start.1) | collective-permute-done | bytes 81952 | tf_op jit(solution)/shard_map/ppermute | solution.py:334
  9.1 0.7 %shard_map.85.b_own = bf16[32,256]{1,0:T(8,128)(2,1)S(1)} custom-call(f32[2,4,37]{2,1,0:T(4,128)S(1)} %copy-done.8), custom_call_target="tpu_custom_call" | custom-call | flops 1000000000 | bytes 17568 | tf_op jit(solution)/shard_map/pallas_call | solution.py:314
  10.2 1.7 %collective-permute-start.8 = (bf16[40,1024]{1,0:T(8,128)(2,1)S(1)}, bf16[40,1024]{1,0:T(8,128)(2,1)S(1)}, u32[]{:S(2)}, u32[]{:S(2)}) collective-permute-start(bf16[40,1024]{1,0:T(8,128)(2,1)S(1)} %get-tuple-element.65.mine), channel_id=1, source_target_pairs={{0,2},{1,3},{2,0},{3,1},{4,6},{5,7},{6,4},{7,5},{8,10},{9,11},{10,... | collective-permute-start | bytes 245768 | tf_op jit(solution)/shard_map/ppermute | solution.py:334
  11.9 0.4 shard_map.86
  12.5 0.5 collective-permute-start.12
  13.0 1.6 %collective-permute-done.4.other = bf16[80,1024]{1,0:T(8,128)(2,1)S(1)} collective-permute-done((bf16[80,1024]{1,0:T(8,128)(2,1)S(1)}, bf16[80,1024]{1,0:T(8,128)(2,1)S(1)}, u32[]{:S(2)}, u32[]{:S(2)}) %collective-permute-start.4) | collective-permute-done | bytes 163872 | tf_op jit(solution)/shard_map/ppermute | solution.py:334
  14.7 1.0 %collective-permute-start.6 = (bf16[40,1024]{1,0:T(8,128)(2,1)S(1)}, bf16[40,1024]{1,0:T(8,128)(2,1)S(1)}, u32[]{:S(2)}, u32[]{:S(2)}) collective-permute-start(bf16[40,1024]{1,0:T(8,128)(2,1)S(1)} %get-tuple-element.63), channel_id=1, source_target_pairs={{0,36},{1,37},{2,38},{3,39},{4,40},{5,41},{6,42},{7,43},{8,44},{9,... | collective-permute-start | bytes 245768 | tf_op jit(solution)/shard_map/ppermute | solution.py:334
  15.7 1.3 %collective-permute-start.7 = (bf16[40,1024]{1,0:T(8,128)(2,1)S(1)}, bf16[40,1024]{1,0:T(8,128)(2,1)S(1)}, u32[]{:S(2)}, u32[]{:S(2)}) collective-permute-start(bf16[40,1024]{1,0:T(8,128)(2,1)S(1)} %get-tuple-element.64), channel_id=1, source_target_pairs={{0,4},{1,5},{2,6},{3,7},{4,8},{5,9},{6,10},{7,11},{8,12},{9,13},{1... | collective-permute-start | bytes 245768 | tf_op jit(solution)/shard_map/ppermute | solution.py:334
  17.0 1.7 %collective-permute-start.9 = (bf16[40,1024]{1,0:T(8,128)(2,1)S(1)}, bf16[40,1024]{1,0:T(8,128)(2,1)S(1)}, u32[]{:S(2)}, u32[]{:S(2)}) collective-permute-start(bf16[40,1024]{1,0:T(8,128)(2,1)S(1)} %shard_map.89), channel_id=1, source_target_pairs={{0,32},{1,33},{2,34},{3,35},{4,36},{5,37},{6,38},{7,39},{8,40},{9,... | collective-permute-start | bytes 245768 | tf_op jit(solution)/shard_map/ppermute | solution.py:334
  18.8 6.4 %collective-permute-done.6.p0 = bf16[40,1024]{1,0:T(8,128)(2,1)S(1)} collective-permute-done((bf16[40,1024]{1,0:T(8,128)(2,1)S(1)}, bf16[40,1024]{1,0:T(8,128)(2,1)S(1)}, u32[]{:S(2)}, u32[]{:S(2)}) %collective-permute-start.6) | collective-permute-done | bytes 81952 | tf_op jit(solution)/shard_map/ppermute | solution.py:334
  25.5 1.6 %shard_map.91 = (bf16[80,1024]{1,0:T(8,128)(2,1)S(1)}, bf16[80,1024]{1,0:T(8,128)(2,1)S(1)}) custom-call(bf16[80,1024]{1,0:T(8,128)(2,1)S(1)} %shard_map.88.xn_a, bf16[40,1024]{1,0:T(8,128)(2,1)S(1)} %collective-permute-done.9.p2.p0, bf16[40,1024]{1,0:T(8,128)(2,1)S(1)} %shard_map.90.p3.p1, bf16[3,1024,256]{2,1,0:T(8,128)(2,1)S(1)} %bitcast.9, ...), custom_call_target="tpu_custom_call" | custom-call | flops 1000000000 | bytes 4882432 | tf_op jit(solution)/shard_map/pallas_call | solution.py:314
  27.0 3.5 %collective-permute-start.13 = (bf16[1024,1024]{1,0:T(8,128)(2,1)S(1)}, bf16[1024,1024]{1,0:T(8,128)(2,1)S(1)}, u32[]{:S(2)}, u32[]{:S(2)}) collective-permute-start(bf16[1024,1024]{1,0:T(8,128)(2,1)S(1)} %copy-done.1), channel_id=1, source_target_pairs={{0,1},{1,0},{2,3},{3,2},{4,5},{5,4},{6,7},{7,6},{8,9},{9,8},{10,11... | collective-permute-start | bytes 6291464 | tf_op jit(solution)/shard_map/ppermute | solution.py:334
  30.5 1.5 %collective-permute-start.15 = (bf16[80,1024]{1,0:T(8,128)(2,1)S(1)}, bf16[80,1024]{1,0:T(8,128)(2,1)S(1)}, u32[]{:S(2)}, u32[]{:S(2)}) collective-permute-start(bf16[80,1024]{1,0:T(8,128)(2,1)S(1)} %get-tuple-element.82.mine), channel_id=1, source_target_pairs={{0,2},{1,3},{2,0},{3,1},{4,6},{5,7},{6,4},{7,5},{8,10},{9,11},{10,... | collective-permute-start | bytes 491528 | tf_op jit(solution)/shard_map/ppermute | solution.py:334
  32.0 4.3 %collective-permute-done.11.other = bf16[80,1024]{1,0:T(8,128)(2,1)S(1)} collective-permute-done((bf16[80,1024]{1,0:T(8,128)(2,1)S(1)}, bf16[80,1024]{1,0:T(8,128)(2,1)S(1)}, u32[]{:S(2)}, u32[]{:S(2)}) %collective-permute-start.11) | collective-permute-done | bytes 163872 | tf_op jit(solution)/shard_map/ppermute | solution.py:334
  36.3 1.8 %shard_map.92.mine = bf16[80,1024]{1,0:T(8,128)(2,1)S(1)} custom-call(bf16[80,1024]{1,0:T(8,128)(2,1)S(1)} %get-tuple-element.74.mine, bf16[80,1024]{1,0:T(8,128)(2,1)S(1)} %collective-permute-done.11.other, bf16[40,1024]{1,0:T(8,128)(2,1)S(1)} %collective-permute-done.6.p0, bf16[40,1024]{1,0:T(8,128)(2,1)S(1)} %collective-permute-done.7.p1, ...), custom_call_target="tpu_custom_call" | custom-call | flops 1000000000 | bytes 9043968 | tf_op jit(solution)/shard_map/pallas_call | solution.py:314
  38.2 1.6 %collective-permute-done.15.other = bf16[80,1024]{1,0:T(8,128)(2,1)S(1)} collective-permute-done((bf16[80,1024]{1,0:T(8,128)(2,1)S(1)}, bf16[80,1024]{1,0:T(8,128)(2,1)S(1)}, u32[]{:S(2)}, u32[]{:S(2)}) %collective-permute-start.15) | collective-permute-done | bytes 163872 | tf_op jit(solution)/shard_map/ppermute | solution.py:334
  39.8 1.8 %shard_map.94.mine = bf16[80,1024]{1,0:T(8,128)(2,1)S(1)} custom-call(bf16[80,1024]{1,0:T(8,128)(2,1)S(1)} %get-tuple-element.82.mine, bf16[80,1024]{1,0:T(8,128)(2,1)S(1)} %collective-permute-done.15.other, bf16[40,1024]{1,0:T(8,128)(2,1)S(1)} %collective-permute-done.9.p2.p0, bf16[40,1024]{1,0:T(8,128)(2,1)S(1)} %shard_map.90.p3.p1, ...), custom_call_target="tpu_custom_call" | custom-call | flops 1000000000 | bytes 9043968 | tf_op jit(solution)/shard_map/pallas_call | solution.py:314
  41.7 0.6 %collective-permute-done.14.other = bf16[80,1024]{1,0:T(8,128)(2,1)S(1)} collective-permute-done((bf16[80,1024]{1,0:T(8,128)(2,1)S(1)}, bf16[80,1024]{1,0:T(8,128)(2,1)S(1)}, u32[]{:S(2)}, u32[]{:S(2)}) %collective-permute-start.14) | collective-permute-done | bytes 163872 | tf_op jit(solution)/shard_map/ppermute | solution.py:334
  42.4 2.6 %collective-permute-start.16 = (bf16[40,1024]{1,0:T(8,128)(2,1)S(1)}, bf16[40,1024]{1,0:T(8,128)(2,1)S(1)}, u32[]{:S(2)}, u32[]{:S(2)}) collective-permute-start(bf16[40,1024]{1,0:T(8,128)(2,1)S(1)} %get-tuple-element.83), channel_id=1, source_target_pairs={{0,254},{1,255},{2,252},{3,253},{4,224},{5,225},{6,226},{7,227},{8... | collective-permute-start | bytes 245768 | tf_op jit(solution)/shard_map/ppermute | solution.py:334
  45.0 0.5 collective-permute-start.17
  45.4 1.2 %collective-permute-done.18.other = bf16[80,1024]{1,0:T(8,128)(2,1)S(1)} collective-permute-done((bf16[80,1024]{1,0:T(8,128)(2,1)S(1)}, bf16[80,1024]{1,0:T(8,128)(2,1)S(1)}, u32[]{:S(2)}, u32[]{:S(2)}) %collective-permute-start.18) | collective-permute-done | bytes 163872 | tf_op jit(solution)/shard_map/ppermute | solution.py:334
  46.7 1.5 %collective-permute-start.19 = (bf16[40,1024]{1,0:T(8,128)(2,1)S(1)}, bf16[40,1024]{1,0:T(8,128)(2,1)S(1)}, u32[]{:S(2)}, u32[]{:S(2)}) collective-permute-start(bf16[40,1024]{1,0:T(8,128)(2,1)S(1)} %get-tuple-element.86), channel_id=1, source_target_pairs={{0,224},{1,225},{2,226},{3,227},{4,228},{5,229},{6,230},{7,231},{8... | collective-permute-start | bytes 245768 | tf_op jit(solution)/shard_map/ppermute | solution.py:334
  48.3 2.4 %collective-permute-done.19.p0 = bf16[40,1024]{1,0:T(8,128)(2,1)S(1)} collective-permute-done((bf16[40,1024]{1,0:T(8,128)(2,1)S(1)}, bf16[40,1024]{1,0:T(8,128)(2,1)S(1)}, u32[]{:S(2)}, u32[]{:S(2)}) %collective-permute-start.19) | collective-permute-done | bytes 81952 | tf_op jit(solution)/shard_map/ppermute | solution.py:334
  50.7 2.5 %collective-permute-start.21 = (bf16[80,1024]{1,0:T(8,128)(2,1)S(1)}, bf16[80,1024]{1,0:T(8,128)(2,1)S(1)}, u32[]{:S(2)}, u32[]{:S(2)}) collective-permute-start(bf16[80,1024]{1,0:T(8,128)(2,1)S(1)} %shard_map.97.m1), channel_id=1, source_target_pairs={{0,1},{1,0},{2,3},{3,2},{4,5},{5,4},{6,7},{7,6},{8,9},{9,8},{10,11... | collective-permute-start | bytes 491528 | tf_op jit(solution)/shard_map/ppermute | solution.py:334
  53.3 0.9 %collective-permute-done.21.s1 = bf16[80,1024]{1,0:T(8,128)(2,1)S(1)} collective-permute-done((bf16[80,1024]{1,0:T(8,128)(2,1)S(1)}, bf16[80,1024]{1,0:T(8,128)(2,1)S(1)}, u32[]{:S(2)}, u32[]{:S(2)}) %collective-permute-start.21) | collective-permute-done | bytes 163872 | tf_op jit(solution)/shard_map/ppermute | solution.py:334
  54.6 1.2 %shard_map.98 = bf16[72,4,1024]{2,1,0:T(4,128)(2,1)} custom-call(bf16[80,1024]{1,0:T(8,128)(2,1)S(1)} %shard_map.95.m0, bf16[80,1024]{1,0:T(8,128)(2,1)S(1)} %shard_map.97.m1, bf16[80,1024]{1,0:T(8,128)(2,1)S(1)} %collective-permute-done.20.s0, bf16[80,1024]{1,0:T(8,128)(2,1)S(1)} %collective-permute-done.21.s1), custom_call_target="tpu_custom_call" | custom-call | flops 200000000 | bytes 2000000 | tf_op jit(solution)/shard_map/pallas_call | solution.py:300
  (47 shorter events, 2.6 us)
Async XLA Ops:
  0.0 5.2 %copy-start.5 = (bf16[1024,3,256]{2,0,1:T(8,128)(2,1)S(1)}, bf16[1024,3,256]{2,0,1:T(8,128)(2,1)}, u32[]{:S(2)}) copy-start(bf16[1024,3,256]{2,0,1:T(8,128)(2,1)} %param.9) | copy-start | bytes 4718596
  0.0 5.2 %copy-start.6 = (bf16[4,6,12,1024]{3,0,2,1:T(4,128)(2,1)S(1)}, bf16[4,6,12,1024]{3,0,2,1:T(4,128)(2,1)}, u32[]{:S(2)}) copy-start(bf16[4,6,12,1024]{3,0,2,1:T(4,128)(2,1)} %param.8) | copy-start | bytes 1769476
  0.0 8.6 %collective-permute-start.3 = (bf16[3,1024,256]{2,1,0:T(8,128)(2,1)}, bf16[3,1024,256]{2,1,0:T(8,128)(2,1)S(1)}, u32[]{:S(2)}, u32[]{:S(2)}) collective-permute-start(bf16[3,1024,256]{2,1,0:T(8,128)(2,1)} %bitcast.8), channel_id=1, source_target_pairs={{0,1},{1,0},{2,3},{3,2},{4,5},{5,4},{6,7},{7,6},{8,9},{9,8},{10,11... | collective-permute-start | bytes 4718600 | tf_op jit(solution)/shard_map/ppermute | solution.py:334
  3.2 4.0 %collective-permute-start = (bf16[256,1024]{1,0:T(8,128)(2,1)}, bf16[256,1024]{1,0:T(8,128)(2,1)S(1)}, u32[]{:S(2)}, u32[]{:S(2)}) collective-permute-start(bf16[256,1024]{1,0:T(8,128)(2,1)} %w0.1), channel_id=1, source_target_pairs={{0,1},{1,0},{2,3},{3,2},{4,5},{5,4},{6,7},{7,6},{8,9},{9,8},{10,11... | collective-permute-start | bytes 1572872 | tf_op jit(solution)/shard_map/ppermute | solution.py:334
  3.2 4.7 %collective-permute-start.2 = (bf16[256,1024]{1,0:T(8,128)(2,1)}, bf16[256,1024]{1,0:T(8,128)(2,1)S(1)}, u32[]{:S(2)}, u32[]{:S(2)}) collective-permute-start(bf16[256,1024]{1,0:T(8,128)(2,1)} %o_own.1), channel_id=1, source_target_pairs={{0,1},{1,0},{2,3},{3,2},{4,5},{5,4},{6,7},{7,6},{8,9},{9,8},{10,11... | collective-permute-start | bytes 1572872 | tf_op jit(solution)/shard_map/ppermute | solution.py:334
  3.8 0.7 %copy-start.7 = (f32[2,4,37]{2,1,0:T(4,128)S(1)}, f32[2,4,37]{2,1,0:T(4,128)}, u32[]{:S(2)}) copy-start(f32[2,4,37]{2,1,0:T(4,128)} %table.2) | copy-start | bytes 3556
  5.2 3.5 %copy-start.4 = (bf16[256,1024]{1,0:T(8,128)(2,1)S(1)}, bf16[256,1024]{1,0:T(8,128)(2,1)}, u32[]{:S(2)}) copy-start(bf16[256,1024]{1,0:T(8,128)(2,1)} %w0.1) | copy-start | bytes 1572868
  5.2 3.9 %copy-start.8 = (f32[2,4,37]{2,1,0:T(4,128)S(1)}, f32[2,4,37]{2,1,0:T(4,128)}, u32[]{:S(2)}) copy-start(f32[2,4,37]{2,1,0:T(4,128)} %table.2) | copy-start | bytes 3556
  7.3 1.4 %collective-permute-start.1 = (bf16[160,256]{1,0:T(8,128)(2,1)S(1)}, bf16[160,256]{1,0:T(8,128)(2,1)S(1)}, u32[]{:S(2)}, u32[]{:S(2)}) collective-permute-start(bf16[160,256]{1,0:T(8,128)(2,1)S(1)} %get-tuple-element.52), channel_id=1, source_target_pairs={{0,1},{1,0},{2,3},{3,2},{4,5},{5,4},{6,7},{7,6},{8,9},{9,8},{10,11... | collective-permute-start | bytes 245768 | tf_op jit(solution)/shard_map/ppermute | solution.py:334
  9.0 5.6 %collective-permute-start.4 = (bf16[80,1024]{1,0:T(8,128)(2,1)S(1)}, bf16[80,1024]{1,0:T(8,128)(2,1)S(1)}, u32[]{:S(2)}, u32[]{:S(2)}) collective-permute-start(bf16[80,1024]{1,0:T(8,128)(2,1)S(1)} %get-tuple-element.55.mine), channel_id=1, source_target_pairs={{0,2},{1,3},{2,0},{3,1},{4,6},{5,7},{6,4},{7,5},{8,10},{9,11},{10,... | collective-permute-start | bytes 491528 | tf_op jit(solution)/shard_map/ppermute | solution.py:334
  9.8 2.6 %copy-start = (bf16[1024,1024]{1,0:T(8,128)(2,1)S(1)}, bf16[1024,1024]{1,0:T(8,128)(2,1)}, u32[]{:S(2)}) copy-start(bf16[1024,1024]{1,0:T(8,128)(2,1)} %u0.3) | copy-start | bytes 6291460
  9.8 3.1 %collective-permute-start.5 = (bf16[32,256]{1,0:T(8,128)(2,1)S(1)}, bf16[32,256]{1,0:T(8,128)(2,1)S(1)}, u32[]{:S(2)}, u32[]{:S(2)}) collective-permute-start(bf16[32,256]{1,0:T(8,128)(2,1)S(1)} %shard_map.85.b_own), channel_id=1, source_target_pairs={{0,1},{1,0},{2,3},{3,2},{4,5},{5,4},{6,7},{7,6},{8,9},{9,8},{10,11... | collective-permute-start | bytes 49160 | tf_op jit(solution)/shard_map/ppermute | solution.py:334
  10.2 6.8 %collective-permute-start.8 = (bf16[40,1024]{1,0:T(8,128)(2,1)S(1)}, bf16[40,1024]{1,0:T(8,128)(2,1)S(1)}, u32[]{:S(2)}, u32[]{:S(2)}) collective-permute-start(bf16[40,1024]{1,0:T(8,128)(2,1)S(1)} %get-tuple-element.65.mine), channel_id=1, source_target_pairs={{0,2},{1,3},{2,0},{3,1},{4,6},{5,7},{6,4},{7,5},{8,10},{9,11},{10,... | collective-permute-start | bytes 245768 | tf_op jit(solution)/shard_map/ppermute | solution.py:334
  12.3 6.4 %collective-permute-start.10 = (bf16[40,1024]{1,0:T(8,128)(2,1)S(1)}, bf16[40,1024]{1,0:T(8,128)(2,1)S(1)}, u32[]{:S(2)}, u32[]{:S(2)}) collective-permute-start(bf16[40,1024]{1,0:T(8,128)(2,1)S(1)} %get-tuple-element.69.mine), channel_id=1, source_target_pairs={{0,2},{1,3},{2,0},{3,1},{4,6},{5,7},{6,4},{7,5},{8,10},{9,11},{10,... | collective-permute-start | bytes 245768 | tf_op jit(solution)/shard_map/ppermute | solution.py:334
  12.5 23.8 %collective-permute-start.12 = (bf16[1024,1024]{1,0:T(8,128)(2,1)S(1)}, bf16[1024,1024]{1,0:T(8,128)(2,1)S(1)}, u32[]{:S(2)}, u32[]{:S(2)}) collective-permute-start(bf16[1024,1024]{1,0:T(8,128)(2,1)S(1)} %copy-done), channel_id=1, source_target_pairs={{0,1},{1,0},{2,3},{3,2},{4,5},{5,4},{6,7},{7,6},{8,9},{9,8},{10,11... | collective-permute-start | bytes 6291464 | tf_op jit(solution)/shard_map/ppermute | solution.py:334
  14.7 10.5 %collective-permute-start.6 = (bf16[40,1024]{1,0:T(8,128)(2,1)S(1)}, bf16[40,1024]{1,0:T(8,128)(2,1)S(1)}, u32[]{:S(2)}, u32[]{:S(2)}) collective-permute-start(bf16[40,1024]{1,0:T(8,128)(2,1)S(1)} %get-tuple-element.63), channel_id=1, source_target_pairs={{0,36},{1,37},{2,38},{3,39},{4,40},{5,41},{6,42},{7,43},{8,44},{9,... | collective-permute-start | bytes 245768 | tf_op jit(solution)/shard_map/ppermute | solution.py:334
  15.7 9.5 %collective-permute-start.7 = (bf16[40,1024]{1,0:T(8,128)(2,1)S(1)}, bf16[40,1024]{1,0:T(8,128)(2,1)S(1)}, u32[]{:S(2)}, u32[]{:S(2)}) collective-permute-start(bf16[40,1024]{1,0:T(8,128)(2,1)S(1)} %get-tuple-element.64), channel_id=1, source_target_pairs={{0,4},{1,5},{2,6},{3,7},{4,8},{5,9},{6,10},{7,11},{8,12},{9,13},{1... | collective-permute-start | bytes 245768 | tf_op jit(solution)/shard_map/ppermute | solution.py:334
  17.0 8.4 %collective-permute-start.9 = (bf16[40,1024]{1,0:T(8,128)(2,1)S(1)}, bf16[40,1024]{1,0:T(8,128)(2,1)S(1)}, u32[]{:S(2)}, u32[]{:S(2)}) collective-permute-start(bf16[40,1024]{1,0:T(8,128)(2,1)S(1)} %shard_map.89), channel_id=1, source_target_pairs={{0,32},{1,33},{2,34},{3,35},{4,36},{5,37},{6,38},{7,39},{8,40},{9,... | collective-permute-start | bytes 245768 | tf_op jit(solution)/shard_map/ppermute | solution.py:334
  18.8 6.6 %copy-start.2 = (bf16[1024,3,256]{2,0,1:T(8,128)(2,1)S(1)}, bf16[1024,3,256]{2,0,1:T(8,128)(2,1)}, u32[]{:S(2)}) copy-start(bf16[1024,3,256]{2,0,1:T(8,128)(2,1)} %param.10) | copy-start | bytes 4718596
  18.8 6.6 %copy-start.3 = (bf16[256,1024]{1,0:T(8,128)(2,1)S(1)}, bf16[256,1024]{1,0:T(8,128)(2,1)}, u32[]{:S(2)}) copy-start(bf16[256,1024]{1,0:T(8,128)(2,1)} %o_own.1) | copy-start | bytes 1572868
  25.4 1.6 %copy-start.1 = (bf16[1024,1024]{1,0:T(8,128)(2,1)S(1)}, bf16[1024,1024]{1,0:T(8,128)(2,1)}, u32[]{:S(2)}) copy-start(bf16[1024,1024]{1,0:T(8,128)(2,1)} %d0.3) | copy-start | bytes 6291460
  27.0 9.2 %collective-permute-start.13 = (bf16[1024,1024]{1,0:T(8,128)(2,1)S(1)}, bf16[1024,1024]{1,0:T(8,128)(2,1)S(1)}, u32[]{:S(2)}, u32[]{:S(2)}) collective-permute-start(bf16[1024,1024]{1,0:T(8,128)(2,1)S(1)} %copy-done.1), channel_id=1, source_target_pairs={{0,1},{1,0},{2,3},{3,2},{4,5},{5,4},{6,7},{7,6},{8,9},{9,8},{10,11... | collective-permute-start | bytes 6291464 | tf_op jit(solution)/shard_map/ppermute | solution.py:334
  30.5 5.8 %collective-permute-start.11 = (bf16[80,1024]{1,0:T(8,128)(2,1)S(1)}, bf16[80,1024]{1,0:T(8,128)(2,1)S(1)}, u32[]{:S(2)}, u32[]{:S(2)}) collective-permute-start(bf16[80,1024]{1,0:T(8,128)(2,1)S(1)} %get-tuple-element.74.mine), channel_id=1, source_target_pairs={{0,2},{1,3},{2,0},{3,1},{4,6},{5,7},{6,4},{7,5},{8,10},{9,11},{10,... | collective-permute-start | bytes 491528 | tf_op jit(solution)/shard_map/ppermute | solution.py:334
  30.5 9.3 %collective-permute-start.15 = (bf16[80,1024]{1,0:T(8,128)(2,1)S(1)}, bf16[80,1024]{1,0:T(8,128)(2,1)S(1)}, u32[]{:S(2)}, u32[]{:S(2)}) collective-permute-start(bf16[80,1024]{1,0:T(8,128)(2,1)S(1)} %get-tuple-element.82.mine), channel_id=1, source_target_pairs={{0,2},{1,3},{2,0},{3,1},{4,6},{5,7},{6,4},{7,5},{8,10},{9,11},{10,... | collective-permute-start | bytes 491528 | tf_op jit(solution)/shard_map/ppermute | solution.py:334
  38.1 4.3 %collective-permute-start.14 = (bf16[80,1024]{1,0:T(8,128)(2,1)S(1)}, bf16[80,1024]{1,0:T(8,128)(2,1)S(1)}, u32[]{:S(2)}, u32[]{:S(2)}) collective-permute-start(bf16[80,1024]{1,0:T(8,128)(2,1)S(1)} %shard_map.92.mine), channel_id=1, source_target_pairs={{0,2},{1,3},{2,0},{3,1},{4,6},{5,7},{6,4},{7,5},{8,10},{9,11},{10,... | collective-permute-start | bytes 491528 | tf_op jit(solution)/shard_map/ppermute | solution.py:334
  41.6 5.0 %collective-permute-start.18 = (bf16[80,1024]{1,0:T(8,128)(2,1)S(1)}, bf16[80,1024]{1,0:T(8,128)(2,1)S(1)}, u32[]{:S(2)}, u32[]{:S(2)}) collective-permute-start(bf16[80,1024]{1,0:T(8,128)(2,1)S(1)} %shard_map.94.mine), channel_id=1, source_target_pairs={{0,2},{1,3},{2,0},{3,1},{4,6},{5,7},{6,4},{7,5},{8,10},{9,11},{10,... | collective-permute-start | bytes 491528 | tf_op jit(solution)/shard_map/ppermute | solution.py:334
  42.4 5.8 %collective-permute-start.16 = (bf16[40,1024]{1,0:T(8,128)(2,1)S(1)}, bf16[40,1024]{1,0:T(8,128)(2,1)S(1)}, u32[]{:S(2)}, u32[]{:S(2)}) collective-permute-start(bf16[40,1024]{1,0:T(8,128)(2,1)S(1)} %get-tuple-element.83), channel_id=1, source_target_pairs={{0,254},{1,255},{2,252},{3,253},{4,224},{5,225},{6,226},{7,227},{8... | collective-permute-start | bytes 245768 | tf_op jit(solution)/shard_map/ppermute | solution.py:334
  45.0 3.3 %collective-permute-start.17 = (bf16[40,1024]{1,0:T(8,128)(2,1)S(1)}, bf16[40,1024]{1,0:T(8,128)(2,1)S(1)}, u32[]{:S(2)}, u32[]{:S(2)}) collective-permute-start(bf16[40,1024]{1,0:T(8,128)(2,1)S(1)} %get-tuple-element.84), channel_id=1, source_target_pairs={{0,30},{1,31},{2,28},{3,29},{4,0},{5,1},{6,2},{7,3},{8,4},{9,5},{1... | collective-permute-start | bytes 245768 | tf_op jit(solution)/shard_map/ppermute | solution.py:334
  46.7 4.0 %collective-permute-start.19 = (bf16[40,1024]{1,0:T(8,128)(2,1)S(1)}, bf16[40,1024]{1,0:T(8,128)(2,1)S(1)}, u32[]{:S(2)}, u32[]{:S(2)}) collective-permute-start(bf16[40,1024]{1,0:T(8,128)(2,1)S(1)} %get-tuple-element.86), channel_id=1, source_target_pairs={{0,224},{1,225},{2,226},{3,227},{4,228},{5,229},{6,230},{7,231},{8... | collective-permute-start | bytes 245768 | tf_op jit(solution)/shard_map/ppermute | solution.py:334
  50.7 3.5 %collective-permute-start.21 = (bf16[80,1024]{1,0:T(8,128)(2,1)S(1)}, bf16[80,1024]{1,0:T(8,128)(2,1)S(1)}, u32[]{:S(2)}, u32[]{:S(2)}) collective-permute-start(bf16[80,1024]{1,0:T(8,128)(2,1)S(1)} %shard_map.97.m1), channel_id=1, source_target_pairs={{0,1},{1,0},{2,3},{3,2},{4,5},{5,4},{6,7},{7,6},{8,9},{9,8},{10,11... | collective-permute-start | bytes 491528 | tf_op jit(solution)/shard_map/ppermute | solution.py:334
  53.2 1.4 %collective-permute-start.20 = (bf16[80,1024]{1,0:T(8,128)(2,1)S(1)}, bf16[80,1024]{1,0:T(8,128)(2,1)S(1)}, u32[]{:S(2)}, u32[]{:S(2)}) collective-permute-start(bf16[80,1024]{1,0:T(8,128)(2,1)S(1)} %shard_map.95.m0), channel_id=1, source_target_pairs={{0,1},{1,0},{2,3},{3,2},{4,5},{5,4},{6,7},{7,6},{8,9},{9,8},{10,11... | collective-permute-start | bytes 491528 | tf_op jit(solution)/shard_map/ppermute | solution.py:334

commit v18 on v17

--- a/solution.py
+++ b/solution.py
@@ -362,13 +362,14 @@
     base_a, base_lat, base_own = call(base_kernel, half + piece * 2, (tok,), 10**9, 8)
     bias2 = call(functools.partial(bias_kernel, 1), features, (rel_tables,), 10**9, 4, table=True)
     bias2_sib = core_swap(bias2)
-    given, up_late, s1, w_sib = tied(core_swap(give), up_weight, s1, w_sib)
+    given, up_late, s1, w_sib, down_late = tied(core_swap(give), up_weight, s1, w_sib, down_weight)
+    d1 = core_swap(down_late)
     u1 = core_swap(up_late)
     part_a, part_lat, part_own = call(partial_kernel, half + piece * 2, (keep, given, out_first, f1), 2 * 10**8, 8)
     other_a = chip_swap(part_a)
     other_lat = chip_swap(part_lat)
     other_own = chip_swap(part_own)
-    other_a, bias2_sib = tied(other_a, bias2_sib)
+    other_a, bias2_sib, d1 = tied(other_a, bias2_sib, d1)
     diag, lon = call(residual_kernel, piece * 2, (part_a, other_a, base_a), 10**6, 8)
     diag, lon, part_lat = tied(diag, lon, part_lat)
     lat = call(residual_kernel, piece, (part_lat, other_lat, base_lat), 10**10, 8)
@@ -386,10 +387,8 @@
         10**9,
         16,
     )
-    part_b, down_late = tied(part_b, down_weight)
     other_a = chip_swap(part_a)
     other_b = chip_swap(part_b)
-    d1 = core_swap(down_late)
     mlp = (up_weight, u1, down_weight, d1)
     part_a = call(mlp_kernel, half, (part_a, other_a, diag, lon, *mlp), 10**9, 20)
     part_a, part_b = tied(part_a, part_b)

time: 56.1 us -> 55.3 us (0.986)
  waiting for transfers between devices: 20.5 us -> 17.6 us
  starting transfers between devices: 23.2 us -> 25.3 us
    ppermute x22, waiting for transfers between devices: 20.5 us -> 17.6 us  [move(): return lax.ppermute(value, AXES, pairs(counts, target))]
    ppermute x22, starting transfers between devices: 23.2 us -> 25.3 us  [move(): return lax.ppermute(value, AXES, pairs(counts, target))]
  transfers between devices with their start and end apart: 22 -> 22, of which waited for: 12 -> 12; matrix products, arithmetic and copies ran while one was open for 0% -> 0% of each run, Pallas kernels for 17% -> 18%
where the time goes in v18:
time: 55.3 us; the launch traced here: 55.2 us
  starting transfers between devices  25.3 us (46%)
  waiting for transfers between devices  17.6 us (32%)
  Pallas kernels  11.2 us (20%)
  local copies, waits for them, and re-layouts  0.73 us (1%)
    ppermute x22, starting transfers between devices, move(): return lax.ppermute(value, AXES, pairs(counts, target))  25.3 us
    ppermute x22, waiting for transfers between devices, move(): return lax.ppermute(value, AXES, pairs(counts, target))  17.6 us
    pallas_call x16, Pallas kernels, call(): pl.pallas_call(kernel, out_shape=shapes, in_specs=[pl.BlockSpec(memory_sp...  9.91 us
    pallas_call x1, Pallas kernels, place_rows(): pl.pallas_call(place_kernel, out_shape=jax.ShapeDtypeStruct(shape, jnp.bf...  1.25 us
  transfers between devices with their start and end apart: 22, of which 12 were waited for; matrix products, arithmetic and copies ran while one was open for 0% of the time, Pallas kernels for 18%

profile of v18, /device:TPU:1, one launch (start us, length us, event | category | flops | bytes accessed | tf_op | source)
XLA Modules:
  0.0 55.2 jit_solution(9437503709053946067)
XLA Ops:
  0.0 3.2 %collective-permute-start.3 = (bf16[3,1024,256]{2,1,0:T(8,128)(2,1)}, bf16[3,1024,256]{2,1,0:T(8,128)(2,1)S(1)}, u32[]{:S(2)}, u32[]{:S(2)}) collective-permute-start(bf16[3,1024,256]{2,1,0:T(8,128)(2,1)} %bitcast.8), channel_id=1, source_target_pairs={{0,1},{1,0},{2,3},{3,2},{4,5},{5,4},{6,7},{7,6},{8,9},{9,8},{10,11... | collective-permute-start | bytes 4718600 | tf_op jit(solution)/shard_map/ppermute | solution.py:334
  3.2 0.5 collective-permute-start.2
  3.8 0.7 %copy-done.7 = f32[2,4,37]{2,1,0:T(4,128)S(1)} copy-done((f32[2,4,37]{2,1,0:T(4,128)S(1)}, f32[2,4,37]{2,1,0:T(4,128)}, u32[]{:S(2)}) %copy-start.7) | copy-done | bytes 1208
  4.4 0.7 %shard_map.82.bias = bf16[32,256]{1,0:T(8,128)(2,1)S(1)} custom-call(f32[2,4,37]{2,1,0:T(4,128)S(1)} %copy-done.7), custom_call_target="tpu_custom_call" | custom-call | flops 5000000000 | bytes 17568 | tf_op jit(solution)/shard_map/pallas_call | solution.py:314
  5.2 2.1 %shard_map.83 = (bf16[160,256]{1,0:T(8,128)(2,1)S(1)}, bf16[160,256]{1,0:T(8,128)(2,1)S(1)}) custom-call(bf16[72,4,1024]{2,1,0:T(4,128)(2,1)S(1)} %bitcast.11, bf16[3,1024,256]{2,1,0:T(8,128)(2,1)S(1)} %bitcast.10, bf16[32,256]{1,0:T(8,128)(2,1)S(1)} %shard_map.82.bias), custom_call_target="tpu_custom_call" | custom-call | flops 1000000000 | bytes 2342912 | tf_op jit(solution)/shard_map/pallas_call | solution.py:314
  7.6 0.4 collective-permute-done.2.o_sib
  8.0 0.7 %collective-permute-done.1.o1 = bf16[160,256]{1,0:T(8,128)(2,1)S(1)} collective-permute-done((bf16[160,256]{1,0:T(8,128)(2,1)S(1)}, bf16[160,256]{1,0:T(8,128)(2,1)S(1)}, u32[]{:S(2)}, u32[]{:S(2)}) %collective-permute-start.1) | collective-permute-done | bytes 81952 | tf_op jit(solution)/shard_map/ppermute | solution.py:334
  9.4 0.7 %shard_map.85.b_own = bf16[32,256]{1,0:T(8,128)(2,1)S(1)} custom-call(f32[2,4,37]{2,1,0:T(4,128)S(1)} %copy-done.8), custom_call_target="tpu_custom_call" | custom-call | flops 1000000000 | bytes 17568 | tf_op jit(solution)/shard_map/pallas_call | solution.py:314
  10.1 0.3 collective-permute-start.5
  10.4 1.7 %collective-permute-start.9 = (bf16[40,1024]{1,0:T(8,128)(2,1)S(1)}, bf16[40,1024]{1,0:T(8,128)(2,1)S(1)}, u32[]{:S(2)}, u32[]{:S(2)}) collective-permute-start(bf16[40,1024]{1,0:T(8,128)(2,1)S(1)} %get-tuple-element.66.mine), channel_id=1, source_target_pairs={{0,2},{1,3},{2,0},{3,1},{4,6},{5,7},{6,4},{7,5},{8,10},{9,11},{10,... | collective-permute-start | bytes 245768 | tf_op jit(solution)/shard_map/ppermute | solution.py:334
  12.2 0.4 shard_map.86
  12.8 0.4 collective-permute-start.13
  13.2 1.6 %collective-permute-done.4.other = bf16[80,1024]{1,0:T(8,128)(2,1)S(1)} collective-permute-done((bf16[80,1024]{1,0:T(8,128)(2,1)S(1)}, bf16[80,1024]{1,0:T(8,128)(2,1)S(1)}, u32[]{:S(2)}, u32[]{:S(2)}) %collective-permute-start.4) | collective-permute-done | bytes 163872 | tf_op jit(solution)/shard_map/ppermute | solution.py:334
  15.0 1.0 %collective-permute-start.7 = (bf16[40,1024]{1,0:T(8,128)(2,1)S(1)}, bf16[40,1024]{1,0:T(8,128)(2,1)S(1)}, u32[]{:S(2)}, u32[]{:S(2)}) collective-permute-start(bf16[40,1024]{1,0:T(8,128)(2,1)S(1)} %get-tuple-element.64), channel_id=1, source_target_pairs={{0,36},{1,37},{2,38},{3,39},{4,40},{5,41},{6,42},{7,43},{8,44},{9,... | collective-permute-start | bytes 245768 | tf_op jit(solution)/shard_map/ppermute | solution.py:334
  16.0 1.3 %collective-permute-start.8 = (bf16[40,1024]{1,0:T(8,128)(2,1)S(1)}, bf16[40,1024]{1,0:T(8,128)(2,1)S(1)}, u32[]{:S(2)}, u32[]{:S(2)}) collective-permute-start(bf16[40,1024]{1,0:T(8,128)(2,1)S(1)} %get-tuple-element.65), channel_id=1, source_target_pairs={{0,4},{1,5},{2,6},{3,7},{4,8},{5,9},{6,10},{7,11},{8,12},{9,13},{1... | collective-permute-start | bytes 245768 | tf_op jit(solution)/shard_map/ppermute | solution.py:334
  17.3 1.9 %collective-permute-start.10 = (bf16[40,1024]{1,0:T(8,128)(2,1)S(1)}, bf16[40,1024]{1,0:T(8,128)(2,1)S(1)}, u32[]{:S(2)}, u32[]{:S(2)}) collective-permute-start(bf16[40,1024]{1,0:T(8,128)(2,1)S(1)} %shard_map.89), channel_id=1, source_target_pairs={{0,32},{1,33},{2,34},{3,35},{4,36},{5,37},{6,38},{7,39},{8,40},{9,... | collective-permute-start | bytes 245768 | tf_op jit(solution)/shard_map/ppermute | solution.py:334
  19.3 6.2 %collective-permute-done.7.p0 = bf16[40,1024]{1,0:T(8,128)(2,1)S(1)} collective-permute-done((bf16[40,1024]{1,0:T(8,128)(2,1)S(1)}, bf16[40,1024]{1,0:T(8,128)(2,1)S(1)}, u32[]{:S(2)}, u32[]{:S(2)}) %collective-permute-start.7) | collective-permute-done | bytes 81952 | tf_op jit(solution)/shard_map/ppermute | solution.py:334
  25.7 1.6 %shard_map.91 = (bf16[80,1024]{1,0:T(8,128)(2,1)S(1)}, bf16[80,1024]{1,0:T(8,128)(2,1)S(1)}) custom-call(bf16[80,1024]{1,0:T(8,128)(2,1)S(1)} %shard_map.88.xn_a, bf16[40,1024]{1,0:T(8,128)(2,1)S(1)} %collective-permute-done.10.p2.p0, bf16[40,1024]{1,0:T(8,128)(2,1)S(1)} %shard_map.90.p3.p1, bf16[3,1024,256]{2,1,0:T(8,128)(2,1)S(1)} %bitcast.9, ...), custom_call_target="tpu_custom_call" | custom-call | flops 1000000000 | bytes 4882432 | tf_op jit(solution)/shard_map/pallas_call | solution.py:314
  27.4 1.5 %collective-permute-start.15 = (bf16[80,1024]{1,0:T(8,128)(2,1)S(1)}, bf16[80,1024]{1,0:T(8,128)(2,1)S(1)}, u32[]{:S(2)}, u32[]{:S(2)}) collective-permute-start(bf16[80,1024]{1,0:T(8,128)(2,1)S(1)} %get-tuple-element.82.mine), channel_id=1, source_target_pairs={{0,2},{1,3},{2,0},{3,1},{4,6},{5,7},{6,4},{7,5},{8,10},{9,11},{10,... | collective-permute-start | bytes 491528 | tf_op jit(solution)/shard_map/ppermute | solution.py:334
  28.8 2.7 %collective-permute-done.12.other = bf16[80,1024]{1,0:T(8,128)(2,1)S(1)} collective-permute-done((bf16[80,1024]{1,0:T(8,128)(2,1)S(1)}, bf16[80,1024]{1,0:T(8,128)(2,1)S(1)}, u32[]{:S(2)}, u32[]{:S(2)}) %collective-permute-start.12) | collective-permute-done | bytes 163872 | tf_op jit(solution)/shard_map/ppermute | solution.py:334
  31.5 1.8 %shard_map.92.mine = bf16[80,1024]{1,0:T(8,128)(2,1)S(1)} custom-call(bf16[80,1024]{1,0:T(8,128)(2,1)S(1)} %get-tuple-element.75.mine, bf16[80,1024]{1,0:T(8,128)(2,1)S(1)} %collective-permute-done.12.other, bf16[40,1024]{1,0:T(8,128)(2,1)S(1)} %collective-permute-done.7.p0, bf16[40,1024]{1,0:T(8,128)(2,1)S(1)} %collective-permute-done.8.p1, ...), custom_call_target="tpu_custom_call" | custom-call | flops 1000000000 | bytes 9043968 | tf_op jit(solution)/shard_map/pallas_call | solution.py:314
  33.5 1.8 %shard_map.94.mine = bf16[80,1024]{1,0:T(8,128)(2,1)S(1)} custom-call(bf16[80,1024]{1,0:T(8,128)(2,1)S(1)} %get-tuple-element.82.mine, bf16[80,1024]{1,0:T(8,128)(2,1)S(1)} %collective-permute-done.15.other, bf16[40,1024]{1,0:T(8,128)(2,1)S(1)} %collective-permute-done.10.p2.p0, bf16[40,1024]{1,0:T(8,128)(2,1)S(1)} %shard_map.90.p3.p1, ...), custom_call_target="tpu_custom_call" | custom-call | flops 1000000000 | bytes 9043968 | tf_op jit(solution)/shard_map/pallas_call | solution.py:314
  35.3 1.5 %collective-permute-start.18 = (bf16[80,1024]{1,0:T(8,128)(2,1)S(1)}, bf16[80,1024]{1,0:T(8,128)(2,1)S(1)}, u32[]{:S(2)}, u32[]{:S(2)}) collective-permute-start(bf16[80,1024]{1,0:T(8,128)(2,1)S(1)} %shard_map.94.mine), channel_id=1, source_target_pairs={{0,2},{1,3},{2,0},{3,1},{4,6},{5,7},{6,4},{7,5},{8,10},{9,11},{10,... | collective-permute-start | bytes 491528 | tf_op jit(solution)/shard_map/ppermute | solution.py:334
  36.8 2.1 %collective-permute-done.14.other = bf16[80,1024]{1,0:T(8,128)(2,1)S(1)} collective-permute-done((bf16[80,1024]{1,0:T(8,128)(2,1)S(1)}, bf16[80,1024]{1,0:T(8,128)(2,1)S(1)}, u32[]{:S(2)}, u32[]{:S(2)}) %collective-permute-start.14) | collective-permute-done | bytes 163872 | tf_op jit(solution)/shard_map/ppermute | solution.py:334
  38.9 3.8 %collective-permute-start.16 = (bf16[40,1024]{1,0:T(8,128)(2,1)S(1)}, bf16[40,1024]{1,0:T(8,128)(2,1)S(1)}, u32[]{:S(2)}, u32[]{:S(2)}) collective-permute-start(bf16[40,1024]{1,0:T(8,128)(2,1)S(1)} %get-tuple-element.83), channel_id=1, source_target_pairs={{0,254},{1,255},{2,252},{3,253},{4,224},{5,225},{6,226},{7,227},{8... | collective-permute-start | bytes 245768 | tf_op jit(solution)/shard_map/ppermute | solution.py:334
  42.8 0.8 %collective-permute-start.19 = (bf16[40,1024]{1,0:T(8,128)(2,1)S(1)}, bf16[40,1024]{1,0:T(8,128)(2,1)S(1)}, u32[]{:S(2)}, u32[]{:S(2)}) collective-permute-start(bf16[40,1024]{1,0:T(8,128)(2,1)S(1)} %get-tuple-element.86), channel_id=1, source_target_pairs={{0,224},{1,225},{2,226},{3,227},{4,228},{5,229},{6,230},{7,231},{8... | collective-permute-start | bytes 245768 | tf_op jit(solution)/shard_map/ppermute | solution.py:334
  43.6 0.6 %collective-permute-done.16.p0 = bf16[40,1024]{1,0:T(8,128)(2,1)S(1)} collective-permute-done((bf16[40,1024]{1,0:T(8,128)(2,1)S(1)}, bf16[40,1024]{1,0:T(8,128)(2,1)S(1)}, u32[]{:S(2)}, u32[]{:S(2)}) %collective-permute-start.16) | collective-permute-done | bytes 81952 | tf_op jit(solution)/shard_map/ppermute | solution.py:334
  44.2 1.8 %collective-permute-done.17.p1 = bf16[40,1024]{1,0:T(8,128)(2,1)S(1)} collective-permute-done((bf16[40,1024]{1,0:T(8,128)(2,1)S(1)}, bf16[40,1024]{1,0:T(8,128)(2,1)S(1)}, u32[]{:S(2)}, u32[]{:S(2)}) %collective-permute-start.17) | collective-permute-done | bytes 81952 | tf_op jit(solution)/shard_map/ppermute | solution.py:334
  46.2 6.2 %collective-permute-start.21 = (bf16[80,1024]{1,0:T(8,128)(2,1)S(1)}, bf16[80,1024]{1,0:T(8,128)(2,1)S(1)}, u32[]{:S(2)}, u32[]{:S(2)}) collective-permute-start(bf16[80,1024]{1,0:T(8,128)(2,1)S(1)} %shard_map.97.m1), channel_id=1, source_target_pairs={{0,1},{1,0},{2,3},{3,2},{4,5},{5,4},{6,7},{7,6},{8,9},{9,8},{10,11... | collective-permute-start | bytes 491528 | tf_op jit(solution)/shard_map/ppermute | solution.py:334
  52.5 0.9 %collective-permute-done.21.s1 = bf16[80,1024]{1,0:T(8,128)(2,1)S(1)} collective-permute-done((bf16[80,1024]{1,0:T(8,128)(2,1)S(1)}, bf16[80,1024]{1,0:T(8,128)(2,1)S(1)}, u32[]{:S(2)}, u32[]{:S(2)}) %collective-permute-start.21) | collective-permute-done | bytes 163872 | tf_op jit(solution)/shard_map/ppermute | solution.py:334
  53.4 0.4 collective-permute-done.20.s0
  53.8 1.3 %shard_map.98 = bf16[72,4,1024]{2,1,0:T(4,128)(2,1)} custom-call(bf16[80,1024]{1,0:T(8,128)(2,1)S(1)} %shard_map.95.m0, bf16[80,1024]{1,0:T(8,128)(2,1)S(1)} %shard_map.97.m1, bf16[80,1024]{1,0:T(8,128)(2,1)S(1)} %collective-permute-done.20.s0, bf16[80,1024]{1,0:T(8,128)(2,1)S(1)} %collective-permute-done.21.s1), custom_call_target="tpu_custom_call" | custom-call | flops 200000000 | bytes 2000000 | tf_op jit(solution)/shard_map/pallas_call | solution.py:300
  (47 shorter events, 2.2 us)
Async XLA Ops:
  0.0 5.2 %copy-start.5 = (bf16[1024,3,256]{2,0,1:T(8,128)(2,1)S(1)}, bf16[1024,3,256]{2,0,1:T(8,128)(2,1)}, u32[]{:S(2)}) copy-start(bf16[1024,3,256]{2,0,1:T(8,128)(2,1)} %param.9) | copy-start | bytes 4718596
  0.0 5.2 %copy-start.6 = (bf16[4,6,12,1024]{3,0,2,1:T(4,128)(2,1)S(1)}, bf16[4,6,12,1024]{3,0,2,1:T(4,128)(2,1)}, u32[]{:S(2)}) copy-start(bf16[4,6,12,1024]{3,0,2,1:T(4,128)(2,1)} %param.8) | copy-start | bytes 1769476
  0.0 8.6 %collective-permute-start.3 = (bf16[3,1024,256]{2,1,0:T(8,128)(2,1)}, bf16[3,1024,256]{2,1,0:T(8,128)(2,1)S(1)}, u32[]{:S(2)}, u32[]{:S(2)}) collective-permute-start(bf16[3,1024,256]{2,1,0:T(8,128)(2,1)} %bitcast.8), channel_id=1, source_target_pairs={{0,1},{1,0},{2,3},{3,2},{4,5},{5,4},{6,7},{7,6},{8,9},{9,8},{10,11... | collective-permute-start | bytes 4718600 | tf_op jit(solution)/shard_map/ppermute | solution.py:334
  3.2 4.0 %collective-permute-start = (bf16[256,1024]{1,0:T(8,128)(2,1)}, bf16[256,1024]{1,0:T(8,128)(2,1)S(1)}, u32[]{:S(2)}, u32[]{:S(2)}) collective-permute-start(bf16[256,1024]{1,0:T(8,128)(2,1)} %w0.1), channel_id=1, source_target_pairs={{0,1},{1,0},{2,3},{3,2},{4,5},{5,4},{6,7},{7,6},{8,9},{9,8},{10,11... | collective-permute-start | bytes 1572872 | tf_op jit(solution)/shard_map/ppermute | solution.py:334
  3.2 4.7 %collective-permute-start.2 = (bf16[256,1024]{1,0:T(8,128)(2,1)}, bf16[256,1024]{1,0:T(8,128)(2,1)S(1)}, u32[]{:S(2)}, u32[]{:S(2)}) collective-permute-start(bf16[256,1024]{1,0:T(8,128)(2,1)} %o_own.1), channel_id=1, source_target_pairs={{0,1},{1,0},{2,3},{3,2},{4,5},{5,4},{6,7},{7,6},{8,9},{9,8},{10,11... | collective-permute-start | bytes 1572872 | tf_op jit(solution)/shard_map/ppermute | solution.py:334
  3.8 0.7 %copy-start.7 = (f32[2,4,37]{2,1,0:T(4,128)S(1)}, f32[2,4,37]{2,1,0:T(4,128)}, u32[]{:S(2)}) copy-start(f32[2,4,37]{2,1,0:T(4,128)} %table.2) | copy-start | bytes 3556
  5.2 3.5 %copy-start.1 = (bf16[1024,1024]{1,0:T(8,128)(2,1)S(1)}, bf16[1024,1024]{1,0:T(8,128)(2,1)}, u32[]{:S(2)}) copy-start(bf16[1024,1024]{1,0:T(8,128)(2,1)} %d0.3) | copy-start | bytes 6291460
  5.2 3.7 %copy-start.4 = (bf16[256,1024]{1,0:T(8,128)(2,1)S(1)}, bf16[256,1024]{1,0:T(8,128)(2,1)}, u32[]{:S(2)}) copy-start(bf16[256,1024]{1,0:T(8,128)(2,1)} %w0.1) | copy-start | bytes 1572868
  5.2 4.1 %copy-start.8 = (f32[2,4,37]{2,1,0:T(4,128)S(1)}, f32[2,4,37]{2,1,0:T(4,128)}, u32[]{:S(2)}) copy-start(f32[2,4,37]{2,1,0:T(4,128)} %table.2) | copy-start | bytes 3556
  7.3 1.4 %collective-permute-start.1 = (bf16[160,256]{1,0:T(8,128)(2,1)S(1)}, bf16[160,256]{1,0:T(8,128)(2,1)S(1)}, u32[]{:S(2)}, u32[]{:S(2)}) collective-permute-start(bf16[160,256]{1,0:T(8,128)(2,1)S(1)} %get-tuple-element.52), channel_id=1, source_target_pairs={{0,1},{1,0},{2,3},{3,2},{4,5},{5,4},{6,7},{7,6},{8,9},{9,8},{10,11... | collective-permute-start | bytes 245768 | tf_op jit(solution)/shard_map/ppermute | solution.py:334
  8.7 6.2 %collective-permute-start.6 = (bf16[1024,1024]{1,0:T(8,128)(2,1)S(1)}, bf16[1024,1024]{1,0:T(8,128)(2,1)S(1)}, u32[]{:S(2)}, u32[]{:S(2)}) collective-permute-start(bf16[1024,1024]{1,0:T(8,128)(2,1)S(1)} %copy-done.1), channel_id=1, source_target_pairs={{0,1},{1,0},{2,3},{3,2},{4,5},{5,4},{6,7},{7,6},{8,9},{9,8},{10,11... | collective-permute-start | bytes 6291464 | tf_op jit(solution)/shard_map/ppermute | solution.py:334
  9.3 5.6 %collective-permute-start.4 = (bf16[80,1024]{1,0:T(8,128)(2,1)S(1)}, bf16[80,1024]{1,0:T(8,128)(2,1)S(1)}, u32[]{:S(2)}, u32[]{:S(2)}) collective-permute-start(bf16[80,1024]{1,0:T(8,128)(2,1)S(1)} %get-tuple-element.55.mine), channel_id=1, source_target_pairs={{0,2},{1,3},{2,0},{3,1},{4,6},{5,7},{6,4},{7,5},{8,10},{9,11},{10,... | collective-permute-start | bytes 491528 | tf_op jit(solution)/shard_map/ppermute | solution.py:334
  10.1 2.8 %copy-start = (bf16[1024,1024]{1,0:T(8,128)(2,1)S(1)}, bf16[1024,1024]{1,0:T(8,128)(2,1)}, u32[]{:S(2)}) copy-start(bf16[1024,1024]{1,0:T(8,128)(2,1)} %u0.3) | copy-start | bytes 6291460
  10.1 2.7 %collective-permute-start.5 = (bf16[32,256]{1,0:T(8,128)(2,1)S(1)}, bf16[32,256]{1,0:T(8,128)(2,1)S(1)}, u32[]{:S(2)}, u32[]{:S(2)}) collective-permute-start(bf16[32,256]{1,0:T(8,128)(2,1)S(1)} %shard_map.85.b_own), channel_id=1, source_target_pairs={{0,1},{1,0},{2,3},{3,2},{4,5},{5,4},{6,7},{7,6},{8,9},{9,8},{10,11... | collective-permute-start | bytes 49160 | tf_op jit(solution)/shard_map/ppermute | solution.py:334
  10.4 6.8 %collective-permute-start.9 = (bf16[40,1024]{1,0:T(8,128)(2,1)S(1)}, bf16[40,1024]{1,0:T(8,128)(2,1)S(1)}, u32[]{:S(2)}, u32[]{:S(2)}) collective-permute-start(bf16[40,1024]{1,0:T(8,128)(2,1)S(1)} %get-tuple-element.66.mine), channel_id=1, source_target_pairs={{0,2},{1,3},{2,0},{3,1},{4,6},{5,7},{6,4},{7,5},{8,10},{9,11},{10,... | collective-permute-start | bytes 245768 | tf_op jit(solution)/shard_map/ppermute | solution.py:334
  12.6 6.6 %collective-permute-start.11 = (bf16[40,1024]{1,0:T(8,128)(2,1)S(1)}, bf16[40,1024]{1,0:T(8,128)(2,1)S(1)}, u32[]{:S(2)}, u32[]{:S(2)}) collective-permute-start(bf16[40,1024]{1,0:T(8,128)(2,1)S(1)} %get-tuple-element.70.mine), channel_id=1, source_target_pairs={{0,2},{1,3},{2,0},{3,1},{4,6},{5,7},{6,4},{7,5},{8,10},{9,11},{10,... | collective-permute-start | bytes 245768 | tf_op jit(solution)/shard_map/ppermute | solution.py:334
  12.8 16.0 %collective-permute-start.13 = (bf16[1024,1024]{1,0:T(8,128)(2,1)S(1)}, bf16[1024,1024]{1,0:T(8,128)(2,1)S(1)}, u32[]{:S(2)}, u32[]{:S(2)}) collective-permute-start(bf16[1024,1024]{1,0:T(8,128)(2,1)S(1)} %copy-done), channel_id=1, source_target_pairs={{0,1},{1,0},{2,3},{3,2},{4,5},{5,4},{6,7},{7,6},{8,9},{9,8},{10,11... | collective-permute-start | bytes 6291464 | tf_op jit(solution)/shard_map/ppermute | solution.py:334
  15.0 10.5 %collective-permute-start.7 = (bf16[40,1024]{1,0:T(8,128)(2,1)S(1)}, bf16[40,1024]{1,0:T(8,128)(2,1)S(1)}, u32[]{:S(2)}, u32[]{:S(2)}) collective-permute-start(bf16[40,1024]{1,0:T(8,128)(2,1)S(1)} %get-tuple-element.64), channel_id=1, source_target_pairs={{0,36},{1,37},{2,38},{3,39},{4,40},{5,41},{6,42},{7,43},{8,44},{9,... | collective-permute-start | bytes 245768 | tf_op jit(solution)/shard_map/ppermute | solution.py:334
  16.0 9.5 %collective-permute-start.8 = (bf16[40,1024]{1,0:T(8,128)(2,1)S(1)}, bf16[40,1024]{1,0:T(8,128)(2,1)S(1)}, u32[]{:S(2)}, u32[]{:S(2)}) collective-permute-start(bf16[40,1024]{1,0:T(8,128)(2,1)S(1)} %get-tuple-element.65), channel_id=1, source_target_pairs={{0,4},{1,5},{2,6},{3,7},{4,8},{5,9},{6,10},{7,11},{8,12},{9,13},{1... | collective-permute-start | bytes 245768 | tf_op jit(solution)/shard_map/ppermute | solution.py:334
  17.3 8.4 %collective-permute-start.10 = (bf16[40,1024]{1,0:T(8,128)(2,1)S(1)}, bf16[40,1024]{1,0:T(8,128)(2,1)S(1)}, u32[]{:S(2)}, u32[]{:S(2)}) collective-permute-start(bf16[40,1024]{1,0:T(8,128)(2,1)S(1)} %shard_map.89), channel_id=1, source_target_pairs={{0,32},{1,33},{2,34},{3,35},{4,36},{5,37},{6,38},{7,39},{8,40},{9,... | collective-permute-start | bytes 245768 | tf_op jit(solution)/shard_map/ppermute | solution.py:334
  19.2 6.4 %copy-start.2 = (bf16[1024,3,256]{2,0,1:T(8,128)(2,1)S(1)}, bf16[1024,3,256]{2,0,1:T(8,128)(2,1)}, u32[]{:S(2)}) copy-start(bf16[1024,3,256]{2,0,1:T(8,128)(2,1)} %param.10) | copy-start | bytes 4718596
  19.3 6.4 %copy-start.3 = (bf16[256,1024]{1,0:T(8,128)(2,1)S(1)}, bf16[256,1024]{1,0:T(8,128)(2,1)}, u32[]{:S(2)}) copy-start(bf16[256,1024]{1,0:T(8,128)(2,1)} %o_own.1) | copy-start | bytes 1572868
  27.3 4.3 %collective-permute-start.12 = (bf16[80,1024]{1,0:T(8,128)(2,1)S(1)}, bf16[80,1024]{1,0:T(8,128)(2,1)S(1)}, u32[]{:S(2)}, u32[]{:S(2)}) collective-permute-start(bf16[80,1024]{1,0:T(8,128)(2,1)S(1)} %get-tuple-element.75.mine), channel_id=1, source_target_pairs={{0,2},{1,3},{2,0},{3,1},{4,6},{5,7},{6,4},{7,5},{8,10},{9,11},{10,... | collective-permute-start | bytes 491528 | tf_op jit(solution)/shard_map/ppermute | solution.py:334
  27.4 6.1 %collective-permute-start.15 = (bf16[80,1024]{1,0:T(8,128)(2,1)S(1)}, bf16[80,1024]{1,0:T(8,128)(2,1)S(1)}, u32[]{:S(2)}, u32[]{:S(2)}) collective-permute-start(bf16[80,1024]{1,0:T(8,128)(2,1)S(1)} %get-tuple-element.82.mine), channel_id=1, source_target_pairs={{0,2},{1,3},{2,0},{3,1},{4,6},{5,7},{6,4},{7,5},{8,10},{9,11},{10,... | collective-permute-start | bytes 491528 | tf_op jit(solution)/shard_map/ppermute | solution.py:334
  33.4 5.5 %collective-permute-start.14 = (bf16[80,1024]{1,0:T(8,128)(2,1)S(1)}, bf16[80,1024]{1,0:T(8,128)(2,1)S(1)}, u32[]{:S(2)}, u32[]{:S(2)}) collective-permute-start(bf16[80,1024]{1,0:T(8,128)(2,1)S(1)} %shard_map.92.mine), channel_id=1, source_target_pairs={{0,2},{1,3},{2,0},{3,1},{4,6},{5,7},{6,4},{7,5},{8,10},{9,11},{10,... | collective-permute-start | bytes 491528 | tf_op jit(solution)/shard_map/ppermute | solution.py:334
  35.3 7.5 %collective-permute-start.18 = (bf16[80,1024]{1,0:T(8,128)(2,1)S(1)}, bf16[80,1024]{1,0:T(8,128)(2,1)S(1)}, u32[]{:S(2)}, u32[]{:S(2)}) collective-permute-start(bf16[80,1024]{1,0:T(8,128)(2,1)S(1)} %shard_map.94.mine), channel_id=1, source_target_pairs={{0,2},{1,3},{2,0},{3,1},{4,6},{5,7},{6,4},{7,5},{8,10},{9,11},{10,... | collective-permute-start | bytes 491528 | tf_op jit(solution)/shard_map/ppermute | solution.py:334
  38.9 5.3 %collective-permute-start.16 = (bf16[40,1024]{1,0:T(8,128)(2,1)S(1)}, bf16[40,1024]{1,0:T(8,128)(2,1)S(1)}, u32[]{:S(2)}, u32[]{:S(2)}) collective-permute-start(bf16[40,1024]{1,0:T(8,128)(2,1)S(1)} %get-tuple-element.83), channel_id=1, source_target_pairs={{0,254},{1,255},{2,252},{3,253},{4,224},{5,225},{6,226},{7,227},{8... | collective-permute-start | bytes 245768 | tf_op jit(solution)/shard_map/ppermute | solution.py:334
  42.7 3.3 %collective-permute-start.17 = (bf16[40,1024]{1,0:T(8,128)(2,1)S(1)}, bf16[40,1024]{1,0:T(8,128)(2,1)S(1)}, u32[]{:S(2)}, u32[]{:S(2)}) collective-permute-start(bf16[40,1024]{1,0:T(8,128)(2,1)S(1)} %get-tuple-element.84), channel_id=1, source_target_pairs={{0,30},{1,31},{2,28},{3,29},{4,0},{5,1},{6,2},{7,3},{8,4},{9,5},{1... | collective-permute-start | bytes 245768 | tf_op jit(solution)/shard_map/ppermute | solution.py:334
  42.8 3.4 %collective-permute-start.19 = (bf16[40,1024]{1,0:T(8,128)(2,1)S(1)}, bf16[40,1024]{1,0:T(8,128)(2,1)S(1)}, u32[]{:S(2)}, u32[]{:S(2)}) collective-permute-start(bf16[40,1024]{1,0:T(8,128)(2,1)S(1)} %get-tuple-element.86), channel_id=1, source_target_pairs={{0,224},{1,225},{2,226},{3,227},{4,228},{5,229},{6,230},{7,231},{8... | collective-permute-start | bytes 245768 | tf_op jit(solution)/shard_map/ppermute | solution.py:334
  46.2 7.2 %collective-permute-start.21 = (bf16[80,1024]{1,0:T(8,128)(2,1)S(1)}, bf16[80,1024]{1,0:T(8,128)(2,1)S(1)}, u32[]{:S(2)}, u32[]{:S(2)}) collective-permute-start(bf16[80,1024]{1,0:T(8,128)(2,1)S(1)} %shard_map.97.m1), channel_id=1, source_target_pairs={{0,1},{1,0},{2,3},{3,2},{4,5},{5,4},{6,7},{7,6},{8,9},{9,8},{10,11... | collective-permute-start | bytes 491528 | tf_op jit(solution)/shard_map/ppermute | solution.py:334
  52.4 1.4 %collective-permute-start.20 = (bf16[80,1024]{1,0:T(8,128)(2,1)S(1)}, bf16[80,1024]{1,0:T(8,128)(2,1)S(1)}, u32[]{:S(2)}, u32[]{:S(2)}) collective-permute-start(bf16[80,1024]{1,0:T(8,128)(2,1)S(1)} %shard_map.95.m0), channel_id=1, source_target_pairs={{0,1},{1,0},{2,3},{3,2},{4,5},{5,4},{6,7},{7,6},{8,9},{9,8},{10,11... | collective-permute-start | bytes 491528 | tf_op jit(solution)/shard_map/ppermute | solution.py:334

commit v19 on v18

--- a/solution.py
+++ b/solution.py
@@ -246,9 +246,14 @@
             cols = pair_cols(pair)
             parts.append((q[:, cols], k[:, cols], v[:, cols], jnp.where(ban, NEG, extra[:, cols]).astype(jnp.bfloat16)))
     heads = attend(parts, feat)
-    total = dot(jnp.concatenate(heads[:2], axis=1), o_own[...])
-    total = total + dot(jnp.concatenate(heads[2:], axis=1), o_sib[...])
-    store_halves(total, outs)
+    mixed = jnp.concatenate(heads, axis=1)
+    project_kernel(mixed[:HALF], o_own, o_sib, outs[0])
+    outs[1][...] = mixed[HALF:]
+
+
+def project_kernel(mixed, o_own, o_sib, out):
+    total = dot(mixed[:, :256], o_own[...]) + dot(mixed[:, 256:], o_sib[...])
+    out[...] = total.astype(jnp.bfloat16)
 
 
 def gelu(x):
@@ -380,14 +385,15 @@
     lat = out_to(lat, 1, 0)
 
     xn_a = call(norm_kernel, half, (diag, lon), 10**10, 8)
-    part_a, part_b = call(
+    part_a, rest = call(
         second_kernel,
-        half * 2,
+        half + [(HALF, 512)],
         (xn_a, lat, own, w_second, w_sib, out_second, s1, bias2, bias2_sib),
         10**9,
         16,
     )
     other_a = chip_swap(part_a)
+    part_b = call(project_kernel, half, (rest, out_second, s1), 10**10, 8)
     other_b = chip_swap(part_b)
     mlp = (up_weight, u1, down_weight, d1)
     part_a = call(mlp_kernel, half, (part_a, other_a, diag, lon, *mlp), 10**9, 20)

time: 55.3 us -> 55.2 us (level)
    pallas_call x16 -> x17, Pallas kernels: 9.91 us -> 10.2 us  [call(): pl.pallas_call(kernel, out_shape=shapes, in_specs=[pl.BlockSpec(memory_sp...]
where the time goes in v19:
time: 55.2 us; the launch traced here: 55.1 us
  starting transfers between devices  25.4 us (46%)
  waiting for transfers between devices  17.2 us (31%)
  Pallas kernels  11.4 us (21%)
  local copies, waits for them, and re-layouts  0.73 us (1%)
    ppermute x22, starting transfers between devices, move(): return lax.ppermute(value, AXES, pairs(counts, target))  25.4 us
    ppermute x22, waiting for transfers between devices, move(): return lax.ppermute(value, AXES, pairs(counts, target))  17.2 us
    pallas_call x17, Pallas kernels, call(): pl.pallas_call(kernel, out_shape=shapes, in_specs=[pl.BlockSpec(memory_sp...  10.2 us
    pallas_call x1, Pallas kernels, place_rows(): pl.pallas_call(place_kernel, out_shape=jax.ShapeDtypeStruct(shape, jnp.bf...  1.24 us
  transfers between devices with their start and end apart: 22, of which 12 were waited for; matrix products, arithmetic and copies ran while one was open for 0% of the time, Pallas kernels for 18%

profile of v19, /device:TPU:1, one launch (start us, length us, event | category | flops | bytes accessed | tf_op | source)
XLA Modules:
  0.0 55.1 jit_solution(11152918723348882210)
XLA Ops:
  0.0 3.2 %collective-permute-start.3 = (bf16[3,1024,256]{2,1,0:T(8,128)(2,1)}, bf16[3,1024,256]{2,1,0:T(8,128)(2,1)S(1)}, u32[]{:S(2)}, u32[]{:S(2)}) collective-permute-start(bf16[3,1024,256]{2,1,0:T(8,128)(2,1)} %bitcast.8), channel_id=1, source_target_pairs={{0,1},{1,0},{2,3},{3,2},{4,5},{5,4},{6,7},{7,6},{8,9},{9,8},{10,11... | collective-permute-start | bytes 4718600 | tf_op jit(solution)/shard_map/ppermute | solution.py:339
  3.2 0.5 collective-permute-start.2
  3.8 0.7 %copy-done.7 = f32[2,4,37]{2,1,0:T(4,128)S(1)} copy-done((f32[2,4,37]{2,1,0:T(4,128)S(1)}, f32[2,4,37]{2,1,0:T(4,128)}, u32[]{:S(2)}) %copy-start.7) | copy-done | bytes 1208
  4.4 0.7 %shard_map.82.bias = bf16[32,256]{1,0:T(8,128)(2,1)S(1)} custom-call(f32[2,4,37]{2,1,0:T(4,128)S(1)} %copy-done.7), custom_call_target="tpu_custom_call" | custom-call | flops 5000000000 | bytes 17568 | tf_op jit(solution)/shard_map/pallas_call | solution.py:319
  5.2 2.1 %shard_map.83 = (bf16[160,256]{1,0:T(8,128)(2,1)S(1)}, bf16[160,256]{1,0:T(8,128)(2,1)S(1)}) custom-call(bf16[72,4,1024]{2,1,0:T(4,128)(2,1)S(1)} %bitcast.11, bf16[3,1024,256]{2,1,0:T(8,128)(2,1)S(1)} %bitcast.10, bf16[32,256]{1,0:T(8,128)(2,1)S(1)} %shard_map.82.bias), custom_call_target="tpu_custom_call" | custom-call | flops 1000000000 | bytes 2342912 | tf_op jit(solution)/shard_map/pallas_call | solution.py:319
  7.6 0.4 collective-permute-done.2.o_sib
  8.0 0.7 %collective-permute-done.1.o1 = bf16[160,256]{1,0:T(8,128)(2,1)S(1)} collective-permute-done((bf16[160,256]{1,0:T(8,128)(2,1)S(1)}, bf16[160,256]{1,0:T(8,128)(2,1)S(1)}, u32[]{:S(2)}, u32[]{:S(2)}) %collective-permute-start.1) | collective-permute-done | bytes 81952 | tf_op jit(solution)/shard_map/ppermute | solution.py:339
  9.4 0.7 %shard_map.85.b_own = bf16[32,256]{1,0:T(8,128)(2,1)S(1)} custom-call(f32[2,4,37]{2,1,0:T(4,128)S(1)} %copy-done.8), custom_call_target="tpu_custom_call" | custom-call | flops 1000000000 | bytes 17568 | tf_op jit(solution)/shard_map/pallas_call | solution.py:319
  10.1 0.3 collective-permute-start.5
  10.4 1.7 %collective-permute-start.9 = (bf16[40,1024]{1,0:T(8,128)(2,1)S(1)}, bf16[40,1024]{1,0:T(8,128)(2,1)S(1)}, u32[]{:S(2)}, u32[]{:S(2)}) collective-permute-start(bf16[40,1024]{1,0:T(8,128)(2,1)S(1)} %get-tuple-element.66.mine), channel_id=1, source_target_pairs={{0,2},{1,3},{2,0},{3,1},{4,6},{5,7},{6,4},{7,5},{8,10},{9,11},{10,... | collective-permute-start | bytes 245768 | tf_op jit(solution)/shard_map/ppermute | solution.py:339
  12.2 0.4 shard_map.86
  12.8 0.4 collective-permute-start.13
  13.2 1.6 %collective-permute-done.4.other = bf16[80,1024]{1,0:T(8,128)(2,1)S(1)} collective-permute-done((bf16[80,1024]{1,0:T(8,128)(2,1)S(1)}, bf16[80,1024]{1,0:T(8,128)(2,1)S(1)}, u32[]{:S(2)}, u32[]{:S(2)}) %collective-permute-start.4) | collective-permute-done | bytes 163872 | tf_op jit(solution)/shard_map/ppermute | solution.py:339
  15.0 1.0 %collective-permute-start.7 = (bf16[40,1024]{1,0:T(8,128)(2,1)S(1)}, bf16[40,1024]{1,0:T(8,128)(2,1)S(1)}, u32[]{:S(2)}, u32[]{:S(2)}) collective-permute-start(bf16[40,1024]{1,0:T(8,128)(2,1)S(1)} %get-tuple-element.64), channel_id=1, source_target_pairs={{0,36},{1,37},{2,38},{3,39},{4,40},{5,41},{6,42},{7,43},{8,44},{9,... | collective-permute-start | bytes 245768 | tf_op jit(solution)/shard_map/ppermute | solution.py:339
  16.0 1.3 %collective-permute-start.8 = (bf16[40,1024]{1,0:T(8,128)(2,1)S(1)}, bf16[40,1024]{1,0:T(8,128)(2,1)S(1)}, u32[]{:S(2)}, u32[]{:S(2)}) collective-permute-start(bf16[40,1024]{1,0:T(8,128)(2,1)S(1)} %get-tuple-element.65), channel_id=1, source_target_pairs={{0,4},{1,5},{2,6},{3,7},{4,8},{5,9},{6,10},{7,11},{8,12},{9,13},{1... | collective-permute-start | bytes 245768 | tf_op jit(solution)/shard_map/ppermute | solution.py:339
  17.3 1.9 %collective-permute-start.10 = (bf16[40,1024]{1,0:T(8,128)(2,1)S(1)}, bf16[40,1024]{1,0:T(8,128)(2,1)S(1)}, u32[]{:S(2)}, u32[]{:S(2)}) collective-permute-start(bf16[40,1024]{1,0:T(8,128)(2,1)S(1)} %shard_map.89), channel_id=1, source_target_pairs={{0,32},{1,33},{2,34},{3,35},{4,36},{5,37},{6,38},{7,39},{8,40},{9,... | collective-permute-start | bytes 245768 | tf_op jit(solution)/shard_map/ppermute | solution.py:339
  19.3 6.2 %collective-permute-done.7.p0 = bf16[40,1024]{1,0:T(8,128)(2,1)S(1)} collective-permute-done((bf16[40,1024]{1,0:T(8,128)(2,1)S(1)}, bf16[40,1024]{1,0:T(8,128)(2,1)S(1)}, u32[]{:S(2)}, u32[]{:S(2)}) %collective-permute-start.7) | collective-permute-done | bytes 81952 | tf_op jit(solution)/shard_map/ppermute | solution.py:339
  25.7 1.5 %shard_map.91 = (bf16[80,1024]{1,0:T(8,128)(2,1)S(1)}, bf16[80,512]{1,0:T(8,128)(2,1)S(1)}) custom-call(bf16[80,1024]{1,0:T(8,128)(2,1)S(1)} %shard_map.88.xn_a, bf16[40,1024]{1,0:T(8,128)(2,1)S(1)} %collective-permute-done.10.p2.p0, bf16[40,1024]{1,0:T(8,128)(2,1)S(1)} %shard_map.90.p3.p1, bf16[3,1024,256]{2,1,0:T(8,128)(2,1)S(1)} %bitcast.9, ...), custom_call_target="tpu_custom_call" | custom-call | flops 1000000000 | bytes 4800512 | tf_op jit(solution)/shard_map/pallas_call | solution.py:319
  27.6 1.5 %collective-permute-start.15 = (bf16[80,1024]{1,0:T(8,128)(2,1)S(1)}, bf16[80,1024]{1,0:T(8,128)(2,1)S(1)}, u32[]{:S(2)}, u32[]{:S(2)}) collective-permute-start(bf16[80,1024]{1,0:T(8,128)(2,1)S(1)} %shard_map.93.mine), channel_id=1, source_target_pairs={{0,2},{1,3},{2,0},{3,1},{4,6},{5,7},{6,4},{7,5},{8,10},{9,11},{10,... | collective-permute-start | bytes 491528 | tf_op jit(solution)/shard_map/ppermute | solution.py:339
  29.2 2.3 %collective-permute-done.12.other = bf16[80,1024]{1,0:T(8,128)(2,1)S(1)} collective-permute-done((bf16[80,1024]{1,0:T(8,128)(2,1)S(1)}, bf16[80,1024]{1,0:T(8,128)(2,1)S(1)}, u32[]{:S(2)}, u32[]{:S(2)}) %collective-permute-start.12) | collective-permute-done | bytes 163872 | tf_op jit(solution)/shard_map/ppermute | solution.py:339
  31.5 1.8 %shard_map.92.mine = bf16[80,1024]{1,0:T(8,128)(2,1)S(1)} custom-call(bf16[80,1024]{1,0:T(8,128)(2,1)S(1)} %get-tuple-element.75.mine, bf16[80,1024]{1,0:T(8,128)(2,1)S(1)} %collective-permute-done.12.other, bf16[40,1024]{1,0:T(8,128)(2,1)S(1)} %collective-permute-done.7.p0, bf16[40,1024]{1,0:T(8,128)(2,1)S(1)} %collective-permute-done.8.p1, ...), custom_call_target="tpu_custom_call" | custom-call | flops 1000000000 | bytes 9043968 | tf_op jit(solution)/shard_map/pallas_call | solution.py:319
  33.4 1.8 %shard_map.95.mine = bf16[80,1024]{1,0:T(8,128)(2,1)S(1)} custom-call(bf16[80,1024]{1,0:T(8,128)(2,1)S(1)} %shard_map.93.mine, bf16[80,1024]{1,0:T(8,128)(2,1)S(1)} %collective-permute-done.15.other, bf16[40,1024]{1,0:T(8,128)(2,1)S(1)} %collective-permute-done.10.p2.p0, bf16[40,1024]{1,0:T(8,128)(2,1)S(1)} %shard_map.90.p3.p1, ...), custom_call_target="tpu_custom_call" | custom-call | flops 1000000000 | bytes 9043968 | tf_op jit(solution)/shard_map/pallas_call | solution.py:319
  35.2 1.5 %collective-permute-start.18 = (bf16[80,1024]{1,0:T(8,128)(2,1)S(1)}, bf16[80,1024]{1,0:T(8,128)(2,1)S(1)}, u32[]{:S(2)}, u32[]{:S(2)}) collective-permute-start(bf16[80,1024]{1,0:T(8,128)(2,1)S(1)} %shard_map.95.mine), channel_id=1, source_target_pairs={{0,2},{1,3},{2,0},{3,1},{4,6},{5,7},{6,4},{7,5},{8,10},{9,11},{10,... | collective-permute-start | bytes 491528 | tf_op jit(solution)/shard_map/ppermute | solution.py:339
  36.8 2.1 %collective-permute-done.14.other = bf16[80,1024]{1,0:T(8,128)(2,1)S(1)} collective-permute-done((bf16[80,1024]{1,0:T(8,128)(2,1)S(1)}, bf16[80,1024]{1,0:T(8,128)(2,1)S(1)}, u32[]{:S(2)}, u32[]{:S(2)}) %collective-permute-start.14) | collective-permute-done | bytes 163872 | tf_op jit(solution)/shard_map/ppermute | solution.py:339
  38.9 3.8 %collective-permute-start.16 = (bf16[40,1024]{1,0:T(8,128)(2,1)S(1)}, bf16[40,1024]{1,0:T(8,128)(2,1)S(1)}, u32[]{:S(2)}, u32[]{:S(2)}) collective-permute-start(bf16[40,1024]{1,0:T(8,128)(2,1)S(1)} %get-tuple-element.83), channel_id=1, source_target_pairs={{0,254},{1,255},{2,252},{3,253},{4,224},{5,225},{6,226},{7,227},{8... | collective-permute-start | bytes 245768 | tf_op jit(solution)/shard_map/ppermute | solution.py:339
  42.7 0.8 %collective-permute-start.19 = (bf16[40,1024]{1,0:T(8,128)(2,1)S(1)}, bf16[40,1024]{1,0:T(8,128)(2,1)S(1)}, u32[]{:S(2)}, u32[]{:S(2)}) collective-permute-start(bf16[40,1024]{1,0:T(8,128)(2,1)S(1)} %get-tuple-element.86), channel_id=1, source_target_pairs={{0,224},{1,225},{2,226},{3,227},{4,228},{5,229},{6,230},{7,231},{8... | collective-permute-start | bytes 245768 | tf_op jit(solution)/shard_map/ppermute | solution.py:339
  43.6 0.6 %collective-permute-done.16.p0 = bf16[40,1024]{1,0:T(8,128)(2,1)S(1)} collective-permute-done((bf16[40,1024]{1,0:T(8,128)(2,1)S(1)}, bf16[40,1024]{1,0:T(8,128)(2,1)S(1)}, u32[]{:S(2)}, u32[]{:S(2)}) %collective-permute-start.16) | collective-permute-done | bytes 81952 | tf_op jit(solution)/shard_map/ppermute | solution.py:339
  44.2 1.8 %collective-permute-done.17.p1 = bf16[40,1024]{1,0:T(8,128)(2,1)S(1)} collective-permute-done((bf16[40,1024]{1,0:T(8,128)(2,1)S(1)}, bf16[40,1024]{1,0:T(8,128)(2,1)S(1)}, u32[]{:S(2)}, u32[]{:S(2)}) %collective-permute-start.17) | collective-permute-done | bytes 81952 | tf_op jit(solution)/shard_map/ppermute | solution.py:339
  46.1 6.2 %collective-permute-start.21 = (bf16[80,1024]{1,0:T(8,128)(2,1)S(1)}, bf16[80,1024]{1,0:T(8,128)(2,1)S(1)}, u32[]{:S(2)}, u32[]{:S(2)}) collective-permute-start(bf16[80,1024]{1,0:T(8,128)(2,1)S(1)} %shard_map.98.m1), channel_id=1, source_target_pairs={{0,1},{1,0},{2,3},{3,2},{4,5},{5,4},{6,7},{7,6},{8,9},{9,8},{10,11... | collective-permute-start | bytes 491528 | tf_op jit(solution)/shard_map/ppermute | solution.py:339
  52.4 0.9 %collective-permute-done.21.s1 = bf16[80,1024]{1,0:T(8,128)(2,1)S(1)} collective-permute-done((bf16[80,1024]{1,0:T(8,128)(2,1)S(1)}, bf16[80,1024]{1,0:T(8,128)(2,1)S(1)}, u32[]{:S(2)}, u32[]{:S(2)}) %collective-permute-start.21) | collective-permute-done | bytes 163872 | tf_op jit(solution)/shard_map/ppermute | solution.py:339
  53.4 0.4 collective-permute-done.20.s0
  53.7 1.2 %shard_map.99 = bf16[72,4,1024]{2,1,0:T(4,128)(2,1)} custom-call(bf16[80,1024]{1,0:T(8,128)(2,1)S(1)} %shard_map.96.m0, bf16[80,1024]{1,0:T(8,128)(2,1)S(1)} %shard_map.98.m1, bf16[80,1024]{1,0:T(8,128)(2,1)S(1)} %collective-permute-done.20.s0, bf16[80,1024]{1,0:T(8,128)(2,1)S(1)} %collective-permute-done.21.s1), custom_call_target="tpu_custom_call" | custom-call | flops 200000000 | bytes 2000000 | tf_op jit(solution)/shard_map/pallas_call | solution.py:305
  (48 shorter events, 2.5 us)
Async XLA Ops:
  0.0 5.2 %copy-start.5 = (bf16[1024,3,256]{2,0,1:T(8,128)(2,1)S(1)}, bf16[1024,3,256]{2,0,1:T(8,128)(2,1)}, u32[]{:S(2)}) copy-start(bf16[1024,3,256]{2,0,1:T(8,128)(2,1)} %param.9) | copy-start | bytes 4718596
  0.0 5.2 %copy-start.6 = (bf16[4,6,12,1024]{3,0,2,1:T(4,128)(2,1)S(1)}, bf16[4,6,12,1024]{3,0,2,1:T(4,128)(2,1)}, u32[]{:S(2)}) copy-start(bf16[4,6,12,1024]{3,0,2,1:T(4,128)(2,1)} %param.8) | copy-start | bytes 1769476
  0.0 8.6 %collective-permute-start.3 = (bf16[3,1024,256]{2,1,0:T(8,128)(2,1)}, bf16[3,1024,256]{2,1,0:T(8,128)(2,1)S(1)}, u32[]{:S(2)}, u32[]{:S(2)}) collective-permute-start(bf16[3,1024,256]{2,1,0:T(8,128)(2,1)} %bitcast.8), channel_id=1, source_target_pairs={{0,1},{1,0},{2,3},{3,2},{4,5},{5,4},{6,7},{7,6},{8,9},{9,8},{10,11... | collective-permute-start | bytes 4718600 | tf_op jit(solution)/shard_map/ppermute | solution.py:339
  3.2 4.0 %collective-permute-start = (bf16[256,1024]{1,0:T(8,128)(2,1)}, bf16[256,1024]{1,0:T(8,128)(2,1)S(1)}, u32[]{:S(2)}, u32[]{:S(2)}) collective-permute-start(bf16[256,1024]{1,0:T(8,128)(2,1)} %w0.1), channel_id=1, source_target_pairs={{0,1},{1,0},{2,3},{3,2},{4,5},{5,4},{6,7},{7,6},{8,9},{9,8},{10,11... | collective-permute-start | bytes 1572872 | tf_op jit(solution)/shard_map/ppermute | solution.py:339
  3.2 4.7 %collective-permute-start.2 = (bf16[256,1024]{1,0:T(8,128)(2,1)}, bf16[256,1024]{1,0:T(8,128)(2,1)S(1)}, u32[]{:S(2)}, u32[]{:S(2)}) collective-permute-start(bf16[256,1024]{1,0:T(8,128)(2,1)} %o_own.3), channel_id=1, source_target_pairs={{0,1},{1,0},{2,3},{3,2},{4,5},{5,4},{6,7},{7,6},{8,9},{9,8},{10,11... | collective-permute-start | bytes 1572872 | tf_op jit(solution)/shard_map/ppermute | solution.py:339
  3.8 0.7 %copy-start.7 = (f32[2,4,37]{2,1,0:T(4,128)S(1)}, f32[2,4,37]{2,1,0:T(4,128)}, u32[]{:S(2)}) copy-start(f32[2,4,37]{2,1,0:T(4,128)} %table.2) | copy-start | bytes 3556
  5.2 3.5 %copy-start.1 = (bf16[1024,1024]{1,0:T(8,128)(2,1)S(1)}, bf16[1024,1024]{1,0:T(8,128)(2,1)}, u32[]{:S(2)}) copy-start(bf16[1024,1024]{1,0:T(8,128)(2,1)} %d0.3) | copy-start | bytes 6291460
  5.2 3.7 %copy-start.4 = (bf16[256,1024]{1,0:T(8,128)(2,1)S(1)}, bf16[256,1024]{1,0:T(8,128)(2,1)}, u32[]{:S(2)}) copy-start(bf16[256,1024]{1,0:T(8,128)(2,1)} %w0.1) | copy-start | bytes 1572868
  5.2 4.1 %copy-start.8 = (f32[2,4,37]{2,1,0:T(4,128)S(1)}, f32[2,4,37]{2,1,0:T(4,128)}, u32[]{:S(2)}) copy-start(f32[2,4,37]{2,1,0:T(4,128)} %table.2) | copy-start | bytes 3556
  7.3 1.4 %collective-permute-start.1 = (bf16[160,256]{1,0:T(8,128)(2,1)S(1)}, bf16[160,256]{1,0:T(8,128)(2,1)S(1)}, u32[]{:S(2)}, u32[]{:S(2)}) collective-permute-start(bf16[160,256]{1,0:T(8,128)(2,1)S(1)} %get-tuple-element.52), channel_id=1, source_target_pairs={{0,1},{1,0},{2,3},{3,2},{4,5},{5,4},{6,7},{7,6},{8,9},{9,8},{10,11... | collective-permute-start | bytes 245768 | tf_op jit(solution)/shard_map/ppermute | solution.py:339
  8.7 6.2 %collective-permute-start.6 = (bf16[1024,1024]{1,0:T(8,128)(2,1)S(1)}, bf16[1024,1024]{1,0:T(8,128)(2,1)S(1)}, u32[]{:S(2)}, u32[]{:S(2)}) collective-permute-start(bf16[1024,1024]{1,0:T(8,128)(2,1)S(1)} %copy-done.1), channel_id=1, source_target_pairs={{0,1},{1,0},{2,3},{3,2},{4,5},{5,4},{6,7},{7,6},{8,9},{9,8},{10,11... | collective-permute-start | bytes 6291464 | tf_op jit(solution)/shard_map/ppermute | solution.py:339
  9.3 5.6 %collective-permute-start.4 = (bf16[80,1024]{1,0:T(8,128)(2,1)S(1)}, bf16[80,1024]{1,0:T(8,128)(2,1)S(1)}, u32[]{:S(2)}, u32[]{:S(2)}) collective-permute-start(bf16[80,1024]{1,0:T(8,128)(2,1)S(1)} %get-tuple-element.55.mine), channel_id=1, source_target_pairs={{0,2},{1,3},{2,0},{3,1},{4,6},{5,7},{6,4},{7,5},{8,10},{9,11},{10,... | collective-permute-start | bytes 491528 | tf_op jit(solution)/shard_map/ppermute | solution.py:339
  10.1 2.8 %copy-start = (bf16[1024,1024]{1,0:T(8,128)(2,1)S(1)}, bf16[1024,1024]{1,0:T(8,128)(2,1)}, u32[]{:S(2)}) copy-start(bf16[1024,1024]{1,0:T(8,128)(2,1)} %u0.3) | copy-start | bytes 6291460
  10.1 2.7 %collective-permute-start.5 = (bf16[32,256]{1,0:T(8,128)(2,1)S(1)}, bf16[32,256]{1,0:T(8,128)(2,1)S(1)}, u32[]{:S(2)}, u32[]{:S(2)}) collective-permute-start(bf16[32,256]{1,0:T(8,128)(2,1)S(1)} %shard_map.85.b_own), channel_id=1, source_target_pairs={{0,1},{1,0},{2,3},{3,2},{4,5},{5,4},{6,7},{7,6},{8,9},{9,8},{10,11... | collective-permute-start | bytes 49160 | tf_op jit(solution)/shard_map/ppermute | solution.py:339
  10.4 6.8 %collective-permute-start.9 = (bf16[40,1024]{1,0:T(8,128)(2,1)S(1)}, bf16[40,1024]{1,0:T(8,128)(2,1)S(1)}, u32[]{:S(2)}, u32[]{:S(2)}) collective-permute-start(bf16[40,1024]{1,0:T(8,128)(2,1)S(1)} %get-tuple-element.66.mine), channel_id=1, source_target_pairs={{0,2},{1,3},{2,0},{3,1},{4,6},{5,7},{6,4},{7,5},{8,10},{9,11},{10,... | collective-permute-start | bytes 245768 | tf_op jit(solution)/shard_map/ppermute | solution.py:339
  12.6 6.6 %collective-permute-start.11 = (bf16[40,1024]{1,0:T(8,128)(2,1)S(1)}, bf16[40,1024]{1,0:T(8,128)(2,1)S(1)}, u32[]{:S(2)}, u32[]{:S(2)}) collective-permute-start(bf16[40,1024]{1,0:T(8,128)(2,1)S(1)} %get-tuple-element.70.mine), channel_id=1, source_target_pairs={{0,2},{1,3},{2,0},{3,1},{4,6},{5,7},{6,4},{7,5},{8,10},{9,11},{10,... | collective-permute-start | bytes 245768 | tf_op jit(solution)/shard_map/ppermute | solution.py:339
  12.8 16.3 %collective-permute-start.13 = (bf16[1024,1024]{1,0:T(8,128)(2,1)S(1)}, bf16[1024,1024]{1,0:T(8,128)(2,1)S(1)}, u32[]{:S(2)}, u32[]{:S(2)}) collective-permute-start(bf16[1024,1024]{1,0:T(8,128)(2,1)S(1)} %copy-done), channel_id=1, source_target_pairs={{0,1},{1,0},{2,3},{3,2},{4,5},{5,4},{6,7},{7,6},{8,9},{9,8},{10,11... | collective-permute-start | bytes 6291464 | tf_op jit(solution)/shard_map/ppermute | solution.py:339
  15.0 10.5 %collective-permute-start.7 = (bf16[40,1024]{1,0:T(8,128)(2,1)S(1)}, bf16[40,1024]{1,0:T(8,128)(2,1)S(1)}, u32[]{:S(2)}, u32[]{:S(2)}) collective-permute-start(bf16[40,1024]{1,0:T(8,128)(2,1)S(1)} %get-tuple-element.64), channel_id=1, source_target_pairs={{0,36},{1,37},{2,38},{3,39},{4,40},{5,41},{6,42},{7,43},{8,44},{9,... | collective-permute-start | bytes 245768 | tf_op jit(solution)/shard_map/ppermute | solution.py:339
  16.0 9.5 %collective-permute-start.8 = (bf16[40,1024]{1,0:T(8,128)(2,1)S(1)}, bf16[40,1024]{1,0:T(8,128)(2,1)S(1)}, u32[]{:S(2)}, u32[]{:S(2)}) collective-permute-start(bf16[40,1024]{1,0:T(8,128)(2,1)S(1)} %get-tuple-element.65), channel_id=1, source_target_pairs={{0,4},{1,5},{2,6},{3,7},{4,8},{5,9},{6,10},{7,11},{8,12},{9,13},{1... | collective-permute-start | bytes 245768 | tf_op jit(solution)/shard_map/ppermute | solution.py:339
  17.3 8.4 %collective-permute-start.10 = (bf16[40,1024]{1,0:T(8,128)(2,1)S(1)}, bf16[40,1024]{1,0:T(8,128)(2,1)S(1)}, u32[]{:S(2)}, u32[]{:S(2)}) collective-permute-start(bf16[40,1024]{1,0:T(8,128)(2,1)S(1)} %shard_map.89), channel_id=1, source_target_pairs={{0,32},{1,33},{2,34},{3,35},{4,36},{5,37},{6,38},{7,39},{8,40},{9,... | collective-permute-start | bytes 245768 | tf_op jit(solution)/shard_map/ppermute | solution.py:339
  19.2 6.4 %copy-start.2 = (bf16[1024,3,256]{2,0,1:T(8,128)(2,1)S(1)}, bf16[1024,3,256]{2,0,1:T(8,128)(2,1)}, u32[]{:S(2)}) copy-start(bf16[1024,3,256]{2,0,1:T(8,128)(2,1)} %param.10) | copy-start | bytes 4718596
  19.3 6.4 %copy-start.3 = (bf16[256,1024]{1,0:T(8,128)(2,1)S(1)}, bf16[256,1024]{1,0:T(8,128)(2,1)}, u32[]{:S(2)}) copy-start(bf16[256,1024]{1,0:T(8,128)(2,1)} %o_own.3) | copy-start | bytes 1572868
  27.2 4.3 %collective-permute-start.12 = (bf16[80,1024]{1,0:T(8,128)(2,1)S(1)}, bf16[80,1024]{1,0:T(8,128)(2,1)S(1)}, u32[]{:S(2)}, u32[]{:S(2)}) collective-permute-start(bf16[80,1024]{1,0:T(8,128)(2,1)S(1)} %get-tuple-element.75.mine), channel_id=1, source_target_pairs={{0,2},{1,3},{2,0},{3,1},{4,6},{5,7},{6,4},{7,5},{8,10},{9,11},{10,... | collective-permute-start | bytes 491528 | tf_op jit(solution)/shard_map/ppermute | solution.py:339
  27.6 5.8 %collective-permute-start.15 = (bf16[80,1024]{1,0:T(8,128)(2,1)S(1)}, bf16[80,1024]{1,0:T(8,128)(2,1)S(1)}, u32[]{:S(2)}, u32[]{:S(2)}) collective-permute-start(bf16[80,1024]{1,0:T(8,128)(2,1)S(1)} %shard_map.93.mine), channel_id=1, source_target_pairs={{0,2},{1,3},{2,0},{3,1},{4,6},{5,7},{6,4},{7,5},{8,10},{9,11},{10,... | collective-permute-start | bytes 491528 | tf_op jit(solution)/shard_map/ppermute | solution.py:339
  33.3 5.5 %collective-permute-start.14 = (bf16[80,1024]{1,0:T(8,128)(2,1)S(1)}, bf16[80,1024]{1,0:T(8,128)(2,1)S(1)}, u32[]{:S(2)}, u32[]{:S(2)}) collective-permute-start(bf16[80,1024]{1,0:T(8,128)(2,1)S(1)} %shard_map.92.mine), channel_id=1, source_target_pairs={{0,2},{1,3},{2,0},{3,1},{4,6},{5,7},{6,4},{7,5},{8,10},{9,11},{10,... | collective-permute-start | bytes 491528 | tf_op jit(solution)/shard_map/ppermute | solution.py:339
  35.2 7.5 %collective-permute-start.18 = (bf16[80,1024]{1,0:T(8,128)(2,1)S(1)}, bf16[80,1024]{1,0:T(8,128)(2,1)S(1)}, u32[]{:S(2)}, u32[]{:S(2)}) collective-permute-start(bf16[80,1024]{1,0:T(8,128)(2,1)S(1)} %shard_map.95.mine), channel_id=1, source_target_pairs={{0,2},{1,3},{2,0},{3,1},{4,6},{5,7},{6,4},{7,5},{8,10},{9,11},{10,... | collective-permute-start | bytes 491528 | tf_op jit(solution)/shard_map/ppermute | solution.py:339
  38.9 5.3 %collective-permute-start.16 = (bf16[40,1024]{1,0:T(8,128)(2,1)S(1)}, bf16[40,1024]{1,0:T(8,128)(2,1)S(1)}, u32[]{:S(2)}, u32[]{:S(2)}) collective-permute-start(bf16[40,1024]{1,0:T(8,128)(2,1)S(1)} %get-tuple-element.83), channel_id=1, source_target_pairs={{0,254},{1,255},{2,252},{3,253},{4,224},{5,225},{6,226},{7,227},{8... | collective-permute-start | bytes 245768 | tf_op jit(solution)/shard_map/ppermute | solution.py:339
  42.7 3.3 %collective-permute-start.17 = (bf16[40,1024]{1,0:T(8,128)(2,1)S(1)}, bf16[40,1024]{1,0:T(8,128)(2,1)S(1)}, u32[]{:S(2)}, u32[]{:S(2)}) collective-permute-start(bf16[40,1024]{1,0:T(8,128)(2,1)S(1)} %get-tuple-element.84), channel_id=1, source_target_pairs={{0,30},{1,31},{2,28},{3,29},{4,0},{5,1},{6,2},{7,3},{8,4},{9,5},{1... | collective-permute-start | bytes 245768 | tf_op jit(solution)/shard_map/ppermute | solution.py:339
  42.7 3.4 %collective-permute-start.19 = (bf16[40,1024]{1,0:T(8,128)(2,1)S(1)}, bf16[40,1024]{1,0:T(8,128)(2,1)S(1)}, u32[]{:S(2)}, u32[]{:S(2)}) collective-permute-start(bf16[40,1024]{1,0:T(8,128)(2,1)S(1)} %get-tuple-element.86), channel_id=1, source_target_pairs={{0,224},{1,225},{2,226},{3,227},{4,228},{5,229},{6,230},{7,231},{8... | collective-permute-start | bytes 245768 | tf_op jit(solution)/shard_map/ppermute | solution.py:339
  46.1 7.2 %collective-permute-start.21 = (bf16[80,1024]{1,0:T(8,128)(2,1)S(1)}, bf16[80,1024]{1,0:T(8,128)(2,1)S(1)}, u32[]{:S(2)}, u32[]{:S(2)}) collective-permute-start(bf16[80,1024]{1,0:T(8,128)(2,1)S(1)} %shard_map.98.m1), channel_id=1, source_target_pairs={{0,1},{1,0},{2,3},{3,2},{4,5},{5,4},{6,7},{7,6},{8,9},{9,8},{10,11... | collective-permute-start | bytes 491528 | tf_op jit(solution)/shard_map/ppermute | solution.py:339
  52.3 1.4 %collective-permute-start.20 = (bf16[80,1024]{1,0:T(8,128)(2,1)S(1)}, bf16[80,1024]{1,0:T(8,128)(2,1)S(1)}, u32[]{:S(2)}, u32[]{:S(2)}) collective-permute-start(bf16[80,1024]{1,0:T(8,128)(2,1)S(1)} %shard_map.96.m0), channel_id=1, source_target_pairs={{0,1},{1,0},{2,3},{3,2},{4,5},{5,4},{6,7},{7,6},{8,9},{9,8},{10,11... | collective-permute-start | bytes 491528 | tf_op jit(solution)/shard_map/ppermute | solution.py:339

commit v20 on v19

--- a/solution.py
+++ b/solution.py
@@ -199,8 +199,12 @@
         out[...] = total[start:stop].astype(jnp.bfloat16)
 
 
-def partial_kernel(o0, o1, w0, w1, *outs):
-    store_three(dot(o0[...], w0[...]) + dot(o1[...], w1[...]), outs)
+def partial_kernel(half, o0, o1, w0, w1, *outs):
+    rows = slice(half * HALF, (half + 1) * HALF)
+    total = dot(o0[rows], w0[...]) + dot(o1[rows], w1[...])
+    count = HALF // len(outs)
+    for p, out in enumerate(outs):
+        out[...] = total[p * count : (p + 1) * count].astype(jnp.bfloat16)
 
 
 def branch_sum(mine, other):
@@ -370,8 +374,10 @@
     given, up_late, s1, w_sib, down_late = tied(core_swap(give), up_weight, s1, w_sib, down_weight)
     d1 = core_swap(down_late)
     u1 = core_swap(up_late)
-    part_a, part_lat, part_own = call(partial_kernel, half + piece * 2, (keep, given, out_first, f1), 2 * 10**8, 8)
+    heads_out = (keep, given, out_first, f1)
+    part_a = call(functools.partial(partial_kernel, 0), half, heads_out, 10**8, 8)
     other_a = chip_swap(part_a)
+    part_lat, part_own = call(functools.partial(partial_kernel, 1), piece * 2, heads_out, 10**8, 8)
     other_lat = chip_swap(part_lat)
     other_own = chip_swap(part_own)
     other_a, bias2_sib, d1 = tied(other_a, bias2_sib, d1)

time: 55.2 us -> 54.9 us (level)
    pallas_call x17 -> x18, Pallas kernels: 10.2 us -> 10.4 us  [call(): pl.pallas_call(kernel, out_shape=shapes, in_specs=[pl.BlockSpec(memory_sp...]
  transfers between devices with their start and end apart: 22 -> 22, of which waited for: 12 -> 11; matrix products, arithmetic and copies ran while one was open for 0% -> 0% of each run, Pallas kernels for 18% -> 19%
where the time goes in v20:
time: 54.9 us; the launch traced here: 54.8 us
  starting transfers between devices  25.3 us (46%)
  waiting for transfers between devices  16.7 us (30%)
  Pallas kernels  11.7 us (21%)
  local copies, waits for them, and re-layouts  0.73 us (1%)
    ppermute x22, starting transfers between devices, move(): return lax.ppermute(value, AXES, pairs(counts, target))  25.3 us
    ppermute x22, waiting for transfers between devices, move(): return lax.ppermute(value, AXES, pairs(counts, target))  16.7 us
    pallas_call x18, Pallas kernels, call(): pl.pallas_call(kernel, out_shape=shapes, in_specs=[pl.BlockSpec(memory_sp...  10.4 us
    pallas_call x1, Pallas kernels, place_rows(): pl.pallas_call(place_kernel, out_shape=jax.ShapeDtypeStruct(shape, jnp.bf...  1.24 us
  transfers between devices with their start and end apart: 22, of which 11 were waited for; matrix products, arithmetic and copies ran while one was open for 0% of the time, Pallas kernels for 19%

profile of v20, /device:TPU:1, one launch (start us, length us, event | category | flops | bytes accessed | tf_op | source)
XLA Modules:
  0.0 54.8 jit_solution(16906439737374392748)
XLA Ops:
  0.0 3.2 %collective-permute-start.3 = (bf16[3,1024,256]{2,1,0:T(8,128)(2,1)}, bf16[3,1024,256]{2,1,0:T(8,128)(2,1)S(1)}, u32[]{:S(2)}, u32[]{:S(2)}) collective-permute-start(bf16[3,1024,256]{2,1,0:T(8,128)(2,1)} %bitcast.8), channel_id=1, source_target_pairs={{0,1},{1,0},{2,3},{3,2},{4,5},{5,4},{6,7},{7,6},{8,9},{9,8},{10,11... | collective-permute-start | bytes 4718600 | tf_op jit(solution)/shard_map/ppermute | solution.py:343
  3.2 0.5 collective-permute-start.2
  3.8 0.7 %copy-done.7 = f32[2,4,37]{2,1,0:T(4,128)S(1)} copy-done((f32[2,4,37]{2,1,0:T(4,128)S(1)}, f32[2,4,37]{2,1,0:T(4,128)}, u32[]{:S(2)}) %copy-start.7) | copy-done | bytes 1208
  4.4 0.7 %shard_map.82.bias = bf16[32,256]{1,0:T(8,128)(2,1)S(1)} custom-call(f32[2,4,37]{2,1,0:T(4,128)S(1)} %copy-done.7), custom_call_target="tpu_custom_call" | custom-call | flops 5000000000 | bytes 17568 | tf_op jit(solution)/shard_map/pallas_call | solution.py:323
  5.2 2.1 %shard_map.83 = (bf16[160,256]{1,0:T(8,128)(2,1)S(1)}, bf16[160,256]{1,0:T(8,128)(2,1)S(1)}) custom-call(bf16[72,4,1024]{2,1,0:T(4,128)(2,1)S(1)} %bitcast.11, bf16[3,1024,256]{2,1,0:T(8,128)(2,1)S(1)} %bitcast.10, bf16[32,256]{1,0:T(8,128)(2,1)S(1)} %shard_map.82.bias), custom_call_target="tpu_custom_call" | custom-call | flops 1000000000 | bytes 2342912 | tf_op jit(solution)/shard_map/pallas_call | solution.py:323
  7.6 0.4 collective-permute-done.2.o_sib
  8.0 0.7 %collective-permute-done.1.o1 = bf16[160,256]{1,0:T(8,128)(2,1)S(1)} collective-permute-done((bf16[160,256]{1,0:T(8,128)(2,1)S(1)}, bf16[160,256]{1,0:T(8,128)(2,1)S(1)}, u32[]{:S(2)}, u32[]{:S(2)}) %collective-permute-start.1) | collective-permute-done | bytes 81952 | tf_op jit(solution)/shard_map/ppermute | solution.py:343
  9.3 0.7 %shard_map.85.b_own = bf16[32,256]{1,0:T(8,128)(2,1)S(1)} custom-call(f32[2,4,37]{2,1,0:T(4,128)S(1)} %copy-done.8), custom_call_target="tpu_custom_call" | custom-call | flops 1000000000 | bytes 17568 | tf_op jit(solution)/shard_map/pallas_call | solution.py:323
  10.0 0.3 collective-permute-start.5
  10.7 1.8 %collective-permute-start.9 = (bf16[40,1024]{1,0:T(8,128)(2,1)S(1)}, bf16[40,1024]{1,0:T(8,128)(2,1)S(1)}, u32[]{:S(2)}, u32[]{:S(2)}) collective-permute-start(bf16[40,1024]{1,0:T(8,128)(2,1)S(1)} %get-tuple-element.64.mine), channel_id=1, source_target_pairs={{0,2},{1,3},{2,0},{3,1},{4,6},{5,7},{6,4},{7,5},{8,10},{9,11},{10,... | collective-permute-start | bytes 245768 | tf_op jit(solution)/shard_map/ppermute | solution.py:343
  12.5 0.4 shard_map.86
  13.1 0.5 collective-permute-start.13
  13.6 1.3 %collective-permute-done.4.other = bf16[80,1024]{1,0:T(8,128)(2,1)S(1)} collective-permute-done((bf16[80,1024]{1,0:T(8,128)(2,1)S(1)}, bf16[80,1024]{1,0:T(8,128)(2,1)S(1)}, u32[]{:S(2)}, u32[]{:S(2)}) %collective-permute-start.4) | collective-permute-done | bytes 163872 | tf_op jit(solution)/shard_map/ppermute | solution.py:343
  14.9 1.0 %collective-permute-start.7 = (bf16[40,1024]{1,0:T(8,128)(2,1)S(1)}, bf16[40,1024]{1,0:T(8,128)(2,1)S(1)}, u32[]{:S(2)}, u32[]{:S(2)}) collective-permute-start(bf16[40,1024]{1,0:T(8,128)(2,1)S(1)} %get-tuple-element.62), channel_id=1, source_target_pairs={{0,36},{1,37},{2,38},{3,39},{4,40},{5,41},{6,42},{7,43},{8,44},{9,... | collective-permute-start | bytes 245768 | tf_op jit(solution)/shard_map/ppermute | solution.py:343
  15.9 1.3 %collective-permute-start.8 = (bf16[40,1024]{1,0:T(8,128)(2,1)S(1)}, bf16[40,1024]{1,0:T(8,128)(2,1)S(1)}, u32[]{:S(2)}, u32[]{:S(2)}) collective-permute-start(bf16[40,1024]{1,0:T(8,128)(2,1)S(1)} %get-tuple-element.63), channel_id=1, source_target_pairs={{0,4},{1,5},{2,6},{3,7},{4,8},{5,9},{6,10},{7,11},{8,12},{9,13},{1... | collective-permute-start | bytes 245768 | tf_op jit(solution)/shard_map/ppermute | solution.py:343
  17.3 1.9 %collective-permute-start.10 = (bf16[40,1024]{1,0:T(8,128)(2,1)S(1)}, bf16[40,1024]{1,0:T(8,128)(2,1)S(1)}, u32[]{:S(2)}, u32[]{:S(2)}) collective-permute-start(bf16[40,1024]{1,0:T(8,128)(2,1)S(1)} %shard_map.90), channel_id=1, source_target_pairs={{0,32},{1,33},{2,34},{3,35},{4,36},{5,37},{6,38},{7,39},{8,40},{9,... | collective-permute-start | bytes 245768 | tf_op jit(solution)/shard_map/ppermute | solution.py:343
  19.2 6.2 %collective-permute-done.7.p0 = bf16[40,1024]{1,0:T(8,128)(2,1)S(1)} collective-permute-done((bf16[40,1024]{1,0:T(8,128)(2,1)S(1)}, bf16[40,1024]{1,0:T(8,128)(2,1)S(1)}, u32[]{:S(2)}, u32[]{:S(2)}) %collective-permute-start.7) | collective-permute-done | bytes 81952 | tf_op jit(solution)/shard_map/ppermute | solution.py:343
  25.7 1.5 %shard_map.92 = (bf16[80,1024]{1,0:T(8,128)(2,1)S(1)}, bf16[80,512]{1,0:T(8,128)(2,1)S(1)}) custom-call(bf16[80,1024]{1,0:T(8,128)(2,1)S(1)} %shard_map.89.xn_a, bf16[40,1024]{1,0:T(8,128)(2,1)S(1)} %collective-permute-done.10.p2.p0, bf16[40,1024]{1,0:T(8,128)(2,1)S(1)} %shard_map.91.p3.p1, bf16[3,1024,256]{2,1,0:T(8,128)(2,1)S(1)} %bitcast.9, ...), custom_call_target="tpu_custom_call" | custom-call | flops 1000000000 | bytes 4800512 | tf_op jit(solution)/shard_map/pallas_call | solution.py:323
  27.6 1.5 %collective-permute-start.15 = (bf16[80,1024]{1,0:T(8,128)(2,1)S(1)}, bf16[80,1024]{1,0:T(8,128)(2,1)S(1)}, u32[]{:S(2)}, u32[]{:S(2)}) collective-permute-start(bf16[80,1024]{1,0:T(8,128)(2,1)S(1)} %shard_map.94.mine), channel_id=1, source_target_pairs={{0,2},{1,3},{2,0},{3,1},{4,6},{5,7},{6,4},{7,5},{8,10},{9,11},{10,... | collective-permute-start | bytes 491528 | tf_op jit(solution)/shard_map/ppermute | solution.py:343
  29.1 2.3 %collective-permute-done.12.other = bf16[80,1024]{1,0:T(8,128)(2,1)S(1)} collective-permute-done((bf16[80,1024]{1,0:T(8,128)(2,1)S(1)}, bf16[80,1024]{1,0:T(8,128)(2,1)S(1)}, u32[]{:S(2)}, u32[]{:S(2)}) %collective-permute-start.12) | collective-permute-done | bytes 163872 | tf_op jit(solution)/shard_map/ppermute | solution.py:343
  31.4 1.8 %shard_map.93.mine = bf16[80,1024]{1,0:T(8,128)(2,1)S(1)} custom-call(bf16[80,1024]{1,0:T(8,128)(2,1)S(1)} %get-tuple-element.73.mine, bf16[80,1024]{1,0:T(8,128)(2,1)S(1)} %collective-permute-done.12.other, bf16[40,1024]{1,0:T(8,128)(2,1)S(1)} %collective-permute-done.7.p0, bf16[40,1024]{1,0:T(8,128)(2,1)S(1)} %collective-permute-done.8.p1, ...), custom_call_target="tpu_custom_call" | custom-call | flops 1000000000 | bytes 9043968 | tf_op jit(solution)/shard_map/pallas_call | solution.py:323
  33.4 1.8 %shard_map.96.mine = bf16[80,1024]{1,0:T(8,128)(2,1)S(1)} custom-call(bf16[80,1024]{1,0:T(8,128)(2,1)S(1)} %shard_map.94.mine, bf16[80,1024]{1,0:T(8,128)(2,1)S(1)} %collective-permute-done.15.other, bf16[40,1024]{1,0:T(8,128)(2,1)S(1)} %collective-permute-done.10.p2.p0, bf16[40,1024]{1,0:T(8,128)(2,1)S(1)} %shard_map.91.p3.p1, ...), custom_call_target="tpu_custom_call" | custom-call | flops 1000000000 | bytes 9043968 | tf_op jit(solution)/shard_map/pallas_call | solution.py:323
  35.2 1.5 %collective-permute-start.18 = (bf16[80,1024]{1,0:T(8,128)(2,1)S(1)}, bf16[80,1024]{1,0:T(8,128)(2,1)S(1)}, u32[]{:S(2)}, u32[]{:S(2)}) collective-permute-start(bf16[80,1024]{1,0:T(8,128)(2,1)S(1)} %shard_map.96.mine), channel_id=1, source_target_pairs={{0,2},{1,3},{2,0},{3,1},{4,6},{5,7},{6,4},{7,5},{8,10},{9,11},{10,... | collective-permute-start | bytes 491528 | tf_op jit(solution)/shard_map/ppermute | solution.py:343
  36.7 2.1 %collective-permute-done.14.other = bf16[80,1024]{1,0:T(8,128)(2,1)S(1)} collective-permute-done((bf16[80,1024]{1,0:T(8,128)(2,1)S(1)}, bf16[80,1024]{1,0:T(8,128)(2,1)S(1)}, u32[]{:S(2)}, u32[]{:S(2)}) %collective-permute-start.14) | collective-permute-done | bytes 163872 | tf_op jit(solution)/shard_map/ppermute | solution.py:343
  38.8 3.6 %collective-permute-start.16 = (bf16[40,1024]{1,0:T(8,128)(2,1)S(1)}, bf16[40,1024]{1,0:T(8,128)(2,1)S(1)}, u32[]{:S(2)}, u32[]{:S(2)}) collective-permute-start(bf16[40,1024]{1,0:T(8,128)(2,1)S(1)} %get-tuple-element.81), channel_id=1, source_target_pairs={{0,254},{1,255},{2,252},{3,253},{4,224},{5,225},{6,226},{7,227},{8... | collective-permute-start | bytes 245768 | tf_op jit(solution)/shard_map/ppermute | solution.py:343
  42.5 0.8 %collective-permute-start.19 = (bf16[40,1024]{1,0:T(8,128)(2,1)S(1)}, bf16[40,1024]{1,0:T(8,128)(2,1)S(1)}, u32[]{:S(2)}, u32[]{:S(2)}) collective-permute-start(bf16[40,1024]{1,0:T(8,128)(2,1)S(1)} %get-tuple-element.84), channel_id=1, source_target_pairs={{0,224},{1,225},{2,226},{3,227},{4,228},{5,229},{6,230},{7,231},{8... | collective-permute-start | bytes 245768 | tf_op jit(solution)/shard_map/ppermute | solution.py:343
  43.3 0.6 %collective-permute-done.16.p0 = bf16[40,1024]{1,0:T(8,128)(2,1)S(1)} collective-permute-done((bf16[40,1024]{1,0:T(8,128)(2,1)S(1)}, bf16[40,1024]{1,0:T(8,128)(2,1)S(1)}, u32[]{:S(2)}, u32[]{:S(2)}) %collective-permute-start.16) | collective-permute-done | bytes 81952 | tf_op jit(solution)/shard_map/ppermute | solution.py:343
  43.9 1.8 %collective-permute-done.17.p1 = bf16[40,1024]{1,0:T(8,128)(2,1)S(1)} collective-permute-done((bf16[40,1024]{1,0:T(8,128)(2,1)S(1)}, bf16[40,1024]{1,0:T(8,128)(2,1)S(1)}, u32[]{:S(2)}, u32[]{:S(2)}) %collective-permute-start.17) | collective-permute-done | bytes 81952 | tf_op jit(solution)/shard_map/ppermute | solution.py:343
  45.9 6.1 %collective-permute-start.21 = (bf16[80,1024]{1,0:T(8,128)(2,1)S(1)}, bf16[80,1024]{1,0:T(8,128)(2,1)S(1)}, u32[]{:S(2)}, u32[]{:S(2)}) collective-permute-start(bf16[80,1024]{1,0:T(8,128)(2,1)S(1)} %shard_map.99.m1), channel_id=1, source_target_pairs={{0,1},{1,0},{2,3},{3,2},{4,5},{5,4},{6,7},{7,6},{8,9},{9,8},{10,11... | collective-permute-start | bytes 491528 | tf_op jit(solution)/shard_map/ppermute | solution.py:343
  52.1 0.9 %collective-permute-done.21.s1 = bf16[80,1024]{1,0:T(8,128)(2,1)S(1)} collective-permute-done((bf16[80,1024]{1,0:T(8,128)(2,1)S(1)}, bf16[80,1024]{1,0:T(8,128)(2,1)S(1)}, u32[]{:S(2)}, u32[]{:S(2)}) %collective-permute-start.21) | collective-permute-done | bytes 163872 | tf_op jit(solution)/shard_map/ppermute | solution.py:343
  53.0 0.4 collective-permute-done.20.s0
  53.4 1.2 %shard_map.100 = bf16[72,4,1024]{2,1,0:T(4,128)(2,1)} custom-call(bf16[80,1024]{1,0:T(8,128)(2,1)S(1)} %shard_map.97.m0, bf16[80,1024]{1,0:T(8,128)(2,1)S(1)} %shard_map.99.m1, bf16[80,1024]{1,0:T(8,128)(2,1)S(1)} %collective-permute-done.20.s0, bf16[80,1024]{1,0:T(8,128)(2,1)S(1)} %collective-permute-done.21.s1), custom_call_target="tpu_custom_call" | custom-call | flops 200000000 | bytes 2000000 | tf_op jit(solution)/shard_map/pallas_call | solution.py:309
  (49 shorter events, 2.6 us)
Async XLA Ops:
  0.0 5.2 %copy-start.5 = (bf16[1024,3,256]{2,0,1:T(8,128)(2,1)S(1)}, bf16[1024,3,256]{2,0,1:T(8,128)(2,1)}, u32[]{:S(2)}) copy-start(bf16[1024,3,256]{2,0,1:T(8,128)(2,1)} %param.9) | copy-start | bytes 4718596
  0.0 5.2 %copy-start.6 = (bf16[4,6,12,1024]{3,0,2,1:T(4,128)(2,1)S(1)}, bf16[4,6,12,1024]{3,0,2,1:T(4,128)(2,1)}, u32[]{:S(2)}) copy-start(bf16[4,6,12,1024]{3,0,2,1:T(4,128)(2,1)} %param.8) | copy-start | bytes 1769476
  0.0 8.6 %collective-permute-start.3 = (bf16[3,1024,256]{2,1,0:T(8,128)(2,1)}, bf16[3,1024,256]{2,1,0:T(8,128)(2,1)S(1)}, u32[]{:S(2)}, u32[]{:S(2)}) collective-permute-start(bf16[3,1024,256]{2,1,0:T(8,128)(2,1)} %bitcast.8), channel_id=1, source_target_pairs={{0,1},{1,0},{2,3},{3,2},{4,5},{5,4},{6,7},{7,6},{8,9},{9,8},{10,11... | collective-permute-start | bytes 4718600 | tf_op jit(solution)/shard_map/ppermute | solution.py:343
  3.2 4.0 %collective-permute-start = (bf16[256,1024]{1,0:T(8,128)(2,1)}, bf16[256,1024]{1,0:T(8,128)(2,1)S(1)}, u32[]{:S(2)}, u32[]{:S(2)}) collective-permute-start(bf16[256,1024]{1,0:T(8,128)(2,1)} %w0.3), channel_id=1, source_target_pairs={{0,1},{1,0},{2,3},{3,2},{4,5},{5,4},{6,7},{7,6},{8,9},{9,8},{10,11... | collective-permute-start | bytes 1572872 | tf_op jit(solution)/shard_map/ppermute | solution.py:343
  3.2 4.7 %collective-permute-start.2 = (bf16[256,1024]{1,0:T(8,128)(2,1)}, bf16[256,1024]{1,0:T(8,128)(2,1)S(1)}, u32[]{:S(2)}, u32[]{:S(2)}) collective-permute-start(bf16[256,1024]{1,0:T(8,128)(2,1)} %o_own.3), channel_id=1, source_target_pairs={{0,1},{1,0},{2,3},{3,2},{4,5},{5,4},{6,7},{7,6},{8,9},{9,8},{10,11... | collective-permute-start | bytes 1572872 | tf_op jit(solution)/shard_map/ppermute | solution.py:343
  3.8 0.7 %copy-start.7 = (f32[2,4,37]{2,1,0:T(4,128)S(1)}, f32[2,4,37]{2,1,0:T(4,128)}, u32[]{:S(2)}) copy-start(f32[2,4,37]{2,1,0:T(4,128)} %table.2) | copy-start | bytes 3556
  5.2 3.5 %copy-start.1 = (bf16[1024,1024]{1,0:T(8,128)(2,1)S(1)}, bf16[1024,1024]{1,0:T(8,128)(2,1)}, u32[]{:S(2)}) copy-start(bf16[1024,1024]{1,0:T(8,128)(2,1)} %d0.3) | copy-start | bytes 6291460
  5.2 3.7 %copy-start.2 = (bf16[256,1024]{1,0:T(8,128)(2,1)S(1)}, bf16[256,1024]{1,0:T(8,128)(2,1)}, u32[]{:S(2)}) copy-start(bf16[256,1024]{1,0:T(8,128)(2,1)} %w0.3) | copy-start | bytes 1572868
  5.2 4.1 %copy-start.8 = (f32[2,4,37]{2,1,0:T(4,128)S(1)}, f32[2,4,37]{2,1,0:T(4,128)}, u32[]{:S(2)}) copy-start(f32[2,4,37]{2,1,0:T(4,128)} %table.2) | copy-start | bytes 3556
  7.3 1.4 %collective-permute-start.1 = (bf16[160,256]{1,0:T(8,128)(2,1)S(1)}, bf16[160,256]{1,0:T(8,128)(2,1)S(1)}, u32[]{:S(2)}, u32[]{:S(2)}) collective-permute-start(bf16[160,256]{1,0:T(8,128)(2,1)S(1)} %get-tuple-element.51), channel_id=1, source_target_pairs={{0,1},{1,0},{2,3},{3,2},{4,5},{5,4},{6,7},{7,6},{8,9},{9,8},{10,11... | collective-permute-start | bytes 245768 | tf_op jit(solution)/shard_map/ppermute | solution.py:343
  8.7 6.2 %collective-permute-start.6 = (bf16[1024,1024]{1,0:T(8,128)(2,1)S(1)}, bf16[1024,1024]{1,0:T(8,128)(2,1)S(1)}, u32[]{:S(2)}, u32[]{:S(2)}) collective-permute-start(bf16[1024,1024]{1,0:T(8,128)(2,1)S(1)} %copy-done.1), channel_id=1, source_target_pairs={{0,1},{1,0},{2,3},{3,2},{4,5},{5,4},{6,7},{7,6},{8,9},{9,8},{10,11... | collective-permute-start | bytes 6291464 | tf_op jit(solution)/shard_map/ppermute | solution.py:343
  9.2 5.6 %collective-permute-start.4 = (bf16[80,1024]{1,0:T(8,128)(2,1)S(1)}, bf16[80,1024]{1,0:T(8,128)(2,1)S(1)}, u32[]{:S(2)}, u32[]{:S(2)}) collective-permute-start(bf16[80,1024]{1,0:T(8,128)(2,1)S(1)} %shard_map.84.mine), channel_id=1, source_target_pairs={{0,2},{1,3},{2,0},{3,1},{4,6},{5,7},{6,4},{7,5},{8,10},{9,11},{10,... | collective-permute-start | bytes 491528 | tf_op jit(solution)/shard_map/ppermute | solution.py:343
  10.0 3.0 %collective-permute-start.5 = (bf16[32,256]{1,0:T(8,128)(2,1)S(1)}, bf16[32,256]{1,0:T(8,128)(2,1)S(1)}, u32[]{:S(2)}, u32[]{:S(2)}) collective-permute-start(bf16[32,256]{1,0:T(8,128)(2,1)S(1)} %shard_map.85.b_own), channel_id=1, source_target_pairs={{0,1},{1,0},{2,3},{3,2},{4,5},{5,4},{6,7},{7,6},{8,9},{9,8},{10,11... | collective-permute-start | bytes 49160 | tf_op jit(solution)/shard_map/ppermute | solution.py:343
  10.7 2.4 %copy-start = (bf16[1024,1024]{1,0:T(8,128)(2,1)S(1)}, bf16[1024,1024]{1,0:T(8,128)(2,1)}, u32[]{:S(2)}) copy-start(bf16[1024,1024]{1,0:T(8,128)(2,1)} %u0.3) | copy-start | bytes 6291460
  10.7 6.5 %collective-permute-start.9 = (bf16[40,1024]{1,0:T(8,128)(2,1)S(1)}, bf16[40,1024]{1,0:T(8,128)(2,1)S(1)}, u32[]{:S(2)}, u32[]{:S(2)}) collective-permute-start(bf16[40,1024]{1,0:T(8,128)(2,1)S(1)} %get-tuple-element.64.mine), channel_id=1, source_target_pairs={{0,2},{1,3},{2,0},{3,1},{4,6},{5,7},{6,4},{7,5},{8,10},{9,11},{10,... | collective-permute-start | bytes 245768 | tf_op jit(solution)/shard_map/ppermute | solution.py:343
  12.9 6.2 %collective-permute-start.11 = (bf16[40,1024]{1,0:T(8,128)(2,1)S(1)}, bf16[40,1024]{1,0:T(8,128)(2,1)S(1)}, u32[]{:S(2)}, u32[]{:S(2)}) collective-permute-start(bf16[40,1024]{1,0:T(8,128)(2,1)S(1)} %get-tuple-element.68.mine), channel_id=1, source_target_pairs={{0,2},{1,3},{2,0},{3,1},{4,6},{5,7},{6,4},{7,5},{8,10},{9,11},{10,... | collective-permute-start | bytes 245768 | tf_op jit(solution)/shard_map/ppermute | solution.py:343
  13.1 16.1 %collective-permute-start.13 = (bf16[1024,1024]{1,0:T(8,128)(2,1)S(1)}, bf16[1024,1024]{1,0:T(8,128)(2,1)S(1)}, u32[]{:S(2)}, u32[]{:S(2)}) collective-permute-start(bf16[1024,1024]{1,0:T(8,128)(2,1)S(1)} %copy-done), channel_id=1, source_target_pairs={{0,1},{1,0},{2,3},{3,2},{4,5},{5,4},{6,7},{7,6},{8,9},{9,8},{10,11... | collective-permute-start | bytes 6291464 | tf_op jit(solution)/shard_map/ppermute | solution.py:343
  14.9 10.5 %collective-permute-start.7 = (bf16[40,1024]{1,0:T(8,128)(2,1)S(1)}, bf16[40,1024]{1,0:T(8,128)(2,1)S(1)}, u32[]{:S(2)}, u32[]{:S(2)}) collective-permute-start(bf16[40,1024]{1,0:T(8,128)(2,1)S(1)} %get-tuple-element.62), channel_id=1, source_target_pairs={{0,36},{1,37},{2,38},{3,39},{4,40},{5,41},{6,42},{7,43},{8,44},{9,... | collective-permute-start | bytes 245768 | tf_op jit(solution)/shard_map/ppermute | solution.py:343
  15.9 9.5 %collective-permute-start.8 = (bf16[40,1024]{1,0:T(8,128)(2,1)S(1)}, bf16[40,1024]{1,0:T(8,128)(2,1)S(1)}, u32[]{:S(2)}, u32[]{:S(2)}) collective-permute-start(bf16[40,1024]{1,0:T(8,128)(2,1)S(1)} %get-tuple-element.63), channel_id=1, source_target_pairs={{0,4},{1,5},{2,6},{3,7},{4,8},{5,9},{6,10},{7,11},{8,12},{9,13},{1... | collective-permute-start | bytes 245768 | tf_op jit(solution)/shard_map/ppermute | solution.py:343
  17.3 8.4 %collective-permute-start.10 = (bf16[40,1024]{1,0:T(8,128)(2,1)S(1)}, bf16[40,1024]{1,0:T(8,128)(2,1)S(1)}, u32[]{:S(2)}, u32[]{:S(2)}) collective-permute-start(bf16[40,1024]{1,0:T(8,128)(2,1)S(1)} %shard_map.90), channel_id=1, source_target_pairs={{0,32},{1,33},{2,34},{3,35},{4,36},{5,37},{6,38},{7,39},{8,40},{9,... | collective-permute-start | bytes 245768 | tf_op jit(solution)/shard_map/ppermute | solution.py:343
  19.2 6.4 %copy-start.3 = (bf16[1024,3,256]{2,0,1:T(8,128)(2,1)S(1)}, bf16[1024,3,256]{2,0,1:T(8,128)(2,1)}, u32[]{:S(2)}) copy-start(bf16[1024,3,256]{2,0,1:T(8,128)(2,1)} %param.10) | copy-start | bytes 4718596
  19.2 6.4 %copy-start.4 = (bf16[256,1024]{1,0:T(8,128)(2,1)S(1)}, bf16[256,1024]{1,0:T(8,128)(2,1)}, u32[]{:S(2)}) copy-start(bf16[256,1024]{1,0:T(8,128)(2,1)} %o_own.3) | copy-start | bytes 1572868
  27.2 4.3 %collective-permute-start.12 = (bf16[80,1024]{1,0:T(8,128)(2,1)S(1)}, bf16[80,1024]{1,0:T(8,128)(2,1)S(1)}, u32[]{:S(2)}, u32[]{:S(2)}) collective-permute-start(bf16[80,1024]{1,0:T(8,128)(2,1)S(1)} %get-tuple-element.73.mine), channel_id=1, source_target_pairs={{0,2},{1,3},{2,0},{3,1},{4,6},{5,7},{6,4},{7,5},{8,10},{9,11},{10,... | collective-permute-start | bytes 491528 | tf_op jit(solution)/shard_map/ppermute | solution.py:343
  27.6 5.8 %collective-permute-start.15 = (bf16[80,1024]{1,0:T(8,128)(2,1)S(1)}, bf16[80,1024]{1,0:T(8,128)(2,1)S(1)}, u32[]{:S(2)}, u32[]{:S(2)}) collective-permute-start(bf16[80,1024]{1,0:T(8,128)(2,1)S(1)} %shard_map.94.mine), channel_id=1, source_target_pairs={{0,2},{1,3},{2,0},{3,1},{4,6},{5,7},{6,4},{7,5},{8,10},{9,11},{10,... | collective-permute-start | bytes 491528 | tf_op jit(solution)/shard_map/ppermute | solution.py:343
  33.3 5.5 %collective-permute-start.14 = (bf16[80,1024]{1,0:T(8,128)(2,1)S(1)}, bf16[80,1024]{1,0:T(8,128)(2,1)S(1)}, u32[]{:S(2)}, u32[]{:S(2)}) collective-permute-start(bf16[80,1024]{1,0:T(8,128)(2,1)S(1)} %shard_map.93.mine), channel_id=1, source_target_pairs={{0,2},{1,3},{2,0},{3,1},{4,6},{5,7},{6,4},{7,5},{8,10},{9,11},{10,... | collective-permute-start | bytes 491528 | tf_op jit(solution)/shard_map/ppermute | solution.py:343
  35.2 7.3 %collective-permute-start.18 = (bf16[80,1024]{1,0:T(8,128)(2,1)S(1)}, bf16[80,1024]{1,0:T(8,128)(2,1)S(1)}, u32[]{:S(2)}, u32[]{:S(2)}) collective-permute-start(bf16[80,1024]{1,0:T(8,128)(2,1)S(1)} %shard_map.96.mine), channel_id=1, source_target_pairs={{0,2},{1,3},{2,0},{3,1},{4,6},{5,7},{6,4},{7,5},{8,10},{9,11},{10,... | collective-permute-start | bytes 491528 | tf_op jit(solution)/shard_map/ppermute | solution.py:343
  38.8 5.1 %collective-permute-start.16 = (bf16[40,1024]{1,0:T(8,128)(2,1)S(1)}, bf16[40,1024]{1,0:T(8,128)(2,1)S(1)}, u32[]{:S(2)}, u32[]{:S(2)}) collective-permute-start(bf16[40,1024]{1,0:T(8,128)(2,1)S(1)} %get-tuple-element.81), channel_id=1, source_target_pairs={{0,254},{1,255},{2,252},{3,253},{4,224},{5,225},{6,226},{7,227},{8... | collective-permute-start | bytes 245768 | tf_op jit(solution)/shard_map/ppermute | solution.py:343
  42.5 3.3 %collective-permute-start.17 = (bf16[40,1024]{1,0:T(8,128)(2,1)S(1)}, bf16[40,1024]{1,0:T(8,128)(2,1)S(1)}, u32[]{:S(2)}, u32[]{:S(2)}) collective-permute-start(bf16[40,1024]{1,0:T(8,128)(2,1)S(1)} %get-tuple-element.82), channel_id=1, source_target_pairs={{0,30},{1,31},{2,28},{3,29},{4,0},{5,1},{6,2},{7,3},{8,4},{9,5},{1... | collective-permute-start | bytes 245768 | tf_op jit(solution)/shard_map/ppermute | solution.py:343
  42.5 3.4 %collective-permute-start.19 = (bf16[40,1024]{1,0:T(8,128)(2,1)S(1)}, bf16[40,1024]{1,0:T(8,128)(2,1)S(1)}, u32[]{:S(2)}, u32[]{:S(2)}) collective-permute-start(bf16[40,1024]{1,0:T(8,128)(2,1)S(1)} %get-tuple-element.84), channel_id=1, source_target_pairs={{0,224},{1,225},{2,226},{3,227},{4,228},{5,229},{6,230},{7,231},{8... | collective-permute-start | bytes 245768 | tf_op jit(solution)/shard_map/ppermute | solution.py:343
  45.9 7.1 %collective-permute-start.21 = (bf16[80,1024]{1,0:T(8,128)(2,1)S(1)}, bf16[80,1024]{1,0:T(8,128)(2,1)S(1)}, u32[]{:S(2)}, u32[]{:S(2)}) collective-permute-start(bf16[80,1024]{1,0:T(8,128)(2,1)S(1)} %shard_map.99.m1), channel_id=1, source_target_pairs={{0,1},{1,0},{2,3},{3,2},{4,5},{5,4},{6,7},{7,6},{8,9},{9,8},{10,11... | collective-permute-start | bytes 491528 | tf_op jit(solution)/shard_map/ppermute | solution.py:343
  52.0 1.4 %collective-permute-start.20 = (bf16[80,1024]{1,0:T(8,128)(2,1)S(1)}, bf16[80,1024]{1,0:T(8,128)(2,1)S(1)}, u32[]{:S(2)}, u32[]{:S(2)}) collective-permute-start(bf16[80,1024]{1,0:T(8,128)(2,1)S(1)} %shard_map.97.m0), channel_id=1, source_target_pairs={{0,1},{1,0},{2,3},{3,2},{4,5},{5,4},{6,7},{7,6},{8,9},{9,8},{10,11... | collective-permute-start | bytes 491528 | tf_op jit(solution)/shard_map/ppermute | solution.py:343

commit v21 on v20

--- a/solution.py
+++ b/solution.py
@@ -279,8 +279,8 @@
         outs[p][...] = total[p * ROWS : (p + 1) * ROWS].astype(jnp.bfloat16)
 
 
-def join_kernel(p0, p1, out):
-    out[...] = joined((p0, p1)).astype(jnp.bfloat16)
+def join_kernel(second, first, out):
+    out[...] = joined((first, second)).astype(jnp.bfloat16)
 
 
 def place_kernel(m0, m1, s0, s1, out, held, sems):
@@ -413,9 +413,9 @@
     lon = home(lon, 0, 1)
     lat, own = call(sum_kernel, piece * 2, (part_b, other_b), 10**10, 8)
     lat = home(lat, 1, 0)
-    mine_a = call(join_kernel, half, (diag, lon), 10**10, 8)
+    mine_a = call(join_kernel, half, (lon, diag), 10**10, 8)
     mine_a, lat, own = tied(mine_a, lat, own)
-    mine_b = call(join_kernel, half, (lat, own), 10**6, 8)
+    mine_b = call(join_kernel, half, (own, lat), 10**6, 8)
     operands = (mine_a, mine_b, core_swap(mine_a), core_swap(mine_b))
     result = place_rows((rows * cols, levels, width), operands)
     return result.reshape(rows, cols, levels, width).transpose(2, 0, 1, 3)

time: 54.9 us -> 55.3 us (level)
  transfers between devices with their start and end apart: 22 -> 22, of which waited for: 11 -> 10; matrix products, arithmetic and copies ran while one was open for 0% -> 0% of each run, Pallas kernels for 19% -> 19%
where the time goes in v21:
time: 55.3 us; the launch traced here: 55.1 us
  starting transfers between devices  25.6 us (46%)
  waiting for transfers between devices  16.7 us (30%)
  Pallas kernels  11.7 us (21%)
  local copies, waits for them, and re-layouts  0.73 us (1%)
    ppermute x22, starting transfers between devices, move(): return lax.ppermute(value, AXES, pairs(counts, target))  25.6 us
    ppermute x22, waiting for transfers between devices, move(): return lax.ppermute(value, AXES, pairs(counts, target))  16.7 us
    pallas_call x18, Pallas kernels, call(): pl.pallas_call(kernel, out_shape=shapes, in_specs=[pl.BlockSpec(memory_sp...  10.4 us
    pallas_call x1, Pallas kernels, place_rows(): pl.pallas_call(place_kernel, out_shape=jax.ShapeDtypeStruct(shape, jnp.bf...  1.26 us
  transfers between devices with their start and end apart: 22, of which 10 were waited for; matrix products, arithmetic and copies ran while one was open for 0% of the time, Pallas kernels for 19%

profile of v21, /device:TPU:1, one launch (start us, length us, event | category | flops | bytes accessed | tf_op | source)
XLA Modules:
  0.0 55.1 jit_solution(14612218808749878803)
XLA Ops:
  0.0 3.2 %collective-permute-start.3 = (bf16[3,1024,256]{2,1,0:T(8,128)(2,1)}, bf16[3,1024,256]{2,1,0:T(8,128)(2,1)S(1)}, u32[]{:S(2)}, u32[]{:S(2)}) collective-permute-start(bf16[3,1024,256]{2,1,0:T(8,128)(2,1)} %bitcast.8), channel_id=1, source_target_pairs={{0,1},{1,0},{2,3},{3,2},{4,5},{5,4},{6,7},{7,6},{8,9},{9,8},{10,11... | collective-permute-start | bytes 4718600 | tf_op jit(solution)/shard_map/ppermute | solution.py:343
  3.2 0.5 collective-permute-start.2
  3.8 0.7 %copy-done.7 = f32[2,4,37]{2,1,0:T(4,128)S(1)} copy-done((f32[2,4,37]{2,1,0:T(4,128)S(1)}, f32[2,4,37]{2,1,0:T(4,128)}, u32[]{:S(2)}) %copy-start.7) | copy-done | bytes 1208
  4.4 0.7 %shard_map.82.bias = bf16[32,256]{1,0:T(8,128)(2,1)S(1)} custom-call(f32[2,4,37]{2,1,0:T(4,128)S(1)} %copy-done.7), custom_call_target="tpu_custom_call" | custom-call | flops 5000000000 | bytes 17568 | tf_op jit(solution)/shard_map/pallas_call | solution.py:323
  5.2 2.1 %shard_map.83 = (bf16[160,256]{1,0:T(8,128)(2,1)S(1)}, bf16[160,256]{1,0:T(8,128)(2,1)S(1)}) custom-call(bf16[72,4,1024]{2,1,0:T(4,128)(2,1)S(1)} %bitcast.11, bf16[3,1024,256]{2,1,0:T(8,128)(2,1)S(1)} %bitcast.10, bf16[32,256]{1,0:T(8,128)(2,1)S(1)} %shard_map.82.bias), custom_call_target="tpu_custom_call" | custom-call | flops 1000000000 | bytes 2342912 | tf_op jit(solution)/shard_map/pallas_call | solution.py:323
  7.6 0.4 collective-permute-done.2.o_sib
  8.0 0.7 %collective-permute-done.1.o1 = bf16[160,256]{1,0:T(8,128)(2,1)S(1)} collective-permute-done((bf16[160,256]{1,0:T(8,128)(2,1)S(1)}, bf16[160,256]{1,0:T(8,128)(2,1)S(1)}, u32[]{:S(2)}, u32[]{:S(2)}) %collective-permute-start.1) | collective-permute-done | bytes 81952 | tf_op jit(solution)/shard_map/ppermute | solution.py:343
  9.3 0.7 %shard_map.85.b_own = bf16[32,256]{1,0:T(8,128)(2,1)S(1)} custom-call(f32[2,4,37]{2,1,0:T(4,128)S(1)} %copy-done.8), custom_call_target="tpu_custom_call" | custom-call | flops 1000000000 | bytes 17568 | tf_op jit(solution)/shard_map/pallas_call | solution.py:323
  10.0 0.3 collective-permute-start.5
  10.7 1.8 %collective-permute-start.9 = (bf16[40,1024]{1,0:T(8,128)(2,1)S(1)}, bf16[40,1024]{1,0:T(8,128)(2,1)S(1)}, u32[]{:S(2)}, u32[]{:S(2)}) collective-permute-start(bf16[40,1024]{1,0:T(8,128)(2,1)S(1)} %get-tuple-element.64.mine), channel_id=1, source_target_pairs={{0,2},{1,3},{2,0},{3,1},{4,6},{5,7},{6,4},{7,5},{8,10},{9,11},{10,... | collective-permute-start | bytes 245768 | tf_op jit(solution)/shard_map/ppermute | solution.py:343
  12.5 0.4 shard_map.86
  13.1 0.5 collective-permute-start.13
  13.6 1.3 %collective-permute-done.4.other = bf16[80,1024]{1,0:T(8,128)(2,1)S(1)} collective-permute-done((bf16[80,1024]{1,0:T(8,128)(2,1)S(1)}, bf16[80,1024]{1,0:T(8,128)(2,1)S(1)}, u32[]{:S(2)}, u32[]{:S(2)}) %collective-permute-start.4) | collective-permute-done | bytes 163872 | tf_op jit(solution)/shard_map/ppermute | solution.py:343
  14.9 1.0 %collective-permute-start.7 = (bf16[40,1024]{1,0:T(8,128)(2,1)S(1)}, bf16[40,1024]{1,0:T(8,128)(2,1)S(1)}, u32[]{:S(2)}, u32[]{:S(2)}) collective-permute-start(bf16[40,1024]{1,0:T(8,128)(2,1)S(1)} %get-tuple-element.62), channel_id=1, source_target_pairs={{0,36},{1,37},{2,38},{3,39},{4,40},{5,41},{6,42},{7,43},{8,44},{9,... | collective-permute-start | bytes 245768 | tf_op jit(solution)/shard_map/ppermute | solution.py:343
  15.9 1.3 %collective-permute-start.8 = (bf16[40,1024]{1,0:T(8,128)(2,1)S(1)}, bf16[40,1024]{1,0:T(8,128)(2,1)S(1)}, u32[]{:S(2)}, u32[]{:S(2)}) collective-permute-start(bf16[40,1024]{1,0:T(8,128)(2,1)S(1)} %get-tuple-element.63), channel_id=1, source_target_pairs={{0,4},{1,5},{2,6},{3,7},{4,8},{5,9},{6,10},{7,11},{8,12},{9,13},{1... | collective-permute-start | bytes 245768 | tf_op jit(solution)/shard_map/ppermute | solution.py:343
  17.3 1.9 %collective-permute-start.10 = (bf16[40,1024]{1,0:T(8,128)(2,1)S(1)}, bf16[40,1024]{1,0:T(8,128)(2,1)S(1)}, u32[]{:S(2)}, u32[]{:S(2)}) collective-permute-start(bf16[40,1024]{1,0:T(8,128)(2,1)S(1)} %shard_map.90), channel_id=1, source_target_pairs={{0,32},{1,33},{2,34},{3,35},{4,36},{5,37},{6,38},{7,39},{8,40},{9,... | collective-permute-start | bytes 245768 | tf_op jit(solution)/shard_map/ppermute | solution.py:343
  19.2 6.2 %collective-permute-done.7.p0 = bf16[40,1024]{1,0:T(8,128)(2,1)S(1)} collective-permute-done((bf16[40,1024]{1,0:T(8,128)(2,1)S(1)}, bf16[40,1024]{1,0:T(8,128)(2,1)S(1)}, u32[]{:S(2)}, u32[]{:S(2)}) %collective-permute-start.7) | collective-permute-done | bytes 81952 | tf_op jit(solution)/shard_map/ppermute | solution.py:343
  25.7 1.5 %shard_map.92 = (bf16[80,1024]{1,0:T(8,128)(2,1)S(1)}, bf16[80,512]{1,0:T(8,128)(2,1)S(1)}) custom-call(bf16[80,1024]{1,0:T(8,128)(2,1)S(1)} %shard_map.89.xn_a, bf16[40,1024]{1,0:T(8,128)(2,1)S(1)} %collective-permute-done.10.p2.p0, bf16[40,1024]{1,0:T(8,128)(2,1)S(1)} %shard_map.91.p3.p1, bf16[3,1024,256]{2,1,0:T(8,128)(2,1)S(1)} %bitcast.9, ...), custom_call_target="tpu_custom_call" | custom-call | flops 1000000000 | bytes 4800512 | tf_op jit(solution)/shard_map/pallas_call | solution.py:323
  27.6 1.5 %collective-permute-start.15 = (bf16[80,1024]{1,0:T(8,128)(2,1)S(1)}, bf16[80,1024]{1,0:T(8,128)(2,1)S(1)}, u32[]{:S(2)}, u32[]{:S(2)}) collective-permute-start(bf16[80,1024]{1,0:T(8,128)(2,1)S(1)} %shard_map.94.mine), channel_id=1, source_target_pairs={{0,2},{1,3},{2,0},{3,1},{4,6},{5,7},{6,4},{7,5},{8,10},{9,11},{10,... | collective-permute-start | bytes 491528 | tf_op jit(solution)/shard_map/ppermute | solution.py:343
  29.1 2.3 %collective-permute-done.12.other = bf16[80,1024]{1,0:T(8,128)(2,1)S(1)} collective-permute-done((bf16[80,1024]{1,0:T(8,128)(2,1)S(1)}, bf16[80,1024]{1,0:T(8,128)(2,1)S(1)}, u32[]{:S(2)}, u32[]{:S(2)}) %collective-permute-start.12) | collective-permute-done | bytes 163872 | tf_op jit(solution)/shard_map/ppermute | solution.py:343
  31.4 1.8 %shard_map.93.mine = bf16[80,1024]{1,0:T(8,128)(2,1)S(1)} custom-call(bf16[80,1024]{1,0:T(8,128)(2,1)S(1)} %get-tuple-element.73.mine, bf16[80,1024]{1,0:T(8,128)(2,1)S(1)} %collective-permute-done.12.other, bf16[40,1024]{1,0:T(8,128)(2,1)S(1)} %collective-permute-done.7.p0, bf16[40,1024]{1,0:T(8,128)(2,1)S(1)} %collective-permute-done.8.p1, ...), custom_call_target="tpu_custom_call" | custom-call | flops 1000000000 | bytes 9043968 | tf_op jit(solution)/shard_map/pallas_call | solution.py:323
  33.4 1.8 %shard_map.96.mine = bf16[80,1024]{1,0:T(8,128)(2,1)S(1)} custom-call(bf16[80,1024]{1,0:T(8,128)(2,1)S(1)} %shard_map.94.mine, bf16[80,1024]{1,0:T(8,128)(2,1)S(1)} %collective-permute-done.15.other, bf16[40,1024]{1,0:T(8,128)(2,1)S(1)} %collective-permute-done.10.p2.p0, bf16[40,1024]{1,0:T(8,128)(2,1)S(1)} %shard_map.91.p3.p1, ...), custom_call_target="tpu_custom_call" | custom-call | flops 1000000000 | bytes 9043968 | tf_op jit(solution)/shard_map/pallas_call | solution.py:323
  35.2 1.5 %collective-permute-start.18 = (bf16[80,1024]{1,0:T(8,128)(2,1)S(1)}, bf16[80,1024]{1,0:T(8,128)(2,1)S(1)}, u32[]{:S(2)}, u32[]{:S(2)}) collective-permute-start(bf16[80,1024]{1,0:T(8,128)(2,1)S(1)} %shard_map.96.mine), channel_id=1, source_target_pairs={{0,2},{1,3},{2,0},{3,1},{4,6},{5,7},{6,4},{7,5},{8,10},{9,11},{10,... | collective-permute-start | bytes 491528 | tf_op jit(solution)/shard_map/ppermute | solution.py:343
  36.7 2.1 %collective-permute-done.14.other = bf16[80,1024]{1,0:T(8,128)(2,1)S(1)} collective-permute-done((bf16[80,1024]{1,0:T(8,128)(2,1)S(1)}, bf16[80,1024]{1,0:T(8,128)(2,1)S(1)}, u32[]{:S(2)}, u32[]{:S(2)}) %collective-permute-start.14) | collective-permute-done | bytes 163872 | tf_op jit(solution)/shard_map/ppermute | solution.py:343
  38.8 2.7 %collective-permute-start.16 = (bf16[40,1024]{1,0:T(8,128)(2,1)S(1)}, bf16[40,1024]{1,0:T(8,128)(2,1)S(1)}, u32[]{:S(2)}, u32[]{:S(2)}) collective-permute-start(bf16[40,1024]{1,0:T(8,128)(2,1)S(1)} %get-tuple-element.81), channel_id=1, source_target_pairs={{0,30},{1,31},{2,28},{3,29},{4,0},{5,1},{6,2},{7,3},{8,4},{9,5},{1... | collective-permute-start | bytes 245768 | tf_op jit(solution)/shard_map/ppermute | solution.py:343
  41.5 1.0 %collective-permute-start.17 = (bf16[40,1024]{1,0:T(8,128)(2,1)S(1)}, bf16[40,1024]{1,0:T(8,128)(2,1)S(1)}, u32[]{:S(2)}, u32[]{:S(2)}) collective-permute-start(bf16[40,1024]{1,0:T(8,128)(2,1)S(1)} %get-tuple-element.82), channel_id=1, source_target_pairs={{0,254},{1,255},{2,252},{3,253},{4,224},{5,225},{6,226},{7,227},{8... | collective-permute-start | bytes 245768 | tf_op jit(solution)/shard_map/ppermute | solution.py:343
  42.6 0.8 %collective-permute-start.19 = (bf16[40,1024]{1,0:T(8,128)(2,1)S(1)}, bf16[40,1024]{1,0:T(8,128)(2,1)S(1)}, u32[]{:S(2)}, u32[]{:S(2)}) collective-permute-start(bf16[40,1024]{1,0:T(8,128)(2,1)S(1)} %get-tuple-element.84), channel_id=1, source_target_pairs={{0,224},{1,225},{2,226},{3,227},{4,228},{5,229},{6,230},{7,231},{8... | collective-permute-start | bytes 245768 | tf_op jit(solution)/shard_map/ppermute | solution.py:343
  43.4 2.3 %collective-permute-done.17.first = bf16[40,1024]{1,0:T(8,128)(2,1)S(1)} collective-permute-done((bf16[40,1024]{1,0:T(8,128)(2,1)S(1)}, bf16[40,1024]{1,0:T(8,128)(2,1)S(1)}, u32[]{:S(2)}, u32[]{:S(2)}) %collective-permute-start.17) | collective-permute-done | bytes 81952 | tf_op jit(solution)/shard_map/ppermute | solution.py:343
  46.0 6.3 %collective-permute-start.21 = (bf16[80,1024]{1,0:T(8,128)(2,1)S(1)}, bf16[80,1024]{1,0:T(8,128)(2,1)S(1)}, u32[]{:S(2)}, u32[]{:S(2)}) collective-permute-start(bf16[80,1024]{1,0:T(8,128)(2,1)S(1)} %shard_map.99.m1), channel_id=1, source_target_pairs={{0,1},{1,0},{2,3},{3,2},{4,5},{5,4},{6,7},{7,6},{8,9},{9,8},{10,11... | collective-permute-start | bytes 491528 | tf_op jit(solution)/shard_map/ppermute | solution.py:343
  52.4 0.9 %collective-permute-done.21.s1 = bf16[80,1024]{1,0:T(8,128)(2,1)S(1)} collective-permute-done((bf16[80,1024]{1,0:T(8,128)(2,1)S(1)}, bf16[80,1024]{1,0:T(8,128)(2,1)S(1)}, u32[]{:S(2)}, u32[]{:S(2)}) %collective-permute-start.21) | collective-permute-done | bytes 163872 | tf_op jit(solution)/shard_map/ppermute | solution.py:343
  53.4 0.4 collective-permute-done.20.s0
  53.7 1.3 %shard_map.100 = bf16[72,4,1024]{2,1,0:T(4,128)(2,1)} custom-call(bf16[80,1024]{1,0:T(8,128)(2,1)S(1)} %shard_map.97.m0, bf16[80,1024]{1,0:T(8,128)(2,1)S(1)} %shard_map.99.m1, bf16[80,1024]{1,0:T(8,128)(2,1)S(1)} %collective-permute-done.20.s0, bf16[80,1024]{1,0:T(8,128)(2,1)S(1)} %collective-permute-done.21.s1), custom_call_target="tpu_custom_call" | custom-call | flops 200000000 | bytes 2000000 | tf_op jit(solution)/shard_map/pallas_call | solution.py:309
  (49 shorter events, 2.7 us)
Async XLA Ops:
  0.0 5.2 %copy-start.5 = (bf16[1024,3,256]{2,0,1:T(8,128)(2,1)S(1)}, bf16[1024,3,256]{2,0,1:T(8,128)(2,1)}, u32[]{:S(2)}) copy-start(bf16[1024,3,256]{2,0,1:T(8,128)(2,1)} %param.9) | copy-start | bytes 4718596
  0.0 5.2 %copy-start.6 = (bf16[4,6,12,1024]{3,0,2,1:T(4,128)(2,1)S(1)}, bf16[4,6,12,1024]{3,0,2,1:T(4,128)(2,1)}, u32[]{:S(2)}) copy-start(bf16[4,6,12,1024]{3,0,2,1:T(4,128)(2,1)} %param.8) | copy-start | bytes 1769476
  0.0 8.6 %collective-permute-start.3 = (bf16[3,1024,256]{2,1,0:T(8,128)(2,1)}, bf16[3,1024,256]{2,1,0:T(8,128)(2,1)S(1)}, u32[]{:S(2)}, u32[]{:S(2)}) collective-permute-start(bf16[3,1024,256]{2,1,0:T(8,128)(2,1)} %bitcast.8), channel_id=1, source_target_pairs={{0,1},{1,0},{2,3},{3,2},{4,5},{5,4},{6,7},{7,6},{8,9},{9,8},{10,11... | collective-permute-start | bytes 4718600 | tf_op jit(solution)/shard_map/ppermute | solution.py:343
  3.2 4.0 %collective-permute-start = (bf16[256,1024]{1,0:T(8,128)(2,1)}, bf16[256,1024]{1,0:T(8,128)(2,1)S(1)}, u32[]{:S(2)}, u32[]{:S(2)}) collective-permute-start(bf16[256,1024]{1,0:T(8,128)(2,1)} %w0.3), channel_id=1, source_target_pairs={{0,1},{1,0},{2,3},{3,2},{4,5},{5,4},{6,7},{7,6},{8,9},{9,8},{10,11... | collective-permute-start | bytes 1572872 | tf_op jit(solution)/shard_map/ppermute | solution.py:343
  3.2 4.7 %collective-permute-start.2 = (bf16[256,1024]{1,0:T(8,128)(2,1)}, bf16[256,1024]{1,0:T(8,128)(2,1)S(1)}, u32[]{:S(2)}, u32[]{:S(2)}) collective-permute-start(bf16[256,1024]{1,0:T(8,128)(2,1)} %o_own.3), channel_id=1, source_target_pairs={{0,1},{1,0},{2,3},{3,2},{4,5},{5,4},{6,7},{7,6},{8,9},{9,8},{10,11... | collective-permute-start | bytes 1572872 | tf_op jit(solution)/shard_map/ppermute | solution.py:343
  3.8 0.7 %copy-start.7 = (f32[2,4,37]{2,1,0:T(4,128)S(1)}, f32[2,4,37]{2,1,0:T(4,128)}, u32[]{:S(2)}) copy-start(f32[2,4,37]{2,1,0:T(4,128)} %table.2) | copy-start | bytes 3556
  5.2 3.5 %copy-start.1 = (bf16[1024,1024]{1,0:T(8,128)(2,1)S(1)}, bf16[1024,1024]{1,0:T(8,128)(2,1)}, u32[]{:S(2)}) copy-start(bf16[1024,1024]{1,0:T(8,128)(2,1)} %d0.3) | copy-start | bytes 6291460
  5.2 3.7 %copy-start.2 = (bf16[256,1024]{1,0:T(8,128)(2,1)S(1)}, bf16[256,1024]{1,0:T(8,128)(2,1)}, u32[]{:S(2)}) copy-start(bf16[256,1024]{1,0:T(8,128)(2,1)} %w0.3) | copy-start | bytes 1572868
  5.2 4.1 %copy-start.8 = (f32[2,4,37]{2,1,0:T(4,128)S(1)}, f32[2,4,37]{2,1,0:T(4,128)}, u32[]{:S(2)}) copy-start(f32[2,4,37]{2,1,0:T(4,128)} %table.2) | copy-start | bytes 3556
  7.3 1.4 %collective-permute-start.1 = (bf16[160,256]{1,0:T(8,128)(2,1)S(1)}, bf16[160,256]{1,0:T(8,128)(2,1)S(1)}, u32[]{:S(2)}, u32[]{:S(2)}) collective-permute-start(bf16[160,256]{1,0:T(8,128)(2,1)S(1)} %get-tuple-element.51), channel_id=1, source_target_pairs={{0,1},{1,0},{2,3},{3,2},{4,5},{5,4},{6,7},{7,6},{8,9},{9,8},{10,11... | collective-permute-start | bytes 245768 | tf_op jit(solution)/shard_map/ppermute | solution.py:343
  8.7 6.2 %collective-permute-start.6 = (bf16[1024,1024]{1,0:T(8,128)(2,1)S(1)}, bf16[1024,1024]{1,0:T(8,128)(2,1)S(1)}, u32[]{:S(2)}, u32[]{:S(2)}) collective-permute-start(bf16[1024,1024]{1,0:T(8,128)(2,1)S(1)} %copy-done.1), channel_id=1, source_target_pairs={{0,1},{1,0},{2,3},{3,2},{4,5},{5,4},{6,7},{7,6},{8,9},{9,8},{10,11... | collective-permute-start | bytes 6291464 | tf_op jit(solution)/shard_map/ppermute | solution.py:343
  9.2 5.6 %collective-permute-start.4 = (bf16[80,1024]{1,0:T(8,128)(2,1)S(1)}, bf16[80,1024]{1,0:T(8,128)(2,1)S(1)}, u32[]{:S(2)}, u32[]{:S(2)}) collective-permute-start(bf16[80,1024]{1,0:T(8,128)(2,1)S(1)} %shard_map.84.mine), channel_id=1, source_target_pairs={{0,2},{1,3},{2,0},{3,1},{4,6},{5,7},{6,4},{7,5},{8,10},{9,11},{10,... | collective-permute-start | bytes 491528 | tf_op jit(solution)/shard_map/ppermute | solution.py:343
  10.0 3.0 %collective-permute-start.5 = (bf16[32,256]{1,0:T(8,128)(2,1)S(1)}, bf16[32,256]{1,0:T(8,128)(2,1)S(1)}, u32[]{:S(2)}, u32[]{:S(2)}) collective-permute-start(bf16[32,256]{1,0:T(8,128)(2,1)S(1)} %shard_map.85.b_own), channel_id=1, source_target_pairs={{0,1},{1,0},{2,3},{3,2},{4,5},{5,4},{6,7},{7,6},{8,9},{9,8},{10,11... | collective-permute-start | bytes 49160 | tf_op jit(solution)/shard_map/ppermute | solution.py:343
  10.7 2.4 %copy-start = (bf16[1024,1024]{1,0:T(8,128)(2,1)S(1)}, bf16[1024,1024]{1,0:T(8,128)(2,1)}, u32[]{:S(2)}) copy-start(bf16[1024,1024]{1,0:T(8,128)(2,1)} %u0.3) | copy-start | bytes 6291460
  10.7 6.5 %collective-permute-start.9 = (bf16[40,1024]{1,0:T(8,128)(2,1)S(1)}, bf16[40,1024]{1,0:T(8,128)(2,1)S(1)}, u32[]{:S(2)}, u32[]{:S(2)}) collective-permute-start(bf16[40,1024]{1,0:T(8,128)(2,1)S(1)} %get-tuple-element.64.mine), channel_id=1, source_target_pairs={{0,2},{1,3},{2,0},{3,1},{4,6},{5,7},{6,4},{7,5},{8,10},{9,11},{10,... | collective-permute-start | bytes 245768 | tf_op jit(solution)/shard_map/ppermute | solution.py:343
  12.9 6.2 %collective-permute-start.11 = (bf16[40,1024]{1,0:T(8,128)(2,1)S(1)}, bf16[40,1024]{1,0:T(8,128)(2,1)S(1)}, u32[]{:S(2)}, u32[]{:S(2)}) collective-permute-start(bf16[40,1024]{1,0:T(8,128)(2,1)S(1)} %get-tuple-element.68.mine), channel_id=1, source_target_pairs={{0,2},{1,3},{2,0},{3,1},{4,6},{5,7},{6,4},{7,5},{8,10},{9,11},{10,... | collective-permute-start | bytes 245768 | tf_op jit(solution)/shard_map/ppermute | solution.py:343
  13.1 16.1 %collective-permute-start.13 = (bf16[1024,1024]{1,0:T(8,128)(2,1)S(1)}, bf16[1024,1024]{1,0:T(8,128)(2,1)S(1)}, u32[]{:S(2)}, u32[]{:S(2)}) collective-permute-start(bf16[1024,1024]{1,0:T(8,128)(2,1)S(1)} %copy-done), channel_id=1, source_target_pairs={{0,1},{1,0},{2,3},{3,2},{4,5},{5,4},{6,7},{7,6},{8,9},{9,8},{10,11... | collective-permute-start | bytes 6291464 | tf_op jit(solution)/shard_map/ppermute | solution.py:343
  14.9 10.5 %collective-permute-start.7 = (bf16[40,1024]{1,0:T(8,128)(2,1)S(1)}, bf16[40,1024]{1,0:T(8,128)(2,1)S(1)}, u32[]{:S(2)}, u32[]{:S(2)}) collective-permute-start(bf16[40,1024]{1,0:T(8,128)(2,1)S(1)} %get-tuple-element.62), channel_id=1, source_target_pairs={{0,36},{1,37},{2,38},{3,39},{4,40},{5,41},{6,42},{7,43},{8,44},{9,... | collective-permute-start | bytes 245768 | tf_op jit(solution)/shard_map/ppermute | solution.py:343
  15.9 9.5 %collective-permute-start.8 = (bf16[40,1024]{1,0:T(8,128)(2,1)S(1)}, bf16[40,1024]{1,0:T(8,128)(2,1)S(1)}, u32[]{:S(2)}, u32[]{:S(2)}) collective-permute-start(bf16[40,1024]{1,0:T(8,128)(2,1)S(1)} %get-tuple-element.63), channel_id=1, source_target_pairs={{0,4},{1,5},{2,6},{3,7},{4,8},{5,9},{6,10},{7,11},{8,12},{9,13},{1... | collective-permute-start | bytes 245768 | tf_op jit(solution)/shard_map/ppermute | solution.py:343
  17.3 8.4 %collective-permute-start.10 = (bf16[40,1024]{1,0:T(8,128)(2,1)S(1)}, bf16[40,1024]{1,0:T(8,128)(2,1)S(1)}, u32[]{:S(2)}, u32[]{:S(2)}) collective-permute-start(bf16[40,1024]{1,0:T(8,128)(2,1)S(1)} %shard_map.90), channel_id=1, source_target_pairs={{0,32},{1,33},{2,34},{3,35},{4,36},{5,37},{6,38},{7,39},{8,40},{9,... | collective-permute-start | bytes 245768 | tf_op jit(solution)/shard_map/ppermute | solution.py:343
  19.2 6.4 %copy-start.3 = (bf16[1024,3,256]{2,0,1:T(8,128)(2,1)S(1)}, bf16[1024,3,256]{2,0,1:T(8,128)(2,1)}, u32[]{:S(2)}) copy-start(bf16[1024,3,256]{2,0,1:T(8,128)(2,1)} %param.10) | copy-start | bytes 4718596
  19.2 6.4 %copy-start.4 = (bf16[256,1024]{1,0:T(8,128)(2,1)S(1)}, bf16[256,1024]{1,0:T(8,128)(2,1)}, u32[]{:S(2)}) copy-start(bf16[256,1024]{1,0:T(8,128)(2,1)} %o_own.3) | copy-start | bytes 1572868
  27.2 4.3 %collective-permute-start.12 = (bf16[80,1024]{1,0:T(8,128)(2,1)S(1)}, bf16[80,1024]{1,0:T(8,128)(2,1)S(1)}, u32[]{:S(2)}, u32[]{:S(2)}) collective-permute-start(bf16[80,1024]{1,0:T(8,128)(2,1)S(1)} %get-tuple-element.73.mine), channel_id=1, source_target_pairs={{0,2},{1,3},{2,0},{3,1},{4,6},{5,7},{6,4},{7,5},{8,10},{9,11},{10,... | collective-permute-start | bytes 491528 | tf_op jit(solution)/shard_map/ppermute | solution.py:343
  27.6 5.8 %collective-permute-start.15 = (bf16[80,1024]{1,0:T(8,128)(2,1)S(1)}, bf16[80,1024]{1,0:T(8,128)(2,1)S(1)}, u32[]{:S(2)}, u32[]{:S(2)}) collective-permute-start(bf16[80,1024]{1,0:T(8,128)(2,1)S(1)} %shard_map.94.mine), channel_id=1, source_target_pairs={{0,2},{1,3},{2,0},{3,1},{4,6},{5,7},{6,4},{7,5},{8,10},{9,11},{10,... | collective-permute-start | bytes 491528 | tf_op jit(solution)/shard_map/ppermute | solution.py:343
  33.3 5.5 %collective-permute-start.14 = (bf16[80,1024]{1,0:T(8,128)(2,1)S(1)}, bf16[80,1024]{1,0:T(8,128)(2,1)S(1)}, u32[]{:S(2)}, u32[]{:S(2)}) collective-permute-start(bf16[80,1024]{1,0:T(8,128)(2,1)S(1)} %shard_map.93.mine), channel_id=1, source_target_pairs={{0,2},{1,3},{2,0},{3,1},{4,6},{5,7},{6,4},{7,5},{8,10},{9,11},{10,... | collective-permute-start | bytes 491528 | tf_op jit(solution)/shard_map/ppermute | solution.py:343
  35.2 7.4 %collective-permute-start.18 = (bf16[80,1024]{1,0:T(8,128)(2,1)S(1)}, bf16[80,1024]{1,0:T(8,128)(2,1)S(1)}, u32[]{:S(2)}, u32[]{:S(2)}) collective-permute-start(bf16[80,1024]{1,0:T(8,128)(2,1)S(1)} %shard_map.96.mine), channel_id=1, source_target_pairs={{0,2},{1,3},{2,0},{3,1},{4,6},{5,7},{6,4},{7,5},{8,10},{9,11},{10,... | collective-permute-start | bytes 491528 | tf_op jit(solution)/shard_map/ppermute | solution.py:343
  38.8 4.6 %collective-permute-start.16 = (bf16[40,1024]{1,0:T(8,128)(2,1)S(1)}, bf16[40,1024]{1,0:T(8,128)(2,1)S(1)}, u32[]{:S(2)}, u32[]{:S(2)}) collective-permute-start(bf16[40,1024]{1,0:T(8,128)(2,1)S(1)} %get-tuple-element.81), channel_id=1, source_target_pairs={{0,30},{1,31},{2,28},{3,29},{4,0},{5,1},{6,2},{7,3},{8,4},{9,5},{1... | collective-permute-start | bytes 245768 | tf_op jit(solution)/shard_map/ppermute | solution.py:343
  41.5 4.2 %collective-permute-start.17 = (bf16[40,1024]{1,0:T(8,128)(2,1)S(1)}, bf16[40,1024]{1,0:T(8,128)(2,1)S(1)}, u32[]{:S(2)}, u32[]{:S(2)}) collective-permute-start(bf16[40,1024]{1,0:T(8,128)(2,1)S(1)} %get-tuple-element.82), channel_id=1, source_target_pairs={{0,254},{1,255},{2,252},{3,253},{4,224},{5,225},{6,226},{7,227},{8... | collective-permute-start | bytes 245768 | tf_op jit(solution)/shard_map/ppermute | solution.py:343
  42.6 3.4 %collective-permute-start.19 = (bf16[40,1024]{1,0:T(8,128)(2,1)S(1)}, bf16[40,1024]{1,0:T(8,128)(2,1)S(1)}, u32[]{:S(2)}, u32[]{:S(2)}) collective-permute-start(bf16[40,1024]{1,0:T(8,128)(2,1)S(1)} %get-tuple-element.84), channel_id=1, source_target_pairs={{0,224},{1,225},{2,226},{3,227},{4,228},{5,229},{6,230},{7,231},{8... | collective-permute-start | bytes 245768 | tf_op jit(solution)/shard_map/ppermute | solution.py:343
  46.0 7.4 %collective-permute-start.21 = (bf16[80,1024]{1,0:T(8,128)(2,1)S(1)}, bf16[80,1024]{1,0:T(8,128)(2,1)S(1)}, u32[]{:S(2)}, u32[]{:S(2)}) collective-permute-start(bf16[80,1024]{1,0:T(8,128)(2,1)S(1)} %shard_map.99.m1), channel_id=1, source_target_pairs={{0,1},{1,0},{2,3},{3,2},{4,5},{5,4},{6,7},{7,6},{8,9},{9,8},{10,11... | collective-permute-start | bytes 491528 | tf_op jit(solution)/shard_map/ppermute | solution.py:343
  52.3 1.4 %collective-permute-start.20 = (bf16[80,1024]{1,0:T(8,128)(2,1)S(1)}, bf16[80,1024]{1,0:T(8,128)(2,1)S(1)}, u32[]{:S(2)}, u32[]{:S(2)}) collective-permute-start(bf16[80,1024]{1,0:T(8,128)(2,1)S(1)} %shard_map.97.m0), channel_id=1, source_target_pairs={{0,1},{1,0},{2,3},{3,2},{4,5},{5,4},{6,7},{7,6},{8,9},{9,8},{10,11... | collective-permute-start | bytes 491528 | tf_op jit(solution)/shard_map/ppermute | solution.py:343
